TPU v7x, 32 devices: a whole 2x2x4 slice. The times are simulated.
32 devices in a mesh: tm: 16 (over z, x, core), grp: 2 (over y).
Axes of the slice: x: 2, y: 2, z: 4, core: 2. Of those that a mesh axis runs over, the one named last changes fastest.
Arguments:
- frames_in: bfloat16 [256, 32, 8, 256], P('tm', 'grp'), may hold values from -6 to 6
- span_frames: int32 [16], P('tm'), may hold values from 5 to 13, as said below
- w_spatial: bfloat16 [3, 3, 256, 256], replicated, may hold values from -0.125 to 0.125
- w_temporal: bfloat16 [3, 256, 256], replicated, may hold values from -0.21875 to 0.21875
- w_down: bfloat16 [2, 2, 256, 256], replicated, may hold values from -0.1875 to 0.1875
- cotangent: bfloat16 [256, 16, 4, 256], P('tm', 'grp'), may hold values from -6 to 6
Outputs:
- down_out: bfloat16 [256, 16, 4, 256], P('tm', 'grp')
- grad_x: bfloat16 [256, 32, 8, 256], P('tm', 'grp')
- grad_spatial: float32 [3, 3, 256, 256], replicated
- grad_temporal: float32 [3, 256, 256], replicated
- grad_down: float32 [2, 2, 256, 256], replicated
Inputs may be any that keep to these rules, and one draw needn't show every extreme that they name: `span_frames`: each entry is 1 + 4k for a whole k >= 1; some time block uses the largest count 16 - 3.
All inputs are finite; a program needn't handle non-finite values.
Results may differ from a plain program's by a relative error of at most 0.01.
Values may be sent and summed in bfloat16 or wider, within the bound.
No kernel may reach another device: no remote copies, remote signals or barrier semaphores. Data moves between devices by JAX's collectives and lax.ppermute only.
A program may use at most 64 MiB of HBM per device.

v0:
```python
import jax
import jax.numpy as jnp
from jax import lax
from jax.sharding import PartitionSpec as P


def passed_along(value, axis, by):
    count = lax.axis_size(axis)
    pairs = [(i, i + by) for i in range(count) if 0 <= i + by < count]
    return lax.ppermute(value, axis, pairs)


def activate(values):
    scaled = values * lax.rsqrt(jnp.mean(values * values, axis=-1, keepdims=True) + 1e-06)
    return jax.nn.silu(scaled)


def conv_forward(padded, weights, height, width):
    total = None
    for row_off in range(3):
        for col_off in range(3):
            piece = padded[:, row_off : row_off + height, col_off : col_off + width]
            term = jnp.einsum(
                "fhwc,cd->fhwd",
                piece,
                weights[row_off, col_off],
                preferred_element_type=jnp.float32,
            )
            total = term if total is None else total + term
    return total


def conv_backward(padded, weights, height, width):
    total = None
    for row_off in range(3):
        for col_off in range(3):
            piece = padded[:, 2 - row_off : 2 - row_off + height, 2 - col_off : 2 - col_off + width]
            term = jnp.einsum(
                "fhwd,cd->fhwc",
                piece,
                weights[row_off, col_off],
                preferred_element_type=jnp.float32,
            )
            total = term if total is None else total + term
    return total


def spatial_grad(padded, grads, height, width):
    rows_out = []
    for row_off in range(3):
        cols_out = []
        for col_off in range(3):
            piece = padded[:, row_off : row_off + height, col_off : col_off + width]
            cols_out.append(
                jnp.einsum("fhwc,fhwd->cd", piece, grads, preferred_element_type=jnp.float32)
            )
        rows_out.append(jnp.stack(cols_out))
    return jnp.stack(rows_out)


def pad_both(values):
    return jnp.pad(values, ((0, 0), (1, 1), (1, 1), (0, 0)))


def body(frames_in, span_frames, w_spatial, w_temporal, w_down, cotangent):
    slots, band_rows, width_cells, channels = frames_in.shape
    count_here = span_frames[0]
    valid = (jnp.arange(slots, dtype=jnp.int32) < count_here).astype(jnp.float32)[
        :, None, None, None
    ]
    x_float = frames_in.astype(jnp.float32)
    activated, pullback = jax.vjp(activate, x_float)
    acts = (activated * valid).astype(jnp.bfloat16)
    members = lax.axis_size("grp")
    grouped = acts.reshape(members, slots // members, band_rows, width_cells, channels)
    frames_only = lax.all_to_all(grouped, "grp", split_axis=0, concat_axis=2, tiled=True)[0]
    padded = pad_both(frames_only)
    result = conv_forward(padded, w_spatial, frames_only.shape[1], width_cells).astype(jnp.bfloat16)
    spatial_frames = result[None]
    padded_frames = padded[None]
    acts_pad = padded_frames[0]
    spatial = lax.all_to_all(
        spatial_frames, "grp", split_axis=2, concat_axis=0, tiled=True
    ).reshape(slots, band_rows, width_cells, channels)
    edge_frames = lax.dynamic_slice_in_dim(spatial, count_here - 2, 2, 0)
    previous = passed_along(edge_frames, "tm", 1)
    extended = jnp.concatenate([previous, spatial], 0)
    temporal_sum = None
    for k in range(3):
        term = jnp.einsum(
            "fhwc,cd->fhwd",
            extended[k : k + slots],
            w_temporal[k],
            preferred_element_type=jnp.float32,
        )
        temporal_sum = term if temporal_sum is None else temporal_sum + term
    y_out = ((x_float + temporal_sum) * valid).astype(jnp.bfloat16)
    y_blocks = y_out.reshape(slots, band_rows // 2, 2, width_cells // 2, 2, channels)
    down_out = jnp.einsum(
        "fiajbc,abcd->fijd", y_blocks, w_down, preferred_element_type=jnp.float32
    ).astype(jnp.bfloat16)
    grad_pre = jnp.einsum(
        "fijd,abcd->fiajbc", cotangent, w_down, preferred_element_type=jnp.float32
    )
    grad_y = (grad_pre.reshape(slots, band_rows, width_cells, channels) * valid).astype(
        jnp.bfloat16
    )
    grad_down = jnp.einsum(
        "fiajbc,fijd->abcd", y_blocks, cotangent, preferred_element_type=jnp.float32
    )
    next_grads = passed_along(grad_y[:2], "tm", -1)
    padded_grads = jnp.concatenate(
        [grad_y, jnp.zeros((2, band_rows, width_cells, channels), jnp.bfloat16)], 0
    )
    anchor = count_here * 0
    placed = lax.dynamic_update_slice(
        padded_grads, next_grads, (count_here, anchor, anchor, anchor)
    )
    grad_sum = None
    for k in range(3):
        term = jnp.einsum(
            "fhwd,cd->fhwc",
            placed[2 - k : 2 - k + slots],
            w_temporal[k],
            preferred_element_type=jnp.float32,
        )
        grad_sum = term if grad_sum is None else grad_sum + term
    grad_s = (grad_sum * valid).astype(jnp.bfloat16)
    grad_temporal = jnp.stack(
        [
            jnp.einsum(
                "fhwc,fhwd->cd", extended[k : k + slots], grad_y, preferred_element_type=jnp.float32
            )
            for k in range(3)
        ]
    )
    grads_frames = lax.all_to_all(grad_s, "grp", split_axis=0, concat_axis=1, tiled=True)
    frame_rows = grads_frames.shape[1]
    grad_a_frames = conv_backward(pad_both(grads_frames), w_spatial, frame_rows, width_cells)
    grad_spatial = spatial_grad(acts_pad, grads_frames, frame_rows, width_cells)
    grad_a = lax.all_to_all(grad_a_frames, "grp", split_axis=1, concat_axis=0, tiled=True)
    grad_x = (grad_y.astype(jnp.float32) + valid * pullback(grad_a)[0]).astype(jnp.bfloat16)
    grad_spatial, grad_temporal, grad_down = lax.psum(
        (grad_spatial, grad_temporal, grad_down), ("tm", "grp")
    )
    return (down_out, grad_x, grad_spatial, grad_temporal, grad_down)


def solution(mesh):
    return jax.shard_map(
        body,
        mesh=mesh,
        in_specs=(P("tm", "grp", None, None), P("tm"), P(), P(), P(), P("tm", "grp", None, None)),
        out_specs=(P("tm", "grp", None, None), P("tm", "grp", None, None), P(), P(), P()),
        check_vma=False,
    )
```

profile of v0, /device:TPU:0, one launch (start us, length us, event | category | flops | bytes accessed | tf_op | source)
XLA Modules:
  0.0 310.4 jit_solution(1756260734271584192)
XLA Ops:
  8.2 2.4 multiply_convert_fusion
  10.7 2.9 copy.84
  13.6 2.7 reshape.49
  16.6 1.4 collective-permute-start.1
  18.1 1.1 concatenate.7
  19.2 0.8 collective-permute-done.1
  20.0 0.7 constant_dynamic-update-slice_fusion
  20.7 1.8 fusion.66
  23.5 17.3 %all_to_all.66 = bf16[16,16,8,256]{3,2,1,0:T(8,128)(2,1)S(1)} all-to-all(bf16[16,16,8,256]{3,2,1,0:T(8,128)(2,1)S(1)} %multiply_convert_fusion.1), channel_id=1, replica_groups=mesh['tm'=16,'grp'=2] {'grp'}, dimensions={0} | all-to-all | bytes 2097152 | tf_op jit(solution)/shard_map/all_to_all | solution.py:137
  44.7 1.1 add_add_fusion.1
  45.9 1.6 copy.86
  47.5 5.1 %all-to-all-start.3 = ((f32[8,32,8,256]{3,2,0,1:T(8,128)}), f32[8,32,8,256]{3,2,0,1:T(8,128)}, u32[]{:S(2)}, u32[]{:S(2)}) async-start(f32[8,32,8,256]{3,2,0,1:T(8,128)} %copy.86), calls=%async_computation.3 | async-start | bytes 4194304 | tf_op jit(solution)/shard_map/all_to_all | solution.py:141
  53.0 25.1 %all-to-all-done.3 = f32[8,32,8,256]{3,2,0,1:T(8,128)} async-done(((f32[8,32,8,256]{3,2,0,1:T(8,128)}), f32[8,32,8,256]{3,2,0,1:T(8,128)}, u32[]{:S(2)}, u32[]{:S(2)}) %all-to-all-start.3) | async-done | bytes 2097184 | tf_op jit(solution)/shard_map/all_to_all | solution.py:141
  78.0 1.8 copy.87
  79.9 0.9 fusion.9
  81.3 1.1 copy-done.4
  82.4 2.3 fusion.12
  84.7 4.6 %all-to-all-start = ((bf16[2,8,16,8,256]{4,3,2,1,0:T(8,128)(2,1)}), bf16[2,8,16,8,256]{4,3,2,1,0:T(8,128)(2,1)}, u32[]{:S(2)}, u32[]{:S(2)}) async-start(bf16[2,8,16,8,256]{4,3,2,1,0:T(8,128)(2,1)} %bitcast.309), calls=%async_computation | async-start | bytes 2097152 | tf_op jit(solution)/shard_map/all_to_all | solution.py:76
  89.2 1.1 copy.88
  90.4 13.5 %all-to-all-done = bf16[2,8,16,8,256]{4,3,2,1,0:T(8,128)(2,1)} async-done(((bf16[2,8,16,8,256]{4,3,2,1,0:T(8,128)(2,1)}), bf16[2,8,16,8,256]{4,3,2,1,0:T(8,128)(2,1)}, u32[]{:S(2)}, u32[]{:S(2)}) %all-to-all-start) | async-done | bytes 1048608 | tf_op jit(solution)/shard_map/all_to_all | solution.py:76
  103.9 1.3 copy.79
  105.2 1.4 fusion.29
  110.9 1.2 convolution_bitcast_fusion.12
  112.1 1.2 convolution_bitcast_fusion.13
  113.3 1.2 convolution_bitcast_fusion.14
  114.6 1.3 convolution_bitcast_fusion.9
  115.8 1.3 convolution_bitcast_fusion.6
  117.1 1.2 convolution_bitcast_fusion.7
  118.3 1.1 fusion.17
  119.4 1.1 copy.80
  120.5 4.4 %all-to-all-start.1 = ((bf16[1,8,32,8,256]{4,3,1,0,2:T(8,128)(2,1)}), bf16[1,8,32,8,256]{4,3,1,0,2:T(8,128)(2,1)}, u32[]{:S(2)}, u32[]{:S(2)}) async-start(bf16[1,8,32,8,256]{4,3,1,0,2:T(8,128)(2,1)} %copy.80), calls=%async_computation.1 | async-start | bytes 2097152 | tf_op jit(solution)/shard_map/all_to_all | solution.py:82
  126.7 1.6 pad_maximum_fusion
  128.3 10.6 %all-to-all-done.1 = bf16[1,8,32,8,256]{4,3,1,0,2:T(8,128)(2,1)} async-done(((bf16[1,8,32,8,256]{4,3,1,0,2:T(8,128)(2,1)}), bf16[1,8,32,8,256]{4,3,1,0,2:T(8,128)(2,1)}, u32[]{:S(2)}, u32[]{:S(2)}) %all-to-all-start.1) | async-done | bytes 1048608 | tf_op jit(solution)/shard_map/all_to_all | solution.py:82
  138.8 1.3 copy.81
  140.2 1.3 collective-permute-start
  141.5 0.8 convolution_bitcast_fusion.5
  143.3 0.8 copy-done.2
  144.0 0.7 fusion.15
  144.7 1.2 reshape.48
  145.9 3.8 %convolution_bitcast_fusion.1 = f32[2,2,256,256]{3,2,1,0:T(8,128)} fusion(bf16[16,8,2,4,2,256]{5,4,3,2,1,0:T(2,128)(2,1)} %reshape.48, bf16[16,8,4,256,1,1]{3,2,1,0,5,4:T(4,128)(2,1)S(1)} %bitcast.312), kind=kOutput, calls=%fused_computation.48 | convolution fusion | flops 268435456 | bytes 2359296 | tf_op jit(solution)/shard_map/fiajbc,fijd->abcd/dot_general | solution.py:108
  150.8 0.9 pad_maximum_fusion.2
  151.8 1.2 copy-done.14
  153.0 0.7 fusion.18
  153.7 0.8 copy.92
  154.5 143.8 %all-reduce.6.cloned.1.call-done = (f32[3,3,256,256]{3,2,1,0:T(8,128)}, f32[3,256,256]{2,1,0:T(8,128)}, f32[2,2,256,256]{3,2,1,0:T(8,128)}) async-done(((f32[3,3,256,256]{3,2,1,0:T(8,128)}, f32[3,256,256]{2,1,0:T(8,128)}, f32[2,2,256,256]{3,2,1,0:T(8,128)}), (f32[3,3,256,256]{3,2,1,0:T(8,128)}, f32[3,256,256]{2,1,0:T(8,128)}, f32[2,2,256,256]{3,2,1,0:T(8,128)})) %all-reduce.6.cloned.1.call-update) | async-done | bytes 4194320 | tf_op jit(solution)/shard_map/psum | solution.py:143
  298.3 3.4 %copy.144 = f32[3,3,256,256]{3,2,1,0:T(8,128)} copy(f32[3,3,256,256]{3,2,1,0:T(8,128)} %get-tuple-element.31) | data formatting | bytes 4718592
  301.7 0.9 copy.145
  302.5 1.0 copy.146
  (81 shorter events, 14.2 us)
Async XLA Ops:
  7.2 1.1 copy-start
  16.3 2.9 copy-start.3
  16.6 1.5 copy-start.6
  16.6 4.1 %copy-start.11 = (bf16[3,256,256]{2,1,0:T(8,128)(2,1)S(1)}, bf16[3,256,256]{2,1,0:T(8,128)(2,1)}, u32[]{:S(2)}) copy-start(bf16[3,256,256]{2,1,0:T(8,128)(2,1)} %param.9) | copy-start | bytes 1179652
  16.6 3.4 %collective-permute-start.1 = (bf16[2,16,8,256]{3,2,1,0:T(8,128)(2,1)S(1)}, bf16[2,16,8,256]{3,2,1,0:T(8,128)(2,1)S(1)}, u32[]{:S(2)}, u32[]{:S(2)}) collective-permute-start(bf16[2,16,8,256]{3,2,1,0:T(8,128)(2,1)S(1)} %slice.161), channel_id=1, source_target_pairs={{2,0},{4,2},{6,4},{8,6},{10,8},{12,10},{14,12},{16,14},{18,16},{20... | collective-permute-start | bytes 393224 | tf_op jit(solution)/shard_map/ppermute | solution.py:10
  20.7 1.8 copy-start.5
  23.5 17.4 %copy-start.8 = (bf16[3,3,256,256]{3,2,1,0:T(8,128)(2,1)S(1)}, bf16[3,3,256,256]{3,2,1,0:T(8,128)(2,1)}, u32[]{:S(2)}) copy-start(bf16[3,3,256,256]{3,2,1,0:T(8,128)(2,1)} %param.8) | copy-start | bytes 3538948
  47.5 5.1 %copy-start.1 = (bf16[16,16,8,256]{3,2,1,0:T(8,128)(2,1)S(1)}, bf16[16,16,8,256]{3,2,1,0:T(8,128)(2,1)}, u32[]{:S(2)}) copy-start(bf16[16,16,8,256]{3,2,1,0:T(8,128)(2,1)} %param.6) | copy-start | bytes 3145732
  47.5 30.6 %all-to-all-start.3 = ((f32[8,32,8,256]{3,2,0,1:T(8,128)}), f32[8,32,8,256]{3,2,0,1:T(8,128)}, u32[]{:S(2)}, u32[]{:S(2)}) async-start(f32[8,32,8,256]{3,2,0,1:T(8,128)} %copy.86), calls=%async_computation.3 | async-start | bytes 4194304 | tf_op jit(solution)/shard_map/all_to_all | solution.py:141
  80.8 1.6 copy-start.4
  84.7 4.6 %copy-start.10 = (bf16[16,8,2,4,2,256]{5,0,3,1,4,2:T(8,128)(2,1)S(1)}, bf16[16,8,2,4,2,256]{5,0,3,1,4,2:T(8,128)(2,1)}, u32[]{:S(2)}) copy-start(bf16[16,8,2,4,2,256]{5,0,3,1,4,2:T(8,128)(2,1)} %get-tuple-element.25) | copy-start | bytes 3145732
  84.7 19.2 %all-to-all-start = ((bf16[2,8,16,8,256]{4,3,2,1,0:T(8,128)(2,1)}), bf16[2,8,16,8,256]{4,3,2,1,0:T(8,128)(2,1)}, u32[]{:S(2)}, u32[]{:S(2)}) async-start(bf16[2,8,16,8,256]{4,3,2,1,0:T(8,128)(2,1)} %bitcast.309), calls=%async_computation | async-start | bytes 2097152 | tf_op jit(solution)/shard_map/all_to_all | solution.py:76
  105.2 1.5 copy-start.9
  120.5 18.3 %all-to-all-start.1 = ((bf16[1,8,32,8,256]{4,3,1,0,2:T(8,128)(2,1)}), bf16[1,8,32,8,256]{4,3,1,0,2:T(8,128)(2,1)}, u32[]{:S(2)}, u32[]{:S(2)}) async-start(bf16[1,8,32,8,256]{4,3,1,0,2:T(8,128)(2,1)} %copy.80), calls=%async_computation.1 | async-start | bytes 2097152 | tf_op jit(solution)/shard_map/all_to_all | solution.py:82
  125.0 173.3 %all-reduce.6.cloned.1.call-start = ((), (), s32[]{:S(2)}) async-start(), calls=%async_computation.4 | async-start | bytes 8388608 | tf_op jit(solution)/shard_map/psum | solution.py:143
  125.2 1.0 copy-start.21
  125.3 1.0 copy-start.22
  125.3 1.1 copy-start.17
  125.3 1.2 copy-start.18
  125.3 1.2 copy-start.19
  125.3 1.3 copy-start.20
  128.3 13.2 %copy-start.12 = (bf16[16,8,2,4,2,256]{5,0,4,3,2,1:T(8,128)(2,1)S(1)}, bf16[16,8,2,4,2,256]{5,0,4,3,2,1:T(8,128)(2,1)}, u32[]{:S(2)}) copy-start(bf16[16,8,2,4,2,256]{5,0,4,3,2,1:T(8,128)(2,1)} %copy.88) | copy-start | bytes 3145732
  140.2 2.6 collective-permute-start
  142.8 1.2 copy-start.2
  144.7 1.2 copy-start.16
  145.9 3.8 %copy-start.7 = (bf16[16,16,8,256]{3,2,1,0:T(8,128)(2,1)S(1)}, bf16[16,16,8,256]{3,2,1,0:T(8,128)(2,1)}, u32[]{:S(2)}) copy-start(bf16[16,16,8,256]{3,2,1,0:T(8,128)(2,1)} %copy-done.6) | copy-start | bytes 3145732
  151.7 1.2 copy-start.14
  298.3 3.4 %copy-start.15 = (f32[3,256,256]{2,1,0:T(8,128)S(1)}, f32[3,256,256]{2,1,0:T(8,128)}, u32[]{:S(2)}) copy-start(f32[3,256,256]{2,1,0:T(8,128)} %get-tuple-element.32) | copy-start | bytes 2359300
  298.3 4.2 %copy-start.13 = (f32[2,2,256,256]{3,2,1,0:T(8,128)S(1)}, f32[2,2,256,256]{3,2,1,0:T(8,128)}, u32[]{:S(2)}) copy-start(f32[2,2,256,256]{3,2,1,0:T(8,128)} %get-tuple-element.33) | copy-start | bytes 3145732
Sparse Core Ops, SparseCore 0:
  151.9 146.3 all-reduce.5
where the time goes:
time: 311 us; the launch traced here: 310 us
  waiting for transfers between devices  194 us (62%)
  matrix products  32.8 us (11%)
  local copies, waits for them, and re-layouts  27.2 us (9%)
  blocking collectives  17.3 us (6%)
  starting transfers between devices  17.1 us (5%)
  between operations  15.3 us (5%)
  other arithmetic  6.95 us (2%)
    psum x1, waiting for transfers between devices, body(): lax.psum((grad_spatial, grad_temporal, grad_down), ('tm', 'grp'))  144 us
    all_to_all x1, waiting for transfers between devices, body(): lax.all_to_all(grad_a_frames, 'grp', split_axis=1, concat_axis=0, tiled=T...  25.1 us
    all_to_all x1, blocking collectives, body(): lax.all_to_all(grad_s, 'grp', split_axis=0, concat_axis=1, tiled=True)  17.3 us
    all_to_all x1, waiting for transfers between devices, body(): lax.all_to_all(grouped, 'grp', split_axis=0, concat_axis=2, tiled=True)[0]  13.5 us
    all_to_all x1, waiting for transfers between devices, body(): lax.all_to_all(spatial_frames, 'grp', split_axis=2, concat_axis=0, tiled=...  10.6 us
    unnamed x50, local copies, waits for them, and re-layouts  10.2 us
    dot_general x9, matrix products, spatial_grad(): jnp.einsum('fhwc,fhwd->cd', piece, grads, preferred_element_type=jnp.floa...  9.08 us
  transfers between devices with their start and end apart: 6, of which 5 were waited for; matrix products, arithmetic and copies ran while one was open for 2% of the time, Pallas kernels for 0%

commit v1 on v0

v1 whole, which is shorter than its diff:
```python
import functools

import jax
import jax.numpy as jnp
from jax import lax
from jax.experimental import pallas as pl
from jax.experimental.pallas import tpu as pltpu
from jax.sharding import PartitionSpec as P

SLOTS = 16
OWN = 14
CH = 256
BF = jnp.bfloat16
F32 = jnp.float32


def mm(a, b):
    return lax.dot_general(a, b, (((1,), (0,)), ((), ())), preferred_element_type=F32)


def mm_nt(a, b):
    return lax.dot_general(a, b, (((1,), (1,)), ((), ())), preferred_element_type=F32)


def iotas(rows, cols):
    return (
        lax.broadcasted_iota(jnp.int32, (rows, cols), 0),
        lax.broadcasted_iota(jnp.int32, (rows, cols), 1),
    )


def to_slots(rows, frames, keep):
    a, b = iotas(rows * SLOTS, frames * rows)
    hit = (a // SLOTS == b % rows) & keep(b // rows, a % SLOTS)
    return jnp.where(hit, 1.0, 0.0).astype(BF)


def to_frames(rows):
    a, b = iotas(SLOTS * rows, rows * SLOTS)
    hit = (a % rows == b // SLOTS) & (a // rows == b % SLOTS)
    return jnp.where(hit, 1.0, 0.0).astype(BF)


def own_frames(count):
    return lambda frame, slot: (frame == slot) & (slot < count)


def own_and_next(count):
    return lambda frame, slot: ((frame < OWN) & (frame == slot) & (slot < count)) | (
        (frame >= OWN) & (slot == count + frame - OWN)
    )


def silu_norm(v):
    scaled = v * lax.rsqrt(jnp.mean(v * v, axis=-1, keepdims=True) + 1e-06)
    return scaled / (1.0 + jnp.exp(-scaled))


def slot_mask(shape, count):
    return lax.broadcasted_iota(jnp.int32, shape, len(shape) - 2) < count


def grad_of_temporal(gy, wt_ref, count):
    n = gy.shape[0]
    flat = gy.reshape(n * SLOTS, CH)
    total = mm_nt(flat, wt_ref[2]).reshape(n, SLOTS, CH)
    for k in (1, 0):
        term = mm_nt(flat, wt_ref[k]).reshape(n, SLOTS, CH)
        total = total + pltpu.roll(term, SLOTS - (2 - k), 1)
    return jnp.where(slot_mask(total.shape, count), total, 0.0).astype(BF)


def first_kernel(
    scal, x_ref, top_ref, bot_ref, cot_ref, nxt_ref, wt_ref, wd_ref,
    xt_ref, acts_ref, cott_ref, gy_ref, gs_ref, gw_ref, at_ref,
):
    count, has_top, has_bot = scal[0], scal[1], scal[2]
    rows, cols = xt_ref.shape[0], xt_ref.shape[1]
    edge = jnp.zeros((rows + 2, SLOTS, CH), BF)
    acts_ref[:, 0] = edge
    acts_ref[:, cols + 1] = edge
    gs_ref[:, 0] = edge[:rows]
    gs_ref[:, cols + 1] = edge[:rows]

    place = to_slots(16, SLOTS, own_frames(count))

    def rows_of(q, _):
        at = pl.multiple_of(q * 16, 16)
        piece = x_ref[:, pl.ds(at, 16), :].reshape(SLOTS * 16, CH)
        v = mm(place, piece)
        xt_ref[pl.ds(2 * q, 2)] = v.astype(BF).reshape(2, cols, SLOTS, CH)
        a = silu_norm(v)
        acts_ref[pl.ds(2 * q + 1, 2), 1 : cols + 1] = a.astype(BF).reshape(2, cols, SLOTS, CH)
        at_ref[:, pl.ds(pl.multiple_of(q * 256 + 128, 128), 256)] = a.T.astype(BF)
        return 0

    lax.fori_loop(0, rows // 2, rows_of, 0)

    place_edge = to_slots(cols, OWN, own_frames(count))
    for ref, flag, row in ((top_ref, has_top, 0), (bot_ref, has_bot, rows + 1)):
        a = silu_norm(mm(place_edge, ref[...])) * flag.astype(F32)
        acts_ref[row, 1 : cols + 1] = a.astype(BF).reshape(cols, SLOTS, CH)
        at_ref[:, row * 128 : row * 128 + 128] = a.T.astype(BF)

    place_next = to_slots(16, SLOTS, own_and_next(count))
    for q in range(rows * cols // 64):
        piece = jnp.concatenate(
            [cot_ref[0:OWN, q * 16 : q * 16 + 16, :], nxt_ref[:, q * 16 : q * 16 + 16, :]], 0
        ).reshape(SLOTS * 16, CH)
        placed = mm(place_next, piece).astype(BF)
        cott_ref[q * 4 : q * 4 + 4] = placed.reshape(4, 4, SLOTS, CH)
        for i in range(2):
            for j in range(2):
                g = mm_nt(placed, wd_ref[i * 2 + j]).astype(BF).reshape(4, 4, SLOTS, CH)
                for r in range(4):
                    for c in range(4):
                        gy_ref[2 * (q * 4 + r) + i, 2 * c + j] = g[r, c]

    def grads_of(q, _):
        g = gy_ref[pl.ds(4 * q, 4)].reshape(4 * cols, SLOTS, CH)
        s = grad_of_temporal(g, wt_ref, count)
        gs_ref[pl.ds(4 * q, 4), 1 : cols + 1] = s.reshape(4, cols, SLOTS, CH)
        return 0

    lax.fori_loop(0, rows // 4, grads_of, 0)

    wide = rows * cols * SLOTS
    for i in range(3):
        for j in range(3):
            right = gs_ref[:, 2 - j : 2 - j + cols].reshape(wide, CH)
            gw_ref[i * 3 + j] = mm(at_ref[:, i * 128 : i * 128 + wide], right).astype(BF)


def spatial_kernel(scal, acts_ref, ws_ref, sp_ref, edge_ref):
    count = scal[0]
    rows, cols = sp_ref.shape[0], sp_ref.shape[1]
    a, b = iotas(32, 256)
    pick = (a // 2 == b // SLOTS) & (b % SLOTS == count - 2 + a % 2)
    pick = jnp.where(pick, 1.0, 0.0).astype(BF)

    def rows_of(q, _):
        total = None
        for i in range(3):
            for j in range(3):
                left = acts_ref[pl.ds(4 * q + i, 4), j : j + cols].reshape(4 * cols * SLOTS, CH)
                term = mm(left, ws_ref[i * 3 + j])
                total = term if total is None else total + term
        out = total.astype(BF)
        sp_ref[pl.ds(4 * q, 4)] = out.reshape(4, cols, SLOTS, CH)
        for half in range(2):
            edge_ref[2 * q + half] = mm(pick, out[half * 256 : half * 256 + 256]).astype(BF)
        return 0

    lax.fori_loop(0, rows // 4, rows_of, 0)


def backward_kernel(
    scal, xt_ref, gy_ref, gs_ref, top_ref, bot_ref, wt_ref, wd_ref, ws_ref, out_ref, pad_ref
):
    count, has_top, has_bot = scal[0], scal[1], scal[2]
    rows, cols = xt_ref.shape[0], xt_ref.shape[1]
    pad_ref[1 : rows + 1] = gs_ref[...]
    place_edge = to_slots(cols // 2, SLOTS, own_and_next(count))
    for ref, flag, i, row in ((top_ref, has_top, 1, 0), (bot_ref, has_bot, 0, rows + 1)):
        placed = mm(place_edge, ref[...]).astype(BF)
        pair = [
            mm_nt(placed, wd_ref[i * 2 + j]).astype(BF).reshape(cols // 2, SLOTS, CH) for j in range(2)
        ]
        g = jnp.stack(pair, axis=1).reshape(cols, SLOTS, CH)
        s = grad_of_temporal(g, wt_ref, count) * flag.astype(BF)
        pad_ref[row, 0] = jnp.zeros((SLOTS, CH), BF)
        pad_ref[row, 1 : cols + 1] = s
        pad_ref[row, cols + 1] = jnp.zeros((SLOTS, CH), BF)

    back = to_frames(16)

    def rows_of(q, _):
        total = None
        for i in range(3):
            for j in range(3):
                left = pad_ref[pl.ds(4 * q + 2 - i, 4), 2 - j : 2 - j + cols].reshape(
                    4 * cols * SLOTS, CH
                )
                term = mm_nt(left, ws_ref[i * 3 + j])
                total = term if total is None else total + term
        v = xt_ref[pl.ds(4 * q, 4)].reshape(4 * cols * SLOTS, CH).astype(F32)
        r = lax.rsqrt(jnp.mean(v * v, axis=-1, keepdims=True) + 1e-06)
        u = v * r
        s = 1.0 / (1.0 + jnp.exp(-u))
        gu = total * (s * (1.0 + u * (1.0 - s)))
        dot = jnp.mean(gu * u, axis=-1, keepdims=True)
        gv = r * (gu - u * dot)
        gx = gy_ref[pl.ds(4 * q, 4)].reshape(4 * cols * SLOTS, CH).astype(F32) + gv
        gx = gx.reshape(4 * cols, SLOTS, CH)
        gx = jnp.where(slot_mask(gx.shape, count), gx, 0.0).astype(BF).reshape(4 * cols * SLOTS, CH)
        for half in range(2):
            o = mm(back, gx[half * 256 : half * 256 + 256]).astype(BF)
            at = pl.multiple_of((2 * q + half) * 16, 16)
            out_ref[:, pl.ds(at, 16), :] = o.reshape(SLOTS, 16, CH)
        return 0

    lax.fori_loop(0, rows // 4, rows_of, 0)


def forward_kernel(
    scal, xt_ref, sp_ref, prev_ref, cott_ref, gy_ref, wt_ref, wd_ref,
    down_ref, gw_ref, y_ref, st_ref, g1_ref, g0_ref, g2_ref,
):
    count = scal[0]
    rows, cols = xt_ref.shape[0], xt_ref.shape[1]
    a, b = iotas(256, 32)
    place = (a // SLOTS == b // 2) & (a % SLOTS == OWN + b % 2)
    place = jnp.where(place, 1.0, 0.0).astype(BF)

    def rows_of(q, _):
        s = sp_ref[pl.ds(2 * q, 2)].reshape(256, CH)
        s = (s.astype(F32) + mm(place, prev_ref[q])).astype(BF)
        st_ref[:, pl.ds(pl.multiple_of(q * 256, 256), 256)] = s.T
        total = mm(s, wt_ref[2]).reshape(2 * cols, SLOTS, CH)
        for k in (1, 0):
            total = total + pltpu.roll(mm(s, wt_ref[k]).reshape(2 * cols, SLOTS, CH), 2 - k, 1)
        x = xt_ref[pl.ds(2 * q, 2)].reshape(2 * cols, SLOTS, CH).astype(F32)
        mask = slot_mask(x.shape, count)
        y = jnp.where(mask, x + total, 0.0).astype(BF)
        y_ref[pl.ds(2 * q, 2)] = y.reshape(2, cols, SLOTS, CH)
        g = gy_ref[pl.ds(2 * q, 2)].reshape(2 * cols, SLOTS, CH).astype(F32)
        g = jnp.where(mask, g, 0.0)
        for ref, k in ((g2_ref, 2), (g1_ref, 1), (g0_ref, 0)):
            shifted = g if k == 2 else pltpu.roll(g, SLOTS - (2 - k), 1)
            ref[pl.ds(2 * q, 2)] = shifted.astype(BF).reshape(2, cols, SLOTS, CH)
        return 0

    lax.fori_loop(0, rows // 2, rows_of, 0)

    wide = rows * cols * SLOTS
    for k, ref in ((0, g0_ref), (1, g1_ref), (2, g2_ref)):
        gw_ref[k] = mm(st_ref[...], ref[...].reshape(wide, CH)).astype(BF)

    small = wide // 4
    total = None
    cot = cott_ref[...].reshape(small, CH)
    for i in range(2):
        for j in range(2):
            tiles = [
                y_ref[2 * r + i, 2 * c + j] for r in range(rows // 2) for c in range(cols // 2)
            ]
            piece = jnp.concatenate(tiles, axis=0)
            term = mm(piece, wd_ref[i * 2 + j])
            total = term if total is None else total + term
            gw_ref[3 + i * 2 + j] = mm(piece.T, cot).astype(BF)
    down = total.astype(BF)
    back = to_frames(16)
    for q in range(small // 256):
        o = mm(back, down[q * 256 : q * 256 + 256]).astype(BF)
        down_ref[:, q * 16 : q * 16 + 16, :] = o.reshape(SLOTS, 16, CH)


def call(kernel, outs, scratch, name, flops, *args):
    specs = [pl.BlockSpec(memory_space=pltpu.SMEM)] + [
        pl.BlockSpec(memory_space=pltpu.VMEM) for _ in args[1:]
    ]
    shapes = [jax.ShapeDtypeStruct(s, BF) for s in outs]
    moved = sum(a.size * a.dtype.itemsize for a in args) + sum(s.size * 2 for s in shapes)
    return pl.pallas_call(
        kernel,
        out_shape=shapes,
        in_specs=specs,
        out_specs=[pl.BlockSpec(memory_space=pltpu.VMEM) for _ in outs],
        scratch_shapes=[pltpu.VMEM(s, BF) for s in scratch],
        compiler_params=pltpu.CompilerParams(vmem_limit_bytes=32 * 2**20),
        cost_estimate=pl.CostEstimate(flops=flops, bytes_accessed=moved, transcendentals=0),
        name=name,
    )(*args)


AXES = ("tm", "grp")


def exchange_plan(tm, grp):
    low = grp.bit_length() - 1
    high = tm.bit_length() - 1
    bits_g = list(range(low))
    bits_t = list(range(low, low + high))
    core, rest = bits_t[0], bits_t[1:]
    first = rest[:1] + bits_g + rest[1:]
    second = rest[1:2] + rest[:1] + bits_g + rest[2:]
    return core, [(core, core)] + list(zip(first, second))


def sum_over_devices(value, tm, grp):
    total = tm * grp
    core, stages = exchange_plan(tm, grp)
    me = lax.axis_index("tm") * grp + lax.axis_index("grp")
    odd = (me >> core) & 1

    def swap(v, stage):
        pairs = [(d, d ^ (1 << stage[(d >> core) & 1])) for d in range(total)]
        return lax.ppermute(v, AXES, pairs)

    def bit_of(stage):
        return jnp.where(odd == 0, (me >> stage[0]) & 1, (me >> stage[1]) & 1)

    halved = []
    for stage in stages:
        rows = value.shape[0]
        if rows % 16 == 0 and rows > 16:
            half = rows // 2
            bit = bit_of(stage)
            keep = lax.dynamic_slice_in_dim(value, bit * half, half, 0)
            send = lax.dynamic_slice_in_dim(value, (1 - bit) * half, half, 0)
            got = swap(send, stage)
            value = (keep.astype(F32) + got.astype(F32)).astype(BF)
            halved.append((stage, bit))
        else:
            value = (value.astype(F32) + swap(value, stage).astype(F32)).astype(BF)
    for stage, bit in reversed(halved):
        got = swap(value, stage)
        value = jnp.where(
            bit == 0, jnp.concatenate([value, got], 0), jnp.concatenate([got, value], 0)
        )
    return value


def along(value, axis, by):
    count = lax.axis_size(axis)
    pairs = [(i, i + by) for i in range(count) if 0 <= i + by < count]
    return lax.ppermute(value, axis, pairs)


def edge_rows(values, rows, members, band):
    frames, wide, _ = values.shape
    flat = (frames * rows, CH)
    if members == 2:
        at = jnp.where(band == 0, wide - rows, 0)
        sent = lax.dynamic_slice_in_dim(values, at, rows, 1).reshape(flat)
        got = lax.ppermute(sent, "grp", [(0, 1), (1, 0)])
        return got, got
    return (
        along(values[:, wide - rows :].reshape(flat), "grp", 1),
        along(values[:, :rows].reshape(flat), "grp", -1),
    )


def body(tm, grp, frames_in, span_frames, w_spatial, w_temporal, w_down, cotangent):
    slots, rows, cols, ch = frames_in.shape
    wide = rows * cols
    x = frames_in.reshape(slots, wide, ch)
    cot = cotangent.reshape(slots, wide // 4, ch)
    ws = w_spatial.reshape(9, ch, ch)
    wd = w_down.reshape(4, ch, ch)
    count = span_frames[0]
    band = lax.axis_index("grp")
    scal = jnp.stack(
        [count, (band > 0).astype(jnp.int32), (band < grp - 1).astype(jnp.int32)]
    )
    tap = 2 * slots * wide * ch * ch

    nxt = along(cot[:2], "tm", -1)
    top, bot = edge_rows(x[:OWN], cols, grp, band)
    cot_all = jnp.concatenate([cot[:OWN], nxt], 0)
    cot_top, cot_bot = edge_rows(cot_all, cols // 2, grp, band)

    tile = (rows, cols, slots, ch)
    xt, acts, cott, gy, gs, gw_s = call(
        first_kernel,
        [tile, (rows + 2, cols + 2, slots, ch), (rows // 2, cols // 2, slots, ch), tile,
         (rows, cols + 2, slots, ch), (9, ch, ch)],
        [(ch, (rows + 2) * 128)],
        "grad_spatial",
        14 * tap,
        scal, x, top, bot, cot, nxt, w_temporal, wd,
    )
    sum_s = sum_over_devices(gw_s.reshape(9 * ch, ch), tm, grp)
    sp, edge = call(
        spatial_kernel, [tile, (rows // 2, 32, ch)], [], "spatial", 9 * tap, scal, acts, ws
    )
    prev = along(edge, "tm", 1)
    (grad_x,) = call(
        backward_kernel,
        [(slots, wide, ch)],
        [(rows + 2, cols + 2, slots, ch)],
        "grad_x",
        10 * tap,
        scal, xt, gy, gs, cot_top, cot_bot, w_temporal, wd, ws,
    )
    down, gw_t = call(
        forward_kernel,
        [(slots, wide // 4, ch), (7, ch, ch)],
        [tile, (ch, slots * wide), tile, tile, tile],
        "forward",
        8 * tap,
        scal, xt, sp, prev, cott, gy, w_temporal, wd,
    )
    sum_t = sum_over_devices(gw_t.reshape(7 * ch, ch), tm, grp).astype(F32)
    return (
        down.reshape(cotangent.shape),
        grad_x.reshape(frames_in.shape),
        sum_s.astype(F32).reshape(w_spatial.shape),
        sum_t[: 3 * ch].reshape(w_temporal.shape),
        sum_t[3 * ch :].reshape(w_down.shape),
    )


def solution(mesh):
    return jax.shard_map(
        functools.partial(body, mesh.shape["tm"], mesh.shape["grp"]),
        mesh=mesh,
        in_specs=(P("tm", "grp", None, None), P("tm"), P(), P(), P(), P("tm", "grp", None, None)),
        out_specs=(P("tm", "grp", None, None), P("tm", "grp", None, None), P(), P(), P()),
        check_vma=False,
    )
```

time: 311 us -> 123 us (0.40)
  waiting for transfers between devices: 194 us -> 38.9 us
  matrix products: 32.8 us -> 0 us
  Pallas kernels: 0 us -> 26.3 us
  blocking collectives: 17.3 us -> 0 us
  between operations: 15.3 us -> 1.72 us
  local copies, waits for them, and re-layouts: 27.2 us -> 17.8 us
  starting transfers between devices: 17.1 us -> 26.2 us
  other arithmetic: 6.95 us -> 11 us
    psum x1 -> x0, waiting for transfers between devices: 144 us -> none  [body(): lax.psum((grad_spatial, grad_temporal, grad_down), ('tm', 'grp'))]
    all_to_all x3 -> x0, waiting for transfers between devices: 49.1 us -> none  [the longest x1 25.1 us: body(): lax.all_to_all(grad_a_frames, 'grp', split_axis=1, concat_axis=0, tiled=T...]
    ppermute x2 -> x24, waiting for transfers between devices: 0.81 us -> 38.9 us  [the longest x20 33.1 us: swap(): return lax.ppermute(v, AXES, pairs)]
    dot_general x39 -> x0, matrix products: 32.8 us -> none  [the longest x9 9.08 us: spatial_grad(): jnp.einsum('fhwc,fhwd->cd', piece, grads, preferred_element_type=jnp.floa...]
    pallas_call x0 -> x4, Pallas kernels: none -> 26.3 us  [call(): pl.pallas_call(kernel, out_shape=shapes, in_specs=specs, out_specs=[pl.Bl...]
    ppermute x2 -> x24, starting transfers between devices: 2.72 us -> 26.2 us  [the longest x20 18 us: swap(): return lax.ppermute(v, AXES, pairs)]
    all_to_all x1 -> x0, blocking collectives: 17.3 us -> none  [body(): lax.all_to_all(grad_s, 'grp', split_axis=0, concat_axis=1, tiled=True)]
    all_to_all x3 -> x0, starting transfers between devices: 14.1 us -> none  [the longest x1 5.13 us: body(): lax.all_to_all(grad_a_frames, 'grp', split_axis=1, concat_axis=0, tiled=T...]
  transfers between devices with their start and end apart: 6 -> 24, of which waited for: 5 -> 18; matrix products, arithmetic and copies ran while one was open for 2% -> 10% of each run, Pallas kernels for 0% -> 6%
where the time goes in v1:
time: 123 us; the launch traced here: 122 us
  waiting for transfers between devices  38.9 us (32%)
  Pallas kernels  26.3 us (21%)
  starting transfers between devices  26.2 us (21%)
  local copies, waits for them, and re-layouts  17.8 us (14%)
  other arithmetic  11 us (9%)
  between operations  1.72 us (1%)
    ppermute x20, waiting for transfers between devices, swap(): return lax.ppermute(v, AXES, pairs)  33.1 us
    pallas_call x4, Pallas kernels, call(): pl.pallas_call(kernel, out_shape=shapes, in_specs=specs, out_specs=[pl.Bl...  26.3 us
    ppermute x20, starting transfers between devices, swap(): return lax.ppermute(v, AXES, pairs)  18 us
    unnamed x38, local copies, waits for them, and re-layouts  10.4 us
    ppermute x2, starting transfers between devices, along(): return lax.ppermute(value, axis, pairs)  5.2 us
    select_n x9, other arithmetic, sum_over_devices(): jnp.where(bit == 0, jnp.concatenate([value, got], 0), jnp.concatenate([go...  5.04 us
    ppermute x2, waiting for transfers between devices, edge_rows(): got = lax.ppermute(sent, 'grp', [(0, 1), (1, 0)])  3.9 us
    ppermute x2, starting transfers between devices, edge_rows(): got = lax.ppermute(sent, 'grp', [(0, 1), (1, 0)])  3.04 us
  transfers between devices with their start and end apart: 24, of which 18 were waited for; matrix products, arithmetic and copies ran while one was open for 10% of the time, Pallas kernels for 6%

profile of v1, /device:TPU:0, one launch (start us, length us, event | category | flops | bytes accessed | tf_op | source)
XLA Modules:
  0.0 121.9 jit_solution(7775009050295200854)
XLA Ops:
  0.7 1.4 %slice_bitcast_fusion = bf16[14,128,256]{2,1,0:T(8,128)(2,1)S(1)} fusion(bf16[16,16,8,256]{3,2,1,0:T(8,128)(2,1)} %param.6), kind=kLoop, calls=%fused_computation.5 | loop fusion | bytes 1835008 | tf_op jit(solution)/shard_map/slice | solution.py:359
  2.7 3.0 %collective-permute-start = (bf16[112,256]{1,0:T(8,128)(2,1)}, bf16[112,256]{1,0:T(8,128)(2,1)S(1)}, u32[]{:S(2)}, u32[]{:S(2)}) collective-permute-start(bf16[112,256]{1,0:T(8,128)(2,1)} %dynamic-slice_bitcast_fusion), channel_id=1, source_target_pairs={{0,1},{1,0},{2,3},{3,2},{4,5},{5,4},{6,7},{7,6},{8,9},{9,8},{10,11... | collective-permute-start | bytes 172040 | tf_op jit(solution)/shard_map/ppermute | solution.py:336
  5.7 1.3 %collective-permute-start.1 = (bf16[2,32,256]{2,1,0:T(8,128)(2,1)S(1)}, bf16[2,32,256]{2,1,0:T(8,128)(2,1)S(1)}, u32[]{:S(2)}, u32[]{:S(2)}) collective-permute-start(bf16[2,32,256]{2,1,0:T(8,128)(2,1)S(1)} %slice.27), channel_id=1, source_target_pairs={{2,0},{4,2},{6,4},{8,6},{10,8},{12,10},{14,12},{16,14},{18,16},{20... | collective-permute-start | bytes 98312 | tf_op jit(solution)/shard_map/ppermute | solution.py:327
  7.8 1.0 collective-permute-done.1.nxt_ref
  8.8 9.0 %grad_spatial.1 = (bf16[16,8,16,256]{3,2,1,0:T(8,128)(2,1)S(1)}, bf16[18,10,16,256]{3,2,1,0:T(8,128)(2,1)S(1)}, bf16[8,4,16,256]{3,2,1,0:T(8,128)(2,1)S(1)}, bf1...) custom-call(s32[3]{0:T(128)S(1)} %pad_add_fusion.scal, ...), custom_call_target="tpu_custom_call" | custom-call | flops 3758096384 | bytes 8699916 | tf_op jit(solution)/shard_map/grad_spatial/pallas_call | solution.py:264
  17.8 1.0 copy-done.7
  18.8 4.3 %spatial.1 = (bf16[16,8,16,256]{3,2,1,0:T(8,128)(2,1)S(1)}, bf16[8,32,256]{2,1,0:T(8,128)(2,1)S(1)}) custom-call(s32[3]{0:T(128)S(1)} %pad_add_fusion.scal, bf16[18,10,16,256]{3,2,1,0:T(8,128)(2,1)S(1)} %get-tuple-element.16.acts_ref, bf16[9,256,256]{2,1,0:T(8,128)(2,1)S(1)} %bitcast.21), custom_call_target="tpu_custom_call" | custom-call | flops 2415919104 | bytes 3833868 | tf_op jit(solution)/shard_map/spatial/pallas_call | solution.py:264
  23.1 1.0 copy-done.13
  24.1 3.9 %collective-permute-start.2 = (bf16[8,32,256]{2,1,0:T(8,128)(2,1)S(1)}, bf16[8,32,256]{2,1,0:T(8,128)(2,1)S(1)}, u32[]{:S(2)}, u32[]{:S(2)}) collective-permute-start(bf16[8,32,256]{2,1,0:T(8,128)(2,1)S(1)} %get-tuple-element.18), channel_id=1, source_target_pairs={{0,2},{2,4},{4,6},{6,8},{8,10},{10,12},{12,14},{14,16},{16,18},{18... | collective-permute-start | bytes 393224 | tf_op jit(solution)/shard_map/ppermute | solution.py:327
  28.0 0.9 collective-permute-done.2.prev_ref
  29.0 1.2 %copy-done.8 = bf16[16,8,16,256]{3,2,1,0:T(8,128)(2,1)S(1)} copy-done((bf16[16,8,16,256]{3,2,1,0:T(8,128)(2,1)S(1)}, bf16[16,8,16,256]{3,2,1,0:T(8,128)(2,1)}, u32[]{:S(2)}) %copy-start.8) | copy-done | bytes 1048600
  30.2 1.2 %copy-done.11 = bf16[16,8,16,256]{3,2,1,0:T(8,128)(2,1)S(1)} copy-done((bf16[16,8,16,256]{3,2,1,0:T(8,128)(2,1)S(1)}, bf16[16,8,16,256]{3,2,1,0:T(8,128)(2,1)}, u32[]{:S(2)}) %copy-start.11) | copy-done | bytes 1048600
  31.4 1.2 %copy-done.14 = bf16[16,8,16,256]{3,2,1,0:T(8,128)(2,1)S(1)} copy-done((bf16[16,8,16,256]{3,2,1,0:T(8,128)(2,1)S(1)}, bf16[16,8,16,256]{3,2,1,0:T(8,128)(2,1)}, u32[]{:S(2)}) %copy-start.14) | copy-done | bytes 1048600
  32.6 0.9 copy-done.16
  33.6 5.7 %forward.1 = (bf16[16,32,256]{2,1,0:T(8,128)(2,1)S(1)}, bf16[7,256,256]{2,1,0:T(8,128)(2,1)S(1)}) custom-call(s32[3]{0:T(128)S(1)} %pad_add_fusion.scal, bf16[16,8,16,256]{3,2,1,0:T(8,128)(2,1)S(1)} %copy-done.8, bf16[16,8,16,256]{3,2,1,0:T(8,128)(2,1)S(1)} %copy-done.14, bf16[8,32,256]{2,1,0:T(8,128)(2,1)S(1)} %collective-permute-done.2.prev_ref, ...), custom_call_target="tpu_custom_call" | custom-call | flops 2147483648 | bytes 5636108 | tf_op jit(solution)/shard_map/forward/pallas_call | solution.py:264
  40.1 1.0 collective-permute-start.14
  41.9 0.9 collective-permute-done.14
  42.8 1.1 add_convert_fusion.1
  44.0 2.8 %collective-permute-start.15 = (bf16[448,256]{1,0:T(8,128)(2,1)S(1)}, bf16[448,256]{1,0:T(8,128)(2,1)S(1)}, u32[]{:S(2)}, u32[]{:S(2)}) collective-permute-start(bf16[448,256]{1,0:T(8,128)(2,1)S(1)} %constant_dynamic-slice_fusion.3), channel_id=1, source_target_pairs={{0,4},{1,5},{2,10},{3,11},{4,0},{5,1},{6,14},{7,15},{8,12},{9,13},... | collective-permute-start | bytes 688136 | tf_op jit(solution)/shard_map/ppermute | solution.py:298
  46.8 1.2 add_convert_fusion
  48.1 2.7 %collective-permute-done.15 = bf16[448,256]{1,0:T(8,128)(2,1)S(1)} collective-permute-done((bf16[448,256]{1,0:T(8,128)(2,1)S(1)}, bf16[448,256]{1,0:T(8,128)(2,1)S(1)}, u32[]{:S(2)}, u32[]{:S(2)}) %collective-permute-start.15) | collective-permute-done | bytes 229408 | tf_op jit(solution)/shard_map/ppermute | solution.py:298
  51.7 3.2 %collective-permute-done.5 = bf16[576,256]{1,0:T(8,128)(2,1)S(1)} collective-permute-done((bf16[576,256]{1,0:T(8,128)(2,1)S(1)}, bf16[576,256]{1,0:T(8,128)(2,1)S(1)}, u32[]{:S(2)}, u32[]{:S(2)}) %collective-permute-start.5) | collective-permute-done | bytes 294944 | tf_op jit(solution)/shard_map/ppermute | solution.py:298
  55.8 3.6 %collective-permute-start.17 = (bf16[112,256]{1,0:T(8,128)(2,1)S(1)}, bf16[112,256]{1,0:T(8,128)(2,1)S(1)}, u32[]{:S(2)}, u32[]{:S(2)}) collective-permute-start(bf16[112,256]{1,0:T(8,128)(2,1)S(1)} %constant_dynamic-slice_fusion.1), channel_id=1, source_target_pairs={{0,8},{1,9},{2,3},{3,2},{4,12},{5,13},{6,7},{7,6},{8,0},{9,1},{10,... | collective-permute-start | bytes 172040 | tf_op jit(solution)/shard_map/ppermute | solution.py:298
  59.9 1.6 %collective-permute-done.17 = bf16[112,256]{1,0:T(8,128)(2,1)S(1)} collective-permute-done((bf16[112,256]{1,0:T(8,128)(2,1)S(1)}, bf16[112,256]{1,0:T(8,128)(2,1)S(1)}, u32[]{:S(2)}, u32[]{:S(2)}) %collective-permute-start.17) | collective-permute-done | bytes 57376 | tf_op jit(solution)/shard_map/ppermute | solution.py:298
  61.5 3.8 %collective-permute-done.6 = bf16[288,256]{1,0:T(8,128)(2,1)S(1)} collective-permute-done((bf16[288,256]{1,0:T(8,128)(2,1)S(1)}, bf16[288,256]{1,0:T(8,128)(2,1)S(1)}, u32[]{:S(2)}, u32[]{:S(2)}) %collective-permute-start.6) | collective-permute-done | bytes 147488 | tf_op jit(solution)/shard_map/ppermute | solution.py:298
  65.5 2.2 %collective-permute-start.18 = (bf16[56,256]{1,0:T(8,128)(2,1)S(1)}, bf16[56,256]{1,0:T(8,128)(2,1)S(1)}, u32[]{:S(2)}, u32[]{:S(2)}) collective-permute-start(bf16[56,256]{1,0:T(8,128)(2,1)S(1)} %constant_dynamic-slice_fusion), channel_id=1, source_target_pairs={{0,16},{1,17},{2,18},{3,19},{4,20},{5,21},{6,22},{7,23},{8,24},{9,... | collective-permute-start | bytes 86024 | tf_op jit(solution)/shard_map/ppermute | solution.py:298
  67.7 2.4 %collective-permute-done.7 = bf16[144,256]{1,0:T(8,128)(2,1)S(1)} collective-permute-done((bf16[144,256]{1,0:T(8,128)(2,1)S(1)}, bf16[144,256]{1,0:T(8,128)(2,1)S(1)}, u32[]{:S(2)}, u32[]{:S(2)}) %collective-permute-start.7) | collective-permute-done | bytes 73760 | tf_op jit(solution)/shard_map/ppermute | solution.py:298
  70.2 1.9 %collective-permute-start.8 = (bf16[72,256]{1,0:T(8,128)(2,1)S(1)}, bf16[72,256]{1,0:T(8,128)(2,1)S(1)}, u32[]{:S(2)}, u32[]{:S(2)}) collective-permute-start(bf16[72,256]{1,0:T(8,128)(2,1)S(1)} %constant_dynamic-slice_fusion.5), channel_id=1, source_target_pairs={{0,16},{1,17},{2,18},{3,19},{4,20},{5,21},{6,22},{7,23},{8,24},{9,... | collective-permute-start | bytes 110600 | tf_op jit(solution)/shard_map/ppermute | solution.py:298
  72.1 1.1 collective-permute-start.19
  73.2 2.1 %collective-permute-done.8 = bf16[72,256]{1,0:T(8,128)(2,1)S(1)} collective-permute-done((bf16[72,256]{1,0:T(8,128)(2,1)S(1)}, bf16[72,256]{1,0:T(8,128)(2,1)S(1)}, u32[]{:S(2)}, u32[]{:S(2)}) %collective-permute-start.8) | collective-permute-done | bytes 36896 | tf_op jit(solution)/shard_map/ppermute | solution.py:298
  75.4 1.8 %collective-permute-start.9 = (bf16[72,256]{1,0:T(8,128)(2,1)S(1)}, bf16[72,256]{1,0:T(8,128)(2,1)S(1)}, u32[]{:S(2)}, u32[]{:S(2)}) collective-permute-start(bf16[72,256]{1,0:T(8,128)(2,1)S(1)} %add_convert_fusion.8), channel_id=1, source_target_pairs={{0,16},{1,17},{2,18},{3,19},{4,20},{5,21},{6,22},{7,23},{8,24},{9,... | collective-permute-start | bytes 110600 | tf_op jit(solution)/shard_map/ppermute | solution.py:298
  77.6 2.7 %collective-permute-done.9 = bf16[72,256]{1,0:T(8,128)(2,1)S(1)} collective-permute-done((bf16[72,256]{1,0:T(8,128)(2,1)S(1)}, bf16[72,256]{1,0:T(8,128)(2,1)S(1)}, u32[]{:S(2)}, u32[]{:S(2)}) %collective-permute-start.9) | collective-permute-done | bytes 36896 | tf_op jit(solution)/shard_map/ppermute | solution.py:298
  80.4 1.0 collective-permute-done.20
  82.2 3.4 %collective-permute-done.10 = bf16[144,256]{1,0:T(8,128)(2,1)S(1)} collective-permute-done((bf16[144,256]{1,0:T(8,128)(2,1)S(1)}, bf16[144,256]{1,0:T(8,128)(2,1)S(1)}, u32[]{:S(2)}, u32[]{:S(2)}) %collective-permute-start.10) | collective-permute-done | bytes 73760 | tf_op jit(solution)/shard_map/ppermute | solution.py:298
  86.9 4.0 %collective-permute-done.11 = bf16[288,256]{1,0:T(8,128)(2,1)S(1)} collective-permute-done((bf16[288,256]{1,0:T(8,128)(2,1)S(1)}, bf16[288,256]{1,0:T(8,128)(2,1)S(1)}, u32[]{:S(2)}, u32[]{:S(2)}) %collective-permute-start.11) | collective-permute-done | bytes 147488 | tf_op jit(solution)/shard_map/ppermute | solution.py:298
  92.6 2.0 %maximum_select_fusion.3 = bf16[896,256]{1,0:T(8,128)(2,1)} fusion(bf16[448,256]{1,0:T(8,128)(2,1)} %collective-permute-done.22, bf16[448,256]{1,0:T(8,128)(2,1)S(1)} %maximum_select_fusion.5, pred[]{:T(512)S(6)} %eq.14), kind=kLoop, calls=%fused_computation.8 | loop fusion | flops 2064384 | bytes 917505 | tf_op jit(solution)/shard_map/jit(_where)/select_n | solution.py:318
  94.5 3.3 %collective-permute-done.12 = bf16[576,256]{1,0:T(8,128)(2,1)} collective-permute-done((bf16[576,256]{1,0:T(8,128)(2,1)S(1)}, bf16[576,256]{1,0:T(8,128)(2,1)}, u32[]{:S(2)}, u32[]{:S(2)}) %collective-permute-start.12) | collective-permute-done | bytes 294944 | tf_op jit(solution)/shard_map/ppermute | solution.py:298
  97.9 1.3 %maximum_select_fusion.2 = bf16[1152,256]{1,0:T(8,128)(2,1)S(1)} fusion(bf16[576,256]{1,0:T(8,128)(2,1)} %collective-permute-done.12, bf16[576,256]{1,0:T(8,128)(2,1)S(1)} %maximum_select_fusion.4, pred[]{:T(512)S(6)} %eq.14), kind=kLoop, calls=%fused_computation.6 | loop fusion | flops 2654208 | bytes 1179649 | tf_op jit(solution)/shard_map/jit(_where)/select_n | solution.py:318
  99.4 3.9 %collective-permute-done.3.top_ref.bot_ref = bf16[64,256]{1,0:T(8,128)(2,1)S(1)} collective-permute-done((bf16[64,256]{1,0:T(8,128)(2,1)S(1)}, bf16[64,256]{1,0:T(8,128)(2,1)S(1)}, u32[]{:S(2)}, u32[]{:S(2)}) %collective-permute-start.3) | collective-permute-done | bytes 32800 | tf_op jit(solution)/shard_map/ppermute | solution.py:336
  103.3 1.3 %copy-done.6 = bf16[16,10,16,256]{3,2,1,0:T(8,128)(2,1)S(1)} copy-done((bf16[16,10,16,256]{3,2,1,0:T(8,128)(2,1)S(1)}, bf16[16,10,16,256]{3,2,1,0:T(8,128)(2,1)}, u32[]{:S(2)}) %copy-start.6) | copy-done | bytes 1310744
  104.6 1.2 %copy-done.9 = bf16[16,8,16,256]{3,2,1,0:T(8,128)(2,1)S(1)} copy-done((bf16[16,8,16,256]{3,2,1,0:T(8,128)(2,1)S(1)}, bf16[16,8,16,256]{3,2,1,0:T(8,128)(2,1)}, u32[]{:S(2)}) %copy-start.9) | copy-done | bytes 1048600
  105.8 1.2 %copy-done.12 = bf16[16,8,16,256]{3,2,1,0:T(8,128)(2,1)S(1)} copy-done((bf16[16,8,16,256]{3,2,1,0:T(8,128)(2,1)S(1)}, bf16[16,8,16,256]{3,2,1,0:T(8,128)(2,1)}, u32[]{:S(2)}) %copy-start.12) | copy-done | bytes 1048600
  107.0 7.4 %grad_x.1 = bf16[16,128,256]{2,1,0:T(8,128)(2,1)} custom-call(s32[3]{0:T(128)S(1)} %pad_add_fusion.scal, bf16[16,8,16,256]{3,2,1,0:T(8,128)(2,1)S(1)} %copy-done.9, bf16[16,8,16,256]{3,2,1,0:T(8,128)(2,1)S(1)} %copy-done.12, bf16[16,10,16,256]{3,2,1,0:T(8,128)(2,1)S(1)} %copy-done.6, bf16[64,256]{1,0:T(8,128)(2,1)S(1)} %collective-permute-done.3.top_ref.bot_ref, ...), custom_call_target="tpu_custom_call" | custom-call | flops 2684354560 | bytes 6619148 | tf_op jit(solution)/shard_map/grad_x/pallas_call | solution.py:264
  115.2 1.6 %fusion = f32[1792,256]{1,0:T(8,128)S(1)} fusion(bf16[896,256]{1,0:T(8,128)(2,1)} %collective-permute-done.23, bf16[896,256]{1,0:T(8,128)(2,1)} %maximum_select_fusion.3, pred[]{:T(512)S(6)} %eq.13), kind=kLoop, calls=%fused_computation.3 | loop fusion | flops 4587520 | bytes 2752513 | tf_op jit(solution)/shard_map/convert_element_type | solution.py:394
  116.8 0.9 slice.32
  117.7 1.0 slice.33
  118.8 1.5 %maximum_select_fusion = bf16[2304,256]{1,0:T(8,128)(2,1)S(1)} fusion(bf16[1152,256]{1,0:T(8,128)(2,1)} %collective-permute-done.13, bf16[1152,256]{1,0:T(8,128)(2,1)S(1)} %maximum_select_fusion.2, pred[]{:T(512)S(6)} %eq.13), kind=kLoop, calls=%fused_computation | loop fusion | flops 5308416 | bytes 2359297 | tf_op jit(solution)/shard_map/jit(_where)/select_n | solution.py:318
  120.3 1.6 %convert.3 = f32[3,3,256,256]{3,2,1,0:T(8,128)} convert(bf16[3,3,256,256]{3,2,1,0:T(8,128)(2,1)S(1)} %bitcast.26) | non-fusion elementwise | flops 589824 | bytes 3538944 | tf_op jit(solution)/shard_map/convert_element_type | solution.py:398
  (88 shorter events, 10.5 us)
Async XLA Ops:
  0.6 5.1 %slice-start = ((bf16[16,8,4,256]{3,2,1,0:T(4,128)(2,1)}), bf16[2,8,4,256]{3,2,1,0:T(4,128)(2,1)S(1)}, s32[]{:S(2)}) async-start(bf16[16,8,4,256]{3,2,1,0:T(4,128)(2,1)} %param.11), calls=%async_computation | async-start | bytes 65536 | tf_op jit(solution)/shard_map/slice | solution.py:358
  0.6 7.1 %copy-start.17 = (bf16[16,8,4,256]{3,2,1,0:T(4,128)(2,1)S(1)}, bf16[16,8,4,256]{3,2,1,0:T(4,128)(2,1)}, u32[]{:S(2)}) copy-start(bf16[16,8,4,256]{3,2,1,0:T(4,128)(2,1)} %param.11) | copy-start | bytes 786436
  0.7 8.2 %copy-start = (bf16[16,16,8,256]{3,2,1,0:T(8,128)(2,1)S(1)}, bf16[16,16,8,256]{3,2,1,0:T(8,128)(2,1)}, u32[]{:S(2)}) copy-start(bf16[16,16,8,256]{3,2,1,0:T(8,128)(2,1)} %param.6) | copy-start | bytes 3145732
  0.7 8.2 %copy-start.3 = (bf16[2,2,256,256]{3,2,1,0:T(8,128)(2,1)S(1)}, bf16[2,2,256,256]{3,2,1,0:T(8,128)(2,1)}, u32[]{:S(2)}) copy-start(bf16[2,2,256,256]{3,2,1,0:T(8,128)(2,1)} %param.10) | copy-start | bytes 1572868
  0.7 8.1 %copy-start.4 = (bf16[3,256,256]{2,1,0:T(8,128)(2,1)S(1)}, bf16[3,256,256]{2,1,0:T(8,128)(2,1)}, u32[]{:S(2)}) copy-start(bf16[3,256,256]{2,1,0:T(8,128)(2,1)} %wt_ref.5) | copy-start | bytes 1179652
  2.7 6.1 %collective-permute-start = (bf16[112,256]{1,0:T(8,128)(2,1)}, bf16[112,256]{1,0:T(8,128)(2,1)S(1)}, u32[]{:S(2)}, u32[]{:S(2)}) collective-permute-start(bf16[112,256]{1,0:T(8,128)(2,1)} %dynamic-slice_bitcast_fusion), channel_id=1, source_target_pairs={{0,1},{1,0},{2,3},{3,2},{4,5},{5,4},{6,7},{7,6},{8,9},{9,8},{10,11... | collective-permute-start | bytes 172040 | tf_op jit(solution)/shard_map/ppermute | solution.py:336
  5.7 3.1 %collective-permute-start.1 = (bf16[2,32,256]{2,1,0:T(8,128)(2,1)S(1)}, bf16[2,32,256]{2,1,0:T(8,128)(2,1)S(1)}, u32[]{:S(2)}, u32[]{:S(2)}) collective-permute-start(bf16[2,32,256]{2,1,0:T(8,128)(2,1)S(1)} %slice.27), channel_id=1, source_target_pairs={{2,0},{4,2},{6,4},{8,6},{10,8},{12,10},{14,12},{16,14},{18,16},{20... | collective-permute-start | bytes 98312 | tf_op jit(solution)/shard_map/ppermute | solution.py:327
  8.8 10.0 %copy-start.1 = (bf16[3,3,256,256]{3,2,1,0:T(8,128)(2,1)S(1)}, bf16[3,3,256,256]{3,2,1,0:T(8,128)(2,1)}, u32[]{:S(2)}) copy-start(bf16[3,3,256,256]{3,2,1,0:T(8,128)(2,1)} %param.8) | copy-start | bytes 3538948
  17.8 1.0 copy-start.7
  18.8 4.3 %copy-start.5 = (bf16[16,10,16,256]{3,2,1,0:T(8,128)(2,1)}, bf16[16,10,16,256]{3,2,1,0:T(8,128)(2,1)S(1)}, u32[]{:S(2)}) copy-start(bf16[16,10,16,256]{3,2,1,0:T(8,128)(2,1)S(1)} %get-tuple-element.22.gs_ref) | copy-start | bytes 3932164
  18.8 4.3 %copy-start.10 = (bf16[16,8,16,256]{3,2,1,0:T(8,128)(2,1)}, bf16[16,8,16,256]{3,2,1,0:T(8,128)(2,1)S(1)}, u32[]{:S(2)}) copy-start(bf16[16,8,16,256]{3,2,1,0:T(8,128)(2,1)S(1)} %get-tuple-element.20.gy_ref) | copy-start | bytes 3145732
  18.8 4.3 %copy-start.15 = (bf16[8,4,16,256]{3,2,1,0:T(8,128)(2,1)}, bf16[8,4,16,256]{3,2,1,0:T(8,128)(2,1)S(1)}, u32[]{:S(2)}) copy-start(bf16[8,4,16,256]{3,2,1,0:T(8,128)(2,1)S(1)} %get-tuple-element.19.cott_ref) | copy-start | bytes 786436
  23.1 1.0 copy-start.13
  24.1 4.9 %collective-permute-start.2 = (bf16[8,32,256]{2,1,0:T(8,128)(2,1)S(1)}, bf16[8,32,256]{2,1,0:T(8,128)(2,1)S(1)}, u32[]{:S(2)}, u32[]{:S(2)}) collective-permute-start(bf16[8,32,256]{2,1,0:T(8,128)(2,1)S(1)} %get-tuple-element.18), channel_id=1, source_target_pairs={{0,2},{2,4},{4,6},{6,8},{8,10},{10,12},{12,14},{14,16},{16,18},{18... | collective-permute-start | bytes 393224 | tf_op jit(solution)/shard_map/ppermute | solution.py:327
  29.0 1.2 %copy-start.8 = (bf16[16,8,16,256]{3,2,1,0:T(8,128)(2,1)S(1)}, bf16[16,8,16,256]{3,2,1,0:T(8,128)(2,1)}, u32[]{:S(2)}) copy-start(bf16[16,8,16,256]{3,2,1,0:T(8,128)(2,1)} %copy-done.7) | copy-start | bytes 3145732
  30.2 1.2 %copy-start.11 = (bf16[16,8,16,256]{3,2,1,0:T(8,128)(2,1)S(1)}, bf16[16,8,16,256]{3,2,1,0:T(8,128)(2,1)}, u32[]{:S(2)}) copy-start(bf16[16,8,16,256]{3,2,1,0:T(8,128)(2,1)} %copy-done.10) | copy-start | bytes 3145732
  31.4 1.2 %copy-start.14 = (bf16[16,8,16,256]{3,2,1,0:T(8,128)(2,1)S(1)}, bf16[16,8,16,256]{3,2,1,0:T(8,128)(2,1)}, u32[]{:S(2)}) copy-start(bf16[16,8,16,256]{3,2,1,0:T(8,128)(2,1)} %copy-done.13) | copy-start | bytes 3145732
  32.6 0.9 copy-start.16
  40.1 2.8 %collective-permute-start.14 = (bf16[896,256]{1,0:T(8,128)(2,1)}, bf16[896,256]{1,0:T(8,128)(2,1)}, u32[]{:S(2)}, u32[]{:S(2)}) collective-permute-start(bf16[896,256]{1,0:T(8,128)(2,1)} %constant_dynamic-slice_fusion.4), channel_id=1, source_target_pairs={{0,2},{1,3},{2,0},{3,1},{4,6},{5,7},{6,4},{7,5},{8,10},{9,11},{10,... | collective-permute-start | bytes 1376264 | tf_op jit(solution)/shard_map/ppermute | solution.py:298
  41.9 4.9 %collective-permute-start.4 = (bf16[1152,256]{1,0:T(8,128)(2,1)}, bf16[1152,256]{1,0:T(8,128)(2,1)}, u32[]{:S(2)}, u32[]{:S(2)}) collective-permute-start(bf16[1152,256]{1,0:T(8,128)(2,1)} %constant_dynamic-slice_fusion.9), channel_id=1, source_target_pairs={{0,2},{1,3},{2,0},{3,1},{4,6},{5,7},{6,4},{7,5},{8,10},{9,11},{10,... | collective-permute-start | bytes 1769480 | tf_op jit(solution)/shard_map/ppermute | solution.py:298
  44.0 6.8 %collective-permute-start.15 = (bf16[448,256]{1,0:T(8,128)(2,1)S(1)}, bf16[448,256]{1,0:T(8,128)(2,1)S(1)}, u32[]{:S(2)}, u32[]{:S(2)}) collective-permute-start(bf16[448,256]{1,0:T(8,128)(2,1)S(1)} %constant_dynamic-slice_fusion.3), channel_id=1, source_target_pairs={{0,4},{1,5},{2,10},{3,11},{4,0},{5,1},{6,14},{7,15},{8,12},{9,13},... | collective-permute-start | bytes 688136 | tf_op jit(solution)/shard_map/ppermute | solution.py:298
  48.0 7.0 %collective-permute-start.5 = (bf16[576,256]{1,0:T(8,128)(2,1)S(1)}, bf16[576,256]{1,0:T(8,128)(2,1)S(1)}, u32[]{:S(2)}, u32[]{:S(2)}) collective-permute-start(bf16[576,256]{1,0:T(8,128)(2,1)S(1)} %constant_dynamic-slice_fusion.8), channel_id=1, source_target_pairs={{0,4},{1,5},{2,10},{3,11},{4,0},{5,1},{6,14},{7,15},{8,12},{9,13},... | collective-permute-start | bytes 884744 | tf_op jit(solution)/shard_map/ppermute | solution.py:298
  50.8 4.9 %collective-permute-start.16 = (bf16[224,256]{1,0:T(8,128)(2,1)S(1)}, bf16[224,256]{1,0:T(8,128)(2,1)S(1)}, u32[]{:S(2)}, u32[]{:S(2)}) collective-permute-start(bf16[224,256]{1,0:T(8,128)(2,1)S(1)} %constant_dynamic-slice_fusion.2), channel_id=1, source_target_pairs={{0,1},{1,0},{2,6},{3,7},{4,5},{5,4},{6,2},{7,3},{8,9},{9,8},{10,14... | collective-permute-start | bytes 344072 | tf_op jit(solution)/shard_map/ppermute | solution.py:298
  55.8 5.7 %collective-permute-start.17 = (bf16[112,256]{1,0:T(8,128)(2,1)S(1)}, bf16[112,256]{1,0:T(8,128)(2,1)S(1)}, u32[]{:S(2)}, u32[]{:S(2)}) collective-permute-start(bf16[112,256]{1,0:T(8,128)(2,1)S(1)} %constant_dynamic-slice_fusion.1), channel_id=1, source_target_pairs={{0,8},{1,9},{2,3},{3,2},{4,12},{5,13},{6,7},{7,6},{8,0},{9,1},{10,... | collective-permute-start | bytes 172040 | tf_op jit(solution)/shard_map/ppermute | solution.py:298
  59.3 6.0 %collective-permute-start.6 = (bf16[288,256]{1,0:T(8,128)(2,1)S(1)}, bf16[288,256]{1,0:T(8,128)(2,1)S(1)}, u32[]{:S(2)}, u32[]{:S(2)}) collective-permute-start(bf16[288,256]{1,0:T(8,128)(2,1)S(1)} %constant_dynamic-slice_fusion.7), channel_id=1, source_target_pairs={{0,1},{1,0},{2,6},{3,7},{4,5},{5,4},{6,2},{7,3},{8,9},{9,8},{10,14... | collective-permute-start | bytes 442376 | tf_op jit(solution)/shard_map/ppermute | solution.py:298
  65.4 4.7 %collective-permute-start.7 = (bf16[144,256]{1,0:T(8,128)(2,1)S(1)}, bf16[144,256]{1,0:T(8,128)(2,1)S(1)}, u32[]{:S(2)}, u32[]{:S(2)}) collective-permute-start(bf16[144,256]{1,0:T(8,128)(2,1)S(1)} %constant_dynamic-slice_fusion.6), channel_id=1, source_target_pairs={{0,8},{1,9},{2,3},{3,2},{4,12},{5,13},{6,7},{7,6},{8,0},{9,1},{10,... | collective-permute-start | bytes 221192 | tf_op jit(solution)/shard_map/ppermute | solution.py:298
  65.5 6.6 %collective-permute-start.18 = (bf16[56,256]{1,0:T(8,128)(2,1)S(1)}, bf16[56,256]{1,0:T(8,128)(2,1)S(1)}, u32[]{:S(2)}, u32[]{:S(2)}) collective-permute-start(bf16[56,256]{1,0:T(8,128)(2,1)S(1)} %constant_dynamic-slice_fusion), channel_id=1, source_target_pairs={{0,16},{1,17},{2,18},{3,19},{4,20},{5,21},{6,22},{7,23},{8,24},{9,... | collective-permute-start | bytes 86024 | tf_op jit(solution)/shard_map/ppermute | solution.py:298
  70.2 5.2 %collective-permute-start.8 = (bf16[72,256]{1,0:T(8,128)(2,1)S(1)}, bf16[72,256]{1,0:T(8,128)(2,1)S(1)}, u32[]{:S(2)}, u32[]{:S(2)}) collective-permute-start(bf16[72,256]{1,0:T(8,128)(2,1)S(1)} %constant_dynamic-slice_fusion.5), channel_id=1, source_target_pairs={{0,16},{1,17},{2,18},{3,19},{4,20},{5,21},{6,22},{7,23},{8,24},{9,... | collective-permute-start | bytes 110600 | tf_op jit(solution)/shard_map/ppermute | solution.py:298
  72.1 18.9 %slice-start.1 = ((bf16[16,8,4,256]{3,2,1,0:T(4,128)(2,1)}), bf16[14,8,4,256]{3,2,1,0:T(4,128)(2,1)S(1)}, s32[]{:S(2)}) async-start(bf16[16,8,4,256]{3,2,1,0:T(4,128)(2,1)} %param.11), calls=%async_computation.1 | async-start | bytes 458752 | tf_op jit(solution)/shard_map/slice | solution.py:360
  72.1 5.0 %collective-permute-start.19 = (bf16[56,256]{1,0:T(8,128)(2,1)S(1)}, bf16[56,256]{1,0:T(8,128)(2,1)S(1)}, u32[]{:S(2)}, u32[]{:S(2)}) collective-permute-start(bf16[56,256]{1,0:T(8,128)(2,1)S(1)} %add_convert_fusion.9), channel_id=1, source_target_pairs={{0,16},{1,17},{2,18},{3,19},{4,20},{5,21},{6,22},{7,23},{8,24},{9,... | collective-permute-start | bytes 86024 | tf_op jit(solution)/shard_map/ppermute | solution.py:298
  75.4 4.9 %collective-permute-start.9 = (bf16[72,256]{1,0:T(8,128)(2,1)S(1)}, bf16[72,256]{1,0:T(8,128)(2,1)S(1)}, u32[]{:S(2)}, u32[]{:S(2)}) collective-permute-start(bf16[72,256]{1,0:T(8,128)(2,1)S(1)} %add_convert_fusion.8), channel_id=1, source_target_pairs={{0,16},{1,17},{2,18},{3,19},{4,20},{5,21},{6,22},{7,23},{8,24},{9,... | collective-permute-start | bytes 110600 | tf_op jit(solution)/shard_map/ppermute | solution.py:298
  77.2 4.2 %collective-permute-start.20 = (bf16[112,256]{1,0:T(8,128)(2,1)S(1)}, bf16[112,256]{1,0:T(8,128)(2,1)S(1)}, u32[]{:S(2)}, u32[]{:S(2)}) collective-permute-start(bf16[112,256]{1,0:T(8,128)(2,1)S(1)} %maximum_select_fusion.9), channel_id=1, source_target_pairs={{0,8},{1,9},{2,3},{3,2},{4,12},{5,13},{6,7},{7,6},{8,0},{9,1},{10,... | collective-permute-start | bytes 172040 | tf_op jit(solution)/shard_map/ppermute | solution.py:298
  80.3 5.3 %collective-permute-start.10 = (bf16[144,256]{1,0:T(8,128)(2,1)S(1)}, bf16[144,256]{1,0:T(8,128)(2,1)S(1)}, u32[]{:S(2)}, u32[]{:S(2)}) collective-permute-start(bf16[144,256]{1,0:T(8,128)(2,1)S(1)} %maximum_select_fusion.8), channel_id=1, source_target_pairs={{0,8},{1,9},{2,3},{3,2},{4,12},{5,13},{6,7},{7,6},{8,0},{9,1},{10,... | collective-permute-start | bytes 221192 | tf_op jit(solution)/shard_map/ppermute | solution.py:298
  81.4 4.9 %collective-permute-start.21 = (bf16[224,256]{1,0:T(8,128)(2,1)S(1)}, bf16[224,256]{1,0:T(8,128)(2,1)S(1)}, u32[]{:S(2)}, u32[]{:S(2)}) collective-permute-start(bf16[224,256]{1,0:T(8,128)(2,1)S(1)} %maximum_select_fusion.7), channel_id=1, source_target_pairs={{0,1},{1,0},{2,6},{3,7},{4,5},{5,4},{6,2},{7,3},{8,9},{9,8},{10,14... | collective-permute-start | bytes 344072 | tf_op jit(solution)/shard_map/ppermute | solution.py:298
  85.6 5.2 %collective-permute-start.11 = (bf16[288,256]{1,0:T(8,128)(2,1)S(1)}, bf16[288,256]{1,0:T(8,128)(2,1)S(1)}, u32[]{:S(2)}, u32[]{:S(2)}) collective-permute-start(bf16[288,256]{1,0:T(8,128)(2,1)S(1)} %maximum_select_fusion.6), channel_id=1, source_target_pairs={{0,1},{1,0},{2,6},{3,7},{4,5},{5,4},{6,2},{7,3},{8,9},{9,8},{10,14... | collective-permute-start | bytes 442376 | tf_op jit(solution)/shard_map/ppermute | solution.py:298
  86.4 6.2 %collective-permute-start.22 = (bf16[448,256]{1,0:T(8,128)(2,1)S(1)}, bf16[448,256]{1,0:T(8,128)(2,1)}, u32[]{:S(2)}, u32[]{:S(2)}) collective-permute-start(bf16[448,256]{1,0:T(8,128)(2,1)S(1)} %maximum_select_fusion.5), channel_id=1, source_target_pairs={{0,4},{1,5},{2,10},{3,11},{4,0},{5,1},{6,14},{7,15},{8,12},{9,13},... | collective-permute-start | bytes 688136 | tf_op jit(solution)/shard_map/ppermute | solution.py:298
  91.0 6.9 %collective-permute-start.12 = (bf16[576,256]{1,0:T(8,128)(2,1)S(1)}, bf16[576,256]{1,0:T(8,128)(2,1)}, u32[]{:S(2)}, u32[]{:S(2)}) collective-permute-start(bf16[576,256]{1,0:T(8,128)(2,1)S(1)} %maximum_select_fusion.4), channel_id=1, source_target_pairs={{0,4},{1,5},{2,10},{3,11},{4,0},{5,1},{6,14},{7,15},{8,12},{9,13},... | collective-permute-start | bytes 884744 | tf_op jit(solution)/shard_map/ppermute | solution.py:298
  91.8 7.4 %copy-start.18 = (bf16[14,32,256]{2,1,0:T(8,128)(2,1)S(1)}, bf16[14,32,256]{2,1,0:T(8,128)(2,1)}, u32[]{:S(2)}) copy-start(bf16[14,32,256]{2,1,0:T(8,128)(2,1)} %slice.29) | copy-start | bytes 688132
  91.8 11.5 %copy-start.2 = (bf16[3,3,256,256]{3,2,1,0:T(8,128)(2,1)S(1)}, bf16[3,3,256,256]{3,2,1,0:T(8,128)(2,1)}, u32[]{:S(2)}) copy-start(bf16[3,3,256,256]{3,2,1,0:T(8,128)(2,1)} %param.8) | copy-start | bytes 3538948
  94.5 20.7 %collective-permute-start.23 = (bf16[896,256]{1,0:T(8,128)(2,1)}, bf16[896,256]{1,0:T(8,128)(2,1)}, u32[]{:S(2)}, u32[]{:S(2)}) collective-permute-start(bf16[896,256]{1,0:T(8,128)(2,1)} %maximum_select_fusion.3), channel_id=1, source_target_pairs={{0,2},{1,3},{2,0},{3,1},{4,6},{5,7},{6,4},{7,5},{8,10},{9,11},{10,... | collective-permute-start | bytes 1376264 | tf_op jit(solution)/shard_map/ppermute | solution.py:298
  99.1 19.6 %collective-permute-start.13 = (bf16[1152,256]{1,0:T(8,128)(2,1)S(1)}, bf16[1152,256]{1,0:T(8,128)(2,1)}, u32[]{:S(2)}, u32[]{:S(2)}) collective-permute-start(bf16[1152,256]{1,0:T(8,128)(2,1)S(1)} %maximum_select_fusion.2), channel_id=1, source_target_pairs={{0,2},{1,3},{2,0},{3,1},{4,6},{5,7},{6,4},{7,5},{8,10},{9,11},{10,... | collective-permute-start | bytes 1769480 | tf_op jit(solution)/shard_map/ppermute | solution.py:298
  99.3 4.0 %collective-permute-start.3 = (bf16[64,256]{1,0:T(8,128)(2,1)S(1)}, bf16[64,256]{1,0:T(8,128)(2,1)S(1)}, u32[]{:S(2)}, u32[]{:S(2)}) collective-permute-start(bf16[64,256]{1,0:T(8,128)(2,1)S(1)} %reshape.62), channel_id=1, source_target_pairs={{0,1},{1,0},{2,3},{3,2},{4,5},{5,4},{6,7},{7,6},{8,9},{9,8},{10,11... | collective-permute-start | bytes 98312 | tf_op jit(solution)/shard_map/ppermute | solution.py:336
  103.3 1.3 %copy-start.6 = (bf16[16,10,16,256]{3,2,1,0:T(8,128)(2,1)S(1)}, bf16[16,10,16,256]{3,2,1,0:T(8,128)(2,1)}, u32[]{:S(2)}) copy-start(bf16[16,10,16,256]{3,2,1,0:T(8,128)(2,1)} %copy-done.5) | copy-start | bytes 3932164
  104.6 1.2 %copy-start.9 = (bf16[16,8,16,256]{3,2,1,0:T(8,128)(2,1)S(1)}, bf16[16,8,16,256]{3,2,1,0:T(8,128)(2,1)}, u32[]{:S(2)}) copy-start(bf16[16,8,16,256]{3,2,1,0:T(8,128)(2,1)} %copy-done.7) | copy-start | bytes 3145732
  105.8 1.2 %copy-start.12 = (bf16[16,8,16,256]{3,2,1,0:T(8,128)(2,1)S(1)}, bf16[16,8,16,256]{3,2,1,0:T(8,128)(2,1)}, u32[]{:S(2)}) copy-start(bf16[16,8,16,256]{3,2,1,0:T(8,128)(2,1)} %copy-done.10) | copy-start | bytes 3145732

commit v2 on v1

--- a/solution.py
+++ b/solution.py
@@ -267,7 +267,7 @@
         in_specs=specs,
         out_specs=[pl.BlockSpec(memory_space=pltpu.VMEM) for _ in outs],
         scratch_shapes=[pltpu.VMEM(s, BF) for s in scratch],
-        compiler_params=pltpu.CompilerParams(vmem_limit_bytes=32 * 2**20),
+        compiler_params=pltpu.CompilerParams(vmem_limit_bytes=10 * 2**20),
         cost_estimate=pl.CostEstimate(flops=flops, bytes_accessed=moved, transcendentals=0),
         name=name,
     )(*args)
@@ -287,37 +287,31 @@
     return core, [(core, core)] + list(zip(first, second))
 
 
-def sum_over_devices(value, tm, grp):
+def scatter_sum(value, tm, grp):
     total = tm * grp
     core, stages = exchange_plan(tm, grp)
     me = lax.axis_index("tm") * grp + lax.axis_index("grp")
     odd = (me >> core) & 1
-
-    def swap(v, stage):
+    bits = len(stages)
+    value = value.reshape((2,) * bits + (value.shape[0] // total, value.shape[1]))
+    left = [list(reversed(range(bits)))] * 2
+
+    for stage in stages:
         pairs = [(d, d ^ (1 << stage[(d >> core) & 1])) for d in range(total)]
-        return lax.ppermute(v, AXES, pairs)
-
-    def bit_of(stage):
-        return jnp.where(odd == 0, (me >> stage[0]) & 1, (me >> stage[1]) & 1)
-
-    halved = []
-    for stage in stages:
-        rows = value.shape[0]
-        if rows % 16 == 0 and rows > 16:
-            half = rows // 2
-            bit = bit_of(stage)
-            keep = lax.dynamic_slice_in_dim(value, bit * half, half, 0)
-            send = lax.dynamic_slice_in_dim(value, (1 - bit) * half, half, 0)
-            got = swap(send, stage)
-            value = (keep.astype(F32) + got.astype(F32)).astype(BF)
-            halved.append((stage, bit))
-        else:
-            value = (value.astype(F32) + swap(value, stage).astype(F32)).astype(BF)
-    for stage, bit in reversed(halved):
-        got = swap(value, stage)
-        value = jnp.where(
-            bit == 0, jnp.concatenate([value, got], 0), jnp.concatenate([got, value], 0)
-        )
+        where = [left[c].index(stage[c]) for c in range(2)]
+
+        def half(flip):
+            parts = [
+                lax.dynamic_index_in_dim(
+                    value, ((me >> stage[c]) & 1) ^ flip, where[c], keepdims=False
+                )
+                for c in range(2)
+            ]
+            return parts[0] if stage[0] == stage[1] else jnp.where(odd == 0, parts[0], parts[1])
+
+        got = lax.ppermute(half(1), AXES, pairs)
+        value = (half(0).astype(F32) + got.astype(F32)).astype(BF)
+        left = [[b for b in left[c] if b != stage[c]] for c in range(2)]
     return value
 
 
@@ -370,7 +364,7 @@
         14 * tap,
         scal, x, top, bot, cot, nxt, w_temporal, wd,
     )
-    sum_s = sum_over_devices(gw_s.reshape(9 * ch, ch), tm, grp)
+    sum_s = lax.psum(gw_s.reshape(9 * ch, ch), AXES)
     sp, edge = call(
         spatial_kernel, [tile, (rows // 2, 32, ch)], [], "spatial", 9 * tap, scal, acts, ws
     )
@@ -391,7 +385,8 @@
         8 * tap,
         scal, xt, sp, prev, cott, gy, w_temporal, wd,
     )
-    sum_t = sum_over_devices(gw_t.reshape(7 * ch, ch), tm, grp).astype(F32)
+    part = scatter_sum(gw_t.reshape(7 * ch, ch), tm, grp)
+    sum_t = lax.all_gather(part, AXES, axis=0, tiled=True).astype(F32)
     return (
         down.reshape(cotangent.shape),
         grad_x.reshape(frames_in.shape),

time: 123 us -> 283 us (2.30)
  waiting for transfers between devices: 38.9 us -> 127 us
  blocking collectives: 0 us -> 70 us
  between operations: 1.72 us -> 14.9 us
  starting transfers between devices: 26.2 us -> 20.4 us
  other arithmetic: 11 us -> 7.22 us
    psum x0 -> x1, waiting for transfers between devices: none -> 114 us  [body(): sum_s = lax.psum(gw_s.reshape(9 * ch, ch), AXES)]
    all_gather x0 -> x1, blocking collectives: none -> 70 us  [body(): sum_t = lax.all_gather(part, AXES, axis=0, tiled=True).astype(F32)]
    ppermute x20 -> x5, waiting for transfers between devices: 33.1 us -> 11.2 us  [scatter_sum(): got = lax.ppermute(half(1), AXES, pairs)]
    ppermute x20 -> x5, starting transfers between devices: 18 us -> 11.7 us  [scatter_sum(): got = lax.ppermute(half(1), AXES, pairs)]
    select_n x9 -> x3, other arithmetic: 5.04 us -> 1.11 us  [half(): jnp.where(odd == 0, parts[0], parts[1])]
    ppermute x2, waiting for transfers between devices: 3.9 us -> 0.01 us  [edge_rows(): got = lax.ppermute(sent, 'grp', [(0, 1), (1, 0)])]
    reshape x0 -> x1, other arithmetic: none -> 2.9 us  [body(): sum_s.astype(F32).reshape(w_spatial.shape)]
    convert_element_type x12 -> x5, other arithmetic: 5.87 us -> 3.11 us  [scatter_sum(): value = (half(0).astype(F32) + got.astype(F32)).astype(BF)]
  transfers between devices with their start and end apart: 24 -> 10, of which waited for: 18 -> 7; matrix products, arithmetic and copies ran while one was open for 10% -> 1% of each run, Pallas kernels for 6% -> 3%
where the time goes in v2:
time: 283 us
  waiting for transfers between devices  127 us (45%)
  blocking collectives  70 us (25%)
  Pallas kernels  27.3 us (10%)
  starting transfers between devices  20.4 us (7%)
  local copies, waits for them, and re-layouts  16.2 us (6%)
  between operations  14.9 us (5%)
  other arithmetic  7.22 us (3%)
    psum x1, waiting for transfers between devices, body(): sum_s = lax.psum(gw_s.reshape(9 * ch, ch), AXES)  114 us
    all_gather x1, blocking collectives, body(): sum_t = lax.all_gather(part, AXES, axis=0, tiled=True).astype(F32)  70 us
    pallas_call x4, Pallas kernels, call(): pl.pallas_call(kernel, out_shape=shapes, in_specs=specs, out_specs=[pl.Bl...  27.3 us
    ppermute x5, starting transfers between devices, scatter_sum(): got = lax.ppermute(half(1), AXES, pairs)  11.7 us
    ppermute x5, waiting for transfers between devices, scatter_sum(): got = lax.ppermute(half(1), AXES, pairs)  11.2 us
    unnamed x34, local copies, waits for them, and re-layouts  10.4 us
  transfers between devices with their start and end apart: 10, of which 7 were waited for; matrix products, arithmetic and copies ran while one was open for 1% of the time, Pallas kernels for 3%

profile of v2, /device:TPU:0, one launch (start us, length us, event | category | flops | bytes accessed | tf_op | source)
XLA Modules:
  0.0 282.8 jit_solution(1079758767654766652)
XLA Ops:
  7.2 0.0 slice-start
  7.2 0.0 all-reduce.2.cloned.1.call-start
  7.3 1.4 slice_bitcast_fusion
  8.7 0.6 dynamic-slice_bitcast_fusion.1
  9.3 3.0 %collective-permute-start = (bf16[112,256]{1,0:T(8,128)(2,1)}, bf16[112,256]{1,0:T(8,128)(2,1)S(1)}, u32[]{:S(2)}, u32[]{:S(2)}) collective-permute-start(bf16[112,256]{1,0:T(8,128)(2,1)} %dynamic-slice_bitcast_fusion.1), channel_id=1, source_target_pairs={{0,1},{1,0},{2,3},{3,2},{4,5},{5,4},{6,7},{7,6},{8,9},{9,8},{10,11... | collective-permute-start | bytes 172040 | tf_op jit(solution)/shard_map/ppermute | solution.py:330
  12.3 1.3 collective-permute-start.1
  14.2 0.1 pad_add_fusion.scal
  14.3 0.1 reshape.64.cot_ref
  14.4 1.0 collective-permute-done.1.nxt_ref
  15.4 0.0 copy-start.1
  15.4 10.0 %grad_spatial.1 = (bf16[16,8,16,256]{3,2,1,0:T(8,128)(2,1)S(1)}, bf16[18,10,16,256]{3,2,1,0:T(8,128)(2,1)S(1)}, bf16[8,4,16,256]{3,2,1,0:T(8,128)(2,1)S(1)}, bf1...) custom-call(s32[3]{0:T(128)S(1)} %pad_add_fusion.scal, ...), custom_call_target="tpu_custom_call" | custom-call | flops 3758096384 | bytes 8699916 | tf_op jit(solution)/shard_map/grad_spatial/pallas_call | solution.py:264
  25.4 1.0 copy-done.6
  26.4 4.3 %spatial.1 = (bf16[16,8,16,256]{3,2,1,0:T(8,128)(2,1)S(1)}, bf16[8,32,256]{2,1,0:T(8,128)(2,1)S(1)}) custom-call(s32[3]{0:T(128)S(1)} %pad_add_fusion.scal, bf16[18,10,16,256]{3,2,1,0:T(8,128)(2,1)S(1)} %get-tuple-element.16.acts_ref, bf16[9,256,256]{2,1,0:T(8,128)(2,1)S(1)} %bitcast.52), custom_call_target="tpu_custom_call" | custom-call | flops 2415919104 | bytes 3833868 | tf_op jit(solution)/shard_map/spatial/pallas_call | solution.py:264
  30.7 0.0 copy-start.12
  30.7 1.0 copy-done.12
  31.7 3.9 %collective-permute-start.2 = (bf16[8,32,256]{2,1,0:T(8,128)(2,1)S(1)}, bf16[8,32,256]{2,1,0:T(8,128)(2,1)S(1)}, u32[]{:S(2)}, u32[]{:S(2)}) collective-permute-start(bf16[8,32,256]{2,1,0:T(8,128)(2,1)S(1)} %get-tuple-element.18), channel_id=1, source_target_pairs={{0,2},{2,4},{4,6},{6,8},{8,10},{10,12},{12,14},{14,16},{16,18},{18... | collective-permute-start | bytes 393224 | tf_op jit(solution)/shard_map/ppermute | solution.py:321
  35.6 0.9 collective-permute-done.2.prev_ref
  36.6 1.2 copy-done.7
  37.8 1.2 copy-done.10
  39.0 1.2 copy-done.13
  40.2 0.9 copy-done.15
  41.2 5.7 %forward.1 = (bf16[16,32,256]{2,1,0:T(8,128)(2,1)S(1)}, bf16[7,256,256]{2,1,0:T(8,128)(2,1)S(1)}) custom-call(s32[3]{0:T(128)S(1)} %pad_add_fusion.scal, bf16[16,8,16,256]{3,2,1,0:T(8,128)(2,1)S(1)} %copy-done.7, bf16[16,8,16,256]{3,2,1,0:T(8,128)(2,1)S(1)} %copy-done.13, bf16[8,32,256]{2,1,0:T(8,128)(2,1)S(1)} %collective-permute-done.2.prev_ref, ...), custom_call_target="tpu_custom_call" | custom-call | flops 2147483648 | bytes 5636108 | tf_op jit(solution)/shard_map/forward/pallas_call | solution.py:264
  46.8 0.8 dynamic-slice_bitcast_fusion
  47.6 1.0 collective-permute-start.4
  48.6 1.8 collective-permute-done.4
  50.4 1.9 fusion
  52.3 1.1 bitcast_select_fusion
  53.4 2.8 collective-permute-start.5
  56.1 4.0 %collective-permute-done.5 = bf16[2,2,2,56,256]{4,3,2,1,0:T(8,128)(2,1)S(1)} collective-permute-done((bf16[2,2,2,56,256]{4,3,2,1,0:T(8,128)(2,1)S(1)}, bf16[2,2,2,56,256]{4,3,2,1,0:T(8,128)(2,1)S(1)}, u32[]{:S(2)}, u32[]{:S(2)}) %collective-permute-start.5) | collective-permute-done | bytes 229408 | tf_op jit(solution)/shard_map/ppermute | solution.py:312
  60.1 1.1 add_convert_fusion
  61.4 0.9 collective-permute-start.6
  62.3 0.1 slice.29
  62.4 3.9 %collective-permute-done.6 = bf16[2,2,56,256]{3,2,0,1:T(8,128)(2,1)S(1)} collective-permute-done((bf16[2,2,56,256]{3,2,0,1:T(8,128)(2,1)S(1)}, bf16[2,2,56,256]{3,2,0,1:T(8,128)(2,1)S(1)}, u32[]{:S(2)}, u32[]{:S(2)}) %collective-permute-start.6) | collective-permute-done | bytes 114720 | tf_op jit(solution)/shard_map/ppermute | solution.py:312
  66.3 3.6 %collective-permute-start.7 = (bf16[2,56,256]{2,1,0:T(8,128)(2,1)S(1)}, bf16[2,56,256]{2,1,0:T(8,128)(2,1)S(1)}, u32[]{:S(2)}, u32[]{:S(2)}) collective-permute-start(bf16[2,56,256]{2,1,0:T(8,128)(2,1)S(1)} %select_bitcast_fusion), channel_id=1, source_target_pairs={{0,8},{1,9},{2,3},{3,2},{4,12},{5,13},{6,7},{7,6},{8,0},{9,1},{10,... | collective-permute-start | bytes 172040 | tf_op jit(solution)/shard_map/ppermute | solution.py:312
  70.0 0.6 collective-permute-start.3
  70.5 0.0 all-reduce.2.cloned.1.call-update
  70.5 1.5 collective-permute-done.7
  72.1 3.4 %collective-permute-start.8 = (bf16[56,256]{1,0:T(8,128)(2,1)S(1)}, bf16[56,256]{1,0:T(8,128)(2,1)S(1)}, u32[]{:S(2)}, u32[]{:S(2)}) collective-permute-start(bf16[56,256]{1,0:T(8,128)(2,1)S(1)} %dynamic-slice_bitcast_fusion.2), channel_id=1, source_target_pairs={{0,16},{1,17},{2,18},{3,19},{4,20},{5,21},{6,22},{7,23},{8,24},{9,... | collective-permute-start | bytes 86024 | tf_op jit(solution)/shard_map/ppermute | solution.py:312
  75.5 1.3 copy-done.5
  76.8 1.2 copy-done.8
  78.1 1.2 copy-done.11
  79.3 7.4 %grad_x.1 = bf16[16,128,256]{2,1,0:T(8,128)(2,1)} custom-call(s32[3]{0:T(128)S(1)} %pad_add_fusion.scal, bf16[16,8,16,256]{3,2,1,0:T(8,128)(2,1)S(1)} %copy-done.8, bf16[16,8,16,256]{3,2,1,0:T(8,128)(2,1)S(1)} %copy-done.11, bf16[16,10,16,256]{3,2,1,0:T(8,128)(2,1)S(1)} %copy-done.5, bf16[64,256]{1,0:T(8,128)(2,1)S(1)} %collective-permute-done.3.top_ref.bot_ref, ...), custom_call_target="tpu_custom_call" | custom-call | flops 2684354560 | bytes 6619148 | tf_op jit(solution)/shard_map/grad_x/pallas_call | solution.py:264
  86.7 0.8 reshape.67
  87.5 113.6 %all-reduce.2.cloned.1.call-done = bf16[3,3,256,256]{3,2,1,0:T(8,128)(2,1)} async-done(((bf16[3,3,256,256]{3,2,1,0:T(8,128)(2,1)}), bf16[3,3,256,256]{3,2,1,0:T(8,128)(2,1)}) %all-reduce.2.cloned.1.call-update) | async-done | bytes 1179664 | tf_op jit(solution)/shard_map/psum | solution.py:367
  201.0 2.9 %reshape.72 = f32[3,3,256,256]{3,2,1,0:T(8,128)} convert(bf16[3,3,256,256]{3,2,1,0:T(8,128)(2,1)} %all-reduce.2.cloned.1.call-done) | non-fusion elementwise | flops 589824 | bytes 3538944 | tf_op jit(solution)/shard_map/reshape | solution.py:393
  204.0 70.0 %all_gather.3 = bf16[1792,256]{1,0:T(8,128)(2,1)S(1)} all-gather(bf16[56,256]{1,0:T(8,128)(2,1)S(1)} %fusion.2), channel_id=1, replica_groups=mesh['tm'=16,'grp'=2] {'tm','grp'}, dimensions={0}, use_global_device_ids=true | all-gather | bytes 946176 | tf_op jit(solution)/shard_map/all_gather | solution.py:389
  274.0 0.9 slice.32
  274.9 1.0 slice.33
  (40 shorter events, 0.3 us)
Async XLA Ops:
  7.2 5.1 %slice-start = ((bf16[16,8,4,256]{3,2,1,0:T(4,128)(2,1)}), bf16[2,8,4,256]{3,2,1,0:T(4,128)(2,1)S(1)}, s32[]{:S(2)}) async-start(bf16[16,8,4,256]{3,2,1,0:T(4,128)(2,1)} %param.11), calls=%async_computation.1 | async-start | bytes 65536 | tf_op jit(solution)/shard_map/slice | solution.py:352
  7.2 7.1 %copy-start.16 = (bf16[16,8,4,256]{3,2,1,0:T(4,128)(2,1)S(1)}, bf16[16,8,4,256]{3,2,1,0:T(4,128)(2,1)}, u32[]{:S(2)}) copy-start(bf16[16,8,4,256]{3,2,1,0:T(4,128)(2,1)} %param.11) | copy-start | bytes 786436
  7.2 193.8 %all-reduce.2.cloned.1.call-start = ((), (), s32[]{:S(2)}) async-start(), calls=%async_computation | async-start | bytes 2359296 | tf_op jit(solution)/shard_map/psum | solution.py:367
  7.2 8.2 %copy-start = (bf16[16,16,8,256]{3,2,1,0:T(8,128)(2,1)S(1)}, bf16[16,16,8,256]{3,2,1,0:T(8,128)(2,1)}, u32[]{:S(2)}) copy-start(bf16[16,16,8,256]{3,2,1,0:T(8,128)(2,1)} %param.6) | copy-start | bytes 3145732
  7.2 8.1 %copy-start.2 = (bf16[2,2,256,256]{3,2,1,0:T(8,128)(2,1)S(1)}, bf16[2,2,256,256]{3,2,1,0:T(8,128)(2,1)}, u32[]{:S(2)}) copy-start(bf16[2,2,256,256]{3,2,1,0:T(8,128)(2,1)} %param.10) | copy-start | bytes 1572868
  7.3 8.1 %copy-start.3 = (bf16[3,256,256]{2,1,0:T(8,128)(2,1)S(1)}, bf16[3,256,256]{2,1,0:T(8,128)(2,1)}, u32[]{:S(2)}) copy-start(bf16[3,256,256]{2,1,0:T(8,128)(2,1)} %wt_ref.5) | copy-start | bytes 1179652
  9.3 6.1 %collective-permute-start = (bf16[112,256]{1,0:T(8,128)(2,1)}, bf16[112,256]{1,0:T(8,128)(2,1)S(1)}, u32[]{:S(2)}, u32[]{:S(2)}) collective-permute-start(bf16[112,256]{1,0:T(8,128)(2,1)} %dynamic-slice_bitcast_fusion.1), channel_id=1, source_target_pairs={{0,1},{1,0},{2,3},{3,2},{4,5},{5,4},{6,7},{7,6},{8,9},{9,8},{10,11... | collective-permute-start | bytes 172040 | tf_op jit(solution)/shard_map/ppermute | solution.py:330
  12.3 3.1 %collective-permute-start.1 = (bf16[2,32,256]{2,1,0:T(8,128)(2,1)S(1)}, bf16[2,32,256]{2,1,0:T(8,128)(2,1)S(1)}, u32[]{:S(2)}, u32[]{:S(2)}) collective-permute-start(bf16[2,32,256]{2,1,0:T(8,128)(2,1)S(1)} %slice.27), channel_id=1, source_target_pairs={{2,0},{4,2},{6,4},{8,6},{10,8},{12,10},{14,12},{16,14},{18,16},{20... | collective-permute-start | bytes 98312 | tf_op jit(solution)/shard_map/ppermute | solution.py:321
  15.4 11.0 %copy-start.1 = (bf16[3,3,256,256]{3,2,1,0:T(8,128)(2,1)S(1)}, bf16[3,3,256,256]{3,2,1,0:T(8,128)(2,1)}, u32[]{:S(2)}) copy-start(bf16[3,3,256,256]{3,2,1,0:T(8,128)(2,1)} %param.8) | copy-start | bytes 3538948
  25.4 1.0 copy-start.6
  26.4 4.3 %copy-start.4 = (bf16[16,10,16,256]{3,2,1,0:T(8,128)(2,1)}, bf16[16,10,16,256]{3,2,1,0:T(8,128)(2,1)S(1)}, u32[]{:S(2)}) copy-start(bf16[16,10,16,256]{3,2,1,0:T(8,128)(2,1)S(1)} %get-tuple-element.22.gs_ref) | copy-start | bytes 3932164
  26.4 4.3 %copy-start.9 = (bf16[16,8,16,256]{3,2,1,0:T(8,128)(2,1)}, bf16[16,8,16,256]{3,2,1,0:T(8,128)(2,1)S(1)}, u32[]{:S(2)}) copy-start(bf16[16,8,16,256]{3,2,1,0:T(8,128)(2,1)S(1)} %get-tuple-element.20.gy_ref) | copy-start | bytes 3145732
  26.4 4.3 %copy-start.14 = (bf16[8,4,16,256]{3,2,1,0:T(8,128)(2,1)}, bf16[8,4,16,256]{3,2,1,0:T(8,128)(2,1)S(1)}, u32[]{:S(2)}) copy-start(bf16[8,4,16,256]{3,2,1,0:T(8,128)(2,1)S(1)} %get-tuple-element.19.cott_ref) | copy-start | bytes 786436
  30.7 1.0 copy-start.12
  31.7 4.9 %collective-permute-start.2 = (bf16[8,32,256]{2,1,0:T(8,128)(2,1)S(1)}, bf16[8,32,256]{2,1,0:T(8,128)(2,1)S(1)}, u32[]{:S(2)}, u32[]{:S(2)}) collective-permute-start(bf16[8,32,256]{2,1,0:T(8,128)(2,1)S(1)} %get-tuple-element.18), channel_id=1, source_target_pairs={{0,2},{2,4},{4,6},{6,8},{8,10},{10,12},{12,14},{14,16},{16,18},{18... | collective-permute-start | bytes 393224 | tf_op jit(solution)/shard_map/ppermute | solution.py:321
  36.6 1.2 copy-start.7
  37.8 1.2 copy-start.10
  39.0 1.2 copy-start.13
  40.2 0.9 copy-start.15
  47.6 2.8 collective-permute-start.4
  53.4 6.8 %collective-permute-start.5 = (bf16[2,2,2,56,256]{4,3,2,1,0:T(8,128)(2,1)S(1)}, bf16[2,2,2,56,256]{4,3,2,1,0:T(8,128)(2,1)S(1)}, u32[]{:S(2)}, u32[]{:S(2)}) collective-permute-start(bf16[2,2,2,56,256]{4,3,2,1,0:T(8,128)(2,1)S(1)} %bitcast_select_fusion), channel_id=1, source_target_pairs={{0,4},{1,5},{2,10},{3,11},{4,0},{5,1},{6,14},{7,15},{8,12},{9,13},... | collective-permute-start | bytes 688136 | tf_op jit(solution)/shard_map/ppermute | solution.py:312
  56.1 6.2 %slice-start.1 = ((bf16[16,8,4,256]{3,2,1,0:T(4,128)(2,1)}), bf16[14,8,4,256]{3,2,1,0:T(4,128)(2,1)S(1)}, s32[]{:S(2)}) async-start(bf16[16,8,4,256]{3,2,1,0:T(4,128)(2,1)} %param.11), calls=%async_computation.2 | async-start | bytes 458752 | tf_op jit(solution)/shard_map/slice | solution.py:354
  61.4 4.9 %collective-permute-start.6 = (bf16[2,2,56,256]{3,2,0,1:T(8,128)(2,1)S(1)}, bf16[2,2,56,256]{3,2,0,1:T(8,128)(2,1)S(1)}, u32[]{:S(2)}, u32[]{:S(2)}) collective-permute-start(bf16[2,2,56,256]{3,2,0,1:T(8,128)(2,1)S(1)} %bitcast_select_fusion.2), channel_id=1, source_target_pairs={{0,1},{1,0},{2,6},{3,7},{4,5},{5,4},{6,2},{7,3},{8,9},{9,8},{10,14... | collective-permute-start | bytes 344072 | tf_op jit(solution)/shard_map/ppermute | solution.py:312
  66.3 5.8 %collective-permute-start.7 = (bf16[2,56,256]{2,1,0:T(8,128)(2,1)S(1)}, bf16[2,56,256]{2,1,0:T(8,128)(2,1)S(1)}, u32[]{:S(2)}, u32[]{:S(2)}) collective-permute-start(bf16[2,56,256]{2,1,0:T(8,128)(2,1)S(1)} %select_bitcast_fusion), channel_id=1, source_target_pairs={{0,8},{1,9},{2,3},{3,2},{4,12},{5,13},{6,7},{7,6},{8,0},{9,1},{10,... | collective-permute-start | bytes 172040 | tf_op jit(solution)/shard_map/ppermute | solution.py:312
  70.0 5.6 %collective-permute-start.3 = (bf16[64,256]{1,0:T(8,128)(2,1)S(1)}, bf16[64,256]{1,0:T(8,128)(2,1)S(1)}, u32[]{:S(2)}, u32[]{:S(2)}) collective-permute-start(bf16[64,256]{1,0:T(8,128)(2,1)S(1)} %reshape.68), channel_id=1, source_target_pairs={{0,1},{1,0},{2,3},{3,2},{4,5},{5,4},{6,7},{7,6},{8,9},{9,8},{10,11... | collective-permute-start | bytes 98312 | tf_op jit(solution)/shard_map/ppermute | solution.py:330
  72.1 131.8 %collective-permute-start.8 = (bf16[56,256]{1,0:T(8,128)(2,1)S(1)}, bf16[56,256]{1,0:T(8,128)(2,1)S(1)}, u32[]{:S(2)}, u32[]{:S(2)}) collective-permute-start(bf16[56,256]{1,0:T(8,128)(2,1)S(1)} %dynamic-slice_bitcast_fusion.2), channel_id=1, source_target_pairs={{0,16},{1,17},{2,18},{3,19},{4,20},{5,21},{6,22},{7,23},{8,24},{9,... | collective-permute-start | bytes 86024 | tf_op jit(solution)/shard_map/ppermute | solution.py:312
  75.5 1.3 copy-start.5
  76.8 1.2 copy-start.8
  78.1 1.2 copy-start.11
Sparse Core Ops, SparseCore 0:
  70.7 130.3 all-reduce.1

commit v3 on v2

v3 whole, which is shorter than its diff:
```python
import functools

import jax
import jax.numpy as jnp
from jax import lax
from jax.experimental import pallas as pl
from jax.experimental.pallas import tpu as pltpu
from jax.sharding import PartitionSpec as P

SLOTS = 16
OWN = 14
CH = 256
BF = jnp.bfloat16
F32 = jnp.float32


def mm(a, b):
    return lax.dot_general(a, b, (((1,), (0,)), ((), ())), preferred_element_type=F32)


def mm_nt(a, b):
    return lax.dot_general(a, b, (((1,), (1,)), ((), ())), preferred_element_type=F32)


def iotas(rows, cols):
    return (
        lax.broadcasted_iota(jnp.int32, (rows, cols), 0),
        lax.broadcasted_iota(jnp.int32, (rows, cols), 1),
    )


def to_slots(rows, frames, keep):
    a, b = iotas(rows * SLOTS, frames * rows)
    hit = (a // SLOTS == b % rows) & keep(b // rows, a % SLOTS)
    return jnp.where(hit, 1.0, 0.0).astype(BF)


def to_frames(rows):
    a, b = iotas(SLOTS * rows, rows * SLOTS)
    hit = (a % rows == b // SLOTS) & (a // rows == b % SLOTS)
    return jnp.where(hit, 1.0, 0.0).astype(BF)


def own_frames(count):
    return lambda frame, slot: (frame == slot) & (slot < count)


def own_and_next(count):
    return lambda frame, slot: ((frame < OWN) & (frame == slot) & (slot < count)) | (
        (frame >= OWN) & (slot == count + frame - OWN)
    )


def silu_norm(v):
    scaled = v * lax.rsqrt(jnp.mean(v * v, axis=-1, keepdims=True) + 1e-06)
    return scaled / (1.0 + jnp.exp(-scaled))


def slot_mask(shape, count):
    return lax.broadcasted_iota(jnp.int32, shape, len(shape) - 2) < count


def grad_of_temporal(gy, wt_ref, count):
    n = gy.shape[0]
    flat = gy.reshape(n * SLOTS, CH)
    total = mm_nt(flat, wt_ref[2]).reshape(n, SLOTS, CH)
    for k in (1, 0):
        term = mm_nt(flat, wt_ref[k]).reshape(n, SLOTS, CH)
        total = total + pltpu.roll(term, SLOTS - (2 - k), 1)
    return jnp.where(slot_mask(total.shape, count), total, 0.0).astype(BF)


def place_bits():
    t, g = lax.axis_index("tm"), lax.axis_index("grp")
    return t & 1, ((t >> 1) & 1) + 2 * (g & 1), (t >> 2) & 3


def split_cores(value, keep_ref, send_ref, k):
    core, _, _ = place_bits()
    low, high = value[:, : CH // 2].astype(BF), value[:, CH // 2 :].astype(BF)
    keep_ref[:, k] = jnp.where(core == 0, low, high).reshape(16, 16, CH // 2)
    send_ref[:, k] = jnp.where(core == 0, high, low).reshape(16, 16, CH // 2)


def edges_kernel(bands, count_ref, x_ref, cot_ref, *rest):
    outs, nxt_ref, buf, sems = rest[: len(rest) - 3], rest[-3], rest[-2], rest[-1]
    count = count_ref[0]
    band = lax.axis_index("grp")
    wide = x_ref.shape[1]
    if bands == 2:
        starts = [jnp.where(band == 0, wide - 16, 0)]
        lower = [band == 0]
    else:
        starts, lower = [wide - 16, 0], [True, False]
    copies = [
        pltpu.make_async_copy(
            x_ref.at[:, pl.ds(pl.multiple_of(at, 16), 16), :], buf.at[k], sems.at[k]
        )
        for k, at in enumerate(starts)
    ]
    for copy in copies:
        copy.start()
    nxt_ref[...] = cot_ref[0:2]
    place = to_slots(16, SLOTS, own_frames(count))
    for k, copy in enumerate(copies):
        copy.wait()
        v = mm(place, buf[k].reshape(SLOTS * 16, CH))
        v = jnp.where(lower[k], v[128:], v[:128])
        outs[k][...] = silu_norm(v).astype(BF)


def acts_kernel(count_ref, x_ref, _, xt_ref, acts_ref, at_ref):
    count = count_ref[0]
    rows, cols = xt_ref.shape[0], xt_ref.shape[1]
    edge = jnp.zeros((rows + 2, SLOTS, CH), BF)
    acts_ref[:, 0] = edge
    acts_ref[:, cols + 1] = edge
    place = to_slots(16, SLOTS, own_frames(count))

    def rows_of(q, _):
        at = pl.multiple_of(q * 16, 16)
        piece = x_ref[:, pl.ds(at, 16), :].reshape(SLOTS * 16, CH)
        v = mm(place, piece)
        xt_ref[pl.ds(2 * q, 2)] = v.astype(BF).reshape(2, cols, SLOTS, CH)
        a = silu_norm(v)
        acts_ref[pl.ds(2 * q + 1, 2), 1 : cols + 1] = a.astype(BF).reshape(2, cols, SLOTS, CH)
        at_ref[:, pl.ds(pl.multiple_of(q * 256 + 128, 128), 256)] = a.T.astype(BF)
        return 0

    lax.fori_loop(0, rows // 2, rows_of, 0)


def spatial_kernel(
    bands, count_ref, top_ref, bot_ref, acts_in, at_in, ws_ref, acts_ref, at_ref, sp_ref, edge_ref
):
    count = count_ref[0]
    band = lax.axis_index("grp")
    rows, cols = sp_ref.shape[0], sp_ref.shape[1]
    for ref, flag, row in ((top_ref, band > 0, 0), (bot_ref, band < bands - 1, rows + 1)):
        a = jnp.where(flag, ref[...].astype(F32), 0.0)
        acts_ref[row, 1 : cols + 1] = a.astype(BF).reshape(cols, SLOTS, CH)
        at_ref[:, row * 128 : row * 128 + 128] = a.T.astype(BF)
    a, b = iotas(32, 256)
    pick = (a // 2 == b // SLOTS) & (b % SLOTS == count - 2 + a % 2)
    pick = jnp.where(pick, 1.0, 0.0).astype(BF)

    def rows_of(q, _):
        total = None
        for i in range(3):
            for j in range(3):
                left = acts_ref[pl.ds(4 * q + i, 4), j : j + cols].reshape(4 * cols * SLOTS, CH)
                term = mm(left, ws_ref[i * 3 + j])
                total = term if total is None else total + term
        out = total.astype(BF)
        sp_ref[pl.ds(4 * q, 4)] = out.reshape(4, cols, SLOTS, CH)
        for half in range(2):
            edge_ref[2 * q + half] = mm(pick, out[half * 256 : half * 256 + 256]).astype(BF)
        return 0

    lax.fori_loop(0, rows // 4, rows_of, 0)


def grad_spatial_kernel(
    count_ref, at_ref, cot_ref, nxt_ref, wt_ref, wd_ref,
    cott_ref, gy_ref, gs_ref, last_ref, first_ref, keep_ref, send_ref,
):
    count = count_ref[0]
    rows, cols = gy_ref.shape[0], gy_ref.shape[1]
    edge = jnp.zeros((rows, SLOTS, CH), BF)
    gs_ref[:, 0] = edge
    gs_ref[:, cols + 1] = edge

    place_next = to_slots(16, SLOTS, own_and_next(count))
    for q in range(rows * cols // 64):
        piece = jnp.concatenate(
            [cot_ref[0:OWN, q * 16 : q * 16 + 16, :], nxt_ref[:, q * 16 : q * 16 + 16, :]], 0
        ).reshape(SLOTS * 16, CH)
        placed = mm(place_next, piece).astype(BF)
        cott_ref[q * 4 : q * 4 + 4] = placed.reshape(4, 4, SLOTS, CH)
        for i in range(2):
            for j in range(2):
                g = mm_nt(placed, wd_ref[i * 2 + j]).astype(BF).reshape(4, 4, SLOTS, CH)
                for r in range(4):
                    for c in range(4):
                        gy_ref[2 * (q * 4 + r) + i, 2 * c + j] = g[r, c]
    last_ref[...] = cott_ref[rows // 2 - 1].reshape(cols // 2 * SLOTS, CH)
    first_ref[...] = cott_ref[0].reshape(cols // 2 * SLOTS, CH)

    def grads_of(q, _):
        g = gy_ref[pl.ds(4 * q, 4)].reshape(4 * cols, SLOTS, CH)
        s = grad_of_temporal(g, wt_ref, count)
        gs_ref[pl.ds(4 * q, 4), 1 : cols + 1] = s.reshape(4, cols, SLOTS, CH)
        return 0

    lax.fori_loop(0, rows // 4, grads_of, 0)

    wide = rows * cols * SLOTS
    for i in range(3):
        for j in range(3):
            right = gs_ref[:, 2 - j : 2 - j + cols].reshape(wide, CH)
            value = mm(at_ref[:, i * 128 : i * 128 + wide], right)
            split_cores(value, keep_ref, send_ref, i * 3 + j)


def forward_kernel(
    count_ref, xt_ref, sp_ref, prev_ref, cott_ref, gy_ref, wt_ref, wd_ref, _,
    down_ref, keep_ref, send_ref, y_ref, st_ref, g1_ref, g0_ref, g2_ref,
):
    count = count_ref[0]
    rows, cols = xt_ref.shape[0], xt_ref.shape[1]
    a, b = iotas(256, 32)
    place = (a // SLOTS == b // 2) & (a % SLOTS == OWN + b % 2)
    place = jnp.where(place, 1.0, 0.0).astype(BF)

    def rows_of(q, _):
        s = sp_ref[pl.ds(2 * q, 2)].reshape(256, CH)
        s = (s.astype(F32) + mm(place, prev_ref[q])).astype(BF)
        st_ref[:, pl.ds(pl.multiple_of(q * 256, 256), 256)] = s.T
        total = mm(s, wt_ref[2]).reshape(2 * cols, SLOTS, CH)
        for k in (1, 0):
            total = total + pltpu.roll(mm(s, wt_ref[k]).reshape(2 * cols, SLOTS, CH), 2 - k, 1)
        x = xt_ref[pl.ds(2 * q, 2)].reshape(2 * cols, SLOTS, CH).astype(F32)
        mask = slot_mask(x.shape, count)
        y = jnp.where(mask, x + total, 0.0).astype(BF)
        y_ref[pl.ds(2 * q, 2)] = y.reshape(2, cols, SLOTS, CH)
        g = gy_ref[pl.ds(2 * q, 2)].reshape(2 * cols, SLOTS, CH).astype(F32)
        g = jnp.where(mask, g, 0.0)
        for ref, k in ((g2_ref, 2), (g1_ref, 1), (g0_ref, 0)):
            shifted = g if k == 2 else pltpu.roll(g, SLOTS - (2 - k), 1)
            ref[pl.ds(2 * q, 2)] = shifted.astype(BF).reshape(2, cols, SLOTS, CH)
        return 0

    lax.fori_loop(0, rows // 2, rows_of, 0)

    wide = rows * cols * SLOTS
    for k, ref in ((0, g0_ref), (1, g1_ref), (2, g2_ref)):
        split_cores(mm(st_ref[...], ref[...].reshape(wide, CH)), keep_ref, send_ref, k)

    small = wide // 4
    total = None
    cot = cott_ref[...].reshape(small, CH)
    for i in range(2):
        for j in range(2):
            tiles = [
                y_ref[2 * r + i, 2 * c + j] for r in range(rows // 2) for c in range(cols // 2)
            ]
            piece = jnp.concatenate(tiles, axis=0)
            term = mm(piece, wd_ref[i * 2 + j])
            total = term if total is None else total + term
            split_cores(mm(piece.T, cot), keep_ref, send_ref, 3 + i * 2 + j)
    down = total.astype(BF)
    back = to_frames(16)
    for q in range(small // 256):
        o = mm(back, down[q * 256 : q * 256 + 256]).astype(BF)
        down_ref[:, q * 16 : q * 16 + 16, :] = o.reshape(SLOTS, 16, CH)


def grad_x_kernel(
    part, bands, count_ref, xt_ref, gy_ref, gs_ref, halo_ref, wt_ref, wd_ref, ws_ref, *rest
):
    out_ref, pad_ref, buf, sem = rest[-4:]
    count = count_ref[0]
    band = lax.axis_index("grp")
    rows, cols = xt_ref.shape[0], xt_ref.shape[1]
    half = rows // 2
    if part == 0:
        flag, i, row = band > 0, 1, 0
        pad_ref[1 : half + 2] = gs_ref[0 : half + 1]
    else:
        flag, i, row = band < bands - 1, 0, half + 1
        pad_ref[0 : half + 1] = gs_ref[half - 1 :]
    pair = [
        mm_nt(halo_ref[...], wd_ref[i * 2 + j]).astype(BF).reshape(cols // 2, SLOTS, CH)
        for j in range(2)
    ]
    g = jnp.stack(pair, axis=1).reshape(cols, SLOTS, CH)
    s = grad_of_temporal(g, wt_ref, jnp.where(flag, count, 0))
    pad_ref[row, 0] = jnp.zeros((SLOTS, CH), BF)
    pad_ref[row, 1 : cols + 1] = s
    pad_ref[row, cols + 1] = jnp.zeros((SLOTS, CH), BF)
    back = to_frames(16)

    def rows_of(q, _):
        total = None
        for i in range(3):
            for j in range(3):
                left = pad_ref[pl.ds(4 * q + 2 - i, 4), 2 - j : 2 - j + cols].reshape(
                    4 * cols * SLOTS, CH
                )
                term = mm_nt(left, ws_ref[i * 3 + j])
                total = term if total is None else total + term
        at = part * half + 4 * q
        v = xt_ref[pl.ds(at, 4)].reshape(4 * cols * SLOTS, CH).astype(F32)
        r = lax.rsqrt(jnp.mean(v * v, axis=-1, keepdims=True) + 1e-06)
        u = v * r
        s = 1.0 / (1.0 + jnp.exp(-u))
        gu = total * (s * (1.0 + u * (1.0 - s)))
        dot = jnp.mean(gu * u, axis=-1, keepdims=True)
        gv = r * (gu - u * dot)
        gx = gy_ref[pl.ds(at, 4)].reshape(4 * cols * SLOTS, CH).astype(F32) + gv
        gx = gx.reshape(4 * cols, SLOTS, CH)
        gx = jnp.where(slot_mask(gx.shape, count), gx, 0.0).astype(BF).reshape(4 * cols * SLOTS, CH)
        for k in range(2):
            o = mm(back, gx[k * 256 : k * 256 + 256]).astype(BF)
            buf[:, pl.ds(pl.multiple_of((2 * q + k) * 16, 16), 16), :] = o.reshape(SLOTS, 16, CH)
        return 0

    lax.fori_loop(0, half // 4, rows_of, 0)
    size = half * cols
    copy = pltpu.make_async_copy(buf, out_ref.at[:, part * size : part * size + size, :], sem)
    copy.start()
    copy.wait()


def plane_send_kernel(keep_ref, got_ref, *rest):
    outs = rest[-4:]
    _, p, _ = place_bits()
    for r in range(4):
        at = pl.ds((p ^ r) * 4, 4)
        outs[r][...] = (keep_ref[at].astype(F32) + got_ref[at].astype(F32)).astype(BF)


def total_at(refs, z):
    return functools.reduce(lambda a, b: a + b, [ref[z].astype(F32) for ref in refs]).astype(BF)


def line_send_kernel(*refs):
    ins, outs = refs[:4], refs[-4:]
    _, _, z = place_bits()
    for r in range(4):
        outs[r][...] = total_at(ins, z ^ r)


def line_sum_kernel(a_ref, b_ref, c_ref, d_ref, out_ref):
    parts = [ref[...].astype(F32) for ref in (a_ref, b_ref, c_ref, d_ref)]
    out_ref[...] = (parts[0] + parts[1] + parts[2] + parts[3]).astype(BF)


def line_gather_kernel(a_ref, b_ref, c_ref, d_ref, out_ref):
    _, _, z = place_bits()
    for r, ref in enumerate((a_ref, b_ref, c_ref, d_ref)):
        out_ref[z ^ r] = ref[...]


def plane_gather_kernel(a_ref, b_ref, c_ref, d_ref, out_ref):
    _, p, _ = place_bits()
    for r, ref in enumerate((a_ref, b_ref, c_ref, d_ref)):
        out_ref[pl.ds((p ^ r) * 4, 4)] = ref[...]


def finish_kernel(own_ref, got_ref, *rest):
    outs, buf, sems = rest[:-2], rest[-2], rest[-1]
    core, _, _ = place_bits()
    copies = []
    k = 0
    for out in outs:
        for m in range(out.shape[0]):
            own = own_ref[:, k].reshape(CH, CH // 2).astype(F32)
            got = got_ref[:, k].reshape(CH, CH // 2).astype(F32)
            buf[k, :, : CH // 2] = jnp.where(core == 0, own, got)
            buf[k, :, CH // 2 :] = jnp.where(core == 0, got, own)
            copies.append(pltpu.make_async_copy(buf.at[k], out.at[m], sems.at[k]))
            copies[-1].start()
            k += 1
    for copy in copies:
        copy.wait()


VMEM = pl.BlockSpec(memory_space=pltpu.VMEM)
SMEM = pl.BlockSpec(memory_space=pltpu.SMEM)
ANY = pl.BlockSpec(memory_space=pl.ANY)


def call(kernel, name, ins, outs, scratch=(), flops=0, alias=None):
    shapes = [jax.ShapeDtypeStruct(o[1], o[2] if len(o) > 2 else BF) for o in outs]
    moved = sum(a.size * a.dtype.itemsize for s, a in ins if s is not ANY)
    moved += sum(s.size * s.dtype.itemsize for s in shapes)
    return pl.pallas_call(
        kernel,
        out_shape=shapes,
        in_specs=[s for s, _ in ins],
        out_specs=[o[0] for o in outs],
        scratch_shapes=list(scratch),
        compiler_params=pltpu.CompilerParams(vmem_limit_bytes=10 * 2**20),
        cost_estimate=pl.CostEstimate(flops=flops, bytes_accessed=moved, transcendentals=0),
        input_output_aliases=alias or {},
        name=name,
    )(*[a for _, a in ins])


AXES = ("tm", "grp")


def plan(tm, grp):
    low, total = grp.bit_length() - 1, (tm * grp).bit_length() - 1
    used = [low, low + 1, 0, low + 2, low + 3]
    return used + [b for b in range(total) if b not in used]


def swap(value, tm, grp, *bits):
    flip = sum(1 << b for b in bits)
    return lax.ppermute(value, AXES, [(d, d ^ flip) for d in range(tm * grp)])


def core_round(send, tm, grp):
    return swap(send, tm, grp, plan(tm, grp)[0])


def plane_send(keep, got, after):
    n = keep.shape[1]
    ins = [(VMEM, keep), (VMEM, got)] + [(ANY, a) for a in after]
    return call(plane_send_kernel, "plane_send", ins, [(VMEM, (4, n, 16, CH // 2))] * 4)


def plane_round(parts, tm, grp):
    _, x, y = plan(tm, grp)[:3]
    return [parts[0], swap(parts[1], tm, grp, x), swap(parts[2], tm, grp, y), swap(parts[3], tm, grp, x, y)]


def line_send(parts, after):
    shape = parts[0].shape[1:]
    ins = [(VMEM, a) for a in parts] + [(ANY, a) for a in after]
    return call(line_send_kernel, "line_send", ins, [(VMEM, shape)] * 4)


def line_round(parts, tm, grp):
    _, _, _, a, b = plan(tm, grp)[:5]
    return [parts[0], swap(parts[1], tm, grp, a), swap(parts[2], tm, grp, b), swap(parts[3], tm, grp, a, b)]


def gather_back(parts, shapes, tm, grp):
    (mine,) = call(line_sum_kernel, "line_sum", [(VMEM, a) for a in parts], [(VMEM, parts[0].shape)])
    for bit in plan(tm, grp)[5:]:
        mine = (mine.astype(F32) + swap(mine, tm, grp, bit).astype(F32)).astype(BF)
    parts = line_round([mine] * 4, tm, grp)
    (mine,) = call(
        line_gather_kernel, "line_gather", [(VMEM, a) for a in parts], [(VMEM, (4,) + mine.shape)]
    )
    parts = plane_round([mine] * 4, tm, grp)
    (mine,) = call(
        plane_gather_kernel, "plane_gather", [(VMEM, a) for a in parts], [(VMEM, (16,) + mine.shape[1:])]
    )
    got = core_round(mine, tm, grp)
    n = mine.shape[1]
    return call(
        finish_kernel,
        "finish",
        [(VMEM, mine), (VMEM, got)],
        [(ANY, (m, CH, CH), F32) for m in shapes],
        [pltpu.VMEM((n, CH, CH), F32), pltpu.SemaphoreType.DMA((n,))],
    )


def along(value, axis, by):
    count = lax.axis_size(axis)
    pairs = [(i, i + by) for i in range(count) if 0 <= i + by < count]
    return lax.ppermute(value, axis, pairs)


def from_bands(parts):
    if len(parts) == 1:
        got = lax.ppermute(parts[0], "grp", [(0, 1), (1, 0)])
        return got, got
    return along(parts[0], "grp", 1), along(parts[1], "grp", -1)


def body(tm, grp, frames_in, span_frames, w_spatial, w_temporal, w_down, cotangent):
    slots, rows, cols, ch = frames_in.shape
    wide = rows * cols
    x = frames_in.reshape(slots, wide, ch)
    cot = cotangent.reshape(slots, wide // 4, ch)
    ws = w_spatial.reshape(9, ch, ch)
    wd = w_down.reshape(4, ch, ch)
    wt = w_temporal
    count = (SMEM, span_frames)
    tap = 2 * slots * wide * ch * ch
    tile = (rows, cols, slots, ch)
    padded = (rows + 2, cols + 2, slots, ch)
    dma = pltpu.SemaphoreType.DMA

    sides = 1 if grp == 2 else 2
    *edge, nxt = call(
        functools.partial(edges_kernel, grp),
        "edges",
        [count, (ANY, x), (VMEM, cot)],
        [(VMEM, (cols * slots, ch))] * sides + [(VMEM, (2, wide // 4, ch))],
        [pltpu.VMEM((sides, slots, 16, ch), BF), dma((sides,))],
        flops=tap // 8,
    )
    top, bot = from_bands(edge)
    nxt_got = along(nxt, "tm", -1)
    xt, acts, at = call(
        acts_kernel,
        "acts",
        [count, (VMEM, x), (ANY, nxt)],
        [(VMEM, tile), (VMEM, padded), (VMEM, (ch, (rows + 2) * 128))],
        flops=2 * tap,
    )
    acts, at, sp, last_two = call(
        functools.partial(spatial_kernel, grp),
        "spatial",
        [count, (VMEM, top), (VMEM, bot), (VMEM, acts), (VMEM, at), (VMEM, ws)],
        [(VMEM, padded), (VMEM, at.shape), (VMEM, tile), (VMEM, (rows // 2, 32, ch))],
        flops=9 * tap,
        alias={3: 0, 4: 1},
    )
    prev = along(last_two, "tm", 1)
    half = (16, 9, 16, ch // 2)
    cott, gy, gs, last, first, keep_a, send_a = call(
        grad_spatial_kernel,
        "grad_spatial",
        [count, (VMEM, at), (VMEM, cot), (VMEM, nxt_got), (VMEM, wt), (VMEM, wd)],
        [(VMEM, (rows // 2, cols // 2, slots, ch)), (VMEM, tile), (VMEM, (rows, cols + 2, slots, ch)),
         (VMEM, (cols // 2 * slots, ch)), (VMEM, (cols // 2 * slots, ch)), (VMEM, half), (VMEM, half)],
        flops=14 * tap,
    )
    got_a = core_round(send_a, tm, grp)
    cot_top, cot_bot = along(last, "grp", 1), along(first, "grp", -1)
    half = (16, 7, 16, ch // 2)
    down, keep_b, send_b = call(
        forward_kernel,
        "forward",
        [count, (VMEM, xt), (VMEM, sp), (VMEM, prev), (VMEM, cott), (VMEM, gy), (VMEM, wt), (VMEM, wd),
         (ANY, send_a)],
        [(VMEM, (slots, wide // 4, ch)), (VMEM, half), (VMEM, half)],
        [pltpu.VMEM(s, BF) for s in (tile, (ch, slots * wide), tile, tile, tile)],
        flops=10 * tap,
    )
    got_b = core_round(send_b, tm, grp)
    parts_a = plane_send(keep_a, got_a, [send_b])

    def grad_x_part(part, halo, after):
        return call(
            functools.partial(grad_x_kernel, part, grp),
            f"grad_x_{part}",
            [count, (VMEM, xt), (VMEM, gy), (VMEM, gs), (VMEM, halo), (VMEM, wt), (VMEM, wd), (VMEM, ws)]
            + [(ANY, a) for a in after],
            [(ANY, (slots, wide, ch))],
            [pltpu.VMEM((rows // 2 + 2, cols + 2, slots, ch), BF),
             pltpu.VMEM((slots, wide // 2, ch), BF), dma],
            flops=5 * tap,
            alias={8: 0} if part else None,
        )[0]

    grad_x = grad_x_part(0, cot_top, [parts_a[3], send_b])
    parts_a = plane_round(parts_a, tm, grp)
    parts_b = plane_send(keep_b, got_b, [grad_x])
    parts_a = line_send(parts_a, [parts_b[0]])
    grad_x = grad_x_part(1, cot_bot, [grad_x, parts_a[3], parts_b[3]])
    parts_b = plane_round(parts_b, tm, grp)
    parts_a = line_round(parts_a, tm, grp)
    parts_b = line_send(parts_b, [grad_x])
    parts_b = line_round(parts_b, tm, grp)
    (sum_s,) = gather_back(parts_a, [9], tm, grp)
    sum_t, sum_d = gather_back(parts_b, [3, 4], tm, grp)
    return (
        down.reshape(cotangent.shape),
        grad_x.reshape(frames_in.shape),
        sum_s.reshape(w_spatial.shape),
        sum_t,
        sum_d.reshape(w_down.shape),
    )


def solution(mesh):
    return jax.shard_map(
        functools.partial(body, mesh.shape["tm"], mesh.shape["grp"]),
        mesh=mesh,
        in_specs=(P("tm", "grp", None, None), P("tm"), P(), P(), P(), P("tm", "grp", None, None)),
        out_specs=(P("tm", "grp", None, None), P("tm", "grp", None, None), P(), P(), P()),
        check_vma=False,
    )
```

time: 283 us -> 100 us (0.35)
  waiting for transfers between devices: 127 us -> 19.6 us
  blocking collectives: 70 us -> 0 us
  starting transfers between devices: 20.4 us -> 44.4 us
  between operations: 14.9 us -> 1.73 us
  local copies, waits for them, and re-layouts: 16.2 us -> 5.47 us
  other arithmetic: 7.22 us -> 0 us
    psum x1 -> x0, waiting for transfers between devices: 114 us -> none  [body(): sum_s = lax.psum(gw_s.reshape(9 * ch, ch), AXES)]
    all_gather x1 -> x0, blocking collectives: 70 us -> none  [body(): sum_t = lax.all_gather(part, AXES, axis=0, tiled=True).astype(F32)]
    ppermute x7 -> x29, starting transfers between devices: 15.2 us -> 36.3 us  [the longest x28 33.2 us: swap(): return lax.ppermute(value, AXES, [(d, d ^ flip) for d in range(tm * grp)])]
    ppermute x7 -> x29, waiting for transfers between devices: 11.2 us -> 19 us  [the longest x28 19 us: swap(): return lax.ppermute(value, AXES, [(d, d ^ flip) for d in range(tm * grp)])]
    unnamed x34 -> x12, local copies, waits for them, and re-layouts: 10.4 us -> 3.68 us
    slice x9 -> x0, local copies, waits for them, and re-layouts: 3.44 us -> none  [the longest x1 1.38 us: body(): top, bot = edge_rows(x[:OWN], cols, grp, band)]
    convert_element_type x5 -> x0, other arithmetic: 3.11 us -> none  [scatter_sum(): value = (half(0).astype(F32) + got.astype(F32)).astype(BF)]
    ppermute x2 -> x4, starting transfers between devices: 5.19 us -> 8.16 us  [along(): return lax.ppermute(value, axis, pairs)]
  transfers between devices with their start and end apart: 10 -> 33, of which waited for: 7 -> 14; matrix products, arithmetic and copies ran while one was open for 1% -> 1% of each run, Pallas kernels for 3% -> 27%
where the time goes in v3:
time: 100 us; the launch traced here: 99.7 us
  starting transfers between devices  44.4 us (44%)
  Pallas kernels  28.5 us (28%)
  waiting for transfers between devices  19.6 us (20%)
  local copies, waits for them, and re-layouts  5.47 us (5%)
  between operations  1.73 us (2%)
    ppermute x28, starting transfers between devices, swap(): return lax.ppermute(value, AXES, [(d, d ^ flip) for d in range(tm * grp)])  33.2 us
    pallas_call x19, Pallas kernels, call(): pl.pallas_call(kernel, out_shape=shapes, in_specs=[s for s, _ in ins], ou...  28.5 us
    ppermute x28, waiting for transfers between devices, swap(): return lax.ppermute(value, AXES, [(d, d ^ flip) for d in range(tm * grp)])  19 us
    ppermute x4, starting transfers between devices, along(): return lax.ppermute(value, axis, pairs)  8.16 us
    unnamed x12, local copies, waits for them, and re-layouts  3.68 us
    ppermute x1, starting transfers between devices, from_bands(): got = lax.ppermute(parts[0], 'grp', [(0, 1), (1, 0)])  3.03 us
  transfers between devices with their start and end apart: 33, of which 14 were waited for; matrix products, arithmetic and copies ran while one was open for 1% of the time, Pallas kernels for 27%

profile of v3, /device:TPU:0, one launch (start us, length us, event | category | flops | bytes accessed | tf_op | source)
XLA Modules:
  0.0 99.7 jit_solution(2441319249641806506)
XLA Ops:
  1.3 1.0 %reshape.35.cot_ref = bf16[16,32,256]{2,1,0:T(8,128)(2,1)S(1)} reshape(bf16[16,8,4,256]{3,2,1,0:T(4,128)(2,1)} %param.11) | data formatting | bytes 524288 | tf_op jit(solution)/shard_map/reshape | solution.py:471
  2.3 1.2 %copy-done.5 = bf16[16,16,8,256]{3,2,1,0:T(8,128)(2,1)S(1)} copy-done((bf16[16,16,8,256]{3,2,1,0:T(8,128)(2,1)S(1)}, bf16[16,16,8,256]{3,2,1,0:T(8,128)(2,1)}, u32[]{:S(2)}) %copy-start.5) | copy-done | bytes 1048600
  3.9 3.0 %collective-permute-start = (bf16[128,256]{1,0:T(8,128)(2,1)S(1)}, bf16[128,256]{1,0:T(8,128)(2,1)S(1)}, u32[]{:S(2)}, u32[]{:S(2)}) collective-permute-start(bf16[128,256]{1,0:T(8,128)(2,1)S(1)} %get-tuple-element.43), channel_id=1, source_target_pairs={{0,1},{1,0},{2,3},{3,2},{4,5},{5,4},{6,7},{7,6},{8,9},{9,8},{10,11... | collective-permute-start | bytes 196616 | tf_op jit(solution)/shard_map/ppermute | solution.py:462
  6.9 1.3 %collective-permute-start.2 = (bf16[2,32,256]{2,1,0:T(8,128)(2,1)S(1)}, bf16[2,32,256]{2,1,0:T(8,128)(2,1)S(1)}, u32[]{:S(2)}, u32[]{:S(2)}) collective-permute-start(bf16[2,32,256]{2,1,0:T(8,128)(2,1)S(1)} %get-tuple-element.41._), channel_id=1, source_target_pairs={{2,0},{4,2},{6,4},{8,6},{10,8},{12,10},{14,12},{16,14},{18,16},{20... | collective-permute-start | bytes 98312 | tf_op jit(solution)/shard_map/ppermute | solution.py:457
  8.2 3.4 %acts.1 = (bf16[16,8,16,256]{3,2,1,0:T(8,128)(2,1)S(1)}, bf16[18,10,16,256]{3,2,1,0:T(8,128)(2,1)S(1)}, bf16[256,2304]{1,0:T(8,128)(2,1)S(1)}) custom-call(s32[1]{0:T(128)S(6)} %copy.17.count_ref, bf16[16,128,256]{2,1,0:T(8,128)(2,1)S(1)} %bitcast.15, bf16[2,32,256]{2,1,0:T(8,128)(2,1)S(1)} %get-tuple-element.41._), custom_call_target="tpu_custom_call" | custom-call | flops 536870912 | bytes 4751364 | tf_op jit(solution)/shard_map/acts/pallas_call | solution.py:378
  11.6 3.8 %spatial.1 = (bf16[18,10,16,256]{3,2,1,0:T(8,128)(2,1)S(1)}, bf16[256,2304]{1,0:T(8,128)(2,1)S(1)}, bf16[16,8,16,256]{3,2,1,0:T(8,128)(2,1)S(1)}, bf16[8,32,256]{2,1,0:T(8,128)(2,1)S(1)}) custom-call(s32[1]{0:T(128)S(6)} %copy.17.count_ref, bf16[128,256]{1,0:T(8,128)(2,1)S(1)} %collective-permute-done.top_ref.bot_ref, ...), custom_call_target="tpu_custom_call", output_to_operand_aliasing={{0}: (3, {}), {1}: (4, {})} | custom-call | flops 2415919104 | bytes 7798788 | tf_op jit(solution)/shard_map/spatial/pallas_call | solution.py:378
  15.5 3.0 %collective-permute-start.1 = (bf16[8,32,256]{2,1,0:T(8,128)(2,1)S(1)}, bf16[8,32,256]{2,1,0:T(8,128)(2,1)S(1)}, u32[]{:S(2)}, u32[]{:S(2)}) collective-permute-start(bf16[8,32,256]{2,1,0:T(8,128)(2,1)S(1)} %get-tuple-element.47), channel_id=1, source_target_pairs={{0,2},{2,4},{4,6},{6,8},{8,10},{10,12},{12,14},{14,16},{16,18},{18... | collective-permute-start | bytes 393224 | tf_op jit(solution)/shard_map/ppermute | solution.py:457
  18.5 5.0 %grad_spatial.1 = (bf16[8,4,16,256]{3,2,1,0:T(8,128)(2,1)S(1)}, bf16[16,8,16,256]{3,2,1,0:T(8,128)(2,1)S(1)}, bf16[16,10,16,256]{3,2,1,0:T(8,128)(2,1)S(1)}, bf1...) custom-call(s32[1]{0:T(128)S(6)} %copy.17.count_ref, ...), custom_call_target="tpu_custom_call" | custom-call | flops 3758096384 | bytes 6258692 | tf_op jit(solution)/shard_map/grad_spatial/pallas_call | solution.py:378
  23.5 1.2 %collective-permute-start.5 = (bf16[16,9,16,128]{3,2,1,0:T(8,128)(2,1)S(1)}, bf16[16,9,16,128]{3,2,1,0:T(8,128)(2,1)S(1)}, u32[]{:S(2)}, u32[]{:S(2)}) collective-permute-start(bf16[16,9,16,128]{3,2,1,0:T(8,128)(2,1)S(1)} %get-tuple-element.51._), channel_id=1, source_target_pairs={{0,2},{1,3},{2,0},{3,1},{4,6},{5,7},{6,4},{7,5},{8,10},{9,11},{10,... | collective-permute-start | bytes 1769480 | tf_op jit(solution)/shard_map/ppermute | solution.py:402
  24.7 5.0 %forward.1 = (bf16[16,32,256]{2,1,0:T(8,128)(2,1)S(1)}, bf16[16,7,16,128]{3,2,1,0:T(8,128)(2,1)S(1)}, bf16[16,7,16,128]{3,2,1,0:T(8,128)(2,1)S(1)}) custom-call(s32[1]{0:T(128)S(6)} %copy.17.count_ref, bf16[16,8,16,256]{3,2,1,0:T(8,128)(2,1)S(1)} %get-tuple-element.42.xt_ref, bf16[16,8,16,256]{3,2,1,0:T(8,128)(2,1)S(1)} %get-tuple-element.46.sp_ref, ...), custom_call_target="tpu_custom_call" | custom-call | flops 2684354560 | bytes 5636100 | tf_op jit(solution)/shard_map/forward/pallas_call | solution.py:378
  29.8 2.4 %collective-permute-start.4 = (bf16[64,256]{1,0:T(8,128)(2,1)S(1)}, bf16[64,256]{1,0:T(8,128)(2,1)S(1)}, u32[]{:S(2)}, u32[]{:S(2)}) collective-permute-start(bf16[64,256]{1,0:T(8,128)(2,1)S(1)} %get-tuple-element.55), channel_id=1, source_target_pairs={{0,1},{2,3},{4,5},{6,7},{8,9},{10,11},{12,13},{14,15},{16,17},{18,... | collective-permute-start | bytes 98312 | tf_op jit(solution)/shard_map/ppermute | solution.py:457
  32.4 2.3 %collective-permute-start.6 = (bf16[4,9,16,128]{3,2,1,0:T(8,128)(2,1)S(1)}, bf16[4,9,16,128]{3,2,1,0:T(8,128)(2,1)S(1)}, u32[]{:S(2)}, u32[]{:S(2)}) collective-permute-start(bf16[4,9,16,128]{3,2,1,0:T(8,128)(2,1)S(1)} %get-tuple-element.60), channel_id=1, source_target_pairs={{0,4},{1,5},{2,6},{3,7},{4,0},{5,1},{6,2},{7,3},{8,12},{9,13},{10,... | collective-permute-start | bytes 442376 | tf_op jit(solution)/shard_map/ppermute | solution.py:402
  34.7 1.5 %collective-permute-start.8 = (bf16[4,9,16,128]{3,2,1,0:T(8,128)(2,1)S(1)}, bf16[4,9,16,128]{3,2,1,0:T(8,128)(2,1)S(1)}, u32[]{:S(2)}, u32[]{:S(2)}) collective-permute-start(bf16[4,9,16,128]{3,2,1,0:T(8,128)(2,1)S(1)} %get-tuple-element.58.rest_0_), channel_id=1, source_target_pairs={{0,5},{1,4},{2,7},{3,6},{4,1},{5,0},{6,3},{7,2},{8,13},{9,12},{10,... | collective-permute-start | bytes 442376 | tf_op jit(solution)/shard_map/ppermute | solution.py:402
  36.2 3.8 %grad_x_0.1.rest_0_ = bf16[16,128,256]{2,1,0:T(8,128)(2,1)} custom-call(s32[1]{0:T(128)S(6)} %copy.17.count_ref, bf16[16,8,16,256]{3,2,1,0:T(8,128)(2,1)S(1)} %get-tuple-element.42.xt_ref, bf16[16,8,16,256]{3,2,1,0:T(8,128)(2,1)S(1)} %get-tuple-element.50.gy_ref, bf16[16,10,16,256]{3,2,1,0:T(8,128)(2,1)S(1)} %get-tuple-element.53.gs_ref, ...), custom_call_target="tpu_custom_call" | custom-call | flops 1342177280 | bytes 6586372 | tf_op jit(solution)/shard_map/grad_x_0/pallas_call | solution.py:378
  40.0 1.2 %copy-done = bf16[16,128,256]{2,1,0:T(8,128)(2,1)S(1)} copy-done((bf16[16,128,256]{2,1,0:T(8,128)(2,1)S(1)}, bf16[16,128,256]{2,1,0:T(8,128)(2,1)}, u32[]{:S(2)}) %copy-start) | copy-done | bytes 1048600
  41.3 2.0 %collective-permute-start.20 = (bf16[4,7,16,128]{3,2,1,0:T(8,128)(2,1)S(1)}, bf16[4,7,16,128]{3,2,1,0:T(8,128)(2,1)S(1)}, u32[]{:S(2)}, u32[]{:S(2)}) collective-permute-start(bf16[4,7,16,128]{3,2,1,0:T(8,128)(2,1)S(1)} %get-tuple-element.69), channel_id=1, source_target_pairs={{0,4},{1,5},{2,6},{3,7},{4,0},{5,1},{6,2},{7,3},{8,12},{9,13},{10,... | collective-permute-start | bytes 344072 | tf_op jit(solution)/shard_map/ppermute | solution.py:402
  43.6 1.6 %collective-permute-start.10 = (bf16[9,16,128]{2,1,0:T(8,128)(2,1)S(1)}, bf16[9,16,128]{2,1,0:T(8,128)(2,1)S(1)}, u32[]{:S(2)}, u32[]{:S(2)}) collective-permute-start(bf16[9,16,128]{2,1,0:T(8,128)(2,1)S(1)} %get-tuple-element.67), channel_id=1, source_target_pairs={{0,8},{1,9},{2,10},{3,11},{4,12},{5,13},{6,14},{7,15},{8,0},{9,1},... | collective-permute-start | bytes 110600 | tf_op jit(solution)/shard_map/ppermute | solution.py:402
  45.2 1.1 %collective-permute-start.11 = (bf16[9,16,128]{2,1,0:T(8,128)(2,1)S(1)}, bf16[9,16,128]{2,1,0:T(8,128)(2,1)S(1)}, u32[]{:S(2)}, u32[]{:S(2)}) collective-permute-start(bf16[9,16,128]{2,1,0:T(8,128)(2,1)S(1)} %get-tuple-element.68), channel_id=1, source_target_pairs={{0,16},{1,17},{2,18},{3,19},{4,20},{5,21},{6,22},{7,23},{8,24},{9,... | collective-permute-start | bytes 110600 | tf_op jit(solution)/shard_map/ppermute | solution.py:402
  46.4 1.7 %collective-permute-start.12 = (bf16[9,16,128]{2,1,0:T(8,128)(2,1)S(1)}, bf16[9,16,128]{2,1,0:T(8,128)(2,1)S(1)}, u32[]{:S(2)}, u32[]{:S(2)}) collective-permute-start(bf16[9,16,128]{2,1,0:T(8,128)(2,1)S(1)} %get-tuple-element.64.rest_1_), channel_id=1, source_target_pairs={{0,24},{1,25},{2,26},{3,27},{4,28},{5,29},{6,30},{7,31},{8,16},{9,... | collective-permute-start | bytes 110600 | tf_op jit(solution)/shard_map/ppermute | solution.py:402
  48.1 2.8 %collective-permute-done.11.c_ref = bf16[9,16,128]{2,1,0:T(8,128)(2,1)S(1)} collective-permute-done((bf16[9,16,128]{2,1,0:T(8,128)(2,1)S(1)}, bf16[9,16,128]{2,1,0:T(8,128)(2,1)S(1)}, u32[]{:S(2)}, u32[]{:S(2)}) %collective-permute-start.11) | collective-permute-done | bytes 36896 | tf_op jit(solution)/shard_map/ppermute | solution.py:402
  50.8 1.3 %collective-permute-done.12.d_ref = bf16[9,16,128]{2,1,0:T(8,128)(2,1)S(1)} collective-permute-done((bf16[9,16,128]{2,1,0:T(8,128)(2,1)S(1)}, bf16[9,16,128]{2,1,0:T(8,128)(2,1)S(1)}, u32[]{:S(2)}, u32[]{:S(2)}) %collective-permute-start.12) | collective-permute-done | bytes 36896 | tf_op jit(solution)/shard_map/ppermute | solution.py:402
  52.2 1.7 %collective-permute-start.15 = (bf16[9,16,128]{2,1,0:T(8,128)(2,1)S(1)}, bf16[9,16,128]{2,1,0:T(8,128)(2,1)S(1)}, u32[]{:S(2)}, u32[]{:S(2)}) collective-permute-start(bf16[9,16,128]{2,1,0:T(8,128)(2,1)S(1)} %line_sum.2.a_ref), channel_id=1, source_target_pairs={{0,24},{1,25},{2,26},{3,27},{4,28},{5,29},{6,30},{7,31},{8,16},{9,... | collective-permute-start | bytes 110600 | tf_op jit(solution)/shard_map/ppermute | solution.py:402
  53.9 2.7 %collective-permute-start.13 = (bf16[9,16,128]{2,1,0:T(8,128)(2,1)S(1)}, bf16[9,16,128]{2,1,0:T(8,128)(2,1)S(1)}, u32[]{:S(2)}, u32[]{:S(2)}) collective-permute-start(bf16[9,16,128]{2,1,0:T(8,128)(2,1)S(1)} %line_sum.2.a_ref), channel_id=1, source_target_pairs={{0,8},{1,9},{2,10},{3,11},{4,12},{5,13},{6,14},{7,15},{8,0},{9,1},... | collective-permute-start | bytes 110600 | tf_op jit(solution)/shard_map/ppermute | solution.py:402
  56.6 1.5 %collective-permute-start.3 = (bf16[64,256]{1,0:T(8,128)(2,1)S(1)}, bf16[64,256]{1,0:T(8,128)(2,1)S(1)}, u32[]{:S(2)}, u32[]{:S(2)}) collective-permute-start(bf16[64,256]{1,0:T(8,128)(2,1)S(1)} %get-tuple-element.54), channel_id=1, source_target_pairs={{1,0},{3,2},{5,4},{7,6},{9,8},{11,10},{13,12},{15,14},{17,16},{19,... | collective-permute-start | bytes 98312 | tf_op jit(solution)/shard_map/ppermute | solution.py:457
  58.1 2.7 %collective-permute-start.21 = (bf16[4,7,16,128]{3,2,1,0:T(8,128)(2,1)S(1)}, bf16[4,7,16,128]{3,2,1,0:T(8,128)(2,1)S(1)}, u32[]{:S(2)}, u32[]{:S(2)}) collective-permute-start(bf16[4,7,16,128]{3,2,1,0:T(8,128)(2,1)S(1)} %get-tuple-element.70), channel_id=1, source_target_pairs={{0,1},{1,0},{2,3},{3,2},{4,5},{5,4},{6,7},{7,6},{8,9},{9,8},{10,11... | collective-permute-start | bytes 344072 | tf_op jit(solution)/shard_map/ppermute | solution.py:402
  60.8 0.8 collective-permute-start.22
  61.6 2.2 %collective-permute-start.18 = (bf16[4,9,16,128]{3,2,1,0:T(8,128)(2,1)S(1)}, bf16[4,9,16,128]{3,2,1,0:T(8,128)(2,1)S(1)}, u32[]{:S(2)}, u32[]{:S(2)}) collective-permute-start(bf16[4,9,16,128]{3,2,1,0:T(8,128)(2,1)S(1)} %line_gather.2.a_ref), channel_id=1, source_target_pairs={{0,5},{1,4},{2,7},{3,6},{4,1},{5,0},{6,3},{7,2},{8,13},{9,12},{10,... | collective-permute-start | bytes 442376 | tf_op jit(solution)/shard_map/ppermute | solution.py:402
  63.8 0.6 collective-permute-done.3.halo_ref
  64.5 0.7 collective-permute-start.16
  65.2 3.8 %grad_x_1.1.refs_4_ = bf16[16,128,256]{2,1,0:T(8,128)(2,1)} custom-call(s32[1]{0:T(128)S(6)} %copy.17.count_ref, bf16[16,8,16,256]{3,2,1,0:T(8,128)(2,1)S(1)} %get-tuple-element.42.xt_ref, bf16[16,8,16,256]{3,2,1,0:T(8,128)(2,1)S(1)} %get-tuple-element.50.gy_ref, ...), custom_call_target="tpu_custom_call", output_to_operand_aliasing={{}: (8, {})} | custom-call | flops 1342177280 | bytes 6586372 | tf_op jit(solution)/shard_map/grad_x_1/pallas_call | solution.py:378
  69.0 0.8 collective-permute-done.21.refs_2_
  69.8 1.2 %copy-done.1 = bf16[16,128,256]{2,1,0:T(8,128)(2,1)S(1)} copy-done((bf16[16,128,256]{2,1,0:T(8,128)(2,1)S(1)}, bf16[16,128,256]{2,1,0:T(8,128)(2,1)}, u32[]{:S(2)}) %copy-start.1) | copy-done | bytes 1048600
  71.4 1.3 %collective-permute-start.24 = (bf16[7,16,128]{2,1,0:T(8,128)(2,1)S(1)}, bf16[7,16,128]{2,1,0:T(8,128)(2,1)S(1)}, u32[]{:S(2)}, u32[]{:S(2)}) collective-permute-start(bf16[7,16,128]{2,1,0:T(8,128)(2,1)S(1)} %get-tuple-element.73), channel_id=1, source_target_pairs={{0,16},{1,17},{2,18},{3,19},{4,20},{5,21},{6,22},{7,23},{8,24},{9,... | collective-permute-start | bytes 86024 | tf_op jit(solution)/shard_map/ppermute | solution.py:402
  72.7 2.3 %collective-permute-done.23.b_ref = bf16[7,16,128]{2,1,0:T(8,128)(2,1)S(1)} collective-permute-done((bf16[7,16,128]{2,1,0:T(8,128)(2,1)S(1)}, bf16[7,16,128]{2,1,0:T(8,128)(2,1)S(1)}, u32[]{:S(2)}, u32[]{:S(2)}) %collective-permute-start.23) | collective-permute-done | bytes 28704 | tf_op jit(solution)/shard_map/ppermute | solution.py:402
  75.0 1.0 %collective-permute-start.25 = (bf16[7,16,128]{2,1,0:T(8,128)(2,1)S(1)}, bf16[7,16,128]{2,1,0:T(8,128)(2,1)S(1)}, u32[]{:S(2)}, u32[]{:S(2)}) collective-permute-start(bf16[7,16,128]{2,1,0:T(8,128)(2,1)S(1)} %get-tuple-element.74), channel_id=1, source_target_pairs={{0,24},{1,25},{2,26},{3,27},{4,28},{5,29},{6,30},{7,31},{8,16},{9,... | collective-permute-start | bytes 86024 | tf_op jit(solution)/shard_map/ppermute | solution.py:402
  76.1 4.5 %collective-permute-done.25.d_ref = bf16[7,16,128]{2,1,0:T(8,128)(2,1)S(1)} collective-permute-done((bf16[7,16,128]{2,1,0:T(8,128)(2,1)S(1)}, bf16[7,16,128]{2,1,0:T(8,128)(2,1)S(1)}, u32[]{:S(2)}, u32[]{:S(2)}) %collective-permute-start.25) | collective-permute-done | bytes 28704 | tf_op jit(solution)/shard_map/ppermute | solution.py:402
  80.7 1.4 %collective-permute-start.28 = (bf16[7,16,128]{2,1,0:T(8,128)(2,1)S(1)}, bf16[7,16,128]{2,1,0:T(8,128)(2,1)S(1)}, u32[]{:S(2)}, u32[]{:S(2)}) collective-permute-start(bf16[7,16,128]{2,1,0:T(8,128)(2,1)S(1)} %line_sum.3.a_ref), channel_id=1, source_target_pairs={{0,24},{1,25},{2,26},{3,27},{4,28},{5,29},{6,30},{7,31},{8,16},{9,... | collective-permute-start | bytes 86024 | tf_op jit(solution)/shard_map/ppermute | solution.py:402
  82.1 3.1 %collective-permute-start.26 = (bf16[7,16,128]{2,1,0:T(8,128)(2,1)S(1)}, bf16[7,16,128]{2,1,0:T(8,128)(2,1)S(1)}, u32[]{:S(2)}, u32[]{:S(2)}) collective-permute-start(bf16[7,16,128]{2,1,0:T(8,128)(2,1)S(1)} %line_sum.3.a_ref), channel_id=1, source_target_pairs={{0,8},{1,9},{2,10},{3,11},{4,12},{5,13},{6,14},{7,15},{8,0},{9,1},... | collective-permute-start | bytes 86024 | tf_op jit(solution)/shard_map/ppermute | solution.py:402
  85.3 1.1 %collective-permute-done.28.d_ref = bf16[7,16,128]{2,1,0:T(8,128)(2,1)S(1)} collective-permute-done((bf16[7,16,128]{2,1,0:T(8,128)(2,1)S(1)}, bf16[7,16,128]{2,1,0:T(8,128)(2,1)S(1)}, u32[]{:S(2)}, u32[]{:S(2)}) %collective-permute-start.28) | collective-permute-done | bytes 28704 | tf_op jit(solution)/shard_map/ppermute | solution.py:402
  86.4 0.7 collective-permute-done.27.c_ref
  87.3 2.1 %collective-permute-start.31 = (bf16[4,7,16,128]{3,2,1,0:T(8,128)(2,1)S(1)}, bf16[4,7,16,128]{3,2,1,0:T(8,128)(2,1)S(1)}, u32[]{:S(2)}, u32[]{:S(2)}) collective-permute-start(bf16[4,7,16,128]{3,2,1,0:T(8,128)(2,1)S(1)} %line_gather.3.a_ref), channel_id=1, source_target_pairs={{0,5},{1,4},{2,7},{3,6},{4,1},{5,0},{6,3},{7,2},{8,13},{9,12},{10,... | collective-permute-start | bytes 344072 | tf_op jit(solution)/shard_map/ppermute | solution.py:402
  89.4 1.5 %collective-permute-start.29 = (bf16[4,7,16,128]{3,2,1,0:T(8,128)(2,1)S(1)}, bf16[4,7,16,128]{3,2,1,0:T(8,128)(2,1)S(1)}, u32[]{:S(2)}, u32[]{:S(2)}) collective-permute-start(bf16[4,7,16,128]{3,2,1,0:T(8,128)(2,1)S(1)} %line_gather.3.a_ref), channel_id=1, source_target_pairs={{0,4},{1,5},{2,6},{3,7},{4,0},{5,1},{6,2},{7,3},{8,12},{9,13},{10,... | collective-permute-start | bytes 344072 | tf_op jit(solution)/shard_map/ppermute | solution.py:402
  90.8 3.0 %collective-permute-done.31.d_ref = bf16[4,7,16,128]{3,2,1,0:T(8,128)(2,1)S(1)} collective-permute-done((bf16[4,7,16,128]{3,2,1,0:T(8,128)(2,1)S(1)}, bf16[4,7,16,128]{3,2,1,0:T(8,128)(2,1)S(1)}, u32[]{:S(2)}, u32[]{:S(2)}) %collective-permute-start.31) | collective-permute-done | bytes 114720 | tf_op jit(solution)/shard_map/ppermute | solution.py:402
  93.9 0.9 collective-permute-done.30.c_ref
  94.9 0.8 reshape.38
  95.7 1.0 %collective-permute-done.32.got_ref = bf16[16,7,16,128]{3,2,1,0:T(8,128)(2,1)S(1)} collective-permute-done((bf16[16,7,16,128]{3,2,1,0:T(8,128)(2,1)S(1)}, bf16[16,7,16,128]{3,2,1,0:T(8,128)(2,1)S(1)}, u32[]{:S(2)}, u32[]{:S(2)}) %collective-permute-start.32) | collective-permute-done | bytes 458784 | tf_op jit(solution)/shard_map/ppermute | solution.py:402
  96.7 1.3 %finish.3 = (f32[3,256,256]{2,1,0:T(8,128)}, f32[4,256,256]{2,1,0:T(8,128)}) custom-call(bf16[16,7,16,128]{3,2,1,0:T(8,128)(2,1)S(1)} %plane_gather.3.own_ref, bf16[16,7,16,128]{3,2,1,0:T(8,128)(2,1)S(1)} %collective-permute-done.32.got_ref), custom_call_target="tpu_custom_call" | custom-call | bytes 2752512 | tf_op jit(solution)/shard_map/finish/pallas_call | solution.py:378
  98.0 1.5 %finish.2 = f32[9,256,256]{2,1,0:T(8,128)} custom-call(bf16[16,9,16,128]{3,2,1,0:T(8,128)(2,1)S(1)} %plane_gather.2.own_ref, bf16[16,9,16,128]{3,2,1,0:T(8,128)(2,1)S(1)} %collective-permute-done.19.got_ref), custom_call_target="tpu_custom_call" | custom-call | bytes 3538944 | tf_op jit(solution)/shard_map/finish/pallas_call | solution.py:378
  (51 shorter events, 2.0 us)
Async XLA Ops:
  2.3 1.2 %copy-start.5 = (bf16[16,16,8,256]{3,2,1,0:T(8,128)(2,1)S(1)}, bf16[16,16,8,256]{3,2,1,0:T(8,128)(2,1)}, u32[]{:S(2)}) copy-start(bf16[16,16,8,256]{3,2,1,0:T(8,128)(2,1)} %param.6) | copy-start | bytes 3145732
  3.9 7.7 %copy-start.2 = (bf16[3,3,256,256]{3,2,1,0:T(8,128)(2,1)S(1)}, bf16[3,3,256,256]{3,2,1,0:T(8,128)(2,1)}, u32[]{:S(2)}) copy-start(bf16[3,3,256,256]{3,2,1,0:T(8,128)(2,1)} %param.8) | copy-start | bytes 3538948
  3.9 7.7 %collective-permute-start = (bf16[128,256]{1,0:T(8,128)(2,1)S(1)}, bf16[128,256]{1,0:T(8,128)(2,1)S(1)}, u32[]{:S(2)}, u32[]{:S(2)}) collective-permute-start(bf16[128,256]{1,0:T(8,128)(2,1)S(1)} %get-tuple-element.43), channel_id=1, source_target_pairs={{0,1},{1,0},{2,3},{3,2},{4,5},{5,4},{6,7},{7,6},{8,9},{9,8},{10,11... | collective-permute-start | bytes 196616 | tf_op jit(solution)/shard_map/ppermute | solution.py:462
  6.9 11.5 %collective-permute-start.2 = (bf16[2,32,256]{2,1,0:T(8,128)(2,1)S(1)}, bf16[2,32,256]{2,1,0:T(8,128)(2,1)S(1)}, u32[]{:S(2)}, u32[]{:S(2)}) collective-permute-start(bf16[2,32,256]{2,1,0:T(8,128)(2,1)S(1)} %get-tuple-element.41._), channel_id=1, source_target_pairs={{2,0},{4,2},{6,4},{8,6},{10,8},{12,10},{14,12},{16,14},{18,16},{20... | collective-permute-start | bytes 98312 | tf_op jit(solution)/shard_map/ppermute | solution.py:457
  11.6 6.9 %copy-start.3 = (bf16[2,2,256,256]{3,2,1,0:T(8,128)(2,1)S(1)}, bf16[2,2,256,256]{3,2,1,0:T(8,128)(2,1)}, u32[]{:S(2)}) copy-start(bf16[2,2,256,256]{3,2,1,0:T(8,128)(2,1)} %param.10) | copy-start | bytes 1572868
  11.6 6.9 %copy-start.4 = (bf16[3,256,256]{2,1,0:T(8,128)(2,1)S(1)}, bf16[3,256,256]{2,1,0:T(8,128)(2,1)}, u32[]{:S(2)}) copy-start(bf16[3,256,256]{2,1,0:T(8,128)(2,1)} %wt_ref.7) | copy-start | bytes 1179652
  15.5 9.3 %collective-permute-start.1 = (bf16[8,32,256]{2,1,0:T(8,128)(2,1)S(1)}, bf16[8,32,256]{2,1,0:T(8,128)(2,1)S(1)}, u32[]{:S(2)}, u32[]{:S(2)}) collective-permute-start(bf16[8,32,256]{2,1,0:T(8,128)(2,1)S(1)} %get-tuple-element.47), channel_id=1, source_target_pairs={{0,2},{2,4},{4,6},{6,8},{8,10},{10,12},{12,14},{14,16},{16,18},{18... | collective-permute-start | bytes 393224 | tf_op jit(solution)/shard_map/ppermute | solution.py:457
  23.5 8.7 %collective-permute-start.5 = (bf16[16,9,16,128]{3,2,1,0:T(8,128)(2,1)S(1)}, bf16[16,9,16,128]{3,2,1,0:T(8,128)(2,1)S(1)}, u32[]{:S(2)}, u32[]{:S(2)}) collective-permute-start(bf16[16,9,16,128]{3,2,1,0:T(8,128)(2,1)S(1)} %get-tuple-element.51._), channel_id=1, source_target_pairs={{0,2},{1,3},{2,0},{3,1},{4,6},{5,7},{6,4},{7,5},{8,10},{9,11},{10,... | collective-permute-start | bytes 1769480 | tf_op jit(solution)/shard_map/ppermute | solution.py:402
  29.8 10.2 %collective-permute-start.9 = (bf16[16,7,16,128]{3,2,1,0:T(8,128)(2,1)S(1)}, bf16[16,7,16,128]{3,2,1,0:T(8,128)(2,1)S(1)}, u32[]{:S(2)}, u32[]{:S(2)}) collective-permute-start(bf16[16,7,16,128]{3,2,1,0:T(8,128)(2,1)S(1)} %get-tuple-element.57.rest_0_.rest_1_), channel_id=1, source_target_pairs={{0,2},{1,3},{2,0},{3,1},{4,6},{5,7},{6,4},{7,5},{8,10},{9,11},{10,... | collective-permute-start | bytes 1376264 | tf_op jit(solution)/shard_map/ppermute | solution.py:402
  29.8 6.4 %collective-permute-start.4 = (bf16[64,256]{1,0:T(8,128)(2,1)S(1)}, bf16[64,256]{1,0:T(8,128)(2,1)S(1)}, u32[]{:S(2)}, u32[]{:S(2)}) collective-permute-start(bf16[64,256]{1,0:T(8,128)(2,1)S(1)} %get-tuple-element.55), channel_id=1, source_target_pairs={{0,1},{2,3},{4,5},{6,7},{8,9},{10,11},{12,13},{14,15},{16,17},{18,... | collective-permute-start | bytes 98312 | tf_op jit(solution)/shard_map/ppermute | solution.py:457
  32.4 11.0 %collective-permute-start.6 = (bf16[4,9,16,128]{3,2,1,0:T(8,128)(2,1)S(1)}, bf16[4,9,16,128]{3,2,1,0:T(8,128)(2,1)S(1)}, u32[]{:S(2)}, u32[]{:S(2)}) collective-permute-start(bf16[4,9,16,128]{3,2,1,0:T(8,128)(2,1)S(1)} %get-tuple-element.60), channel_id=1, source_target_pairs={{0,4},{1,5},{2,6},{3,7},{4,0},{5,1},{6,2},{7,3},{8,12},{9,13},{10,... | collective-permute-start | bytes 442376 | tf_op jit(solution)/shard_map/ppermute | solution.py:402
  34.7 8.8 %collective-permute-start.7 = (bf16[4,9,16,128]{3,2,1,0:T(8,128)(2,1)S(1)}, bf16[4,9,16,128]{3,2,1,0:T(8,128)(2,1)S(1)}, u32[]{:S(2)}, u32[]{:S(2)}) collective-permute-start(bf16[4,9,16,128]{3,2,1,0:T(8,128)(2,1)S(1)} %get-tuple-element.61), channel_id=1, source_target_pairs={{0,1},{1,0},{2,3},{3,2},{4,5},{5,4},{6,7},{7,6},{8,9},{9,8},{10,11... | collective-permute-start | bytes 442376 | tf_op jit(solution)/shard_map/ppermute | solution.py:402
  34.7 8.8 %collective-permute-start.8 = (bf16[4,9,16,128]{3,2,1,0:T(8,128)(2,1)S(1)}, bf16[4,9,16,128]{3,2,1,0:T(8,128)(2,1)S(1)}, u32[]{:S(2)}, u32[]{:S(2)}) collective-permute-start(bf16[4,9,16,128]{3,2,1,0:T(8,128)(2,1)S(1)} %get-tuple-element.58.rest_0_), channel_id=1, source_target_pairs={{0,5},{1,4},{2,7},{3,6},{4,1},{5,0},{6,3},{7,2},{8,13},{9,12},{10,... | collective-permute-start | bytes 442376 | tf_op jit(solution)/shard_map/ppermute | solution.py:402
  40.0 1.2 %copy-start = (bf16[16,128,256]{2,1,0:T(8,128)(2,1)S(1)}, bf16[16,128,256]{2,1,0:T(8,128)(2,1)}, u32[]{:S(2)}) copy-start(bf16[16,128,256]{2,1,0:T(8,128)(2,1)} %grad_x_0.1.rest_0_) | copy-start | bytes 3145732
  41.3 23.1 %collective-permute-start.20 = (bf16[4,7,16,128]{3,2,1,0:T(8,128)(2,1)S(1)}, bf16[4,7,16,128]{3,2,1,0:T(8,128)(2,1)S(1)}, u32[]{:S(2)}, u32[]{:S(2)}) collective-permute-start(bf16[4,7,16,128]{3,2,1,0:T(8,128)(2,1)S(1)} %get-tuple-element.69), channel_id=1, source_target_pairs={{0,4},{1,5},{2,6},{3,7},{4,0},{5,1},{6,2},{7,3},{8,12},{9,13},{10,... | collective-permute-start | bytes 344072 | tf_op jit(solution)/shard_map/ppermute | solution.py:402
  43.6 4.5 %collective-permute-start.10 = (bf16[9,16,128]{2,1,0:T(8,128)(2,1)S(1)}, bf16[9,16,128]{2,1,0:T(8,128)(2,1)S(1)}, u32[]{:S(2)}, u32[]{:S(2)}) collective-permute-start(bf16[9,16,128]{2,1,0:T(8,128)(2,1)S(1)} %get-tuple-element.67), channel_id=1, source_target_pairs={{0,8},{1,9},{2,10},{3,11},{4,12},{5,13},{6,14},{7,15},{8,0},{9,1},... | collective-permute-start | bytes 110600 | tf_op jit(solution)/shard_map/ppermute | solution.py:402
  45.2 5.6 %collective-permute-start.11 = (bf16[9,16,128]{2,1,0:T(8,128)(2,1)S(1)}, bf16[9,16,128]{2,1,0:T(8,128)(2,1)S(1)}, u32[]{:S(2)}, u32[]{:S(2)}) collective-permute-start(bf16[9,16,128]{2,1,0:T(8,128)(2,1)S(1)} %get-tuple-element.68), channel_id=1, source_target_pairs={{0,16},{1,17},{2,18},{3,19},{4,20},{5,21},{6,22},{7,23},{8,24},{9,... | collective-permute-start | bytes 110600 | tf_op jit(solution)/shard_map/ppermute | solution.py:402
  46.4 5.8 %collective-permute-start.12 = (bf16[9,16,128]{2,1,0:T(8,128)(2,1)S(1)}, bf16[9,16,128]{2,1,0:T(8,128)(2,1)S(1)}, u32[]{:S(2)}, u32[]{:S(2)}) collective-permute-start(bf16[9,16,128]{2,1,0:T(8,128)(2,1)S(1)} %get-tuple-element.64.rest_1_), channel_id=1, source_target_pairs={{0,24},{1,25},{2,26},{3,27},{4,28},{5,29},{6,30},{7,31},{8,16},{9,... | collective-permute-start | bytes 110600 | tf_op jit(solution)/shard_map/ppermute | solution.py:402
  52.2 5.9 %collective-permute-start.15 = (bf16[9,16,128]{2,1,0:T(8,128)(2,1)S(1)}, bf16[9,16,128]{2,1,0:T(8,128)(2,1)S(1)}, u32[]{:S(2)}, u32[]{:S(2)}) collective-permute-start(bf16[9,16,128]{2,1,0:T(8,128)(2,1)S(1)} %line_sum.2.a_ref), channel_id=1, source_target_pairs={{0,24},{1,25},{2,26},{3,27},{4,28},{5,29},{6,30},{7,31},{8,16},{9,... | collective-permute-start | bytes 110600 | tf_op jit(solution)/shard_map/ppermute | solution.py:402
  53.9 6.9 %collective-permute-start.14 = (bf16[9,16,128]{2,1,0:T(8,128)(2,1)S(1)}, bf16[9,16,128]{2,1,0:T(8,128)(2,1)S(1)}, u32[]{:S(2)}, u32[]{:S(2)}) collective-permute-start(bf16[9,16,128]{2,1,0:T(8,128)(2,1)S(1)} %line_sum.2.a_ref), channel_id=1, source_target_pairs={{0,16},{1,17},{2,18},{3,19},{4,20},{5,21},{6,22},{7,23},{8,24},{9,... | collective-permute-start | bytes 110600 | tf_op jit(solution)/shard_map/ppermute | solution.py:402
  53.9 7.7 %collective-permute-start.13 = (bf16[9,16,128]{2,1,0:T(8,128)(2,1)S(1)}, bf16[9,16,128]{2,1,0:T(8,128)(2,1)S(1)}, u32[]{:S(2)}, u32[]{:S(2)}) collective-permute-start(bf16[9,16,128]{2,1,0:T(8,128)(2,1)S(1)} %line_sum.2.a_ref), channel_id=1, source_target_pairs={{0,8},{1,9},{2,10},{3,11},{4,12},{5,13},{6,14},{7,15},{8,0},{9,1},... | collective-permute-start | bytes 110600 | tf_op jit(solution)/shard_map/ppermute | solution.py:402
  56.6 7.8 %collective-permute-start.3 = (bf16[64,256]{1,0:T(8,128)(2,1)S(1)}, bf16[64,256]{1,0:T(8,128)(2,1)S(1)}, u32[]{:S(2)}, u32[]{:S(2)}) collective-permute-start(bf16[64,256]{1,0:T(8,128)(2,1)S(1)} %get-tuple-element.54), channel_id=1, source_target_pairs={{1,0},{3,2},{5,4},{7,6},{9,8},{11,10},{13,12},{15,14},{17,16},{19,... | collective-permute-start | bytes 98312 | tf_op jit(solution)/shard_map/ppermute | solution.py:457
  58.1 11.6 %collective-permute-start.21 = (bf16[4,7,16,128]{3,2,1,0:T(8,128)(2,1)S(1)}, bf16[4,7,16,128]{3,2,1,0:T(8,128)(2,1)S(1)}, u32[]{:S(2)}, u32[]{:S(2)}) collective-permute-start(bf16[4,7,16,128]{3,2,1,0:T(8,128)(2,1)S(1)} %get-tuple-element.70), channel_id=1, source_target_pairs={{0,1},{1,0},{2,3},{3,2},{4,5},{5,4},{6,7},{7,6},{8,9},{9,8},{10,11... | collective-permute-start | bytes 344072 | tf_op jit(solution)/shard_map/ppermute | solution.py:402
  60.8 8.9 %collective-permute-start.22 = (bf16[4,7,16,128]{3,2,1,0:T(8,128)(2,1)S(1)}, bf16[4,7,16,128]{3,2,1,0:T(8,128)(2,1)S(1)}, u32[]{:S(2)}, u32[]{:S(2)}) collective-permute-start(bf16[4,7,16,128]{3,2,1,0:T(8,128)(2,1)S(1)} %get-tuple-element.65.rest_2_), channel_id=1, source_target_pairs={{0,5},{1,4},{2,7},{3,6},{4,1},{5,0},{6,3},{7,2},{8,13},{9,12},{10,... | collective-permute-start | bytes 344072 | tf_op jit(solution)/shard_map/ppermute | solution.py:402
  61.6 20.4 %collective-permute-start.18 = (bf16[4,9,16,128]{3,2,1,0:T(8,128)(2,1)S(1)}, bf16[4,9,16,128]{3,2,1,0:T(8,128)(2,1)S(1)}, u32[]{:S(2)}, u32[]{:S(2)}) collective-permute-start(bf16[4,9,16,128]{3,2,1,0:T(8,128)(2,1)S(1)} %line_gather.2.a_ref), channel_id=1, source_target_pairs={{0,5},{1,4},{2,7},{3,6},{4,1},{5,0},{6,3},{7,2},{8,13},{9,12},{10,... | collective-permute-start | bytes 442376 | tf_op jit(solution)/shard_map/ppermute | solution.py:402
  64.5 20.6 %collective-permute-start.17 = (bf16[4,9,16,128]{3,2,1,0:T(8,128)(2,1)S(1)}, bf16[4,9,16,128]{3,2,1,0:T(8,128)(2,1)S(1)}, u32[]{:S(2)}, u32[]{:S(2)}) collective-permute-start(bf16[4,9,16,128]{3,2,1,0:T(8,128)(2,1)S(1)} %line_gather.2.a_ref), channel_id=1, source_target_pairs={{0,1},{1,0},{2,3},{3,2},{4,5},{5,4},{6,7},{7,6},{8,9},{9,8},{10,11... | collective-permute-start | bytes 442376 | tf_op jit(solution)/shard_map/ppermute | solution.py:402
  64.5 20.6 %collective-permute-start.16 = (bf16[4,9,16,128]{3,2,1,0:T(8,128)(2,1)S(1)}, bf16[4,9,16,128]{3,2,1,0:T(8,128)(2,1)S(1)}, u32[]{:S(2)}, u32[]{:S(2)}) collective-permute-start(bf16[4,9,16,128]{3,2,1,0:T(8,128)(2,1)S(1)} %line_gather.2.a_ref), channel_id=1, source_target_pairs={{0,4},{1,5},{2,6},{3,7},{4,0},{5,1},{6,2},{7,3},{8,12},{9,13},{10,... | collective-permute-start | bytes 442376 | tf_op jit(solution)/shard_map/ppermute | solution.py:402
  69.7 1.2 %copy-start.1 = (bf16[16,128,256]{2,1,0:T(8,128)(2,1)S(1)}, bf16[16,128,256]{2,1,0:T(8,128)(2,1)}, u32[]{:S(2)}) copy-start(bf16[16,128,256]{2,1,0:T(8,128)(2,1)} %grad_x_1.1.refs_4_) | copy-start | bytes 3145732
  71.0 3.9 %collective-permute-start.23 = (bf16[7,16,128]{2,1,0:T(8,128)(2,1)S(1)}, bf16[7,16,128]{2,1,0:T(8,128)(2,1)S(1)}, u32[]{:S(2)}, u32[]{:S(2)}) collective-permute-start(bf16[7,16,128]{2,1,0:T(8,128)(2,1)S(1)} %get-tuple-element.72), channel_id=1, source_target_pairs={{0,8},{1,9},{2,10},{3,11},{4,12},{5,13},{6,14},{7,15},{8,0},{9,1},... | collective-permute-start | bytes 86024 | tf_op jit(solution)/shard_map/ppermute | solution.py:402
  71.4 4.8 %collective-permute-start.24 = (bf16[7,16,128]{2,1,0:T(8,128)(2,1)S(1)}, bf16[7,16,128]{2,1,0:T(8,128)(2,1)S(1)}, u32[]{:S(2)}, u32[]{:S(2)}) collective-permute-start(bf16[7,16,128]{2,1,0:T(8,128)(2,1)S(1)} %get-tuple-element.73), channel_id=1, source_target_pairs={{0,16},{1,17},{2,18},{3,19},{4,20},{5,21},{6,22},{7,23},{8,24},{9,... | collective-permute-start | bytes 86024 | tf_op jit(solution)/shard_map/ppermute | solution.py:402
  75.0 5.7 %collective-permute-start.25 = (bf16[7,16,128]{2,1,0:T(8,128)(2,1)S(1)}, bf16[7,16,128]{2,1,0:T(8,128)(2,1)S(1)}, u32[]{:S(2)}, u32[]{:S(2)}) collective-permute-start(bf16[7,16,128]{2,1,0:T(8,128)(2,1)S(1)} %get-tuple-element.74), channel_id=1, source_target_pairs={{0,24},{1,25},{2,26},{3,27},{4,28},{5,29},{6,30},{7,31},{8,16},{9,... | collective-permute-start | bytes 86024 | tf_op jit(solution)/shard_map/ppermute | solution.py:402
  80.7 5.7 %collective-permute-start.28 = (bf16[7,16,128]{2,1,0:T(8,128)(2,1)S(1)}, bf16[7,16,128]{2,1,0:T(8,128)(2,1)S(1)}, u32[]{:S(2)}, u32[]{:S(2)}) collective-permute-start(bf16[7,16,128]{2,1,0:T(8,128)(2,1)S(1)} %line_sum.3.a_ref), channel_id=1, source_target_pairs={{0,24},{1,25},{2,26},{3,27},{4,28},{5,29},{6,30},{7,31},{8,16},{9,... | collective-permute-start | bytes 86024 | tf_op jit(solution)/shard_map/ppermute | solution.py:402
  82.1 5.1 %collective-permute-start.27 = (bf16[7,16,128]{2,1,0:T(8,128)(2,1)S(1)}, bf16[7,16,128]{2,1,0:T(8,128)(2,1)S(1)}, u32[]{:S(2)}, u32[]{:S(2)}) collective-permute-start(bf16[7,16,128]{2,1,0:T(8,128)(2,1)S(1)} %line_sum.3.a_ref), channel_id=1, source_target_pairs={{0,16},{1,17},{2,18},{3,19},{4,20},{5,21},{6,22},{7,23},{8,24},{9,... | collective-permute-start | bytes 86024 | tf_op jit(solution)/shard_map/ppermute | solution.py:402
  82.1 5.2 %collective-permute-start.26 = (bf16[7,16,128]{2,1,0:T(8,128)(2,1)S(1)}, bf16[7,16,128]{2,1,0:T(8,128)(2,1)S(1)}, u32[]{:S(2)}, u32[]{:S(2)}) collective-permute-start(bf16[7,16,128]{2,1,0:T(8,128)(2,1)S(1)} %line_sum.3.a_ref), channel_id=1, source_target_pairs={{0,8},{1,9},{2,10},{3,11},{4,12},{5,13},{6,14},{7,15},{8,0},{9,1},... | collective-permute-start | bytes 86024 | tf_op jit(solution)/shard_map/ppermute | solution.py:402
  85.2 12.8 %collective-permute-start.19 = (bf16[16,9,16,128]{3,2,1,0:T(8,128)(2,1)S(1)}, bf16[16,9,16,128]{3,2,1,0:T(8,128)(2,1)S(1)}, u32[]{:S(2)}, u32[]{:S(2)}) collective-permute-start(bf16[16,9,16,128]{3,2,1,0:T(8,128)(2,1)S(1)} %plane_gather.2.own_ref), channel_id=1, source_target_pairs={{0,2},{1,3},{2,0},{3,1},{4,6},{5,7},{6,4},{7,5},{8,10},{9,11},{10,... | collective-permute-start | bytes 1769480 | tf_op jit(solution)/shard_map/ppermute | solution.py:402
  87.3 6.6 %collective-permute-start.31 = (bf16[4,7,16,128]{3,2,1,0:T(8,128)(2,1)S(1)}, bf16[4,7,16,128]{3,2,1,0:T(8,128)(2,1)S(1)}, u32[]{:S(2)}, u32[]{:S(2)}) collective-permute-start(bf16[4,7,16,128]{3,2,1,0:T(8,128)(2,1)S(1)} %line_gather.3.a_ref), channel_id=1, source_target_pairs={{0,5},{1,4},{2,7},{3,6},{4,1},{5,0},{6,3},{7,2},{8,13},{9,12},{10,... | collective-permute-start | bytes 344072 | tf_op jit(solution)/shard_map/ppermute | solution.py:402
  89.3 5.4 %collective-permute-start.30 = (bf16[4,7,16,128]{3,2,1,0:T(8,128)(2,1)S(1)}, bf16[4,7,16,128]{3,2,1,0:T(8,128)(2,1)S(1)}, u32[]{:S(2)}, u32[]{:S(2)}) collective-permute-start(bf16[4,7,16,128]{3,2,1,0:T(8,128)(2,1)S(1)} %line_gather.3.a_ref), channel_id=1, source_target_pairs={{0,1},{1,0},{2,3},{3,2},{4,5},{5,4},{6,7},{7,6},{8,9},{9,8},{10,11... | collective-permute-start | bytes 344072 | tf_op jit(solution)/shard_map/ppermute | solution.py:402
  89.4 5.4 %collective-permute-start.29 = (bf16[4,7,16,128]{3,2,1,0:T(8,128)(2,1)S(1)}, bf16[4,7,16,128]{3,2,1,0:T(8,128)(2,1)S(1)}, u32[]{:S(2)}, u32[]{:S(2)}) collective-permute-start(bf16[4,7,16,128]{3,2,1,0:T(8,128)(2,1)S(1)} %line_gather.3.a_ref), channel_id=1, source_target_pairs={{0,4},{1,5},{2,6},{3,7},{4,0},{5,1},{6,2},{7,3},{8,12},{9,13},{10,... | collective-permute-start | bytes 344072 | tf_op jit(solution)/shard_map/ppermute | solution.py:402
  94.8 1.9 %collective-permute-start.32 = (bf16[16,7,16,128]{3,2,1,0:T(8,128)(2,1)S(1)}, bf16[16,7,16,128]{3,2,1,0:T(8,128)(2,1)S(1)}, u32[]{:S(2)}, u32[]{:S(2)}) collective-permute-start(bf16[16,7,16,128]{3,2,1,0:T(8,128)(2,1)S(1)} %plane_gather.3.own_ref), channel_id=1, source_target_pairs={{0,2},{1,3},{2,0},{3,1},{4,6},{5,7},{6,4},{7,5},{8,10},{9,11},{10,... | collective-permute-start | bytes 1376264 | tf_op jit(solution)/shard_map/ppermute | solution.py:402

commit v4 on v3

--- a/solution.py
+++ b/solution.py
@@ -131,7 +131,7 @@
 
 
 def spatial_kernel(
-    bands, count_ref, top_ref, bot_ref, acts_in, at_in, ws_ref, acts_ref, at_ref, sp_ref, edge_ref
+    bands, count_ref, top_ref, bot_ref, acts_in, ws_ref, _, acts_ref, sp_ref, edge_ref
 ):
     count = count_ref[0]
     band = lax.axis_index("grp")
@@ -139,7 +139,6 @@
     for ref, flag, row in ((top_ref, band > 0, 0), (bot_ref, band < bands - 1, rows + 1)):
         a = jnp.where(flag, ref[...].astype(F32), 0.0)
         acts_ref[row, 1 : cols + 1] = a.astype(BF).reshape(cols, SLOTS, CH)
-        at_ref[:, row * 128 : row * 128 + 128] = a.T.astype(BF)
     a, b = iotas(32, 256)
     pick = (a // 2 == b // SLOTS) & (b % SLOTS == count - 2 + a % 2)
     pick = jnp.where(pick, 1.0, 0.0).astype(BF)
@@ -161,11 +160,15 @@
 
 
 def grad_spatial_kernel(
-    count_ref, at_ref, cot_ref, nxt_ref, wt_ref, wd_ref,
-    cott_ref, gy_ref, gs_ref, last_ref, first_ref, keep_ref, send_ref,
+    bands, count_ref, at_in, top_ref, bot_ref, cot_ref, nxt_ref, wt_ref, wd_ref,
+    at_ref, cott_ref, gy_ref, gs_ref, keep_ref, send_ref, *edge_refs,
 ):
     count = count_ref[0]
+    band = lax.axis_index("grp")
     rows, cols = gy_ref.shape[0], gy_ref.shape[1]
+    for ref, flag, row in ((top_ref, band > 0, 0), (bot_ref, band < bands - 1, rows + 1)):
+        a = jnp.where(flag, ref[...].astype(F32), 0.0)
+        at_ref[:, row * 128 : row * 128 + 128] = a.T.astype(BF)
     edge = jnp.zeros((rows, SLOTS, CH), BF)
     gs_ref[:, 0] = edge
     gs_ref[:, cols + 1] = edge
@@ -183,8 +186,13 @@
                 for r in range(4):
                     for c in range(4):
                         gy_ref[2 * (q * 4 + r) + i, 2 * c + j] = g[r, c]
-    last_ref[...] = cott_ref[rows // 2 - 1].reshape(cols // 2 * SLOTS, CH)
-    first_ref[...] = cott_ref[0].reshape(cols // 2 * SLOTS, CH)
+    last = cott_ref[rows // 2 - 1].reshape(cols // 2 * SLOTS, CH)
+    first = cott_ref[0].reshape(cols // 2 * SLOTS, CH)
+    if bands == 2:
+        edge_refs[0][...] = jnp.where(band == 0, last, first)
+    else:
+        edge_refs[0][...] = last
+        edge_refs[1][...] = first
 
     def grads_of(q, _):
         g = gy_ref[pl.ds(4 * q, 4)].reshape(4 * cols, SLOTS, CH)
@@ -203,9 +211,9 @@
 
 
 def forward_kernel(
-    count_ref, xt_ref, sp_ref, prev_ref, cott_ref, gy_ref, wt_ref, wd_ref, _,
-    down_ref, keep_ref, send_ref, y_ref, st_ref, g1_ref, g0_ref, g2_ref,
+    count_ref, xt_ref, sp_ref, prev_ref, cott_ref, gy_ref, wt_ref, wd_ref, *rest
 ):
+    down_ref, keep_ref, send_ref, y_ref, st_ref, g1_ref, g0_ref, g2_ref = rest[-8:]
     count = count_ref[0]
     rows, cols = xt_ref.shape[0], xt_ref.shape[1]
     a, b = iotas(256, 32)
@@ -256,28 +264,23 @@
 
 
 def grad_x_kernel(
-    part, bands, count_ref, xt_ref, gy_ref, gs_ref, halo_ref, wt_ref, wd_ref, ws_ref, *rest
+    bands, count_ref, xt_ref, gy_ref, gs_ref, top_ref, bot_ref, wt_ref, wd_ref, ws_ref, *rest
 ):
-    out_ref, pad_ref, buf, sem = rest[-4:]
+    out_ref, pad_ref, buf, sems = rest[-4:]
     count = count_ref[0]
     band = lax.axis_index("grp")
     rows, cols = xt_ref.shape[0], xt_ref.shape[1]
-    half = rows // 2
-    if part == 0:
-        flag, i, row = band > 0, 1, 0
-        pad_ref[1 : half + 2] = gs_ref[0 : half + 1]
-    else:
-        flag, i, row = band < bands - 1, 0, half + 1
-        pad_ref[0 : half + 1] = gs_ref[half - 1 :]
-    pair = [
-        mm_nt(halo_ref[...], wd_ref[i * 2 + j]).astype(BF).reshape(cols // 2, SLOTS, CH)
-        for j in range(2)
-    ]
-    g = jnp.stack(pair, axis=1).reshape(cols, SLOTS, CH)
-    s = grad_of_temporal(g, wt_ref, jnp.where(flag, count, 0))
-    pad_ref[row, 0] = jnp.zeros((SLOTS, CH), BF)
-    pad_ref[row, 1 : cols + 1] = s
-    pad_ref[row, cols + 1] = jnp.zeros((SLOTS, CH), BF)
+    pad_ref[1 : rows + 1] = gs_ref[...]
+    edge = jnp.zeros((SLOTS, CH), BF)
+    for ref, flag, i, row in ((top_ref, band > 0, 1, 0), (bot_ref, band < bands - 1, 0, rows + 1)):
+        pair = [
+            mm_nt(ref[...], wd_ref[i * 2 + j]).astype(BF).reshape(cols // 2, SLOTS, CH)
+            for j in range(2)
+        ]
+        g = jnp.stack(pair, axis=1).reshape(cols, SLOTS, CH)
+        pad_ref[row, 0] = edge
+        pad_ref[row, 1 : cols + 1] = grad_of_temporal(g, wt_ref, jnp.where(flag, count, 0))
+        pad_ref[row, cols + 1] = edge
     back = to_frames(16)
 
     def rows_of(q, _):
@@ -289,7 +292,7 @@
                 )
                 term = mm_nt(left, ws_ref[i * 3 + j])
                 total = term if total is None else total + term
-        at = part * half + 4 * q
+        at = 4 * q
         v = xt_ref[pl.ds(at, 4)].reshape(4 * cols * SLOTS, CH).astype(F32)
         r = lax.rsqrt(jnp.mean(v * v, axis=-1, keepdims=True) + 1e-06)
         u = v * r
@@ -305,9 +308,8 @@
             buf[:, pl.ds(pl.multiple_of((2 * q + k) * 16, 16), 16), :] = o.reshape(SLOTS, 16, CH)
         return 0
 
-    lax.fori_loop(0, half // 4, rows_of, 0)
-    size = half * cols
-    copy = pltpu.make_async_copy(buf, out_ref.at[:, part * size : part * size + size, :], sem)
+    lax.fori_loop(0, rows // 4, rows_of, 0)
+    copy = pltpu.make_async_copy(buf, out_ref, sems.at[0])
     copy.start()
     copy.wait()
 
@@ -324,11 +326,16 @@
     return functools.reduce(lambda a, b: a + b, [ref[z].astype(F32) for ref in refs]).astype(BF)
 
 
-def line_send_kernel(*refs):
-    ins, outs = refs[:4], refs[-4:]
+def line_send_kernel(chains, *refs):
+    outs = refs[-4:]
     _, _, z = place_bits()
     for r in range(4):
-        outs[r][...] = total_at(ins, z ^ r)
+        at = 0
+        for c in range(chains):
+            ins = refs[4 * c : 4 * c + 4]
+            n = ins[0].shape[1]
+            outs[r][at : at + n] = total_at(ins, z ^ r)
+            at += n
 
 
 def line_sum_kernel(a_ref, b_ref, c_ref, d_ref, out_ref):
@@ -342,24 +349,30 @@
         out_ref[z ^ r] = ref[...]
 
 
-def plane_gather_kernel(a_ref, b_ref, c_ref, d_ref, out_ref):
+def plane_gather_kernel(a_ref, b_ref, c_ref, d_ref, *rest):
+    out_ref = rest[-1]
     _, p, _ = place_bits()
     for r, ref in enumerate((a_ref, b_ref, c_ref, d_ref)):
         out_ref[pl.ds((p ^ r) * 4, 4)] = ref[...]
 
 
-def finish_kernel(own_ref, got_ref, *rest):
-    outs, buf, sems = rest[:-2], rest[-2], rest[-1]
+def pass_kernel(*_):
+    pass
+
+
+def finish_kernel(own, half_ref, *rest):
+    buf, sems = rest[-2:]
+    outs = rest[-5:-2]
     core, _, _ = place_bits()
+    at = pl.multiple_of((core if own else 1 - core) * (CH // 2), CH // 2)
     copies = []
     k = 0
     for out in outs:
         for m in range(out.shape[0]):
-            own = own_ref[:, k].reshape(CH, CH // 2).astype(F32)
-            got = got_ref[:, k].reshape(CH, CH // 2).astype(F32)
-            buf[k, :, : CH // 2] = jnp.where(core == 0, own, got)
-            buf[k, :, CH // 2 :] = jnp.where(core == 0, got, own)
-            copies.append(pltpu.make_async_copy(buf.at[k], out.at[m], sems.at[k]))
+            buf[k] = half_ref[:, k].reshape(CH, CH // 2).astype(F32)
+            copies.append(
+                pltpu.make_async_copy(buf.at[k], out.at[m, :, pl.ds(at, CH // 2)], sems.at[k])
+            )
             copies[-1].start()
             k += 1
     for copy in copies:
@@ -369,6 +382,7 @@
 VMEM = pl.BlockSpec(memory_space=pltpu.VMEM)
 SMEM = pl.BlockSpec(memory_space=pltpu.SMEM)
 ANY = pl.BlockSpec(memory_space=pl.ANY)
+HBM = pl.BlockSpec(memory_space=pltpu.HBM)
 
 
 def call(kernel, name, ins, outs, scratch=(), flops=0, alias=None):
@@ -417,10 +431,11 @@
     return [parts[0], swap(parts[1], tm, grp, x), swap(parts[2], tm, grp, y), swap(parts[3], tm, grp, x, y)]
 
 
-def line_send(parts, after):
-    shape = parts[0].shape[1:]
-    ins = [(VMEM, a) for a in parts] + [(ANY, a) for a in after]
-    return call(line_send_kernel, "line_send", ins, [(VMEM, shape)] * 4)
+def line_send(*chains):
+    n = sum(parts[0].shape[1] for parts in chains)
+    ins = [(VMEM, a) for parts in chains for a in parts]
+    kernel = functools.partial(line_send_kernel, len(chains))
+    return call(kernel, "line_send", ins, [(VMEM, (n, 16, CH // 2))] * 4)
 
 
 def line_round(parts, tm, grp):
@@ -428,26 +443,30 @@
     return [parts[0], swap(parts[1], tm, grp, a), swap(parts[2], tm, grp, b), swap(parts[3], tm, grp, a, b)]
 
 
-def gather_back(parts, shapes, tm, grp):
+def line_gather(parts, tm, grp):
     (mine,) = call(line_sum_kernel, "line_sum", [(VMEM, a) for a in parts], [(VMEM, parts[0].shape)])
     for bit in plan(tm, grp)[5:]:
         mine = (mine.astype(F32) + swap(mine, tm, grp, bit).astype(F32)).astype(BF)
     parts = line_round([mine] * 4, tm, grp)
-    (mine,) = call(
+    return call(
         line_gather_kernel, "line_gather", [(VMEM, a) for a in parts], [(VMEM, (4,) + mine.shape)]
-    )
-    parts = plane_round([mine] * 4, tm, grp)
-    (mine,) = call(
-        plane_gather_kernel, "plane_gather", [(VMEM, a) for a in parts], [(VMEM, (16,) + mine.shape[1:])]
-    )
-    got = core_round(mine, tm, grp)
-    n = mine.shape[1]
+    )[0]
+
+
+def plane_gather(mine, parts, after):
+    ins = [(VMEM, a) for a in parts] + [(ANY, a) for a in after]
+    return call(plane_gather_kernel, "plane_gather", ins, [(VMEM, (16,) + mine.shape[1:])])[0]
+
+
+def finish(own, half, before):
+    n = half.shape[1]
     return call(
-        finish_kernel,
+        functools.partial(finish_kernel, own),
         "finish",
-        [(VMEM, mine), (VMEM, got)],
-        [(ANY, (m, CH, CH), F32) for m in shapes],
-        [pltpu.VMEM((n, CH, CH), F32), pltpu.SemaphoreType.DMA((n,))],
+        [(VMEM, half)] + [(HBM, a) for a in before],
+        [(HBM, (m, CH, CH), F32) for m in (9, 3, 4)],
+        [pltpu.VMEM((n, CH, CH // 2), F32), pltpu.SemaphoreType.DMA((n,))],
+        alias={1 + i: i for i in range(len(before))},
     )
 
 
@@ -482,7 +501,7 @@
     *edge, nxt = call(
         functools.partial(edges_kernel, grp),
         "edges",
-        [count, (ANY, x), (VMEM, cot)],
+        [count, (HBM, x), (VMEM, cot)],
         [(VMEM, (cols * slots, ch))] * sides + [(VMEM, (2, wide // 4, ch))],
         [pltpu.VMEM((sides, slots, 16, ch), BF), dma((sides,))],
         flops=tap // 8,
@@ -496,63 +515,64 @@
         [(VMEM, tile), (VMEM, padded), (VMEM, (ch, (rows + 2) * 128))],
         flops=2 * tap,
     )
-    acts, at, sp, last_two = call(
+    half = (16, 9, 16, ch // 2)
+    at, cott, gy, gs, keep_a, send_a, *edge = call(
+        functools.partial(grad_spatial_kernel, grp),
+        "grad_spatial",
+        [count, (VMEM, at), (VMEM, top), (VMEM, bot), (VMEM, cot), (VMEM, nxt_got), (VMEM, wt), (VMEM, wd)],
+        [(VMEM, at.shape), (VMEM, (rows // 2, cols // 2, slots, ch)), (VMEM, tile),
+         (VMEM, (rows, cols + 2, slots, ch)), (VMEM, half), (VMEM, half)]
+        + [(VMEM, (cols // 2 * slots, ch))] * sides,
+        flops=14 * tap,
+        alias={1: 0},
+    )
+    got_a = core_round(send_a, tm, grp)
+    acts, sp, last_two = call(
         functools.partial(spatial_kernel, grp),
         "spatial",
-        [count, (VMEM, top), (VMEM, bot), (VMEM, acts), (VMEM, at), (VMEM, ws)],
-        [(VMEM, padded), (VMEM, at.shape), (VMEM, tile), (VMEM, (rows // 2, 32, ch))],
+        [count, (VMEM, top), (VMEM, bot), (VMEM, acts), (VMEM, ws), (ANY, send_a)],
+        [(VMEM, padded), (VMEM, tile), (VMEM, (rows // 2, 32, ch))],
         flops=9 * tap,
-        alias={3: 0, 4: 1},
+        alias={3: 0},
     )
     prev = along(last_two, "tm", 1)
-    half = (16, 9, 16, ch // 2)
-    cott, gy, gs, last, first, keep_a, send_a = call(
-        grad_spatial_kernel,
-        "grad_spatial",
-        [count, (VMEM, at), (VMEM, cot), (VMEM, nxt_got), (VMEM, wt), (VMEM, wd)],
-        [(VMEM, (rows // 2, cols // 2, slots, ch)), (VMEM, tile), (VMEM, (rows, cols + 2, slots, ch)),
-         (VMEM, (cols // 2 * slots, ch)), (VMEM, (cols // 2 * slots, ch)), (VMEM, half), (VMEM, half)],
-        flops=14 * tap,
-    )
-    got_a = core_round(send_a, tm, grp)
-    cot_top, cot_bot = along(last, "grp", 1), along(first, "grp", -1)
+    parts_a = plane_send(keep_a, got_a, [last_two])
+    cot_top, cot_bot = from_bands(edge)
     half = (16, 7, 16, ch // 2)
     down, keep_b, send_b = call(
         forward_kernel,
         "forward",
-        [count, (VMEM, xt), (VMEM, sp), (VMEM, prev), (VMEM, cott), (VMEM, gy), (VMEM, wt), (VMEM, wd),
-         (ANY, send_a)],
+        [count, (VMEM, xt), (VMEM, sp), (VMEM, prev), (VMEM, cott), (VMEM, gy), (VMEM, wt), (VMEM, wd)]
+        + [(ANY, a) for a in parts_a],
         [(VMEM, (slots, wide // 4, ch)), (VMEM, half), (VMEM, half)],
         [pltpu.VMEM(s, BF) for s in (tile, (ch, slots * wide), tile, tile, tile)],
         flops=10 * tap,
     )
-    got_b = core_round(send_b, tm, grp)
-    parts_a = plane_send(keep_a, got_a, [send_b])
-
-    def grad_x_part(part, halo, after):
-        return call(
-            functools.partial(grad_x_kernel, part, grp),
-            f"grad_x_{part}",
-            [count, (VMEM, xt), (VMEM, gy), (VMEM, gs), (VMEM, halo), (VMEM, wt), (VMEM, wd), (VMEM, ws)]
-            + [(ANY, a) for a in after],
-            [(ANY, (slots, wide, ch))],
-            [pltpu.VMEM((rows // 2 + 2, cols + 2, slots, ch), BF),
-             pltpu.VMEM((slots, wide // 2, ch), BF), dma],
-            flops=5 * tap,
-            alias={8: 0} if part else None,
-        )[0]
-
-    grad_x = grad_x_part(0, cot_top, [parts_a[3], send_b])
     parts_a = plane_round(parts_a, tm, grp)
-    parts_b = plane_send(keep_b, got_b, [grad_x])
-    parts_a = line_send(parts_a, [parts_b[0]])
-    grad_x = grad_x_part(1, cot_bot, [grad_x, parts_a[3], parts_b[3]])
+    (send_b,) = call(
+        pass_kernel,
+        "pass",
+        [(ANY, send_b)] + [(ANY, a) for a in parts_a[1:]],
+        [(ANY, send_b.shape)],
+        alias={0: 0},
+    )
+    parts_b = plane_send(keep_b, core_round(send_b, tm, grp), [])
     parts_b = plane_round(parts_b, tm, grp)
-    parts_a = line_round(parts_a, tm, grp)
-    parts_b = line_send(parts_b, [grad_x])
-    parts_b = line_round(parts_b, tm, grp)
-    (sum_s,) = gather_back(parts_a, [9], tm, grp)
-    sum_t, sum_d = gather_back(parts_b, [3, 4], tm, grp)
+    mine = line_gather(line_round(line_send(parts_a, parts_b), tm, grp), tm, grp)
+    parts = plane_round([mine] * 4, tm, grp)
+    (grad_x,) = call(
+        functools.partial(grad_x_kernel, grp),
+        "grad_x",
+        [count, (VMEM, xt), (VMEM, gy), (VMEM, gs), (VMEM, cot_top), (VMEM, cot_bot), (VMEM, wt),
+         (VMEM, wd), (VMEM, ws), (ANY, mine)],
+        [(HBM, (slots, wide, ch))],
+        [pltpu.VMEM(padded, BF), pltpu.VMEM((slots, wide, ch), BF), dma((1,))],
+        flops=10 * tap,
+    )
+    mine = plane_gather(mine, parts, [grad_x])
+    got = core_round(mine, tm, grp)
+    outs = list(finish(True, mine, []))
+    sum_s, sum_t, sum_d = finish(False, got, outs)
     return (
         down.reshape(cotangent.shape),
         grad_x.reshape(frames_in.shape),

time: 100 us -> 81.5 us (0.81)
  starting transfers between devices: 44.4 us -> 28.7 us
  local copies, waits for them, and re-layouts: 5.47 us -> 4.24 us
    ppermute x28 -> x18, starting transfers between devices: 33.2 us -> 21.7 us  [swap(): return lax.ppermute(value, AXES, [(d, d ^ flip) for d in range(tm * grp)])]
    ppermute x4 -> x2, starting transfers between devices: 8.16 us -> 3.21 us  [along(): return lax.ppermute(value, axis, pairs)]
    unnamed x12 -> x10, local copies, waits for them, and re-layouts: 3.68 us -> 2.46 us
    pallas_call x19 -> x15, Pallas kernels: 28.5 us -> 27.7 us  [call(): pl.pallas_call(kernel, out_shape=shapes, in_specs=[s for s, _ in ins], ou...]
    ppermute x1 -> x2, starting transfers between devices: 3.03 us -> 3.79 us  [from_bands(): got = lax.ppermute(parts[0], 'grp', [(0, 1), (1, 0)])]
    ppermute x28 -> x18, waiting for transfers between devices: 19 us -> 18.7 us  [swap(): return lax.ppermute(value, AXES, [(d, d ^ flip) for d in range(tm * grp)])]
  transfers between devices with their start and end apart: 33 -> 22, of which waited for: 14 -> 11; matrix products, arithmetic and copies ran while one was open for 1% -> 1% of each run, Pallas kernels for 27% -> 25%
where the time goes in v4:
time: 81.5 us; the launch traced here: 81.2 us
  starting transfers between devices  28.7 us (35%)
  Pallas kernels  27.7 us (34%)
  waiting for transfers between devices  19.1 us (23%)
  local copies, waits for them, and re-layouts  4.24 us (5%)
  between operations  1.47 us (2%)
    pallas_call x15, Pallas kernels, call(): pl.pallas_call(kernel, out_shape=shapes, in_specs=[s for s, _ in ins], ou...  27.7 us
    ppermute x18, starting transfers between devices, swap(): return lax.ppermute(value, AXES, [(d, d ^ flip) for d in range(tm * grp)])  21.7 us
    ppermute x18, waiting for transfers between devices, swap(): return lax.ppermute(value, AXES, [(d, d ^ flip) for d in range(tm * grp)])  18.7 us
    ppermute x2, starting transfers between devices, from_bands(): got = lax.ppermute(parts[0], 'grp', [(0, 1), (1, 0)])  3.79 us
    ppermute x2, starting transfers between devices, along(): return lax.ppermute(value, axis, pairs)  3.21 us
    unnamed x10, local copies, waits for them, and re-layouts  2.46 us
  transfers between devices with their start and end apart: 22, of which 11 were waited for; matrix products, arithmetic and copies ran while one was open for 1% of the time, Pallas kernels for 25%

profile of v4, /device:TPU:0, one launch (start us, length us, event | category | flops | bytes accessed | tf_op | source)
XLA Modules:
  0.0 81.2 jit_solution(13739072397238195304)
XLA Ops:
  1.3 1.0 %reshape.35.cot_ref = bf16[16,32,256]{2,1,0:T(8,128)(2,1)S(1)} reshape(bf16[16,8,4,256]{3,2,1,0:T(4,128)(2,1)} %param.11) | data formatting | bytes 524288 | tf_op jit(solution)/shard_map/reshape | solution.py:490
  2.3 0.0 copy-start.1
  2.3 1.2 %copy-done.1 = bf16[16,16,8,256]{3,2,1,0:T(8,128)(2,1)S(1)} copy-done((bf16[16,16,8,256]{3,2,1,0:T(8,128)(2,1)S(1)}, bf16[16,16,8,256]{3,2,1,0:T(8,128)(2,1)}, u32[]{:S(2)}) %copy-start.1) | copy-done | bytes 1048600
  3.5 0.4 edges.1
  3.9 3.0 %collective-permute-start = (bf16[128,256]{1,0:T(8,128)(2,1)S(1)}, bf16[128,256]{1,0:T(8,128)(2,1)S(1)}, u32[]{:S(2)}, u32[]{:S(2)}) collective-permute-start(bf16[128,256]{1,0:T(8,128)(2,1)S(1)} %get-tuple-element.41), channel_id=1, source_target_pairs={{0,1},{1,0},{2,3},{3,2},{4,5},{5,4},{6,7},{7,6},{8,9},{9,8},{10,11... | collective-permute-start | bytes 196616 | tf_op jit(solution)/shard_map/ppermute | solution.py:481
  6.9 1.3 %collective-permute-start.1 = (bf16[2,32,256]{2,1,0:T(8,128)(2,1)S(1)}, bf16[2,32,256]{2,1,0:T(8,128)(2,1)S(1)}, u32[]{:S(2)}, u32[]{:S(2)}) collective-permute-start(bf16[2,32,256]{2,1,0:T(8,128)(2,1)S(1)} %get-tuple-element.39._), channel_id=1, source_target_pairs={{2,0},{4,2},{6,4},{8,6},{10,8},{12,10},{14,12},{16,14},{18,16},{20... | collective-permute-start | bytes 98312 | tf_op jit(solution)/shard_map/ppermute | solution.py:476
  8.2 3.4 %acts.1 = (bf16[16,8,16,256]{3,2,1,0:T(8,128)(2,1)S(1)}, bf16[18,10,16,256]{3,2,1,0:T(8,128)(2,1)S(1)}, bf16[256,2304]{1,0:T(8,128)(2,1)S(1)}) custom-call(s32[1]{0:T(128)S(6)} %copy.23.count_ref, bf16[16,128,256]{2,1,0:T(8,128)(2,1)S(1)} %bitcast.8, bf16[2,32,256]{2,1,0:T(8,128)(2,1)S(1)} %get-tuple-element.39._), custom_call_target="tpu_custom_call" | custom-call | flops 536870912 | bytes 4751364 | tf_op jit(solution)/shard_map/acts/pallas_call | solution.py:392
  11.6 5.0 %grad_spatial.1 = (bf16[256,2304]{1,0:T(8,128)(2,1)S(1)}, bf16[8,4,16,256]{3,2,1,0:T(8,128)(2,1)S(1)}, bf16[16,8,16,256]{3,2,1,0:T(8,128)(2,1)S(1)}, bf16[16,10,...) custom-call(s32[1]{0:T(128)S(6)} %copy.23.count_ref, ...), custom_call_target="tpu_custom_call", output_to_operand_aliasing={{0}: (1, {})} | custom-call | flops 3758096384 | bytes 7536644 | tf_op jit(solution)/shard_map/grad_spatial/pallas_call | solution.py:392
  16.7 1.2 %collective-permute-start.3 = (bf16[16,9,16,128]{3,2,1,0:T(8,128)(2,1)S(1)}, bf16[16,9,16,128]{3,2,1,0:T(8,128)(2,1)S(1)}, u32[]{:S(2)}, u32[]{:S(2)}) collective-permute-start(bf16[16,9,16,128]{3,2,1,0:T(8,128)(2,1)S(1)} %get-tuple-element.44._), channel_id=1, source_target_pairs={{0,2},{1,3},{2,0},{3,1},{4,6},{5,7},{6,4},{7,5},{8,10},{9,11},{10,... | collective-permute-start | bytes 1769480 | tf_op jit(solution)/shard_map/ppermute | solution.py:416
  17.9 3.7 %spatial.1 = (bf16[18,10,16,256]{3,2,1,0:T(8,128)(2,1)S(1)}, bf16[16,8,16,256]{3,2,1,0:T(8,128)(2,1)S(1)}, bf16[8,32,256]{2,1,0:T(8,128)(2,1)S(1)}) custom-call(s32[1]{0:T(128)S(6)} %copy.23.count_ref, bf16[128,256]{1,0:T(8,128)(2,1)S(1)} %collective-permute-done.top_ref.bot_ref, ...), custom_call_target="tpu_custom_call", output_to_operand_aliasing={{0}: (3, {})} | custom-call | flops 2415919104 | bytes 5439492 | tf_op jit(solution)/shard_map/spatial/pallas_call | solution.py:392
  21.6 1.9 %collective-permute-start.2 = (bf16[8,32,256]{2,1,0:T(8,128)(2,1)S(1)}, bf16[8,32,256]{2,1,0:T(8,128)(2,1)S(1)}, u32[]{:S(2)}, u32[]{:S(2)}) collective-permute-start(bf16[8,32,256]{2,1,0:T(8,128)(2,1)S(1)} %get-tuple-element.46.rest_0_), channel_id=1, source_target_pairs={{0,2},{2,4},{4,6},{6,8},{8,10},{10,12},{12,14},{14,16},{16,18},{18... | collective-permute-start | bytes 393224 | tf_op jit(solution)/shard_map/ppermute | solution.py:476
  23.5 0.2 plane_send.2
  23.7 1.6 %collective-permute-start.5 = (bf16[4,9,16,128]{3,2,1,0:T(8,128)(2,1)S(1)}, bf16[4,9,16,128]{3,2,1,0:T(8,128)(2,1)S(1)}, u32[]{:S(2)}, u32[]{:S(2)}) collective-permute-start(bf16[4,9,16,128]{3,2,1,0:T(8,128)(2,1)S(1)} %get-tuple-element.51.rest_1_), channel_id=1, source_target_pairs={{0,4},{1,5},{2,6},{3,7},{4,0},{5,1},{6,2},{7,3},{8,12},{9,13},{10,... | collective-permute-start | bytes 442376 | tf_op jit(solution)/shard_map/ppermute | solution.py:416
  25.2 0.5 collective-permute-start.6
  25.8 1.5 %collective-permute-start.7 = (bf16[4,9,16,128]{3,2,1,0:T(8,128)(2,1)S(1)}, bf16[4,9,16,128]{3,2,1,0:T(8,128)(2,1)S(1)}, u32[]{:S(2)}, u32[]{:S(2)}) collective-permute-start(bf16[4,9,16,128]{3,2,1,0:T(8,128)(2,1)S(1)} %get-tuple-element.53.rest_3_), channel_id=1, source_target_pairs={{0,5},{1,4},{2,7},{3,6},{4,1},{5,0},{6,3},{7,2},{8,13},{9,12},{10,... | collective-permute-start | bytes 442376 | tf_op jit(solution)/shard_map/ppermute | solution.py:416
  27.2 5.0 %forward.1 = (bf16[16,32,256]{2,1,0:T(8,128)(2,1)S(1)}, bf16[16,7,16,128]{3,2,1,0:T(8,128)(2,1)S(1)}, bf16[16,7,16,128]{3,2,1,0:T(8,128)(2,1)S(1)}) custom-call(s32[1]{0:T(128)S(6)} %copy.23.count_ref, bf16[16,8,16,256]{3,2,1,0:T(8,128)(2,1)S(1)} %get-tuple-element.40.xt_ref, bf16[16,8,16,256]{3,2,1,0:T(8,128)(2,1)S(1)} %get-tuple-element.45.sp_ref, ...), custom_call_target="tpu_custom_call" | custom-call | flops 2684354560 | bytes 5636100 | tf_op jit(solution)/shard_map/forward/pallas_call | solution.py:392
  32.3 2.5 %collective-permute-done.6.__2_.refs_2_ = bf16[4,9,16,128]{3,2,1,0:T(8,128)(2,1)S(1)} collective-permute-done((bf16[4,9,16,128]{3,2,1,0:T(8,128)(2,1)S(1)}, bf16[4,9,16,128]{3,2,1,0:T(8,128)(2,1)S(1)}, u32[]{:S(2)}, u32[]{:S(2)}) %collective-permute-start.6) | collective-permute-done | bytes 147488 | tf_op jit(solution)/shard_map/ppermute | solution.py:416
  34.8 0.2 collective-permute-start.8
  35.0 1.6 %collective-permute-done.8.got_ref = bf16[16,7,16,128]{3,2,1,0:T(8,128)(2,1)S(1)} collective-permute-done((bf16[16,7,16,128]{3,2,1,0:T(8,128)(2,1)S(1)}, bf16[16,7,16,128]{3,2,1,0:T(8,128)(2,1)S(1)}, u32[]{:S(2)}, u32[]{:S(2)}) %collective-permute-start.8) | collective-permute-done | bytes 458784 | tf_op jit(solution)/shard_map/ppermute | solution.py:416
  36.6 0.1 plane_send.3
  36.7 0.4 collective-permute-start.9
  37.1 1.5 %collective-permute-start.10 = (bf16[4,7,16,128]{3,2,1,0:T(8,128)(2,1)S(1)}, bf16[4,7,16,128]{3,2,1,0:T(8,128)(2,1)S(1)}, u32[]{:S(2)}, u32[]{:S(2)}) collective-permute-start(bf16[4,7,16,128]{3,2,1,0:T(8,128)(2,1)S(1)} %get-tuple-element.61), channel_id=1, source_target_pairs={{0,1},{1,0},{2,3},{3,2},{4,5},{5,4},{6,7},{7,6},{8,9},{9,8},{10,11... | collective-permute-start | bytes 344072 | tf_op jit(solution)/shard_map/ppermute | solution.py:416
  38.6 1.7 %collective-permute-start.11 = (bf16[4,7,16,128]{3,2,1,0:T(8,128)(2,1)S(1)}, bf16[4,7,16,128]{3,2,1,0:T(8,128)(2,1)S(1)}, u32[]{:S(2)}, u32[]{:S(2)}) collective-permute-start(bf16[4,7,16,128]{3,2,1,0:T(8,128)(2,1)S(1)} %get-tuple-element.62), channel_id=1, source_target_pairs={{0,5},{1,4},{2,7},{3,6},{4,1},{5,0},{6,3},{7,2},{8,13},{9,12},{10,... | collective-permute-start | bytes 344072 | tf_op jit(solution)/shard_map/ppermute | solution.py:416
  40.3 2.5 %collective-permute-done.9.refs_5_ = bf16[4,7,16,128]{3,2,1,0:T(8,128)(2,1)S(1)} collective-permute-done((bf16[4,7,16,128]{3,2,1,0:T(8,128)(2,1)S(1)}, bf16[4,7,16,128]{3,2,1,0:T(8,128)(2,1)S(1)}, u32[]{:S(2)}, u32[]{:S(2)}) %collective-permute-start.9) | collective-permute-done | bytes 114720 | tf_op jit(solution)/shard_map/ppermute | solution.py:416
  42.8 2.0 %collective-permute-done.10.refs_6_ = bf16[4,7,16,128]{3,2,1,0:T(8,128)(2,1)S(1)} collective-permute-done((bf16[4,7,16,128]{3,2,1,0:T(8,128)(2,1)S(1)}, bf16[4,7,16,128]{3,2,1,0:T(8,128)(2,1)S(1)}, u32[]{:S(2)}, u32[]{:S(2)}) %collective-permute-start.10) | collective-permute-done | bytes 114720 | tf_op jit(solution)/shard_map/ppermute | solution.py:416
  44.7 0.1 line_send.1
  44.8 2.6 %collective-permute-start.12 = (bf16[16,16,128]{2,1,0:T(8,128)(2,1)S(1)}, bf16[16,16,128]{2,1,0:T(8,128)(2,1)S(1)}, u32[]{:S(2)}, u32[]{:S(2)}) collective-permute-start(bf16[16,16,128]{2,1,0:T(8,128)(2,1)S(1)} %get-tuple-element.64), channel_id=1, source_target_pairs={{0,8},{1,9},{2,10},{3,11},{4,12},{5,13},{6,14},{7,15},{8,0},{9,1},... | collective-permute-start | bytes 196616 | tf_op jit(solution)/shard_map/ppermute | solution.py:416
  47.4 2.6 %collective-permute-start.13 = (bf16[16,16,128]{2,1,0:T(8,128)(2,1)S(1)}, bf16[16,16,128]{2,1,0:T(8,128)(2,1)S(1)}, u32[]{:S(2)}, u32[]{:S(2)}) collective-permute-start(bf16[16,16,128]{2,1,0:T(8,128)(2,1)S(1)} %get-tuple-element.65), channel_id=1, source_target_pairs={{0,16},{1,17},{2,18},{3,19},{4,20},{5,21},{6,22},{7,23},{8,24},{9,... | collective-permute-start | bytes 196616 | tf_op jit(solution)/shard_map/ppermute | solution.py:416
  50.0 4.1 %collective-permute-done.13.c_ref = bf16[16,16,128]{2,1,0:T(8,128)(2,1)S(1)} collective-permute-done((bf16[16,16,128]{2,1,0:T(8,128)(2,1)S(1)}, bf16[16,16,128]{2,1,0:T(8,128)(2,1)S(1)}, u32[]{:S(2)}, u32[]{:S(2)}) %collective-permute-start.13) | collective-permute-done | bytes 65568 | tf_op jit(solution)/shard_map/ppermute | solution.py:416
  54.2 1.9 %collective-permute-done.14.d_ref = bf16[16,16,128]{2,1,0:T(8,128)(2,1)S(1)} collective-permute-done((bf16[16,16,128]{2,1,0:T(8,128)(2,1)S(1)}, bf16[16,16,128]{2,1,0:T(8,128)(2,1)S(1)}, u32[]{:S(2)}, u32[]{:S(2)}) %collective-permute-start.14) | collective-permute-done | bytes 65568 | tf_op jit(solution)/shard_map/ppermute | solution.py:416
  56.1 1.3 %collective-permute-start.17 = (bf16[16,16,128]{2,1,0:T(8,128)(2,1)S(1)}, bf16[16,16,128]{2,1,0:T(8,128)(2,1)S(1)}, u32[]{:S(2)}, u32[]{:S(2)}) collective-permute-start(bf16[16,16,128]{2,1,0:T(8,128)(2,1)S(1)} %line_sum.1.a_ref), channel_id=1, source_target_pairs={{0,24},{1,25},{2,26},{3,27},{4,28},{5,29},{6,30},{7,31},{8,16},{9,... | collective-permute-start | bytes 196616 | tf_op jit(solution)/shard_map/ppermute | solution.py:416
  57.5 3.1 %collective-permute-start.15 = (bf16[16,16,128]{2,1,0:T(8,128)(2,1)S(1)}, bf16[16,16,128]{2,1,0:T(8,128)(2,1)S(1)}, u32[]{:S(2)}, u32[]{:S(2)}) collective-permute-start(bf16[16,16,128]{2,1,0:T(8,128)(2,1)S(1)} %line_sum.1.a_ref), channel_id=1, source_target_pairs={{0,8},{1,9},{2,10},{3,11},{4,12},{5,13},{6,14},{7,15},{8,0},{9,1},... | collective-permute-start | bytes 196616 | tf_op jit(solution)/shard_map/ppermute | solution.py:416
  60.6 0.8 collective-permute-start.4
  61.3 1.0 %collective-permute-done.17.d_ref = bf16[16,16,128]{2,1,0:T(8,128)(2,1)S(1)} collective-permute-done((bf16[16,16,128]{2,1,0:T(8,128)(2,1)S(1)}, bf16[16,16,128]{2,1,0:T(8,128)(2,1)S(1)}, u32[]{:S(2)}, u32[]{:S(2)}) %collective-permute-start.17) | collective-permute-done | bytes 65568 | tf_op jit(solution)/shard_map/ppermute | solution.py:416
  62.3 1.4 %collective-permute-done.16.c_ref = bf16[16,16,128]{2,1,0:T(8,128)(2,1)S(1)} collective-permute-done((bf16[16,16,128]{2,1,0:T(8,128)(2,1)S(1)}, bf16[16,16,128]{2,1,0:T(8,128)(2,1)S(1)}, u32[]{:S(2)}, u32[]{:S(2)}) %collective-permute-start.16) | collective-permute-done | bytes 65568 | tf_op jit(solution)/shard_map/ppermute | solution.py:416
  63.7 1.7 %collective-permute-start.20 = (bf16[4,16,16,128]{3,2,1,0:T(8,128)(2,1)S(1)}, bf16[4,16,16,128]{3,2,1,0:T(8,128)(2,1)S(1)}, u32[]{:S(2)}, u32[]{:S(2)}) collective-permute-start(bf16[4,16,16,128]{3,2,1,0:T(8,128)(2,1)S(1)} %line_gather.1.rest_0_.a_ref), channel_id=1, source_target_pairs={{0,5},{1,4},{2,7},{3,6},{4,1},{5,0},{6,3},{7,2},{8,13},{9,12},{10,... | collective-permute-start | bytes 786440 | tf_op jit(solution)/shard_map/ppermute | solution.py:416
  65.4 0.5 collective-permute-start.19
  65.9 1.3 %collective-permute-start.18 = (bf16[4,16,16,128]{3,2,1,0:T(8,128)(2,1)S(1)}, bf16[4,16,16,128]{3,2,1,0:T(8,128)(2,1)S(1)}, u32[]{:S(2)}, u32[]{:S(2)}) collective-permute-start(bf16[4,16,16,128]{3,2,1,0:T(8,128)(2,1)S(1)} %line_gather.1.rest_0_.a_ref), channel_id=1, source_target_pairs={{0,4},{1,5},{2,6},{3,7},{4,0},{5,1},{6,2},{7,3},{8,12},{9,13},{10,... | collective-permute-start | bytes 786440 | tf_op jit(solution)/shard_map/ppermute | solution.py:416
  67.3 0.4 collective-permute-done.4.top_ref.bot_ref
  67.7 6.7 %grad_x.1.rest_0_ = bf16[16,128,256]{2,1,0:T(8,128)(2,1)} custom-call(s32[1]{0:T(128)S(6)} %copy.23.count_ref, bf16[16,8,16,256]{3,2,1,0:T(8,128)(2,1)S(1)} %get-tuple-element.40.xt_ref, bf16[16,8,16,256]{3,2,1,0:T(8,128)(2,1)S(1)} %get-tuple-element.48.gy_ref, bf16[16,10,16,256]{3,2,1,0:T(8,128)(2,1)S(1)} %get-tuple-element.55.gs_ref, ...), custom_call_target="tpu_custom_call" | custom-call | flops 2684354560 | bytes 6619140 | tf_op jit(solution)/shard_map/grad_x/pallas_call | solution.py:392
  74.4 1.3 %collective-permute-done.19.c_ref = bf16[4,16,16,128]{3,2,1,0:T(8,128)(2,1)S(1)} collective-permute-done((bf16[4,16,16,128]{3,2,1,0:T(8,128)(2,1)S(1)}, bf16[4,16,16,128]{3,2,1,0:T(8,128)(2,1)S(1)}, u32[]{:S(2)}, u32[]{:S(2)}) %collective-permute-start.19) | collective-permute-done | bytes 262176 | tf_op jit(solution)/shard_map/ppermute | solution.py:416
  75.7 1.2 %copy-done = bf16[16,128,256]{2,1,0:T(8,128)(2,1)S(1)} copy-done((bf16[16,128,256]{2,1,0:T(8,128)(2,1)S(1)}, bf16[16,128,256]{2,1,0:T(8,128)(2,1)}, u32[]{:S(2)}) %copy-start) | copy-done | bytes 1048600
  76.9 0.1 plane_gather.1.half_ref
  77.0 0.1 collective-permute-start.21
  77.1 0.8 reshape.38
  77.9 1.5 %finish.2 = (f32[9,256,256]{2,1,0:T(8,128)}, f32[3,256,256]{2,1,0:T(8,128)}, f32[4,256,256]{2,1,0:T(8,128)}) custom-call(bf16[16,16,16,128]{3,2,1,0:T(8,128)(2,1)S(1)} %plane_gather.1.half_ref), custom_call_target="tpu_custom_call" | custom-call | bytes 5242880 | tf_op jit(solution)/shard_map/finish/pallas_call | solution.py:392
  79.3 0.4 collective-permute-done.21.half_ref
  79.7 1.5 %finish.3 = (f32[9,256,256]{2,1,0:T(8,128)}, f32[3,256,256]{2,1,0:T(8,128)}, f32[4,256,256]{2,1,0:T(8,128)}) custom-call(bf16[16,16,16,128]{3,2,1,0:T(8,128)(2,1)S(1)} %collective-permute-done.21.half_ref, f32[9,256,256]{2,1,0:T(8,128)} %get-tuple-element.67.rest_0_, ...), custom_call_target="tpu_custom_call", output_to_operand_aliasing={{0}: (1, {}), {1}: (2, {}), {2}: (3, {})} | custom-call | bytes 9437184 | tf_op jit(solution)/shard_map/finish/pallas_call | solution.py:392
  (23 shorter events, 0.1 us)
Async XLA Ops:
  2.3 1.2 %copy-start.1 = (bf16[16,16,8,256]{3,2,1,0:T(8,128)(2,1)S(1)}, bf16[16,16,8,256]{3,2,1,0:T(8,128)(2,1)}, u32[]{:S(2)}) copy-start(bf16[16,16,8,256]{3,2,1,0:T(8,128)(2,1)} %param.6) | copy-start | bytes 3145732
  3.5 8.1 %copy-start.3 = (bf16[2,2,256,256]{3,2,1,0:T(8,128)(2,1)S(1)}, bf16[2,2,256,256]{3,2,1,0:T(8,128)(2,1)}, u32[]{:S(2)}) copy-start(bf16[2,2,256,256]{3,2,1,0:T(8,128)(2,1)} %param.10) | copy-start | bytes 1572868
  3.5 8.1 %copy-start.4 = (bf16[3,256,256]{2,1,0:T(8,128)(2,1)S(1)}, bf16[3,256,256]{2,1,0:T(8,128)(2,1)}, u32[]{:S(2)}) copy-start(bf16[3,256,256]{2,1,0:T(8,128)(2,1)} %wt_ref.5) | copy-start | bytes 1179652
  3.9 7.7 %collective-permute-start = (bf16[128,256]{1,0:T(8,128)(2,1)S(1)}, bf16[128,256]{1,0:T(8,128)(2,1)S(1)}, u32[]{:S(2)}, u32[]{:S(2)}) collective-permute-start(bf16[128,256]{1,0:T(8,128)(2,1)S(1)} %get-tuple-element.41), channel_id=1, source_target_pairs={{0,1},{1,0},{2,3},{3,2},{4,5},{5,4},{6,7},{7,6},{8,9},{9,8},{10,11... | collective-permute-start | bytes 196616 | tf_op jit(solution)/shard_map/ppermute | solution.py:481
  6.9 4.7 %collective-permute-start.1 = (bf16[2,32,256]{2,1,0:T(8,128)(2,1)S(1)}, bf16[2,32,256]{2,1,0:T(8,128)(2,1)S(1)}, u32[]{:S(2)}, u32[]{:S(2)}) collective-permute-start(bf16[2,32,256]{2,1,0:T(8,128)(2,1)S(1)} %get-tuple-element.39._), channel_id=1, source_target_pairs={{2,0},{4,2},{6,4},{8,6},{10,8},{12,10},{14,12},{16,14},{18,16},{20... | collective-permute-start | bytes 98312 | tf_op jit(solution)/shard_map/ppermute | solution.py:476
  11.6 6.2 %copy-start.2 = (bf16[3,3,256,256]{3,2,1,0:T(8,128)(2,1)S(1)}, bf16[3,3,256,256]{3,2,1,0:T(8,128)(2,1)}, u32[]{:S(2)}) copy-start(bf16[3,3,256,256]{3,2,1,0:T(8,128)(2,1)} %param.8) | copy-start | bytes 3538948
  16.7 6.9 %collective-permute-start.3 = (bf16[16,9,16,128]{3,2,1,0:T(8,128)(2,1)S(1)}, bf16[16,9,16,128]{3,2,1,0:T(8,128)(2,1)S(1)}, u32[]{:S(2)}, u32[]{:S(2)}) collective-permute-start(bf16[16,9,16,128]{3,2,1,0:T(8,128)(2,1)S(1)} %get-tuple-element.44._), channel_id=1, source_target_pairs={{0,2},{1,3},{2,0},{3,1},{4,6},{5,7},{6,4},{7,5},{8,10},{9,11},{10,... | collective-permute-start | bytes 1769480 | tf_op jit(solution)/shard_map/ppermute | solution.py:416
  21.6 5.7 %collective-permute-start.2 = (bf16[8,32,256]{2,1,0:T(8,128)(2,1)S(1)}, bf16[8,32,256]{2,1,0:T(8,128)(2,1)S(1)}, u32[]{:S(2)}, u32[]{:S(2)}) collective-permute-start(bf16[8,32,256]{2,1,0:T(8,128)(2,1)S(1)} %get-tuple-element.46.rest_0_), channel_id=1, source_target_pairs={{0,2},{2,4},{4,6},{6,8},{8,10},{10,12},{12,14},{14,16},{16,18},{18... | collective-permute-start | bytes 393224 | tf_op jit(solution)/shard_map/ppermute | solution.py:476
  23.7 8.6 %collective-permute-start.5 = (bf16[4,9,16,128]{3,2,1,0:T(8,128)(2,1)S(1)}, bf16[4,9,16,128]{3,2,1,0:T(8,128)(2,1)S(1)}, u32[]{:S(2)}, u32[]{:S(2)}) collective-permute-start(bf16[4,9,16,128]{3,2,1,0:T(8,128)(2,1)S(1)} %get-tuple-element.51.rest_1_), channel_id=1, source_target_pairs={{0,4},{1,5},{2,6},{3,7},{4,0},{5,1},{6,2},{7,3},{8,12},{9,13},{10,... | collective-permute-start | bytes 442376 | tf_op jit(solution)/shard_map/ppermute | solution.py:416
  25.2 9.5 %collective-permute-start.6 = (bf16[4,9,16,128]{3,2,1,0:T(8,128)(2,1)S(1)}, bf16[4,9,16,128]{3,2,1,0:T(8,128)(2,1)S(1)}, u32[]{:S(2)}, u32[]{:S(2)}) collective-permute-start(bf16[4,9,16,128]{3,2,1,0:T(8,128)(2,1)S(1)} %get-tuple-element.52.rest_2_), channel_id=1, source_target_pairs={{0,1},{1,0},{2,3},{3,2},{4,5},{5,4},{6,7},{7,6},{8,9},{9,8},{10,11... | collective-permute-start | bytes 442376 | tf_op jit(solution)/shard_map/ppermute | solution.py:416
  25.8 9.0 %collective-permute-start.7 = (bf16[4,9,16,128]{3,2,1,0:T(8,128)(2,1)S(1)}, bf16[4,9,16,128]{3,2,1,0:T(8,128)(2,1)S(1)}, u32[]{:S(2)}, u32[]{:S(2)}) collective-permute-start(bf16[4,9,16,128]{3,2,1,0:T(8,128)(2,1)S(1)} %get-tuple-element.53.rest_3_), channel_id=1, source_target_pairs={{0,5},{1,4},{2,7},{3,6},{4,1},{5,0},{6,3},{7,2},{8,13},{9,12},{10,... | collective-permute-start | bytes 442376 | tf_op jit(solution)/shard_map/ppermute | solution.py:416
  34.8 1.8 %collective-permute-start.8 = (bf16[16,7,16,128]{3,2,1,0:T(8,128)(2,1)S(1)}, bf16[16,7,16,128]{3,2,1,0:T(8,128)(2,1)S(1)}, u32[]{:S(2)}, u32[]{:S(2)}) collective-permute-start(bf16[16,7,16,128]{3,2,1,0:T(8,128)(2,1)S(1)} %pass.1), channel_id=1, source_target_pairs={{0,2},{1,3},{2,0},{3,1},{4,6},{5,7},{6,4},{7,5},{8,10},{9,11},{10,... | collective-permute-start | bytes 1376264 | tf_op jit(solution)/shard_map/ppermute | solution.py:416
  36.7 6.1 %collective-permute-start.9 = (bf16[4,7,16,128]{3,2,1,0:T(8,128)(2,1)S(1)}, bf16[4,7,16,128]{3,2,1,0:T(8,128)(2,1)S(1)}, u32[]{:S(2)}, u32[]{:S(2)}) collective-permute-start(bf16[4,7,16,128]{3,2,1,0:T(8,128)(2,1)S(1)} %get-tuple-element.60), channel_id=1, source_target_pairs={{0,4},{1,5},{2,6},{3,7},{4,0},{5,1},{6,2},{7,3},{8,12},{9,13},{10,... | collective-permute-start | bytes 344072 | tf_op jit(solution)/shard_map/ppermute | solution.py:416
  37.1 7.6 %collective-permute-start.10 = (bf16[4,7,16,128]{3,2,1,0:T(8,128)(2,1)S(1)}, bf16[4,7,16,128]{3,2,1,0:T(8,128)(2,1)S(1)}, u32[]{:S(2)}, u32[]{:S(2)}) collective-permute-start(bf16[4,7,16,128]{3,2,1,0:T(8,128)(2,1)S(1)} %get-tuple-element.61), channel_id=1, source_target_pairs={{0,1},{1,0},{2,3},{3,2},{4,5},{5,4},{6,7},{7,6},{8,9},{9,8},{10,11... | collective-permute-start | bytes 344072 | tf_op jit(solution)/shard_map/ppermute | solution.py:416
  38.6 6.1 %collective-permute-start.11 = (bf16[4,7,16,128]{3,2,1,0:T(8,128)(2,1)S(1)}, bf16[4,7,16,128]{3,2,1,0:T(8,128)(2,1)S(1)}, u32[]{:S(2)}, u32[]{:S(2)}) collective-permute-start(bf16[4,7,16,128]{3,2,1,0:T(8,128)(2,1)S(1)} %get-tuple-element.62), channel_id=1, source_target_pairs={{0,5},{1,4},{2,7},{3,6},{4,1},{5,0},{6,3},{7,2},{8,13},{9,12},{10,... | collective-permute-start | bytes 344072 | tf_op jit(solution)/shard_map/ppermute | solution.py:416
  44.8 5.2 %collective-permute-start.12 = (bf16[16,16,128]{2,1,0:T(8,128)(2,1)S(1)}, bf16[16,16,128]{2,1,0:T(8,128)(2,1)S(1)}, u32[]{:S(2)}, u32[]{:S(2)}) collective-permute-start(bf16[16,16,128]{2,1,0:T(8,128)(2,1)S(1)} %get-tuple-element.64), channel_id=1, source_target_pairs={{0,8},{1,9},{2,10},{3,11},{4,12},{5,13},{6,14},{7,15},{8,0},{9,1},... | collective-permute-start | bytes 196616 | tf_op jit(solution)/shard_map/ppermute | solution.py:416
  47.4 6.7 %collective-permute-start.13 = (bf16[16,16,128]{2,1,0:T(8,128)(2,1)S(1)}, bf16[16,16,128]{2,1,0:T(8,128)(2,1)S(1)}, u32[]{:S(2)}, u32[]{:S(2)}) collective-permute-start(bf16[16,16,128]{2,1,0:T(8,128)(2,1)S(1)} %get-tuple-element.65), channel_id=1, source_target_pairs={{0,16},{1,17},{2,18},{3,19},{4,20},{5,21},{6,22},{7,23},{8,24},{9,... | collective-permute-start | bytes 196616 | tf_op jit(solution)/shard_map/ppermute | solution.py:416
  50.0 6.1 %collective-permute-start.14 = (bf16[16,16,128]{2,1,0:T(8,128)(2,1)S(1)}, bf16[16,16,128]{2,1,0:T(8,128)(2,1)S(1)}, u32[]{:S(2)}, u32[]{:S(2)}) collective-permute-start(bf16[16,16,128]{2,1,0:T(8,128)(2,1)S(1)} %get-tuple-element.66), channel_id=1, source_target_pairs={{0,24},{1,25},{2,26},{3,27},{4,28},{5,29},{6,30},{7,31},{8,16},{9,... | collective-permute-start | bytes 196616 | tf_op jit(solution)/shard_map/ppermute | solution.py:416
  56.1 6.2 %collective-permute-start.17 = (bf16[16,16,128]{2,1,0:T(8,128)(2,1)S(1)}, bf16[16,16,128]{2,1,0:T(8,128)(2,1)S(1)}, u32[]{:S(2)}, u32[]{:S(2)}) collective-permute-start(bf16[16,16,128]{2,1,0:T(8,128)(2,1)S(1)} %line_sum.1.a_ref), channel_id=1, source_target_pairs={{0,24},{1,25},{2,26},{3,27},{4,28},{5,29},{6,30},{7,31},{8,16},{9,... | collective-permute-start | bytes 196616 | tf_op jit(solution)/shard_map/ppermute | solution.py:416
  57.5 6.2 %collective-permute-start.16 = (bf16[16,16,128]{2,1,0:T(8,128)(2,1)S(1)}, bf16[16,16,128]{2,1,0:T(8,128)(2,1)S(1)}, u32[]{:S(2)}, u32[]{:S(2)}) collective-permute-start(bf16[16,16,128]{2,1,0:T(8,128)(2,1)S(1)} %line_sum.1.a_ref), channel_id=1, source_target_pairs={{0,16},{1,17},{2,18},{3,19},{4,20},{5,21},{6,22},{7,23},{8,24},{9,... | collective-permute-start | bytes 196616 | tf_op jit(solution)/shard_map/ppermute | solution.py:416
  57.5 6.2 %collective-permute-start.15 = (bf16[16,16,128]{2,1,0:T(8,128)(2,1)S(1)}, bf16[16,16,128]{2,1,0:T(8,128)(2,1)S(1)}, u32[]{:S(2)}, u32[]{:S(2)}) collective-permute-start(bf16[16,16,128]{2,1,0:T(8,128)(2,1)S(1)} %line_sum.1.a_ref), channel_id=1, source_target_pairs={{0,8},{1,9},{2,10},{3,11},{4,12},{5,13},{6,14},{7,15},{8,0},{9,1},... | collective-permute-start | bytes 196616 | tf_op jit(solution)/shard_map/ppermute | solution.py:416
  60.6 7.1 %collective-permute-start.4 = (bf16[64,256]{1,0:T(8,128)(2,1)S(1)}, bf16[64,256]{1,0:T(8,128)(2,1)S(1)}, u32[]{:S(2)}, u32[]{:S(2)}) collective-permute-start(bf16[64,256]{1,0:T(8,128)(2,1)S(1)} %get-tuple-element.56), channel_id=1, source_target_pairs={{0,1},{1,0},{2,3},{3,2},{4,5},{5,4},{6,7},{7,6},{8,9},{9,8},{10,11... | collective-permute-start | bytes 98312 | tf_op jit(solution)/shard_map/ppermute | solution.py:481
  63.7 10.7 %collective-permute-start.20 = (bf16[4,16,16,128]{3,2,1,0:T(8,128)(2,1)S(1)}, bf16[4,16,16,128]{3,2,1,0:T(8,128)(2,1)S(1)}, u32[]{:S(2)}, u32[]{:S(2)}) collective-permute-start(bf16[4,16,16,128]{3,2,1,0:T(8,128)(2,1)S(1)} %line_gather.1.rest_0_.a_ref), channel_id=1, source_target_pairs={{0,5},{1,4},{2,7},{3,6},{4,1},{5,0},{6,3},{7,2},{8,13},{9,12},{10,... | collective-permute-start | bytes 786440 | tf_op jit(solution)/shard_map/ppermute | solution.py:416
  65.4 10.3 %collective-permute-start.19 = (bf16[4,16,16,128]{3,2,1,0:T(8,128)(2,1)S(1)}, bf16[4,16,16,128]{3,2,1,0:T(8,128)(2,1)S(1)}, u32[]{:S(2)}, u32[]{:S(2)}) collective-permute-start(bf16[4,16,16,128]{3,2,1,0:T(8,128)(2,1)S(1)} %line_gather.1.rest_0_.a_ref), channel_id=1, source_target_pairs={{0,1},{1,0},{2,3},{3,2},{4,5},{5,4},{6,7},{7,6},{8,9},{9,8},{10,11... | collective-permute-start | bytes 786440 | tf_op jit(solution)/shard_map/ppermute | solution.py:416
  65.9 9.8 %collective-permute-start.18 = (bf16[4,16,16,128]{3,2,1,0:T(8,128)(2,1)S(1)}, bf16[4,16,16,128]{3,2,1,0:T(8,128)(2,1)S(1)}, u32[]{:S(2)}, u32[]{:S(2)}) collective-permute-start(bf16[4,16,16,128]{3,2,1,0:T(8,128)(2,1)S(1)} %line_gather.1.rest_0_.a_ref), channel_id=1, source_target_pairs={{0,4},{1,5},{2,6},{3,7},{4,0},{5,1},{6,2},{7,3},{8,12},{9,13},{10,... | collective-permute-start | bytes 786440 | tf_op jit(solution)/shard_map/ppermute | solution.py:416
  75.7 1.2 %copy-start = (bf16[16,128,256]{2,1,0:T(8,128)(2,1)S(1)}, bf16[16,128,256]{2,1,0:T(8,128)(2,1)}, u32[]{:S(2)}) copy-start(bf16[16,128,256]{2,1,0:T(8,128)(2,1)} %grad_x.1.rest_0_) | copy-start | bytes 3145732
  77.0 2.7 %collective-permute-start.21 = (bf16[16,16,16,128]{3,2,1,0:T(8,128)(2,1)S(1)}, bf16[16,16,16,128]{3,2,1,0:T(8,128)(2,1)S(1)}, u32[]{:S(2)}, u32[]{:S(2)}) collective-permute-start(bf16[16,16,16,128]{3,2,1,0:T(8,128)(2,1)S(1)} %plane_gather.1.half_ref), channel_id=1, source_target_pairs={{0,2},{1,3},{2,0},{3,1},{4,6},{5,7},{6,4},{7,5},{8,10},{9,11},{10,... | collective-permute-start | bytes 3145736 | tf_op jit(solution)/shard_map/ppermute | solution.py:416

commit v5 on v4

--- a/solution.py
+++ b/solution.py
@@ -70,20 +70,27 @@
     return jnp.where(slot_mask(total.shape, count), total, 0.0).astype(BF)
 
 
-def place_bits():
+def halving_bits():
     t, g = lax.axis_index("tm"), lax.axis_index("grp")
-    return t & 1, ((t >> 1) & 1) + 2 * (g & 1), (t >> 2) & 3
+    x, y, z0, z1 = (t >> 1) & 1, g & 1, (t >> 2) & 1, (t >> 3) & 1
+    return t & 1, ((x, y, z0, z1), (z0, x, y, z1))
+
+
+def round_bit(k):
+    core, (first, second) = halving_bits()
+    return jnp.where(core == 0, first[k], second[k])
 
 
 def split_cores(value, keep_ref, send_ref, k):
-    core, _, _ = place_bits()
+    core, _ = halving_bits()
     low, high = value[:, : CH // 2].astype(BF), value[:, CH // 2 :].astype(BF)
     keep_ref[:, k] = jnp.where(core == 0, low, high).reshape(16, 16, CH // 2)
     send_ref[:, k] = jnp.where(core == 0, high, low).reshape(16, 16, CH // 2)
 
 
 def edges_kernel(bands, count_ref, x_ref, cot_ref, *rest):
-    outs, nxt_ref, buf, sems = rest[: len(rest) - 3], rest[-3], rest[-2], rest[-1]
+    outs, (nxt_ref, token_ref, buf, sems) = rest[:-4], rest[-4:]
+    token_ref[...] = jnp.zeros_like(token_ref)
     count = count_ref[0]
     band = lax.axis_index("grp")
     wide = x_ref.shape[1]
@@ -109,8 +116,17 @@
         outs[k][...] = silu_norm(v).astype(BF)
 
 
-def acts_kernel(count_ref, x_ref, _, xt_ref, acts_ref, at_ref):
+def acts_kernel(count_ref, x_hbm, _, xt_ref, acts_ref, at_ref, x_ref, sems):
     count = count_ref[0]
+    pieces = sems.shape[0]
+    size = x_hbm.shape[1] // pieces
+
+    def copy_of(k):
+        at = pl.ds(pl.multiple_of(k * size, size), size)
+        return pltpu.make_async_copy(x_hbm.at[:, at, :], x_ref.at[:, at, :], sems.at[k])
+
+    for k in range(pieces):
+        copy_of(k).start()
     rows, cols = xt_ref.shape[0], xt_ref.shape[1]
     edge = jnp.zeros((rows + 2, SLOTS, CH), BF)
     acts_ref[:, 0] = edge
@@ -119,6 +135,11 @@
 
     def rows_of(q, _):
         at = pl.multiple_of(q * 16, 16)
+
+        @pl.when(q % 2 == 0)
+        def _():
+            copy_of(q // 2).wait()
+
         piece = x_ref[:, pl.ds(at, 16), :].reshape(SLOTS * 16, CH)
         v = mm(place, piece)
         xt_ref[pl.ds(2 * q, 2)] = v.astype(BF).reshape(2, cols, SLOTS, CH)
@@ -264,23 +285,28 @@
 
 
 def grad_x_kernel(
-    bands, count_ref, xt_ref, gy_ref, gs_ref, top_ref, bot_ref, wt_ref, wd_ref, ws_ref, *rest
+    part, bands, count_ref, xt_ref, gy_ref, gs_ref, halo_ref, wt_ref, wd_ref, ws_ref, *rest
 ):
-    out_ref, pad_ref, buf, sems = rest[-4:]
+    out_ref, token_ref, pad_ref, buf, sems = rest[-5:]
     count = count_ref[0]
     band = lax.axis_index("grp")
     rows, cols = xt_ref.shape[0], xt_ref.shape[1]
-    pad_ref[1 : rows + 1] = gs_ref[...]
+    half = rows // 2
+    if part == 0:
+        flag, i, row = band > 0, 1, 0
+        pad_ref[1 : half + 2] = gs_ref[0 : half + 1]
+    else:
+        flag, i, row = band < bands - 1, 0, half + 1
+        pad_ref[0 : half + 1] = gs_ref[half - 1 :]
     edge = jnp.zeros((SLOTS, CH), BF)
-    for ref, flag, i, row in ((top_ref, band > 0, 1, 0), (bot_ref, band < bands - 1, 0, rows + 1)):
-        pair = [
-            mm_nt(ref[...], wd_ref[i * 2 + j]).astype(BF).reshape(cols // 2, SLOTS, CH)
-            for j in range(2)
-        ]
-        g = jnp.stack(pair, axis=1).reshape(cols, SLOTS, CH)
-        pad_ref[row, 0] = edge
-        pad_ref[row, 1 : cols + 1] = grad_of_temporal(g, wt_ref, jnp.where(flag, count, 0))
-        pad_ref[row, cols + 1] = edge
+    pair = [
+        mm_nt(halo_ref[...], wd_ref[i * 2 + j]).astype(BF).reshape(cols // 2, SLOTS, CH)
+        for j in range(2)
+    ]
+    g = jnp.stack(pair, axis=1).reshape(cols, SLOTS, CH)
+    pad_ref[row, 0] = edge
+    pad_ref[row, 1 : cols + 1] = grad_of_temporal(g, wt_ref, jnp.where(flag, count, 0))
+    pad_ref[row, cols + 1] = edge
     back = to_frames(16)
 
     def rows_of(q, _):
@@ -292,7 +318,7 @@
                 )
                 term = mm_nt(left, ws_ref[i * 3 + j])
                 total = term if total is None else total + term
-        at = 4 * q
+        at = part * half + 4 * q
         v = xt_ref[pl.ds(at, 4)].reshape(4 * cols * SLOTS, CH).astype(F32)
         r = lax.rsqrt(jnp.mean(v * v, axis=-1, keepdims=True) + 1e-06)
         u = v * r
@@ -308,73 +334,65 @@
             buf[:, pl.ds(pl.multiple_of((2 * q + k) * 16, 16), 16), :] = o.reshape(SLOTS, 16, CH)
         return 0
 
-    lax.fori_loop(0, rows // 4, rows_of, 0)
-    copy = pltpu.make_async_copy(buf, out_ref, sems.at[0])
+    lax.fori_loop(0, half // 4, rows_of, 0)
+    size = half * cols
+    copy = pltpu.make_async_copy(buf, out_ref.at[:, part * size : part * size + size, :], sems.at[0])
+    token_ref[...] = jnp.zeros_like(token_ref)
     copy.start()
     copy.wait()
 
 
-def plane_send_kernel(keep_ref, got_ref, *rest):
-    outs = rest[-4:]
-    _, p, _ = place_bits()
-    for r in range(4):
-        at = pl.ds((p ^ r) * 4, 4)
-        outs[r][...] = (keep_ref[at].astype(F32) + got_ref[at].astype(F32)).astype(BF)
-
-
-def total_at(refs, z):
-    return functools.reduce(lambda a, b: a + b, [ref[z].astype(F32) for ref in refs]).astype(BF)
-
-
-def line_send_kernel(chains, *refs):
-    outs = refs[-4:]
-    _, _, z = place_bits()
-    for r in range(4):
-        at = 0
-        for c in range(chains):
-            ins = refs[4 * c : 4 * c + 4]
-            n = ins[0].shape[1]
-            outs[r][at : at + n] = total_at(ins, z ^ r)
-            at += n
-
-
-def line_sum_kernel(a_ref, b_ref, c_ref, d_ref, out_ref):
-    parts = [ref[...].astype(F32) for ref in (a_ref, b_ref, c_ref, d_ref)]
-    out_ref[...] = (parts[0] + parts[1] + parts[2] + parts[3]).astype(BF)
-
-
-def line_gather_kernel(a_ref, b_ref, c_ref, d_ref, out_ref):
-    _, _, z = place_bits()
-    for r, ref in enumerate((a_ref, b_ref, c_ref, d_ref)):
-        out_ref[z ^ r] = ref[...]
-
-
-def plane_gather_kernel(a_ref, b_ref, c_ref, d_ref, *rest):
+def halve_kernel(k, chains, *refs):
+    send_ref, keep_ref = refs[-2:]
+    bit = round_bit(k)
+    m = send_ref.shape[0]
+    at = 0
+    for c in range(chains):
+        a, b = refs[2 * c : 2 * c + 2]
+        n = a.shape[1]
+        for ref, side in ((send_ref, 1 - bit), (keep_ref, bit)):
+            part = pl.ds(side * m, m)
+            ref[:, at : at + n] = (a[part].astype(F32) + b[part].astype(F32)).astype(BF)
+        at += n
+
+
+def add_kernel(a_ref, b_ref, out_ref):
+    out_ref[...] = (a_ref[...].astype(F32) + b_ref[...].astype(F32)).astype(BF)
+
+
+def double_kernel(k, own_ref, got_ref, *rest):
     out_ref = rest[-1]
-    _, p, _ = place_bits()
-    for r, ref in enumerate((a_ref, b_ref, c_ref, d_ref)):
-        out_ref[pl.ds((p ^ r) * 4, 4)] = ref[...]
+    bit = round_bit(k)
+    m = own_ref.shape[0]
+    out_ref[pl.ds(bit * m, m)] = own_ref[...]
+    out_ref[pl.ds((1 - bit) * m, m)] = got_ref[...]
 
 
 def pass_kernel(*_):
     pass
 
 
-def finish_kernel(own, half_ref, *rest):
-    buf, sems = rest[-2:]
-    outs = rest[-5:-2]
-    core, _, _ = place_bits()
-    at = pl.multiple_of((core if own else 1 - core) * (CH // 2), CH // 2)
+def finish_kernel(which, *refs):
+    buf, sems = refs[-2:]
+    outs, token_ref = refs[-6:-3], refs[-3]
+    token_ref[...] = jnp.zeros_like(token_ref)
+    core, (first, second) = halving_bits()
+    mine = jnp.where(core == 0, first[0], second[0])
+    other = jnp.where(core == 0, second[0], first[0])
     copies = []
     k = 0
-    for out in outs:
-        for m in range(out.shape[0]):
-            buf[k] = half_ref[:, k].reshape(CH, CH // 2).astype(F32)
-            copies.append(
-                pltpu.make_async_copy(buf.at[k], out.at[m, :, pl.ds(at, CH // 2)], sems.at[k])
-            )
-            copies[-1].start()
-            k += 1
+    for ref, (sibling, far) in zip(refs, which):
+        rows = other if sibling else mine
+        rows = pl.ds(pl.multiple_of((1 - rows if far else rows) * (CH // 2), CH // 2), CH // 2)
+        cols = pl.ds(pl.multiple_of((1 - core if sibling else core) * (CH // 2), CH // 2), CH // 2)
+        m = 0
+        for out in outs:
+            for o in range(out.shape[0]):
+                buf[k] = ref[:, m].reshape(CH // 2, CH // 2).astype(F32)
+                copies.append(pltpu.make_async_copy(buf.at[k], out.at[o, rows, cols], sems.at[k]))
+                copies[-1].start()
+                k += 1
+                m += 1
     for copy in copies:
         copy.wait()
 
@@ -383,9 +401,10 @@
 SMEM = pl.BlockSpec(memory_space=pltpu.SMEM)
 ANY = pl.BlockSpec(memory_space=pl.ANY)
 HBM = pl.BlockSpec(memory_space=pltpu.HBM)
-
-
-def call(kernel, name, ins, outs, scratch=(), flops=0, alias=None):
+TOKEN = (VMEM, (8, 128), F32)
+
+
+def call(kernel, name, ins, outs, scratch=(), flops=0, alias=None, grant=10):
     shapes = [jax.ShapeDtypeStruct(o[1], o[2] if len(o) > 2 else BF) for o in outs]
     moved = sum(a.size * a.dtype.itemsize for s, a in ins if s is not ANY)
     moved += sum(s.size * s.dtype.itemsize for s in shapes)
@@ -395,7 +414,7 @@
         in_specs=[s for s, _ in ins],
         out_specs=[o[0] for o in outs],
         scratch_shapes=list(scratch),
-        compiler_params=pltpu.CompilerParams(vmem_limit_bytes=10 * 2**20),
+        compiler_params=pltpu.CompilerParams(vmem_limit_bytes=grant * 2**20),
         cost_estimate=pl.CostEstimate(flops=flops, bytes_accessed=moved, transcendentals=0),
         input_output_aliases=alias or {},
         name=name,
@@ -408,66 +427,57 @@
 def plan(tm, grp):
     low, total = grp.bit_length() - 1, (tm * grp).bit_length() - 1
     used = [low, low + 1, 0, low + 2, low + 3]
-    return used + [b for b in range(total) if b not in used]
-
-
-def swap(value, tm, grp, *bits):
-    flip = sum(1 << b for b in bits)
-    return lax.ppermute(value, AXES, [(d, d ^ flip) for d in range(tm * grp)])
-
-
-def core_round(send, tm, grp):
-    return swap(send, tm, grp, plan(tm, grp)[0])
-
-
-def plane_send(keep, got, after):
-    n = keep.shape[1]
-    ins = [(VMEM, keep), (VMEM, got)] + [(ANY, a) for a in after]
-    return call(plane_send_kernel, "plane_send", ins, [(VMEM, (4, n, 16, CH // 2))] * 4)
-
-
-def plane_round(parts, tm, grp):
-    _, x, y = plan(tm, grp)[:3]
-    return [parts[0], swap(parts[1], tm, grp, x), swap(parts[2], tm, grp, y), swap(parts[3], tm, grp, x, y)]
-
-
-def line_send(*chains):
-    n = sum(parts[0].shape[1] for parts in chains)
-    ins = [(VMEM, a) for parts in chains for a in parts]
-    kernel = functools.partial(line_send_kernel, len(chains))
-    return call(kernel, "line_send", ins, [(VMEM, (n, 16, CH // 2))] * 4)
-
-
-def line_round(parts, tm, grp):
-    _, _, _, a, b = plan(tm, grp)[:5]
-    return [parts[0], swap(parts[1], tm, grp, a), swap(parts[2], tm, grp, b), swap(parts[3], tm, grp, a, b)]
-
-
-def line_gather(parts, tm, grp):
-    (mine,) = call(line_sum_kernel, "line_sum", [(VMEM, a) for a in parts], [(VMEM, parts[0].shape)])
-    for bit in plan(tm, grp)[5:]:
-        mine = (mine.astype(F32) + swap(mine, tm, grp, bit).astype(F32)).astype(BF)
-    parts = line_round([mine] * 4, tm, grp)
-    return call(
-        line_gather_kernel, "line_gather", [(VMEM, a) for a in parts], [(VMEM, (4,) + mine.shape)]
-    )[0]
-
-
-def plane_gather(mine, parts, after):
-    ins = [(VMEM, a) for a in parts] + [(ANY, a) for a in after]
-    return call(plane_gather_kernel, "plane_gather", ins, [(VMEM, (16,) + mine.shape[1:])])[0]
-
-
-def finish(own, half, before):
-    n = half.shape[1]
-    return call(
-        functools.partial(finish_kernel, own),
-        "finish",
-        [(VMEM, half)] + [(HBM, a) for a in before],
-        [(HBM, (m, CH, CH), F32) for m in (9, 3, 4)],
-        [pltpu.VMEM((n, CH, CH // 2), F32), pltpu.SemaphoreType.DMA((n,))],
-        alias={1 + i: i for i in range(len(before))},
-    )
+    return used, [b for b in range(total) if b not in used]
+
+
+def swap(value, tm, grp, first, second):
+    core = plan(tm, grp)[0][0]
+    pairs = [(d, d ^ (1 << (second if (d >> core) & 1 else first))) for d in range(tm * grp)]
+    return lax.ppermute(value, AXES, pairs)
+
+
+def core_round(value, tm, grp):
+    core = plan(tm, grp)[0][0]
+    return swap(value, tm, grp, core, core)
+
+
+def link_round(k, value, tm, grp):
+    _, x, y, z0, z1 = plan(tm, grp)[0]
+    return swap(value, tm, grp, (x, y, z0, z1)[k], (z0, x, y, z1)[k])
+
+
+def halve(k, chains, after=()):
+    n = sum(a.shape[1] for a, _ in chains)
+    shape = (chains[0][0].shape[0] // 2, n, 16, CH // 2)
+    ins = [(VMEM, a) for pair in chains for a in pair] + [(ANY, a) for a in after]
+    kernel = functools.partial(halve_kernel, k, len(chains))
+    return call(kernel, f"halve_{k}", ins, [(VMEM, shape)] * 2)
+
+
+def double(k, own, got, after=()):
+    shape = (own.shape[0] * 2,) + own.shape[1:]
+    ins = [(VMEM, own), (VMEM, got)] + [(ANY, a) for a in after]
+    return call(functools.partial(double_kernel, k), f"double_{k}", ins, [(VMEM, shape)])[0]
+
+
+def passed(value, after):
+    ins = [(ANY, value)] + [(ANY, a) for a in after]
+    return call(pass_kernel, "pass", ins, [(ANY, value.shape)], alias={0: 0})[0]
+
+
+def finish(quarters, before):
+    n = quarters[0][0].shape[1] * len(quarters)
+    *outs, token = (
+        call(
+            functools.partial(finish_kernel, [q[1:] for q in quarters]),
+            "finish",
+            [(VMEM, q[0]) for q in quarters] + [(HBM, a) for a in before],
+            [(HBM, (m, CH, CH), F32) for m in (9, 3, 4)] + [TOKEN],
+            [pltpu.VMEM((n, CH // 2, CH // 2), F32), pltpu.SemaphoreType.DMA((n,))],
+            alias={len(quarters) + i: i for i in range(len(before))},
+        )
+    )
+    return outs, token
 
 
 def along(value, axis, by):
@@ -498,21 +508,23 @@
     dma = pltpu.SemaphoreType.DMA
 
     sides = 1 if grp == 2 else 2
-    *edge, nxt = call(
+    *edge, nxt, token = call(
         functools.partial(edges_kernel, grp),
         "edges",
         [count, (HBM, x), (VMEM, cot)],
-        [(VMEM, (cols * slots, ch))] * sides + [(VMEM, (2, wide // 4, ch))],
+        [(VMEM, (cols * slots, ch))] * sides + [(VMEM, (2, wide // 4, ch)), TOKEN],
         [pltpu.VMEM((sides, slots, 16, ch), BF), dma((sides,))],
         flops=tap // 8,
+        grant=56,
     )
     top, bot = from_bands(edge)
     nxt_got = along(nxt, "tm", -1)
     xt, acts, at = call(
         acts_kernel,
         "acts",
-        [count, (VMEM, x), (ANY, nxt)],
+        [count, (HBM, x), (ANY, token)],
         [(VMEM, tile), (VMEM, padded), (VMEM, (ch, (rows + 2) * 128))],
+        [pltpu.VMEM((slots, wide, ch), BF), dma((4,))],
         flops=2 * tap,
     )
     half = (16, 9, 16, ch // 2)
@@ -536,43 +548,57 @@
         alias={3: 0},
     )
     prev = along(last_two, "tm", 1)
-    parts_a = plane_send(keep_a, got_a, [last_two])
+    send_a, keep_a = halve(0, [(keep_a, got_a)], [last_two])
     cot_top, cot_bot = from_bands(edge)
     half = (16, 7, 16, ch // 2)
     down, keep_b, send_b = call(
         forward_kernel,
         "forward",
         [count, (VMEM, xt), (VMEM, sp), (VMEM, prev), (VMEM, cott), (VMEM, gy), (VMEM, wt), (VMEM, wd)]
-        + [(ANY, a) for a in parts_a],
+        + [(ANY, send_a)],
         [(VMEM, (slots, wide // 4, ch)), (VMEM, half), (VMEM, half)],
         [pltpu.VMEM(s, BF) for s in (tile, (ch, slots * wide), tile, tile, tile)],
         flops=10 * tap,
     )
-    parts_a = plane_round(parts_a, tm, grp)
-    (send_b,) = call(
-        pass_kernel,
-        "pass",
-        [(ANY, send_b)] + [(ANY, a) for a in parts_a[1:]],
-        [(ANY, send_b.shape)],
-        alias={0: 0},
-    )
-    parts_b = plane_send(keep_b, core_round(send_b, tm, grp), [])
-    parts_b = plane_round(parts_b, tm, grp)
-    mine = line_gather(line_round(line_send(parts_a, parts_b), tm, grp), tm, grp)
-    parts = plane_round([mine] * 4, tm, grp)
-    (grad_x,) = call(
-        functools.partial(grad_x_kernel, grp),
-        "grad_x",
-        [count, (VMEM, xt), (VMEM, gy), (VMEM, gs), (VMEM, cot_top), (VMEM, cot_bot), (VMEM, wt),
-         (VMEM, wd), (VMEM, ws), (ANY, mine)],
-        [(HBM, (slots, wide, ch))],
-        [pltpu.VMEM(padded, BF), pltpu.VMEM((slots, wide, ch), BF), dma((1,))],
-        flops=10 * tap,
-    )
-    mine = plane_gather(mine, parts, [grad_x])
-    got = core_round(mine, tm, grp)
-    outs = list(finish(True, mine, []))
-    sum_s, sum_t, sum_d = finish(False, got, outs)
+    got_a = link_round(0, send_a, tm, grp)
+    send_b = passed(send_b, [got_a])
+    send_b, keep_b = halve(0, [(keep_b, core_round(send_b, tm, grp))])
+    got_b = link_round(0, send_b, tm, grp)
+    send, keep = halve(1, [(keep_a, got_a), (keep_b, got_b)])
+    for k in (2, 3):
+        send, keep = halve(k, [(keep, link_round(k - 1, send, tm, grp))])
+    got = link_round(3, send, tm, grp)
+    (mine,) = call(add_kernel, "add", [(VMEM, keep), (VMEM, got)], [(VMEM, keep.shape)])
+    for bit in plan(tm, grp)[1]:
+        mine = (mine.astype(F32) + swap(mine, tm, grp, bit, bit).astype(F32)).astype(BF)
+    for k in (3, 2):
+        mine = double(k, mine, link_round(k, mine, tm, grp))
+
+    def grad_x_part(part, halo, before, after):
+        return call(
+            functools.partial(grad_x_kernel, part, grp),
+            "grad_x",
+            [count, (VMEM, xt), (VMEM, gy), (VMEM, gs), (VMEM, halo), (VMEM, wt), (VMEM, wd), (VMEM, ws)]
+            + [(HBM, a) for a in before] + [(ANY, a) for a in after],
+            [(HBM, (slots, wide, ch)), TOKEN],
+            [pltpu.VMEM((rows // 2 + 2, cols + 2, slots, ch), BF),
+             pltpu.VMEM((slots, wide // 2, ch), BF), dma((1,))],
+            flops=5 * tap,
+            alias={8: 0} if before else None,
+        )
+
+    got = link_round(1, mine, tm, grp)
+    grad_x, token = grad_x_part(0, cot_top, [], [mine])
+    mine = double(1, mine, got, [token])
+    far = link_round(0, mine, tm, grp)
+    side = core_round(mine, tm, grp)
+    grad_x, token = grad_x_part(1, cot_bot, [grad_x], [mine])
+    outs, ended = finish([(mine, False, False), (side, True, False)], [])
+    far = passed(far, [token, ended])
+    side = core_round(far, tm, grp)
+    outs, _ = finish([(far, False, True)], outs)
+    outs, _ = finish([(side, True, True)], outs)
+    sum_s, sum_t, sum_d = outs
     return (
         down.reshape(cotangent.shape),
         grad_x.reshape(frames_in.shape),

time: 81.5 us -> 97.9 us (1.20)
  waiting for transfers between devices: 19.1 us -> 29.6 us
  Pallas kernels: 27.7 us -> 33.2 us
  starting transfers between devices: 28.7 us -> 30 us
  local copies, waits for them, and re-layouts: 4.24 us -> 3.19 us
    ppermute x18 -> x13, waiting for transfers between devices: 18.7 us -> 24.9 us  [swap(): return lax.ppermute(value, AXES, pairs)]
    pallas_call x15 -> x21, Pallas kernels: 27.7 us -> 33.2 us  [call(): pl.pallas_call(kernel, out_shape=shapes, in_specs=[s for s, _ in ins], ou...]
    ppermute x2, waiting for transfers between devices: 0.39 us -> 4.7 us  [from_bands(): got = lax.ppermute(parts[0], 'grp', [(0, 1), (1, 0)])]
    unnamed x10 -> x12, local copies, waits for them, and re-layouts: 2.46 us -> 0.71 us
    ppermute x18 -> x13, starting transfers between devices: 21.7 us -> 22.2 us  [swap(): return lax.ppermute(value, AXES, pairs)]
  transfers between devices with their start and end apart: 22 -> 17, of which waited for: 11 -> 10; matrix products, arithmetic and copies ran while one was open for 1% -> 1% of each run, Pallas kernels for 25% -> 24%
where the time goes in v5:
time: 97.9 us; the launch traced here: 97.6 us
  Pallas kernels  33.2 us (34%)
  starting transfers between devices  30 us (31%)
  waiting for transfers between devices  29.6 us (30%)
  local copies, waits for them, and re-layouts  3.19 us (3%)
  between operations  1.61 us (2%)
    pallas_call x21, Pallas kernels, call(): pl.pallas_call(kernel, out_shape=shapes, in_specs=[s for s, _ in ins], ou...  33.2 us
    ppermute x13, waiting for transfers between devices, swap(): return lax.ppermute(value, AXES, pairs)  24.9 us
    ppermute x13, starting transfers between devices, swap(): return lax.ppermute(value, AXES, pairs)  22.2 us
    ppermute x2, waiting for transfers between devices, from_bands(): got = lax.ppermute(parts[0], 'grp', [(0, 1), (1, 0)])  4.7 us
    ppermute x2, starting transfers between devices, from_bands(): got = lax.ppermute(parts[0], 'grp', [(0, 1), (1, 0)])  4.59 us
    ppermute x2, starting transfers between devices, along(): return lax.ppermute(value, axis, pairs)  3.23 us
  transfers between devices with their start and end apart: 17, of which 10 were waited for; matrix products, arithmetic and copies ran while one was open for 1% of the time, Pallas kernels for 24%

profile of v5, /device:TPU:0, one launch (start us, length us, event | category | flops | bytes accessed | tf_op | source)
XLA Modules:
  0.0 97.6 jit_solution(11744377348289747434)
XLA Ops:
  0.6 0.0 copy-start.4
  1.4 1.7 %reshape.35.cot_ref = bf16[16,32,256]{2,1,0:T(8,128)(2,1)} reshape(bf16[16,8,4,256]{3,2,1,0:T(4,128)(2,1)} %param.11) | data formatting | bytes 524288 | tf_op jit(solution)/shard_map/reshape | solution.py:500
  3.1 2.9 %edges.1 = (bf16[128,256]{1,0:T(8,128)(2,1)}, bf16[2,32,256]{2,1,0:T(8,128)(2,1)}, f32[8,128]{1,0:T(8,128)}) custom-call(s32[1]{0:T(128)S(6)} %copy.33.count_ref, bf16[16,128,256]{2,1,0:T(8,128)(2,1)} %bitcast.13, bf16[16,32,256]{2,1,0:T(8,128)(2,1)} %reshape.35.cot_ref), custom_call_target="tpu_custom_call" | custom-call | flops 33554432 | bytes 1413124 | tf_op jit(solution)/shard_map/edges/pallas_call | solution.py:411
  6.0 3.0 %collective-permute-start = (bf16[128,256]{1,0:T(8,128)(2,1)}, bf16[128,256]{1,0:T(8,128)(2,1)S(1)}, u32[]{:S(2)}, u32[]{:S(2)}) collective-permute-start(bf16[128,256]{1,0:T(8,128)(2,1)} %get-tuple-element.48), channel_id=1, source_target_pairs={{0,1},{1,0},{2,3},{3,2},{4,5},{5,4},{6,7},{7,6},{8,9},{9,8},{10,11... | collective-permute-start | bytes 196616 | tf_op jit(solution)/shard_map/ppermute | solution.py:491
  9.0 1.3 %collective-permute-start.1 = (bf16[2,32,256]{2,1,0:T(8,128)(2,1)}, bf16[2,32,256]{2,1,0:T(8,128)(2,1)S(1)}, u32[]{:S(2)}, u32[]{:S(2)}) collective-permute-start(bf16[2,32,256]{2,1,0:T(8,128)(2,1)} %get-tuple-element.51), channel_id=1, source_target_pairs={{2,0},{4,2},{6,4},{8,6},{10,8},{12,10},{14,12},{16,14},{18,16},{20... | collective-permute-start | bytes 98312 | tf_op jit(solution)/shard_map/ppermute | solution.py:486
  10.3 0.0 copy-start.5
  10.4 0.7 copy-done.5
  11.0 3.5 %acts.1 = (bf16[16,8,16,256]{3,2,1,0:T(8,128)(2,1)S(1)}, bf16[18,10,16,256]{3,2,1,0:T(8,128)(2,1)S(1)}, bf16[256,2304]{1,0:T(8,128)(2,1)S(1)}) custom-call(s32[1]{0:T(128)S(6)} %copy.33.count_ref, bf16[16,128,256]{2,1,0:T(8,128)(2,1)S(1)} %bitcast.14, f32[8,128]{1,0:T(8,128)S(1)} %copy-done.5), custom_call_target="tpu_custom_call" | custom-call | flops 536870912 | bytes 4751364 | tf_op jit(solution)/shard_map/acts/pallas_call | solution.py:411
  14.5 0.0 collective-permute-done.1.nxt_ref
  14.6 0.0 copy-start
  14.6 5.0 %grad_spatial.1 = (bf16[256,2304]{1,0:T(8,128)(2,1)S(1)}, bf16[8,4,16,256]{3,2,1,0:T(8,128)(2,1)S(1)}, bf16[16,8,16,256]{3,2,1,0:T(8,128)(2,1)S(1)}, bf16[16,10,...) custom-call(s32[1]{0:T(128)S(6)} %copy.33.count_ref, ...), custom_call_target="tpu_custom_call", output_to_operand_aliasing={{0}: (1, {})} | custom-call | flops 3758096384 | bytes 7536644 | tf_op jit(solution)/shard_map/grad_spatial/pallas_call | solution.py:411
  19.6 1.2 %collective-permute-start.3 = (bf16[16,9,16,128]{3,2,1,0:T(8,128)(2,1)S(1)}, bf16[16,9,16,128]{3,2,1,0:T(8,128)(2,1)S(1)}, u32[]{:S(2)}, u32[]{:S(2)}) collective-permute-start(bf16[16,9,16,128]{3,2,1,0:T(8,128)(2,1)S(1)} %get-tuple-element.52._), channel_id=1, source_target_pairs={{0,2},{1,3},{2,0},{3,1},{4,6},{5,7},{6,4},{7,5},{8,10},{9,11},{10,... | collective-permute-start | bytes 1769480 | tf_op jit(solution)/shard_map/ppermute | solution.py:436
  20.8 3.7 %spatial.1 = (bf16[18,10,16,256]{3,2,1,0:T(8,128)(2,1)S(1)}, bf16[16,8,16,256]{3,2,1,0:T(8,128)(2,1)S(1)}, bf16[8,32,256]{2,1,0:T(8,128)(2,1)S(1)}) custom-call(s32[1]{0:T(128)S(6)} %copy.33.count_ref, bf16[128,256]{1,0:T(8,128)(2,1)S(1)} %collective-permute-done.top_ref.bot_ref, ...), custom_call_target="tpu_custom_call", output_to_operand_aliasing={{0}: (3, {})} | custom-call | flops 2415919104 | bytes 5439492 | tf_op jit(solution)/shard_map/spatial/pallas_call | solution.py:411
  24.5 1.9 %collective-permute-start.2 = (bf16[8,32,256]{2,1,0:T(8,128)(2,1)S(1)}, bf16[8,32,256]{2,1,0:T(8,128)(2,1)S(1)}, u32[]{:S(2)}, u32[]{:S(2)}) collective-permute-start(bf16[8,32,256]{2,1,0:T(8,128)(2,1)S(1)} %get-tuple-element.54.refs_2_), channel_id=1, source_target_pairs={{0,2},{2,4},{4,6},{6,8},{8,10},{10,12},{12,14},{14,16},{16,18},{18... | collective-permute-start | bytes 393224 | tf_op jit(solution)/shard_map/ppermute | solution.py:486
  26.5 0.2 halve_0.2
  26.6 1.6 %collective-permute-start.5 = (bf16[8,9,16,128]{3,2,1,0:T(8,128)(2,1)S(1)}, bf16[8,9,16,128]{3,2,1,0:T(8,128)(2,1)S(1)}, u32[]{:S(2)}, u32[]{:S(2)}) collective-permute-start(bf16[8,9,16,128]{3,2,1,0:T(8,128)(2,1)S(1)} %get-tuple-element.58.rest_0_), channel_id=1, source_target_pairs={{0,4},{1,5},{2,10},{3,11},{4,0},{5,1},{6,14},{7,15},{8,12},{9,13},... | collective-permute-start | bytes 884744 | tf_op jit(solution)/shard_map/ppermute | solution.py:436
  28.2 5.0 %forward.1 = (bf16[16,32,256]{2,1,0:T(8,128)(2,1)S(1)}, bf16[16,7,16,128]{3,2,1,0:T(8,128)(2,1)S(1)}, bf16[16,7,16,128]{3,2,1,0:T(8,128)(2,1)S(1)}) custom-call(s32[1]{0:T(128)S(6)} %copy.33.count_ref, bf16[16,8,16,256]{3,2,1,0:T(8,128)(2,1)S(1)} %get-tuple-element.47.xt_ref, bf16[16,8,16,256]{3,2,1,0:T(8,128)(2,1)S(1)} %get-tuple-element.53.sp_ref, ...), custom_call_target="tpu_custom_call" | custom-call | flops 2684354560 | bytes 5636100 | tf_op jit(solution)/shard_map/forward/pallas_call | solution.py:411
  33.2 0.2 collective-permute-done.5.__1_.refs_1_
  33.4 2.2 %collective-permute-start.6 = (bf16[16,7,16,128]{3,2,1,0:T(8,128)(2,1)S(1)}, bf16[16,7,16,128]{3,2,1,0:T(8,128)(2,1)S(1)}, u32[]{:S(2)}, u32[]{:S(2)}) collective-permute-start(bf16[16,7,16,128]{3,2,1,0:T(8,128)(2,1)S(1)} %pass.2), channel_id=1, source_target_pairs={{0,2},{1,3},{2,0},{3,1},{4,6},{5,7},{6,4},{7,5},{8,10},{9,11},{10,... | collective-permute-start | bytes 1376264 | tf_op jit(solution)/shard_map/ppermute | solution.py:436
  35.6 1.4 %collective-permute-done.6.refs_1_ = bf16[16,7,16,128]{3,2,1,0:T(8,128)(2,1)S(1)} collective-permute-done((bf16[16,7,16,128]{3,2,1,0:T(8,128)(2,1)S(1)}, bf16[16,7,16,128]{3,2,1,0:T(8,128)(2,1)S(1)}, u32[]{:S(2)}, u32[]{:S(2)}) %collective-permute-start.6) | collective-permute-done | bytes 458784 | tf_op jit(solution)/shard_map/ppermute | solution.py:436
  37.1 0.1 halve_0.3
  37.2 2.8 %collective-permute-start.7 = (bf16[8,7,16,128]{3,2,1,0:T(8,128)(2,1)S(1)}, bf16[8,7,16,128]{3,2,1,0:T(8,128)(2,1)S(1)}, u32[]{:S(2)}, u32[]{:S(2)}) collective-permute-start(bf16[8,7,16,128]{3,2,1,0:T(8,128)(2,1)S(1)} %get-tuple-element.66), channel_id=1, source_target_pairs={{0,4},{1,5},{2,10},{3,11},{4,0},{5,1},{6,14},{7,15},{8,12},{9,13},... | collective-permute-start | bytes 688136 | tf_op jit(solution)/shard_map/ppermute | solution.py:436
  40.0 4.0 %collective-permute-done.7.refs_3_ = bf16[8,7,16,128]{3,2,1,0:T(8,128)(2,1)S(1)} collective-permute-done((bf16[8,7,16,128]{3,2,1,0:T(8,128)(2,1)S(1)}, bf16[8,7,16,128]{3,2,1,0:T(8,128)(2,1)S(1)}, u32[]{:S(2)}, u32[]{:S(2)}) %collective-permute-start.7) | collective-permute-done | bytes 229408 | tf_op jit(solution)/shard_map/ppermute | solution.py:436
  44.0 0.1 halve_1.1
  44.1 0.6 collective-permute-start.8
  44.7 5.9 %collective-permute-done.8.refs_1_ = bf16[4,16,16,128]{3,2,1,0:T(8,128)(2,1)S(1)} collective-permute-done((bf16[4,16,16,128]{3,2,1,0:T(8,128)(2,1)S(1)}, bf16[4,16,16,128]{3,2,1,0:T(8,128)(2,1)S(1)}, u32[]{:S(2)}, u32[]{:S(2)}) %collective-permute-start.8) | collective-permute-done | bytes 262176 | tf_op jit(solution)/shard_map/ppermute | solution.py:436
  50.5 0.1 halve_2.1
  50.6 2.6 %collective-permute-start.9 = (bf16[2,16,16,128]{3,2,1,0:T(8,128)(2,1)S(1)}, bf16[2,16,16,128]{3,2,1,0:T(8,128)(2,1)S(1)}, u32[]{:S(2)}, u32[]{:S(2)}) collective-permute-start(bf16[2,16,16,128]{3,2,1,0:T(8,128)(2,1)S(1)} %get-tuple-element.70), channel_id=1, source_target_pairs={{0,8},{1,9},{2,3},{3,2},{4,12},{5,13},{6,7},{7,6},{8,0},{9,1},{10,... | collective-permute-start | bytes 393224 | tf_op jit(solution)/shard_map/ppermute | solution.py:436
  53.3 2.9 %collective-permute-done.9.refs_1_ = bf16[2,16,16,128]{3,2,1,0:T(8,128)(2,1)S(1)} collective-permute-done((bf16[2,16,16,128]{3,2,1,0:T(8,128)(2,1)S(1)}, bf16[2,16,16,128]{3,2,1,0:T(8,128)(2,1)S(1)}, u32[]{:S(2)}, u32[]{:S(2)}) %collective-permute-start.9) | collective-permute-done | bytes 131104 | tf_op jit(solution)/shard_map/ppermute | solution.py:436
  56.2 3.2 %collective-permute-start.10 = (bf16[1,16,16,128]{3,2,1,0:T(8,128)(2,1)S(1)}, bf16[1,16,16,128]{3,2,1,0:T(8,128)(2,1)S(1)}, u32[]{:S(2)}, u32[]{:S(2)}) collective-permute-start(bf16[1,16,16,128]{3,2,1,0:T(8,128)(2,1)S(1)} %get-tuple-element.72), channel_id=1, source_target_pairs={{0,16},{1,17},{2,18},{3,19},{4,20},{5,21},{6,22},{7,23},{8,24},{9,... | collective-permute-start | bytes 196616 | tf_op jit(solution)/shard_map/ppermute | solution.py:436
  59.4 2.3 %collective-permute-done.10.b_ref = bf16[1,16,16,128]{3,2,1,0:T(8,128)(2,1)S(1)} collective-permute-done((bf16[1,16,16,128]{3,2,1,0:T(8,128)(2,1)S(1)}, bf16[1,16,16,128]{3,2,1,0:T(8,128)(2,1)S(1)}, u32[]{:S(2)}, u32[]{:S(2)}) %collective-permute-start.10) | collective-permute-done | bytes 65568 | tf_op jit(solution)/shard_map/ppermute | solution.py:436
  61.8 3.4 %collective-permute-start.11 = (bf16[1,16,16,128]{3,2,1,0:T(8,128)(2,1)S(1)}, bf16[1,16,16,128]{3,2,1,0:T(8,128)(2,1)S(1)}, u32[]{:S(2)}, u32[]{:S(2)}) collective-permute-start(bf16[1,16,16,128]{3,2,1,0:T(8,128)(2,1)S(1)} %add.1.own_ref), channel_id=1, source_target_pairs={{0,16},{1,17},{2,18},{3,19},{4,20},{5,21},{6,22},{7,23},{8,24},{9,... | collective-permute-start | bytes 196616 | tf_op jit(solution)/shard_map/ppermute | solution.py:436
  65.2 2.2 %collective-permute-done.11.got_ref = bf16[1,16,16,128]{3,2,1,0:T(8,128)(2,1)S(1)} collective-permute-done((bf16[1,16,16,128]{3,2,1,0:T(8,128)(2,1)S(1)}, bf16[1,16,16,128]{3,2,1,0:T(8,128)(2,1)S(1)}, u32[]{:S(2)}, u32[]{:S(2)}) %collective-permute-start.11) | collective-permute-done | bytes 65568 | tf_op jit(solution)/shard_map/ppermute | solution.py:436
  67.5 3.0 %collective-permute-start.12 = (bf16[2,16,16,128]{3,2,1,0:T(8,128)(2,1)S(1)}, bf16[2,16,16,128]{3,2,1,0:T(8,128)(2,1)S(1)}, u32[]{:S(2)}, u32[]{:S(2)}) collective-permute-start(bf16[2,16,16,128]{3,2,1,0:T(8,128)(2,1)S(1)} %double_3.1.own_ref), channel_id=1, source_target_pairs={{0,8},{1,9},{2,3},{3,2},{4,12},{5,13},{6,7},{7,6},{8,0},{9,1},{10,... | collective-permute-start | bytes 393224 | tf_op jit(solution)/shard_map/ppermute | solution.py:436
  70.5 2.9 %collective-permute-done.12.got_ref = bf16[2,16,16,128]{3,2,1,0:T(8,128)(2,1)S(1)} collective-permute-done((bf16[2,16,16,128]{3,2,1,0:T(8,128)(2,1)S(1)}, bf16[2,16,16,128]{3,2,1,0:T(8,128)(2,1)S(1)}, u32[]{:S(2)}, u32[]{:S(2)}) %collective-permute-start.12) | collective-permute-done | bytes 131104 | tf_op jit(solution)/shard_map/ppermute | solution.py:436
  73.5 0.5 collective-permute-start.13
  74.0 1.6 %collective-permute-start.4 = (bf16[64,256]{1,0:T(8,128)(2,1)S(1)}, bf16[64,256]{1,0:T(8,128)(2,1)S(1)}, u32[]{:S(2)}, u32[]{:S(2)}) collective-permute-start(bf16[64,256]{1,0:T(8,128)(2,1)S(1)} %get-tuple-element.61), channel_id=1, source_target_pairs={{0,1},{1,0},{2,3},{3,2},{4,5},{5,4},{6,7},{7,6},{8,9},{9,8},{10,11... | collective-permute-start | bytes 98312 | tf_op jit(solution)/shard_map/ppermute | solution.py:491
  75.6 4.7 %collective-permute-done.4.halo_ref = bf16[64,256]{1,0:T(8,128)(2,1)S(1)} collective-permute-done((bf16[64,256]{1,0:T(8,128)(2,1)S(1)}, bf16[64,256]{1,0:T(8,128)(2,1)S(1)}, u32[]{:S(2)}, u32[]{:S(2)}) %collective-permute-start.4) | collective-permute-done | bytes 32800 | tf_op jit(solution)/shard_map/ppermute | solution.py:491
  80.3 3.8 %grad_x.2 = (bf16[16,128,256]{2,1,0:T(8,128)(2,1)}, f32[8,128]{1,0:T(8,128)S(1)}) custom-call(s32[1]{0:T(128)S(6)} %copy.33.count_ref, bf16[16,8,16,256]{3,2,1,0:T(8,128)(2,1)S(1)} %get-tuple-element.47.xt_ref, bf16[16,8,16,256]{3,2,1,0:T(8,128)(2,1)S(1)} %get-tuple-element.56.gy_ref, bf16[16,10,16,256]{3,2,1,0:T(8,128)(2,1)S(1)} %get-tuple-element.60.gs_ref, ...), custom_call_target="tpu_custom_call" | custom-call | flops 1342177280 | bytes 6590468 | tf_op jit(solution)/shard_map/grad_x/pallas_call | solution.py:411
  84.1 0.1 double_1.1.rest_1_.refs_0_
  84.1 0.1 collective-permute-start.15
  84.2 1.0 %collective-permute-start.14 = (bf16[8,16,16,128]{3,2,1,0:T(8,128)(2,1)S(1)}, bf16[8,16,16,128]{3,2,1,0:T(8,128)(2,1)S(1)}, u32[]{:S(2)}, u32[]{:S(2)}) collective-permute-start(bf16[8,16,16,128]{3,2,1,0:T(8,128)(2,1)S(1)} %double_1.1.rest_1_.refs_0_), channel_id=1, source_target_pairs={{0,4},{1,5},{2,10},{3,11},{4,0},{5,1},{6,14},{7,15},{8,12},{9,13},... | collective-permute-start | bytes 1572872 | tf_op jit(solution)/shard_map/ppermute | solution.py:436
  85.2 3.8 %grad_x.3 = (bf16[16,128,256]{2,1,0:T(8,128)(2,1)}, f32[8,128]{1,0:T(8,128)S(1)}) custom-call(s32[1]{0:T(128)S(6)} %copy.33.count_ref, bf16[16,8,16,256]{3,2,1,0:T(8,128)(2,1)S(1)} %get-tuple-element.47.xt_ref, bf16[16,8,16,256]{3,2,1,0:T(8,128)(2,1)S(1)} %get-tuple-element.56.gy_ref, ...), custom_call_target="tpu_custom_call", output_to_operand_aliasing={{0}: (8, {})} | custom-call | flops 1342177280 | bytes 7639044 | tf_op jit(solution)/shard_map/grad_x/pallas_call | solution.py:411
  89.0 1.6 %finish.3 = (f32[9,256,256]{2,1,0:T(8,128)}, f32[3,256,256]{2,1,0:T(8,128)}, f32[4,256,256]{2,1,0:T(8,128)}, f32[8,128]{1,0:T(8,128)S(1)}) custom-call(bf16[8,16,16,128]{3,2,1,0:T(8,128)(2,1)S(1)} %double_1.1.rest_1_.refs_0_, bf16[8,16,16,128]{3,2,1,0:T(8,128)(2,1)S(1)} %collective-permute-done.15.refs_1_), custom_call_target="tpu_custom_call" | custom-call | bytes 5246976 | tf_op jit(solution)/shard_map/finish/pallas_call | solution.py:411
  90.6 2.9 %collective-permute-done.14.__0_ = bf16[8,16,16,128]{3,2,1,0:T(8,128)(2,1)S(1)} collective-permute-done((bf16[8,16,16,128]{3,2,1,0:T(8,128)(2,1)S(1)}, bf16[8,16,16,128]{3,2,1,0:T(8,128)(2,1)S(1)}, u32[]{:S(2)}, u32[]{:S(2)}) %collective-permute-start.14) | collective-permute-done | bytes 524320 | tf_op jit(solution)/shard_map/ppermute | solution.py:436
  93.4 0.8 reshape.38
  94.2 1.7 %finish.4 = (f32[9,256,256]{2,1,0:T(8,128)}, f32[3,256,256]{2,1,0:T(8,128)}, f32[4,256,256]{2,1,0:T(8,128)}, f32[8,128]{1,0:T(8,128)}) custom-call(bf16[8,16,16,128]{3,2,1,0:T(8,128)(2,1)S(1)} %pass.3.refs_0_, f32[9,256,256]{2,1,0:T(8,128)} %get-tuple-element.78.refs_1_, ...), custom_call_target="tpu_custom_call", output_to_operand_aliasing={{0}: (1, {}), {1}: (2, {}), {2}: (3, {})} | custom-call | bytes 8916992 | tf_op jit(solution)/shard_map/finish/pallas_call | solution.py:411
  95.9 1.7 %finish.5 = (f32[9,256,256]{2,1,0:T(8,128)}, f32[3,256,256]{2,1,0:T(8,128)}, f32[4,256,256]{2,1,0:T(8,128)}, f32[8,128]{1,0:T(8,128)}) custom-call(bf16[8,16,16,128]{3,2,1,0:T(8,128)(2,1)S(1)} %collective-permute-done.16.refs_0_, f32[9,256,256]{2,1,0:T(8,128)} %get-tuple-element.81.refs_1_, ...), custom_call_target="tpu_custom_call", output_to_operand_aliasing={{0}: (1, {}), {1}: (2, {}), {2}: (3, {})} | custom-call | bytes 8916992 | tf_op jit(solution)/shard_map/finish/pallas_call | solution.py:411
  (21 shorter events, 0.1 us)
Async XLA Ops:
  0.6 9.7 %copy-start.4 = (bf16[16,16,8,256]{3,2,1,0:T(8,128)(2,1)S(1)}, bf16[16,16,8,256]{3,2,1,0:T(8,128)(2,1)}, u32[]{:S(2)}) copy-start(bf16[16,16,8,256]{3,2,1,0:T(8,128)(2,1)} %param.6) | copy-start | bytes 3145732
  3.1 11.4 %copy-start.1 = (bf16[2,2,256,256]{3,2,1,0:T(8,128)(2,1)S(1)}, bf16[2,2,256,256]{3,2,1,0:T(8,128)(2,1)}, u32[]{:S(2)}) copy-start(bf16[2,2,256,256]{3,2,1,0:T(8,128)(2,1)} %param.10) | copy-start | bytes 1572868
  3.1 11.4 %copy-start.2 = (bf16[3,256,256]{2,1,0:T(8,128)(2,1)S(1)}, bf16[3,256,256]{2,1,0:T(8,128)(2,1)}, u32[]{:S(2)}) copy-start(bf16[3,256,256]{2,1,0:T(8,128)(2,1)} %wt_ref.7) | copy-start | bytes 1179652
  3.1 11.5 %copy-start.3 = (bf16[16,32,256]{2,1,0:T(8,128)(2,1)S(1)}, bf16[16,32,256]{2,1,0:T(8,128)(2,1)}, u32[]{:S(2)}) copy-start(bf16[16,32,256]{2,1,0:T(8,128)(2,1)} %reshape.35.cot_ref) | copy-start | bytes 786436
  6.0 8.5 %collective-permute-start = (bf16[128,256]{1,0:T(8,128)(2,1)}, bf16[128,256]{1,0:T(8,128)(2,1)S(1)}, u32[]{:S(2)}, u32[]{:S(2)}) collective-permute-start(bf16[128,256]{1,0:T(8,128)(2,1)} %get-tuple-element.48), channel_id=1, source_target_pairs={{0,1},{1,0},{2,3},{3,2},{4,5},{5,4},{6,7},{7,6},{8,9},{9,8},{10,11... | collective-permute-start | bytes 196616 | tf_op jit(solution)/shard_map/ppermute | solution.py:491
  9.0 5.5 %collective-permute-start.1 = (bf16[2,32,256]{2,1,0:T(8,128)(2,1)}, bf16[2,32,256]{2,1,0:T(8,128)(2,1)S(1)}, u32[]{:S(2)}, u32[]{:S(2)}) collective-permute-start(bf16[2,32,256]{2,1,0:T(8,128)(2,1)} %get-tuple-element.51), channel_id=1, source_target_pairs={{2,0},{4,2},{6,4},{8,6},{10,8},{12,10},{14,12},{16,14},{18,16},{20... | collective-permute-start | bytes 98312 | tf_op jit(solution)/shard_map/ppermute | solution.py:486
  10.3 0.7 copy-start.5
  14.6 6.2 %copy-start = (bf16[3,3,256,256]{3,2,1,0:T(8,128)(2,1)S(1)}, bf16[3,3,256,256]{3,2,1,0:T(8,128)(2,1)}, u32[]{:S(2)}) copy-start(bf16[3,3,256,256]{3,2,1,0:T(8,128)(2,1)} %param.8) | copy-start | bytes 3538948
  19.6 6.9 %collective-permute-start.3 = (bf16[16,9,16,128]{3,2,1,0:T(8,128)(2,1)S(1)}, bf16[16,9,16,128]{3,2,1,0:T(8,128)(2,1)S(1)}, u32[]{:S(2)}, u32[]{:S(2)}) collective-permute-start(bf16[16,9,16,128]{3,2,1,0:T(8,128)(2,1)S(1)} %get-tuple-element.52._), channel_id=1, source_target_pairs={{0,2},{1,3},{2,0},{3,1},{4,6},{5,7},{6,4},{7,5},{8,10},{9,11},{10,... | collective-permute-start | bytes 1769480 | tf_op jit(solution)/shard_map/ppermute | solution.py:436
  24.5 3.7 %collective-permute-start.2 = (bf16[8,32,256]{2,1,0:T(8,128)(2,1)S(1)}, bf16[8,32,256]{2,1,0:T(8,128)(2,1)S(1)}, u32[]{:S(2)}, u32[]{:S(2)}) collective-permute-start(bf16[8,32,256]{2,1,0:T(8,128)(2,1)S(1)} %get-tuple-element.54.refs_2_), channel_id=1, source_target_pairs={{0,2},{2,4},{4,6},{6,8},{8,10},{10,12},{12,14},{14,16},{16,18},{18... | collective-permute-start | bytes 393224 | tf_op jit(solution)/shard_map/ppermute | solution.py:486
  26.6 6.8 %collective-permute-start.5 = (bf16[8,9,16,128]{3,2,1,0:T(8,128)(2,1)S(1)}, bf16[8,9,16,128]{3,2,1,0:T(8,128)(2,1)S(1)}, u32[]{:S(2)}, u32[]{:S(2)}) collective-permute-start(bf16[8,9,16,128]{3,2,1,0:T(8,128)(2,1)S(1)} %get-tuple-element.58.rest_0_), channel_id=1, source_target_pairs={{0,4},{1,5},{2,10},{3,11},{4,0},{5,1},{6,14},{7,15},{8,12},{9,13},... | collective-permute-start | bytes 884744 | tf_op jit(solution)/shard_map/ppermute | solution.py:436
  33.4 3.7 %collective-permute-start.6 = (bf16[16,7,16,128]{3,2,1,0:T(8,128)(2,1)S(1)}, bf16[16,7,16,128]{3,2,1,0:T(8,128)(2,1)S(1)}, u32[]{:S(2)}, u32[]{:S(2)}) collective-permute-start(bf16[16,7,16,128]{3,2,1,0:T(8,128)(2,1)S(1)} %pass.2), channel_id=1, source_target_pairs={{0,2},{1,3},{2,0},{3,1},{4,6},{5,7},{6,4},{7,5},{8,10},{9,11},{10,... | collective-permute-start | bytes 1376264 | tf_op jit(solution)/shard_map/ppermute | solution.py:436
  37.2 6.8 %collective-permute-start.7 = (bf16[8,7,16,128]{3,2,1,0:T(8,128)(2,1)S(1)}, bf16[8,7,16,128]{3,2,1,0:T(8,128)(2,1)S(1)}, u32[]{:S(2)}, u32[]{:S(2)}) collective-permute-start(bf16[8,7,16,128]{3,2,1,0:T(8,128)(2,1)S(1)} %get-tuple-element.66), channel_id=1, source_target_pairs={{0,4},{1,5},{2,10},{3,11},{4,0},{5,1},{6,14},{7,15},{8,12},{9,13},... | collective-permute-start | bytes 688136 | tf_op jit(solution)/shard_map/ppermute | solution.py:436
  44.1 6.4 %collective-permute-start.8 = (bf16[4,16,16,128]{3,2,1,0:T(8,128)(2,1)S(1)}, bf16[4,16,16,128]{3,2,1,0:T(8,128)(2,1)S(1)}, u32[]{:S(2)}, u32[]{:S(2)}) collective-permute-start(bf16[4,16,16,128]{3,2,1,0:T(8,128)(2,1)S(1)} %get-tuple-element.68), channel_id=1, source_target_pairs={{0,1},{1,0},{2,6},{3,7},{4,5},{5,4},{6,2},{7,3},{8,9},{9,8},{10,14... | collective-permute-start | bytes 786440 | tf_op jit(solution)/shard_map/ppermute | solution.py:436
  50.6 5.6 %collective-permute-start.9 = (bf16[2,16,16,128]{3,2,1,0:T(8,128)(2,1)S(1)}, bf16[2,16,16,128]{3,2,1,0:T(8,128)(2,1)S(1)}, u32[]{:S(2)}, u32[]{:S(2)}) collective-permute-start(bf16[2,16,16,128]{3,2,1,0:T(8,128)(2,1)S(1)} %get-tuple-element.70), channel_id=1, source_target_pairs={{0,8},{1,9},{2,3},{3,2},{4,12},{5,13},{6,7},{7,6},{8,0},{9,1},{10,... | collective-permute-start | bytes 393224 | tf_op jit(solution)/shard_map/ppermute | solution.py:436
  56.2 5.6 %collective-permute-start.10 = (bf16[1,16,16,128]{3,2,1,0:T(8,128)(2,1)S(1)}, bf16[1,16,16,128]{3,2,1,0:T(8,128)(2,1)S(1)}, u32[]{:S(2)}, u32[]{:S(2)}) collective-permute-start(bf16[1,16,16,128]{3,2,1,0:T(8,128)(2,1)S(1)} %get-tuple-element.72), channel_id=1, source_target_pairs={{0,16},{1,17},{2,18},{3,19},{4,20},{5,21},{6,22},{7,23},{8,24},{9,... | collective-permute-start | bytes 196616 | tf_op jit(solution)/shard_map/ppermute | solution.py:436
  61.8 5.7 %collective-permute-start.11 = (bf16[1,16,16,128]{3,2,1,0:T(8,128)(2,1)S(1)}, bf16[1,16,16,128]{3,2,1,0:T(8,128)(2,1)S(1)}, u32[]{:S(2)}, u32[]{:S(2)}) collective-permute-start(bf16[1,16,16,128]{3,2,1,0:T(8,128)(2,1)S(1)} %add.1.own_ref), channel_id=1, source_target_pairs={{0,16},{1,17},{2,18},{3,19},{4,20},{5,21},{6,22},{7,23},{8,24},{9,... | collective-permute-start | bytes 196616 | tf_op jit(solution)/shard_map/ppermute | solution.py:436
  67.5 6.0 %collective-permute-start.12 = (bf16[2,16,16,128]{3,2,1,0:T(8,128)(2,1)S(1)}, bf16[2,16,16,128]{3,2,1,0:T(8,128)(2,1)S(1)}, u32[]{:S(2)}, u32[]{:S(2)}) collective-permute-start(bf16[2,16,16,128]{3,2,1,0:T(8,128)(2,1)S(1)} %double_3.1.own_ref), channel_id=1, source_target_pairs={{0,8},{1,9},{2,3},{3,2},{4,12},{5,13},{6,7},{7,6},{8,0},{9,1},{10,... | collective-permute-start | bytes 393224 | tf_op jit(solution)/shard_map/ppermute | solution.py:436
  73.5 10.6 %collective-permute-start.13 = (bf16[4,16,16,128]{3,2,1,0:T(8,128)(2,1)S(1)}, bf16[4,16,16,128]{3,2,1,0:T(8,128)(2,1)S(1)}, u32[]{:S(2)}, u32[]{:S(2)}) collective-permute-start(bf16[4,16,16,128]{3,2,1,0:T(8,128)(2,1)S(1)} %double_2.1.rest_0_.own_ref), channel_id=1, source_target_pairs={{0,1},{1,0},{2,6},{3,7},{4,5},{5,4},{6,2},{7,3},{8,9},{9,8},{10,14... | collective-permute-start | bytes 786440 | tf_op jit(solution)/shard_map/ppermute | solution.py:436
  74.0 6.3 %collective-permute-start.4 = (bf16[64,256]{1,0:T(8,128)(2,1)S(1)}, bf16[64,256]{1,0:T(8,128)(2,1)S(1)}, u32[]{:S(2)}, u32[]{:S(2)}) collective-permute-start(bf16[64,256]{1,0:T(8,128)(2,1)S(1)} %get-tuple-element.61), channel_id=1, source_target_pairs={{0,1},{1,0},{2,3},{3,2},{4,5},{5,4},{6,7},{7,6},{8,9},{9,8},{10,11... | collective-permute-start | bytes 98312 | tf_op jit(solution)/shard_map/ppermute | solution.py:491
  84.1 4.9 %collective-permute-start.15 = (bf16[8,16,16,128]{3,2,1,0:T(8,128)(2,1)S(1)}, bf16[8,16,16,128]{3,2,1,0:T(8,128)(2,1)S(1)}, u32[]{:S(2)}, u32[]{:S(2)}) collective-permute-start(bf16[8,16,16,128]{3,2,1,0:T(8,128)(2,1)S(1)} %double_1.1.rest_1_.refs_0_), channel_id=1, source_target_pairs={{0,2},{1,3},{2,0},{3,1},{4,6},{5,7},{6,4},{7,5},{8,10},{9,11},{10,... | collective-permute-start | bytes 1572872 | tf_op jit(solution)/shard_map/ppermute | solution.py:436
  84.2 9.2 %collective-permute-start.14 = (bf16[8,16,16,128]{3,2,1,0:T(8,128)(2,1)S(1)}, bf16[8,16,16,128]{3,2,1,0:T(8,128)(2,1)S(1)}, u32[]{:S(2)}, u32[]{:S(2)}) collective-permute-start(bf16[8,16,16,128]{3,2,1,0:T(8,128)(2,1)S(1)} %double_1.1.rest_1_.refs_0_), channel_id=1, source_target_pairs={{0,4},{1,5},{2,10},{3,11},{4,0},{5,1},{6,14},{7,15},{8,12},{9,13},... | collective-permute-start | bytes 1572872 | tf_op jit(solution)/shard_map/ppermute | solution.py:436
  93.4 2.5 %collective-permute-start.16 = (bf16[8,16,16,128]{3,2,1,0:T(8,128)(2,1)S(1)}, bf16[8,16,16,128]{3,2,1,0:T(8,128)(2,1)S(1)}, u32[]{:S(2)}, u32[]{:S(2)}) collective-permute-start(bf16[8,16,16,128]{3,2,1,0:T(8,128)(2,1)S(1)} %pass.3.refs_0_), channel_id=1, source_target_pairs={{0,2},{1,3},{2,0},{3,1},{4,6},{5,7},{6,4},{7,5},{8,10},{9,11},{10,... | collective-permute-start | bytes 1572872 | tf_op jit(solution)/shard_map/ppermute | solution.py:436

commit v6 on v5

--- a/solution.py
+++ b/solution.py
@@ -70,63 +70,39 @@
     return jnp.where(slot_mask(total.shape, count), total, 0.0).astype(BF)
 
 
-def halving_bits():
+def place_bits():
     t, g = lax.axis_index("tm"), lax.axis_index("grp")
-    x, y, z0, z1 = (t >> 1) & 1, g & 1, (t >> 2) & 1, (t >> 3) & 1
-    return t & 1, ((x, y, z0, z1), (z0, x, y, z1))
-
-
-def round_bit(k):
-    core, (first, second) = halving_bits()
-    return jnp.where(core == 0, first[k], second[k])
+    return t & 1, ((t >> 1) & 1) + 2 * (g & 1) + 4 * ((t >> 2) & 1)
 
 
 def split_cores(value, keep_ref, send_ref, k):
-    core, _ = halving_bits()
+    core, _ = place_bits()
     low, high = value[:, : CH // 2].astype(BF), value[:, CH // 2 :].astype(BF)
-    keep_ref[:, k] = jnp.where(core == 0, low, high).reshape(16, 16, CH // 2)
-    send_ref[:, k] = jnp.where(core == 0, high, low).reshape(16, 16, CH // 2)
+    keep_ref[:, k] = jnp.where(core == 0, low, high).reshape(8, 32, CH // 2)
+    send_ref[:, k] = jnp.where(core == 0, high, low).reshape(8, 32, CH // 2)
 
 
 def edges_kernel(bands, count_ref, x_ref, cot_ref, *rest):
-    outs, (nxt_ref, token_ref, buf, sems) = rest[:-4], rest[-4:]
+    outs, (nxt_ref, token_ref) = rest[:-2], rest[-2:]
     token_ref[...] = jnp.zeros_like(token_ref)
     count = count_ref[0]
     band = lax.axis_index("grp")
     wide = x_ref.shape[1]
     if bands == 2:
-        starts = [jnp.where(band == 0, wide - 16, 0)]
-        lower = [band == 0]
+        starts, lower = [jnp.where(band == 0, wide - 16, 0)], [band == 0]
     else:
         starts, lower = [wide - 16, 0], [True, False]
-    copies = [
-        pltpu.make_async_copy(
-            x_ref.at[:, pl.ds(pl.multiple_of(at, 16), 16), :], buf.at[k], sems.at[k]
-        )
-        for k, at in enumerate(starts)
-    ]
-    for copy in copies:
-        copy.start()
     nxt_ref[...] = cot_ref[0:2]
     place = to_slots(16, SLOTS, own_frames(count))
-    for k, copy in enumerate(copies):
-        copy.wait()
-        v = mm(place, buf[k].reshape(SLOTS * 16, CH))
+    for k, at in enumerate(starts):
+        piece = x_ref[:, pl.ds(pl.multiple_of(at, 16), 16), :].reshape(SLOTS * 16, CH)
+        v = mm(place, piece)
         v = jnp.where(lower[k], v[128:], v[:128])
         outs[k][...] = silu_norm(v).astype(BF)
 
 
-def acts_kernel(count_ref, x_hbm, _, xt_ref, acts_ref, at_ref, x_ref, sems):
+def acts_kernel(count_ref, x_ref, _, xt_ref, acts_ref, at_ref):
     count = count_ref[0]
-    pieces = sems.shape[0]
-    size = x_hbm.shape[1] // pieces
-
-    def copy_of(k):
-        at = pl.ds(pl.multiple_of(k * size, size), size)
-        return pltpu.make_async_copy(x_hbm.at[:, at, :], x_ref.at[:, at, :], sems.at[k])
-
-    for k in range(pieces):
-        copy_of(k).start()
     rows, cols = xt_ref.shape[0], xt_ref.shape[1]
     edge = jnp.zeros((rows + 2, SLOTS, CH), BF)
     acts_ref[:, 0] = edge
@@ -135,11 +111,6 @@
 
     def rows_of(q, _):
         at = pl.multiple_of(q * 16, 16)
-
-        @pl.when(q % 2 == 0)
-        def _():
-            copy_of(q // 2).wait()
-
         piece = x_ref[:, pl.ds(at, 16), :].reshape(SLOTS * 16, CH)
         v = mm(place, piece)
         xt_ref[pl.ds(2 * q, 2)] = v.astype(BF).reshape(2, cols, SLOTS, CH)
@@ -152,7 +123,7 @@
 
 
 def spatial_kernel(
-    bands, count_ref, top_ref, bot_ref, acts_in, ws_ref, _, acts_ref, sp_ref, edge_ref
+    bands, count_ref, top_ref, bot_ref, acts_in, ws_ref, acts_ref, sp_ref, edge_ref
 ):
     count = count_ref[0]
     band = lax.axis_index("grp")
@@ -181,7 +152,7 @@
 
 
 def grad_spatial_kernel(
-    bands, count_ref, at_in, top_ref, bot_ref, cot_ref, nxt_ref, wt_ref, wd_ref,
+    bands, count_ref, at_in, top_ref, bot_ref, cot_ref, nxt_ref, wt_ref, wd_ref, _,
     at_ref, cott_ref, gy_ref, gs_ref, keep_ref, send_ref, *edge_refs,
 ):
     count = count_ref[0]
@@ -196,8 +167,9 @@
 
     place_next = to_slots(16, SLOTS, own_and_next(count))
     for q in range(rows * cols // 64):
+        four = slice(q * 4, q * 4 + 4)
         piece = jnp.concatenate(
-            [cot_ref[0:OWN, q * 16 : q * 16 + 16, :], nxt_ref[:, q * 16 : q * 16 + 16, :]], 0
+            [cot_ref[0:OWN, four].reshape(OWN, 16, CH), nxt_ref[:, four].reshape(2, 16, CH)], 0
         ).reshape(SLOTS * 16, CH)
         placed = mm(place_next, piece).astype(BF)
         cott_ref[q * 4 : q * 4 + 4] = placed.reshape(4, 4, SLOTS, CH)
@@ -281,7 +253,7 @@
     back = to_frames(16)
     for q in range(small // 256):
         o = mm(back, down[q * 256 : q * 256 + 256]).astype(BF)
-        down_ref[:, q * 16 : q * 16 + 16, :] = o.reshape(SLOTS, 16, CH)
+        down_ref[:, q * 4 : q * 4 + 4] = o.reshape(SLOTS, 4, cols // 2, CH)
 
 
 def grad_x_kernel(
@@ -342,57 +314,51 @@
     copy.wait()
 
 
-def halve_kernel(k, chains, *refs):
-    send_ref, keep_ref = refs[-2:]
-    bit = round_bit(k)
-    m = send_ref.shape[0]
-    at = 0
-    for c in range(chains):
-        a, b = refs[2 * c : 2 * c + 2]
-        n = a.shape[1]
-        for ref, side in ((send_ref, 1 - bit), (keep_ref, bit)):
-            part = pl.ds(side * m, m)
-            ref[:, at : at + n] = (a[part].astype(F32) + b[part].astype(F32)).astype(BF)
-        at += n
+def scatter_kernel(keep_a, got_a, keep_b, got_b, *outs):
+    _, p = place_bits()
+    n = keep_a.shape[1]
+    for r, out in enumerate(outs):
+        c = p ^ r
+        out[:n] = (keep_a[c].astype(F32) + got_a[c].astype(F32)).astype(BF)
+        out[n:] = (keep_b[c].astype(F32) + got_b[c].astype(F32)).astype(BF)
+
+
+def sum_kernel(*refs):
+    total = refs[0][...].astype(F32)
+    for ref in refs[1:8]:
+        total = total + ref[...].astype(F32)
+    refs[-1][...] = total.astype(BF)
+
+
+def gather_kernel(*refs):
+    _, p = place_bits()
+    for r in range(8):
+        refs[-1][p ^ r] = refs[r][...]
 
 
 def add_kernel(a_ref, b_ref, out_ref):
     out_ref[...] = (a_ref[...].astype(F32) + b_ref[...].astype(F32)).astype(BF)
 
 
-def double_kernel(k, own_ref, got_ref, *rest):
-    out_ref = rest[-1]
-    bit = round_bit(k)
-    m = own_ref.shape[0]
-    out_ref[pl.ds(bit * m, m)] = own_ref[...]
-    out_ref[pl.ds((1 - bit) * m, m)] = got_ref[...]
-
-
 def pass_kernel(*_):
     pass
 
 
-def finish_kernel(which, *refs):
-    buf, sems = refs[-2:]
-    outs, token_ref = refs[-6:-3], refs[-3]
-    token_ref[...] = jnp.zeros_like(token_ref)
-    core, (first, second) = halving_bits()
-    mine = jnp.where(core == 0, first[0], second[0])
-    other = jnp.where(core == 0, second[0], first[0])
+def finish_kernel(own, half_ref, *rest):
+    buf, sems = rest[-2:]
+    outs = rest[-5:-2]
+    core, _ = place_bits()
+    at = pl.multiple_of((core if own else 1 - core) * (CH // 2), CH // 2)
     copies = []
     k = 0
-    for ref, (sibling, far) in zip(refs, which):
-        rows = other if sibling else mine
-        rows = pl.ds(pl.multiple_of((1 - rows if far else rows) * (CH // 2), CH // 2), CH // 2)
-        cols = pl.ds(pl.multiple_of((1 - core if sibling else core) * (CH // 2), CH // 2), CH // 2)
-        m = 0
-        for out in outs:
-            for o in range(out.shape[0]):
-                buf[k] = ref[:, m].reshape(CH // 2, CH // 2).astype(F32)
-                copies.append(pltpu.make_async_copy(buf.at[k], out.at[o, rows, cols], sems.at[k]))
-                copies[-1].start()
-                k += 1
-                m += 1
+    for out in outs:
+        for m in range(out.shape[0]):
+            buf[k] = half_ref[:, k].reshape(CH, CH // 2).astype(F32)
+            copies.append(
+                pltpu.make_async_copy(buf.at[k], out.at[m, :, pl.ds(at, CH // 2)], sems.at[k])
+            )
+            copies[-1].start()
+            k += 1
     for copy in copies:
         copy.wait()
 
@@ -426,38 +392,24 @@
 
 def plan(tm, grp):
     low, total = grp.bit_length() - 1, (tm * grp).bit_length() - 1
-    used = [low, low + 1, 0, low + 2, low + 3]
-    return used, [b for b in range(total) if b not in used]
-
-
-def swap(value, tm, grp, first, second):
-    core = plan(tm, grp)[0][0]
-    pairs = [(d, d ^ (1 << (second if (d >> core) & 1 else first))) for d in range(tm * grp)]
-    return lax.ppermute(value, AXES, pairs)
+    eight = [low + 1, 0, low + 2]
+    return low, eight, [b for b in range(total) if b != low and b not in eight]
+
+
+def swap(value, tm, grp, *bits):
+    flip = sum(1 << b for b in bits)
+    return lax.ppermute(value, AXES, [(d, d ^ flip) for d in range(tm * grp)])
 
 
 def core_round(value, tm, grp):
-    core = plan(tm, grp)[0][0]
-    return swap(value, tm, grp, core, core)
-
-
-def link_round(k, value, tm, grp):
-    _, x, y, z0, z1 = plan(tm, grp)[0]
-    return swap(value, tm, grp, (x, y, z0, z1)[k], (z0, x, y, z1)[k])
-
-
-def halve(k, chains, after=()):
-    n = sum(a.shape[1] for a, _ in chains)
-    shape = (chains[0][0].shape[0] // 2, n, 16, CH // 2)
-    ins = [(VMEM, a) for pair in chains for a in pair] + [(ANY, a) for a in after]
-    kernel = functools.partial(halve_kernel, k, len(chains))
-    return call(kernel, f"halve_{k}", ins, [(VMEM, shape)] * 2)
-
-
-def double(k, own, got, after=()):
-    shape = (own.shape[0] * 2,) + own.shape[1:]
-    ins = [(VMEM, own), (VMEM, got)] + [(ANY, a) for a in after]
-    return call(functools.partial(double_kernel, k), f"double_{k}", ins, [(VMEM, shape)])[0]
+    return swap(value, tm, grp, plan(tm, grp)[0])
+
+
+def eight_round(parts, tm, grp):
+    bits = plan(tm, grp)[1]
+    return parts[:1] + [
+        swap(parts[r], tm, grp, *(b for i, b in enumerate(bits) if r >> i & 1)) for r in range(1, 8)
+    ]
 
 
 def passed(value, after):
@@ -465,19 +417,18 @@
     return call(pass_kernel, "pass", ins, [(ANY, value.shape)], alias={0: 0})[0]
 
 
-def finish(quarters, before):
-    n = quarters[0][0].shape[1] * len(quarters)
-    *outs, token = (
+def finish(own, half, before):
+    n = half.shape[1]
+    return list(
         call(
-            functools.partial(finish_kernel, [q[1:] for q in quarters]),
+            functools.partial(finish_kernel, own),
             "finish",
-            [(VMEM, q[0]) for q in quarters] + [(HBM, a) for a in before],
-            [(HBM, (m, CH, CH), F32) for m in (9, 3, 4)] + [TOKEN],
-            [pltpu.VMEM((n, CH // 2, CH // 2), F32), pltpu.SemaphoreType.DMA((n,))],
-            alias={len(quarters) + i: i for i in range(len(before))},
+            [(VMEM, half)] + [(HBM, a) for a in before],
+            [(HBM, (m, CH, CH), F32) for m in (9, 3, 4)],
+            [pltpu.VMEM((n, CH, CH // 2), F32), pltpu.SemaphoreType.DMA((n,))],
+            alias={1 + i: i for i in range(len(before))},
         )
     )
-    return outs, token
 
 
 def along(value, axis, by):
@@ -497,7 +448,6 @@
     slots, rows, cols, ch = frames_in.shape
     wide = rows * cols
     x = frames_in.reshape(slots, wide, ch)
-    cot = cotangent.reshape(slots, wide // 4, ch)
     ws = w_spatial.reshape(9, ch, ch)
     wd = w_down.reshape(4, ch, ch)
     wt = w_temporal
@@ -511,69 +461,52 @@
     *edge, nxt, token = call(
         functools.partial(edges_kernel, grp),
         "edges",
-        [count, (HBM, x), (VMEM, cot)],
-        [(VMEM, (cols * slots, ch))] * sides + [(VMEM, (2, wide // 4, ch)), TOKEN],
-        [pltpu.VMEM((sides, slots, 16, ch), BF), dma((sides,))],
+        [count, (VMEM, x), (VMEM, cotangent)],
+        [(VMEM, (cols * slots, ch))] * sides + [(VMEM, (2,) + cotangent.shape[1:]), TOKEN],
         flops=tap // 8,
-        grant=56,
     )
     top, bot = from_bands(edge)
     nxt_got = along(nxt, "tm", -1)
     xt, acts, at = call(
         acts_kernel,
         "acts",
-        [count, (HBM, x), (ANY, token)],
+        [count, (VMEM, x), (ANY, token)],
         [(VMEM, tile), (VMEM, padded), (VMEM, (ch, (rows + 2) * 128))],
-        [pltpu.VMEM((slots, wide, ch), BF), dma((4,))],
         flops=2 * tap,
     )
-    half = (16, 9, 16, ch // 2)
+    acts, sp, last_two = call(
+        functools.partial(spatial_kernel, grp),
+        "spatial",
+        [count, (VMEM, top), (VMEM, bot), (VMEM, acts), (VMEM, ws)],
+        [(VMEM, padded), (VMEM, tile), (VMEM, (rows // 2, 32, ch))],
+        flops=9 * tap,
+        alias={3: 0},
+    )
+    prev = along(last_two, "tm", 1)
+    half = (8, 9, 32, ch // 2)
     at, cott, gy, gs, keep_a, send_a, *edge = call(
         functools.partial(grad_spatial_kernel, grp),
         "grad_spatial",
-        [count, (VMEM, at), (VMEM, top), (VMEM, bot), (VMEM, cot), (VMEM, nxt_got), (VMEM, wt), (VMEM, wd)],
+        [count, (VMEM, at), (VMEM, top), (VMEM, bot), (VMEM, cotangent), (VMEM, nxt_got), (VMEM, wt), (VMEM, wd),
+         (ANY, last_two)],
         [(VMEM, at.shape), (VMEM, (rows // 2, cols // 2, slots, ch)), (VMEM, tile),
          (VMEM, (rows, cols + 2, slots, ch)), (VMEM, half), (VMEM, half)]
         + [(VMEM, (cols // 2 * slots, ch))] * sides,
         flops=14 * tap,
         alias={1: 0},
     )
-    got_a = core_round(send_a, tm, grp)
-    acts, sp, last_two = call(
-        functools.partial(spatial_kernel, grp),
-        "spatial",
-        [count, (VMEM, top), (VMEM, bot), (VMEM, acts), (VMEM, ws), (ANY, send_a)],
-        [(VMEM, padded), (VMEM, tile), (VMEM, (rows // 2, 32, ch))],
-        flops=9 * tap,
-        alias={3: 0},
-    )
-    prev = along(last_two, "tm", 1)
-    send_a, keep_a = halve(0, [(keep_a, got_a)], [last_two])
+    got_a = core_round(passed(send_a, [prev]), tm, grp)
     cot_top, cot_bot = from_bands(edge)
-    half = (16, 7, 16, ch // 2)
+    half = (8, 7, 32, ch // 2)
     down, keep_b, send_b = call(
         forward_kernel,
         "forward",
         [count, (VMEM, xt), (VMEM, sp), (VMEM, prev), (VMEM, cott), (VMEM, gy), (VMEM, wt), (VMEM, wd)]
         + [(ANY, send_a)],
-        [(VMEM, (slots, wide // 4, ch)), (VMEM, half), (VMEM, half)],
+        [(VMEM, cotangent.shape), (VMEM, half), (VMEM, half)],
         [pltpu.VMEM(s, BF) for s in (tile, (ch, slots * wide), tile, tile, tile)],
         flops=10 * tap,
     )
-    got_a = link_round(0, send_a, tm, grp)
-    send_b = passed(send_b, [got_a])
-    send_b, keep_b = halve(0, [(keep_b, core_round(send_b, tm, grp))])
-    got_b = link_round(0, send_b, tm, grp)
-    send, keep = halve(1, [(keep_a, got_a), (keep_b, got_b)])
-    for k in (2, 3):
-        send, keep = halve(k, [(keep, link_round(k - 1, send, tm, grp))])
-    got = link_round(3, send, tm, grp)
-    (mine,) = call(add_kernel, "add", [(VMEM, keep), (VMEM, got)], [(VMEM, keep.shape)])
-    for bit in plan(tm, grp)[1]:
-        mine = (mine.astype(F32) + swap(mine, tm, grp, bit, bit).astype(F32)).astype(BF)
-    for k in (3, 2):
-        mine = double(k, mine, link_round(k, mine, tm, grp))
-
     def grad_x_part(part, halo, before, after):
         return call(
             functools.partial(grad_x_kernel, part, grp),
@@ -587,20 +520,30 @@
             alias={8: 0} if before else None,
         )
 
-    got = link_round(1, mine, tm, grp)
-    grad_x, token = grad_x_part(0, cot_top, [], [mine])
-    mine = double(1, mine, got, [token])
-    far = link_round(0, mine, tm, grp)
-    side = core_round(mine, tm, grp)
+    send_b = passed(send_b, [got_a])
+    got_b = core_round(send_b, tm, grp)
+    parts = call(
+        scatter_kernel,
+        "scatter",
+        [(VMEM, a) for a in (keep_a, got_a, keep_b, got_b)],
+        [(VMEM, (16, 32, ch // 2))] * 8,
+    )
+    grad_x, token = grad_x_part(0, cot_top, [], [parts[7]])
+    parts = eight_round(list(parts), tm, grp)
+    ins = [(VMEM, a) for a in parts] + [(ANY, token)]
+    (mine,) = call(sum_kernel, "sum", ins, [(VMEM, parts[0].shape)])
+    for bit in plan(tm, grp)[2]:
+        got = swap(mine, tm, grp, bit)
+        (mine,) = call(add_kernel, "add", [(VMEM, mine), (VMEM, got)], [(VMEM, mine.shape)])
+    parts = eight_round([mine] * 8, tm, grp)
     grad_x, token = grad_x_part(1, cot_bot, [grad_x], [mine])
-    outs, ended = finish([(mine, False, False), (side, True, False)], [])
-    far = passed(far, [token, ended])
-    side = core_round(far, tm, grp)
-    outs, _ = finish([(far, False, True)], outs)
-    outs, _ = finish([(side, True, True)], outs)
-    sum_s, sum_t, sum_d = outs
+    ins = [(VMEM, a) for a in parts] + [(ANY, token)]
+    (mine,) = call(gather_kernel, "gather", ins, [(VMEM, (8,) + mine.shape)])
+    got = core_round(mine, tm, grp)
+    outs = finish(True, mine, [])
+    sum_s, sum_t, sum_d = finish(False, got, outs)
     return (
-        down.reshape(cotangent.shape),
+        down,
         grad_x.reshape(frames_in.shape),
         sum_s.reshape(w_spatial.shape),
         sum_t,

time: 97.9 us -> 84.7 us (0.87)
  waiting for transfers between devices: 29.6 us -> 19.1 us
  Pallas kernels: 33.2 us -> 29.1 us
  starting transfers between devices: 30 us -> 32.5 us
  local copies, waits for them, and re-layouts: 3.19 us -> 2.19 us
    ppermute x13 -> x18, waiting for transfers between devices: 24.9 us -> 13.7 us  [swap(): return lax.ppermute(value, AXES, [(d, d ^ flip) for d in range(tm * grp)])]
    pallas_call x21 -> x15, Pallas kernels: 33.2 us -> 29.1 us  [call(): pl.pallas_call(kernel, out_shape=shapes, in_specs=[s for s, _ in ins], ou...]
    reshape x2 -> x0, local copies, waits for them, and re-layouts: 2.49 us -> none  [the longest x1 1.72 us: body(): cot = cotangent.reshape(slots, wide // 4, ch)]
    unnamed x12, local copies, waits for them, and re-layouts: 0.71 us -> 2.19 us
    ppermute x13 -> x18, starting transfers between devices: 22.2 us -> 23.7 us  [swap(): return lax.ppermute(value, AXES, [(d, d ^ flip) for d in range(tm * grp)])]
    ppermute x2, starting transfers between devices: 3.23 us -> 4.31 us  [along(): return lax.ppermute(value, axis, pairs)]
  transfers between devices with their start and end apart: 17 -> 22, of which waited for: 10 -> 8; matrix products, arithmetic and copies ran while one was open for 1% -> 0% of each run, Pallas kernels for 24% -> 25%
where the time goes in v6:
time: 84.7 us; the launch traced here: 84.4 us
  starting transfers between devices  32.5 us (38%)
  Pallas kernels  29.1 us (34%)
  waiting for transfers between devices  19.1 us (23%)
  local copies, waits for them, and re-layouts  2.19 us (3%)
  between operations  1.54 us (2%)
    pallas_call x15, Pallas kernels, call(): pl.pallas_call(kernel, out_shape=shapes, in_specs=[s for s, _ in ins], ou...  29.1 us
    ppermute x18, starting transfers between devices, swap(): return lax.ppermute(value, AXES, [(d, d ^ flip) for d in range(tm * grp)])  23.7 us
    ppermute x18, waiting for transfers between devices, swap(): return lax.ppermute(value, AXES, [(d, d ^ flip) for d in range(tm * grp)])  13.7 us
    ppermute x2, waiting for transfers between devices, from_bands(): got = lax.ppermute(parts[0], 'grp', [(0, 1), (1, 0)])  5.36 us
    ppermute x2, starting transfers between devices, from_bands(): got = lax.ppermute(parts[0], 'grp', [(0, 1), (1, 0)])  4.54 us
    ppermute x2, starting transfers between devices, along(): return lax.ppermute(value, axis, pairs)  4.31 us
    unnamed x12, local copies, waits for them, and re-layouts  2.19 us
  transfers between devices with their start and end apart: 22, of which 8 were waited for; matrix products, arithmetic and copies ran while one was open for 0% of the time, Pallas kernels for 25%

profile of v6, /device:TPU:0, one launch (start us, length us, event | category | flops | bytes accessed | tf_op | source)
XLA Modules:
  0.0 84.4 jit_solution(281279665867574941)
XLA Ops:
  1.3 1.2 %copy-done.3 = bf16[16,16,8,256]{3,2,1,0:T(8,128)(2,1)S(1)} copy-done((bf16[16,16,8,256]{3,2,1,0:T(8,128)(2,1)S(1)}, bf16[16,16,8,256]{3,2,1,0:T(8,128)(2,1)}, u32[]{:S(2)}) %copy-start.3) | copy-done | bytes 1048600
  2.5 0.9 %copy-done.4 = bf16[16,8,4,256]{3,2,1,0:T(4,128)(2,1)S(1)} copy-done((bf16[16,8,4,256]{3,2,1,0:T(4,128)(2,1)S(1)}, bf16[16,8,4,256]{3,2,1,0:T(4,128)(2,1)}, u32[]{:S(2)}) %copy-start.4) | copy-done | bytes 262168
  3.5 0.3 edges.1
  3.8 3.0 %collective-permute-start = (bf16[128,256]{1,0:T(8,128)(2,1)S(1)}, bf16[128,256]{1,0:T(8,128)(2,1)S(1)}, u32[]{:S(2)}, u32[]{:S(2)}) collective-permute-start(bf16[128,256]{1,0:T(8,128)(2,1)S(1)} %get-tuple-element.42), channel_id=1, source_target_pairs={{0,1},{1,0},{2,3},{3,2},{4,5},{5,4},{6,7},{7,6},{8,9},{9,8},{10,11... | collective-permute-start | bytes 196616 | tf_op jit(solution)/shard_map/ppermute | solution.py:442
  6.8 1.3 %collective-permute-start.2 = (bf16[2,8,4,256]{3,2,1,0:T(4,128)(2,1)S(1)}, bf16[2,8,4,256]{3,2,1,0:T(4,128)(2,1)S(1)}, u32[]{:S(2)}, u32[]{:S(2)}) collective-permute-start(bf16[2,8,4,256]{3,2,1,0:T(4,128)(2,1)S(1)} %get-tuple-element.47), channel_id=1, source_target_pairs={{2,0},{4,2},{6,4},{8,6},{10,8},{12,10},{14,12},{16,14},{18,16},{20... | collective-permute-start | bytes 98312 | tf_op jit(solution)/shard_map/ppermute | solution.py:437
  8.1 3.3 %acts.1 = (bf16[16,8,16,256]{3,2,1,0:T(8,128)(2,1)S(1)}, bf16[18,10,16,256]{3,2,1,0:T(8,128)(2,1)S(1)}, bf16[256,2304]{1,0:T(8,128)(2,1)S(1)}) custom-call(s32[1]{0:T(128)S(6)} %copy.27.count_ref, bf16[16,128,256]{2,1,0:T(8,128)(2,1)S(1)} %bitcast.14, f32[8,128]{1,0:T(8,128)S(1)} %get-tuple-element.40._), custom_call_target="tpu_custom_call" | custom-call | flops 536870912 | bytes 4751364 | tf_op jit(solution)/shard_map/acts/pallas_call | solution.py:377
  11.4 0.0 collective-permute-done.top_ref.bot_ref
  11.5 0.0 copy-start.1
  11.5 0.0 copy-start.2
  11.5 0.0 copy-start.5
  11.5 3.8 %spatial.1 = (bf16[18,10,16,256]{3,2,1,0:T(8,128)(2,1)S(1)}, bf16[16,8,16,256]{3,2,1,0:T(8,128)(2,1)S(1)}, bf16[8,32,256]{2,1,0:T(8,128)(2,1)S(1)}) custom-call(s32[1]{0:T(128)S(6)} %copy.27.count_ref, bf16[128,256]{1,0:T(8,128)(2,1)S(1)} %collective-permute-done.top_ref.bot_ref, ...), custom_call_target="tpu_custom_call", output_to_operand_aliasing={{0}: (3, {})} | custom-call | flops 2415919104 | bytes 5439492 | tf_op jit(solution)/shard_map/spatial/pallas_call | solution.py:377
  15.3 3.0 %collective-permute-start.1 = (bf16[8,32,256]{2,1,0:T(8,128)(2,1)S(1)}, bf16[8,32,256]{2,1,0:T(8,128)(2,1)S(1)}, u32[]{:S(2)}, u32[]{:S(2)}) collective-permute-start(bf16[8,32,256]{2,1,0:T(8,128)(2,1)S(1)} %get-tuple-element.45._), channel_id=1, source_target_pairs={{0,2},{2,4},{4,6},{6,8},{8,10},{10,12},{12,14},{14,16},{16,18},{18... | collective-permute-start | bytes 393224 | tf_op jit(solution)/shard_map/ppermute | solution.py:437
  18.3 5.0 %grad_spatial.1 = (bf16[256,2304]{1,0:T(8,128)(2,1)S(1)}, bf16[8,4,16,256]{3,2,1,0:T(8,128)(2,1)S(1)}, bf16[16,8,16,256]{3,2,1,0:T(8,128)(2,1)S(1)}, bf16[16,10,...) custom-call(s32[1]{0:T(128)S(6)} %copy.27.count_ref, ...), custom_call_target="tpu_custom_call", output_to_operand_aliasing={{0}: (1, {})} | custom-call | flops 3758096384 | bytes 7536644 | tf_op jit(solution)/shard_map/grad_spatial/pallas_call | solution.py:377
  23.4 5.7 %forward.1 = (bf16[16,8,4,256]{3,2,1,0:T(4,128)(2,1)}, bf16[8,7,32,128]{3,2,1,0:T(8,128)(2,1)S(1)}, bf16[8,7,32,128]{3,2,1,0:T(8,128)(2,1)S(1)}) custom-call(s32[1]{0:T(128)S(6)} %copy.27.count_ref, bf16[16,8,16,256]{3,2,1,0:T(8,128)(2,1)S(1)} %get-tuple-element.41.xt_ref, bf16[16,8,16,256]{3,2,1,0:T(8,128)(2,1)S(1)} %get-tuple-element.44.sp_ref, ...), custom_call_target="tpu_custom_call" | custom-call | flops 2684354560 | bytes 5636100 | tf_op jit(solution)/shard_map/forward/pallas_call | solution.py:377
  29.1 1.1 %collective-permute-start.4 = (bf16[8,9,32,128]{3,2,1,0:T(8,128)(2,1)S(1)}, bf16[8,9,32,128]{3,2,1,0:T(8,128)(2,1)S(1)}, u32[]{:S(2)}, u32[]{:S(2)}) collective-permute-start(bf16[8,9,32,128]{3,2,1,0:T(8,128)(2,1)S(1)} %pass.2), channel_id=1, source_target_pairs={{0,2},{1,3},{2,0},{3,1},{4,6},{5,7},{6,4},{7,5},{8,10},{9,11},{10,... | collective-permute-start | bytes 1769480 | tf_op jit(solution)/shard_map/ppermute | solution.py:401
  30.2 1.6 %collective-permute-done.4.__1_.got_a = bf16[8,9,32,128]{3,2,1,0:T(8,128)(2,1)S(1)} collective-permute-done((bf16[8,9,32,128]{3,2,1,0:T(8,128)(2,1)S(1)}, bf16[8,9,32,128]{3,2,1,0:T(8,128)(2,1)S(1)}, u32[]{:S(2)}, u32[]{:S(2)}) %collective-permute-start.4) | collective-permute-done | bytes 589856 | tf_op jit(solution)/shard_map/ppermute | solution.py:401
  31.9 0.4 collective-permute-start.5
  32.2 1.4 %collective-permute-done.5.got_b = bf16[8,7,32,128]{3,2,1,0:T(8,128)(2,1)S(1)} collective-permute-done((bf16[8,7,32,128]{3,2,1,0:T(8,128)(2,1)S(1)}, bf16[8,7,32,128]{3,2,1,0:T(8,128)(2,1)S(1)}, u32[]{:S(2)}, u32[]{:S(2)}) %collective-permute-start.5) | collective-permute-done | bytes 458784 | tf_op jit(solution)/shard_map/ppermute | solution.py:401
  33.7 0.2 scatter.1
  33.9 2.1 %collective-permute-start.6 = (bf16[16,32,128]{2,1,0:T(8,128)(2,1)S(1)}, bf16[16,32,128]{2,1,0:T(8,128)(2,1)S(1)}, u32[]{:S(2)}, u32[]{:S(2)}) collective-permute-start(bf16[16,32,128]{2,1,0:T(8,128)(2,1)S(1)} %get-tuple-element.60), channel_id=1, source_target_pairs={{0,4},{1,5},{2,6},{3,7},{4,0},{5,1},{6,2},{7,3},{8,12},{9,13},{10,... | collective-permute-start | bytes 393224 | tf_op jit(solution)/shard_map/ppermute | solution.py:401
  36.1 0.5 collective-permute-start.7
  36.6 1.5 %collective-permute-start.3 = (bf16[64,256]{1,0:T(8,128)(2,1)S(1)}, bf16[64,256]{1,0:T(8,128)(2,1)S(1)}, u32[]{:S(2)}, u32[]{:S(2)}) collective-permute-start(bf16[64,256]{1,0:T(8,128)(2,1)S(1)} %get-tuple-element.53), channel_id=1, source_target_pairs={{0,1},{1,0},{2,3},{3,2},{4,5},{5,4},{6,7},{7,6},{8,9},{9,8},{10,11... | collective-permute-start | bytes 98312 | tf_op jit(solution)/shard_map/ppermute | solution.py:442
  38.1 0.0 collective-permute-start.8
  38.1 1.6 %collective-permute-start.9 = (bf16[16,32,128]{2,1,0:T(8,128)(2,1)S(1)}, bf16[16,32,128]{2,1,0:T(8,128)(2,1)S(1)}, u32[]{:S(2)}, u32[]{:S(2)}) collective-permute-start(bf16[16,32,128]{2,1,0:T(8,128)(2,1)S(1)} %get-tuple-element.63), channel_id=1, source_target_pairs={{0,8},{1,9},{2,10},{3,11},{4,12},{5,13},{6,14},{7,15},{8,0},{9,1},... | collective-permute-start | bytes 393224 | tf_op jit(solution)/shard_map/ppermute | solution.py:401
  39.7 5.4 %collective-permute-done.3.halo_ref = bf16[64,256]{1,0:T(8,128)(2,1)S(1)} collective-permute-done((bf16[64,256]{1,0:T(8,128)(2,1)S(1)}, bf16[64,256]{1,0:T(8,128)(2,1)S(1)}, u32[]{:S(2)}, u32[]{:S(2)}) %collective-permute-start.3) | collective-permute-done | bytes 32800 | tf_op jit(solution)/shard_map/ppermute | solution.py:442
  45.1 1.4 %collective-permute-start.10 = (bf16[16,32,128]{2,1,0:T(8,128)(2,1)S(1)}, bf16[16,32,128]{2,1,0:T(8,128)(2,1)S(1)}, u32[]{:S(2)}, u32[]{:S(2)}) collective-permute-start(bf16[16,32,128]{2,1,0:T(8,128)(2,1)S(1)} %get-tuple-element.64), channel_id=1, source_target_pairs={{0,12},{1,13},{2,14},{3,15},{4,8},{5,9},{6,10},{7,11},{8,4},{9,5},... | collective-permute-start | bytes 393224 | tf_op jit(solution)/shard_map/ppermute | solution.py:401
  46.4 0.2 collective-permute-start.11
  46.6 3.9 %collective-permute-start.12 = (bf16[16,32,128]{2,1,0:T(8,128)(2,1)S(1)}, bf16[16,32,128]{2,1,0:T(8,128)(2,1)S(1)}, u32[]{:S(2)}, u32[]{:S(2)}) collective-permute-start(bf16[16,32,128]{2,1,0:T(8,128)(2,1)S(1)} %get-tuple-element.57.rest_0_), channel_id=1, source_target_pairs={{0,13},{1,12},{2,15},{3,14},{4,9},{5,8},{6,11},{7,10},{8,5},{9,4},... | collective-permute-start | bytes 393224 | tf_op jit(solution)/shard_map/ppermute | solution.py:401
  50.5 3.8 %grad_x.2 = (bf16[16,128,256]{2,1,0:T(8,128)(2,1)}, f32[8,128]{1,0:T(8,128)S(1)}) custom-call(s32[1]{0:T(128)S(6)} %copy.27.count_ref, bf16[16,8,16,256]{3,2,1,0:T(8,128)(2,1)S(1)} %get-tuple-element.41.xt_ref, bf16[16,8,16,256]{3,2,1,0:T(8,128)(2,1)S(1)} %get-tuple-element.49.gy_ref, bf16[16,10,16,256]{3,2,1,0:T(8,128)(2,1)S(1)} %get-tuple-element.52.gs_ref, ...), custom_call_target="tpu_custom_call" | custom-call | flops 1342177280 | bytes 6590468 | tf_op jit(solution)/shard_map/grad_x/pallas_call | solution.py:377
  54.3 2.2 %collective-permute-done.12.refs_7_ = bf16[16,32,128]{2,1,0:T(8,128)(2,1)S(1)} collective-permute-done((bf16[16,32,128]{2,1,0:T(8,128)(2,1)S(1)}, bf16[16,32,128]{2,1,0:T(8,128)(2,1)S(1)}, u32[]{:S(2)}, u32[]{:S(2)}) %collective-permute-start.12) | collective-permute-done | bytes 131104 | tf_op jit(solution)/shard_map/ppermute | solution.py:401
  56.5 0.1 sum.1.a_ref
  56.6 2.3 %collective-permute-start.13 = (bf16[16,32,128]{2,1,0:T(8,128)(2,1)S(1)}, bf16[16,32,128]{2,1,0:T(8,128)(2,1)S(1)}, u32[]{:S(2)}, u32[]{:S(2)}) collective-permute-start(bf16[16,32,128]{2,1,0:T(8,128)(2,1)S(1)} %sum.1.a_ref), channel_id=1, source_target_pairs={{0,16},{1,17},{2,18},{3,19},{4,20},{5,21},{6,22},{7,23},{8,24},{9,... | collective-permute-start | bytes 393224 | tf_op jit(solution)/shard_map/ppermute | solution.py:401
  59.0 5.6 %collective-permute-done.13.b_ref = bf16[16,32,128]{2,1,0:T(8,128)(2,1)S(1)} collective-permute-done((bf16[16,32,128]{2,1,0:T(8,128)(2,1)S(1)}, bf16[16,32,128]{2,1,0:T(8,128)(2,1)S(1)}, u32[]{:S(2)}, u32[]{:S(2)}) %collective-permute-start.13) | collective-permute-done | bytes 131104 | tf_op jit(solution)/shard_map/ppermute | solution.py:401
  64.6 0.6 collective-permute-start.20
  65.2 1.9 %collective-permute-start.19 = (bf16[16,32,128]{2,1,0:T(8,128)(2,1)S(1)}, bf16[16,32,128]{2,1,0:T(8,128)(2,1)S(1)}, u32[]{:S(2)}, u32[]{:S(2)}) collective-permute-start(bf16[16,32,128]{2,1,0:T(8,128)(2,1)S(1)} %add.1.rest_1_.refs_0_), channel_id=1, source_target_pairs={{0,9},{1,8},{2,11},{3,10},{4,13},{5,12},{6,15},{7,14},{8,1},{9,0},... | collective-permute-start | bytes 393224 | tf_op jit(solution)/shard_map/ppermute | solution.py:401
  67.1 0.7 collective-permute-start.18
  67.8 2.6 %collective-permute-start.17 = (bf16[16,32,128]{2,1,0:T(8,128)(2,1)S(1)}, bf16[16,32,128]{2,1,0:T(8,128)(2,1)S(1)}, u32[]{:S(2)}, u32[]{:S(2)}) collective-permute-start(bf16[16,32,128]{2,1,0:T(8,128)(2,1)S(1)} %add.1.rest_1_.refs_0_), channel_id=1, source_target_pairs={{0,8},{1,9},{2,10},{3,11},{4,12},{5,13},{6,14},{7,15},{8,0},{9,1},... | collective-permute-start | bytes 393224 | tf_op jit(solution)/shard_map/ppermute | solution.py:401
  70.5 1.1 %collective-permute-start.16 = (bf16[16,32,128]{2,1,0:T(8,128)(2,1)S(1)}, bf16[16,32,128]{2,1,0:T(8,128)(2,1)S(1)}, u32[]{:S(2)}, u32[]{:S(2)}) collective-permute-start(bf16[16,32,128]{2,1,0:T(8,128)(2,1)S(1)} %add.1.rest_1_.refs_0_), channel_id=1, source_target_pairs={{0,5},{1,4},{2,7},{3,6},{4,1},{5,0},{6,3},{7,2},{8,13},{9,12},{10,... | collective-permute-start | bytes 393224 | tf_op jit(solution)/shard_map/ppermute | solution.py:401
  71.6 1.4 %collective-permute-done.20.refs_7_ = bf16[16,32,128]{2,1,0:T(8,128)(2,1)S(1)} collective-permute-done((bf16[16,32,128]{2,1,0:T(8,128)(2,1)S(1)}, bf16[16,32,128]{2,1,0:T(8,128)(2,1)S(1)}, u32[]{:S(2)}, u32[]{:S(2)}) %collective-permute-start.20) | collective-permute-done | bytes 131104 | tf_op jit(solution)/shard_map/ppermute | solution.py:401
  73.0 1.2 %collective-permute-start.15 = (bf16[16,32,128]{2,1,0:T(8,128)(2,1)S(1)}, bf16[16,32,128]{2,1,0:T(8,128)(2,1)S(1)}, u32[]{:S(2)}, u32[]{:S(2)}) collective-permute-start(bf16[16,32,128]{2,1,0:T(8,128)(2,1)S(1)} %add.1.rest_1_.refs_0_), channel_id=1, source_target_pairs={{0,1},{1,0},{2,3},{3,2},{4,5},{5,4},{6,7},{7,6},{8,9},{9,8},{10,11... | collective-permute-start | bytes 393224 | tf_op jit(solution)/shard_map/ppermute | solution.py:401
  74.2 0.3 collective-permute-done.19.refs_6_
  74.4 1.9 %collective-permute-start.14 = (bf16[16,32,128]{2,1,0:T(8,128)(2,1)S(1)}, bf16[16,32,128]{2,1,0:T(8,128)(2,1)S(1)}, u32[]{:S(2)}, u32[]{:S(2)}) collective-permute-start(bf16[16,32,128]{2,1,0:T(8,128)(2,1)S(1)} %add.1.rest_1_.refs_0_), channel_id=1, source_target_pairs={{0,4},{1,5},{2,6},{3,7},{4,0},{5,1},{6,2},{7,3},{8,12},{9,13},{10,... | collective-permute-start | bytes 393224 | tf_op jit(solution)/shard_map/ppermute | solution.py:401
  76.3 3.8 %grad_x.3 = (bf16[16,128,256]{2,1,0:T(8,128)(2,1)}, f32[8,128]{1,0:T(8,128)S(1)}) custom-call(s32[1]{0:T(128)S(6)} %copy.27.count_ref, bf16[16,8,16,256]{3,2,1,0:T(8,128)(2,1)S(1)} %get-tuple-element.41.xt_ref, bf16[16,8,16,256]{3,2,1,0:T(8,128)(2,1)S(1)} %get-tuple-element.49.gy_ref, ...), custom_call_target="tpu_custom_call", output_to_operand_aliasing={{0}: (8, {})} | custom-call | flops 1342177280 | bytes 7639044 | tf_op jit(solution)/shard_map/grad_x/pallas_call | solution.py:377
  80.2 0.1 gather.1.half_ref
  80.3 0.1 collective-permute-start.21
  80.3 1.4 %finish.2 = (f32[9,256,256]{2,1,0:T(8,128)}, f32[3,256,256]{2,1,0:T(8,128)}, f32[4,256,256]{2,1,0:T(8,128)}) custom-call(bf16[8,16,32,128]{3,2,1,0:T(8,128)(2,1)S(1)} %gather.1.half_ref), custom_call_target="tpu_custom_call" | custom-call | bytes 5242880 | tf_op jit(solution)/shard_map/finish/pallas_call | solution.py:377
  81.8 1.2 %collective-permute-done.21.half_ref = bf16[8,16,32,128]{3,2,1,0:T(8,128)(2,1)S(1)} collective-permute-done((bf16[8,16,32,128]{3,2,1,0:T(8,128)(2,1)S(1)}, bf16[8,16,32,128]{3,2,1,0:T(8,128)(2,1)S(1)}, u32[]{:S(2)}, u32[]{:S(2)}) %collective-permute-start.21) | collective-permute-done | bytes 1048608 | tf_op jit(solution)/shard_map/ppermute | solution.py:401
  83.0 1.4 %finish.3 = (f32[9,256,256]{2,1,0:T(8,128)}, f32[3,256,256]{2,1,0:T(8,128)}, f32[4,256,256]{2,1,0:T(8,128)}) custom-call(bf16[8,16,32,128]{3,2,1,0:T(8,128)(2,1)S(1)} %collective-permute-done.21.half_ref, f32[9,256,256]{2,1,0:T(8,128)} %get-tuple-element.69.rest_0_, ...), custom_call_target="tpu_custom_call", output_to_operand_aliasing={{0}: (1, {}), {1}: (2, {}), {2}: (3, {})} | custom-call | bytes 9437184 | tf_op jit(solution)/shard_map/finish/pallas_call | solution.py:377
  (23 shorter events, 0.1 us)
Async XLA Ops:
  1.3 1.2 %copy-start.3 = (bf16[16,16,8,256]{3,2,1,0:T(8,128)(2,1)S(1)}, bf16[16,16,8,256]{3,2,1,0:T(8,128)(2,1)}, u32[]{:S(2)}) copy-start(bf16[16,16,8,256]{3,2,1,0:T(8,128)(2,1)} %param.6) | copy-start | bytes 3145732
  2.5 0.9 %copy-start.4 = (bf16[16,8,4,256]{3,2,1,0:T(4,128)(2,1)S(1)}, bf16[16,8,4,256]{3,2,1,0:T(4,128)(2,1)}, u32[]{:S(2)}) copy-start(bf16[16,8,4,256]{3,2,1,0:T(4,128)(2,1)} %cot_ref.3) | copy-start | bytes 786436
  3.5 8.0 %copy-start = (bf16[3,3,256,256]{3,2,1,0:T(8,128)(2,1)S(1)}, bf16[3,3,256,256]{3,2,1,0:T(8,128)(2,1)}, u32[]{:S(2)}) copy-start(bf16[3,3,256,256]{3,2,1,0:T(8,128)(2,1)} %param.8) | copy-start | bytes 3538948
  3.8 7.7 %collective-permute-start = (bf16[128,256]{1,0:T(8,128)(2,1)S(1)}, bf16[128,256]{1,0:T(8,128)(2,1)S(1)}, u32[]{:S(2)}, u32[]{:S(2)}) collective-permute-start(bf16[128,256]{1,0:T(8,128)(2,1)S(1)} %get-tuple-element.42), channel_id=1, source_target_pairs={{0,1},{1,0},{2,3},{3,2},{4,5},{5,4},{6,7},{7,6},{8,9},{9,8},{10,11... | collective-permute-start | bytes 196616 | tf_op jit(solution)/shard_map/ppermute | solution.py:442
  6.8 11.5 %collective-permute-start.2 = (bf16[2,8,4,256]{3,2,1,0:T(4,128)(2,1)S(1)}, bf16[2,8,4,256]{3,2,1,0:T(4,128)(2,1)S(1)}, u32[]{:S(2)}, u32[]{:S(2)}) collective-permute-start(bf16[2,8,4,256]{3,2,1,0:T(4,128)(2,1)S(1)} %get-tuple-element.47), channel_id=1, source_target_pairs={{2,0},{4,2},{6,4},{8,6},{10,8},{12,10},{14,12},{16,14},{18,16},{20... | collective-permute-start | bytes 98312 | tf_op jit(solution)/shard_map/ppermute | solution.py:437
  11.5 6.8 %copy-start.1 = (bf16[2,2,256,256]{3,2,1,0:T(8,128)(2,1)S(1)}, bf16[2,2,256,256]{3,2,1,0:T(8,128)(2,1)}, u32[]{:S(2)}) copy-start(bf16[2,2,256,256]{3,2,1,0:T(8,128)(2,1)} %param.10) | copy-start | bytes 1572868
  11.5 6.8 %copy-start.2 = (bf16[3,256,256]{2,1,0:T(8,128)(2,1)S(1)}, bf16[3,256,256]{2,1,0:T(8,128)(2,1)}, u32[]{:S(2)}) copy-start(bf16[3,256,256]{2,1,0:T(8,128)(2,1)} %wt_ref.7) | copy-start | bytes 1179652
  11.5 6.8 %copy-start.5 = (bf16[16,8,4,256]{3,2,1,0:T(4,128)(2,1)S(1)}, bf16[16,8,4,256]{3,2,1,0:T(4,128)(2,1)}, u32[]{:S(2)}) copy-start(bf16[16,8,4,256]{3,2,1,0:T(4,128)(2,1)} %cot_ref.3) | copy-start | bytes 786436
  15.3 8.1 %collective-permute-start.1 = (bf16[8,32,256]{2,1,0:T(8,128)(2,1)S(1)}, bf16[8,32,256]{2,1,0:T(8,128)(2,1)S(1)}, u32[]{:S(2)}, u32[]{:S(2)}) collective-permute-start(bf16[8,32,256]{2,1,0:T(8,128)(2,1)S(1)} %get-tuple-element.45._), channel_id=1, source_target_pairs={{0,2},{2,4},{4,6},{6,8},{8,10},{10,12},{12,14},{14,16},{16,18},{18... | collective-permute-start | bytes 393224 | tf_op jit(solution)/shard_map/ppermute | solution.py:437
  29.1 2.7 %collective-permute-start.4 = (bf16[8,9,32,128]{3,2,1,0:T(8,128)(2,1)S(1)}, bf16[8,9,32,128]{3,2,1,0:T(8,128)(2,1)S(1)}, u32[]{:S(2)}, u32[]{:S(2)}) collective-permute-start(bf16[8,9,32,128]{3,2,1,0:T(8,128)(2,1)S(1)} %pass.2), channel_id=1, source_target_pairs={{0,2},{1,3},{2,0},{3,1},{4,6},{5,7},{6,4},{7,5},{8,10},{9,11},{10,... | collective-permute-start | bytes 1769480 | tf_op jit(solution)/shard_map/ppermute | solution.py:401
  31.9 1.8 %collective-permute-start.5 = (bf16[8,7,32,128]{3,2,1,0:T(8,128)(2,1)S(1)}, bf16[8,7,32,128]{3,2,1,0:T(8,128)(2,1)S(1)}, u32[]{:S(2)}, u32[]{:S(2)}) collective-permute-start(bf16[8,7,32,128]{3,2,1,0:T(8,128)(2,1)S(1)} %pass.3), channel_id=1, source_target_pairs={{0,2},{1,3},{2,0},{3,1},{4,6},{5,7},{6,4},{7,5},{8,10},{9,11},{10,... | collective-permute-start | bytes 1376264 | tf_op jit(solution)/shard_map/ppermute | solution.py:401
  33.9 12.5 %collective-permute-start.6 = (bf16[16,32,128]{2,1,0:T(8,128)(2,1)S(1)}, bf16[16,32,128]{2,1,0:T(8,128)(2,1)S(1)}, u32[]{:S(2)}, u32[]{:S(2)}) collective-permute-start(bf16[16,32,128]{2,1,0:T(8,128)(2,1)S(1)} %get-tuple-element.60), channel_id=1, source_target_pairs={{0,4},{1,5},{2,6},{3,7},{4,0},{5,1},{6,2},{7,3},{8,12},{9,13},{10,... | collective-permute-start | bytes 393224 | tf_op jit(solution)/shard_map/ppermute | solution.py:401
  36.1 10.5 %collective-permute-start.7 = (bf16[16,32,128]{2,1,0:T(8,128)(2,1)S(1)}, bf16[16,32,128]{2,1,0:T(8,128)(2,1)S(1)}, u32[]{:S(2)}, u32[]{:S(2)}) collective-permute-start(bf16[16,32,128]{2,1,0:T(8,128)(2,1)S(1)} %get-tuple-element.61), channel_id=1, source_target_pairs={{0,1},{1,0},{2,3},{3,2},{4,5},{5,4},{6,7},{7,6},{8,9},{9,8},{10,11... | collective-permute-start | bytes 393224 | tf_op jit(solution)/shard_map/ppermute | solution.py:401
  36.6 8.5 %collective-permute-start.3 = (bf16[64,256]{1,0:T(8,128)(2,1)S(1)}, bf16[64,256]{1,0:T(8,128)(2,1)S(1)}, u32[]{:S(2)}, u32[]{:S(2)}) collective-permute-start(bf16[64,256]{1,0:T(8,128)(2,1)S(1)} %get-tuple-element.53), channel_id=1, source_target_pairs={{0,1},{1,0},{2,3},{3,2},{4,5},{5,4},{6,7},{7,6},{8,9},{9,8},{10,11... | collective-permute-start | bytes 98312 | tf_op jit(solution)/shard_map/ppermute | solution.py:442
  38.1 16.2 %collective-permute-start.8 = (bf16[16,32,128]{2,1,0:T(8,128)(2,1)S(1)}, bf16[16,32,128]{2,1,0:T(8,128)(2,1)S(1)}, u32[]{:S(2)}, u32[]{:S(2)}) collective-permute-start(bf16[16,32,128]{2,1,0:T(8,128)(2,1)S(1)} %get-tuple-element.62), channel_id=1, source_target_pairs={{0,5},{1,4},{2,7},{3,6},{4,1},{5,0},{6,3},{7,2},{8,13},{9,12},{10,... | collective-permute-start | bytes 393224 | tf_op jit(solution)/shard_map/ppermute | solution.py:401
  38.1 16.1 %collective-permute-start.9 = (bf16[16,32,128]{2,1,0:T(8,128)(2,1)S(1)}, bf16[16,32,128]{2,1,0:T(8,128)(2,1)S(1)}, u32[]{:S(2)}, u32[]{:S(2)}) collective-permute-start(bf16[16,32,128]{2,1,0:T(8,128)(2,1)S(1)} %get-tuple-element.63), channel_id=1, source_target_pairs={{0,8},{1,9},{2,10},{3,11},{4,12},{5,13},{6,14},{7,15},{8,0},{9,1},... | collective-permute-start | bytes 393224 | tf_op jit(solution)/shard_map/ppermute | solution.py:401
  45.1 9.2 %collective-permute-start.10 = (bf16[16,32,128]{2,1,0:T(8,128)(2,1)S(1)}, bf16[16,32,128]{2,1,0:T(8,128)(2,1)S(1)}, u32[]{:S(2)}, u32[]{:S(2)}) collective-permute-start(bf16[16,32,128]{2,1,0:T(8,128)(2,1)S(1)} %get-tuple-element.64), channel_id=1, source_target_pairs={{0,12},{1,13},{2,14},{3,15},{4,8},{5,9},{6,10},{7,11},{8,4},{9,5},... | collective-permute-start | bytes 393224 | tf_op jit(solution)/shard_map/ppermute | solution.py:401
  46.4 7.8 %collective-permute-start.11 = (bf16[16,32,128]{2,1,0:T(8,128)(2,1)S(1)}, bf16[16,32,128]{2,1,0:T(8,128)(2,1)S(1)}, u32[]{:S(2)}, u32[]{:S(2)}) collective-permute-start(bf16[16,32,128]{2,1,0:T(8,128)(2,1)S(1)} %get-tuple-element.65), channel_id=1, source_target_pairs={{0,9},{1,8},{2,11},{3,10},{4,13},{5,12},{6,15},{7,14},{8,1},{9,0},... | collective-permute-start | bytes 393224 | tf_op jit(solution)/shard_map/ppermute | solution.py:401
  46.6 9.9 %collective-permute-start.12 = (bf16[16,32,128]{2,1,0:T(8,128)(2,1)S(1)}, bf16[16,32,128]{2,1,0:T(8,128)(2,1)S(1)}, u32[]{:S(2)}, u32[]{:S(2)}) collective-permute-start(bf16[16,32,128]{2,1,0:T(8,128)(2,1)S(1)} %get-tuple-element.57.rest_0_), channel_id=1, source_target_pairs={{0,13},{1,12},{2,15},{3,14},{4,9},{5,8},{6,11},{7,10},{8,5},{9,4},... | collective-permute-start | bytes 393224 | tf_op jit(solution)/shard_map/ppermute | solution.py:401
  56.6 7.9 %collective-permute-start.13 = (bf16[16,32,128]{2,1,0:T(8,128)(2,1)S(1)}, bf16[16,32,128]{2,1,0:T(8,128)(2,1)S(1)}, u32[]{:S(2)}, u32[]{:S(2)}) collective-permute-start(bf16[16,32,128]{2,1,0:T(8,128)(2,1)S(1)} %sum.1.a_ref), channel_id=1, source_target_pairs={{0,16},{1,17},{2,18},{3,19},{4,20},{5,21},{6,22},{7,23},{8,24},{9,... | collective-permute-start | bytes 393224 | tf_op jit(solution)/shard_map/ppermute | solution.py:401
  64.6 8.5 %collective-permute-start.20 = (bf16[16,32,128]{2,1,0:T(8,128)(2,1)S(1)}, bf16[16,32,128]{2,1,0:T(8,128)(2,1)S(1)}, u32[]{:S(2)}, u32[]{:S(2)}) collective-permute-start(bf16[16,32,128]{2,1,0:T(8,128)(2,1)S(1)} %add.1.rest_1_.refs_0_), channel_id=1, source_target_pairs={{0,13},{1,12},{2,15},{3,14},{4,9},{5,8},{6,11},{7,10},{8,5},{9,4},... | collective-permute-start | bytes 393224 | tf_op jit(solution)/shard_map/ppermute | solution.py:401
  65.2 9.2 %collective-permute-start.19 = (bf16[16,32,128]{2,1,0:T(8,128)(2,1)S(1)}, bf16[16,32,128]{2,1,0:T(8,128)(2,1)S(1)}, u32[]{:S(2)}, u32[]{:S(2)}) collective-permute-start(bf16[16,32,128]{2,1,0:T(8,128)(2,1)S(1)} %add.1.rest_1_.refs_0_), channel_id=1, source_target_pairs={{0,9},{1,8},{2,11},{3,10},{4,13},{5,12},{6,15},{7,14},{8,1},{9,0},... | collective-permute-start | bytes 393224 | tf_op jit(solution)/shard_map/ppermute | solution.py:401
  67.1 13.0 %collective-permute-start.18 = (bf16[16,32,128]{2,1,0:T(8,128)(2,1)S(1)}, bf16[16,32,128]{2,1,0:T(8,128)(2,1)S(1)}, u32[]{:S(2)}, u32[]{:S(2)}) collective-permute-start(bf16[16,32,128]{2,1,0:T(8,128)(2,1)S(1)} %add.1.rest_1_.refs_0_), channel_id=1, source_target_pairs={{0,12},{1,13},{2,14},{3,15},{4,8},{5,9},{6,10},{7,11},{8,4},{9,5},... | collective-permute-start | bytes 393224 | tf_op jit(solution)/shard_map/ppermute | solution.py:401
  67.8 12.3 %collective-permute-start.17 = (bf16[16,32,128]{2,1,0:T(8,128)(2,1)S(1)}, bf16[16,32,128]{2,1,0:T(8,128)(2,1)S(1)}, u32[]{:S(2)}, u32[]{:S(2)}) collective-permute-start(bf16[16,32,128]{2,1,0:T(8,128)(2,1)S(1)} %add.1.rest_1_.refs_0_), channel_id=1, source_target_pairs={{0,8},{1,9},{2,10},{3,11},{4,12},{5,13},{6,14},{7,15},{8,0},{9,1},... | collective-permute-start | bytes 393224 | tf_op jit(solution)/shard_map/ppermute | solution.py:401
  70.5 9.7 %collective-permute-start.16 = (bf16[16,32,128]{2,1,0:T(8,128)(2,1)S(1)}, bf16[16,32,128]{2,1,0:T(8,128)(2,1)S(1)}, u32[]{:S(2)}, u32[]{:S(2)}) collective-permute-start(bf16[16,32,128]{2,1,0:T(8,128)(2,1)S(1)} %add.1.rest_1_.refs_0_), channel_id=1, source_target_pairs={{0,5},{1,4},{2,7},{3,6},{4,1},{5,0},{6,3},{7,2},{8,13},{9,12},{10,... | collective-permute-start | bytes 393224 | tf_op jit(solution)/shard_map/ppermute | solution.py:401
  73.0 7.1 %collective-permute-start.15 = (bf16[16,32,128]{2,1,0:T(8,128)(2,1)S(1)}, bf16[16,32,128]{2,1,0:T(8,128)(2,1)S(1)}, u32[]{:S(2)}, u32[]{:S(2)}) collective-permute-start(bf16[16,32,128]{2,1,0:T(8,128)(2,1)S(1)} %add.1.rest_1_.refs_0_), channel_id=1, source_target_pairs={{0,1},{1,0},{2,3},{3,2},{4,5},{5,4},{6,7},{7,6},{8,9},{9,8},{10,11... | collective-permute-start | bytes 393224 | tf_op jit(solution)/shard_map/ppermute | solution.py:401
  74.4 5.7 %collective-permute-start.14 = (bf16[16,32,128]{2,1,0:T(8,128)(2,1)S(1)}, bf16[16,32,128]{2,1,0:T(8,128)(2,1)S(1)}, u32[]{:S(2)}, u32[]{:S(2)}) collective-permute-start(bf16[16,32,128]{2,1,0:T(8,128)(2,1)S(1)} %add.1.rest_1_.refs_0_), channel_id=1, source_target_pairs={{0,4},{1,5},{2,6},{3,7},{4,0},{5,1},{6,2},{7,3},{8,12},{9,13},{10,... | collective-permute-start | bytes 393224 | tf_op jit(solution)/shard_map/ppermute | solution.py:401
  80.3 2.7 %collective-permute-start.21 = (bf16[8,16,32,128]{3,2,1,0:T(8,128)(2,1)S(1)}, bf16[8,16,32,128]{3,2,1,0:T(8,128)(2,1)S(1)}, u32[]{:S(2)}, u32[]{:S(2)}) collective-permute-start(bf16[8,16,32,128]{3,2,1,0:T(8,128)(2,1)S(1)} %gather.1.half_ref), channel_id=1, source_target_pairs={{0,2},{1,3},{2,0},{3,1},{4,6},{5,7},{6,4},{7,5},{8,10},{9,11},{10,... | collective-permute-start | bytes 3145736 | tf_op jit(solution)/shard_map/ppermute | solution.py:401

commit v7 on v6

--- a/solution.py
+++ b/solution.py
@@ -53,7 +53,7 @@
 
 def silu_norm(v):
     scaled = v * lax.rsqrt(jnp.mean(v * v, axis=-1, keepdims=True) + 1e-06)
-    return scaled / (1.0 + jnp.exp(-scaled))
+    return scaled * (0.5 + 0.5 * jnp.tanh(0.5 * scaled))
 
 
 def slot_mask(shape, count):
@@ -72,14 +72,14 @@
 
 def place_bits():
     t, g = lax.axis_index("tm"), lax.axis_index("grp")
-    return t & 1, ((t >> 1) & 1) + 2 * (g & 1) + 4 * ((t >> 2) & 1)
+    return t & 1, ((t >> 1) & 1) + 2 * (g & 1), (t >> 2) & 3
 
 
 def split_cores(value, keep_ref, send_ref, k):
-    core, _ = place_bits()
+    core, _, _ = place_bits()
     low, high = value[:, : CH // 2].astype(BF), value[:, CH // 2 :].astype(BF)
-    keep_ref[:, k] = jnp.where(core == 0, low, high).reshape(8, 32, CH // 2)
-    send_ref[:, k] = jnp.where(core == 0, high, low).reshape(8, 32, CH // 2)
+    keep_ref[:, k] = jnp.where(core == 0, low, high).reshape(16, 16, CH // 2)
+    send_ref[:, k] = jnp.where(core == 0, high, low).reshape(16, 16, CH // 2)
 
 
 def edges_kernel(bands, count_ref, x_ref, cot_ref, *rest):
@@ -114,9 +114,12 @@
         piece = x_ref[:, pl.ds(at, 16), :].reshape(SLOTS * 16, CH)
         v = mm(place, piece)
         xt_ref[pl.ds(2 * q, 2)] = v.astype(BF).reshape(2, cols, SLOTS, CH)
-        a = silu_norm(v)
-        acts_ref[pl.ds(2 * q + 1, 2), 1 : cols + 1] = a.astype(BF).reshape(2, cols, SLOTS, CH)
-        at_ref[:, pl.ds(pl.multiple_of(q * 256 + 128, 128), 256)] = a.T.astype(BF)
+        a = silu_norm(v).astype(BF)
+        acts_ref[pl.ds(2 * q + 1, 2), 1 : cols + 1] = a.reshape(2, cols, SLOTS, CH)
+        flipped = a.T
+        for i in range(3):
+            at = pl.multiple_of((2 * q + 3 - i) * 128, 128)
+            at_ref[i * CH : i * CH + CH, pl.ds(at, 256)] = flipped
         return 0
 
     lax.fori_loop(0, rows // 2, rows_of, 0)
@@ -136,13 +139,12 @@
     pick = jnp.where(pick, 1.0, 0.0).astype(BF)
 
     def rows_of(q, _):
-        total = None
-        for i in range(3):
-            for j in range(3):
-                left = acts_ref[pl.ds(4 * q + i, 4), j : j + cols].reshape(4 * cols * SLOTS, CH)
-                term = mm(left, ws_ref[i * 3 + j])
-                total = term if total is None else total + term
-        out = total.astype(BF)
+        left = [
+            acts_ref[pl.ds(4 * q + i, 4), j : j + cols].reshape(4 * cols * SLOTS, CH)
+            for i in range(3)
+            for j in range(3)
+        ]
+        out = mm(jnp.concatenate(left, axis=1), ws_ref[...].reshape(9 * CH, CH)).astype(BF)
         sp_ref[pl.ds(4 * q, 4)] = out.reshape(4, cols, SLOTS, CH)
         for half in range(2):
             edge_ref[2 * q + half] = mm(pick, out[half * 256 : half * 256 + 256]).astype(BF)
@@ -158,9 +160,10 @@
     count = count_ref[0]
     band = lax.axis_index("grp")
     rows, cols = gy_ref.shape[0], gy_ref.shape[1]
-    for ref, flag, row in ((top_ref, band > 0, 0), (bot_ref, band < bands - 1, rows + 1)):
+    for ref, flag, i, row in ((top_ref, band > 0, 0, 0), (bot_ref, band < bands - 1, 2, rows + 1)):
         a = jnp.where(flag, ref[...].astype(F32), 0.0)
-        at_ref[:, row * 128 : row * 128 + 128] = a.T.astype(BF)
+        at = (row - i + 2) * 128
+        at_ref[i * CH : i * CH + CH, at : at + 128] = a.T.astype(BF)
     edge = jnp.zeros((rows, SLOTS, CH), BF)
     gs_ref[:, 0] = edge
     gs_ref[:, cols + 1] = edge
@@ -191,22 +194,24 @@
         g = gy_ref[pl.ds(4 * q, 4)].reshape(4 * cols, SLOTS, CH)
         s = grad_of_temporal(g, wt_ref, count)
         gs_ref[pl.ds(4 * q, 4), 1 : cols + 1] = s.reshape(4, cols, SLOTS, CH)
+        g = jnp.where(slot_mask(g.shape, count), g.astype(F32), 0.0)
+        gy_ref[pl.ds(4 * q, 4)] = g.astype(BF).reshape(4, cols, SLOTS, CH)
         return 0
 
     lax.fori_loop(0, rows // 4, grads_of, 0)
 
     wide = rows * cols * SLOTS
-    for i in range(3):
-        for j in range(3):
-            right = gs_ref[:, 2 - j : 2 - j + cols].reshape(wide, CH)
-            value = mm(at_ref[:, i * 128 : i * 128 + wide], right)
-            split_cores(value, keep_ref, send_ref, i * 3 + j)
+    for j in range(3):
+        right = gs_ref[:, 2 - j : 2 - j + cols].reshape(wide, CH)
+        value = mm(at_ref[:, 256 : 256 + wide], right)
+        for i in range(3):
+            split_cores(value[i * CH : i * CH + CH], keep_ref, send_ref, i * 3 + j)
 
 
 def forward_kernel(
     count_ref, xt_ref, sp_ref, prev_ref, cott_ref, gy_ref, wt_ref, wd_ref, *rest
 ):
-    down_ref, keep_ref, send_ref, y_ref, st_ref, g1_ref, g0_ref, g2_ref = rest[-8:]
+    down_ref, keep_ref, send_ref, y_ref, st_ref, yt_ref = rest[-6:]
     count = count_ref[0]
     rows, cols = xt_ref.shape[0], xt_ref.shape[1]
     a, b = iotas(256, 32)
@@ -214,71 +219,66 @@
     place = jnp.where(place, 1.0, 0.0).astype(BF)
 
     def rows_of(q, _):
-        s = sp_ref[pl.ds(2 * q, 2)].reshape(256, CH)
-        s = (s.astype(F32) + mm(place, prev_ref[q])).astype(BF)
-        st_ref[:, pl.ds(pl.multiple_of(q * 256, 256), 256)] = s.T
-        total = mm(s, wt_ref[2]).reshape(2 * cols, SLOTS, CH)
-        for k in (1, 0):
-            total = total + pltpu.roll(mm(s, wt_ref[k]).reshape(2 * cols, SLOTS, CH), 2 - k, 1)
-        x = xt_ref[pl.ds(2 * q, 2)].reshape(2 * cols, SLOTS, CH).astype(F32)
-        mask = slot_mask(x.shape, count)
-        y = jnp.where(mask, x + total, 0.0).astype(BF)
-        y_ref[pl.ds(2 * q, 2)] = y.reshape(2, cols, SLOTS, CH)
-        g = gy_ref[pl.ds(2 * q, 2)].reshape(2 * cols, SLOTS, CH).astype(F32)
-        g = jnp.where(mask, g, 0.0)
-        for ref, k in ((g2_ref, 2), (g1_ref, 1), (g0_ref, 0)):
-            shifted = g if k == 2 else pltpu.roll(g, SLOTS - (2 - k), 1)
-            ref[pl.ds(2 * q, 2)] = shifted.astype(BF).reshape(2, cols, SLOTS, CH)
+        s = sp_ref[pl.ds(4 * q, 4)].reshape(4 * cols * SLOTS, CH).astype(F32)
+        s = s + jnp.concatenate([mm(place, prev_ref[2 * q]), mm(place, prev_ref[2 * q + 1])], 0)
+        s = s.reshape(4 * cols, SLOTS, CH)
+        total = None
+        for k in range(3):
+            shifted = s if k == 2 else pltpu.roll(s, 2 - k, 1)
+            shifted = shifted.astype(BF).reshape(4 * cols * SLOTS, CH)
+            at = pl.ds(pl.multiple_of(q * 512, 512), 512)
+            st_ref[k * CH : k * CH + CH, at] = shifted.T
+            term = mm(shifted, wt_ref[k])
+            total = term if total is None else total + term
+        x = xt_ref[pl.ds(4 * q, 4)].reshape(4 * cols, SLOTS, CH).astype(F32)
+        y = jnp.where(slot_mask(x.shape, count), x + total.reshape(x.shape), 0.0).astype(BF)
+        y_ref[pl.ds(4 * q, 4)] = y.reshape(4, cols, SLOTS, CH)
         return 0
 
-    lax.fori_loop(0, rows // 2, rows_of, 0)
+    lax.fori_loop(0, rows // 4, rows_of, 0)
 
     wide = rows * cols * SLOTS
-    for k, ref in ((0, g0_ref), (1, g1_ref), (2, g2_ref)):
-        split_cores(mm(st_ref[...], ref[...].reshape(wide, CH)), keep_ref, send_ref, k)
+    value = mm(st_ref[...], gy_ref[...].reshape(wide, CH))
+    for k in range(3):
+        split_cores(value[k * CH : k * CH + CH], keep_ref, send_ref, k)
 
     small = wide // 4
     total = None
-    cot = cott_ref[...].reshape(small, CH)
     for i in range(2):
         for j in range(2):
             tiles = [
                 y_ref[2 * r + i, 2 * c + j] for r in range(rows // 2) for c in range(cols // 2)
             ]
             piece = jnp.concatenate(tiles, axis=0)
-            term = mm(piece, wd_ref[i * 2 + j])
+            k = i * 2 + j
+            yt_ref[k * CH : k * CH + CH] = piece.T
+            term = mm(piece, wd_ref[k])
             total = term if total is None else total + term
-            split_cores(mm(piece.T, cot), keep_ref, send_ref, 3 + i * 2 + j)
-    down = total.astype(BF)
-    back = to_frames(16)
-    for q in range(small // 256):
-        o = mm(back, down[q * 256 : q * 256 + 256]).astype(BF)
-        down_ref[:, q * 4 : q * 4 + 4] = o.reshape(SLOTS, 4, cols // 2, CH)
+    down_ref[...] = total.astype(BF)
+    value = mm(yt_ref[...], cott_ref[...].reshape(small, CH))
+    for k in range(4):
+        split_cores(value[k * CH : k * CH + CH], keep_ref, send_ref, 3 + k)
 
 
 def grad_x_kernel(
-    part, bands, count_ref, xt_ref, gy_ref, gs_ref, halo_ref, wt_ref, wd_ref, ws_ref, *rest
+    bands, count_ref, xt_ref, gy_ref, gs_ref, top_ref, bot_ref, wt_ref, wd_ref, ws_ref, slot_ref, *rest
 ):
-    out_ref, token_ref, pad_ref, buf, sems = rest[-5:]
+    out_ref, down_ref, token_ref, pad_ref, buf, sems = rest[-6:]
+    token_ref[...] = jnp.zeros_like(token_ref)
     count = count_ref[0]
     band = lax.axis_index("grp")
     rows, cols = xt_ref.shape[0], xt_ref.shape[1]
-    half = rows // 2
-    if part == 0:
-        flag, i, row = band > 0, 1, 0
-        pad_ref[1 : half + 2] = gs_ref[0 : half + 1]
-    else:
-        flag, i, row = band < bands - 1, 0, half + 1
-        pad_ref[0 : half + 1] = gs_ref[half - 1 :]
+    pad_ref[1 : rows + 1] = gs_ref[...]
     edge = jnp.zeros((SLOTS, CH), BF)
-    pair = [
-        mm_nt(halo_ref[...], wd_ref[i * 2 + j]).astype(BF).reshape(cols // 2, SLOTS, CH)
-        for j in range(2)
-    ]
-    g = jnp.stack(pair, axis=1).reshape(cols, SLOTS, CH)
-    pad_ref[row, 0] = edge
-    pad_ref[row, 1 : cols + 1] = grad_of_temporal(g, wt_ref, jnp.where(flag, count, 0))
-    pad_ref[row, cols + 1] = edge
+    for ref, flag, i, row in ((top_ref, band > 0, 1, 0), (bot_ref, band < bands - 1, 0, rows + 1)):
+        pair = [
+            mm_nt(ref[...], wd_ref[i * 2 + j]).astype(BF).reshape(cols // 2, SLOTS, CH)
+            for j in range(2)
+        ]
+        g = jnp.stack(pair, axis=1).reshape(cols, SLOTS, CH)
+        pad_ref[row, 0] = edge
+        pad_ref[row, 1 : cols + 1] = grad_of_temporal(g, wt_ref, jnp.where(flag, count, 0))
+        pad_ref[row, cols + 1] = edge
     back = to_frames(16)
 
     def rows_of(q, _):
@@ -290,11 +290,11 @@
                 )
                 term = mm_nt(left, ws_ref[i * 3 + j])
                 total = term if total is None else total + term
-        at = part * half + 4 * q
+        at = 4 * q
         v = xt_ref[pl.ds(at, 4)].reshape(4 * cols * SLOTS, CH).astype(F32)
         r = lax.rsqrt(jnp.mean(v * v, axis=-1, keepdims=True) + 1e-06)
         u = v * r
-        s = 1.0 / (1.0 + jnp.exp(-u))
+        s = 0.5 + 0.5 * jnp.tanh(0.5 * u)
         gu = total * (s * (1.0 + u * (1.0 - s)))
         dot = jnp.mean(gu * u, axis=-1, keepdims=True)
         gv = r * (gu - u * dot)
@@ -306,34 +306,41 @@
             buf[:, pl.ds(pl.multiple_of((2 * q + k) * 16, 16), 16), :] = o.reshape(SLOTS, 16, CH)
         return 0
 
-    lax.fori_loop(0, half // 4, rows_of, 0)
-    size = half * cols
-    copy = pltpu.make_async_copy(buf, out_ref.at[:, part * size : part * size + size, :], sems.at[0])
-    token_ref[...] = jnp.zeros_like(token_ref)
+    lax.fori_loop(0, rows // 4, rows_of, 0)
+    copy = pltpu.make_async_copy(buf, out_ref, sems.at[0])
     copy.start()
+    for q in range(down_ref.shape[1] // 4):
+        o = mm(back, slot_ref[q * 256 : q * 256 + 256]).astype(BF)
+        down_ref[:, q * 4 : q * 4 + 4] = o.reshape(SLOTS, 4, cols // 2, CH)
     copy.wait()
 
 
-def scatter_kernel(keep_a, got_a, keep_b, got_b, *outs):
-    _, p = place_bits()
+def plane_send_kernel(keep_a, got_a, keep_b, got_b, *outs):
+    _, p, _ = place_bits()
     n = keep_a.shape[1]
     for r, out in enumerate(outs):
-        c = p ^ r
-        out[:n] = (keep_a[c].astype(F32) + got_a[c].astype(F32)).astype(BF)
-        out[n:] = (keep_b[c].astype(F32) + got_b[c].astype(F32)).astype(BF)
-
-
-def sum_kernel(*refs):
-    total = refs[0][...].astype(F32)
-    for ref in refs[1:8]:
-        total = total + ref[...].astype(F32)
-    refs[-1][...] = total.astype(BF)
-
-
-def gather_kernel(*refs):
-    _, p = place_bits()
-    for r in range(8):
-        refs[-1][p ^ r] = refs[r][...]
+        at = pl.ds((p ^ r) * 4, 4)
+        out[:, :n] = (keep_a[at].astype(F32) + got_a[at].astype(F32)).astype(BF)
+        out[:, n:] = (keep_b[at].astype(F32) + got_b[at].astype(F32)).astype(BF)
+
+
+def line_send_kernel(a_ref, b_ref, c_ref, d_ref, *rest):
+    outs = rest[-4:]
+    _, _, z = place_bits()
+    for r in range(4):
+        parts = [ref[z ^ r].astype(F32) for ref in (a_ref, b_ref, c_ref, d_ref)]
+        outs[r][...] = (parts[0] + parts[1] + parts[2] + parts[3]).astype(BF)
+
+
+def line_sum_kernel(a_ref, b_ref, c_ref, d_ref, out_ref):
+    parts = [ref[...].astype(F32) for ref in (a_ref, b_ref, c_ref, d_ref)]
+    out_ref[...] = (parts[0] + parts[1] + parts[2] + parts[3]).astype(BF)
+
+
+def line_gather_kernel(a_ref, b_ref, c_ref, d_ref, out_ref):
+    _, _, z = place_bits()
+    for r, ref in enumerate((a_ref, b_ref, c_ref, d_ref)):
+        out_ref[z ^ r] = ref[...]
 
 
 def add_kernel(a_ref, b_ref, out_ref):
@@ -344,21 +351,27 @@
     pass
 
 
-def finish_kernel(own, half_ref, *rest):
-    buf, sems = rest[-2:]
-    outs = rest[-5:-2]
-    core, _ = place_bits()
-    at = pl.multiple_of((core if own else 1 - core) * (CH // 2), CH // 2)
+def finish_kernel(which, *refs):
+    buf, sems = refs[-2:]
+    outs, token_ref = refs[-6:-3], refs[-3]
+    token_ref[...] = jnp.zeros_like(token_ref)
+    core, p, _ = place_bits()
     copies = []
-    k = 0
-    for out in outs:
-        for m in range(out.shape[0]):
-            buf[k] = half_ref[:, k].reshape(CH, CH // 2).astype(F32)
-            copies.append(
-                pltpu.make_async_copy(buf.at[k], out.at[m, :, pl.ds(at, CH // 2)], sems.at[k])
+    for f, (ref, (sibling, r)) in enumerate(zip(refs, which)):
+        rows = pl.ds(pl.multiple_of((p ^ r) * 64, 64), 64)
+        cols = (1 - core if sibling else core) * (CH // 2)
+        cols = pl.ds(pl.multiple_of(cols, CH // 2), CH // 2)
+        m = 0
+        for o, out in enumerate(outs):
+            n = out.shape[0]
+            for k in range(n):
+                buf[f, m + k] = ref[:, m + k].reshape(64, CH // 2).astype(F32)
+            copy = pltpu.make_async_copy(
+                buf.at[f, pl.ds(m, n)], out.at[:, rows, cols], sems.at[f, o]
             )
-            copies[-1].start()
-            k += 1
+            copy.start()
+            copies.append(copy)
+            m += n
     for copy in copies:
         copy.wait()
 
@@ -392,8 +405,8 @@
 
 def plan(tm, grp):
     low, total = grp.bit_length() - 1, (tm * grp).bit_length() - 1
-    eight = [low + 1, 0, low + 2]
-    return low, eight, [b for b in range(total) if b != low and b not in eight]
+    plane, line = [low + 1, 0], [low + 2, low + 3]
+    return low, plane, line, [b for b in range(total) if b not in [low] + plane + line]
 
 
 def swap(value, tm, grp, *bits):
@@ -405,10 +418,12 @@
     return swap(value, tm, grp, plan(tm, grp)[0])
 
 
-def eight_round(parts, tm, grp):
-    bits = plan(tm, grp)[1]
-    return parts[:1] + [
-        swap(parts[r], tm, grp, *(b for i, b in enumerate(bits) if r >> i & 1)) for r in range(1, 8)
+def four_round(parts, bits, tm, grp):
+    return [
+        parts[0],
+        swap(parts[1], tm, grp, bits[0]),
+        swap(parts[2], tm, grp, bits[1]),
+        swap(parts[3], tm, grp, *bits),
     ]
 
 
@@ -417,18 +432,17 @@
     return call(pass_kernel, "pass", ins, [(ANY, value.shape)], alias={0: 0})[0]
 
 
-def finish(own, half, before):
-    n = half.shape[1]
-    return list(
-        call(
-            functools.partial(finish_kernel, own),
-            "finish",
-            [(VMEM, half)] + [(HBM, a) for a in before],
-            [(HBM, (m, CH, CH), F32) for m in (9, 3, 4)],
-            [pltpu.VMEM((n, CH, CH // 2), F32), pltpu.SemaphoreType.DMA((n,))],
-            alias={1 + i: i for i in range(len(before))},
-        )
-    )
+def finish(blocks, before, after):
+    n = blocks[0][0].shape[1]
+    *outs, token = call(
+        functools.partial(finish_kernel, [b[1:] for b in blocks]),
+        "finish",
+        [(VMEM, b[0]) for b in blocks] + [(HBM, a) for a in before] + [(ANY, a) for a in after],
+        [(HBM, (m, CH, CH), F32) for m in (9, 3, 4)] + [TOKEN],
+        [pltpu.VMEM((len(blocks), n, 64, CH // 2), F32), pltpu.SemaphoreType.DMA((len(blocks), 3))],
+        alias={len(blocks) + i: i for i in range(len(before))},
+    )
+    return outs, token
 
 
 def along(value, axis, by):
@@ -471,7 +485,7 @@
         acts_kernel,
         "acts",
         [count, (VMEM, x), (ANY, token)],
-        [(VMEM, tile), (VMEM, padded), (VMEM, (ch, (rows + 2) * 128))],
+        [(VMEM, tile), (VMEM, padded), (VMEM, (3 * ch, (rows + 4) * 128))],
         flops=2 * tap,
     )
     acts, sp, last_two = call(
@@ -483,7 +497,7 @@
         alias={3: 0},
     )
     prev = along(last_two, "tm", 1)
-    half = (8, 9, 32, ch // 2)
+    half = (16, 9, 16, ch // 2)
     at, cott, gy, gs, keep_a, send_a, *edge = call(
         functools.partial(grad_spatial_kernel, grp),
         "grad_spatial",
@@ -495,53 +509,63 @@
         flops=14 * tap,
         alias={1: 0},
     )
-    got_a = core_round(passed(send_a, [prev]), tm, grp)
+    send_a = passed(send_a, [prev])
+    got_a = core_round(send_a, tm, grp)
     cot_top, cot_bot = from_bands(edge)
-    half = (8, 7, 32, ch // 2)
+    half = (16, 7, 16, ch // 2)
     down, keep_b, send_b = call(
         forward_kernel,
         "forward",
-        [count, (VMEM, xt), (VMEM, sp), (VMEM, prev), (VMEM, cott), (VMEM, gy), (VMEM, wt), (VMEM, wd)]
-        + [(ANY, send_a)],
-        [(VMEM, cotangent.shape), (VMEM, half), (VMEM, half)],
-        [pltpu.VMEM(s, BF) for s in (tile, (ch, slots * wide), tile, tile, tile)],
+        [count, (VMEM, xt), (VMEM, sp), (VMEM, prev), (VMEM, cott), (VMEM, gy), (VMEM, wt), (VMEM, wd),
+         (ANY, send_a)],
+        [(VMEM, (slots * wide // 4, ch)), (VMEM, half), (VMEM, half)],
+        [pltpu.VMEM(v, BF) for v in (tile, (3 * ch, slots * wide), (4 * ch, slots * wide // 4))],
         flops=10 * tap,
-    )
-    def grad_x_part(part, halo, before, after):
-        return call(
-            functools.partial(grad_x_kernel, part, grp),
-            "grad_x",
-            [count, (VMEM, xt), (VMEM, gy), (VMEM, gs), (VMEM, halo), (VMEM, wt), (VMEM, wd), (VMEM, ws)]
-            + [(HBM, a) for a in before] + [(ANY, a) for a in after],
-            [(HBM, (slots, wide, ch)), TOKEN],
-            [pltpu.VMEM((rows // 2 + 2, cols + 2, slots, ch), BF),
-             pltpu.VMEM((slots, wide // 2, ch), BF), dma((1,))],
-            flops=5 * tap,
-            alias={8: 0} if before else None,
-        )
-
-    send_b = passed(send_b, [got_a])
+        grant=14,
+    )
+    send_b = passed(send_b, [got_a, cot_top, cot_bot][: 1 + sides])
     got_b = core_round(send_b, tm, grp)
+    _, plane, line, others = plan(tm, grp)
     parts = call(
-        scatter_kernel,
-        "scatter",
+        plane_send_kernel,
+        "plane_send",
         [(VMEM, a) for a in (keep_a, got_a, keep_b, got_b)],
-        [(VMEM, (16, 32, ch // 2))] * 8,
-    )
-    grad_x, token = grad_x_part(0, cot_top, [], [parts[7]])
-    parts = eight_round(list(parts), tm, grp)
-    ins = [(VMEM, a) for a in parts] + [(ANY, token)]
-    (mine,) = call(sum_kernel, "sum", ins, [(VMEM, parts[0].shape)])
-    for bit in plan(tm, grp)[2]:
+        [(VMEM, (4, 16, 16, ch // 2))] * 4,
+    )
+    grad_x, down, token = call(
+        functools.partial(grad_x_kernel, grp),
+        "grad_x",
+        [count, (VMEM, xt), (VMEM, gy), (VMEM, gs), (VMEM, cot_top), (VMEM, cot_bot), (VMEM, wt),
+         (VMEM, wd), (VMEM, ws), (VMEM, down), (ANY, parts[3])],
+        [(HBM, (slots, wide, ch)), (VMEM, cotangent.shape), TOKEN],
+        [pltpu.VMEM(padded, BF), pltpu.VMEM((slots, wide, ch), BF), dma((1,))],
+        flops=10 * tap,
+    )
+    parts = four_round(list(parts), plane, tm, grp)
+    parts = call(
+        line_send_kernel,
+        "line_send",
+        [(VMEM, a) for a in parts] + [(ANY, token)],
+        [(VMEM, (16, 16, ch // 2))] * 4,
+    )
+    parts = four_round(list(parts), line, tm, grp)
+    (mine,) = call(line_sum_kernel, "line_sum", [(VMEM, a) for a in parts], [(VMEM, parts[0].shape)])
+    for bit in others:
         got = swap(mine, tm, grp, bit)
         (mine,) = call(add_kernel, "add", [(VMEM, mine), (VMEM, got)], [(VMEM, mine.shape)])
-    parts = eight_round([mine] * 8, tm, grp)
-    grad_x, token = grad_x_part(1, cot_bot, [grad_x], [mine])
-    ins = [(VMEM, a) for a in parts] + [(ANY, token)]
-    (mine,) = call(gather_kernel, "gather", ins, [(VMEM, (8,) + mine.shape)])
-    got = core_round(mine, tm, grp)
-    outs = finish(True, mine, [])
-    sum_s, sum_t, sum_d = finish(False, got, outs)
+    parts = four_round([mine] * 4, line, tm, grp)
+    (mine,) = call(
+        line_gather_kernel, "line_gather", [(VMEM, a) for a in parts], [(VMEM, (4,) + mine.shape)]
+    )
+    parts = four_round([mine] * 4, plane, tm, grp)
+    side = core_round(mine, tm, grp)
+    outs, token = finish([(mine, False, 0), (side, True, 0)], [], [])
+    parts[1] = passed(parts[1], [token])
+    sides = [side] + [core_round(part, tm, grp) for part in parts[1:]]
+    blocks = [(parts[r], False, r) for r in (1, 2, 3)] + [(sides[r], True, r) for r in (1, 2)]
+    outs, _ = finish(blocks, outs, [])
+    outs, _ = finish([(sides[3], True, 3)], outs, [])
+    sum_s, sum_t, sum_d = outs
     return (
         down,
         grad_x.reshape(frames_in.shape),

time: 84.7 us -> 85.8 us (1.013)
  waiting for transfers between devices: 19.1 us -> 27.5 us
  starting transfers between devices: 32.5 us -> 25.8 us
    ppermute x18, waiting for transfers between devices: 13.7 us -> 27.5 us  [swap(): return lax.ppermute(value, AXES, [(d, d ^ flip) for d in range(tm * grp)])]
    ppermute x18, starting transfers between devices: 23.7 us -> 17.9 us  [swap(): return lax.ppermute(value, AXES, [(d, d ^ flip) for d in range(tm * grp)])]
    ppermute x2, waiting for transfers between devices: 5.36 us -> 0.01 us  [from_bands(): got = lax.ppermute(parts[0], 'grp', [(0, 1), (1, 0)])]
    ppermute x2, starting transfers between devices: 4.54 us -> 3.53 us  [from_bands(): got = lax.ppermute(parts[0], 'grp', [(0, 1), (1, 0)])]
    pallas_call x15 -> x16, Pallas kernels: 29.1 us -> 28.6 us  [call(): pl.pallas_call(kernel, out_shape=shapes, in_specs=[s for s, _ in ins], ou...]
  transfers between devices with their start and end apart: 22 -> 22, of which waited for: 8 -> 10; matrix products, arithmetic and copies ran while one was open for 0% -> 0% of each run, Pallas kernels for 25% -> 31%
where the time goes in v7:
time: 85.8 us; the launch traced here: 85.6 us
  Pallas kernels  28.6 us (33%)
  waiting for transfers between devices  27.5 us (32%)
  starting transfers between devices  25.8 us (30%)
  local copies, waits for them, and re-layouts  2.19 us (3%)
  between operations  1.53 us (2%)
    pallas_call x16, Pallas kernels, call(): pl.pallas_call(kernel, out_shape=shapes, in_specs=[s for s, _ in ins], ou...  28.6 us
    ppermute x18, waiting for transfers between devices, swap(): return lax.ppermute(value, AXES, [(d, d ^ flip) for d in range(tm * grp)])  27.5 us
    ppermute x18, starting transfers between devices, swap(): return lax.ppermute(value, AXES, [(d, d ^ flip) for d in range(tm * grp)])  17.9 us
    ppermute x2, starting transfers between devices, along(): return lax.ppermute(value, axis, pairs)  4.33 us
    ppermute x2, starting transfers between devices, from_bands(): got = lax.ppermute(parts[0], 'grp', [(0, 1), (1, 0)])  3.53 us
    unnamed x12, local copies, waits for them, and re-layouts  2.19 us
  transfers between devices with their start and end apart: 22, of which 10 were waited for; matrix products, arithmetic and copies ran while one was open for 0% of the time, Pallas kernels for 31%

profile of v7, /device:TPU:0, one launch (start us, length us, event | category | flops | bytes accessed | tf_op | source)
XLA Modules:
  0.0 85.6 jit_solution(4110505926092487113)
XLA Ops:
  1.3 1.2 %copy-done = bf16[16,16,8,256]{3,2,1,0:T(8,128)(2,1)S(1)} copy-done((bf16[16,16,8,256]{3,2,1,0:T(8,128)(2,1)S(1)}, bf16[16,16,8,256]{3,2,1,0:T(8,128)(2,1)}, u32[]{:S(2)}) %copy-start) | copy-done | bytes 1048600
  2.5 0.9 %copy-done.1 = bf16[16,8,4,256]{3,2,1,0:T(4,128)(2,1)S(1)} copy-done((bf16[16,8,4,256]{3,2,1,0:T(4,128)(2,1)S(1)}, bf16[16,8,4,256]{3,2,1,0:T(4,128)(2,1)}, u32[]{:S(2)}) %copy-start.1) | copy-done | bytes 262168
  3.5 0.3 edges.1
  3.8 3.0 %collective-permute-start = (bf16[128,256]{1,0:T(8,128)(2,1)S(1)}, bf16[128,256]{1,0:T(8,128)(2,1)S(1)}, u32[]{:S(2)}, u32[]{:S(2)}) collective-permute-start(bf16[128,256]{1,0:T(8,128)(2,1)S(1)} %get-tuple-element.46), channel_id=1, source_target_pairs={{0,1},{1,0},{2,3},{3,2},{4,5},{5,4},{6,7},{7,6},{8,9},{9,8},{10,11... | collective-permute-start | bytes 196616 | tf_op jit(solution)/shard_map/ppermute | solution.py:456
  6.8 1.3 %collective-permute-start.1 = (bf16[2,8,4,256]{3,2,1,0:T(4,128)(2,1)S(1)}, bf16[2,8,4,256]{3,2,1,0:T(4,128)(2,1)S(1)}, u32[]{:S(2)}, u32[]{:S(2)}) collective-permute-start(bf16[2,8,4,256]{3,2,1,0:T(4,128)(2,1)S(1)} %get-tuple-element.47), channel_id=1, source_target_pairs={{2,0},{4,2},{6,4},{8,6},{10,8},{12,10},{14,12},{16,14},{18,16},{20... | collective-permute-start | bytes 98312 | tf_op jit(solution)/shard_map/ppermute | solution.py:451
  8.1 3.2 %acts.1 = (bf16[16,8,16,256]{3,2,1,0:T(8,128)(2,1)S(1)}, bf16[18,10,16,256]{3,2,1,0:T(8,128)(2,1)S(1)}, bf16[768,2560]{1,0:T(8,128)(2,1)S(1)}) custom-call(s32[1]{0:T(128)S(6)} %copy.33.count_ref, bf16[16,128,256]{2,1,0:T(8,128)(2,1)S(1)} %bitcast.7, f32[8,128]{1,0:T(8,128)S(1)} %get-tuple-element.43._), custom_call_target="tpu_custom_call" | custom-call | flops 536870912 | bytes 7503876 | tf_op jit(solution)/shard_map/acts/pallas_call | solution.py:390
  11.3 0.0 copy-start.2
  11.4 0.0 copy-start.4
  11.4 0.0 copy-start.5
  11.4 3.7 %spatial.1 = (bf16[18,10,16,256]{3,2,1,0:T(8,128)(2,1)S(1)}, bf16[16,8,16,256]{3,2,1,0:T(8,128)(2,1)S(1)}, bf16[8,32,256]{2,1,0:T(8,128)(2,1)S(1)}) custom-call(s32[1]{0:T(128)S(6)} %copy.33.count_ref, bf16[128,256]{1,0:T(8,128)(2,1)S(1)} %collective-permute-done.top_ref.bot_ref, ...), custom_call_target="tpu_custom_call", output_to_operand_aliasing={{0}: (3, {})} | custom-call | flops 2415919104 | bytes 5439492 | tf_op jit(solution)/shard_map/spatial/pallas_call | solution.py:390
  15.1 3.0 %collective-permute-start.3 = (bf16[8,32,256]{2,1,0:T(8,128)(2,1)S(1)}, bf16[8,32,256]{2,1,0:T(8,128)(2,1)S(1)}, u32[]{:S(2)}, u32[]{:S(2)}) collective-permute-start(bf16[8,32,256]{2,1,0:T(8,128)(2,1)S(1)} %get-tuple-element.49._), channel_id=1, source_target_pairs={{0,2},{2,4},{4,6},{6,8},{8,10},{10,12},{12,14},{14,16},{16,18},{18... | collective-permute-start | bytes 393224 | tf_op jit(solution)/shard_map/ppermute | solution.py:451
  18.2 0.0 collective-permute-done.1.nxt_ref
  18.2 5.0 %grad_spatial.1 = (bf16[768,2560]{1,0:T(8,128)(2,1)S(1)}, bf16[8,4,16,256]{3,2,1,0:T(8,128)(2,1)S(1)}, bf16[16,8,16,256]{3,2,1,0:T(8,128)(2,1)S(1)}, bf16[16,10,...) custom-call(s32[1]{0:T(128)S(6)} %copy.33.count_ref, ...), custom_call_target="tpu_custom_call", output_to_operand_aliasing={{0}: (1, {})} | custom-call | flops 3758096384 | bytes 13041668 | tf_op jit(solution)/shard_map/grad_spatial/pallas_call | solution.py:390
  23.2 1.1 %collective-permute-start.4 = (bf16[16,9,16,128]{3,2,1,0:T(8,128)(2,1)S(1)}, bf16[16,9,16,128]{3,2,1,0:T(8,128)(2,1)S(1)}, u32[]{:S(2)}, u32[]{:S(2)}) collective-permute-start(bf16[16,9,16,128]{3,2,1,0:T(8,128)(2,1)S(1)} %pass.3.rest_0_), channel_id=1, source_target_pairs={{0,2},{1,3},{2,0},{3,1},{4,6},{5,7},{6,4},{7,5},{8,10},{9,11},{10,... | collective-permute-start | bytes 1769480 | tf_op jit(solution)/shard_map/ppermute | solution.py:414
  24.4 0.5 collective-permute-start.2
  24.9 3.8 %forward.1 = (bf16[512,256]{1,0:T(8,128)(2,1)S(1)}, bf16[16,7,16,128]{3,2,1,0:T(8,128)(2,1)S(1)}, bf16[16,7,16,128]{3,2,1,0:T(8,128)(2,1)S(1)}) custom-call(s32[1]{0:T(128)S(6)} %copy.33.count_ref, bf16[16,8,16,256]{3,2,1,0:T(8,128)(2,1)S(1)} %get-tuple-element.44.xt_ref, bf16[16,8,16,256]{3,2,1,0:T(8,128)(2,1)S(1)} %get-tuple-element.53.sp_ref, ...), custom_call_target="tpu_custom_call" | custom-call | flops 2684354560 | bytes 5636100 | tf_op jit(solution)/shard_map/forward/pallas_call | solution.py:390
  28.7 0.0 collective-permute-done.4.__1_.got_a
  28.7 0.1 collective-permute-start.5
  28.8 1.8 %collective-permute-done.5.got_b = bf16[16,7,16,128]{3,2,1,0:T(8,128)(2,1)S(1)} collective-permute-done((bf16[16,7,16,128]{3,2,1,0:T(8,128)(2,1)S(1)}, bf16[16,7,16,128]{3,2,1,0:T(8,128)(2,1)S(1)}, u32[]{:S(2)}, u32[]{:S(2)}) %collective-permute-start.5) | collective-permute-done | bytes 458784 | tf_op jit(solution)/shard_map/ppermute | solution.py:414
  30.6 0.2 plane_send.1
  30.8 2.1 %collective-permute-start.6 = (bf16[4,16,16,128]{3,2,1,0:T(8,128)(2,1)S(1)}, bf16[4,16,16,128]{3,2,1,0:T(8,128)(2,1)S(1)}, u32[]{:S(2)}, u32[]{:S(2)}) collective-permute-start(bf16[4,16,16,128]{3,2,1,0:T(8,128)(2,1)S(1)} %get-tuple-element.64), channel_id=1, source_target_pairs={{0,4},{1,5},{2,6},{3,7},{4,0},{5,1},{6,2},{7,3},{8,12},{9,13},{10,... | collective-permute-start | bytes 786440 | tf_op jit(solution)/shard_map/ppermute | solution.py:414
  33.0 1.5 %collective-permute-start.7 = (bf16[4,16,16,128]{3,2,1,0:T(8,128)(2,1)S(1)}, bf16[4,16,16,128]{3,2,1,0:T(8,128)(2,1)S(1)}, u32[]{:S(2)}, u32[]{:S(2)}) collective-permute-start(bf16[4,16,16,128]{3,2,1,0:T(8,128)(2,1)S(1)} %get-tuple-element.65), channel_id=1, source_target_pairs={{0,1},{1,0},{2,3},{3,2},{4,5},{5,4},{6,7},{7,6},{8,9},{9,8},{10,11... | collective-permute-start | bytes 786440 | tf_op jit(solution)/shard_map/ppermute | solution.py:414
  34.5 0.0 collective-permute-start.8
  34.5 7.4 %grad_x.1 = (bf16[16,128,256]{2,1,0:T(8,128)(2,1)}, bf16[16,8,4,256]{3,2,1,0:T(4,128)(2,1)}, f32[8,128]{1,0:T(8,128)S(1)}) custom-call(s32[1]{0:T(128)S(6)} %copy.33.count_ref, bf16[16,8,16,256]{3,2,1,0:T(8,128)(2,1)S(1)} %get-tuple-element.44.xt_ref, bf16[16,8,16,256]{3,2,1,0:T(8,128)(2,1)S(1)} %get-tuple-element.50.gy_ref, ...), custom_call_target="tpu_custom_call" | custom-call | flops 2684354560 | bytes 7147524 | tf_op jit(solution)/shard_map/grad_x/pallas_call | solution.py:390
  42.0 4.7 %collective-permute-done.7.c_ref = bf16[4,16,16,128]{3,2,1,0:T(8,128)(2,1)S(1)} collective-permute-done((bf16[4,16,16,128]{3,2,1,0:T(8,128)(2,1)S(1)}, bf16[4,16,16,128]{3,2,1,0:T(8,128)(2,1)S(1)}, u32[]{:S(2)}, u32[]{:S(2)}) %collective-permute-start.7) | collective-permute-done | bytes 262176 | tf_op jit(solution)/shard_map/ppermute | solution.py:414
  46.7 0.1 line_send.1
  46.8 1.7 %collective-permute-start.9 = (bf16[16,16,128]{2,1,0:T(8,128)(2,1)S(1)}, bf16[16,16,128]{2,1,0:T(8,128)(2,1)S(1)}, u32[]{:S(2)}, u32[]{:S(2)}) collective-permute-start(bf16[16,16,128]{2,1,0:T(8,128)(2,1)S(1)} %get-tuple-element.68), channel_id=1, source_target_pairs={{0,8},{1,9},{2,10},{3,11},{4,12},{5,13},{6,14},{7,15},{8,0},{9,1},... | collective-permute-start | bytes 196616 | tf_op jit(solution)/shard_map/ppermute | solution.py:414
  48.5 1.7 %collective-permute-start.10 = (bf16[16,16,128]{2,1,0:T(8,128)(2,1)S(1)}, bf16[16,16,128]{2,1,0:T(8,128)(2,1)S(1)}, u32[]{:S(2)}, u32[]{:S(2)}) collective-permute-start(bf16[16,16,128]{2,1,0:T(8,128)(2,1)S(1)} %get-tuple-element.69), channel_id=1, source_target_pairs={{0,16},{1,17},{2,18},{3,19},{4,20},{5,21},{6,22},{7,23},{8,24},{9,... | collective-permute-start | bytes 196616 | tf_op jit(solution)/shard_map/ppermute | solution.py:414
  50.2 1.1 %collective-permute-start.11 = (bf16[16,16,128]{2,1,0:T(8,128)(2,1)S(1)}, bf16[16,16,128]{2,1,0:T(8,128)(2,1)S(1)}, u32[]{:S(2)}, u32[]{:S(2)}) collective-permute-start(bf16[16,16,128]{2,1,0:T(8,128)(2,1)S(1)} %get-tuple-element.70), channel_id=1, source_target_pairs={{0,24},{1,25},{2,26},{3,27},{4,28},{5,29},{6,30},{7,31},{8,16},{9,... | collective-permute-start | bytes 196616 | tf_op jit(solution)/shard_map/ppermute | solution.py:414
  51.3 0.5 collective-permute-done.9.b_ref
  51.8 3.3 %collective-permute-done.10.c_ref = bf16[16,16,128]{2,1,0:T(8,128)(2,1)S(1)} collective-permute-done((bf16[16,16,128]{2,1,0:T(8,128)(2,1)S(1)}, bf16[16,16,128]{2,1,0:T(8,128)(2,1)S(1)}, u32[]{:S(2)}, u32[]{:S(2)}) %collective-permute-start.10) | collective-permute-done | bytes 65568 | tf_op jit(solution)/shard_map/ppermute | solution.py:414
  55.0 1.3 %collective-permute-done.11.d_ref = bf16[16,16,128]{2,1,0:T(8,128)(2,1)S(1)} collective-permute-done((bf16[16,16,128]{2,1,0:T(8,128)(2,1)S(1)}, bf16[16,16,128]{2,1,0:T(8,128)(2,1)S(1)}, u32[]{:S(2)}, u32[]{:S(2)}) %collective-permute-start.11) | collective-permute-done | bytes 65568 | tf_op jit(solution)/shard_map/ppermute | solution.py:414
  56.4 0.7 collective-permute-start.12
  57.1 1.8 %collective-permute-start.13 = (bf16[16,16,128]{2,1,0:T(8,128)(2,1)S(1)}, bf16[16,16,128]{2,1,0:T(8,128)(2,1)S(1)}, u32[]{:S(2)}, u32[]{:S(2)}) collective-permute-start(bf16[16,16,128]{2,1,0:T(8,128)(2,1)S(1)} %line_sum.1.a_ref), channel_id=1, source_target_pairs={{0,16},{1,17},{2,18},{3,19},{4,20},{5,21},{6,22},{7,23},{8,24},{9,... | collective-permute-start | bytes 196616 | tf_op jit(solution)/shard_map/ppermute | solution.py:414
  58.9 2.0 %collective-permute-start.14 = (bf16[16,16,128]{2,1,0:T(8,128)(2,1)S(1)}, bf16[16,16,128]{2,1,0:T(8,128)(2,1)S(1)}, u32[]{:S(2)}, u32[]{:S(2)}) collective-permute-start(bf16[16,16,128]{2,1,0:T(8,128)(2,1)S(1)} %line_sum.1.a_ref), channel_id=1, source_target_pairs={{0,24},{1,25},{2,26},{3,27},{4,28},{5,29},{6,30},{7,31},{8,16},{9,... | collective-permute-start | bytes 196616 | tf_op jit(solution)/shard_map/ppermute | solution.py:414
  60.9 2.5 %collective-permute-done.13.c_ref = bf16[16,16,128]{2,1,0:T(8,128)(2,1)S(1)} collective-permute-done((bf16[16,16,128]{2,1,0:T(8,128)(2,1)S(1)}, bf16[16,16,128]{2,1,0:T(8,128)(2,1)S(1)}, u32[]{:S(2)}, u32[]{:S(2)}) %collective-permute-start.13) | collective-permute-done | bytes 65568 | tf_op jit(solution)/shard_map/ppermute | solution.py:414
  63.4 1.6 %collective-permute-done.14.d_ref = bf16[16,16,128]{2,1,0:T(8,128)(2,1)S(1)} collective-permute-done((bf16[16,16,128]{2,1,0:T(8,128)(2,1)S(1)}, bf16[16,16,128]{2,1,0:T(8,128)(2,1)S(1)}, u32[]{:S(2)}, u32[]{:S(2)}) %collective-permute-start.14) | collective-permute-done | bytes 65568 | tf_op jit(solution)/shard_map/ppermute | solution.py:414
  65.0 0.1 collective-permute-start.18
  65.1 1.3 %collective-permute-start.17 = (bf16[4,16,16,128]{3,2,1,0:T(8,128)(2,1)S(1)}, bf16[4,16,16,128]{3,2,1,0:T(8,128)(2,1)S(1)}, u32[]{:S(2)}, u32[]{:S(2)}) collective-permute-start(bf16[4,16,16,128]{3,2,1,0:T(8,128)(2,1)S(1)} %line_gather.1.refs_0_), channel_id=1, source_target_pairs={{0,4},{1,5},{2,6},{3,7},{4,0},{5,1},{6,2},{7,3},{8,12},{9,13},{10,... | collective-permute-start | bytes 786440 | tf_op jit(solution)/shard_map/ppermute | solution.py:414
  66.4 0.7 collective-permute-start.19
  67.1 1.6 %collective-permute-start.15 = (bf16[4,16,16,128]{3,2,1,0:T(8,128)(2,1)S(1)}, bf16[4,16,16,128]{3,2,1,0:T(8,128)(2,1)S(1)}, u32[]{:S(2)}, u32[]{:S(2)}) collective-permute-start(bf16[4,16,16,128]{3,2,1,0:T(8,128)(2,1)S(1)} %line_gather.1.refs_0_), channel_id=1, source_target_pairs={{0,5},{1,4},{2,7},{3,6},{4,1},{5,0},{6,3},{7,2},{8,13},{9,12},{10,... | collective-permute-start | bytes 786440 | tf_op jit(solution)/shard_map/ppermute | solution.py:414
  68.6 1.0 %finish.3 = (f32[9,256,256]{2,1,0:T(8,128)}, f32[3,256,256]{2,1,0:T(8,128)}, f32[4,256,256]{2,1,0:T(8,128)}, f32[8,128]{1,0:T(8,128)S(1)}) custom-call(bf16[4,16,16,128]{3,2,1,0:T(8,128)(2,1)S(1)} %line_gather.1.refs_0_, bf16[4,16,16,128]{3,2,1,0:T(8,128)(2,1)S(1)} %collective-permute-done.18.refs_1_), custom_call_target="tpu_custom_call" | custom-call | bytes 4722688 | tf_op jit(solution)/shard_map/finish/pallas_call | solution.py:390
  69.7 4.6 %collective-permute-done.17.__0_ = bf16[4,16,16,128]{3,2,1,0:T(8,128)(2,1)S(1)} collective-permute-done((bf16[4,16,16,128]{3,2,1,0:T(8,128)(2,1)S(1)}, bf16[4,16,16,128]{3,2,1,0:T(8,128)(2,1)S(1)}, u32[]{:S(2)}, u32[]{:S(2)}) %collective-permute-start.17) | collective-permute-done | bytes 262176 | tf_op jit(solution)/shard_map/ppermute | solution.py:414
  74.2 6.2 %collective-permute-done.19.refs_1_ = bf16[4,16,16,128]{3,2,1,0:T(8,128)(2,1)S(1)} collective-permute-done((bf16[4,16,16,128]{3,2,1,0:T(8,128)(2,1)S(1)}, bf16[4,16,16,128]{3,2,1,0:T(8,128)(2,1)S(1)}, u32[]{:S(2)}, u32[]{:S(2)}) %collective-permute-start.19) | collective-permute-done | bytes 262176 | tf_op jit(solution)/shard_map/ppermute | solution.py:414
  80.4 0.5 collective-permute-start.16
  80.9 1.0 %collective-permute-done.21.refs_4_ = bf16[4,16,16,128]{3,2,1,0:T(8,128)(2,1)S(1)} collective-permute-done((bf16[4,16,16,128]{3,2,1,0:T(8,128)(2,1)S(1)}, bf16[4,16,16,128]{3,2,1,0:T(8,128)(2,1)S(1)}, u32[]{:S(2)}, u32[]{:S(2)}) %collective-permute-start.21) | collective-permute-done | bytes 262176 | tf_op jit(solution)/shard_map/ppermute | solution.py:414
  81.9 2.2 %finish.4 = (f32[9,256,256]{2,1,0:T(8,128)}, f32[3,256,256]{2,1,0:T(8,128)}, f32[4,256,256]{2,1,0:T(8,128)}, f32[8,128]{1,0:T(8,128)}) custom-call(bf16[4,16,16,128]{3,2,1,0:T(8,128)(2,1)S(1)} %pass.5.refs_0_, bf16[4,16,16,128]{3,2,1,0:T(8,128)(2,1)S(1)} %collective-permute-done.19.refs_1_, ...), custom_call_target="tpu_custom_call", output_to_operand_aliasing={{0}: (5, {}), {1}: (6, {}), {2}: (7, {})} | custom-call | bytes 9703424 | tf_op jit(solution)/shard_map/finish/pallas_call | solution.py:390
  84.2 1.4 %finish.5 = (f32[9,256,256]{2,1,0:T(8,128)}, f32[3,256,256]{2,1,0:T(8,128)}, f32[4,256,256]{2,1,0:T(8,128)}, f32[8,128]{1,0:T(8,128)}) custom-call(bf16[4,16,16,128]{3,2,1,0:T(8,128)(2,1)S(1)} %collective-permute-done.16.refs_0_, f32[9,256,256]{2,1,0:T(8,128)} %get-tuple-element.75.refs_1_, ...), custom_call_target="tpu_custom_call", output_to_operand_aliasing={{0}: (1, {}), {1}: (2, {}), {2}: (3, {})} | custom-call | bytes 8654848 | tf_op jit(solution)/shard_map/finish/pallas_call | solution.py:390
  (24 shorter events, 0.1 us)
Async XLA Ops:
  1.3 1.2 %copy-start = (bf16[16,16,8,256]{3,2,1,0:T(8,128)(2,1)S(1)}, bf16[16,16,8,256]{3,2,1,0:T(8,128)(2,1)}, u32[]{:S(2)}) copy-start(bf16[16,16,8,256]{3,2,1,0:T(8,128)(2,1)} %param.6) | copy-start | bytes 3145732
  2.5 0.9 %copy-start.1 = (bf16[16,8,4,256]{3,2,1,0:T(4,128)(2,1)S(1)}, bf16[16,8,4,256]{3,2,1,0:T(4,128)(2,1)}, u32[]{:S(2)}) copy-start(bf16[16,8,4,256]{3,2,1,0:T(4,128)(2,1)} %cot_ref.3) | copy-start | bytes 786436
  3.5 7.9 %copy-start.3 = (bf16[3,3,256,256]{3,2,1,0:T(8,128)(2,1)S(1)}, bf16[3,3,256,256]{3,2,1,0:T(8,128)(2,1)}, u32[]{:S(2)}) copy-start(bf16[3,3,256,256]{3,2,1,0:T(8,128)(2,1)} %param.8) | copy-start | bytes 3538948
  3.8 7.6 %collective-permute-start = (bf16[128,256]{1,0:T(8,128)(2,1)S(1)}, bf16[128,256]{1,0:T(8,128)(2,1)S(1)}, u32[]{:S(2)}, u32[]{:S(2)}) collective-permute-start(bf16[128,256]{1,0:T(8,128)(2,1)S(1)} %get-tuple-element.46), channel_id=1, source_target_pairs={{0,1},{1,0},{2,3},{3,2},{4,5},{5,4},{6,7},{7,6},{8,9},{9,8},{10,11... | collective-permute-start | bytes 196616 | tf_op jit(solution)/shard_map/ppermute | solution.py:456
  6.8 11.4 %collective-permute-start.1 = (bf16[2,8,4,256]{3,2,1,0:T(4,128)(2,1)S(1)}, bf16[2,8,4,256]{3,2,1,0:T(4,128)(2,1)S(1)}, u32[]{:S(2)}, u32[]{:S(2)}) collective-permute-start(bf16[2,8,4,256]{3,2,1,0:T(4,128)(2,1)S(1)} %get-tuple-element.47), channel_id=1, source_target_pairs={{2,0},{4,2},{6,4},{8,6},{10,8},{12,10},{14,12},{16,14},{18,16},{20... | collective-permute-start | bytes 98312 | tf_op jit(solution)/shard_map/ppermute | solution.py:451
  11.3 6.8 %copy-start.2 = (bf16[16,8,4,256]{3,2,1,0:T(4,128)(2,1)S(1)}, bf16[16,8,4,256]{3,2,1,0:T(4,128)(2,1)}, u32[]{:S(2)}) copy-start(bf16[16,8,4,256]{3,2,1,0:T(4,128)(2,1)} %cot_ref.3) | copy-start | bytes 786436
  11.4 6.8 %copy-start.4 = (bf16[2,2,256,256]{3,2,1,0:T(8,128)(2,1)S(1)}, bf16[2,2,256,256]{3,2,1,0:T(8,128)(2,1)}, u32[]{:S(2)}) copy-start(bf16[2,2,256,256]{3,2,1,0:T(8,128)(2,1)} %param.10) | copy-start | bytes 1572868
  11.4 6.8 %copy-start.5 = (bf16[3,256,256]{2,1,0:T(8,128)(2,1)S(1)}, bf16[3,256,256]{2,1,0:T(8,128)(2,1)}, u32[]{:S(2)}) copy-start(bf16[3,256,256]{2,1,0:T(8,128)(2,1)} %wt_ref.5) | copy-start | bytes 1179652
  15.1 8.1 %collective-permute-start.3 = (bf16[8,32,256]{2,1,0:T(8,128)(2,1)S(1)}, bf16[8,32,256]{2,1,0:T(8,128)(2,1)S(1)}, u32[]{:S(2)}, u32[]{:S(2)}) collective-permute-start(bf16[8,32,256]{2,1,0:T(8,128)(2,1)S(1)} %get-tuple-element.49._), channel_id=1, source_target_pairs={{0,2},{2,4},{4,6},{6,8},{8,10},{10,12},{12,14},{14,16},{16,18},{18... | collective-permute-start | bytes 393224 | tf_op jit(solution)/shard_map/ppermute | solution.py:451
  23.2 5.4 %collective-permute-start.4 = (bf16[16,9,16,128]{3,2,1,0:T(8,128)(2,1)S(1)}, bf16[16,9,16,128]{3,2,1,0:T(8,128)(2,1)S(1)}, u32[]{:S(2)}, u32[]{:S(2)}) collective-permute-start(bf16[16,9,16,128]{3,2,1,0:T(8,128)(2,1)S(1)} %pass.3.rest_0_), channel_id=1, source_target_pairs={{0,2},{1,3},{2,0},{3,1},{4,6},{5,7},{6,4},{7,5},{8,10},{9,11},{10,... | collective-permute-start | bytes 1769480 | tf_op jit(solution)/shard_map/ppermute | solution.py:414
  24.4 4.3 %collective-permute-start.2 = (bf16[64,256]{1,0:T(8,128)(2,1)S(1)}, bf16[64,256]{1,0:T(8,128)(2,1)S(1)}, u32[]{:S(2)}, u32[]{:S(2)}) collective-permute-start(bf16[64,256]{1,0:T(8,128)(2,1)S(1)} %get-tuple-element.52), channel_id=1, source_target_pairs={{0,1},{1,0},{2,3},{3,2},{4,5},{5,4},{6,7},{7,6},{8,9},{9,8},{10,11... | collective-permute-start | bytes 98312 | tf_op jit(solution)/shard_map/ppermute | solution.py:456
  28.7 1.9 %collective-permute-start.5 = (bf16[16,7,16,128]{3,2,1,0:T(8,128)(2,1)S(1)}, bf16[16,7,16,128]{3,2,1,0:T(8,128)(2,1)S(1)}, u32[]{:S(2)}, u32[]{:S(2)}) collective-permute-start(bf16[16,7,16,128]{3,2,1,0:T(8,128)(2,1)S(1)} %pass.4), channel_id=1, source_target_pairs={{0,2},{1,3},{2,0},{3,1},{4,6},{5,7},{6,4},{7,5},{8,10},{9,11},{10,... | collective-permute-start | bytes 1376264 | tf_op jit(solution)/shard_map/ppermute | solution.py:414
  30.8 11.1 %collective-permute-start.6 = (bf16[4,16,16,128]{3,2,1,0:T(8,128)(2,1)S(1)}, bf16[4,16,16,128]{3,2,1,0:T(8,128)(2,1)S(1)}, u32[]{:S(2)}, u32[]{:S(2)}) collective-permute-start(bf16[4,16,16,128]{3,2,1,0:T(8,128)(2,1)S(1)} %get-tuple-element.64), channel_id=1, source_target_pairs={{0,4},{1,5},{2,6},{3,7},{4,0},{5,1},{6,2},{7,3},{8,12},{9,13},{10,... | collective-permute-start | bytes 786440 | tf_op jit(solution)/shard_map/ppermute | solution.py:414
  33.0 13.7 %collective-permute-start.7 = (bf16[4,16,16,128]{3,2,1,0:T(8,128)(2,1)S(1)}, bf16[4,16,16,128]{3,2,1,0:T(8,128)(2,1)S(1)}, u32[]{:S(2)}, u32[]{:S(2)}) collective-permute-start(bf16[4,16,16,128]{3,2,1,0:T(8,128)(2,1)S(1)} %get-tuple-element.65), channel_id=1, source_target_pairs={{0,1},{1,0},{2,3},{3,2},{4,5},{5,4},{6,7},{7,6},{8,9},{9,8},{10,11... | collective-permute-start | bytes 786440 | tf_op jit(solution)/shard_map/ppermute | solution.py:414
  34.5 12.2 %collective-permute-start.8 = (bf16[4,16,16,128]{3,2,1,0:T(8,128)(2,1)S(1)}, bf16[4,16,16,128]{3,2,1,0:T(8,128)(2,1)S(1)}, u32[]{:S(2)}, u32[]{:S(2)}) collective-permute-start(bf16[4,16,16,128]{3,2,1,0:T(8,128)(2,1)S(1)} %get-tuple-element.60.rest_0_), channel_id=1, source_target_pairs={{0,5},{1,4},{2,7},{3,6},{4,1},{5,0},{6,3},{7,2},{8,13},{9,12},{10,... | collective-permute-start | bytes 786440 | tf_op jit(solution)/shard_map/ppermute | solution.py:414
  46.8 5.0 %collective-permute-start.9 = (bf16[16,16,128]{2,1,0:T(8,128)(2,1)S(1)}, bf16[16,16,128]{2,1,0:T(8,128)(2,1)S(1)}, u32[]{:S(2)}, u32[]{:S(2)}) collective-permute-start(bf16[16,16,128]{2,1,0:T(8,128)(2,1)S(1)} %get-tuple-element.68), channel_id=1, source_target_pairs={{0,8},{1,9},{2,10},{3,11},{4,12},{5,13},{6,14},{7,15},{8,0},{9,1},... | collective-permute-start | bytes 196616 | tf_op jit(solution)/shard_map/ppermute | solution.py:414
  48.5 6.6 %collective-permute-start.10 = (bf16[16,16,128]{2,1,0:T(8,128)(2,1)S(1)}, bf16[16,16,128]{2,1,0:T(8,128)(2,1)S(1)}, u32[]{:S(2)}, u32[]{:S(2)}) collective-permute-start(bf16[16,16,128]{2,1,0:T(8,128)(2,1)S(1)} %get-tuple-element.69), channel_id=1, source_target_pairs={{0,16},{1,17},{2,18},{3,19},{4,20},{5,21},{6,22},{7,23},{8,24},{9,... | collective-permute-start | bytes 196616 | tf_op jit(solution)/shard_map/ppermute | solution.py:414
  50.2 6.2 %collective-permute-start.11 = (bf16[16,16,128]{2,1,0:T(8,128)(2,1)S(1)}, bf16[16,16,128]{2,1,0:T(8,128)(2,1)S(1)}, u32[]{:S(2)}, u32[]{:S(2)}) collective-permute-start(bf16[16,16,128]{2,1,0:T(8,128)(2,1)S(1)} %get-tuple-element.70), channel_id=1, source_target_pairs={{0,24},{1,25},{2,26},{3,27},{4,28},{5,29},{6,30},{7,31},{8,16},{9,... | collective-permute-start | bytes 196616 | tf_op jit(solution)/shard_map/ppermute | solution.py:414
  56.4 4.5 %collective-permute-start.12 = (bf16[16,16,128]{2,1,0:T(8,128)(2,1)S(1)}, bf16[16,16,128]{2,1,0:T(8,128)(2,1)S(1)}, u32[]{:S(2)}, u32[]{:S(2)}) collective-permute-start(bf16[16,16,128]{2,1,0:T(8,128)(2,1)S(1)} %line_sum.1.a_ref), channel_id=1, source_target_pairs={{0,8},{1,9},{2,10},{3,11},{4,12},{5,13},{6,14},{7,15},{8,0},{9,1},... | collective-permute-start | bytes 196616 | tf_op jit(solution)/shard_map/ppermute | solution.py:414
  57.1 6.2 %collective-permute-start.13 = (bf16[16,16,128]{2,1,0:T(8,128)(2,1)S(1)}, bf16[16,16,128]{2,1,0:T(8,128)(2,1)S(1)}, u32[]{:S(2)}, u32[]{:S(2)}) collective-permute-start(bf16[16,16,128]{2,1,0:T(8,128)(2,1)S(1)} %line_sum.1.a_ref), channel_id=1, source_target_pairs={{0,16},{1,17},{2,18},{3,19},{4,20},{5,21},{6,22},{7,23},{8,24},{9,... | collective-permute-start | bytes 196616 | tf_op jit(solution)/shard_map/ppermute | solution.py:414
  58.9 6.1 %collective-permute-start.14 = (bf16[16,16,128]{2,1,0:T(8,128)(2,1)S(1)}, bf16[16,16,128]{2,1,0:T(8,128)(2,1)S(1)}, u32[]{:S(2)}, u32[]{:S(2)}) collective-permute-start(bf16[16,16,128]{2,1,0:T(8,128)(2,1)S(1)} %line_sum.1.a_ref), channel_id=1, source_target_pairs={{0,24},{1,25},{2,26},{3,27},{4,28},{5,29},{6,30},{7,31},{8,16},{9,... | collective-permute-start | bytes 196616 | tf_op jit(solution)/shard_map/ppermute | solution.py:414
  65.0 3.6 %collective-permute-start.18 = (bf16[4,16,16,128]{3,2,1,0:T(8,128)(2,1)S(1)}, bf16[4,16,16,128]{3,2,1,0:T(8,128)(2,1)S(1)}, u32[]{:S(2)}, u32[]{:S(2)}) collective-permute-start(bf16[4,16,16,128]{3,2,1,0:T(8,128)(2,1)S(1)} %line_gather.1.refs_0_), channel_id=1, source_target_pairs={{0,2},{1,3},{2,0},{3,1},{4,6},{5,7},{6,4},{7,5},{8,10},{9,11},{10,... | collective-permute-start | bytes 786440 | tf_op jit(solution)/shard_map/ppermute | solution.py:414
  65.1 9.2 %collective-permute-start.17 = (bf16[4,16,16,128]{3,2,1,0:T(8,128)(2,1)S(1)}, bf16[4,16,16,128]{3,2,1,0:T(8,128)(2,1)S(1)}, u32[]{:S(2)}, u32[]{:S(2)}) collective-permute-start(bf16[4,16,16,128]{3,2,1,0:T(8,128)(2,1)S(1)} %line_gather.1.refs_0_), channel_id=1, source_target_pairs={{0,4},{1,5},{2,6},{3,7},{4,0},{5,1},{6,2},{7,3},{8,12},{9,13},{10,... | collective-permute-start | bytes 786440 | tf_op jit(solution)/shard_map/ppermute | solution.py:414
  66.4 14.0 %collective-permute-start.19 = (bf16[4,16,16,128]{3,2,1,0:T(8,128)(2,1)S(1)}, bf16[4,16,16,128]{3,2,1,0:T(8,128)(2,1)S(1)}, u32[]{:S(2)}, u32[]{:S(2)}) collective-permute-start(bf16[4,16,16,128]{3,2,1,0:T(8,128)(2,1)S(1)} %line_gather.1.refs_0_), channel_id=1, source_target_pairs={{0,1},{1,0},{2,3},{3,2},{4,5},{5,4},{6,7},{7,6},{8,9},{9,8},{10,11... | collective-permute-start | bytes 786440 | tf_op jit(solution)/shard_map/ppermute | solution.py:414
  67.1 13.3 %collective-permute-start.15 = (bf16[4,16,16,128]{3,2,1,0:T(8,128)(2,1)S(1)}, bf16[4,16,16,128]{3,2,1,0:T(8,128)(2,1)S(1)}, u32[]{:S(2)}, u32[]{:S(2)}) collective-permute-start(bf16[4,16,16,128]{3,2,1,0:T(8,128)(2,1)S(1)} %line_gather.1.refs_0_), channel_id=1, source_target_pairs={{0,5},{1,4},{2,7},{3,6},{4,1},{5,0},{6,3},{7,2},{8,13},{9,12},{10,... | collective-permute-start | bytes 786440 | tf_op jit(solution)/shard_map/ppermute | solution.py:414
  74.2 6.7 %collective-permute-start.20 = (bf16[4,16,16,128]{3,2,1,0:T(8,128)(2,1)S(1)}, bf16[4,16,16,128]{3,2,1,0:T(8,128)(2,1)S(1)}, u32[]{:S(2)}, u32[]{:S(2)}) collective-permute-start(bf16[4,16,16,128]{3,2,1,0:T(8,128)(2,1)S(1)} %pass.5.refs_0_), channel_id=1, source_target_pairs={{0,2},{1,3},{2,0},{3,1},{4,6},{5,7},{6,4},{7,5},{8,10},{9,11},{10,... | collective-permute-start | bytes 786440 | tf_op jit(solution)/shard_map/ppermute | solution.py:414
  80.4 1.5 %collective-permute-start.21 = (bf16[4,16,16,128]{3,2,1,0:T(8,128)(2,1)S(1)}, bf16[4,16,16,128]{3,2,1,0:T(8,128)(2,1)S(1)}, u32[]{:S(2)}, u32[]{:S(2)}) collective-permute-start(bf16[4,16,16,128]{3,2,1,0:T(8,128)(2,1)S(1)} %collective-permute-done.19.refs_1_), channel_id=1, source_target_pairs={{0,2},{1,3},{2,0},{3,1},{4,6},{5,7},{6,4},{7,5},{8,10},{9,11},{10,... | collective-permute-start | bytes 786440 | tf_op jit(solution)/shard_map/ppermute | solution.py:414
  80.4 3.8 %collective-permute-start.16 = (bf16[4,16,16,128]{3,2,1,0:T(8,128)(2,1)S(1)}, bf16[4,16,16,128]{3,2,1,0:T(8,128)(2,1)S(1)}, u32[]{:S(2)}, u32[]{:S(2)}) collective-permute-start(bf16[4,16,16,128]{3,2,1,0:T(8,128)(2,1)S(1)} %collective-permute-done.15.refs_2_), channel_id=1, source_target_pairs={{0,2},{1,3},{2,0},{3,1},{4,6},{5,7},{6,4},{7,5},{8,10},{9,11},{10,... | collective-permute-start | bytes 786440 | tf_op jit(solution)/shard_map/ppermute | solution.py:414

commit v8 on v7

--- a/solution.py
+++ b/solution.py
@@ -31,13 +31,15 @@
 
 def to_slots(rows, frames, keep):
     a, b = iotas(rows * SLOTS, frames * rows)
-    hit = (a // SLOTS == b % rows) & keep(b // rows, a % SLOTS)
+    bits = rows.bit_length() - 1
+    hit = ((a >> 4) == (b & (rows - 1))) & keep(b >> bits, a & 15)
     return jnp.where(hit, 1.0, 0.0).astype(BF)
 
 
 def to_frames(rows):
     a, b = iotas(SLOTS * rows, rows * SLOTS)
-    hit = (a % rows == b // SLOTS) & (a // rows == b % SLOTS)
+    bits = rows.bit_length() - 1
+    hit = ((a & (rows - 1)) == (b >> 4)) & ((a >> bits) == (b & 15))
     return jnp.where(hit, 1.0, 0.0).astype(BF)
 
 
@@ -82,8 +84,8 @@
     send_ref[:, k] = jnp.where(core == 0, high, low).reshape(16, 16, CH // 2)
 
 
-def edges_kernel(bands, count_ref, x_ref, cot_ref, *rest):
-    outs, (nxt_ref, token_ref) = rest[:-2], rest[-2:]
+def edges_kernel(bands, count_ref, x_ref, *rest):
+    outs, token_ref = rest[:-1], rest[-1]
     token_ref[...] = jnp.zeros_like(token_ref)
     count = count_ref[0]
     band = lax.axis_index("grp")
@@ -92,7 +94,6 @@
         starts, lower = [jnp.where(band == 0, wide - 16, 0)], [band == 0]
     else:
         starts, lower = [wide - 16, 0], [True, False]
-    nxt_ref[...] = cot_ref[0:2]
     place = to_slots(16, SLOTS, own_frames(count))
     for k, at in enumerate(starts):
         piece = x_ref[:, pl.ds(pl.multiple_of(at, 16), 16), :].reshape(SLOTS * 16, CH)
@@ -122,7 +123,7 @@
             at_ref[i * CH : i * CH + CH, pl.ds(at, 256)] = flipped
         return 0
 
-    lax.fori_loop(0, rows // 2, rows_of, 0)
+    lax.fori_loop(0, rows // 2, rows_of, 0, unroll=4)
 
 
 def spatial_kernel(
@@ -135,7 +136,7 @@
         a = jnp.where(flag, ref[...].astype(F32), 0.0)
         acts_ref[row, 1 : cols + 1] = a.astype(BF).reshape(cols, SLOTS, CH)
     a, b = iotas(32, 256)
-    pick = (a // 2 == b // SLOTS) & (b % SLOTS == count - 2 + a % 2)
+    pick = ((a >> 1) == (b >> 4)) & ((b & 15) == count - 2 + (a & 1))
     pick = jnp.where(pick, 1.0, 0.0).astype(BF)
 
     def rows_of(q, _):
@@ -150,7 +151,7 @@
             edge_ref[2 * q + half] = mm(pick, out[half * 256 : half * 256 + 256]).astype(BF)
         return 0
 
-    lax.fori_loop(0, rows // 4, rows_of, 0)
+    lax.fori_loop(0, rows // 4, rows_of, 0, unroll=2)
 
 
 def grad_spatial_kernel(
@@ -198,7 +199,7 @@
         gy_ref[pl.ds(4 * q, 4)] = g.astype(BF).reshape(4, cols, SLOTS, CH)
         return 0
 
-    lax.fori_loop(0, rows // 4, grads_of, 0)
+    lax.fori_loop(0, rows // 4, grads_of, 0, unroll=2)
 
     wide = rows * cols * SLOTS
     for j in range(3):
@@ -215,7 +216,7 @@
     count = count_ref[0]
     rows, cols = xt_ref.shape[0], xt_ref.shape[1]
     a, b = iotas(256, 32)
-    place = (a // SLOTS == b // 2) & (a % SLOTS == OWN + b % 2)
+    place = ((a >> 4) == (b >> 1)) & ((a & 15) == OWN + (b & 1))
     place = jnp.where(place, 1.0, 0.0).astype(BF)
 
     def rows_of(q, _):
@@ -235,7 +236,7 @@
         y_ref[pl.ds(4 * q, 4)] = y.reshape(4, cols, SLOTS, CH)
         return 0
 
-    lax.fori_loop(0, rows // 4, rows_of, 0)
+    lax.fori_loop(0, rows // 4, rows_of, 0, unroll=2)
 
     wide = rows * cols * SLOTS
     value = mm(st_ref[...], gy_ref[...].reshape(wide, CH))
@@ -306,7 +307,7 @@
             buf[:, pl.ds(pl.multiple_of((2 * q + k) * 16, 16), 16), :] = o.reshape(SLOTS, 16, CH)
         return 0
 
-    lax.fori_loop(0, rows // 4, rows_of, 0)
+    lax.fori_loop(0, rows // 4, rows_of, 0, unroll=2)
     copy = pltpu.make_async_copy(buf, out_ref, sems.at[0])
     copy.start()
     for q in range(down_ref.shape[1] // 4):
@@ -315,10 +316,13 @@
     copy.wait()
 
 
+ORDER = (0, 3, 2, 1)
+
+
 def plane_send_kernel(keep_a, got_a, keep_b, got_b, *outs):
     _, p, _ = place_bits()
     n = keep_a.shape[1]
-    for r, out in enumerate(outs):
+    for r, out in zip(ORDER, outs):
         at = pl.ds((p ^ r) * 4, 4)
         out[:, :n] = (keep_a[at].astype(F32) + got_a[at].astype(F32)).astype(BF)
         out[:, n:] = (keep_b[at].astype(F32) + got_b[at].astype(F32)).astype(BF)
@@ -327,9 +331,9 @@
 def line_send_kernel(a_ref, b_ref, c_ref, d_ref, *rest):
     outs = rest[-4:]
     _, _, z = place_bits()
-    for r in range(4):
+    for k, r in enumerate(ORDER):
         parts = [ref[z ^ r].astype(F32) for ref in (a_ref, b_ref, c_ref, d_ref)]
-        outs[r][...] = (parts[0] + parts[1] + parts[2] + parts[3]).astype(BF)
+        outs[k][...] = (parts[0] + parts[1] + parts[2] + parts[3]).astype(BF)
 
 
 def line_sum_kernel(a_ref, b_ref, c_ref, d_ref, out_ref):
@@ -339,8 +343,14 @@
 
 def line_gather_kernel(a_ref, b_ref, c_ref, d_ref, out_ref):
     _, _, z = place_bits()
-    for r, ref in enumerate((a_ref, b_ref, c_ref, d_ref)):
+    for r, ref in zip(ORDER, (a_ref, b_ref, c_ref, d_ref)):
         out_ref[z ^ r] = ref[...]
+
+
+def plane_gather_kernel(a_ref, b_ref, c_ref, d_ref, out_ref):
+    _, p, _ = place_bits()
+    for r, ref in zip(ORDER, (a_ref, b_ref, c_ref, d_ref)):
+        out_ref[pl.ds((p ^ r) * 4, 4)] = ref[...]
 
 
 def add_kernel(a_ref, b_ref, out_ref):
@@ -351,27 +361,21 @@
     pass
 
 
-def finish_kernel(which, *refs):
-    buf, sems = refs[-2:]
-    outs, token_ref = refs[-6:-3], refs[-3]
-    token_ref[...] = jnp.zeros_like(token_ref)
-    core, p, _ = place_bits()
+def finish_kernel(own, half_ref, *rest):
+    buf, sems = rest[-2:]
+    outs = rest[-5:-2]
+    core, _, _ = place_bits()
+    at = pl.multiple_of((core if own else 1 - core) * (CH // 2), CH // 2)
     copies = []
-    for f, (ref, (sibling, r)) in enumerate(zip(refs, which)):
-        rows = pl.ds(pl.multiple_of((p ^ r) * 64, 64), 64)
-        cols = (1 - core if sibling else core) * (CH // 2)
-        cols = pl.ds(pl.multiple_of(cols, CH // 2), CH // 2)
-        m = 0
-        for o, out in enumerate(outs):
-            n = out.shape[0]
-            for k in range(n):
-                buf[f, m + k] = ref[:, m + k].reshape(64, CH // 2).astype(F32)
-            copy = pltpu.make_async_copy(
-                buf.at[f, pl.ds(m, n)], out.at[:, rows, cols], sems.at[f, o]
+    k = 0
+    for out in outs:
+        for m in range(out.shape[0]):
+            buf[k] = half_ref[:, k].reshape(CH, CH // 2).astype(F32)
+            copies.append(
+                pltpu.make_async_copy(buf.at[k], out.at[m, :, pl.ds(at, CH // 2)], sems.at[k])
             )
-            copy.start()
-            copies.append(copy)
-            m += n
+            copies[-1].start()
+            k += 1
     for copy in copies:
         copy.wait()
 
@@ -421,9 +425,9 @@
 def four_round(parts, bits, tm, grp):
     return [
         parts[0],
-        swap(parts[1], tm, grp, bits[0]),
+        swap(parts[1], tm, grp, *bits),
         swap(parts[2], tm, grp, bits[1]),
-        swap(parts[3], tm, grp, *bits),
+        swap(parts[3], tm, grp, bits[0]),
     ]
 
 
@@ -432,17 +436,18 @@
     return call(pass_kernel, "pass", ins, [(ANY, value.shape)], alias={0: 0})[0]
 
 
-def finish(blocks, before, after):
-    n = blocks[0][0].shape[1]
-    *outs, token = call(
-        functools.partial(finish_kernel, [b[1:] for b in blocks]),
-        "finish",
-        [(VMEM, b[0]) for b in blocks] + [(HBM, a) for a in before] + [(ANY, a) for a in after],
-        [(HBM, (m, CH, CH), F32) for m in (9, 3, 4)] + [TOKEN],
-        [pltpu.VMEM((len(blocks), n, 64, CH // 2), F32), pltpu.SemaphoreType.DMA((len(blocks), 3))],
-        alias={len(blocks) + i: i for i in range(len(before))},
-    )
-    return outs, token
+def finish(own, half, before):
+    n = half.shape[1]
+    return list(
+        call(
+            functools.partial(finish_kernel, own),
+            "finish",
+            [(VMEM, half)] + [(HBM, a) for a in before],
+            [(HBM, (m, CH, CH), F32) for m in (9, 3, 4)],
+            [pltpu.VMEM((n, CH, CH // 2), F32), pltpu.SemaphoreType.DMA((n,))],
+            alias={1 + i: i for i in range(len(before))},
+        )
+    )
 
 
 def along(value, axis, by):
@@ -472,15 +477,15 @@
     dma = pltpu.SemaphoreType.DMA
 
     sides = 1 if grp == 2 else 2
-    *edge, nxt, token = call(
+    *edge, token = call(
         functools.partial(edges_kernel, grp),
         "edges",
-        [count, (VMEM, x), (VMEM, cotangent)],
-        [(VMEM, (cols * slots, ch))] * sides + [(VMEM, (2,) + cotangent.shape[1:]), TOKEN],
+        [count, (VMEM, x)],
+        [(VMEM, (cols * slots, ch))] * sides + [TOKEN],
         flops=tap // 8,
     )
     top, bot = from_bands(edge)
-    nxt_got = along(nxt, "tm", -1)
+    nxt_got = along(cotangent[:2], "tm", -1)
     xt, acts, at = call(
         acts_kernel,
         "acts",
@@ -558,14 +563,11 @@
         line_gather_kernel, "line_gather", [(VMEM, a) for a in parts], [(VMEM, (4,) + mine.shape)]
     )
     parts = four_round([mine] * 4, plane, tm, grp)
-    side = core_round(mine, tm, grp)
-    outs, token = finish([(mine, False, 0), (side, True, 0)], [], [])
-    parts[1] = passed(parts[1], [token])
-    sides = [side] + [core_round(part, tm, grp) for part in parts[1:]]
-    blocks = [(parts[r], False, r) for r in (1, 2, 3)] + [(sides[r], True, r) for r in (1, 2)]
-    outs, _ = finish(blocks, outs, [])
-    outs, _ = finish([(sides[3], True, 3)], outs, [])
-    sum_s, sum_t, sum_d = outs
+    ins = [(VMEM, a) for a in parts]
+    (mine,) = call(plane_gather_kernel, "plane_gather", ins, [(VMEM, (16,) + mine.shape[1:])])
+    got = core_round(mine, tm, grp)
+    outs = finish(True, mine, [])
+    sum_s, sum_t, sum_d = finish(False, got, outs)
     return (
         down,
         grad_x.reshape(frames_in.shape),

time: 85.8 us -> 85.2 us (level)
  local copies, waits for them, and re-layouts: 2.19 us -> 4.49 us
  waiting for transfers between devices: 27.5 us -> 25.4 us
    ppermute x18 -> x15, waiting for transfers between devices: 27.5 us -> 25.2 us  [swap(): return lax.ppermute(value, AXES, [(d, d ^ flip) for d in range(tm * grp)])]
    unnamed x12 -> x14, local copies, waits for them, and re-layouts: 2.19 us -> 3.72 us
    pallas_call x16 -> x15, Pallas kernels: 28.6 us -> 27.9 us  [call(): pl.pallas_call(kernel, out_shape=shapes, in_specs=[s for s, _ in ins], ou...]
    ppermute x18 -> x15, starting transfers between devices: 17.9 us -> 17.4 us  [swap(): return lax.ppermute(value, AXES, [(d, d ^ flip) for d in range(tm * grp)])]
  transfers between devices with their start and end apart: 22 -> 19, of which waited for: 10 -> 10; matrix products, arithmetic and copies ran while one was open for 0% -> 1% of each run, Pallas kernels for 31% -> 30%
where the time goes in v8:
time: 85.2 us; the launch traced here: 84.9 us
  Pallas kernels  27.9 us (33%)
  starting transfers between devices  25.5 us (30%)
  waiting for transfers between devices  25.4 us (30%)
  local copies, waits for them, and re-layouts  4.49 us (5%)
  between operations  1.65 us (2%)
    pallas_call x15, Pallas kernels, call(): pl.pallas_call(kernel, out_shape=shapes, in_specs=[s for s, _ in ins], ou...  27.9 us
    ppermute x15, waiting for transfers between devices, swap(): return lax.ppermute(value, AXES, [(d, d ^ flip) for d in range(tm * grp)])  25.2 us
    ppermute x15, starting transfers between devices, swap(): return lax.ppermute(value, AXES, [(d, d ^ flip) for d in range(tm * grp)])  17.4 us
    ppermute x2, starting transfers between devices, along(): return lax.ppermute(value, axis, pairs)  4.51 us
    unnamed x14, local copies, waits for them, and re-layouts  3.72 us
    ppermute x2, starting transfers between devices, from_bands(): got = lax.ppermute(parts[0], 'grp', [(0, 1), (1, 0)])  3.54 us
  transfers between devices with their start and end apart: 19, of which 10 were waited for; matrix products, arithmetic and copies ran while one was open for 1% of the time, Pallas kernels for 30%

profile of v8, /device:TPU:0, one launch (start us, length us, event | category | flops | bytes accessed | tf_op | source)
XLA Modules:
  0.0 84.9 jit_solution(1406326284007100357)
XLA Ops:
  1.3 0.0 copy-start
  1.3 1.2 %copy-done = bf16[16,16,8,256]{3,2,1,0:T(8,128)(2,1)S(1)} copy-done((bf16[16,16,8,256]{3,2,1,0:T(8,128)(2,1)S(1)}, bf16[16,16,8,256]{3,2,1,0:T(8,128)(2,1)}, u32[]{:S(2)}) %copy-start) | copy-done | bytes 1048600
  2.5 0.3 edges.1
  2.8 3.0 %collective-permute-start = (bf16[128,256]{1,0:T(8,128)(2,1)S(1)}, bf16[128,256]{1,0:T(8,128)(2,1)S(1)}, u32[]{:S(2)}, u32[]{:S(2)}) collective-permute-start(bf16[128,256]{1,0:T(8,128)(2,1)S(1)} %get-tuple-element.41), channel_id=1, source_target_pairs={{0,1},{1,0},{2,3},{3,2},{4,5},{5,4},{6,7},{7,6},{8,9},{9,8},{10,11... | collective-permute-start | bytes 196616 | tf_op jit(solution)/shard_map/ppermute | solution.py:461
  5.8 0.8 slice.3
  6.6 1.3 %collective-permute-start.1 = (bf16[2,8,4,256]{3,2,1,0:T(4,128)(2,1)S(1)}, bf16[2,8,4,256]{3,2,1,0:T(4,128)(2,1)S(1)}, u32[]{:S(2)}, u32[]{:S(2)}) collective-permute-start(bf16[2,8,4,256]{3,2,1,0:T(4,128)(2,1)S(1)} %slice.3), channel_id=1, source_target_pairs={{2,0},{4,2},{6,4},{8,6},{10,8},{12,10},{14,12},{16,14},{18,16},{20... | collective-permute-start | bytes 98312 | tf_op jit(solution)/shard_map/ppermute | solution.py:456
  7.9 0.0 copy-start.1
  7.9 1.2 %copy-done.1 = bf16[16,16,8,256]{3,2,1,0:T(8,128)(2,1)S(1)} copy-done((bf16[16,16,8,256]{3,2,1,0:T(8,128)(2,1)S(1)}, bf16[16,16,8,256]{3,2,1,0:T(8,128)(2,1)}, u32[]{:S(2)}) %copy-start.1) | copy-done | bytes 1048600
  9.1 1.5 %acts.1 = (bf16[16,8,16,256]{3,2,1,0:T(8,128)(2,1)S(1)}, bf16[18,10,16,256]{3,2,1,0:T(8,128)(2,1)S(1)}, bf16[768,2560]{1,0:T(8,128)(2,1)S(1)}) custom-call(s32[1]{0:T(128)S(6)} %copy.25.count_ref, bf16[16,128,256]{2,1,0:T(8,128)(2,1)S(1)} %bitcast.7, f32[8,128]{1,0:T(8,128)S(1)} %get-tuple-element.38._), custom_call_target="tpu_custom_call" | custom-call | flops 536870912 | bytes 7503876 | tf_op jit(solution)/shard_map/acts/pallas_call | solution.py:394
  10.6 0.0 copy-start.3
  10.7 1.3 %copy-done.3 = bf16[3,3,256,256]{3,2,1,0:T(8,128)(2,1)S(1)} copy-done((bf16[3,3,256,256]{3,2,1,0:T(8,128)(2,1)S(1)}, bf16[3,3,256,256]{3,2,1,0:T(8,128)(2,1)}, u32[]{:S(2)}) %copy-start.3) | copy-done | bytes 1179672
  11.9 5.7 %spatial.1 = (bf16[18,10,16,256]{3,2,1,0:T(8,128)(2,1)S(1)}, bf16[16,8,16,256]{3,2,1,0:T(8,128)(2,1)S(1)}, bf16[8,32,256]{2,1,0:T(8,128)(2,1)S(1)}) custom-call(s32[1]{0:T(128)S(6)} %copy.25.count_ref, bf16[128,256]{1,0:T(8,128)(2,1)S(1)} %collective-permute-done.top_ref.bot_ref, ...), custom_call_target="tpu_custom_call", output_to_operand_aliasing={{0}: (3, {})} | custom-call | flops 2415919104 | bytes 5439492 | tf_op jit(solution)/shard_map/spatial/pallas_call | solution.py:394
  17.6 3.2 %collective-permute-start.3 = (bf16[8,32,256]{2,1,0:T(8,128)(2,1)S(1)}, bf16[8,32,256]{2,1,0:T(8,128)(2,1)S(1)}, u32[]{:S(2)}, u32[]{:S(2)}) collective-permute-start(bf16[8,32,256]{2,1,0:T(8,128)(2,1)S(1)} %get-tuple-element.43._), channel_id=1, source_target_pairs={{0,2},{2,4},{4,6},{6,8},{8,10},{10,12},{12,14},{14,16},{16,18},{18... | collective-permute-start | bytes 393224 | tf_op jit(solution)/shard_map/ppermute | solution.py:456
  20.9 4.7 %grad_spatial.1 = (bf16[768,2560]{1,0:T(8,128)(2,1)S(1)}, bf16[8,4,16,256]{3,2,1,0:T(8,128)(2,1)S(1)}, bf16[16,8,16,256]{3,2,1,0:T(8,128)(2,1)S(1)}, bf16[16,10,...) custom-call(s32[1]{0:T(128)S(6)} %copy.25.count_ref, ...), custom_call_target="tpu_custom_call", output_to_operand_aliasing={{0}: (1, {})} | custom-call | flops 3758096384 | bytes 13041668 | tf_op jit(solution)/shard_map/grad_spatial/pallas_call | solution.py:394
  25.6 1.2 %collective-permute-start.4 = (bf16[16,9,16,128]{3,2,1,0:T(8,128)(2,1)S(1)}, bf16[16,9,16,128]{3,2,1,0:T(8,128)(2,1)S(1)}, u32[]{:S(2)}, u32[]{:S(2)}) collective-permute-start(bf16[16,9,16,128]{3,2,1,0:T(8,128)(2,1)S(1)} %pass.2.rest_0_), channel_id=1, source_target_pairs={{0,2},{1,3},{2,0},{3,1},{4,6},{5,7},{6,4},{7,5},{8,10},{9,11},{10,... | collective-permute-start | bytes 1769480 | tf_op jit(solution)/shard_map/ppermute | solution.py:418
  26.8 0.5 collective-permute-start.2
  27.3 3.3 %forward.1 = (bf16[512,256]{1,0:T(8,128)(2,1)S(1)}, bf16[16,7,16,128]{3,2,1,0:T(8,128)(2,1)S(1)}, bf16[16,7,16,128]{3,2,1,0:T(8,128)(2,1)S(1)}) custom-call(s32[1]{0:T(128)S(6)} %copy.25.count_ref, bf16[16,8,16,256]{3,2,1,0:T(8,128)(2,1)S(1)} %get-tuple-element.39.xt_ref, bf16[16,8,16,256]{3,2,1,0:T(8,128)(2,1)S(1)} %get-tuple-element.47.sp_ref, ...), custom_call_target="tpu_custom_call" | custom-call | flops 2684354560 | bytes 5636100 | tf_op jit(solution)/shard_map/forward/pallas_call | solution.py:394
  30.6 0.0 copy-start.4
  30.6 0.1 collective-permute-done.2.__2_.top_ref.bot_ref
  30.7 0.0 collective-permute-done.4.__1_.got_a
  30.7 0.0 collective-permute-start.5
  30.7 1.8 %collective-permute-done.5.got_b = bf16[16,7,16,128]{3,2,1,0:T(8,128)(2,1)S(1)} collective-permute-done((bf16[16,7,16,128]{3,2,1,0:T(8,128)(2,1)S(1)}, bf16[16,7,16,128]{3,2,1,0:T(8,128)(2,1)S(1)}, u32[]{:S(2)}, u32[]{:S(2)}) %collective-permute-start.5) | collective-permute-done | bytes 458784 | tf_op jit(solution)/shard_map/ppermute | solution.py:418
  32.5 0.2 plane_send.1
  32.8 3.1 %collective-permute-start.6 = (bf16[4,16,16,128]{3,2,1,0:T(8,128)(2,1)S(1)}, bf16[4,16,16,128]{3,2,1,0:T(8,128)(2,1)S(1)}, u32[]{:S(2)}, u32[]{:S(2)}) collective-permute-start(bf16[4,16,16,128]{3,2,1,0:T(8,128)(2,1)S(1)} %get-tuple-element.58), channel_id=1, source_target_pairs={{0,5},{1,4},{2,7},{3,6},{4,1},{5,0},{6,3},{7,2},{8,13},{9,12},{10,... | collective-permute-start | bytes 786440 | tf_op jit(solution)/shard_map/ppermute | solution.py:418
  35.8 0.5 collective-permute-start.7
  36.4 0.1 collective-permute-start.8
  36.5 9.1 %grad_x.1 = (bf16[16,128,256]{2,1,0:T(8,128)(2,1)}, bf16[16,8,4,256]{3,2,1,0:T(4,128)(2,1)}, f32[8,128]{1,0:T(8,128)S(1)}) custom-call(s32[1]{0:T(128)S(6)} %copy.25.count_ref, bf16[16,8,16,256]{3,2,1,0:T(8,128)(2,1)S(1)} %get-tuple-element.39.xt_ref, bf16[16,8,16,256]{3,2,1,0:T(8,128)(2,1)S(1)} %get-tuple-element.44.gy_ref, ...), custom_call_target="tpu_custom_call" | custom-call | flops 2684354560 | bytes 7147524 | tf_op jit(solution)/shard_map/grad_x/pallas_call | solution.py:394
  45.5 0.0 collective-permute-done.6.b_ref
  45.5 2.5 %collective-permute-done.7.c_ref = bf16[4,16,16,128]{3,2,1,0:T(8,128)(2,1)S(1)} collective-permute-done((bf16[4,16,16,128]{3,2,1,0:T(8,128)(2,1)S(1)}, bf16[4,16,16,128]{3,2,1,0:T(8,128)(2,1)S(1)}, u32[]{:S(2)}, u32[]{:S(2)}) %collective-permute-start.7) | collective-permute-done | bytes 262176 | tf_op jit(solution)/shard_map/ppermute | solution.py:418
  48.1 0.1 line_send.1
  48.2 3.4 %collective-permute-start.9 = (bf16[16,16,128]{2,1,0:T(8,128)(2,1)S(1)}, bf16[16,16,128]{2,1,0:T(8,128)(2,1)S(1)}, u32[]{:S(2)}, u32[]{:S(2)}) collective-permute-start(bf16[16,16,128]{2,1,0:T(8,128)(2,1)S(1)} %get-tuple-element.62), channel_id=1, source_target_pairs={{0,24},{1,25},{2,26},{3,27},{4,28},{5,29},{6,30},{7,31},{8,16},{9,... | collective-permute-start | bytes 196616 | tf_op jit(solution)/shard_map/ppermute | solution.py:418
  51.6 1.1 %collective-permute-start.11 = (bf16[16,16,128]{2,1,0:T(8,128)(2,1)S(1)}, bf16[16,16,128]{2,1,0:T(8,128)(2,1)S(1)}, u32[]{:S(2)}, u32[]{:S(2)}) collective-permute-start(bf16[16,16,128]{2,1,0:T(8,128)(2,1)S(1)} %get-tuple-element.64), channel_id=1, source_target_pairs={{0,8},{1,9},{2,10},{3,11},{4,12},{5,13},{6,14},{7,15},{8,0},{9,1},... | collective-permute-start | bytes 196616 | tf_op jit(solution)/shard_map/ppermute | solution.py:418
  52.7 2.0 %collective-permute-done.9.b_ref = bf16[16,16,128]{2,1,0:T(8,128)(2,1)S(1)} collective-permute-done((bf16[16,16,128]{2,1,0:T(8,128)(2,1)S(1)}, bf16[16,16,128]{2,1,0:T(8,128)(2,1)S(1)}, u32[]{:S(2)}, u32[]{:S(2)}) %collective-permute-start.9) | collective-permute-done | bytes 65568 | tf_op jit(solution)/shard_map/ppermute | solution.py:418
  54.7 2.9 %collective-permute-done.10.c_ref = bf16[16,16,128]{2,1,0:T(8,128)(2,1)S(1)} collective-permute-done((bf16[16,16,128]{2,1,0:T(8,128)(2,1)S(1)}, bf16[16,16,128]{2,1,0:T(8,128)(2,1)S(1)}, u32[]{:S(2)}, u32[]{:S(2)}) %collective-permute-start.10) | collective-permute-done | bytes 65568 | tf_op jit(solution)/shard_map/ppermute | solution.py:418
  57.6 2.7 %collective-permute-start.12 = (bf16[16,16,128]{2,1,0:T(8,128)(2,1)S(1)}, bf16[16,16,128]{2,1,0:T(8,128)(2,1)S(1)}, u32[]{:S(2)}, u32[]{:S(2)}) collective-permute-start(bf16[16,16,128]{2,1,0:T(8,128)(2,1)S(1)} %line_sum.1.a_ref), channel_id=1, source_target_pairs={{0,24},{1,25},{2,26},{3,27},{4,28},{5,29},{6,30},{7,31},{8,16},{9,... | collective-permute-start | bytes 196616 | tf_op jit(solution)/shard_map/ppermute | solution.py:418
  60.3 1.7 %collective-permute-start.14 = (bf16[16,16,128]{2,1,0:T(8,128)(2,1)S(1)}, bf16[16,16,128]{2,1,0:T(8,128)(2,1)S(1)}, u32[]{:S(2)}, u32[]{:S(2)}) collective-permute-start(bf16[16,16,128]{2,1,0:T(8,128)(2,1)S(1)} %line_sum.1.a_ref), channel_id=1, source_target_pairs={{0,8},{1,9},{2,10},{3,11},{4,12},{5,13},{6,14},{7,15},{8,0},{9,1},... | collective-permute-start | bytes 196616 | tf_op jit(solution)/shard_map/ppermute | solution.py:418
  62.1 2.1 %collective-permute-done.12.b_ref = bf16[16,16,128]{2,1,0:T(8,128)(2,1)S(1)} collective-permute-done((bf16[16,16,128]{2,1,0:T(8,128)(2,1)S(1)}, bf16[16,16,128]{2,1,0:T(8,128)(2,1)S(1)}, u32[]{:S(2)}, u32[]{:S(2)}) %collective-permute-start.12) | collective-permute-done | bytes 65568 | tf_op jit(solution)/shard_map/ppermute | solution.py:418
  64.2 2.2 %collective-permute-done.13.c_ref = bf16[16,16,128]{2,1,0:T(8,128)(2,1)S(1)} collective-permute-done((bf16[16,16,128]{2,1,0:T(8,128)(2,1)S(1)}, bf16[16,16,128]{2,1,0:T(8,128)(2,1)S(1)}, u32[]{:S(2)}, u32[]{:S(2)}) %collective-permute-start.13) | collective-permute-done | bytes 65568 | tf_op jit(solution)/shard_map/ppermute | solution.py:418
  66.4 1.3 %collective-permute-start.15 = (bf16[4,16,16,128]{3,2,1,0:T(8,128)(2,1)S(1)}, bf16[4,16,16,128]{3,2,1,0:T(8,128)(2,1)S(1)}, u32[]{:S(2)}, u32[]{:S(2)}) collective-permute-start(bf16[4,16,16,128]{3,2,1,0:T(8,128)(2,1)S(1)} %line_gather.1.a_ref), channel_id=1, source_target_pairs={{0,5},{1,4},{2,7},{3,6},{4,1},{5,0},{6,3},{7,2},{8,13},{9,12},{10,... | collective-permute-start | bytes 786440 | tf_op jit(solution)/shard_map/ppermute | solution.py:418
  67.7 1.3 %collective-permute-start.16 = (bf16[4,16,16,128]{3,2,1,0:T(8,128)(2,1)S(1)}, bf16[4,16,16,128]{3,2,1,0:T(8,128)(2,1)S(1)}, u32[]{:S(2)}, u32[]{:S(2)}) collective-permute-start(bf16[4,16,16,128]{3,2,1,0:T(8,128)(2,1)S(1)} %line_gather.1.a_ref), channel_id=1, source_target_pairs={{0,1},{1,0},{2,3},{3,2},{4,5},{5,4},{6,7},{7,6},{8,9},{9,8},{10,11... | collective-permute-start | bytes 786440 | tf_op jit(solution)/shard_map/ppermute | solution.py:418
  69.0 1.0 %collective-permute-start.17 = (bf16[4,16,16,128]{3,2,1,0:T(8,128)(2,1)S(1)}, bf16[4,16,16,128]{3,2,1,0:T(8,128)(2,1)S(1)}, u32[]{:S(2)}, u32[]{:S(2)}) collective-permute-start(bf16[4,16,16,128]{3,2,1,0:T(8,128)(2,1)S(1)} %line_gather.1.a_ref), channel_id=1, source_target_pairs={{0,4},{1,5},{2,6},{3,7},{4,0},{5,1},{6,2},{7,3},{8,12},{9,13},{10,... | collective-permute-start | bytes 786440 | tf_op jit(solution)/shard_map/ppermute | solution.py:418
  70.0 6.6 %collective-permute-done.15.b_ref = bf16[4,16,16,128]{3,2,1,0:T(8,128)(2,1)S(1)} collective-permute-done((bf16[4,16,16,128]{3,2,1,0:T(8,128)(2,1)S(1)}, bf16[4,16,16,128]{3,2,1,0:T(8,128)(2,1)S(1)}, u32[]{:S(2)}, u32[]{:S(2)}) %collective-permute-start.15) | collective-permute-done | bytes 262176 | tf_op jit(solution)/shard_map/ppermute | solution.py:418
  76.6 3.9 %collective-permute-done.16.c_ref = bf16[4,16,16,128]{3,2,1,0:T(8,128)(2,1)S(1)} collective-permute-done((bf16[4,16,16,128]{3,2,1,0:T(8,128)(2,1)S(1)}, bf16[4,16,16,128]{3,2,1,0:T(8,128)(2,1)S(1)}, u32[]{:S(2)}, u32[]{:S(2)}) %collective-permute-start.16) | collective-permute-done | bytes 262176 | tf_op jit(solution)/shard_map/ppermute | solution.py:418
  80.5 0.1 plane_gather.1.half_ref
  80.5 0.1 collective-permute-start.18
  80.6 1.5 %finish.2 = (f32[9,256,256]{2,1,0:T(8,128)}, f32[3,256,256]{2,1,0:T(8,128)}, f32[4,256,256]{2,1,0:T(8,128)}) custom-call(bf16[16,16,16,128]{3,2,1,0:T(8,128)(2,1)S(1)} %plane_gather.1.half_ref), custom_call_target="tpu_custom_call" | custom-call | bytes 5242880 | tf_op jit(solution)/shard_map/finish/pallas_call | solution.py:394
  82.1 1.2 %collective-permute-done.18.half_ref = bf16[16,16,16,128]{3,2,1,0:T(8,128)(2,1)S(1)} collective-permute-done((bf16[16,16,16,128]{3,2,1,0:T(8,128)(2,1)S(1)}, bf16[16,16,16,128]{3,2,1,0:T(8,128)(2,1)S(1)}, u32[]{:S(2)}, u32[]{:S(2)}) %collective-permute-start.18) | collective-permute-done | bytes 1048608 | tf_op jit(solution)/shard_map/ppermute | solution.py:418
  83.3 1.5 %finish.3 = (f32[9,256,256]{2,1,0:T(8,128)}, f32[3,256,256]{2,1,0:T(8,128)}, f32[4,256,256]{2,1,0:T(8,128)}) custom-call(bf16[16,16,16,128]{3,2,1,0:T(8,128)(2,1)S(1)} %collective-permute-done.18.half_ref, f32[9,256,256]{2,1,0:T(8,128)} %get-tuple-element.65.rest_0_, ...), custom_call_target="tpu_custom_call", output_to_operand_aliasing={{0}: (1, {}), {1}: (2, {}), {2}: (3, {})} | custom-call | bytes 9437184 | tf_op jit(solution)/shard_map/finish/pallas_call | solution.py:394
  (20 shorter events, 0.1 us)
Async XLA Ops:
  1.3 1.2 %copy-start = (bf16[16,16,8,256]{3,2,1,0:T(8,128)(2,1)S(1)}, bf16[16,16,8,256]{3,2,1,0:T(8,128)(2,1)}, u32[]{:S(2)}) copy-start(bf16[16,16,8,256]{3,2,1,0:T(8,128)(2,1)} %param.6) | copy-start | bytes 3145732
  2.8 7.8 %collective-permute-start = (bf16[128,256]{1,0:T(8,128)(2,1)S(1)}, bf16[128,256]{1,0:T(8,128)(2,1)S(1)}, u32[]{:S(2)}, u32[]{:S(2)}) collective-permute-start(bf16[128,256]{1,0:T(8,128)(2,1)S(1)} %get-tuple-element.41), channel_id=1, source_target_pairs={{0,1},{1,0},{2,3},{3,2},{4,5},{5,4},{6,7},{7,6},{8,9},{9,8},{10,11... | collective-permute-start | bytes 196616 | tf_op jit(solution)/shard_map/ppermute | solution.py:461
  6.6 14.3 %collective-permute-start.1 = (bf16[2,8,4,256]{3,2,1,0:T(4,128)(2,1)S(1)}, bf16[2,8,4,256]{3,2,1,0:T(4,128)(2,1)S(1)}, u32[]{:S(2)}, u32[]{:S(2)}) collective-permute-start(bf16[2,8,4,256]{3,2,1,0:T(4,128)(2,1)S(1)} %slice.3), channel_id=1, source_target_pairs={{2,0},{4,2},{6,4},{8,6},{10,8},{12,10},{14,12},{16,14},{18,16},{20... | collective-permute-start | bytes 98312 | tf_op jit(solution)/shard_map/ppermute | solution.py:456
  7.9 1.2 %copy-start.1 = (bf16[16,16,8,256]{3,2,1,0:T(8,128)(2,1)S(1)}, bf16[16,16,8,256]{3,2,1,0:T(8,128)(2,1)}, u32[]{:S(2)}) copy-start(bf16[16,16,8,256]{3,2,1,0:T(8,128)(2,1)} %param.6) | copy-start | bytes 3145732
  10.6 1.3 %copy-start.3 = (bf16[3,3,256,256]{3,2,1,0:T(8,128)(2,1)S(1)}, bf16[3,3,256,256]{3,2,1,0:T(8,128)(2,1)}, u32[]{:S(2)}) copy-start(bf16[3,3,256,256]{3,2,1,0:T(8,128)(2,1)} %param.8) | copy-start | bytes 3538948
  11.9 9.0 %copy-start.2 = (bf16[16,8,4,256]{3,2,1,0:T(4,128)(2,1)S(1)}, bf16[16,8,4,256]{3,2,1,0:T(4,128)(2,1)}, u32[]{:S(2)}) copy-start(bf16[16,8,4,256]{3,2,1,0:T(4,128)(2,1)} %cot_ref.1) | copy-start | bytes 786436
  11.9 9.0 %copy-start.5 = (bf16[2,2,256,256]{3,2,1,0:T(8,128)(2,1)S(1)}, bf16[2,2,256,256]{3,2,1,0:T(8,128)(2,1)}, u32[]{:S(2)}) copy-start(bf16[2,2,256,256]{3,2,1,0:T(8,128)(2,1)} %param.10) | copy-start | bytes 1572868
  11.9 9.0 %copy-start.6 = (bf16[3,256,256]{2,1,0:T(8,128)(2,1)S(1)}, bf16[3,256,256]{2,1,0:T(8,128)(2,1)}, u32[]{:S(2)}) copy-start(bf16[3,256,256]{2,1,0:T(8,128)(2,1)} %wt_ref.5) | copy-start | bytes 1179652
  17.6 7.9 %collective-permute-start.3 = (bf16[8,32,256]{2,1,0:T(8,128)(2,1)S(1)}, bf16[8,32,256]{2,1,0:T(8,128)(2,1)S(1)}, u32[]{:S(2)}, u32[]{:S(2)}) collective-permute-start(bf16[8,32,256]{2,1,0:T(8,128)(2,1)S(1)} %get-tuple-element.43._), channel_id=1, source_target_pairs={{0,2},{2,4},{4,6},{6,8},{8,10},{10,12},{12,14},{14,16},{16,18},{18... | collective-permute-start | bytes 393224 | tf_op jit(solution)/shard_map/ppermute | solution.py:456
  25.6 5.1 %collective-permute-start.4 = (bf16[16,9,16,128]{3,2,1,0:T(8,128)(2,1)S(1)}, bf16[16,9,16,128]{3,2,1,0:T(8,128)(2,1)S(1)}, u32[]{:S(2)}, u32[]{:S(2)}) collective-permute-start(bf16[16,9,16,128]{3,2,1,0:T(8,128)(2,1)S(1)} %pass.2.rest_0_), channel_id=1, source_target_pairs={{0,2},{1,3},{2,0},{3,1},{4,6},{5,7},{6,4},{7,5},{8,10},{9,11},{10,... | collective-permute-start | bytes 1769480 | tf_op jit(solution)/shard_map/ppermute | solution.py:418
  26.8 3.9 %collective-permute-start.2 = (bf16[64,256]{1,0:T(8,128)(2,1)S(1)}, bf16[64,256]{1,0:T(8,128)(2,1)S(1)}, u32[]{:S(2)}, u32[]{:S(2)}) collective-permute-start(bf16[64,256]{1,0:T(8,128)(2,1)S(1)} %get-tuple-element.46), channel_id=1, source_target_pairs={{0,1},{1,0},{2,3},{3,2},{4,5},{5,4},{6,7},{7,6},{8,9},{9,8},{10,11... | collective-permute-start | bytes 98312 | tf_op jit(solution)/shard_map/ppermute | solution.py:461
  30.6 5.9 %copy-start.4 = (bf16[3,3,256,256]{3,2,1,0:T(8,128)(2,1)S(1)}, bf16[3,3,256,256]{3,2,1,0:T(8,128)(2,1)}, u32[]{:S(2)}) copy-start(bf16[3,3,256,256]{3,2,1,0:T(8,128)(2,1)} %param.8) | copy-start | bytes 3538948
  30.7 1.8 %collective-permute-start.5 = (bf16[16,7,16,128]{3,2,1,0:T(8,128)(2,1)S(1)}, bf16[16,7,16,128]{3,2,1,0:T(8,128)(2,1)S(1)}, u32[]{:S(2)}, u32[]{:S(2)}) collective-permute-start(bf16[16,7,16,128]{3,2,1,0:T(8,128)(2,1)S(1)} %pass.3), channel_id=1, source_target_pairs={{0,2},{1,3},{2,0},{3,1},{4,6},{5,7},{6,4},{7,5},{8,10},{9,11},{10,... | collective-permute-start | bytes 1376264 | tf_op jit(solution)/shard_map/ppermute | solution.py:418
  32.8 12.8 %collective-permute-start.6 = (bf16[4,16,16,128]{3,2,1,0:T(8,128)(2,1)S(1)}, bf16[4,16,16,128]{3,2,1,0:T(8,128)(2,1)S(1)}, u32[]{:S(2)}, u32[]{:S(2)}) collective-permute-start(bf16[4,16,16,128]{3,2,1,0:T(8,128)(2,1)S(1)} %get-tuple-element.58), channel_id=1, source_target_pairs={{0,5},{1,4},{2,7},{3,6},{4,1},{5,0},{6,3},{7,2},{8,13},{9,12},{10,... | collective-permute-start | bytes 786440 | tf_op jit(solution)/shard_map/ppermute | solution.py:418
  35.8 12.2 %collective-permute-start.7 = (bf16[4,16,16,128]{3,2,1,0:T(8,128)(2,1)S(1)}, bf16[4,16,16,128]{3,2,1,0:T(8,128)(2,1)S(1)}, u32[]{:S(2)}, u32[]{:S(2)}) collective-permute-start(bf16[4,16,16,128]{3,2,1,0:T(8,128)(2,1)S(1)} %get-tuple-element.59), channel_id=1, source_target_pairs={{0,1},{1,0},{2,3},{3,2},{4,5},{5,4},{6,7},{7,6},{8,9},{9,8},{10,11... | collective-permute-start | bytes 786440 | tf_op jit(solution)/shard_map/ppermute | solution.py:418
  36.4 11.7 %collective-permute-start.8 = (bf16[4,16,16,128]{3,2,1,0:T(8,128)(2,1)S(1)}, bf16[4,16,16,128]{3,2,1,0:T(8,128)(2,1)S(1)}, u32[]{:S(2)}, u32[]{:S(2)}) collective-permute-start(bf16[4,16,16,128]{3,2,1,0:T(8,128)(2,1)S(1)} %get-tuple-element.54.rest_0_), channel_id=1, source_target_pairs={{0,4},{1,5},{2,6},{3,7},{4,0},{5,1},{6,2},{7,3},{8,12},{9,13},{10,... | collective-permute-start | bytes 786440 | tf_op jit(solution)/shard_map/ppermute | solution.py:418
  48.2 6.5 %collective-permute-start.9 = (bf16[16,16,128]{2,1,0:T(8,128)(2,1)S(1)}, bf16[16,16,128]{2,1,0:T(8,128)(2,1)S(1)}, u32[]{:S(2)}, u32[]{:S(2)}) collective-permute-start(bf16[16,16,128]{2,1,0:T(8,128)(2,1)S(1)} %get-tuple-element.62), channel_id=1, source_target_pairs={{0,24},{1,25},{2,26},{3,27},{4,28},{5,29},{6,30},{7,31},{8,16},{9,... | collective-permute-start | bytes 196616 | tf_op jit(solution)/shard_map/ppermute | solution.py:418
  51.6 6.0 %collective-permute-start.10 = (bf16[16,16,128]{2,1,0:T(8,128)(2,1)S(1)}, bf16[16,16,128]{2,1,0:T(8,128)(2,1)S(1)}, u32[]{:S(2)}, u32[]{:S(2)}) collective-permute-start(bf16[16,16,128]{2,1,0:T(8,128)(2,1)S(1)} %get-tuple-element.63), channel_id=1, source_target_pairs={{0,16},{1,17},{2,18},{3,19},{4,20},{5,21},{6,22},{7,23},{8,24},{9,... | collective-permute-start | bytes 196616 | tf_op jit(solution)/shard_map/ppermute | solution.py:418
  51.6 6.0 %collective-permute-start.11 = (bf16[16,16,128]{2,1,0:T(8,128)(2,1)S(1)}, bf16[16,16,128]{2,1,0:T(8,128)(2,1)S(1)}, u32[]{:S(2)}, u32[]{:S(2)}) collective-permute-start(bf16[16,16,128]{2,1,0:T(8,128)(2,1)S(1)} %get-tuple-element.64), channel_id=1, source_target_pairs={{0,8},{1,9},{2,10},{3,11},{4,12},{5,13},{6,14},{7,15},{8,0},{9,1},... | collective-permute-start | bytes 196616 | tf_op jit(solution)/shard_map/ppermute | solution.py:418
  57.6 6.5 %collective-permute-start.12 = (bf16[16,16,128]{2,1,0:T(8,128)(2,1)S(1)}, bf16[16,16,128]{2,1,0:T(8,128)(2,1)S(1)}, u32[]{:S(2)}, u32[]{:S(2)}) collective-permute-start(bf16[16,16,128]{2,1,0:T(8,128)(2,1)S(1)} %line_sum.1.a_ref), channel_id=1, source_target_pairs={{0,24},{1,25},{2,26},{3,27},{4,28},{5,29},{6,30},{7,31},{8,16},{9,... | collective-permute-start | bytes 196616 | tf_op jit(solution)/shard_map/ppermute | solution.py:418
  60.3 6.1 %collective-permute-start.13 = (bf16[16,16,128]{2,1,0:T(8,128)(2,1)S(1)}, bf16[16,16,128]{2,1,0:T(8,128)(2,1)S(1)}, u32[]{:S(2)}, u32[]{:S(2)}) collective-permute-start(bf16[16,16,128]{2,1,0:T(8,128)(2,1)S(1)} %line_sum.1.a_ref), channel_id=1, source_target_pairs={{0,16},{1,17},{2,18},{3,19},{4,20},{5,21},{6,22},{7,23},{8,24},{9,... | collective-permute-start | bytes 196616 | tf_op jit(solution)/shard_map/ppermute | solution.py:418
  60.3 6.1 %collective-permute-start.14 = (bf16[16,16,128]{2,1,0:T(8,128)(2,1)S(1)}, bf16[16,16,128]{2,1,0:T(8,128)(2,1)S(1)}, u32[]{:S(2)}, u32[]{:S(2)}) collective-permute-start(bf16[16,16,128]{2,1,0:T(8,128)(2,1)S(1)} %line_sum.1.a_ref), channel_id=1, source_target_pairs={{0,8},{1,9},{2,10},{3,11},{4,12},{5,13},{6,14},{7,15},{8,0},{9,1},... | collective-permute-start | bytes 196616 | tf_op jit(solution)/shard_map/ppermute | solution.py:418
  66.4 10.2 %collective-permute-start.15 = (bf16[4,16,16,128]{3,2,1,0:T(8,128)(2,1)S(1)}, bf16[4,16,16,128]{3,2,1,0:T(8,128)(2,1)S(1)}, u32[]{:S(2)}, u32[]{:S(2)}) collective-permute-start(bf16[4,16,16,128]{3,2,1,0:T(8,128)(2,1)S(1)} %line_gather.1.a_ref), channel_id=1, source_target_pairs={{0,5},{1,4},{2,7},{3,6},{4,1},{5,0},{6,3},{7,2},{8,13},{9,12},{10,... | collective-permute-start | bytes 786440 | tf_op jit(solution)/shard_map/ppermute | solution.py:418
  67.7 12.7 %collective-permute-start.16 = (bf16[4,16,16,128]{3,2,1,0:T(8,128)(2,1)S(1)}, bf16[4,16,16,128]{3,2,1,0:T(8,128)(2,1)S(1)}, u32[]{:S(2)}, u32[]{:S(2)}) collective-permute-start(bf16[4,16,16,128]{3,2,1,0:T(8,128)(2,1)S(1)} %line_gather.1.a_ref), channel_id=1, source_target_pairs={{0,1},{1,0},{2,3},{3,2},{4,5},{5,4},{6,7},{7,6},{8,9},{9,8},{10,11... | collective-permute-start | bytes 786440 | tf_op jit(solution)/shard_map/ppermute | solution.py:418
  69.0 11.4 %collective-permute-start.17 = (bf16[4,16,16,128]{3,2,1,0:T(8,128)(2,1)S(1)}, bf16[4,16,16,128]{3,2,1,0:T(8,128)(2,1)S(1)}, u32[]{:S(2)}, u32[]{:S(2)}) collective-permute-start(bf16[4,16,16,128]{3,2,1,0:T(8,128)(2,1)S(1)} %line_gather.1.a_ref), channel_id=1, source_target_pairs={{0,4},{1,5},{2,6},{3,7},{4,0},{5,1},{6,2},{7,3},{8,12},{9,13},{10,... | collective-permute-start | bytes 786440 | tf_op jit(solution)/shard_map/ppermute | solution.py:418
  80.5 2.7 %collective-permute-start.18 = (bf16[16,16,16,128]{3,2,1,0:T(8,128)(2,1)S(1)}, bf16[16,16,16,128]{3,2,1,0:T(8,128)(2,1)S(1)}, u32[]{:S(2)}, u32[]{:S(2)}) collective-permute-start(bf16[16,16,16,128]{3,2,1,0:T(8,128)(2,1)S(1)} %plane_gather.1.half_ref), channel_id=1, source_target_pairs={{0,2},{1,3},{2,0},{3,1},{4,6},{5,7},{6,4},{7,5},{8,10},{9,11},{10,... | collective-permute-start | bytes 3145736 | tf_op jit(solution)/shard_map/ppermute | solution.py:418

commit v9 on v8

--- a/solution.py
+++ b/solution.py
@@ -84,8 +84,9 @@
     send_ref[:, k] = jnp.where(core == 0, high, low).reshape(16, 16, CH // 2)
 
 
-def edges_kernel(bands, count_ref, x_ref, *rest):
-    outs, token_ref = rest[:-1], rest[-1]
+def edges_kernel(bands, count_ref, x_ref, cot_ref, *rest):
+    outs, (nxt_ref, token_ref) = rest[:-2], rest[-2:]
+    nxt_ref[...] = cot_ref[0:2]
     token_ref[...] = jnp.zeros_like(token_ref)
     count = count_ref[0]
     band = lax.axis_index("grp")
@@ -127,7 +128,7 @@
 
 
 def spatial_kernel(
-    bands, count_ref, top_ref, bot_ref, acts_in, ws_ref, acts_ref, sp_ref, edge_ref
+    bands, count_ref, top_ref, bot_ref, acts_in, ws_ref, _, acts_ref, sp_ref, edge_ref, sum_ref
 ):
     count = count_ref[0]
     band = lax.axis_index("grp")
@@ -139,23 +140,25 @@
     pick = ((a >> 1) == (b >> 4)) & ((b & 15) == count - 2 + (a & 1))
     pick = jnp.where(pick, 1.0, 0.0).astype(BF)
 
-    def rows_of(q, _):
-        left = [
-            acts_ref[pl.ds(4 * q + i, 4), j : j + cols].reshape(4 * cols * SLOTS, CH)
-            for i in range(3)
-            for j in range(3)
-        ]
-        out = mm(jnp.concatenate(left, axis=1), ws_ref[...].reshape(9 * CH, CH)).astype(BF)
-        sp_ref[pl.ds(4 * q, 4)] = out.reshape(4, cols, SLOTS, CH)
-        for half in range(2):
-            edge_ref[2 * q + half] = mm(pick, out[half * 256 : half * 256 + 256]).astype(BF)
-        return 0
-
-    lax.fori_loop(0, rows // 4, rows_of, 0, unroll=2)
+    high = rows // 2
+    for q in range(2):
+        for i in range(3):
+            for j in range(3):
+                left = acts_ref[high * q + i : high * q + i + high, j : j + cols]
+                term = mm(left.reshape(high * cols * SLOTS, CH), ws_ref[i * 3 + j])
+                if i + j == 0:
+                    sum_ref[...] = term
+                elif i + j < 4:
+                    sum_ref[...] += term
+                else:
+                    out = (sum_ref[...] + term).astype(BF)
+        sp_ref[high * q : high * q + high] = out.reshape(high, cols, SLOTS, CH)
+        for k in range(high // 2):
+            edge_ref[high // 2 * q + k] = mm(pick, out[k * 256 : k * 256 + 256]).astype(BF)
 
 
 def grad_spatial_kernel(
-    bands, count_ref, at_in, top_ref, bot_ref, cot_ref, nxt_ref, wt_ref, wd_ref, _,
+    bands, count_ref, at_in, top_ref, bot_ref, cot_ref, nxt_ref, wt_ref, wd_ref,
     at_ref, cott_ref, gy_ref, gs_ref, keep_ref, send_ref, *edge_refs,
 ):
     count = count_ref[0]
@@ -170,19 +173,21 @@
     gs_ref[:, cols + 1] = edge
 
     place_next = to_slots(16, SLOTS, own_and_next(count))
+    halves = []
     for q in range(rows * cols // 64):
         four = slice(q * 4, q * 4 + 4)
         piece = jnp.concatenate(
             [cot_ref[0:OWN, four].reshape(OWN, 16, CH), nxt_ref[:, four].reshape(2, 16, CH)], 0
         ).reshape(SLOTS * 16, CH)
-        placed = mm(place_next, piece).astype(BF)
-        cott_ref[q * 4 : q * 4 + 4] = placed.reshape(4, 4, SLOTS, CH)
-        for i in range(2):
-            for j in range(2):
-                g = mm_nt(placed, wd_ref[i * 2 + j]).astype(BF).reshape(4, 4, SLOTS, CH)
-                for r in range(4):
-                    for c in range(4):
-                        gy_ref[2 * (q * 4 + r) + i, 2 * c + j] = g[r, c]
+        halves.append(mm(place_next, piece).astype(BF))
+    placed = jnp.concatenate(halves, 0)
+    cott_ref[...] = placed.reshape(rows // 2, cols // 2, SLOTS, CH)
+    for i in range(2):
+        for j in range(2):
+            g = mm_nt(placed, wd_ref[i * 2 + j]).astype(BF).reshape(rows // 2, cols // 2, SLOTS, CH)
+            for r in range(rows // 2):
+                for c in range(cols // 2):
+                    gy_ref[2 * r + i, 2 * c + j] = g[r, c]
     last = cott_ref[rows // 2 - 1].reshape(cols // 2 * SLOTS, CH)
     first = cott_ref[0].reshape(cols // 2 * SLOTS, CH)
     if bands == 2:
@@ -192,14 +197,14 @@
         edge_refs[1][...] = first
 
     def grads_of(q, _):
-        g = gy_ref[pl.ds(4 * q, 4)].reshape(4 * cols, SLOTS, CH)
+        g = gy_ref[pl.ds(8 * q, 8)].reshape(8 * cols, SLOTS, CH)
         s = grad_of_temporal(g, wt_ref, count)
-        gs_ref[pl.ds(4 * q, 4), 1 : cols + 1] = s.reshape(4, cols, SLOTS, CH)
+        gs_ref[pl.ds(8 * q, 8), 1 : cols + 1] = s.reshape(8, cols, SLOTS, CH)
         g = jnp.where(slot_mask(g.shape, count), g.astype(F32), 0.0)
-        gy_ref[pl.ds(4 * q, 4)] = g.astype(BF).reshape(4, cols, SLOTS, CH)
+        gy_ref[pl.ds(8 * q, 8)] = g.astype(BF).reshape(8, cols, SLOTS, CH)
         return 0
 
-    lax.fori_loop(0, rows // 4, grads_of, 0, unroll=2)
+    lax.fori_loop(0, rows // 8, grads_of, 0)
 
     wide = rows * cols * SLOTS
     for j in range(3):
@@ -220,23 +225,23 @@
     place = jnp.where(place, 1.0, 0.0).astype(BF)
 
     def rows_of(q, _):
-        s = sp_ref[pl.ds(4 * q, 4)].reshape(4 * cols * SLOTS, CH).astype(F32)
-        s = s + jnp.concatenate([mm(place, prev_ref[2 * q]), mm(place, prev_ref[2 * q + 1])], 0)
-        s = s.reshape(4 * cols, SLOTS, CH)
+        s = sp_ref[pl.ds(8 * q, 8)].reshape(8 * cols * SLOTS, CH).astype(F32)
+        s = s + jnp.concatenate([mm(place, prev_ref[4 * q + k]) for k in range(4)], 0)
+        s = s.reshape(8 * cols, SLOTS, CH)
         total = None
         for k in range(3):
             shifted = s if k == 2 else pltpu.roll(s, 2 - k, 1)
-            shifted = shifted.astype(BF).reshape(4 * cols * SLOTS, CH)
-            at = pl.ds(pl.multiple_of(q * 512, 512), 512)
+            shifted = shifted.astype(BF).reshape(8 * cols * SLOTS, CH)
+            at = pl.ds(pl.multiple_of(q * 1024, 1024), 1024)
             st_ref[k * CH : k * CH + CH, at] = shifted.T
             term = mm(shifted, wt_ref[k])
             total = term if total is None else total + term
-        x = xt_ref[pl.ds(4 * q, 4)].reshape(4 * cols, SLOTS, CH).astype(F32)
+        x = xt_ref[pl.ds(8 * q, 8)].reshape(8 * cols, SLOTS, CH).astype(F32)
         y = jnp.where(slot_mask(x.shape, count), x + total.reshape(x.shape), 0.0).astype(BF)
-        y_ref[pl.ds(4 * q, 4)] = y.reshape(4, cols, SLOTS, CH)
+        y_ref[pl.ds(8 * q, 8)] = y.reshape(8, cols, SLOTS, CH)
         return 0
 
-    lax.fori_loop(0, rows // 4, rows_of, 0, unroll=2)
+    lax.fori_loop(0, rows // 8, rows_of, 0)
 
     wide = rows * cols * SLOTS
     value = mm(st_ref[...], gy_ref[...].reshape(wide, CH))
@@ -307,7 +312,7 @@
             buf[:, pl.ds(pl.multiple_of((2 * q + k) * 16, 16), 16), :] = o.reshape(SLOTS, 16, CH)
         return 0
 
-    lax.fori_loop(0, rows // 4, rows_of, 0, unroll=2)
+    lax.fori_loop(0, rows // 4, rows_of, 0)
     copy = pltpu.make_async_copy(buf, out_ref, sems.at[0])
     copy.start()
     for q in range(down_ref.shape[1] // 4):
@@ -319,21 +324,23 @@
 ORDER = (0, 3, 2, 1)
 
 
-def plane_send_kernel(keep_a, got_a, keep_b, got_b, *outs):
+def plane_send_kernel(keep_ref, got_ref, *rest):
     _, p, _ = place_bits()
-    n = keep_a.shape[1]
-    for r, out in zip(ORDER, outs):
+    for r, out in zip(ORDER, rest[-4:]):
         at = pl.ds((p ^ r) * 4, 4)
-        out[:, :n] = (keep_a[at].astype(F32) + got_a[at].astype(F32)).astype(BF)
-        out[:, n:] = (keep_b[at].astype(F32) + got_b[at].astype(F32)).astype(BF)
-
-
-def line_send_kernel(a_ref, b_ref, c_ref, d_ref, *rest):
-    outs = rest[-4:]
+        out[...] = (keep_ref[at].astype(F32) + got_ref[at].astype(F32)).astype(BF)
+
+
+def line_send_kernel(*refs):
+    outs = refs[8:]
     _, _, z = place_bits()
-    for k, r in enumerate(ORDER):
-        parts = [ref[z ^ r].astype(F32) for ref in (a_ref, b_ref, c_ref, d_ref)]
-        outs[k][...] = (parts[0] + parts[1] + parts[2] + parts[3]).astype(BF)
+    for out, r in zip(outs, ORDER):
+        at = 0
+        for chain in (refs[:4], refs[4:8]):
+            parts = [ref[z ^ r].astype(F32) for ref in chain]
+            n = parts[0].shape[0]
+            out[at : at + n] = (parts[0] + parts[1] + parts[2] + parts[3]).astype(BF)
+            at += n
 
 
 def line_sum_kernel(a_ref, b_ref, c_ref, d_ref, out_ref):
@@ -347,7 +354,7 @@
         out_ref[z ^ r] = ref[...]
 
 
-def plane_gather_kernel(a_ref, b_ref, c_ref, d_ref, out_ref):
+def plane_gather_kernel(a_ref, b_ref, c_ref, d_ref, _, out_ref):
     _, p, _ = place_bits()
     for r, ref in zip(ORDER, (a_ref, b_ref, c_ref, d_ref)):
         out_ref[pl.ds((p ^ r) * 4, 4)] = ref[...]
@@ -431,6 +438,12 @@
     ]
 
 
+def plane_send(keep, got, after):
+    ins = [(VMEM, keep), (VMEM, got)] + [(ANY, a) for a in after]
+    shape = (4, keep.shape[1], 16, CH // 2)
+    return list(call(plane_send_kernel, "plane_send", ins, [(VMEM, shape)] * 4))
+
+
 def passed(value, after):
     ins = [(ANY, value)] + [(ANY, a) for a in after]
     return call(pass_kernel, "pass", ins, [(ANY, value.shape)], alias={0: 0})[0]
@@ -477,15 +490,15 @@
     dma = pltpu.SemaphoreType.DMA
 
     sides = 1 if grp == 2 else 2
-    *edge, token = call(
+    *edge, nxt, token = call(
         functools.partial(edges_kernel, grp),
         "edges",
-        [count, (VMEM, x)],
-        [(VMEM, (cols * slots, ch))] * sides + [TOKEN],
+        [count, (VMEM, x), (VMEM, cotangent)],
+        [(VMEM, (cols * slots, ch))] * sides + [(VMEM, (2,) + cotangent.shape[1:]), TOKEN],
         flops=tap // 8,
     )
     top, bot = from_bands(edge)
-    nxt_got = along(cotangent[:2], "tm", -1)
+    nxt_got = along(nxt, "tm", -1)
     xt, acts, at = call(
         acts_kernel,
         "acts",
@@ -493,64 +506,50 @@
         [(VMEM, tile), (VMEM, padded), (VMEM, (3 * ch, (rows + 4) * 128))],
         flops=2 * tap,
     )
-    acts, sp, last_two = call(
-        functools.partial(spatial_kernel, grp),
-        "spatial",
-        [count, (VMEM, top), (VMEM, bot), (VMEM, acts), (VMEM, ws)],
-        [(VMEM, padded), (VMEM, tile), (VMEM, (rows // 2, 32, ch))],
-        flops=9 * tap,
-        alias={3: 0},
-    )
-    prev = along(last_two, "tm", 1)
     half = (16, 9, 16, ch // 2)
     at, cott, gy, gs, keep_a, send_a, *edge = call(
         functools.partial(grad_spatial_kernel, grp),
         "grad_spatial",
-        [count, (VMEM, at), (VMEM, top), (VMEM, bot), (VMEM, cotangent), (VMEM, nxt_got), (VMEM, wt), (VMEM, wd),
-         (ANY, last_two)],
+        [count, (VMEM, at), (VMEM, top), (VMEM, bot), (VMEM, cotangent), (VMEM, nxt_got), (VMEM, wt), (VMEM, wd)],
         [(VMEM, at.shape), (VMEM, (rows // 2, cols // 2, slots, ch)), (VMEM, tile),
          (VMEM, (rows, cols + 2, slots, ch)), (VMEM, half), (VMEM, half)]
         + [(VMEM, (cols // 2 * slots, ch))] * sides,
         flops=14 * tap,
         alias={1: 0},
     )
-    send_a = passed(send_a, [prev])
     got_a = core_round(send_a, tm, grp)
     cot_top, cot_bot = from_bands(edge)
+    acts, sp, last_two = call(
+        functools.partial(spatial_kernel, grp),
+        "spatial",
+        [count, (VMEM, top), (VMEM, bot), (VMEM, acts), (VMEM, ws), (ANY, send_a)],
+        [(VMEM, padded), (VMEM, tile), (VMEM, (rows // 2, 32, ch))],
+        [pltpu.VMEM((slots * wide // 2, ch), F32)],
+        flops=9 * tap,
+        alias={3: 0},
+    )
+    prev = along(last_two, "tm", 1)
+    _, plane, line, others = plan(tm, grp)
+    parts_a = plane_send(keep_a, got_a, [last_two])
     half = (16, 7, 16, ch // 2)
     down, keep_b, send_b = call(
         forward_kernel,
         "forward",
         [count, (VMEM, xt), (VMEM, sp), (VMEM, prev), (VMEM, cott), (VMEM, gy), (VMEM, wt), (VMEM, wd),
-         (ANY, send_a)],
+         *((ANY, a) for a in parts_a)],
         [(VMEM, (slots * wide // 4, ch)), (VMEM, half), (VMEM, half)],
         [pltpu.VMEM(v, BF) for v in (tile, (3 * ch, slots * wide), (4 * ch, slots * wide // 4))],
         flops=10 * tap,
         grant=14,
     )
-    send_b = passed(send_b, [got_a, cot_top, cot_bot][: 1 + sides])
-    got_b = core_round(send_b, tm, grp)
-    _, plane, line, others = plan(tm, grp)
-    parts = call(
-        plane_send_kernel,
-        "plane_send",
-        [(VMEM, a) for a in (keep_a, got_a, keep_b, got_b)],
-        [(VMEM, (4, 16, 16, ch // 2))] * 4,
-    )
-    grad_x, down, token = call(
-        functools.partial(grad_x_kernel, grp),
-        "grad_x",
-        [count, (VMEM, xt), (VMEM, gy), (VMEM, gs), (VMEM, cot_top), (VMEM, cot_bot), (VMEM, wt),
-         (VMEM, wd), (VMEM, ws), (VMEM, down), (ANY, parts[3])],
-        [(HBM, (slots, wide, ch)), (VMEM, cotangent.shape), TOKEN],
-        [pltpu.VMEM(padded, BF), pltpu.VMEM((slots, wide, ch), BF), dma((1,))],
-        flops=10 * tap,
-    )
-    parts = four_round(list(parts), plane, tm, grp)
+    parts_a = four_round(parts_a, plane, tm, grp)
+    send_b = passed(send_b, parts_a[1:] + [cot_top, cot_bot][:sides])
+    parts_b = plane_send(keep_b, core_round(send_b, tm, grp), [])
+    parts_b = four_round(parts_b, plane, tm, grp)
     parts = call(
         line_send_kernel,
         "line_send",
-        [(VMEM, a) for a in parts] + [(ANY, token)],
+        [(VMEM, a) for a in parts_a + parts_b],
         [(VMEM, (16, 16, ch // 2))] * 4,
     )
     parts = four_round(list(parts), line, tm, grp)
@@ -563,7 +562,16 @@
         line_gather_kernel, "line_gather", [(VMEM, a) for a in parts], [(VMEM, (4,) + mine.shape)]
     )
     parts = four_round([mine] * 4, plane, tm, grp)
-    ins = [(VMEM, a) for a in parts]
+    grad_x, down, token = call(
+        functools.partial(grad_x_kernel, grp),
+        "grad_x",
+        [count, (VMEM, xt), (VMEM, gy), (VMEM, gs), (VMEM, cot_top), (VMEM, cot_bot), (VMEM, wt),
+         (VMEM, wd), (VMEM, ws), (VMEM, down), (ANY, mine)],
+        [(HBM, (slots, wide, ch)), (VMEM, cotangent.shape), TOKEN],
+        [pltpu.VMEM(padded, BF), pltpu.VMEM((slots, wide, ch), BF), dma((1,))],
+        flops=10 * tap,
+    )
+    ins = [(VMEM, a) for a in parts] + [(ANY, token)]
     (mine,) = call(plane_gather_kernel, "plane_gather", ins, [(VMEM, (16,) + mine.shape[1:])])
     got = core_round(mine, tm, grp)
     outs = finish(True, mine, [])

time: 85.2 us -> 82.8 us (0.972)
  starting transfers between devices: 25.5 us -> 29 us
  local copies, waits for them, and re-layouts: 4.49 us -> 2.18 us
  Pallas kernels: 27.9 us -> 25.6 us
  waiting for transfers between devices: 25.4 us -> 24.3 us
    ppermute x15 -> x18, starting transfers between devices: 17.4 us -> 22 us  [swap(): return lax.ppermute(value, AXES, [(d, d ^ flip) for d in range(tm * grp)])]
    pallas_call x15, Pallas kernels: 27.9 us -> 25.6 us  [call(): pl.pallas_call(kernel, out_shape=shapes, in_specs=[s for s, _ in ins], ou...]
    unnamed x14 -> x12, local copies, waits for them, and re-layouts: 3.72 us -> 2.18 us
    ppermute x15 -> x18, waiting for transfers between devices: 25.2 us -> 23.9 us  [swap(): return lax.ppermute(value, AXES, [(d, d ^ flip) for d in range(tm * grp)])]
    ppermute x2, starting transfers between devices: 4.51 us -> 3.4 us  [along(): return lax.ppermute(value, axis, pairs)]
  transfers between devices with their start and end apart: 19 -> 22, of which waited for: 10 -> 13; matrix products, arithmetic and copies ran while one was open for 1% -> 0% of each run, Pallas kernels for 30% -> 23%
where the time goes in v9:
time: 82.8 us; the launch traced here: 82.6 us
  starting transfers between devices  29 us (35%)
  Pallas kernels  25.6 us (31%)
  waiting for transfers between devices  24.3 us (29%)
  local copies, waits for them, and re-layouts  2.18 us (3%)
  between operations  1.6 us (2%)
    pallas_call x15, Pallas kernels, call(): pl.pallas_call(kernel, out_shape=shapes, in_specs=[s for s, _ in ins], ou...  25.6 us
    ppermute x18, waiting for transfers between devices, swap(): return lax.ppermute(value, AXES, [(d, d ^ flip) for d in range(tm * grp)])  23.9 us
    ppermute x18, starting transfers between devices, swap(): return lax.ppermute(value, AXES, [(d, d ^ flip) for d in range(tm * grp)])  22 us
    ppermute x2, starting transfers between devices, from_bands(): got = lax.ppermute(parts[0], 'grp', [(0, 1), (1, 0)])  3.6 us
    ppermute x2, starting transfers between devices, along(): return lax.ppermute(value, axis, pairs)  3.4 us
    unnamed x12, local copies, waits for them, and re-layouts  2.18 us
  transfers between devices with their start and end apart: 22, of which 13 were waited for; matrix products, arithmetic and copies ran while one was open for 0% of the time, Pallas kernels for 23%

profile of v9, /device:TPU:0, one launch (start us, length us, event | category | flops | bytes accessed | tf_op | source)
XLA Modules:
  0.0 82.6 jit_solution(5704760186245933026)
XLA Ops:
  1.3 1.2 %copy-done = bf16[16,16,8,256]{3,2,1,0:T(8,128)(2,1)S(1)} copy-done((bf16[16,16,8,256]{3,2,1,0:T(8,128)(2,1)S(1)}, bf16[16,16,8,256]{3,2,1,0:T(8,128)(2,1)}, u32[]{:S(2)}) %copy-start) | copy-done | bytes 1048600
  2.5 0.9 %copy-done.1 = bf16[16,8,4,256]{3,2,1,0:T(4,128)(2,1)S(1)} copy-done((bf16[16,8,4,256]{3,2,1,0:T(4,128)(2,1)S(1)}, bf16[16,8,4,256]{3,2,1,0:T(4,128)(2,1)}, u32[]{:S(2)}) %copy-start.1) | copy-done | bytes 262168
  3.5 0.3 edges.1
  3.8 3.0 %collective-permute-start = (bf16[128,256]{1,0:T(8,128)(2,1)S(1)}, bf16[128,256]{1,0:T(8,128)(2,1)S(1)}, u32[]{:S(2)}, u32[]{:S(2)}) collective-permute-start(bf16[128,256]{1,0:T(8,128)(2,1)S(1)} %get-tuple-element.46), channel_id=1, source_target_pairs={{0,1},{1,0},{2,3},{3,2},{4,5},{5,4},{6,7},{7,6},{8,9},{9,8},{10,11... | collective-permute-start | bytes 196616 | tf_op jit(solution)/shard_map/ppermute | solution.py:474
  6.8 1.3 %collective-permute-start.1 = (bf16[2,8,4,256]{3,2,1,0:T(4,128)(2,1)S(1)}, bf16[2,8,4,256]{3,2,1,0:T(4,128)(2,1)S(1)}, u32[]{:S(2)}, u32[]{:S(2)}) collective-permute-start(bf16[2,8,4,256]{3,2,1,0:T(4,128)(2,1)S(1)} %get-tuple-element.47), channel_id=1, source_target_pairs={{2,0},{4,2},{6,4},{8,6},{10,8},{12,10},{14,12},{16,14},{18,16},{20... | collective-permute-start | bytes 98312 | tf_op jit(solution)/shard_map/ppermute | solution.py:469
  8.1 1.5 %acts.1 = (bf16[16,8,16,256]{3,2,1,0:T(8,128)(2,1)S(1)}, bf16[18,10,16,256]{3,2,1,0:T(8,128)(2,1)S(1)}, bf16[768,2560]{1,0:T(8,128)(2,1)S(1)}) custom-call(s32[1]{0:T(128)S(6)} %copy.23.count_ref, bf16[16,128,256]{2,1,0:T(8,128)(2,1)S(1)} %bitcast.7, f32[8,128]{1,0:T(8,128)S(1)} %get-tuple-element.43._), custom_call_target="tpu_custom_call" | custom-call | flops 536870912 | bytes 7503876 | tf_op jit(solution)/shard_map/acts/pallas_call | solution.py:401
  9.6 0.3 collective-permute-done.1.nxt_ref
  9.9 4.5 %grad_spatial.1 = (bf16[768,2560]{1,0:T(8,128)(2,1)S(1)}, bf16[8,4,16,256]{3,2,1,0:T(8,128)(2,1)S(1)}, bf16[16,8,16,256]{3,2,1,0:T(8,128)(2,1)S(1)}, bf16[16,10,...) custom-call(s32[1]{0:T(128)S(6)} %copy.23.count_ref, ...), custom_call_target="tpu_custom_call", output_to_operand_aliasing={{0}: (1, {})} | custom-call | flops 3758096384 | bytes 13041668 | tf_op jit(solution)/shard_map/grad_spatial/pallas_call | solution.py:401
  14.4 2.1 %collective-permute-start.4 = (bf16[16,9,16,128]{3,2,1,0:T(8,128)(2,1)S(1)}, bf16[16,9,16,128]{3,2,1,0:T(8,128)(2,1)S(1)}, u32[]{:S(2)}, u32[]{:S(2)}) collective-permute-start(bf16[16,9,16,128]{3,2,1,0:T(8,128)(2,1)S(1)} %get-tuple-element.52._), channel_id=1, source_target_pairs={{0,2},{1,3},{2,0},{3,1},{4,6},{5,7},{6,4},{7,5},{8,10},{9,11},{10,... | collective-permute-start | bytes 1769480 | tf_op jit(solution)/shard_map/ppermute | solution.py:425
  16.5 5.3 %spatial.1 = (bf16[18,10,16,256]{3,2,1,0:T(8,128)(2,1)S(1)}, bf16[16,8,16,256]{3,2,1,0:T(8,128)(2,1)S(1)}, bf16[8,32,256]{2,1,0:T(8,128)(2,1)S(1)}) custom-call(s32[1]{0:T(128)S(6)} %copy.23.count_ref, bf16[128,256]{1,0:T(8,128)(2,1)S(1)} %collective-permute-done.top_ref.bot_ref, ...), custom_call_target="tpu_custom_call", output_to_operand_aliasing={{0}: (3, {})} | custom-call | flops 2415919104 | bytes 5439492 | tf_op jit(solution)/shard_map/spatial/pallas_call | solution.py:401
  21.8 2.1 %collective-permute-start.3 = (bf16[8,32,256]{2,1,0:T(8,128)(2,1)S(1)}, bf16[8,32,256]{2,1,0:T(8,128)(2,1)S(1)}, u32[]{:S(2)}, u32[]{:S(2)}) collective-permute-start(bf16[8,32,256]{2,1,0:T(8,128)(2,1)S(1)} %get-tuple-element.54.rest_0_), channel_id=1, source_target_pairs={{0,2},{2,4},{4,6},{6,8},{8,10},{10,12},{12,14},{14,16},{16,18},{18... | collective-permute-start | bytes 393224 | tf_op jit(solution)/shard_map/ppermute | solution.py:469
  23.9 0.6 collective-permute-start.2
  24.5 0.1 plane_send.2
  24.6 3.1 %collective-permute-start.5 = (bf16[4,9,16,128]{3,2,1,0:T(8,128)(2,1)S(1)}, bf16[4,9,16,128]{3,2,1,0:T(8,128)(2,1)S(1)}, u32[]{:S(2)}, u32[]{:S(2)}) collective-permute-start(bf16[4,9,16,128]{3,2,1,0:T(8,128)(2,1)S(1)} %get-tuple-element.58.rest_1_), channel_id=1, source_target_pairs={{0,5},{1,4},{2,7},{3,6},{4,1},{5,0},{6,3},{7,2},{8,13},{9,12},{10,... | collective-permute-start | bytes 442376 | tf_op jit(solution)/shard_map/ppermute | solution.py:425
  27.7 0.5 collective-permute-start.6
  28.2 0.1 collective-permute-start.7
  28.4 3.1 %forward.1 = (bf16[512,256]{1,0:T(8,128)(2,1)S(1)}, bf16[16,7,16,128]{3,2,1,0:T(8,128)(2,1)S(1)}, bf16[16,7,16,128]{3,2,1,0:T(8,128)(2,1)S(1)}) custom-call(s32[1]{0:T(128)S(6)} %copy.23.count_ref, bf16[16,8,16,256]{3,2,1,0:T(8,128)(2,1)S(1)} %get-tuple-element.44.xt_ref, bf16[16,8,16,256]{3,2,1,0:T(8,128)(2,1)S(1)} %get-tuple-element.53.sp_ref, ...), custom_call_target="tpu_custom_call" | custom-call | flops 2684354560 | bytes 5636100 | tf_op jit(solution)/shard_map/forward/pallas_call | solution.py:401
  31.5 0.5 collective-permute-done.5.__1_.refs_1_
  32.0 3.6 %collective-permute-done.6.__2_.refs_2_ = bf16[4,9,16,128]{3,2,1,0:T(8,128)(2,1)S(1)} collective-permute-done((bf16[4,9,16,128]{3,2,1,0:T(8,128)(2,1)S(1)}, bf16[4,9,16,128]{3,2,1,0:T(8,128)(2,1)S(1)}, u32[]{:S(2)}, u32[]{:S(2)}) %collective-permute-start.6) | collective-permute-done | bytes 147488 | tf_op jit(solution)/shard_map/ppermute | solution.py:425
  35.6 0.1 collective-permute-start.8
  35.7 1.7 %collective-permute-done.8.got_ref = bf16[16,7,16,128]{3,2,1,0:T(8,128)(2,1)S(1)} collective-permute-done((bf16[16,7,16,128]{3,2,1,0:T(8,128)(2,1)S(1)}, bf16[16,7,16,128]{3,2,1,0:T(8,128)(2,1)S(1)}, u32[]{:S(2)}, u32[]{:S(2)}) %collective-permute-start.8) | collective-permute-done | bytes 458784 | tf_op jit(solution)/shard_map/ppermute | solution.py:425
  37.4 0.1 plane_send.3
  37.5 1.9 %collective-permute-start.9 = (bf16[4,7,16,128]{3,2,1,0:T(8,128)(2,1)S(1)}, bf16[4,7,16,128]{3,2,1,0:T(8,128)(2,1)S(1)}, u32[]{:S(2)}, u32[]{:S(2)}) collective-permute-start(bf16[4,7,16,128]{3,2,1,0:T(8,128)(2,1)S(1)} %get-tuple-element.65), channel_id=1, source_target_pairs={{0,5},{1,4},{2,7},{3,6},{4,1},{5,0},{6,3},{7,2},{8,13},{9,12},{10,... | collective-permute-start | bytes 344072 | tf_op jit(solution)/shard_map/ppermute | solution.py:425
  39.4 1.5 %collective-permute-start.10 = (bf16[4,7,16,128]{3,2,1,0:T(8,128)(2,1)S(1)}, bf16[4,7,16,128]{3,2,1,0:T(8,128)(2,1)S(1)}, u32[]{:S(2)}, u32[]{:S(2)}) collective-permute-start(bf16[4,7,16,128]{3,2,1,0:T(8,128)(2,1)S(1)} %get-tuple-element.66), channel_id=1, source_target_pairs={{0,1},{1,0},{2,3},{3,2},{4,5},{5,4},{6,7},{7,6},{8,9},{9,8},{10,11... | collective-permute-start | bytes 344072 | tf_op jit(solution)/shard_map/ppermute | solution.py:425
  40.9 0.2 collective-permute-start.11
  41.1 3.2 %collective-permute-done.9.refs_5_ = bf16[4,7,16,128]{3,2,1,0:T(8,128)(2,1)S(1)} collective-permute-done((bf16[4,7,16,128]{3,2,1,0:T(8,128)(2,1)S(1)}, bf16[4,7,16,128]{3,2,1,0:T(8,128)(2,1)S(1)}, u32[]{:S(2)}, u32[]{:S(2)}) %collective-permute-start.9) | collective-permute-done | bytes 114720 | tf_op jit(solution)/shard_map/ppermute | solution.py:425
  44.3 1.8 %collective-permute-done.10.refs_6_ = bf16[4,7,16,128]{3,2,1,0:T(8,128)(2,1)S(1)} collective-permute-done((bf16[4,7,16,128]{3,2,1,0:T(8,128)(2,1)S(1)}, bf16[4,7,16,128]{3,2,1,0:T(8,128)(2,1)S(1)}, u32[]{:S(2)}, u32[]{:S(2)}) %collective-permute-start.10) | collective-permute-done | bytes 114720 | tf_op jit(solution)/shard_map/ppermute | solution.py:425
  46.1 0.1 line_send.1
  46.3 2.6 %collective-permute-start.12 = (bf16[16,16,128]{2,1,0:T(8,128)(2,1)S(1)}, bf16[16,16,128]{2,1,0:T(8,128)(2,1)S(1)}, u32[]{:S(2)}, u32[]{:S(2)}) collective-permute-start(bf16[16,16,128]{2,1,0:T(8,128)(2,1)S(1)} %get-tuple-element.69), channel_id=1, source_target_pairs={{0,24},{1,25},{2,26},{3,27},{4,28},{5,29},{6,30},{7,31},{8,16},{9,... | collective-permute-start | bytes 196616 | tf_op jit(solution)/shard_map/ppermute | solution.py:425
  48.9 0.5 collective-permute-start.13
  49.4 1.3 %collective-permute-start.14 = (bf16[16,16,128]{2,1,0:T(8,128)(2,1)S(1)}, bf16[16,16,128]{2,1,0:T(8,128)(2,1)S(1)}, u32[]{:S(2)}, u32[]{:S(2)}) collective-permute-start(bf16[16,16,128]{2,1,0:T(8,128)(2,1)S(1)} %get-tuple-element.71), channel_id=1, source_target_pairs={{0,8},{1,9},{2,10},{3,11},{4,12},{5,13},{6,14},{7,15},{8,0},{9,1},... | collective-permute-start | bytes 196616 | tf_op jit(solution)/shard_map/ppermute | solution.py:425
  50.7 2.0 %collective-permute-done.12.b_ref = bf16[16,16,128]{2,1,0:T(8,128)(2,1)S(1)} collective-permute-done((bf16[16,16,128]{2,1,0:T(8,128)(2,1)S(1)}, bf16[16,16,128]{2,1,0:T(8,128)(2,1)S(1)}, u32[]{:S(2)}, u32[]{:S(2)}) %collective-permute-start.12) | collective-permute-done | bytes 65568 | tf_op jit(solution)/shard_map/ppermute | solution.py:425
  52.7 2.9 %collective-permute-done.13.c_ref = bf16[16,16,128]{2,1,0:T(8,128)(2,1)S(1)} collective-permute-done((bf16[16,16,128]{2,1,0:T(8,128)(2,1)S(1)}, bf16[16,16,128]{2,1,0:T(8,128)(2,1)S(1)}, u32[]{:S(2)}, u32[]{:S(2)}) %collective-permute-start.13) | collective-permute-done | bytes 65568 | tf_op jit(solution)/shard_map/ppermute | solution.py:425
  55.7 0.1 collective-permute-start.17
  55.8 2.9 %collective-permute-start.16 = (bf16[16,16,128]{2,1,0:T(8,128)(2,1)S(1)}, bf16[16,16,128]{2,1,0:T(8,128)(2,1)S(1)}, u32[]{:S(2)}, u32[]{:S(2)}) collective-permute-start(bf16[16,16,128]{2,1,0:T(8,128)(2,1)S(1)} %line_sum.1.a_ref), channel_id=1, source_target_pairs={{0,16},{1,17},{2,18},{3,19},{4,20},{5,21},{6,22},{7,23},{8,24},{9,... | collective-permute-start | bytes 196616 | tf_op jit(solution)/shard_map/ppermute | solution.py:425
  58.7 1.4 %collective-permute-start.15 = (bf16[16,16,128]{2,1,0:T(8,128)(2,1)S(1)}, bf16[16,16,128]{2,1,0:T(8,128)(2,1)S(1)}, u32[]{:S(2)}, u32[]{:S(2)}) collective-permute-start(bf16[16,16,128]{2,1,0:T(8,128)(2,1)S(1)} %line_sum.1.a_ref), channel_id=1, source_target_pairs={{0,24},{1,25},{2,26},{3,27},{4,28},{5,29},{6,30},{7,31},{8,16},{9,... | collective-permute-start | bytes 196616 | tf_op jit(solution)/shard_map/ppermute | solution.py:425
  60.1 0.5 collective-permute-done.17.d_ref
  60.7 2.9 %collective-permute-done.16.c_ref = bf16[16,16,128]{2,1,0:T(8,128)(2,1)S(1)} collective-permute-done((bf16[16,16,128]{2,1,0:T(8,128)(2,1)S(1)}, bf16[16,16,128]{2,1,0:T(8,128)(2,1)S(1)}, u32[]{:S(2)}, u32[]{:S(2)}) %collective-permute-start.16) | collective-permute-done | bytes 65568 | tf_op jit(solution)/shard_map/ppermute | solution.py:425
  63.5 1.3 %collective-permute-done.15.b_ref = bf16[16,16,128]{2,1,0:T(8,128)(2,1)S(1)} collective-permute-done((bf16[16,16,128]{2,1,0:T(8,128)(2,1)S(1)}, bf16[16,16,128]{2,1,0:T(8,128)(2,1)S(1)}, u32[]{:S(2)}, u32[]{:S(2)}) %collective-permute-start.15) | collective-permute-done | bytes 65568 | tf_op jit(solution)/shard_map/ppermute | solution.py:425
  64.9 1.4 %collective-permute-start.20 = (bf16[4,16,16,128]{3,2,1,0:T(8,128)(2,1)S(1)}, bf16[4,16,16,128]{3,2,1,0:T(8,128)(2,1)S(1)}, u32[]{:S(2)}, u32[]{:S(2)}) collective-permute-start(bf16[4,16,16,128]{3,2,1,0:T(8,128)(2,1)S(1)} %line_gather.1.rest_0_.a_ref), channel_id=1, source_target_pairs={{0,4},{1,5},{2,6},{3,7},{4,0},{5,1},{6,2},{7,3},{8,12},{9,13},{10,... | collective-permute-start | bytes 786440 | tf_op jit(solution)/shard_map/ppermute | solution.py:425
  66.3 0.9 %collective-permute-start.19 = (bf16[4,16,16,128]{3,2,1,0:T(8,128)(2,1)S(1)}, bf16[4,16,16,128]{3,2,1,0:T(8,128)(2,1)S(1)}, u32[]{:S(2)}, u32[]{:S(2)}) collective-permute-start(bf16[4,16,16,128]{3,2,1,0:T(8,128)(2,1)S(1)} %line_gather.1.rest_0_.a_ref), channel_id=1, source_target_pairs={{0,1},{1,0},{2,3},{3,2},{4,5},{5,4},{6,7},{7,6},{8,9},{9,8},{10,11... | collective-permute-start | bytes 786440 | tf_op jit(solution)/shard_map/ppermute | solution.py:425
  67.2 1.2 %collective-permute-start.18 = (bf16[4,16,16,128]{3,2,1,0:T(8,128)(2,1)S(1)}, bf16[4,16,16,128]{3,2,1,0:T(8,128)(2,1)S(1)}, u32[]{:S(2)}, u32[]{:S(2)}) collective-permute-start(bf16[4,16,16,128]{3,2,1,0:T(8,128)(2,1)S(1)} %line_gather.1.rest_0_.a_ref), channel_id=1, source_target_pairs={{0,5},{1,4},{2,7},{3,6},{4,1},{5,0},{6,3},{7,2},{8,13},{9,12},{10,... | collective-permute-start | bytes 786440 | tf_op jit(solution)/shard_map/ppermute | solution.py:425
  68.5 7.4 %grad_x.1 = (bf16[16,128,256]{2,1,0:T(8,128)(2,1)}, bf16[16,8,4,256]{3,2,1,0:T(4,128)(2,1)}, f32[8,128]{1,0:T(8,128)S(1)}) custom-call(s32[1]{0:T(128)S(6)} %copy.23.count_ref, bf16[16,8,16,256]{3,2,1,0:T(8,128)(2,1)S(1)} %get-tuple-element.44.xt_ref, bf16[16,8,16,256]{3,2,1,0:T(8,128)(2,1)S(1)} %get-tuple-element.48.gy_ref, ...), custom_call_target="tpu_custom_call" | custom-call | flops 2684354560 | bytes 7147524 | tf_op jit(solution)/shard_map/grad_x/pallas_call | solution.py:401
  75.9 2.3 %collective-permute-done.19.c_ref = bf16[4,16,16,128]{3,2,1,0:T(8,128)(2,1)S(1)} collective-permute-done((bf16[4,16,16,128]{3,2,1,0:T(8,128)(2,1)S(1)}, bf16[4,16,16,128]{3,2,1,0:T(8,128)(2,1)S(1)}, u32[]{:S(2)}, u32[]{:S(2)}) %collective-permute-start.19) | collective-permute-done | bytes 262176 | tf_op jit(solution)/shard_map/ppermute | solution.py:425
  78.2 0.1 plane_gather.1.half_ref
  78.4 1.5 %finish.2 = (f32[9,256,256]{2,1,0:T(8,128)}, f32[3,256,256]{2,1,0:T(8,128)}, f32[4,256,256]{2,1,0:T(8,128)}) custom-call(bf16[16,16,16,128]{3,2,1,0:T(8,128)(2,1)S(1)} %plane_gather.1.half_ref), custom_call_target="tpu_custom_call" | custom-call | bytes 5242880 | tf_op jit(solution)/shard_map/finish/pallas_call | solution.py:401
  79.8 1.2 %collective-permute-done.21.half_ref = bf16[16,16,16,128]{3,2,1,0:T(8,128)(2,1)S(1)} collective-permute-done((bf16[16,16,16,128]{3,2,1,0:T(8,128)(2,1)S(1)}, bf16[16,16,16,128]{3,2,1,0:T(8,128)(2,1)S(1)}, u32[]{:S(2)}, u32[]{:S(2)}) %collective-permute-start.21) | collective-permute-done | bytes 1048608 | tf_op jit(solution)/shard_map/ppermute | solution.py:425
  81.0 1.5 %finish.3 = (f32[9,256,256]{2,1,0:T(8,128)}, f32[3,256,256]{2,1,0:T(8,128)}, f32[4,256,256]{2,1,0:T(8,128)}) custom-call(bf16[16,16,16,128]{3,2,1,0:T(8,128)(2,1)S(1)} %collective-permute-done.21.half_ref, f32[9,256,256]{2,1,0:T(8,128)} %get-tuple-element.75.rest_0_, ...), custom_call_target="tpu_custom_call", output_to_operand_aliasing={{0}: (1, {}), {1}: (2, {}), {2}: (3, {})} | custom-call | bytes 9437184 | tf_op jit(solution)/shard_map/finish/pallas_call | solution.py:401
  (23 shorter events, 0.2 us)
Async XLA Ops:
  1.3 1.2 %copy-start = (bf16[16,16,8,256]{3,2,1,0:T(8,128)(2,1)S(1)}, bf16[16,16,8,256]{3,2,1,0:T(8,128)(2,1)}, u32[]{:S(2)}) copy-start(bf16[16,16,8,256]{3,2,1,0:T(8,128)(2,1)} %param.6) | copy-start | bytes 3145732
  2.5 0.9 %copy-start.1 = (bf16[16,8,4,256]{3,2,1,0:T(4,128)(2,1)S(1)}, bf16[16,8,4,256]{3,2,1,0:T(4,128)(2,1)}, u32[]{:S(2)}) copy-start(bf16[16,8,4,256]{3,2,1,0:T(4,128)(2,1)} %cot_ref.3) | copy-start | bytes 786436
  3.5 6.4 %copy-start.2 = (bf16[16,8,4,256]{3,2,1,0:T(4,128)(2,1)S(1)}, bf16[16,8,4,256]{3,2,1,0:T(4,128)(2,1)}, u32[]{:S(2)}) copy-start(bf16[16,8,4,256]{3,2,1,0:T(4,128)(2,1)} %cot_ref.3) | copy-start | bytes 786436
  3.5 6.4 %copy-start.4 = (bf16[2,2,256,256]{3,2,1,0:T(8,128)(2,1)S(1)}, bf16[2,2,256,256]{3,2,1,0:T(8,128)(2,1)}, u32[]{:S(2)}) copy-start(bf16[2,2,256,256]{3,2,1,0:T(8,128)(2,1)} %param.10) | copy-start | bytes 1572868
  3.5 6.4 %copy-start.5 = (bf16[3,256,256]{2,1,0:T(8,128)(2,1)S(1)}, bf16[3,256,256]{2,1,0:T(8,128)(2,1)}, u32[]{:S(2)}) copy-start(bf16[3,256,256]{2,1,0:T(8,128)(2,1)} %wt_ref.5) | copy-start | bytes 1179652
  3.8 6.1 %collective-permute-start = (bf16[128,256]{1,0:T(8,128)(2,1)S(1)}, bf16[128,256]{1,0:T(8,128)(2,1)S(1)}, u32[]{:S(2)}, u32[]{:S(2)}) collective-permute-start(bf16[128,256]{1,0:T(8,128)(2,1)S(1)} %get-tuple-element.46), channel_id=1, source_target_pairs={{0,1},{1,0},{2,3},{3,2},{4,5},{5,4},{6,7},{7,6},{8,9},{9,8},{10,11... | collective-permute-start | bytes 196616 | tf_op jit(solution)/shard_map/ppermute | solution.py:474
  6.8 3.1 %collective-permute-start.1 = (bf16[2,8,4,256]{3,2,1,0:T(4,128)(2,1)S(1)}, bf16[2,8,4,256]{3,2,1,0:T(4,128)(2,1)S(1)}, u32[]{:S(2)}, u32[]{:S(2)}) collective-permute-start(bf16[2,8,4,256]{3,2,1,0:T(4,128)(2,1)S(1)} %get-tuple-element.47), channel_id=1, source_target_pairs={{2,0},{4,2},{6,4},{8,6},{10,8},{12,10},{14,12},{16,14},{18,16},{20... | collective-permute-start | bytes 98312 | tf_op jit(solution)/shard_map/ppermute | solution.py:469
  9.9 6.6 %copy-start.3 = (bf16[3,3,256,256]{3,2,1,0:T(8,128)(2,1)S(1)}, bf16[3,3,256,256]{3,2,1,0:T(8,128)(2,1)}, u32[]{:S(2)}) copy-start(bf16[3,3,256,256]{3,2,1,0:T(8,128)(2,1)} %param.8) | copy-start | bytes 3538948
  14.4 10.0 %collective-permute-start.4 = (bf16[16,9,16,128]{3,2,1,0:T(8,128)(2,1)S(1)}, bf16[16,9,16,128]{3,2,1,0:T(8,128)(2,1)S(1)}, u32[]{:S(2)}, u32[]{:S(2)}) collective-permute-start(bf16[16,9,16,128]{3,2,1,0:T(8,128)(2,1)S(1)} %get-tuple-element.52._), channel_id=1, source_target_pairs={{0,2},{1,3},{2,0},{3,1},{4,6},{5,7},{6,4},{7,5},{8,10},{9,11},{10,... | collective-permute-start | bytes 1769480 | tf_op jit(solution)/shard_map/ppermute | solution.py:425
  21.8 6.6 %collective-permute-start.3 = (bf16[8,32,256]{2,1,0:T(8,128)(2,1)S(1)}, bf16[8,32,256]{2,1,0:T(8,128)(2,1)S(1)}, u32[]{:S(2)}, u32[]{:S(2)}) collective-permute-start(bf16[8,32,256]{2,1,0:T(8,128)(2,1)S(1)} %get-tuple-element.54.rest_0_), channel_id=1, source_target_pairs={{0,2},{2,4},{4,6},{6,8},{8,10},{10,12},{12,14},{14,16},{16,18},{18... | collective-permute-start | bytes 393224 | tf_op jit(solution)/shard_map/ppermute | solution.py:469
  23.9 7.6 %collective-permute-start.2 = (bf16[64,256]{1,0:T(8,128)(2,1)S(1)}, bf16[64,256]{1,0:T(8,128)(2,1)S(1)}, u32[]{:S(2)}, u32[]{:S(2)}) collective-permute-start(bf16[64,256]{1,0:T(8,128)(2,1)S(1)} %get-tuple-element.50), channel_id=1, source_target_pairs={{0,1},{1,0},{2,3},{3,2},{4,5},{5,4},{6,7},{7,6},{8,9},{9,8},{10,11... | collective-permute-start | bytes 98312 | tf_op jit(solution)/shard_map/ppermute | solution.py:474
  24.6 7.4 %collective-permute-start.5 = (bf16[4,9,16,128]{3,2,1,0:T(8,128)(2,1)S(1)}, bf16[4,9,16,128]{3,2,1,0:T(8,128)(2,1)S(1)}, u32[]{:S(2)}, u32[]{:S(2)}) collective-permute-start(bf16[4,9,16,128]{3,2,1,0:T(8,128)(2,1)S(1)} %get-tuple-element.58.rest_1_), channel_id=1, source_target_pairs={{0,5},{1,4},{2,7},{3,6},{4,1},{5,0},{6,3},{7,2},{8,13},{9,12},{10,... | collective-permute-start | bytes 442376 | tf_op jit(solution)/shard_map/ppermute | solution.py:425
  27.7 7.9 %collective-permute-start.6 = (bf16[4,9,16,128]{3,2,1,0:T(8,128)(2,1)S(1)}, bf16[4,9,16,128]{3,2,1,0:T(8,128)(2,1)S(1)}, u32[]{:S(2)}, u32[]{:S(2)}) collective-permute-start(bf16[4,9,16,128]{3,2,1,0:T(8,128)(2,1)S(1)} %get-tuple-element.59.rest_2_), channel_id=1, source_target_pairs={{0,1},{1,0},{2,3},{3,2},{4,5},{5,4},{6,7},{7,6},{8,9},{9,8},{10,11... | collective-permute-start | bytes 442376 | tf_op jit(solution)/shard_map/ppermute | solution.py:425
  28.2 7.4 %collective-permute-start.7 = (bf16[4,9,16,128]{3,2,1,0:T(8,128)(2,1)S(1)}, bf16[4,9,16,128]{3,2,1,0:T(8,128)(2,1)S(1)}, u32[]{:S(2)}, u32[]{:S(2)}) collective-permute-start(bf16[4,9,16,128]{3,2,1,0:T(8,128)(2,1)S(1)} %get-tuple-element.60.rest_3_), channel_id=1, source_target_pairs={{0,4},{1,5},{2,6},{3,7},{4,0},{5,1},{6,2},{7,3},{8,12},{9,13},{10,... | collective-permute-start | bytes 442376 | tf_op jit(solution)/shard_map/ppermute | solution.py:425
  35.6 1.8 %collective-permute-start.8 = (bf16[16,7,16,128]{3,2,1,0:T(8,128)(2,1)S(1)}, bf16[16,7,16,128]{3,2,1,0:T(8,128)(2,1)S(1)}, u32[]{:S(2)}, u32[]{:S(2)}) collective-permute-start(bf16[16,7,16,128]{3,2,1,0:T(8,128)(2,1)S(1)} %pass.1), channel_id=1, source_target_pairs={{0,2},{1,3},{2,0},{3,1},{4,6},{5,7},{6,4},{7,5},{8,10},{9,11},{10,... | collective-permute-start | bytes 1376264 | tf_op jit(solution)/shard_map/ppermute | solution.py:425
  37.5 6.8 %collective-permute-start.9 = (bf16[4,7,16,128]{3,2,1,0:T(8,128)(2,1)S(1)}, bf16[4,7,16,128]{3,2,1,0:T(8,128)(2,1)S(1)}, u32[]{:S(2)}, u32[]{:S(2)}) collective-permute-start(bf16[4,7,16,128]{3,2,1,0:T(8,128)(2,1)S(1)} %get-tuple-element.65), channel_id=1, source_target_pairs={{0,5},{1,4},{2,7},{3,6},{4,1},{5,0},{6,3},{7,2},{8,13},{9,12},{10,... | collective-permute-start | bytes 344072 | tf_op jit(solution)/shard_map/ppermute | solution.py:425
  39.4 6.7 %collective-permute-start.10 = (bf16[4,7,16,128]{3,2,1,0:T(8,128)(2,1)S(1)}, bf16[4,7,16,128]{3,2,1,0:T(8,128)(2,1)S(1)}, u32[]{:S(2)}, u32[]{:S(2)}) collective-permute-start(bf16[4,7,16,128]{3,2,1,0:T(8,128)(2,1)S(1)} %get-tuple-element.66), channel_id=1, source_target_pairs={{0,1},{1,0},{2,3},{3,2},{4,5},{5,4},{6,7},{7,6},{8,9},{9,8},{10,11... | collective-permute-start | bytes 344072 | tf_op jit(solution)/shard_map/ppermute | solution.py:425
  40.9 5.2 %collective-permute-start.11 = (bf16[4,7,16,128]{3,2,1,0:T(8,128)(2,1)S(1)}, bf16[4,7,16,128]{3,2,1,0:T(8,128)(2,1)S(1)}, u32[]{:S(2)}, u32[]{:S(2)}) collective-permute-start(bf16[4,7,16,128]{3,2,1,0:T(8,128)(2,1)S(1)} %get-tuple-element.67), channel_id=1, source_target_pairs={{0,4},{1,5},{2,6},{3,7},{4,0},{5,1},{6,2},{7,3},{8,12},{9,13},{10,... | collective-permute-start | bytes 344072 | tf_op jit(solution)/shard_map/ppermute | solution.py:425
  46.3 6.4 %collective-permute-start.12 = (bf16[16,16,128]{2,1,0:T(8,128)(2,1)S(1)}, bf16[16,16,128]{2,1,0:T(8,128)(2,1)S(1)}, u32[]{:S(2)}, u32[]{:S(2)}) collective-permute-start(bf16[16,16,128]{2,1,0:T(8,128)(2,1)S(1)} %get-tuple-element.69), channel_id=1, source_target_pairs={{0,24},{1,25},{2,26},{3,27},{4,28},{5,29},{6,30},{7,31},{8,16},{9,... | collective-permute-start | bytes 196616 | tf_op jit(solution)/shard_map/ppermute | solution.py:425
  48.9 6.8 %collective-permute-start.13 = (bf16[16,16,128]{2,1,0:T(8,128)(2,1)S(1)}, bf16[16,16,128]{2,1,0:T(8,128)(2,1)S(1)}, u32[]{:S(2)}, u32[]{:S(2)}) collective-permute-start(bf16[16,16,128]{2,1,0:T(8,128)(2,1)S(1)} %get-tuple-element.70), channel_id=1, source_target_pairs={{0,16},{1,17},{2,18},{3,19},{4,20},{5,21},{6,22},{7,23},{8,24},{9,... | collective-permute-start | bytes 196616 | tf_op jit(solution)/shard_map/ppermute | solution.py:425
  49.4 6.3 %collective-permute-start.14 = (bf16[16,16,128]{2,1,0:T(8,128)(2,1)S(1)}, bf16[16,16,128]{2,1,0:T(8,128)(2,1)S(1)}, u32[]{:S(2)}, u32[]{:S(2)}) collective-permute-start(bf16[16,16,128]{2,1,0:T(8,128)(2,1)S(1)} %get-tuple-element.71), channel_id=1, source_target_pairs={{0,8},{1,9},{2,10},{3,11},{4,12},{5,13},{6,14},{7,15},{8,0},{9,1},... | collective-permute-start | bytes 196616 | tf_op jit(solution)/shard_map/ppermute | solution.py:425
  55.7 5.0 %collective-permute-start.17 = (bf16[16,16,128]{2,1,0:T(8,128)(2,1)S(1)}, bf16[16,16,128]{2,1,0:T(8,128)(2,1)S(1)}, u32[]{:S(2)}, u32[]{:S(2)}) collective-permute-start(bf16[16,16,128]{2,1,0:T(8,128)(2,1)S(1)} %line_sum.1.a_ref), channel_id=1, source_target_pairs={{0,8},{1,9},{2,10},{3,11},{4,12},{5,13},{6,14},{7,15},{8,0},{9,1},... | collective-permute-start | bytes 196616 | tf_op jit(solution)/shard_map/ppermute | solution.py:425
  55.8 7.8 %collective-permute-start.16 = (bf16[16,16,128]{2,1,0:T(8,128)(2,1)S(1)}, bf16[16,16,128]{2,1,0:T(8,128)(2,1)S(1)}, u32[]{:S(2)}, u32[]{:S(2)}) collective-permute-start(bf16[16,16,128]{2,1,0:T(8,128)(2,1)S(1)} %line_sum.1.a_ref), channel_id=1, source_target_pairs={{0,16},{1,17},{2,18},{3,19},{4,20},{5,21},{6,22},{7,23},{8,24},{9,... | collective-permute-start | bytes 196616 | tf_op jit(solution)/shard_map/ppermute | solution.py:425
  58.7 6.2 %collective-permute-start.15 = (bf16[16,16,128]{2,1,0:T(8,128)(2,1)S(1)}, bf16[16,16,128]{2,1,0:T(8,128)(2,1)S(1)}, u32[]{:S(2)}, u32[]{:S(2)}) collective-permute-start(bf16[16,16,128]{2,1,0:T(8,128)(2,1)S(1)} %line_sum.1.a_ref), channel_id=1, source_target_pairs={{0,24},{1,25},{2,26},{3,27},{4,28},{5,29},{6,30},{7,31},{8,16},{9,... | collective-permute-start | bytes 196616 | tf_op jit(solution)/shard_map/ppermute | solution.py:425
  64.9 11.0 %collective-permute-start.20 = (bf16[4,16,16,128]{3,2,1,0:T(8,128)(2,1)S(1)}, bf16[4,16,16,128]{3,2,1,0:T(8,128)(2,1)S(1)}, u32[]{:S(2)}, u32[]{:S(2)}) collective-permute-start(bf16[4,16,16,128]{3,2,1,0:T(8,128)(2,1)S(1)} %line_gather.1.rest_0_.a_ref), channel_id=1, source_target_pairs={{0,4},{1,5},{2,6},{3,7},{4,0},{5,1},{6,2},{7,3},{8,12},{9,13},{10,... | collective-permute-start | bytes 786440 | tf_op jit(solution)/shard_map/ppermute | solution.py:425
  66.3 11.9 %collective-permute-start.19 = (bf16[4,16,16,128]{3,2,1,0:T(8,128)(2,1)S(1)}, bf16[4,16,16,128]{3,2,1,0:T(8,128)(2,1)S(1)}, u32[]{:S(2)}, u32[]{:S(2)}) collective-permute-start(bf16[4,16,16,128]{3,2,1,0:T(8,128)(2,1)S(1)} %line_gather.1.rest_0_.a_ref), channel_id=1, source_target_pairs={{0,1},{1,0},{2,3},{3,2},{4,5},{5,4},{6,7},{7,6},{8,9},{9,8},{10,11... | collective-permute-start | bytes 786440 | tf_op jit(solution)/shard_map/ppermute | solution.py:425
  67.2 10.9 %collective-permute-start.18 = (bf16[4,16,16,128]{3,2,1,0:T(8,128)(2,1)S(1)}, bf16[4,16,16,128]{3,2,1,0:T(8,128)(2,1)S(1)}, u32[]{:S(2)}, u32[]{:S(2)}) collective-permute-start(bf16[4,16,16,128]{3,2,1,0:T(8,128)(2,1)S(1)} %line_gather.1.rest_0_.a_ref), channel_id=1, source_target_pairs={{0,5},{1,4},{2,7},{3,6},{4,1},{5,0},{6,3},{7,2},{8,13},{9,12},{10,... | collective-permute-start | bytes 786440 | tf_op jit(solution)/shard_map/ppermute | solution.py:425
  78.3 2.7 %collective-permute-start.21 = (bf16[16,16,16,128]{3,2,1,0:T(8,128)(2,1)S(1)}, bf16[16,16,16,128]{3,2,1,0:T(8,128)(2,1)S(1)}, u32[]{:S(2)}, u32[]{:S(2)}) collective-permute-start(bf16[16,16,16,128]{3,2,1,0:T(8,128)(2,1)S(1)} %plane_gather.1.half_ref), channel_id=1, source_target_pairs={{0,2},{1,3},{2,0},{3,1},{4,6},{5,7},{6,4},{7,5},{8,10},{9,11},{10,... | collective-permute-start | bytes 3145736 | tf_op jit(solution)/shard_map/ppermute | solution.py:425

commit v10 on v9

--- a/solution.py
+++ b/solution.py
@@ -128,7 +128,7 @@
 
 
 def spatial_kernel(
-    bands, count_ref, top_ref, bot_ref, acts_in, ws_ref, _, acts_ref, sp_ref, edge_ref, sum_ref
+    bands, count_ref, top_ref, bot_ref, acts_in, ws_ref, _, acts_ref, sp_ref, edge_ref
 ):
     count = count_ref[0]
     band = lax.axis_index("grp")
@@ -140,21 +140,18 @@
     pick = ((a >> 1) == (b >> 4)) & ((b & 15) == count - 2 + (a & 1))
     pick = jnp.where(pick, 1.0, 0.0).astype(BF)
 
-    high = rows // 2
-    for q in range(2):
-        for i in range(3):
-            for j in range(3):
-                left = acts_ref[high * q + i : high * q + i + high, j : j + cols]
-                term = mm(left.reshape(high * cols * SLOTS, CH), ws_ref[i * 3 + j])
-                if i + j == 0:
-                    sum_ref[...] = term
-                elif i + j < 4:
-                    sum_ref[...] += term
-                else:
-                    out = (sum_ref[...] + term).astype(BF)
-        sp_ref[high * q : high * q + high] = out.reshape(high, cols, SLOTS, CH)
-        for k in range(high // 2):
-            edge_ref[high // 2 * q + k] = mm(pick, out[k * 256 : k * 256 + 256]).astype(BF)
+    def rows_of(q, _):
+        left = [
+            acts_ref[pl.ds(2 * q + i, 2), j : j + cols].reshape(256, CH)
+            for i in range(3)
+            for j in range(3)
+        ]
+        out = mm(jnp.concatenate(left, axis=1), ws_ref[...].reshape(9 * CH, CH)).astype(BF)
+        sp_ref[pl.ds(2 * q, 2)] = out.reshape(2, cols, SLOTS, CH)
+        edge_ref[q] = mm(pick, out).astype(BF)
+        return 0
+
+    lax.fori_loop(0, rows // 2, rows_of, 0)
 
 
 def grad_spatial_kernel(
@@ -343,7 +340,8 @@
             at += n
 
 
-def line_sum_kernel(a_ref, b_ref, c_ref, d_ref, out_ref):
+def line_sum_kernel(a_ref, b_ref, c_ref, d_ref, *rest):
+    out_ref = rest[-1]
     parts = [ref[...].astype(F32) for ref in (a_ref, b_ref, c_ref, d_ref)]
     out_ref[...] = (parts[0] + parts[1] + parts[2] + parts[3]).astype(BF)
 
@@ -524,7 +522,6 @@
         "spatial",
         [count, (VMEM, top), (VMEM, bot), (VMEM, acts), (VMEM, ws), (ANY, send_a)],
         [(VMEM, padded), (VMEM, tile), (VMEM, (rows // 2, 32, ch))],
-        [pltpu.VMEM((slots * wide // 2, ch), F32)],
         flops=9 * tap,
         alias={3: 0},
     )
@@ -543,7 +540,7 @@
         grant=14,
     )
     parts_a = four_round(parts_a, plane, tm, grp)
-    send_b = passed(send_b, parts_a[1:] + [cot_top, cot_bot][:sides])
+    send_b = passed(send_b, parts_a[1:2])
     parts_b = plane_send(keep_b, core_round(send_b, tm, grp), [])
     parts_b = four_round(parts_b, plane, tm, grp)
     parts = call(
@@ -553,7 +550,8 @@
         [(VMEM, (16, 16, ch // 2))] * 4,
     )
     parts = four_round(list(parts), line, tm, grp)
-    (mine,) = call(line_sum_kernel, "line_sum", [(VMEM, a) for a in parts], [(VMEM, parts[0].shape)])
+    ins = [(VMEM, a) for a in parts] + [(ANY, a) for a in [cot_top, cot_bot][:sides]]
+    (mine,) = call(line_sum_kernel, "line_sum", ins, [(VMEM, parts[0].shape)])
     for bit in others:
         got = swap(mine, tm, grp, bit)
         (mine,) = call(add_kernel, "add", [(VMEM, mine), (VMEM, got)], [(VMEM, mine.shape)])

time: 82.8 us -> 79 us (0.954)
  waiting for transfers between devices: 24.3 us -> 17.6 us
  starting transfers between devices: 29 us -> 32.4 us
    ppermute x18, waiting for transfers between devices: 23.9 us -> 14.8 us  [swap(): return lax.ppermute(value, AXES, [(d, d ^ flip) for d in range(tm * grp)])]
    ppermute x18, starting transfers between devices: 22 us -> 24.7 us  [swap(): return lax.ppermute(value, AXES, [(d, d ^ flip) for d in range(tm * grp)])]
    ppermute x2, waiting for transfers between devices: 0.01 us -> 2.42 us  [from_bands(): got = lax.ppermute(parts[0], 'grp', [(0, 1), (1, 0)])]
    ppermute x2, starting transfers between devices: 3.6 us -> 4.53 us  [from_bands(): got = lax.ppermute(parts[0], 'grp', [(0, 1), (1, 0)])]
  transfers between devices with their start and end apart: 22 -> 22, of which waited for: 13 -> 12; matrix products, arithmetic and copies ran while one was open for 0% -> 0% of each run, Pallas kernels for 23% -> 24%
where the time goes in v10:
time: 79 us; the launch traced here: 78.8 us
  starting transfers between devices  32.4 us (41%)
  Pallas kernels  25.1 us (32%)
  waiting for transfers between devices  17.6 us (22%)
  local copies, waits for them, and re-layouts  2.18 us (3%)
  between operations  1.44 us (2%)
    pallas_call x15, Pallas kernels, call(): pl.pallas_call(kernel, out_shape=shapes, in_specs=[s for s, _ in ins], ou...  25.1 us
    ppermute x18, starting transfers between devices, swap(): return lax.ppermute(value, AXES, [(d, d ^ flip) for d in range(tm * grp)])  24.7 us
    ppermute x18, waiting for transfers between devices, swap(): return lax.ppermute(value, AXES, [(d, d ^ flip) for d in range(tm * grp)])  14.8 us
    ppermute x2, starting transfers between devices, from_bands(): got = lax.ppermute(parts[0], 'grp', [(0, 1), (1, 0)])  4.53 us
    ppermute x2, starting transfers between devices, along(): return lax.ppermute(value, axis, pairs)  3.21 us
    ppermute x2, waiting for transfers between devices, from_bands(): got = lax.ppermute(parts[0], 'grp', [(0, 1), (1, 0)])  2.42 us
    unnamed x12, local copies, waits for them, and re-layouts  2.18 us
  transfers between devices with their start and end apart: 22, of which 12 were waited for; matrix products, arithmetic and copies ran while one was open for 0% of the time, Pallas kernels for 24%

profile of v10, /device:TPU:0, one launch (start us, length us, event | category | flops | bytes accessed | tf_op | source)
XLA Modules:
  0.0 78.8 jit_solution(2299224105459262703)
XLA Ops:
  1.3 1.2 %copy-done = bf16[16,16,8,256]{3,2,1,0:T(8,128)(2,1)S(1)} copy-done((bf16[16,16,8,256]{3,2,1,0:T(8,128)(2,1)S(1)}, bf16[16,16,8,256]{3,2,1,0:T(8,128)(2,1)}, u32[]{:S(2)}) %copy-start) | copy-done | bytes 1048600
  2.5 0.9 %copy-done.1 = bf16[16,8,4,256]{3,2,1,0:T(4,128)(2,1)S(1)} copy-done((bf16[16,8,4,256]{3,2,1,0:T(4,128)(2,1)S(1)}, bf16[16,8,4,256]{3,2,1,0:T(4,128)(2,1)}, u32[]{:S(2)}) %copy-start.1) | copy-done | bytes 262168
  3.5 0.3 edges.1
  3.8 3.0 %collective-permute-start = (bf16[128,256]{1,0:T(8,128)(2,1)S(1)}, bf16[128,256]{1,0:T(8,128)(2,1)S(1)}, u32[]{:S(2)}, u32[]{:S(2)}) collective-permute-start(bf16[128,256]{1,0:T(8,128)(2,1)S(1)} %get-tuple-element.46), channel_id=1, source_target_pairs={{0,1},{1,0},{2,3},{3,2},{4,5},{5,4},{6,7},{7,6},{8,9},{9,8},{10,11... | collective-permute-start | bytes 196616 | tf_op jit(solution)/shard_map/ppermute | solution.py:472
  6.8 1.3 %collective-permute-start.1 = (bf16[2,8,4,256]{3,2,1,0:T(4,128)(2,1)S(1)}, bf16[2,8,4,256]{3,2,1,0:T(4,128)(2,1)S(1)}, u32[]{:S(2)}, u32[]{:S(2)}) collective-permute-start(bf16[2,8,4,256]{3,2,1,0:T(4,128)(2,1)S(1)} %get-tuple-element.47), channel_id=1, source_target_pairs={{2,0},{4,2},{6,4},{8,6},{10,8},{12,10},{14,12},{16,14},{18,16},{20... | collective-permute-start | bytes 98312 | tf_op jit(solution)/shard_map/ppermute | solution.py:467
  8.1 1.5 %acts.1 = (bf16[16,8,16,256]{3,2,1,0:T(8,128)(2,1)S(1)}, bf16[18,10,16,256]{3,2,1,0:T(8,128)(2,1)S(1)}, bf16[768,2560]{1,0:T(8,128)(2,1)S(1)}) custom-call(s32[1]{0:T(128)S(6)} %copy.23.count_ref, bf16[16,128,256]{2,1,0:T(8,128)(2,1)S(1)} %bitcast.7, f32[8,128]{1,0:T(8,128)S(1)} %get-tuple-element.43._), custom_call_target="tpu_custom_call" | custom-call | flops 536870912 | bytes 7503876 | tf_op jit(solution)/shard_map/acts/pallas_call | solution.py:399
  9.6 0.3 collective-permute-done.1.nxt_ref
  9.9 0.0 copy-start.3
  9.9 4.5 %grad_spatial.1 = (bf16[768,2560]{1,0:T(8,128)(2,1)S(1)}, bf16[8,4,16,256]{3,2,1,0:T(8,128)(2,1)S(1)}, bf16[16,8,16,256]{3,2,1,0:T(8,128)(2,1)S(1)}, bf16[16,10,...) custom-call(s32[1]{0:T(128)S(6)} %copy.23.count_ref, ...), custom_call_target="tpu_custom_call", output_to_operand_aliasing={{0}: (1, {})} | custom-call | flops 3758096384 | bytes 13041668 | tf_op jit(solution)/shard_map/grad_spatial/pallas_call | solution.py:399
  14.5 2.1 %collective-permute-start.4 = (bf16[16,9,16,128]{3,2,1,0:T(8,128)(2,1)S(1)}, bf16[16,9,16,128]{3,2,1,0:T(8,128)(2,1)S(1)}, u32[]{:S(2)}, u32[]{:S(2)}) collective-permute-start(bf16[16,9,16,128]{3,2,1,0:T(8,128)(2,1)S(1)} %get-tuple-element.52._), channel_id=1, source_target_pairs={{0,2},{1,3},{2,0},{3,1},{4,6},{5,7},{6,4},{7,5},{8,10},{9,11},{10,... | collective-permute-start | bytes 1769480 | tf_op jit(solution)/shard_map/ppermute | solution.py:423
  16.5 4.8 %spatial.1 = (bf16[18,10,16,256]{3,2,1,0:T(8,128)(2,1)S(1)}, bf16[16,8,16,256]{3,2,1,0:T(8,128)(2,1)S(1)}, bf16[8,32,256]{2,1,0:T(8,128)(2,1)S(1)}) custom-call(s32[1]{0:T(128)S(6)} %copy.23.count_ref, bf16[128,256]{1,0:T(8,128)(2,1)S(1)} %collective-permute-done.top_ref.bot_ref, ...), custom_call_target="tpu_custom_call", output_to_operand_aliasing={{0}: (3, {})} | custom-call | flops 2415919104 | bytes 5439492 | tf_op jit(solution)/shard_map/spatial/pallas_call | solution.py:399
  21.3 1.9 %collective-permute-start.3 = (bf16[8,32,256]{2,1,0:T(8,128)(2,1)S(1)}, bf16[8,32,256]{2,1,0:T(8,128)(2,1)S(1)}, u32[]{:S(2)}, u32[]{:S(2)}) collective-permute-start(bf16[8,32,256]{2,1,0:T(8,128)(2,1)S(1)} %get-tuple-element.54.rest_0_), channel_id=1, source_target_pairs={{0,2},{2,4},{4,6},{6,8},{8,10},{10,12},{12,14},{14,16},{16,18},{18... | collective-permute-start | bytes 393224 | tf_op jit(solution)/shard_map/ppermute | solution.py:467
  23.3 0.2 plane_send.2
  23.4 2.1 %collective-permute-start.5 = (bf16[4,9,16,128]{3,2,1,0:T(8,128)(2,1)S(1)}, bf16[4,9,16,128]{3,2,1,0:T(8,128)(2,1)S(1)}, u32[]{:S(2)}, u32[]{:S(2)}) collective-permute-start(bf16[4,9,16,128]{3,2,1,0:T(8,128)(2,1)S(1)} %get-tuple-element.58.rest_1_), channel_id=1, source_target_pairs={{0,5},{1,4},{2,7},{3,6},{4,1},{5,0},{6,3},{7,2},{8,13},{9,12},{10,... | collective-permute-start | bytes 442376 | tf_op jit(solution)/shard_map/ppermute | solution.py:423
  25.5 3.1 %forward.1 = (bf16[512,256]{1,0:T(8,128)(2,1)S(1)}, bf16[16,7,16,128]{3,2,1,0:T(8,128)(2,1)S(1)}, bf16[16,7,16,128]{3,2,1,0:T(8,128)(2,1)S(1)}) custom-call(s32[1]{0:T(128)S(6)} %copy.23.count_ref, bf16[16,8,16,256]{3,2,1,0:T(8,128)(2,1)S(1)} %get-tuple-element.44.xt_ref, bf16[16,8,16,256]{3,2,1,0:T(8,128)(2,1)S(1)} %get-tuple-element.53.sp_ref, ...), custom_call_target="tpu_custom_call" | custom-call | flops 2684354560 | bytes 5636100 | tf_op jit(solution)/shard_map/forward/pallas_call | solution.py:399
  28.7 1.2 %collective-permute-done.5.__1_.refs_1_ = bf16[4,9,16,128]{3,2,1,0:T(8,128)(2,1)S(1)} collective-permute-done((bf16[4,9,16,128]{3,2,1,0:T(8,128)(2,1)S(1)}, bf16[4,9,16,128]{3,2,1,0:T(8,128)(2,1)S(1)}, u32[]{:S(2)}, u32[]{:S(2)}) %collective-permute-start.5) | collective-permute-done | bytes 147488 | tf_op jit(solution)/shard_map/ppermute | solution.py:423
  29.9 1.3 %collective-permute-start.8 = (bf16[16,7,16,128]{3,2,1,0:T(8,128)(2,1)S(1)}, bf16[16,7,16,128]{3,2,1,0:T(8,128)(2,1)S(1)}, u32[]{:S(2)}, u32[]{:S(2)}) collective-permute-start(bf16[16,7,16,128]{3,2,1,0:T(8,128)(2,1)S(1)} %pass.1), channel_id=1, source_target_pairs={{0,2},{1,3},{2,0},{3,1},{4,6},{5,7},{6,4},{7,5},{8,10},{9,11},{10,... | collective-permute-start | bytes 1376264 | tf_op jit(solution)/shard_map/ppermute | solution.py:423
  31.2 0.4 collective-permute-start.6
  31.6 2.6 %collective-permute-start.7 = (bf16[4,9,16,128]{3,2,1,0:T(8,128)(2,1)S(1)}, bf16[4,9,16,128]{3,2,1,0:T(8,128)(2,1)S(1)}, u32[]{:S(2)}, u32[]{:S(2)}) collective-permute-start(bf16[4,9,16,128]{3,2,1,0:T(8,128)(2,1)S(1)} %get-tuple-element.60.rest_3_), channel_id=1, source_target_pairs={{0,4},{1,5},{2,6},{3,7},{4,0},{5,1},{6,2},{7,3},{8,12},{9,13},{10,... | collective-permute-start | bytes 442376 | tf_op jit(solution)/shard_map/ppermute | solution.py:423
  34.1 0.1 plane_send.3
  34.2 1.0 %collective-permute-start.9 = (bf16[4,7,16,128]{3,2,1,0:T(8,128)(2,1)S(1)}, bf16[4,7,16,128]{3,2,1,0:T(8,128)(2,1)S(1)}, u32[]{:S(2)}, u32[]{:S(2)}) collective-permute-start(bf16[4,7,16,128]{3,2,1,0:T(8,128)(2,1)S(1)} %get-tuple-element.65), channel_id=1, source_target_pairs={{0,5},{1,4},{2,7},{3,6},{4,1},{5,0},{6,3},{7,2},{8,13},{9,12},{10,... | collective-permute-start | bytes 344072 | tf_op jit(solution)/shard_map/ppermute | solution.py:423
  35.3 1.7 %collective-permute-start.10 = (bf16[4,7,16,128]{3,2,1,0:T(8,128)(2,1)S(1)}, bf16[4,7,16,128]{3,2,1,0:T(8,128)(2,1)S(1)}, u32[]{:S(2)}, u32[]{:S(2)}) collective-permute-start(bf16[4,7,16,128]{3,2,1,0:T(8,128)(2,1)S(1)} %get-tuple-element.66), channel_id=1, source_target_pairs={{0,1},{1,0},{2,3},{3,2},{4,5},{5,4},{6,7},{7,6},{8,9},{9,8},{10,11... | collective-permute-start | bytes 344072 | tf_op jit(solution)/shard_map/ppermute | solution.py:423
  37.0 0.8 %collective-permute-start.11 = (bf16[4,7,16,128]{3,2,1,0:T(8,128)(2,1)S(1)}, bf16[4,7,16,128]{3,2,1,0:T(8,128)(2,1)S(1)}, u32[]{:S(2)}, u32[]{:S(2)}) collective-permute-start(bf16[4,7,16,128]{3,2,1,0:T(8,128)(2,1)S(1)} %get-tuple-element.67), channel_id=1, source_target_pairs={{0,4},{1,5},{2,6},{3,7},{4,0},{5,1},{6,2},{7,3},{8,12},{9,13},{10,... | collective-permute-start | bytes 344072 | tf_op jit(solution)/shard_map/ppermute | solution.py:423
  37.8 0.6 collective-permute-done.7.refs_3_
  38.4 3.8 %collective-permute-done.9.refs_5_ = bf16[4,7,16,128]{3,2,1,0:T(8,128)(2,1)S(1)} collective-permute-done((bf16[4,7,16,128]{3,2,1,0:T(8,128)(2,1)S(1)}, bf16[4,7,16,128]{3,2,1,0:T(8,128)(2,1)S(1)}, u32[]{:S(2)}, u32[]{:S(2)}) %collective-permute-start.9) | collective-permute-done | bytes 114720 | tf_op jit(solution)/shard_map/ppermute | solution.py:423
  42.2 0.6 collective-permute-done.10.refs_6_
  42.8 0.2 collective-permute-done.11.refs_7_
  43.0 0.1 line_send.1
  43.2 4.1 %collective-permute-start.12 = (bf16[16,16,128]{2,1,0:T(8,128)(2,1)S(1)}, bf16[16,16,128]{2,1,0:T(8,128)(2,1)S(1)}, u32[]{:S(2)}, u32[]{:S(2)}) collective-permute-start(bf16[16,16,128]{2,1,0:T(8,128)(2,1)S(1)} %get-tuple-element.69), channel_id=1, source_target_pairs={{0,24},{1,25},{2,26},{3,27},{4,28},{5,29},{6,30},{7,31},{8,16},{9,... | collective-permute-start | bytes 196616 | tf_op jit(solution)/shard_map/ppermute | solution.py:423
  47.3 0.6 collective-permute-start.14
  47.9 1.5 %collective-permute-start.2 = (bf16[64,256]{1,0:T(8,128)(2,1)S(1)}, bf16[64,256]{1,0:T(8,128)(2,1)S(1)}, u32[]{:S(2)}, u32[]{:S(2)}) collective-permute-start(bf16[64,256]{1,0:T(8,128)(2,1)S(1)} %get-tuple-element.50), channel_id=1, source_target_pairs={{0,1},{1,0},{2,3},{3,2},{4,5},{5,4},{6,7},{7,6},{8,9},{9,8},{10,11... | collective-permute-start | bytes 98312 | tf_op jit(solution)/shard_map/ppermute | solution.py:472
  49.4 2.4 %collective-permute-done.2.rest_0_.top_ref.bot_ref = bf16[64,256]{1,0:T(8,128)(2,1)S(1)} collective-permute-done((bf16[64,256]{1,0:T(8,128)(2,1)S(1)}, bf16[64,256]{1,0:T(8,128)(2,1)S(1)}, u32[]{:S(2)}, u32[]{:S(2)}) %collective-permute-start.2) | collective-permute-done | bytes 32800 | tf_op jit(solution)/shard_map/ppermute | solution.py:472
  51.8 1.1 %collective-permute-done.13.c_ref = bf16[16,16,128]{2,1,0:T(8,128)(2,1)S(1)} collective-permute-done((bf16[16,16,128]{2,1,0:T(8,128)(2,1)S(1)}, bf16[16,16,128]{2,1,0:T(8,128)(2,1)S(1)}, u32[]{:S(2)}, u32[]{:S(2)}) %collective-permute-start.13) | collective-permute-done | bytes 65568 | tf_op jit(solution)/shard_map/ppermute | solution.py:423
  53.0 0.6 collective-permute-start.17
  53.6 2.7 %collective-permute-start.16 = (bf16[16,16,128]{2,1,0:T(8,128)(2,1)S(1)}, bf16[16,16,128]{2,1,0:T(8,128)(2,1)S(1)}, u32[]{:S(2)}, u32[]{:S(2)}) collective-permute-start(bf16[16,16,128]{2,1,0:T(8,128)(2,1)S(1)} %line_sum.1.a_ref), channel_id=1, source_target_pairs={{0,16},{1,17},{2,18},{3,19},{4,20},{5,21},{6,22},{7,23},{8,24},{9,... | collective-permute-start | bytes 196616 | tf_op jit(solution)/shard_map/ppermute | solution.py:423
  56.2 1.2 %collective-permute-start.15 = (bf16[16,16,128]{2,1,0:T(8,128)(2,1)S(1)}, bf16[16,16,128]{2,1,0:T(8,128)(2,1)S(1)}, u32[]{:S(2)}, u32[]{:S(2)}) collective-permute-start(bf16[16,16,128]{2,1,0:T(8,128)(2,1)S(1)} %line_sum.1.a_ref), channel_id=1, source_target_pairs={{0,24},{1,25},{2,26},{3,27},{4,28},{5,29},{6,30},{7,31},{8,16},{9,... | collective-permute-start | bytes 196616 | tf_op jit(solution)/shard_map/ppermute | solution.py:423
  57.4 2.6 %collective-permute-done.16.c_ref = bf16[16,16,128]{2,1,0:T(8,128)(2,1)S(1)} collective-permute-done((bf16[16,16,128]{2,1,0:T(8,128)(2,1)S(1)}, bf16[16,16,128]{2,1,0:T(8,128)(2,1)S(1)}, u32[]{:S(2)}, u32[]{:S(2)}) %collective-permute-start.16) | collective-permute-done | bytes 65568 | tf_op jit(solution)/shard_map/ppermute | solution.py:423
  60.0 2.3 %collective-permute-done.15.b_ref = bf16[16,16,128]{2,1,0:T(8,128)(2,1)S(1)} collective-permute-done((bf16[16,16,128]{2,1,0:T(8,128)(2,1)S(1)}, bf16[16,16,128]{2,1,0:T(8,128)(2,1)S(1)}, u32[]{:S(2)}, u32[]{:S(2)}) %collective-permute-start.15) | collective-permute-done | bytes 65568 | tf_op jit(solution)/shard_map/ppermute | solution.py:423
  62.3 0.5 collective-permute-start.20
  62.8 1.9 %collective-permute-start.19 = (bf16[4,16,16,128]{3,2,1,0:T(8,128)(2,1)S(1)}, bf16[4,16,16,128]{3,2,1,0:T(8,128)(2,1)S(1)}, u32[]{:S(2)}, u32[]{:S(2)}) collective-permute-start(bf16[4,16,16,128]{3,2,1,0:T(8,128)(2,1)S(1)} %line_gather.1.rest_0_.a_ref), channel_id=1, source_target_pairs={{0,1},{1,0},{2,3},{3,2},{4,5},{5,4},{6,7},{7,6},{8,9},{9,8},{10,11... | collective-permute-start | bytes 786440 | tf_op jit(solution)/shard_map/ppermute | solution.py:423
  64.7 1.2 %collective-permute-start.18 = (bf16[4,16,16,128]{3,2,1,0:T(8,128)(2,1)S(1)}, bf16[4,16,16,128]{3,2,1,0:T(8,128)(2,1)S(1)}, u32[]{:S(2)}, u32[]{:S(2)}) collective-permute-start(bf16[4,16,16,128]{3,2,1,0:T(8,128)(2,1)S(1)} %line_gather.1.rest_0_.a_ref), channel_id=1, source_target_pairs={{0,5},{1,4},{2,7},{3,6},{4,1},{5,0},{6,3},{7,2},{8,13},{9,12},{10,... | collective-permute-start | bytes 786440 | tf_op jit(solution)/shard_map/ppermute | solution.py:423
  65.9 7.4 %grad_x.1 = (bf16[16,128,256]{2,1,0:T(8,128)(2,1)}, bf16[16,8,4,256]{3,2,1,0:T(4,128)(2,1)}, f32[8,128]{1,0:T(8,128)S(1)}) custom-call(s32[1]{0:T(128)S(6)} %copy.23.count_ref, bf16[16,8,16,256]{3,2,1,0:T(8,128)(2,1)S(1)} %get-tuple-element.44.xt_ref, bf16[16,8,16,256]{3,2,1,0:T(8,128)(2,1)S(1)} %get-tuple-element.48.gy_ref, ...), custom_call_target="tpu_custom_call" | custom-call | flops 2684354560 | bytes 7147524 | tf_op jit(solution)/shard_map/grad_x/pallas_call | solution.py:399
  73.3 1.1 %collective-permute-done.19.c_ref = bf16[4,16,16,128]{3,2,1,0:T(8,128)(2,1)S(1)} collective-permute-done((bf16[4,16,16,128]{3,2,1,0:T(8,128)(2,1)S(1)}, bf16[4,16,16,128]{3,2,1,0:T(8,128)(2,1)S(1)}, u32[]{:S(2)}, u32[]{:S(2)}) %collective-permute-start.19) | collective-permute-done | bytes 262176 | tf_op jit(solution)/shard_map/ppermute | solution.py:423
  74.5 0.1 plane_gather.1.half_ref
  74.6 0.1 collective-permute-start.21
  74.7 1.5 %finish.2 = (f32[9,256,256]{2,1,0:T(8,128)}, f32[3,256,256]{2,1,0:T(8,128)}, f32[4,256,256]{2,1,0:T(8,128)}) custom-call(bf16[16,16,16,128]{3,2,1,0:T(8,128)(2,1)S(1)} %plane_gather.1.half_ref), custom_call_target="tpu_custom_call" | custom-call | bytes 5242880 | tf_op jit(solution)/shard_map/finish/pallas_call | solution.py:399
  76.1 1.2 %collective-permute-done.21.half_ref = bf16[16,16,16,128]{3,2,1,0:T(8,128)(2,1)S(1)} collective-permute-done((bf16[16,16,16,128]{3,2,1,0:T(8,128)(2,1)S(1)}, bf16[16,16,16,128]{3,2,1,0:T(8,128)(2,1)S(1)}, u32[]{:S(2)}, u32[]{:S(2)}) %collective-permute-start.21) | collective-permute-done | bytes 1048608 | tf_op jit(solution)/shard_map/ppermute | solution.py:423
  77.3 1.5 %finish.3 = (f32[9,256,256]{2,1,0:T(8,128)}, f32[3,256,256]{2,1,0:T(8,128)}, f32[4,256,256]{2,1,0:T(8,128)}) custom-call(bf16[16,16,16,128]{3,2,1,0:T(8,128)(2,1)S(1)} %collective-permute-done.21.half_ref, f32[9,256,256]{2,1,0:T(8,128)} %get-tuple-element.75.rest_0_, ...), custom_call_target="tpu_custom_call", output_to_operand_aliasing={{0}: (1, {}), {1}: (2, {}), {2}: (3, {})} | custom-call | bytes 9437184 | tf_op jit(solution)/shard_map/finish/pallas_call | solution.py:399
  (23 shorter events, 0.1 us)
Async XLA Ops:
  1.3 1.2 %copy-start = (bf16[16,16,8,256]{3,2,1,0:T(8,128)(2,1)S(1)}, bf16[16,16,8,256]{3,2,1,0:T(8,128)(2,1)}, u32[]{:S(2)}) copy-start(bf16[16,16,8,256]{3,2,1,0:T(8,128)(2,1)} %param.6) | copy-start | bytes 3145732
  2.5 0.9 %copy-start.1 = (bf16[16,8,4,256]{3,2,1,0:T(4,128)(2,1)S(1)}, bf16[16,8,4,256]{3,2,1,0:T(4,128)(2,1)}, u32[]{:S(2)}) copy-start(bf16[16,8,4,256]{3,2,1,0:T(4,128)(2,1)} %cot_ref.3) | copy-start | bytes 786436
  3.5 6.4 %copy-start.2 = (bf16[16,8,4,256]{3,2,1,0:T(4,128)(2,1)S(1)}, bf16[16,8,4,256]{3,2,1,0:T(4,128)(2,1)}, u32[]{:S(2)}) copy-start(bf16[16,8,4,256]{3,2,1,0:T(4,128)(2,1)} %cot_ref.3) | copy-start | bytes 786436
  3.5 6.4 %copy-start.4 = (bf16[2,2,256,256]{3,2,1,0:T(8,128)(2,1)S(1)}, bf16[2,2,256,256]{3,2,1,0:T(8,128)(2,1)}, u32[]{:S(2)}) copy-start(bf16[2,2,256,256]{3,2,1,0:T(8,128)(2,1)} %param.10) | copy-start | bytes 1572868
  3.5 6.4 %copy-start.5 = (bf16[3,256,256]{2,1,0:T(8,128)(2,1)S(1)}, bf16[3,256,256]{2,1,0:T(8,128)(2,1)}, u32[]{:S(2)}) copy-start(bf16[3,256,256]{2,1,0:T(8,128)(2,1)} %wt_ref.5) | copy-start | bytes 1179652
  3.8 6.1 %collective-permute-start = (bf16[128,256]{1,0:T(8,128)(2,1)S(1)}, bf16[128,256]{1,0:T(8,128)(2,1)S(1)}, u32[]{:S(2)}, u32[]{:S(2)}) collective-permute-start(bf16[128,256]{1,0:T(8,128)(2,1)S(1)} %get-tuple-element.46), channel_id=1, source_target_pairs={{0,1},{1,0},{2,3},{3,2},{4,5},{5,4},{6,7},{7,6},{8,9},{9,8},{10,11... | collective-permute-start | bytes 196616 | tf_op jit(solution)/shard_map/ppermute | solution.py:472
  6.8 3.1 %collective-permute-start.1 = (bf16[2,8,4,256]{3,2,1,0:T(4,128)(2,1)S(1)}, bf16[2,8,4,256]{3,2,1,0:T(4,128)(2,1)S(1)}, u32[]{:S(2)}, u32[]{:S(2)}) collective-permute-start(bf16[2,8,4,256]{3,2,1,0:T(4,128)(2,1)S(1)} %get-tuple-element.47), channel_id=1, source_target_pairs={{2,0},{4,2},{6,4},{8,6},{10,8},{12,10},{14,12},{16,14},{18,16},{20... | collective-permute-start | bytes 98312 | tf_op jit(solution)/shard_map/ppermute | solution.py:467
  9.9 6.6 %copy-start.3 = (bf16[3,3,256,256]{3,2,1,0:T(8,128)(2,1)S(1)}, bf16[3,3,256,256]{3,2,1,0:T(8,128)(2,1)}, u32[]{:S(2)}) copy-start(bf16[3,3,256,256]{3,2,1,0:T(8,128)(2,1)} %param.8) | copy-start | bytes 3538948
  14.5 8.8 %collective-permute-start.4 = (bf16[16,9,16,128]{3,2,1,0:T(8,128)(2,1)S(1)}, bf16[16,9,16,128]{3,2,1,0:T(8,128)(2,1)S(1)}, u32[]{:S(2)}, u32[]{:S(2)}) collective-permute-start(bf16[16,9,16,128]{3,2,1,0:T(8,128)(2,1)S(1)} %get-tuple-element.52._), channel_id=1, source_target_pairs={{0,2},{1,3},{2,0},{3,1},{4,6},{5,7},{6,4},{7,5},{8,10},{9,11},{10,... | collective-permute-start | bytes 1769480 | tf_op jit(solution)/shard_map/ppermute | solution.py:423
  21.3 4.2 %collective-permute-start.3 = (bf16[8,32,256]{2,1,0:T(8,128)(2,1)S(1)}, bf16[8,32,256]{2,1,0:T(8,128)(2,1)S(1)}, u32[]{:S(2)}, u32[]{:S(2)}) collective-permute-start(bf16[8,32,256]{2,1,0:T(8,128)(2,1)S(1)} %get-tuple-element.54.rest_0_), channel_id=1, source_target_pairs={{0,2},{2,4},{4,6},{6,8},{8,10},{10,12},{12,14},{14,16},{16,18},{18... | collective-permute-start | bytes 393224 | tf_op jit(solution)/shard_map/ppermute | solution.py:467
  23.4 6.5 %collective-permute-start.5 = (bf16[4,9,16,128]{3,2,1,0:T(8,128)(2,1)S(1)}, bf16[4,9,16,128]{3,2,1,0:T(8,128)(2,1)S(1)}, u32[]{:S(2)}, u32[]{:S(2)}) collective-permute-start(bf16[4,9,16,128]{3,2,1,0:T(8,128)(2,1)S(1)} %get-tuple-element.58.rest_1_), channel_id=1, source_target_pairs={{0,5},{1,4},{2,7},{3,6},{4,1},{5,0},{6,3},{7,2},{8,13},{9,12},{10,... | collective-permute-start | bytes 442376 | tf_op jit(solution)/shard_map/ppermute | solution.py:423
  29.9 4.2 %collective-permute-start.8 = (bf16[16,7,16,128]{3,2,1,0:T(8,128)(2,1)S(1)}, bf16[16,7,16,128]{3,2,1,0:T(8,128)(2,1)S(1)}, u32[]{:S(2)}, u32[]{:S(2)}) collective-permute-start(bf16[16,7,16,128]{3,2,1,0:T(8,128)(2,1)S(1)} %pass.1), channel_id=1, source_target_pairs={{0,2},{1,3},{2,0},{3,1},{4,6},{5,7},{6,4},{7,5},{8,10},{9,11},{10,... | collective-permute-start | bytes 1376264 | tf_op jit(solution)/shard_map/ppermute | solution.py:423
  31.2 6.6 %collective-permute-start.6 = (bf16[4,9,16,128]{3,2,1,0:T(8,128)(2,1)S(1)}, bf16[4,9,16,128]{3,2,1,0:T(8,128)(2,1)S(1)}, u32[]{:S(2)}, u32[]{:S(2)}) collective-permute-start(bf16[4,9,16,128]{3,2,1,0:T(8,128)(2,1)S(1)} %get-tuple-element.59.rest_2_), channel_id=1, source_target_pairs={{0,1},{1,0},{2,3},{3,2},{4,5},{5,4},{6,7},{7,6},{8,9},{9,8},{10,11... | collective-permute-start | bytes 442376 | tf_op jit(solution)/shard_map/ppermute | solution.py:423
  31.6 6.8 %collective-permute-start.7 = (bf16[4,9,16,128]{3,2,1,0:T(8,128)(2,1)S(1)}, bf16[4,9,16,128]{3,2,1,0:T(8,128)(2,1)S(1)}, u32[]{:S(2)}, u32[]{:S(2)}) collective-permute-start(bf16[4,9,16,128]{3,2,1,0:T(8,128)(2,1)S(1)} %get-tuple-element.60.rest_3_), channel_id=1, source_target_pairs={{0,4},{1,5},{2,6},{3,7},{4,0},{5,1},{6,2},{7,3},{8,12},{9,13},{10,... | collective-permute-start | bytes 442376 | tf_op jit(solution)/shard_map/ppermute | solution.py:423
  34.2 8.0 %collective-permute-start.9 = (bf16[4,7,16,128]{3,2,1,0:T(8,128)(2,1)S(1)}, bf16[4,7,16,128]{3,2,1,0:T(8,128)(2,1)S(1)}, u32[]{:S(2)}, u32[]{:S(2)}) collective-permute-start(bf16[4,7,16,128]{3,2,1,0:T(8,128)(2,1)S(1)} %get-tuple-element.65), channel_id=1, source_target_pairs={{0,5},{1,4},{2,7},{3,6},{4,1},{5,0},{6,3},{7,2},{8,13},{9,12},{10,... | collective-permute-start | bytes 344072 | tf_op jit(solution)/shard_map/ppermute | solution.py:423
  35.3 7.5 %collective-permute-start.10 = (bf16[4,7,16,128]{3,2,1,0:T(8,128)(2,1)S(1)}, bf16[4,7,16,128]{3,2,1,0:T(8,128)(2,1)S(1)}, u32[]{:S(2)}, u32[]{:S(2)}) collective-permute-start(bf16[4,7,16,128]{3,2,1,0:T(8,128)(2,1)S(1)} %get-tuple-element.66), channel_id=1, source_target_pairs={{0,1},{1,0},{2,3},{3,2},{4,5},{5,4},{6,7},{7,6},{8,9},{9,8},{10,11... | collective-permute-start | bytes 344072 | tf_op jit(solution)/shard_map/ppermute | solution.py:423
  37.0 6.0 %collective-permute-start.11 = (bf16[4,7,16,128]{3,2,1,0:T(8,128)(2,1)S(1)}, bf16[4,7,16,128]{3,2,1,0:T(8,128)(2,1)S(1)}, u32[]{:S(2)}, u32[]{:S(2)}) collective-permute-start(bf16[4,7,16,128]{3,2,1,0:T(8,128)(2,1)S(1)} %get-tuple-element.67), channel_id=1, source_target_pairs={{0,4},{1,5},{2,6},{3,7},{4,0},{5,1},{6,2},{7,3},{8,12},{9,13},{10,... | collective-permute-start | bytes 344072 | tf_op jit(solution)/shard_map/ppermute | solution.py:423
  43.2 8.6 %collective-permute-start.12 = (bf16[16,16,128]{2,1,0:T(8,128)(2,1)S(1)}, bf16[16,16,128]{2,1,0:T(8,128)(2,1)S(1)}, u32[]{:S(2)}, u32[]{:S(2)}) collective-permute-start(bf16[16,16,128]{2,1,0:T(8,128)(2,1)S(1)} %get-tuple-element.69), channel_id=1, source_target_pairs={{0,24},{1,25},{2,26},{3,27},{4,28},{5,29},{6,30},{7,31},{8,16},{9,... | collective-permute-start | bytes 196616 | tf_op jit(solution)/shard_map/ppermute | solution.py:423
  47.2 5.7 %collective-permute-start.13 = (bf16[16,16,128]{2,1,0:T(8,128)(2,1)S(1)}, bf16[16,16,128]{2,1,0:T(8,128)(2,1)S(1)}, u32[]{:S(2)}, u32[]{:S(2)}) collective-permute-start(bf16[16,16,128]{2,1,0:T(8,128)(2,1)S(1)} %get-tuple-element.70), channel_id=1, source_target_pairs={{0,16},{1,17},{2,18},{3,19},{4,20},{5,21},{6,22},{7,23},{8,24},{9,... | collective-permute-start | bytes 196616 | tf_op jit(solution)/shard_map/ppermute | solution.py:423
  47.3 5.7 %collective-permute-start.14 = (bf16[16,16,128]{2,1,0:T(8,128)(2,1)S(1)}, bf16[16,16,128]{2,1,0:T(8,128)(2,1)S(1)}, u32[]{:S(2)}, u32[]{:S(2)}) collective-permute-start(bf16[16,16,128]{2,1,0:T(8,128)(2,1)S(1)} %get-tuple-element.71), channel_id=1, source_target_pairs={{0,8},{1,9},{2,10},{3,11},{4,12},{5,13},{6,14},{7,15},{8,0},{9,1},... | collective-permute-start | bytes 196616 | tf_op jit(solution)/shard_map/ppermute | solution.py:423
  47.9 3.9 %collective-permute-start.2 = (bf16[64,256]{1,0:T(8,128)(2,1)S(1)}, bf16[64,256]{1,0:T(8,128)(2,1)S(1)}, u32[]{:S(2)}, u32[]{:S(2)}) collective-permute-start(bf16[64,256]{1,0:T(8,128)(2,1)S(1)} %get-tuple-element.50), channel_id=1, source_target_pairs={{0,1},{1,0},{2,3},{3,2},{4,5},{5,4},{6,7},{7,6},{8,9},{9,8},{10,11... | collective-permute-start | bytes 98312 | tf_op jit(solution)/shard_map/ppermute | solution.py:472
  53.0 4.5 %collective-permute-start.17 = (bf16[16,16,128]{2,1,0:T(8,128)(2,1)S(1)}, bf16[16,16,128]{2,1,0:T(8,128)(2,1)S(1)}, u32[]{:S(2)}, u32[]{:S(2)}) collective-permute-start(bf16[16,16,128]{2,1,0:T(8,128)(2,1)S(1)} %line_sum.1.a_ref), channel_id=1, source_target_pairs={{0,8},{1,9},{2,10},{3,11},{4,12},{5,13},{6,14},{7,15},{8,0},{9,1},... | collective-permute-start | bytes 196616 | tf_op jit(solution)/shard_map/ppermute | solution.py:423
  53.6 6.4 %collective-permute-start.16 = (bf16[16,16,128]{2,1,0:T(8,128)(2,1)S(1)}, bf16[16,16,128]{2,1,0:T(8,128)(2,1)S(1)}, u32[]{:S(2)}, u32[]{:S(2)}) collective-permute-start(bf16[16,16,128]{2,1,0:T(8,128)(2,1)S(1)} %line_sum.1.a_ref), channel_id=1, source_target_pairs={{0,16},{1,17},{2,18},{3,19},{4,20},{5,21},{6,22},{7,23},{8,24},{9,... | collective-permute-start | bytes 196616 | tf_op jit(solution)/shard_map/ppermute | solution.py:423
  56.2 6.1 %collective-permute-start.15 = (bf16[16,16,128]{2,1,0:T(8,128)(2,1)S(1)}, bf16[16,16,128]{2,1,0:T(8,128)(2,1)S(1)}, u32[]{:S(2)}, u32[]{:S(2)}) collective-permute-start(bf16[16,16,128]{2,1,0:T(8,128)(2,1)S(1)} %line_sum.1.a_ref), channel_id=1, source_target_pairs={{0,24},{1,25},{2,26},{3,27},{4,28},{5,29},{6,30},{7,31},{8,16},{9,... | collective-permute-start | bytes 196616 | tf_op jit(solution)/shard_map/ppermute | solution.py:423
  62.3 11.0 %collective-permute-start.20 = (bf16[4,16,16,128]{3,2,1,0:T(8,128)(2,1)S(1)}, bf16[4,16,16,128]{3,2,1,0:T(8,128)(2,1)S(1)}, u32[]{:S(2)}, u32[]{:S(2)}) collective-permute-start(bf16[4,16,16,128]{3,2,1,0:T(8,128)(2,1)S(1)} %line_gather.1.rest_0_.a_ref), channel_id=1, source_target_pairs={{0,4},{1,5},{2,6},{3,7},{4,0},{5,1},{6,2},{7,3},{8,12},{9,13},{10,... | collective-permute-start | bytes 786440 | tf_op jit(solution)/shard_map/ppermute | solution.py:423
  62.8 11.7 %collective-permute-start.19 = (bf16[4,16,16,128]{3,2,1,0:T(8,128)(2,1)S(1)}, bf16[4,16,16,128]{3,2,1,0:T(8,128)(2,1)S(1)}, u32[]{:S(2)}, u32[]{:S(2)}) collective-permute-start(bf16[4,16,16,128]{3,2,1,0:T(8,128)(2,1)S(1)} %line_gather.1.rest_0_.a_ref), channel_id=1, source_target_pairs={{0,1},{1,0},{2,3},{3,2},{4,5},{5,4},{6,7},{7,6},{8,9},{9,8},{10,11... | collective-permute-start | bytes 786440 | tf_op jit(solution)/shard_map/ppermute | solution.py:423
  64.7 9.8 %collective-permute-start.18 = (bf16[4,16,16,128]{3,2,1,0:T(8,128)(2,1)S(1)}, bf16[4,16,16,128]{3,2,1,0:T(8,128)(2,1)S(1)}, u32[]{:S(2)}, u32[]{:S(2)}) collective-permute-start(bf16[4,16,16,128]{3,2,1,0:T(8,128)(2,1)S(1)} %line_gather.1.rest_0_.a_ref), channel_id=1, source_target_pairs={{0,5},{1,4},{2,7},{3,6},{4,1},{5,0},{6,3},{7,2},{8,13},{9,12},{10,... | collective-permute-start | bytes 786440 | tf_op jit(solution)/shard_map/ppermute | solution.py:423
  74.6 2.7 %collective-permute-start.21 = (bf16[16,16,16,128]{3,2,1,0:T(8,128)(2,1)S(1)}, bf16[16,16,16,128]{3,2,1,0:T(8,128)(2,1)S(1)}, u32[]{:S(2)}, u32[]{:S(2)}) collective-permute-start(bf16[16,16,16,128]{3,2,1,0:T(8,128)(2,1)S(1)} %plane_gather.1.half_ref), channel_id=1, source_target_pairs={{0,2},{1,3},{2,0},{3,1},{4,6},{5,7},{6,4},{7,5},{8,10},{9,11},{10,... | collective-permute-start | bytes 3145736 | tf_op jit(solution)/shard_map/ppermute | solution.py:423

commit v11 on v10

--- a/solution.py
+++ b/solution.py
@@ -85,9 +85,8 @@
 
 
 def edges_kernel(bands, count_ref, x_ref, cot_ref, *rest):
-    outs, (nxt_ref, token_ref) = rest[:-2], rest[-2:]
+    outs, nxt_ref = rest[:-1], rest[-1]
     nxt_ref[...] = cot_ref[0:2]
-    token_ref[...] = jnp.zeros_like(token_ref)
     count = count_ref[0]
     band = lax.axis_index("grp")
     wide = x_ref.shape[1]
@@ -103,13 +102,17 @@
         outs[k][...] = silu_norm(v).astype(BF)
 
 
-def acts_kernel(count_ref, x_ref, _, xt_ref, acts_ref, at_ref):
+def acts_kernel(bands, count_ref, x_ref, top_ref, bot_ref, xt_ref, acts_ref, at_ref, last_ref):
     count = count_ref[0]
+    band = lax.axis_index("grp")
     rows, cols = xt_ref.shape[0], xt_ref.shape[1]
     edge = jnp.zeros((rows + 2, SLOTS, CH), BF)
     acts_ref[:, 0] = edge
     acts_ref[:, cols + 1] = edge
     place = to_slots(16, SLOTS, own_frames(count))
+    a, b = iotas(32, 256)
+    pick = ((a >> 1) == (b >> 4)) & ((b & 15) == count - 2 + (a & 1))
+    pick = jnp.where(pick, 1.0, 0.0).astype(BF)
 
     def rows_of(q, _):
         at = pl.multiple_of(q * 16, 16)
@@ -117,6 +120,7 @@
         v = mm(place, piece)
         xt_ref[pl.ds(2 * q, 2)] = v.astype(BF).reshape(2, cols, SLOTS, CH)
         a = silu_norm(v).astype(BF)
+        last_ref[q] = mm(pick, a).astype(BF)
         acts_ref[pl.ds(2 * q + 1, 2), 1 : cols + 1] = a.reshape(2, cols, SLOTS, CH)
         flipped = a.T
         for i in range(3):
@@ -125,46 +129,47 @@
         return 0
 
     lax.fori_loop(0, rows // 2, rows_of, 0, unroll=4)
-
-
-def spatial_kernel(
-    bands, count_ref, top_ref, bot_ref, acts_in, ws_ref, _, acts_ref, sp_ref, edge_ref
-):
-    count = count_ref[0]
-    band = lax.axis_index("grp")
+    halo = []
+    for ref, flag, i, row in ((top_ref, band > 0, 0, 0), (bot_ref, band < bands - 1, 2, rows + 1)):
+        a = jnp.where(flag, ref[...].astype(F32), 0.0).astype(BF)
+        acts_ref[row, 1 : cols + 1] = a.reshape(cols, SLOTS, CH)
+        at = (row - i + 2) * 128
+        at_ref[i * CH : i * CH + CH, at : at + 128] = a.T
+        halo.append(a)
+    last_ref[rows // 2] = mm(pick, jnp.concatenate(halo, 0)).astype(BF)
+
+
+def spatial_kernel(count_ref, acts_in, prev_ref, ws_ref, _, acts_ref, sp_ref):
     rows, cols = sp_ref.shape[0], sp_ref.shape[1]
-    for ref, flag, row in ((top_ref, band > 0, 0), (bot_ref, band < bands - 1, rows + 1)):
-        a = jnp.where(flag, ref[...].astype(F32), 0.0)
-        acts_ref[row, 1 : cols + 1] = a.astype(BF).reshape(cols, SLOTS, CH)
-    a, b = iotas(32, 256)
-    pick = ((a >> 1) == (b >> 4)) & ((b & 15) == count - 2 + (a & 1))
-    pick = jnp.where(pick, 1.0, 0.0).astype(BF)
+    a, b = iotas(256, 32)
+    place = ((a >> 4) == (b >> 1)) & ((a & 15) == OWN + (b & 1))
+    place = jnp.where(place, 1.0, 0.0).astype(BF)
+    for q in range(rows // 2 + 1):
+        both = slice(0, rows + 2, rows + 1) if q == rows // 2 else slice(2 * q + 1, 2 * q + 3)
+        prev = mm(place, prev_ref[q]).astype(BF).reshape(2, cols, SLOTS, CH)
+        for k, row in enumerate(range(rows + 2)[both]):
+            acts_ref[row, 1 : cols + 1] = acts_ref[row, 1 : cols + 1] + prev[k]
 
     def rows_of(q, _):
-        left = [
-            acts_ref[pl.ds(2 * q + i, 2), j : j + cols].reshape(256, CH)
-            for i in range(3)
-            for j in range(3)
-        ]
-        out = mm(jnp.concatenate(left, axis=1), ws_ref[...].reshape(9 * CH, CH)).astype(BF)
-        sp_ref[pl.ds(2 * q, 2)] = out.reshape(2, cols, SLOTS, CH)
-        edge_ref[q] = mm(pick, out).astype(BF)
+        total = None
+        for i in range(3):
+            for j in range(3):
+                left = acts_ref[pl.ds(4 * q + i, 4), j : j + cols].reshape(4 * cols * SLOTS, CH)
+                term = mm(left, ws_ref[i * 3 + j])
+                total = term if total is None else total + term
+        sp_ref[pl.ds(4 * q, 4)] = total.astype(BF).reshape(4, cols, SLOTS, CH)
         return 0
 
-    lax.fori_loop(0, rows // 2, rows_of, 0)
+    lax.fori_loop(0, rows // 4, rows_of, 0)
 
 
 def grad_spatial_kernel(
-    bands, count_ref, at_in, top_ref, bot_ref, cot_ref, nxt_ref, wt_ref, wd_ref,
-    at_ref, cott_ref, gy_ref, gs_ref, keep_ref, send_ref, *edge_refs,
+    bands, count_ref, at_ref, cot_ref, nxt_ref, wt_ref, wd_ref,
+    cott_ref, gy_ref, gs_ref, keep_ref, send_ref, *edge_refs,
 ):
     count = count_ref[0]
     band = lax.axis_index("grp")
     rows, cols = gy_ref.shape[0], gy_ref.shape[1]
-    for ref, flag, i, row in ((top_ref, band > 0, 0, 0), (bot_ref, band < bands - 1, 2, rows + 1)):
-        a = jnp.where(flag, ref[...].astype(F32), 0.0)
-        at = (row - i + 2) * 128
-        at_ref[i * CH : i * CH + CH, at : at + 128] = a.T.astype(BF)
     edge = jnp.zeros((rows, SLOTS, CH), BF)
     gs_ref[:, 0] = edge
     gs_ref[:, cols + 1] = edge
@@ -212,18 +217,13 @@
 
 
 def forward_kernel(
-    count_ref, xt_ref, sp_ref, prev_ref, cott_ref, gy_ref, wt_ref, wd_ref, *rest
+    count_ref, xt_ref, sp_ref, cott_ref, gy_ref, wt_ref, wd_ref, *rest
 ):
     down_ref, keep_ref, send_ref, y_ref, st_ref, yt_ref = rest[-6:]
     count = count_ref[0]
     rows, cols = xt_ref.shape[0], xt_ref.shape[1]
-    a, b = iotas(256, 32)
-    place = ((a >> 4) == (b >> 1)) & ((a & 15) == OWN + (b & 1))
-    place = jnp.where(place, 1.0, 0.0).astype(BF)
-
     def rows_of(q, _):
         s = sp_ref[pl.ds(8 * q, 8)].reshape(8 * cols * SLOTS, CH).astype(F32)
-        s = s + jnp.concatenate([mm(place, prev_ref[4 * q + k]) for k in range(4)], 0)
         s = s.reshape(8 * cols, SLOTS, CH)
         total = None
         for k in range(3):
@@ -488,51 +488,51 @@
     dma = pltpu.SemaphoreType.DMA
 
     sides = 1 if grp == 2 else 2
-    *edge, nxt, token = call(
+    *edge, nxt = call(
         functools.partial(edges_kernel, grp),
         "edges",
         [count, (VMEM, x), (VMEM, cotangent)],
-        [(VMEM, (cols * slots, ch))] * sides + [(VMEM, (2,) + cotangent.shape[1:]), TOKEN],
+        [(VMEM, (cols * slots, ch))] * sides + [(VMEM, (2,) + cotangent.shape[1:])],
         flops=tap // 8,
     )
     top, bot = from_bands(edge)
     nxt_got = along(nxt, "tm", -1)
-    xt, acts, at = call(
-        acts_kernel,
+    xt, acts, at, last_two = call(
+        functools.partial(acts_kernel, grp),
         "acts",
-        [count, (VMEM, x), (ANY, token)],
-        [(VMEM, tile), (VMEM, padded), (VMEM, (3 * ch, (rows + 4) * 128))],
+        [count, (VMEM, x), (VMEM, top), (VMEM, bot)],
+        [(VMEM, tile), (VMEM, padded), (VMEM, (3 * ch, (rows + 4) * 128)), (VMEM, (rows // 2 + 1, 32, ch))],
         flops=2 * tap,
     )
+    prev = along(last_two, "tm", 1)
     half = (16, 9, 16, ch // 2)
-    at, cott, gy, gs, keep_a, send_a, *edge = call(
+    cott, gy, gs, keep_a, send_a, *edge = call(
         functools.partial(grad_spatial_kernel, grp),
         "grad_spatial",
-        [count, (VMEM, at), (VMEM, top), (VMEM, bot), (VMEM, cotangent), (VMEM, nxt_got), (VMEM, wt), (VMEM, wd)],
-        [(VMEM, at.shape), (VMEM, (rows // 2, cols // 2, slots, ch)), (VMEM, tile),
+        [count, (VMEM, at), (VMEM, cotangent), (VMEM, nxt_got), (VMEM, wt), (VMEM, wd)],
+        [(VMEM, (rows // 2, cols // 2, slots, ch)), (VMEM, tile),
          (VMEM, (rows, cols + 2, slots, ch)), (VMEM, half), (VMEM, half)]
         + [(VMEM, (cols // 2 * slots, ch))] * sides,
         flops=14 * tap,
-        alias={1: 0},
-    )
+    )
+    send_a = passed(send_a, [prev])
     got_a = core_round(send_a, tm, grp)
     cot_top, cot_bot = from_bands(edge)
-    acts, sp, last_two = call(
-        functools.partial(spatial_kernel, grp),
+    acts, sp = call(
+        spatial_kernel,
         "spatial",
-        [count, (VMEM, top), (VMEM, bot), (VMEM, acts), (VMEM, ws), (ANY, send_a)],
-        [(VMEM, padded), (VMEM, tile), (VMEM, (rows // 2, 32, ch))],
+        [count, (VMEM, acts), (VMEM, prev), (VMEM, ws), (ANY, send_a)],
+        [(VMEM, padded), (VMEM, tile)],
         flops=9 * tap,
-        alias={3: 0},
-    )
-    prev = along(last_two, "tm", 1)
+        alias={1: 0},
+    )
     _, plane, line, others = plan(tm, grp)
-    parts_a = plane_send(keep_a, got_a, [last_two])
+    parts_a = plane_send(keep_a, got_a, [sp])
     half = (16, 7, 16, ch // 2)
     down, keep_b, send_b = call(
         forward_kernel,
         "forward",
-        [count, (VMEM, xt), (VMEM, sp), (VMEM, prev), (VMEM, cott), (VMEM, gy), (VMEM, wt), (VMEM, wd),
+        [count, (VMEM, xt), (VMEM, sp), (VMEM, cott), (VMEM, gy), (VMEM, wt), (VMEM, wd),
          *((ANY, a) for a in parts_a)],
         [(VMEM, (slots * wide // 4, ch)), (VMEM, half), (VMEM, half)],
         [pltpu.VMEM(v, BF) for v in (tile, (3 * ch, slots * wide), (4 * ch, slots * wide // 4))],

time: 79 us -> 79.4 us (level)
  waiting for transfers between devices: 17.6 us -> 19.8 us
  starting transfers between devices: 32.4 us -> 30.6 us
    ppermute x2, waiting for transfers between devices: 2.42 us -> 4.36 us  [from_bands(): got = lax.ppermute(parts[0], 'grp', [(0, 1), (1, 0)])]
    ppermute x18, starting transfers between devices: 24.7 us -> 23.7 us  [swap(): return lax.ppermute(value, AXES, [(d, d ^ flip) for d in range(tm * grp)])]
    ppermute x2, starting transfers between devices: 4.53 us -> 3.54 us  [from_bands(): got = lax.ppermute(parts[0], 'grp', [(0, 1), (1, 0)])]
    pallas_call x15 -> x16, Pallas kernels: 25.1 us -> 25.1 us  [call(): pl.pallas_call(kernel, out_shape=shapes, in_specs=[s for s, _ in ins], ou...]
  transfers between devices with their start and end apart: 22 -> 22, of which waited for: 12 -> 12; matrix products, arithmetic and copies ran while one was open for 0% -> 0% of each run, Pallas kernels for 24% -> 29%
where the time goes in v11:
time: 79.4 us; the launch traced here: 79.2 us
  starting transfers between devices  30.6 us (39%)
  Pallas kernels  25.1 us (32%)
  waiting for transfers between devices  19.8 us (25%)
  local copies, waits for them, and re-layouts  2.18 us (3%)
  between operations  1.47 us (2%)
    pallas_call x16, Pallas kernels, call(): pl.pallas_call(kernel, out_shape=shapes, in_specs=[s for s, _ in ins], ou...  25.1 us
    ppermute x18, starting transfers between devices, swap(): return lax.ppermute(value, AXES, [(d, d ^ flip) for d in range(tm * grp)])  23.7 us
    ppermute x18, waiting for transfers between devices, swap(): return lax.ppermute(value, AXES, [(d, d ^ flip) for d in range(tm * grp)])  15.4 us
    ppermute x2, waiting for transfers between devices, from_bands(): got = lax.ppermute(parts[0], 'grp', [(0, 1), (1, 0)])  4.36 us
    ppermute x2, starting transfers between devices, from_bands(): got = lax.ppermute(parts[0], 'grp', [(0, 1), (1, 0)])  3.54 us
    ppermute x2, starting transfers between devices, along(): return lax.ppermute(value, axis, pairs)  3.37 us
    unnamed x12, local copies, waits for them, and re-layouts  2.18 us
  transfers between devices with their start and end apart: 22, of which 12 were waited for; matrix products, arithmetic and copies ran while one was open for 0% of the time, Pallas kernels for 29%

profile of v11, /device:TPU:0, one launch (start us, length us, event | category | flops | bytes accessed | tf_op | source)
XLA Modules:
  0.0 79.2 jit_solution(16820381055008421601)
XLA Ops:
  1.3 1.2 %copy-done = bf16[16,16,8,256]{3,2,1,0:T(8,128)(2,1)S(1)} copy-done((bf16[16,16,8,256]{3,2,1,0:T(8,128)(2,1)S(1)}, bf16[16,16,8,256]{3,2,1,0:T(8,128)(2,1)}, u32[]{:S(2)}) %copy-start) | copy-done | bytes 1048600
  2.5 0.9 %copy-done.1 = bf16[16,8,4,256]{3,2,1,0:T(4,128)(2,1)S(1)} copy-done((bf16[16,8,4,256]{3,2,1,0:T(4,128)(2,1)S(1)}, bf16[16,8,4,256]{3,2,1,0:T(4,128)(2,1)}, u32[]{:S(2)}) %copy-start.1) | copy-done | bytes 262168
  3.5 0.3 edges.1
  3.8 3.0 %collective-permute-start = (bf16[128,256]{1,0:T(8,128)(2,1)S(1)}, bf16[128,256]{1,0:T(8,128)(2,1)S(1)}, u32[]{:S(2)}, u32[]{:S(2)}) collective-permute-start(bf16[128,256]{1,0:T(8,128)(2,1)S(1)} %get-tuple-element.42), channel_id=1, source_target_pairs={{0,1},{1,0},{2,3},{3,2},{4,5},{5,4},{6,7},{7,6},{8,9},{9,8},{10,11... | collective-permute-start | bytes 196616 | tf_op jit(solution)/shard_map/ppermute | solution.py:472
  6.8 1.3 %collective-permute-start.1 = (bf16[2,8,4,256]{3,2,1,0:T(4,128)(2,1)S(1)}, bf16[2,8,4,256]{3,2,1,0:T(4,128)(2,1)S(1)}, u32[]{:S(2)}, u32[]{:S(2)}) collective-permute-start(bf16[2,8,4,256]{3,2,1,0:T(4,128)(2,1)S(1)} %get-tuple-element.45), channel_id=1, source_target_pairs={{2,0},{4,2},{6,4},{8,6},{10,8},{12,10},{14,12},{16,14},{18,16},{20... | collective-permute-start | bytes 98312 | tf_op jit(solution)/shard_map/ppermute | solution.py:467
  8.1 1.0 %collective-permute-done.top_ref.bot_ref = bf16[128,256]{1,0:T(8,128)(2,1)S(1)} collective-permute-done((bf16[128,256]{1,0:T(8,128)(2,1)S(1)}, bf16[128,256]{1,0:T(8,128)(2,1)S(1)}, u32[]{:S(2)}, u32[]{:S(2)}) %collective-permute-start) | collective-permute-done | bytes 65568 | tf_op jit(solution)/shard_map/ppermute | solution.py:472
  9.0 3.0 %acts.1 = (bf16[16,8,16,256]{3,2,1,0:T(8,128)(2,1)S(1)}, bf16[18,10,16,256]{3,2,1,0:T(8,128)(2,1)S(1)}, bf16[768,2560]{1,0:T(8,128)(2,1)S(1)}, bf16[9,32,256]{2,1,0:T(8,128)(2,1)S(1)}) custom-call(s32[1]{0:T(128)S(6)} %copy.23.count_ref, bf16[16,128,256]{2,1,0:T(8,128)(2,1)S(1)} %bitcast.7, bf16[128,256]{1,0:T(8,128)(2,1)S(1)} %collective-permute-done.top_ref.bot_ref, ...), custom_call_target="tpu_custom_call" | custom-call | flops 536870912 | bytes 7782404 | tf_op jit(solution)/shard_map/acts/pallas_call | solution.py:399
  12.1 2.1 %collective-permute-start.3 = (bf16[9,32,256]{2,1,0:T(8,128)(2,1)S(1)}, bf16[9,32,256]{2,1,0:T(8,128)(2,1)S(1)}, u32[]{:S(2)}, u32[]{:S(2)}) collective-permute-start(bf16[9,32,256]{2,1,0:T(8,128)(2,1)S(1)} %get-tuple-element.50), channel_id=1, source_target_pairs={{0,2},{2,4},{4,6},{6,8},{8,10},{10,12},{12,14},{14,16},{16,18},{18... | collective-permute-start | bytes 442376 | tf_op jit(solution)/shard_map/ppermute | solution.py:467
  14.2 0.0 copy-start.3
  14.2 4.5 %grad_spatial.1 = (bf16[8,4,16,256]{3,2,1,0:T(8,128)(2,1)S(1)}, bf16[16,8,16,256]{3,2,1,0:T(8,128)(2,1)S(1)}, bf16[16,10,16,256]{3,2,1,0:T(8,128)(2,1)S(1)}, bf1...) custom-call(s32[1]{0:T(128)S(6)} %copy.23.count_ref, ...), custom_call_target="tpu_custom_call" | custom-call | flops 3758096384 | bytes 8978436 | tf_op jit(solution)/shard_map/grad_spatial/pallas_call | solution.py:399
  18.8 2.0 %collective-permute-start.4 = (bf16[16,9,16,128]{3,2,1,0:T(8,128)(2,1)S(1)}, bf16[16,9,16,128]{3,2,1,0:T(8,128)(2,1)S(1)}, u32[]{:S(2)}, u32[]{:S(2)}) collective-permute-start(bf16[16,9,16,128]{3,2,1,0:T(8,128)(2,1)S(1)} %pass.2._), channel_id=1, source_target_pairs={{0,2},{1,3},{2,0},{3,1},{4,6},{5,7},{6,4},{7,5},{8,10},{9,11},{10,... | collective-permute-start | bytes 1769480 | tf_op jit(solution)/shard_map/ppermute | solution.py:423
  20.8 3.6 %spatial.1 = (bf16[18,10,16,256]{3,2,1,0:T(8,128)(2,1)S(1)}, bf16[16,8,16,256]{3,2,1,0:T(8,128)(2,1)S(1)}) custom-call(s32[1]{0:T(128)S(6)} %copy.23.count_ref, bf16[18,10,16,256]{3,2,1,0:T(8,128)(2,1)S(1)} %get-tuple-element.49.acts_in, bf16[9,32,256]{2,1,0:T(8,128)(2,1)S(1)} %collective-permute-done.3.__1_.prev_ref, ...), custom_call_target="tpu_custom_call", output_to_operand_aliasing={{0}: (1, {})} | custom-call | flops 2415919104 | bytes 5324804 | tf_op jit(solution)/shard_map/spatial/pallas_call | solution.py:399
  24.4 0.2 plane_send.2
  24.5 2.6 %collective-permute-start.5 = (bf16[4,9,16,128]{3,2,1,0:T(8,128)(2,1)S(1)}, bf16[4,9,16,128]{3,2,1,0:T(8,128)(2,1)S(1)}, u32[]{:S(2)}, u32[]{:S(2)}) collective-permute-start(bf16[4,9,16,128]{3,2,1,0:T(8,128)(2,1)S(1)} %get-tuple-element.56.rest_1_), channel_id=1, source_target_pairs={{0,5},{1,4},{2,7},{3,6},{4,1},{5,0},{6,3},{7,2},{8,13},{9,12},{10,... | collective-permute-start | bytes 442376 | tf_op jit(solution)/shard_map/ppermute | solution.py:423
  27.1 2.8 %forward.1 = (bf16[512,256]{1,0:T(8,128)(2,1)S(1)}, bf16[16,7,16,128]{3,2,1,0:T(8,128)(2,1)S(1)}, bf16[16,7,16,128]{3,2,1,0:T(8,128)(2,1)S(1)}) custom-call(s32[1]{0:T(128)S(6)} %copy.23.count_ref, bf16[16,8,16,256]{3,2,1,0:T(8,128)(2,1)S(1)} %get-tuple-element.43.xt_ref, bf16[16,8,16,256]{3,2,1,0:T(8,128)(2,1)S(1)} %get-tuple-element.52.rest_0_.sp_ref, ...), custom_call_target="tpu_custom_call" | custom-call | flops 2684354560 | bytes 5505028 | tf_op jit(solution)/shard_map/forward/pallas_call | solution.py:399
  29.9 1.4 %collective-permute-done.5.__1_.refs_1_ = bf16[4,9,16,128]{3,2,1,0:T(8,128)(2,1)S(1)} collective-permute-done((bf16[4,9,16,128]{3,2,1,0:T(8,128)(2,1)S(1)}, bf16[4,9,16,128]{3,2,1,0:T(8,128)(2,1)S(1)}, u32[]{:S(2)}, u32[]{:S(2)}) %collective-permute-start.5) | collective-permute-done | bytes 147488 | tf_op jit(solution)/shard_map/ppermute | solution.py:423
  31.3 1.5 %collective-permute-start.6 = (bf16[4,9,16,128]{3,2,1,0:T(8,128)(2,1)S(1)}, bf16[4,9,16,128]{3,2,1,0:T(8,128)(2,1)S(1)}, u32[]{:S(2)}, u32[]{:S(2)}) collective-permute-start(bf16[4,9,16,128]{3,2,1,0:T(8,128)(2,1)S(1)} %get-tuple-element.57.rest_2_), channel_id=1, source_target_pairs={{0,1},{1,0},{2,3},{3,2},{4,5},{5,4},{6,7},{7,6},{8,9},{9,8},{10,11... | collective-permute-start | bytes 442376 | tf_op jit(solution)/shard_map/ppermute | solution.py:423
  32.8 1.5 %collective-permute-start.7 = (bf16[4,9,16,128]{3,2,1,0:T(8,128)(2,1)S(1)}, bf16[4,9,16,128]{3,2,1,0:T(8,128)(2,1)S(1)}, u32[]{:S(2)}, u32[]{:S(2)}) collective-permute-start(bf16[4,9,16,128]{3,2,1,0:T(8,128)(2,1)S(1)} %get-tuple-element.58.rest_3_), channel_id=1, source_target_pairs={{0,4},{1,5},{2,6},{3,7},{4,0},{5,1},{6,2},{7,3},{8,12},{9,13},{10,... | collective-permute-start | bytes 442376 | tf_op jit(solution)/shard_map/ppermute | solution.py:423
  34.3 0.1 plane_send.3
  34.4 1.3 %collective-permute-start.9 = (bf16[4,7,16,128]{3,2,1,0:T(8,128)(2,1)S(1)}, bf16[4,7,16,128]{3,2,1,0:T(8,128)(2,1)S(1)}, u32[]{:S(2)}, u32[]{:S(2)}) collective-permute-start(bf16[4,7,16,128]{3,2,1,0:T(8,128)(2,1)S(1)} %get-tuple-element.63), channel_id=1, source_target_pairs={{0,5},{1,4},{2,7},{3,6},{4,1},{5,0},{6,3},{7,2},{8,13},{9,12},{10,... | collective-permute-start | bytes 344072 | tf_op jit(solution)/shard_map/ppermute | solution.py:423
  35.7 0.7 collective-permute-start.10
  36.4 1.5 %collective-permute-start.11 = (bf16[4,7,16,128]{3,2,1,0:T(8,128)(2,1)S(1)}, bf16[4,7,16,128]{3,2,1,0:T(8,128)(2,1)S(1)}, u32[]{:S(2)}, u32[]{:S(2)}) collective-permute-start(bf16[4,7,16,128]{3,2,1,0:T(8,128)(2,1)S(1)} %get-tuple-element.65), channel_id=1, source_target_pairs={{0,4},{1,5},{2,6},{3,7},{4,0},{5,1},{6,2},{7,3},{8,12},{9,13},{10,... | collective-permute-start | bytes 344072 | tf_op jit(solution)/shard_map/ppermute | solution.py:423
  38.0 1.5 %collective-permute-done.7.refs_3_ = bf16[4,9,16,128]{3,2,1,0:T(8,128)(2,1)S(1)} collective-permute-done((bf16[4,9,16,128]{3,2,1,0:T(8,128)(2,1)S(1)}, bf16[4,9,16,128]{3,2,1,0:T(8,128)(2,1)S(1)}, u32[]{:S(2)}, u32[]{:S(2)}) %collective-permute-start.7) | collective-permute-done | bytes 147488 | tf_op jit(solution)/shard_map/ppermute | solution.py:423
  39.5 2.4 %collective-permute-done.9.refs_5_ = bf16[4,7,16,128]{3,2,1,0:T(8,128)(2,1)S(1)} collective-permute-done((bf16[4,7,16,128]{3,2,1,0:T(8,128)(2,1)S(1)}, bf16[4,7,16,128]{3,2,1,0:T(8,128)(2,1)S(1)}, u32[]{:S(2)}, u32[]{:S(2)}) %collective-permute-start.9) | collective-permute-done | bytes 114720 | tf_op jit(solution)/shard_map/ppermute | solution.py:423
  41.9 1.1 %collective-permute-done.10.refs_6_ = bf16[4,7,16,128]{3,2,1,0:T(8,128)(2,1)S(1)} collective-permute-done((bf16[4,7,16,128]{3,2,1,0:T(8,128)(2,1)S(1)}, bf16[4,7,16,128]{3,2,1,0:T(8,128)(2,1)S(1)}, u32[]{:S(2)}, u32[]{:S(2)}) %collective-permute-start.10) | collective-permute-done | bytes 114720 | tf_op jit(solution)/shard_map/ppermute | solution.py:423
  43.0 0.7 collective-permute-done.11.refs_7_
  43.7 0.1 line_send.1
  43.9 3.7 %collective-permute-start.12 = (bf16[16,16,128]{2,1,0:T(8,128)(2,1)S(1)}, bf16[16,16,128]{2,1,0:T(8,128)(2,1)S(1)}, u32[]{:S(2)}, u32[]{:S(2)}) collective-permute-start(bf16[16,16,128]{2,1,0:T(8,128)(2,1)S(1)} %get-tuple-element.67), channel_id=1, source_target_pairs={{0,24},{1,25},{2,26},{3,27},{4,28},{5,29},{6,30},{7,31},{8,16},{9,... | collective-permute-start | bytes 196616 | tf_op jit(solution)/shard_map/ppermute | solution.py:423
  47.5 0.8 collective-permute-start.14
  48.3 0.5 collective-permute-start.2
  48.8 3.4 %collective-permute-done.2.rest_0_.top_ref.bot_ref = bf16[64,256]{1,0:T(8,128)(2,1)S(1)} collective-permute-done((bf16[64,256]{1,0:T(8,128)(2,1)S(1)}, bf16[64,256]{1,0:T(8,128)(2,1)S(1)}, u32[]{:S(2)}, u32[]{:S(2)}) %collective-permute-start.2) | collective-permute-done | bytes 32800 | tf_op jit(solution)/shard_map/ppermute | solution.py:472
  52.2 0.6 collective-permute-done.13.c_ref
  52.8 0.0 collective-permute-done.14.d_ref
  52.9 1.0 %collective-permute-start.17 = (bf16[16,16,128]{2,1,0:T(8,128)(2,1)S(1)}, bf16[16,16,128]{2,1,0:T(8,128)(2,1)S(1)}, u32[]{:S(2)}, u32[]{:S(2)}) collective-permute-start(bf16[16,16,128]{2,1,0:T(8,128)(2,1)S(1)} %line_sum.1.a_ref), channel_id=1, source_target_pairs={{0,8},{1,9},{2,10},{3,11},{4,12},{5,13},{6,14},{7,15},{8,0},{9,1},... | collective-permute-start | bytes 196616 | tf_op jit(solution)/shard_map/ppermute | solution.py:423
  53.9 2.6 %collective-permute-start.16 = (bf16[16,16,128]{2,1,0:T(8,128)(2,1)S(1)}, bf16[16,16,128]{2,1,0:T(8,128)(2,1)S(1)}, u32[]{:S(2)}, u32[]{:S(2)}) collective-permute-start(bf16[16,16,128]{2,1,0:T(8,128)(2,1)S(1)} %line_sum.1.a_ref), channel_id=1, source_target_pairs={{0,16},{1,17},{2,18},{3,19},{4,20},{5,21},{6,22},{7,23},{8,24},{9,... | collective-permute-start | bytes 196616 | tf_op jit(solution)/shard_map/ppermute | solution.py:423
  56.5 0.8 %collective-permute-start.15 = (bf16[16,16,128]{2,1,0:T(8,128)(2,1)S(1)}, bf16[16,16,128]{2,1,0:T(8,128)(2,1)S(1)}, u32[]{:S(2)}, u32[]{:S(2)}) collective-permute-start(bf16[16,16,128]{2,1,0:T(8,128)(2,1)S(1)} %line_sum.1.a_ref), channel_id=1, source_target_pairs={{0,24},{1,25},{2,26},{3,27},{4,28},{5,29},{6,30},{7,31},{8,16},{9,... | collective-permute-start | bytes 196616 | tf_op jit(solution)/shard_map/ppermute | solution.py:423
  57.3 3.0 %collective-permute-done.16.c_ref = bf16[16,16,128]{2,1,0:T(8,128)(2,1)S(1)} collective-permute-done((bf16[16,16,128]{2,1,0:T(8,128)(2,1)S(1)}, bf16[16,16,128]{2,1,0:T(8,128)(2,1)S(1)}, u32[]{:S(2)}, u32[]{:S(2)}) %collective-permute-start.16) | collective-permute-done | bytes 65568 | tf_op jit(solution)/shard_map/ppermute | solution.py:423
  60.3 2.3 %collective-permute-done.15.b_ref = bf16[16,16,128]{2,1,0:T(8,128)(2,1)S(1)} collective-permute-done((bf16[16,16,128]{2,1,0:T(8,128)(2,1)S(1)}, bf16[16,16,128]{2,1,0:T(8,128)(2,1)S(1)}, u32[]{:S(2)}, u32[]{:S(2)}) %collective-permute-start.15) | collective-permute-done | bytes 65568 | tf_op jit(solution)/shard_map/ppermute | solution.py:423
  62.6 0.9 %collective-permute-start.20 = (bf16[4,16,16,128]{3,2,1,0:T(8,128)(2,1)S(1)}, bf16[4,16,16,128]{3,2,1,0:T(8,128)(2,1)S(1)}, u32[]{:S(2)}, u32[]{:S(2)}) collective-permute-start(bf16[4,16,16,128]{3,2,1,0:T(8,128)(2,1)S(1)} %line_gather.1.rest_0_.a_ref), channel_id=1, source_target_pairs={{0,4},{1,5},{2,6},{3,7},{4,0},{5,1},{6,2},{7,3},{8,12},{9,13},{10,... | collective-permute-start | bytes 786440 | tf_op jit(solution)/shard_map/ppermute | solution.py:423
  63.5 0.6 collective-permute-start.19
  64.1 2.1 %collective-permute-start.18 = (bf16[4,16,16,128]{3,2,1,0:T(8,128)(2,1)S(1)}, bf16[4,16,16,128]{3,2,1,0:T(8,128)(2,1)S(1)}, u32[]{:S(2)}, u32[]{:S(2)}) collective-permute-start(bf16[4,16,16,128]{3,2,1,0:T(8,128)(2,1)S(1)} %line_gather.1.rest_0_.a_ref), channel_id=1, source_target_pairs={{0,5},{1,4},{2,7},{3,6},{4,1},{5,0},{6,3},{7,2},{8,13},{9,12},{10,... | collective-permute-start | bytes 786440 | tf_op jit(solution)/shard_map/ppermute | solution.py:423
  66.2 7.4 %grad_x.1 = (bf16[16,128,256]{2,1,0:T(8,128)(2,1)}, bf16[16,8,4,256]{3,2,1,0:T(4,128)(2,1)}, f32[8,128]{1,0:T(8,128)S(1)}) custom-call(s32[1]{0:T(128)S(6)} %copy.23.count_ref, bf16[16,8,16,256]{3,2,1,0:T(8,128)(2,1)S(1)} %get-tuple-element.43.xt_ref, bf16[16,8,16,256]{3,2,1,0:T(8,128)(2,1)S(1)} %get-tuple-element.46.gy_ref, ...), custom_call_target="tpu_custom_call" | custom-call | flops 2684354560 | bytes 7147524 | tf_op jit(solution)/shard_map/grad_x/pallas_call | solution.py:399
  73.6 1.3 %collective-permute-done.19.c_ref = bf16[4,16,16,128]{3,2,1,0:T(8,128)(2,1)S(1)} collective-permute-done((bf16[4,16,16,128]{3,2,1,0:T(8,128)(2,1)S(1)}, bf16[4,16,16,128]{3,2,1,0:T(8,128)(2,1)S(1)}, u32[]{:S(2)}, u32[]{:S(2)}) %collective-permute-start.19) | collective-permute-done | bytes 262176 | tf_op jit(solution)/shard_map/ppermute | solution.py:423
  74.9 0.1 plane_gather.1.half_ref
  75.0 0.1 collective-permute-start.21
  75.1 1.5 %finish.2 = (f32[9,256,256]{2,1,0:T(8,128)}, f32[3,256,256]{2,1,0:T(8,128)}, f32[4,256,256]{2,1,0:T(8,128)}) custom-call(bf16[16,16,16,128]{3,2,1,0:T(8,128)(2,1)S(1)} %plane_gather.1.half_ref), custom_call_target="tpu_custom_call" | custom-call | bytes 5242880 | tf_op jit(solution)/shard_map/finish/pallas_call | solution.py:399
  76.6 1.2 %collective-permute-done.21.half_ref = bf16[16,16,16,128]{3,2,1,0:T(8,128)(2,1)S(1)} collective-permute-done((bf16[16,16,16,128]{3,2,1,0:T(8,128)(2,1)S(1)}, bf16[16,16,16,128]{3,2,1,0:T(8,128)(2,1)S(1)}, u32[]{:S(2)}, u32[]{:S(2)}) %collective-permute-start.21) | collective-permute-done | bytes 1048608 | tf_op jit(solution)/shard_map/ppermute | solution.py:423
  77.7 1.5 %finish.3 = (f32[9,256,256]{2,1,0:T(8,128)}, f32[3,256,256]{2,1,0:T(8,128)}, f32[4,256,256]{2,1,0:T(8,128)}) custom-call(bf16[16,16,16,128]{3,2,1,0:T(8,128)(2,1)S(1)} %collective-permute-done.21.half_ref, f32[9,256,256]{2,1,0:T(8,128)} %get-tuple-element.73.rest_0_, ...), custom_call_target="tpu_custom_call", output_to_operand_aliasing={{0}: (1, {}), {1}: (2, {}), {2}: (3, {})} | custom-call | bytes 9437184 | tf_op jit(solution)/shard_map/finish/pallas_call | solution.py:399
  (24 shorter events, 0.1 us)
Async XLA Ops:
  1.3 1.2 %copy-start = (bf16[16,16,8,256]{3,2,1,0:T(8,128)(2,1)S(1)}, bf16[16,16,8,256]{3,2,1,0:T(8,128)(2,1)}, u32[]{:S(2)}) copy-start(bf16[16,16,8,256]{3,2,1,0:T(8,128)(2,1)} %param.6) | copy-start | bytes 3145732
  2.5 0.9 %copy-start.1 = (bf16[16,8,4,256]{3,2,1,0:T(4,128)(2,1)S(1)}, bf16[16,8,4,256]{3,2,1,0:T(4,128)(2,1)}, u32[]{:S(2)}) copy-start(bf16[16,8,4,256]{3,2,1,0:T(4,128)(2,1)} %cot_ref.3) | copy-start | bytes 786436
  3.5 10.7 %copy-start.2 = (bf16[16,8,4,256]{3,2,1,0:T(4,128)(2,1)S(1)}, bf16[16,8,4,256]{3,2,1,0:T(4,128)(2,1)}, u32[]{:S(2)}) copy-start(bf16[16,8,4,256]{3,2,1,0:T(4,128)(2,1)} %cot_ref.3) | copy-start | bytes 786436
  3.5 10.8 %copy-start.4 = (bf16[2,2,256,256]{3,2,1,0:T(8,128)(2,1)S(1)}, bf16[2,2,256,256]{3,2,1,0:T(8,128)(2,1)}, u32[]{:S(2)}) copy-start(bf16[2,2,256,256]{3,2,1,0:T(8,128)(2,1)} %param.10) | copy-start | bytes 1572868
  3.5 10.8 %copy-start.5 = (bf16[3,256,256]{2,1,0:T(8,128)(2,1)S(1)}, bf16[3,256,256]{2,1,0:T(8,128)(2,1)}, u32[]{:S(2)}) copy-start(bf16[3,256,256]{2,1,0:T(8,128)(2,1)} %wt_ref.5) | copy-start | bytes 1179652
  3.8 5.3 %collective-permute-start = (bf16[128,256]{1,0:T(8,128)(2,1)S(1)}, bf16[128,256]{1,0:T(8,128)(2,1)S(1)}, u32[]{:S(2)}, u32[]{:S(2)}) collective-permute-start(bf16[128,256]{1,0:T(8,128)(2,1)S(1)} %get-tuple-element.42), channel_id=1, source_target_pairs={{0,1},{1,0},{2,3},{3,2},{4,5},{5,4},{6,7},{7,6},{8,9},{9,8},{10,11... | collective-permute-start | bytes 196616 | tf_op jit(solution)/shard_map/ppermute | solution.py:472
  6.8 7.4 %collective-permute-start.1 = (bf16[2,8,4,256]{3,2,1,0:T(4,128)(2,1)S(1)}, bf16[2,8,4,256]{3,2,1,0:T(4,128)(2,1)S(1)}, u32[]{:S(2)}, u32[]{:S(2)}) collective-permute-start(bf16[2,8,4,256]{3,2,1,0:T(4,128)(2,1)S(1)} %get-tuple-element.45), channel_id=1, source_target_pairs={{2,0},{4,2},{6,4},{8,6},{10,8},{12,10},{14,12},{16,14},{18,16},{20... | collective-permute-start | bytes 98312 | tf_op jit(solution)/shard_map/ppermute | solution.py:467
  12.1 6.7 %collective-permute-start.3 = (bf16[9,32,256]{2,1,0:T(8,128)(2,1)S(1)}, bf16[9,32,256]{2,1,0:T(8,128)(2,1)S(1)}, u32[]{:S(2)}, u32[]{:S(2)}) collective-permute-start(bf16[9,32,256]{2,1,0:T(8,128)(2,1)S(1)} %get-tuple-element.50), channel_id=1, source_target_pairs={{0,2},{2,4},{4,6},{6,8},{8,10},{10,12},{12,14},{14,16},{16,18},{18... | collective-permute-start | bytes 442376 | tf_op jit(solution)/shard_map/ppermute | solution.py:467
  14.2 6.5 %copy-start.3 = (bf16[3,3,256,256]{3,2,1,0:T(8,128)(2,1)S(1)}, bf16[3,3,256,256]{3,2,1,0:T(8,128)(2,1)}, u32[]{:S(2)}) copy-start(bf16[3,3,256,256]{3,2,1,0:T(8,128)(2,1)} %param.8) | copy-start | bytes 3538948
  18.8 5.6 %collective-permute-start.4 = (bf16[16,9,16,128]{3,2,1,0:T(8,128)(2,1)S(1)}, bf16[16,9,16,128]{3,2,1,0:T(8,128)(2,1)S(1)}, u32[]{:S(2)}, u32[]{:S(2)}) collective-permute-start(bf16[16,9,16,128]{3,2,1,0:T(8,128)(2,1)S(1)} %pass.2._), channel_id=1, source_target_pairs={{0,2},{1,3},{2,0},{3,1},{4,6},{5,7},{6,4},{7,5},{8,10},{9,11},{10,... | collective-permute-start | bytes 1769480 | tf_op jit(solution)/shard_map/ppermute | solution.py:423
  24.5 6.7 %collective-permute-start.5 = (bf16[4,9,16,128]{3,2,1,0:T(8,128)(2,1)S(1)}, bf16[4,9,16,128]{3,2,1,0:T(8,128)(2,1)S(1)}, u32[]{:S(2)}, u32[]{:S(2)}) collective-permute-start(bf16[4,9,16,128]{3,2,1,0:T(8,128)(2,1)S(1)} %get-tuple-element.56.rest_1_), channel_id=1, source_target_pairs={{0,5},{1,4},{2,7},{3,6},{4,1},{5,0},{6,3},{7,2},{8,13},{9,12},{10,... | collective-permute-start | bytes 442376 | tf_op jit(solution)/shard_map/ppermute | solution.py:423
  31.3 3.1 %collective-permute-start.8 = (bf16[16,7,16,128]{3,2,1,0:T(8,128)(2,1)S(1)}, bf16[16,7,16,128]{3,2,1,0:T(8,128)(2,1)S(1)}, u32[]{:S(2)}, u32[]{:S(2)}) collective-permute-start(bf16[16,7,16,128]{3,2,1,0:T(8,128)(2,1)S(1)} %pass.3), channel_id=1, source_target_pairs={{0,2},{1,3},{2,0},{3,1},{4,6},{5,7},{6,4},{7,5},{8,10},{9,11},{10,... | collective-permute-start | bytes 1376264 | tf_op jit(solution)/shard_map/ppermute | solution.py:423
  31.3 6.7 %collective-permute-start.6 = (bf16[4,9,16,128]{3,2,1,0:T(8,128)(2,1)S(1)}, bf16[4,9,16,128]{3,2,1,0:T(8,128)(2,1)S(1)}, u32[]{:S(2)}, u32[]{:S(2)}) collective-permute-start(bf16[4,9,16,128]{3,2,1,0:T(8,128)(2,1)S(1)} %get-tuple-element.57.rest_2_), channel_id=1, source_target_pairs={{0,1},{1,0},{2,3},{3,2},{4,5},{5,4},{6,7},{7,6},{8,9},{9,8},{10,11... | collective-permute-start | bytes 442376 | tf_op jit(solution)/shard_map/ppermute | solution.py:423
  32.8 6.7 %collective-permute-start.7 = (bf16[4,9,16,128]{3,2,1,0:T(8,128)(2,1)S(1)}, bf16[4,9,16,128]{3,2,1,0:T(8,128)(2,1)S(1)}, u32[]{:S(2)}, u32[]{:S(2)}) collective-permute-start(bf16[4,9,16,128]{3,2,1,0:T(8,128)(2,1)S(1)} %get-tuple-element.58.rest_3_), channel_id=1, source_target_pairs={{0,4},{1,5},{2,6},{3,7},{4,0},{5,1},{6,2},{7,3},{8,12},{9,13},{10,... | collective-permute-start | bytes 442376 | tf_op jit(solution)/shard_map/ppermute | solution.py:423
  34.4 7.5 %collective-permute-start.9 = (bf16[4,7,16,128]{3,2,1,0:T(8,128)(2,1)S(1)}, bf16[4,7,16,128]{3,2,1,0:T(8,128)(2,1)S(1)}, u32[]{:S(2)}, u32[]{:S(2)}) collective-permute-start(bf16[4,7,16,128]{3,2,1,0:T(8,128)(2,1)S(1)} %get-tuple-element.63), channel_id=1, source_target_pairs={{0,5},{1,4},{2,7},{3,6},{4,1},{5,0},{6,3},{7,2},{8,13},{9,12},{10,... | collective-permute-start | bytes 344072 | tf_op jit(solution)/shard_map/ppermute | solution.py:423
  35.7 7.3 %collective-permute-start.10 = (bf16[4,7,16,128]{3,2,1,0:T(8,128)(2,1)S(1)}, bf16[4,7,16,128]{3,2,1,0:T(8,128)(2,1)S(1)}, u32[]{:S(2)}, u32[]{:S(2)}) collective-permute-start(bf16[4,7,16,128]{3,2,1,0:T(8,128)(2,1)S(1)} %get-tuple-element.64), channel_id=1, source_target_pairs={{0,1},{1,0},{2,3},{3,2},{4,5},{5,4},{6,7},{7,6},{8,9},{9,8},{10,11... | collective-permute-start | bytes 344072 | tf_op jit(solution)/shard_map/ppermute | solution.py:423
  36.4 7.3 %collective-permute-start.11 = (bf16[4,7,16,128]{3,2,1,0:T(8,128)(2,1)S(1)}, bf16[4,7,16,128]{3,2,1,0:T(8,128)(2,1)S(1)}, u32[]{:S(2)}, u32[]{:S(2)}) collective-permute-start(bf16[4,7,16,128]{3,2,1,0:T(8,128)(2,1)S(1)} %get-tuple-element.65), channel_id=1, source_target_pairs={{0,4},{1,5},{2,6},{3,7},{4,0},{5,1},{6,2},{7,3},{8,12},{9,13},{10,... | collective-permute-start | bytes 344072 | tf_op jit(solution)/shard_map/ppermute | solution.py:423
  43.9 8.4 %collective-permute-start.12 = (bf16[16,16,128]{2,1,0:T(8,128)(2,1)S(1)}, bf16[16,16,128]{2,1,0:T(8,128)(2,1)S(1)}, u32[]{:S(2)}, u32[]{:S(2)}) collective-permute-start(bf16[16,16,128]{2,1,0:T(8,128)(2,1)S(1)} %get-tuple-element.67), channel_id=1, source_target_pairs={{0,24},{1,25},{2,26},{3,27},{4,28},{5,29},{6,30},{7,31},{8,16},{9,... | collective-permute-start | bytes 196616 | tf_op jit(solution)/shard_map/ppermute | solution.py:423
  47.5 5.3 %collective-permute-start.13 = (bf16[16,16,128]{2,1,0:T(8,128)(2,1)S(1)}, bf16[16,16,128]{2,1,0:T(8,128)(2,1)S(1)}, u32[]{:S(2)}, u32[]{:S(2)}) collective-permute-start(bf16[16,16,128]{2,1,0:T(8,128)(2,1)S(1)} %get-tuple-element.68), channel_id=1, source_target_pairs={{0,16},{1,17},{2,18},{3,19},{4,20},{5,21},{6,22},{7,23},{8,24},{9,... | collective-permute-start | bytes 196616 | tf_op jit(solution)/shard_map/ppermute | solution.py:423
  47.5 5.3 %collective-permute-start.14 = (bf16[16,16,128]{2,1,0:T(8,128)(2,1)S(1)}, bf16[16,16,128]{2,1,0:T(8,128)(2,1)S(1)}, u32[]{:S(2)}, u32[]{:S(2)}) collective-permute-start(bf16[16,16,128]{2,1,0:T(8,128)(2,1)S(1)} %get-tuple-element.69), channel_id=1, source_target_pairs={{0,8},{1,9},{2,10},{3,11},{4,12},{5,13},{6,14},{7,15},{8,0},{9,1},... | collective-permute-start | bytes 196616 | tf_op jit(solution)/shard_map/ppermute | solution.py:423
  48.3 3.9 %collective-permute-start.2 = (bf16[64,256]{1,0:T(8,128)(2,1)S(1)}, bf16[64,256]{1,0:T(8,128)(2,1)S(1)}, u32[]{:S(2)}, u32[]{:S(2)}) collective-permute-start(bf16[64,256]{1,0:T(8,128)(2,1)S(1)} %get-tuple-element.48), channel_id=1, source_target_pairs={{0,1},{1,0},{2,3},{3,2},{4,5},{5,4},{6,7},{7,6},{8,9},{9,8},{10,11... | collective-permute-start | bytes 98312 | tf_op jit(solution)/shard_map/ppermute | solution.py:472
  52.9 4.5 %collective-permute-start.17 = (bf16[16,16,128]{2,1,0:T(8,128)(2,1)S(1)}, bf16[16,16,128]{2,1,0:T(8,128)(2,1)S(1)}, u32[]{:S(2)}, u32[]{:S(2)}) collective-permute-start(bf16[16,16,128]{2,1,0:T(8,128)(2,1)S(1)} %line_sum.1.a_ref), channel_id=1, source_target_pairs={{0,8},{1,9},{2,10},{3,11},{4,12},{5,13},{6,14},{7,15},{8,0},{9,1},... | collective-permute-start | bytes 196616 | tf_op jit(solution)/shard_map/ppermute | solution.py:423
  53.9 6.4 %collective-permute-start.16 = (bf16[16,16,128]{2,1,0:T(8,128)(2,1)S(1)}, bf16[16,16,128]{2,1,0:T(8,128)(2,1)S(1)}, u32[]{:S(2)}, u32[]{:S(2)}) collective-permute-start(bf16[16,16,128]{2,1,0:T(8,128)(2,1)S(1)} %line_sum.1.a_ref), channel_id=1, source_target_pairs={{0,16},{1,17},{2,18},{3,19},{4,20},{5,21},{6,22},{7,23},{8,24},{9,... | collective-permute-start | bytes 196616 | tf_op jit(solution)/shard_map/ppermute | solution.py:423
  56.5 6.1 %collective-permute-start.15 = (bf16[16,16,128]{2,1,0:T(8,128)(2,1)S(1)}, bf16[16,16,128]{2,1,0:T(8,128)(2,1)S(1)}, u32[]{:S(2)}, u32[]{:S(2)}) collective-permute-start(bf16[16,16,128]{2,1,0:T(8,128)(2,1)S(1)} %line_sum.1.a_ref), channel_id=1, source_target_pairs={{0,24},{1,25},{2,26},{3,27},{4,28},{5,29},{6,30},{7,31},{8,16},{9,... | collective-permute-start | bytes 196616 | tf_op jit(solution)/shard_map/ppermute | solution.py:423
  62.6 11.0 %collective-permute-start.20 = (bf16[4,16,16,128]{3,2,1,0:T(8,128)(2,1)S(1)}, bf16[4,16,16,128]{3,2,1,0:T(8,128)(2,1)S(1)}, u32[]{:S(2)}, u32[]{:S(2)}) collective-permute-start(bf16[4,16,16,128]{3,2,1,0:T(8,128)(2,1)S(1)} %line_gather.1.rest_0_.a_ref), channel_id=1, source_target_pairs={{0,4},{1,5},{2,6},{3,7},{4,0},{5,1},{6,2},{7,3},{8,12},{9,13},{10,... | collective-permute-start | bytes 786440 | tf_op jit(solution)/shard_map/ppermute | solution.py:423
  63.5 11.5 %collective-permute-start.19 = (bf16[4,16,16,128]{3,2,1,0:T(8,128)(2,1)S(1)}, bf16[4,16,16,128]{3,2,1,0:T(8,128)(2,1)S(1)}, u32[]{:S(2)}, u32[]{:S(2)}) collective-permute-start(bf16[4,16,16,128]{3,2,1,0:T(8,128)(2,1)S(1)} %line_gather.1.rest_0_.a_ref), channel_id=1, source_target_pairs={{0,1},{1,0},{2,3},{3,2},{4,5},{5,4},{6,7},{7,6},{8,9},{9,8},{10,11... | collective-permute-start | bytes 786440 | tf_op jit(solution)/shard_map/ppermute | solution.py:423
  64.1 10.9 %collective-permute-start.18 = (bf16[4,16,16,128]{3,2,1,0:T(8,128)(2,1)S(1)}, bf16[4,16,16,128]{3,2,1,0:T(8,128)(2,1)S(1)}, u32[]{:S(2)}, u32[]{:S(2)}) collective-permute-start(bf16[4,16,16,128]{3,2,1,0:T(8,128)(2,1)S(1)} %line_gather.1.rest_0_.a_ref), channel_id=1, source_target_pairs={{0,5},{1,4},{2,7},{3,6},{4,1},{5,0},{6,3},{7,2},{8,13},{9,12},{10,... | collective-permute-start | bytes 786440 | tf_op jit(solution)/shard_map/ppermute | solution.py:423
  75.0 2.7 %collective-permute-start.21 = (bf16[16,16,16,128]{3,2,1,0:T(8,128)(2,1)S(1)}, bf16[16,16,16,128]{3,2,1,0:T(8,128)(2,1)S(1)}, u32[]{:S(2)}, u32[]{:S(2)}) collective-permute-start(bf16[16,16,16,128]{3,2,1,0:T(8,128)(2,1)S(1)} %plane_gather.1.half_ref), channel_id=1, source_target_pairs={{0,2},{1,3},{2,0},{3,1},{4,6},{5,7},{6,4},{7,5},{8,10},{9,11},{10,... | collective-permute-start | bytes 3145736 | tf_op jit(solution)/shard_map/ppermute | solution.py:423

commit v12 on v11

--- a/solution.py
+++ b/solution.py
@@ -47,9 +47,10 @@
     return lambda frame, slot: (frame == slot) & (slot < count)
 
 
-def own_and_next(count):
+def own_and_next(count, blocks):
+    after = jnp.where(lax.axis_index("tm") < blocks - 1, count, 64)
     return lambda frame, slot: ((frame < OWN) & (frame == slot) & (slot < count)) | (
-        (frame >= OWN) & (slot == count + frame - OWN)
+        (frame >= OWN) & (slot == after + frame - OWN)
     )
 
 
@@ -110,9 +111,8 @@
     acts_ref[:, 0] = edge
     acts_ref[:, cols + 1] = edge
     place = to_slots(16, SLOTS, own_frames(count))
-    a, b = iotas(32, 256)
-    pick = ((a >> 1) == (b >> 4)) & ((b & 15) == count - 2 + (a & 1))
-    pick = jnp.where(pick, 1.0, 0.0).astype(BF)
+    last = silu_norm(x_ref[pl.ds(count - 2, 2)].reshape(2 * rows * cols, CH).astype(F32))
+    last_ref[0 : 2 * rows * cols] = last.astype(BF)
 
     def rows_of(q, _):
         at = pl.multiple_of(q * 16, 16)
@@ -120,7 +120,6 @@
         v = mm(place, piece)
         xt_ref[pl.ds(2 * q, 2)] = v.astype(BF).reshape(2, cols, SLOTS, CH)
         a = silu_norm(v).astype(BF)
-        last_ref[q] = mm(pick, a).astype(BF)
         acts_ref[pl.ds(2 * q + 1, 2), 1 : cols + 1] = a.reshape(2, cols, SLOTS, CH)
         flipped = a.T
         for i in range(3):
@@ -136,17 +135,26 @@
         at = (row - i + 2) * 128
         at_ref[i * CH : i * CH + CH, at : at + 128] = a.T
         halo.append(a)
-    last_ref[rows // 2] = mm(pick, jnp.concatenate(halo, 0)).astype(BF)
+    a, b = iotas(32, 256)
+    pick = ((a & 15) == (b >> 4)) & ((b & 15) == count - 2 + (a >> 4))
+    pick = jnp.where(pick, 1.0, 0.0).astype(BF)
+    last_ref[2 * rows * cols :] = mm(pick, jnp.concatenate(halo, 0)).astype(BF)
 
 
 def spatial_kernel(count_ref, acts_in, prev_ref, ws_ref, _, acts_ref, sp_ref):
     rows, cols = sp_ref.shape[0], sp_ref.shape[1]
     a, b = iotas(256, 32)
-    place = ((a >> 4) == (b >> 1)) & ((a & 15) == OWN + (b & 1))
+    place = ((a >> 4) == (b & 15)) & ((a & 15) == OWN + (b >> 4)) & (lax.axis_index("tm") > 0)
     place = jnp.where(place, 1.0, 0.0).astype(BF)
+    size = rows * cols
     for q in range(rows // 2 + 1):
-        both = slice(0, rows + 2, rows + 1) if q == rows // 2 else slice(2 * q + 1, 2 * q + 3)
-        prev = mm(place, prev_ref[q]).astype(BF).reshape(2, cols, SLOTS, CH)
+        if q == rows // 2:
+            both, prev = slice(0, rows + 2, rows + 1), prev_ref[2 * size :]
+        else:
+            both = slice(2 * q + 1, 2 * q + 3)
+            parts = [prev_ref[f * size + q * 16 : f * size + q * 16 + 16] for f in range(2)]
+            prev = jnp.concatenate(parts, 0)
+        prev = mm(place, prev).astype(BF).reshape(2, cols, SLOTS, CH)
         for k, row in enumerate(range(rows + 2)[both]):
             acts_ref[row, 1 : cols + 1] = acts_ref[row, 1 : cols + 1] + prev[k]
 
@@ -164,7 +172,7 @@
 
 
 def grad_spatial_kernel(
-    bands, count_ref, at_ref, cot_ref, nxt_ref, wt_ref, wd_ref,
+    blocks, bands, count_ref, at_ref, cot_ref, nxt_ref, wt_ref, wd_ref,
     cott_ref, gy_ref, gs_ref, keep_ref, send_ref, *edge_refs,
 ):
     count = count_ref[0]
@@ -174,7 +182,7 @@
     gs_ref[:, 0] = edge
     gs_ref[:, cols + 1] = edge
 
-    place_next = to_slots(16, SLOTS, own_and_next(count))
+    place_next = to_slots(16, SLOTS, own_and_next(count, blocks))
     halves = []
     for q in range(rows * cols // 64):
         four = slice(q * 4, q * 4 + 4)
@@ -467,6 +475,11 @@
     return lax.ppermute(value, axis, pairs)
 
 
+def around(value, axis, by):
+    count = lax.axis_size(axis)
+    return lax.ppermute(value, axis, [(i, (i + by) % count) for i in range(count)])
+
+
 def from_bands(parts):
     if len(parts) == 1:
         got = lax.ppermute(parts[0], "grp", [(0, 1), (1, 0)])
@@ -496,18 +509,18 @@
         flops=tap // 8,
     )
     top, bot = from_bands(edge)
-    nxt_got = along(nxt, "tm", -1)
+    nxt_got = around(nxt, "tm", -1)
     xt, acts, at, last_two = call(
         functools.partial(acts_kernel, grp),
         "acts",
         [count, (VMEM, x), (VMEM, top), (VMEM, bot)],
-        [(VMEM, tile), (VMEM, padded), (VMEM, (3 * ch, (rows + 4) * 128)), (VMEM, (rows // 2 + 1, 32, ch))],
+        [(VMEM, tile), (VMEM, padded), (VMEM, (3 * ch, (rows + 4) * 128)), (VMEM, (2 * wide + 32, ch))],
         flops=2 * tap,
     )
-    prev = along(last_two, "tm", 1)
+    prev = around(last_two, "tm", 1)
     half = (16, 9, 16, ch // 2)
     cott, gy, gs, keep_a, send_a, *edge = call(
-        functools.partial(grad_spatial_kernel, grp),
+        functools.partial(grad_spatial_kernel, tm, grp),
         "grad_spatial",
         [count, (VMEM, at), (VMEM, cotangent), (VMEM, nxt_got), (VMEM, wt), (VMEM, wd)],
         [(VMEM, (rows // 2, cols // 2, slots, ch)), (VMEM, tile),

time: 79.4 us -> 76.8 us (0.967)
  starting transfers between devices: 30.6 us -> 25.7 us
  waiting for transfers between devices: 19.8 us -> 23.4 us
  Pallas kernels: 25.1 us -> 23.9 us
    ppermute x18, starting transfers between devices: 23.7 us -> 17.5 us  [swap(): return lax.ppermute(value, AXES, [(d, d ^ flip) for d in range(tm * grp)])]
    ppermute x18, waiting for transfers between devices: 15.4 us -> 18.3 us  [swap(): return lax.ppermute(value, AXES, [(d, d ^ flip) for d in range(tm * grp)])]
    ppermute x2, waiting for transfers between devices: 0.01 us -> 2.67 us  [around(): lax.ppermute(value, axis, [(i, (i + by) % count) for i in range(count)])]
    ppermute x2, waiting for transfers between devices: 4.36 us -> 2.46 us  [from_bands(): got = lax.ppermute(parts[0], 'grp', [(0, 1), (1, 0)])]
    pallas_call x16, Pallas kernels: 25.1 us -> 23.9 us  [call(): pl.pallas_call(kernel, out_shape=shapes, in_specs=[s for s, _ in ins], ou...]
    ppermute x2, starting transfers between devices: 3.54 us -> 4.49 us  [from_bands(): got = lax.ppermute(parts[0], 'grp', [(0, 1), (1, 0)])]
  transfers between devices with their start and end apart: 22 -> 22, of which waited for: 12 -> 14; matrix products, arithmetic and copies ran while one was open for 0% -> 0% of each run, Pallas kernels for 29% -> 28%
where the time goes in v12:
time: 76.8 us; the launch traced here: 76.6 us
  starting transfers between devices  25.7 us (33%)
  Pallas kernels  23.9 us (31%)
  waiting for transfers between devices  23.4 us (30%)
  local copies, waits for them, and re-layouts  2.18 us (3%)
  between operations  1.46 us (2%)
    pallas_call x16, Pallas kernels, call(): pl.pallas_call(kernel, out_shape=shapes, in_specs=[s for s, _ in ins], ou...  23.9 us
    ppermute x18, waiting for transfers between devices, swap(): return lax.ppermute(value, AXES, [(d, d ^ flip) for d in range(tm * grp)])  18.3 us
    ppermute x18, starting transfers between devices, swap(): return lax.ppermute(value, AXES, [(d, d ^ flip) for d in range(tm * grp)])  17.5 us
    ppermute x2, starting transfers between devices, from_bands(): got = lax.ppermute(parts[0], 'grp', [(0, 1), (1, 0)])  4.49 us
    ppermute x2, starting transfers between devices, around(): lax.ppermute(value, axis, [(i, (i + by) % count) for i in range(count)])  3.7 us
    ppermute x2, waiting for transfers between devices, around(): lax.ppermute(value, axis, [(i, (i + by) % count) for i in range(count)])  2.67 us
    ppermute x2, waiting for transfers between devices, from_bands(): got = lax.ppermute(parts[0], 'grp', [(0, 1), (1, 0)])  2.46 us
    unnamed x12, local copies, waits for them, and re-layouts  2.18 us
  transfers between devices with their start and end apart: 22, of which 14 were waited for; matrix products, arithmetic and copies ran while one was open for 0% of the time, Pallas kernels for 28%

profile of v12, /device:TPU:0, one launch (start us, length us, event | category | flops | bytes accessed | tf_op | source)
XLA Modules:
  0.0 76.6 jit_solution(15443314727134839944)
XLA Ops:
  1.3 1.2 %copy-done = bf16[16,16,8,256]{3,2,1,0:T(8,128)(2,1)S(1)} copy-done((bf16[16,16,8,256]{3,2,1,0:T(8,128)(2,1)S(1)}, bf16[16,16,8,256]{3,2,1,0:T(8,128)(2,1)}, u32[]{:S(2)}) %copy-start) | copy-done | bytes 1048600
  2.5 0.9 %copy-done.1 = bf16[16,8,4,256]{3,2,1,0:T(4,128)(2,1)S(1)} copy-done((bf16[16,8,4,256]{3,2,1,0:T(4,128)(2,1)S(1)}, bf16[16,8,4,256]{3,2,1,0:T(4,128)(2,1)}, u32[]{:S(2)}) %copy-start.1) | copy-done | bytes 262168
  3.5 0.3 edges.1
  3.8 3.0 %collective-permute-start = (bf16[128,256]{1,0:T(8,128)(2,1)S(1)}, bf16[128,256]{1,0:T(8,128)(2,1)S(1)}, u32[]{:S(2)}, u32[]{:S(2)}) collective-permute-start(bf16[128,256]{1,0:T(8,128)(2,1)S(1)} %get-tuple-element.42), channel_id=1, source_target_pairs={{0,1},{1,0},{2,3},{3,2},{4,5},{5,4},{6,7},{7,6},{8,9},{9,8},{10,11... | collective-permute-start | bytes 196616 | tf_op jit(solution)/shard_map/ppermute | solution.py:485
  6.8 3.7 %collective-permute-start.1 = (bf16[2,8,4,256]{3,2,1,0:T(4,128)(2,1)S(1)}, bf16[2,8,4,256]{3,2,1,0:T(4,128)(2,1)S(1)}, u32[]{:S(2)}, u32[]{:S(2)}) collective-permute-start(bf16[2,8,4,256]{3,2,1,0:T(4,128)(2,1)S(1)} %get-tuple-element.45), channel_id=1, source_target_pairs={{0,30},{2,0},{4,2},{6,4},{8,6},{10,8},{12,10},{14,12},{16,14},{18,... | collective-permute-start | bytes 98312 | tf_op jit(solution)/shard_map/ppermute | solution.py:480
  10.5 1.8 %acts.1 = (bf16[16,8,16,256]{3,2,1,0:T(8,128)(2,1)S(1)}, bf16[18,10,16,256]{3,2,1,0:T(8,128)(2,1)S(1)}, bf16[768,2560]{1,0:T(8,128)(2,1)S(1)}, bf16[288,256]{1,0:T(8,128)(2,1)S(1)}) custom-call(s32[1]{0:T(128)S(6)} %copy.23.count_ref, bf16[16,128,256]{2,1,0:T(8,128)(2,1)S(1)} %bitcast.7, bf16[128,256]{1,0:T(8,128)(2,1)S(1)} %collective-permute-done.top_ref.bot_ref, ...), custom_call_target="tpu_custom_call" | custom-call | flops 536870912 | bytes 7782404 | tf_op jit(solution)/shard_map/acts/pallas_call | solution.py:407
  12.3 0.0 collective-permute-start.3
  12.3 0.0 copy-start.3
  12.3 4.5 %grad_spatial.1 = (bf16[8,4,16,256]{3,2,1,0:T(8,128)(2,1)S(1)}, bf16[16,8,16,256]{3,2,1,0:T(8,128)(2,1)S(1)}, bf16[16,10,16,256]{3,2,1,0:T(8,128)(2,1)S(1)}, bf1...) custom-call(s32[1]{0:T(128)S(6)} %copy.23.count_ref, ...), custom_call_target="tpu_custom_call" | custom-call | flops 3758096384 | bytes 8978436 | tf_op jit(solution)/shard_map/grad_spatial/pallas_call | solution.py:407
  16.9 2.7 %collective-permute-done.3.__1_.prev_ref = bf16[288,256]{1,0:T(8,128)(2,1)S(1)} collective-permute-done((bf16[288,256]{1,0:T(8,128)(2,1)S(1)}, bf16[288,256]{1,0:T(8,128)(2,1)S(1)}, u32[]{:S(2)}, u32[]{:S(2)}) %collective-permute-start.3) | collective-permute-done | bytes 147488 | tf_op jit(solution)/shard_map/ppermute | solution.py:480
  19.6 3.6 %spatial.1 = (bf16[18,10,16,256]{3,2,1,0:T(8,128)(2,1)S(1)}, bf16[16,8,16,256]{3,2,1,0:T(8,128)(2,1)S(1)}) custom-call(s32[1]{0:T(128)S(6)} %copy.23.count_ref, bf16[18,10,16,256]{3,2,1,0:T(8,128)(2,1)S(1)} %get-tuple-element.49.acts_in, bf16[288,256]{1,0:T(8,128)(2,1)S(1)} %collective-permute-done.3.__1_.prev_ref, ...), custom_call_target="tpu_custom_call", output_to_operand_aliasing={{0}: (1, {})} | custom-call | flops 2415919104 | bytes 5324804 | tf_op jit(solution)/shard_map/spatial/pallas_call | solution.py:407
  23.1 0.2 plane_send.2
  23.3 0.6 collective-permute-start.5
  23.9 2.8 %forward.1 = (bf16[512,256]{1,0:T(8,128)(2,1)S(1)}, bf16[16,7,16,128]{3,2,1,0:T(8,128)(2,1)S(1)}, bf16[16,7,16,128]{3,2,1,0:T(8,128)(2,1)S(1)}) custom-call(s32[1]{0:T(128)S(6)} %copy.23.count_ref, bf16[16,8,16,256]{3,2,1,0:T(8,128)(2,1)S(1)} %get-tuple-element.43.xt_ref, bf16[16,8,16,256]{3,2,1,0:T(8,128)(2,1)S(1)} %get-tuple-element.52.rest_0_.sp_ref, ...), custom_call_target="tpu_custom_call" | custom-call | flops 2684354560 | bytes 5505028 | tf_op jit(solution)/shard_map/forward/pallas_call | solution.py:407
  26.7 3.8 %collective-permute-done.5.__1_.refs_1_ = bf16[4,9,16,128]{3,2,1,0:T(8,128)(2,1)S(1)} collective-permute-done((bf16[4,9,16,128]{3,2,1,0:T(8,128)(2,1)S(1)}, bf16[4,9,16,128]{3,2,1,0:T(8,128)(2,1)S(1)}, u32[]{:S(2)}, u32[]{:S(2)}) %collective-permute-start.5) | collective-permute-done | bytes 147488 | tf_op jit(solution)/shard_map/ppermute | solution.py:431
  30.5 0.6 collective-permute-start.6
  31.1 0.3 collective-permute-start.7
  31.4 1.0 %collective-permute-done.8.got_ref = bf16[16,7,16,128]{3,2,1,0:T(8,128)(2,1)S(1)} collective-permute-done((bf16[16,7,16,128]{3,2,1,0:T(8,128)(2,1)S(1)}, bf16[16,7,16,128]{3,2,1,0:T(8,128)(2,1)S(1)}, u32[]{:S(2)}, u32[]{:S(2)}) %collective-permute-start.8) | collective-permute-done | bytes 458784 | tf_op jit(solution)/shard_map/ppermute | solution.py:431
  32.3 0.1 plane_send.3
  32.5 1.7 %collective-permute-start.9 = (bf16[4,7,16,128]{3,2,1,0:T(8,128)(2,1)S(1)}, bf16[4,7,16,128]{3,2,1,0:T(8,128)(2,1)S(1)}, u32[]{:S(2)}, u32[]{:S(2)}) collective-permute-start(bf16[4,7,16,128]{3,2,1,0:T(8,128)(2,1)S(1)} %get-tuple-element.63), channel_id=1, source_target_pairs={{0,5},{1,4},{2,7},{3,6},{4,1},{5,0},{6,3},{7,2},{8,13},{9,12},{10,... | collective-permute-start | bytes 344072 | tf_op jit(solution)/shard_map/ppermute | solution.py:431
  34.2 0.6 collective-permute-start.10
  34.8 1.2 %collective-permute-start.11 = (bf16[4,7,16,128]{3,2,1,0:T(8,128)(2,1)S(1)}, bf16[4,7,16,128]{3,2,1,0:T(8,128)(2,1)S(1)}, u32[]{:S(2)}, u32[]{:S(2)}) collective-permute-start(bf16[4,7,16,128]{3,2,1,0:T(8,128)(2,1)S(1)} %get-tuple-element.65), channel_id=1, source_target_pairs={{0,4},{1,5},{2,6},{3,7},{4,0},{5,1},{6,2},{7,3},{8,12},{9,13},{10,... | collective-permute-start | bytes 344072 | tf_op jit(solution)/shard_map/ppermute | solution.py:431
  36.0 1.0 %collective-permute-done.6.refs_2_ = bf16[4,9,16,128]{3,2,1,0:T(8,128)(2,1)S(1)} collective-permute-done((bf16[4,9,16,128]{3,2,1,0:T(8,128)(2,1)S(1)}, bf16[4,9,16,128]{3,2,1,0:T(8,128)(2,1)S(1)}, u32[]{:S(2)}, u32[]{:S(2)}) %collective-permute-start.6) | collective-permute-done | bytes 147488 | tf_op jit(solution)/shard_map/ppermute | solution.py:431
  37.1 0.7 collective-permute-done.7.refs_3_
  37.8 3.4 %collective-permute-done.9.refs_5_ = bf16[4,7,16,128]{3,2,1,0:T(8,128)(2,1)S(1)} collective-permute-done((bf16[4,7,16,128]{3,2,1,0:T(8,128)(2,1)S(1)}, bf16[4,7,16,128]{3,2,1,0:T(8,128)(2,1)S(1)}, u32[]{:S(2)}, u32[]{:S(2)}) %collective-permute-start.9) | collective-permute-done | bytes 114720 | tf_op jit(solution)/shard_map/ppermute | solution.py:431
  41.2 0.5 collective-permute-done.10.refs_6_
  41.7 0.3 collective-permute-done.11.refs_7_
  42.0 0.1 line_send.1
  42.2 2.2 %collective-permute-start.12 = (bf16[16,16,128]{2,1,0:T(8,128)(2,1)S(1)}, bf16[16,16,128]{2,1,0:T(8,128)(2,1)S(1)}, u32[]{:S(2)}, u32[]{:S(2)}) collective-permute-start(bf16[16,16,128]{2,1,0:T(8,128)(2,1)S(1)} %get-tuple-element.67), channel_id=1, source_target_pairs={{0,24},{1,25},{2,26},{3,27},{4,28},{5,29},{6,30},{7,31},{8,16},{9,... | collective-permute-start | bytes 196616 | tf_op jit(solution)/shard_map/ppermute | solution.py:431
  44.3 2.3 %collective-permute-start.14 = (bf16[16,16,128]{2,1,0:T(8,128)(2,1)S(1)}, bf16[16,16,128]{2,1,0:T(8,128)(2,1)S(1)}, u32[]{:S(2)}, u32[]{:S(2)}) collective-permute-start(bf16[16,16,128]{2,1,0:T(8,128)(2,1)S(1)} %get-tuple-element.69), channel_id=1, source_target_pairs={{0,8},{1,9},{2,10},{3,11},{4,12},{5,13},{6,14},{7,15},{8,0},{9,1},... | collective-permute-start | bytes 196616 | tf_op jit(solution)/shard_map/ppermute | solution.py:431
  46.6 1.5 %collective-permute-start.2 = (bf16[64,256]{1,0:T(8,128)(2,1)S(1)}, bf16[64,256]{1,0:T(8,128)(2,1)S(1)}, u32[]{:S(2)}, u32[]{:S(2)}) collective-permute-start(bf16[64,256]{1,0:T(8,128)(2,1)S(1)} %get-tuple-element.48), channel_id=1, source_target_pairs={{0,1},{1,0},{2,3},{3,2},{4,5},{5,4},{6,7},{7,6},{8,9},{9,8},{10,11... | collective-permute-start | bytes 98312 | tf_op jit(solution)/shard_map/ppermute | solution.py:485
  48.1 2.5 %collective-permute-done.2.rest_0_.top_ref.bot_ref = bf16[64,256]{1,0:T(8,128)(2,1)S(1)} collective-permute-done((bf16[64,256]{1,0:T(8,128)(2,1)S(1)}, bf16[64,256]{1,0:T(8,128)(2,1)S(1)}, u32[]{:S(2)}, u32[]{:S(2)}) %collective-permute-start.2) | collective-permute-done | bytes 32800 | tf_op jit(solution)/shard_map/ppermute | solution.py:485
  50.6 0.4 collective-permute-start.17
  51.0 2.4 %collective-permute-start.16 = (bf16[16,16,128]{2,1,0:T(8,128)(2,1)S(1)}, bf16[16,16,128]{2,1,0:T(8,128)(2,1)S(1)}, u32[]{:S(2)}, u32[]{:S(2)}) collective-permute-start(bf16[16,16,128]{2,1,0:T(8,128)(2,1)S(1)} %line_sum.1.a_ref), channel_id=1, source_target_pairs={{0,16},{1,17},{2,18},{3,19},{4,20},{5,21},{6,22},{7,23},{8,24},{9,... | collective-permute-start | bytes 196616 | tf_op jit(solution)/shard_map/ppermute | solution.py:431
  53.4 1.7 %collective-permute-start.15 = (bf16[16,16,128]{2,1,0:T(8,128)(2,1)S(1)}, bf16[16,16,128]{2,1,0:T(8,128)(2,1)S(1)}, u32[]{:S(2)}, u32[]{:S(2)}) collective-permute-start(bf16[16,16,128]{2,1,0:T(8,128)(2,1)S(1)} %line_sum.1.a_ref), channel_id=1, source_target_pairs={{0,24},{1,25},{2,26},{3,27},{4,28},{5,29},{6,30},{7,31},{8,16},{9,... | collective-permute-start | bytes 196616 | tf_op jit(solution)/shard_map/ppermute | solution.py:431
  55.1 0.1 collective-permute-done.17.d_ref
  55.2 1.5 %collective-permute-done.16.c_ref = bf16[16,16,128]{2,1,0:T(8,128)(2,1)S(1)} collective-permute-done((bf16[16,16,128]{2,1,0:T(8,128)(2,1)S(1)}, bf16[16,16,128]{2,1,0:T(8,128)(2,1)S(1)}, u32[]{:S(2)}, u32[]{:S(2)}) %collective-permute-start.16) | collective-permute-done | bytes 65568 | tf_op jit(solution)/shard_map/ppermute | solution.py:431
  56.7 2.8 %collective-permute-done.15.b_ref = bf16[16,16,128]{2,1,0:T(8,128)(2,1)S(1)} collective-permute-done((bf16[16,16,128]{2,1,0:T(8,128)(2,1)S(1)}, bf16[16,16,128]{2,1,0:T(8,128)(2,1)S(1)}, u32[]{:S(2)}, u32[]{:S(2)}) %collective-permute-start.15) | collective-permute-done | bytes 65568 | tf_op jit(solution)/shard_map/ppermute | solution.py:431
  59.5 0.9 %collective-permute-start.20 = (bf16[4,16,16,128]{3,2,1,0:T(8,128)(2,1)S(1)}, bf16[4,16,16,128]{3,2,1,0:T(8,128)(2,1)S(1)}, u32[]{:S(2)}, u32[]{:S(2)}) collective-permute-start(bf16[4,16,16,128]{3,2,1,0:T(8,128)(2,1)S(1)} %line_gather.1.rest_0_.a_ref), channel_id=1, source_target_pairs={{0,4},{1,5},{2,6},{3,7},{4,0},{5,1},{6,2},{7,3},{8,12},{9,13},{10,... | collective-permute-start | bytes 786440 | tf_op jit(solution)/shard_map/ppermute | solution.py:431
  60.4 1.3 %collective-permute-start.19 = (bf16[4,16,16,128]{3,2,1,0:T(8,128)(2,1)S(1)}, bf16[4,16,16,128]{3,2,1,0:T(8,128)(2,1)S(1)}, u32[]{:S(2)}, u32[]{:S(2)}) collective-permute-start(bf16[4,16,16,128]{3,2,1,0:T(8,128)(2,1)S(1)} %line_gather.1.rest_0_.a_ref), channel_id=1, source_target_pairs={{0,1},{1,0},{2,3},{3,2},{4,5},{5,4},{6,7},{7,6},{8,9},{9,8},{10,11... | collective-permute-start | bytes 786440 | tf_op jit(solution)/shard_map/ppermute | solution.py:431
  61.7 1.4 %collective-permute-start.18 = (bf16[4,16,16,128]{3,2,1,0:T(8,128)(2,1)S(1)}, bf16[4,16,16,128]{3,2,1,0:T(8,128)(2,1)S(1)}, u32[]{:S(2)}, u32[]{:S(2)}) collective-permute-start(bf16[4,16,16,128]{3,2,1,0:T(8,128)(2,1)S(1)} %line_gather.1.rest_0_.a_ref), channel_id=1, source_target_pairs={{0,5},{1,4},{2,7},{3,6},{4,1},{5,0},{6,3},{7,2},{8,13},{9,12},{10,... | collective-permute-start | bytes 786440 | tf_op jit(solution)/shard_map/ppermute | solution.py:431
  63.0 7.4 %grad_x.1 = (bf16[16,128,256]{2,1,0:T(8,128)(2,1)}, bf16[16,8,4,256]{3,2,1,0:T(4,128)(2,1)}, f32[8,128]{1,0:T(8,128)S(1)}) custom-call(s32[1]{0:T(128)S(6)} %copy.23.count_ref, bf16[16,8,16,256]{3,2,1,0:T(8,128)(2,1)S(1)} %get-tuple-element.43.xt_ref, bf16[16,8,16,256]{3,2,1,0:T(8,128)(2,1)S(1)} %get-tuple-element.46.gy_ref, ...), custom_call_target="tpu_custom_call" | custom-call | flops 2684354560 | bytes 7147524 | tf_op jit(solution)/shard_map/grad_x/pallas_call | solution.py:407
  70.5 1.9 %collective-permute-done.19.c_ref = bf16[4,16,16,128]{3,2,1,0:T(8,128)(2,1)S(1)} collective-permute-done((bf16[4,16,16,128]{3,2,1,0:T(8,128)(2,1)S(1)}, bf16[4,16,16,128]{3,2,1,0:T(8,128)(2,1)S(1)}, u32[]{:S(2)}, u32[]{:S(2)}) %collective-permute-start.19) | collective-permute-done | bytes 262176 | tf_op jit(solution)/shard_map/ppermute | solution.py:431
  72.4 0.1 plane_gather.1.half_ref
  72.5 0.1 collective-permute-start.21
  72.5 1.5 %finish.2 = (f32[9,256,256]{2,1,0:T(8,128)}, f32[3,256,256]{2,1,0:T(8,128)}, f32[4,256,256]{2,1,0:T(8,128)}) custom-call(bf16[16,16,16,128]{3,2,1,0:T(8,128)(2,1)S(1)} %plane_gather.1.half_ref), custom_call_target="tpu_custom_call" | custom-call | bytes 5242880 | tf_op jit(solution)/shard_map/finish/pallas_call | solution.py:407
  74.0 1.2 %collective-permute-done.21.half_ref = bf16[16,16,16,128]{3,2,1,0:T(8,128)(2,1)S(1)} collective-permute-done((bf16[16,16,16,128]{3,2,1,0:T(8,128)(2,1)S(1)}, bf16[16,16,16,128]{3,2,1,0:T(8,128)(2,1)S(1)}, u32[]{:S(2)}, u32[]{:S(2)}) %collective-permute-start.21) | collective-permute-done | bytes 1048608 | tf_op jit(solution)/shard_map/ppermute | solution.py:431
  75.2 1.5 %finish.3 = (f32[9,256,256]{2,1,0:T(8,128)}, f32[3,256,256]{2,1,0:T(8,128)}, f32[4,256,256]{2,1,0:T(8,128)}) custom-call(bf16[16,16,16,128]{3,2,1,0:T(8,128)(2,1)S(1)} %collective-permute-done.21.half_ref, f32[9,256,256]{2,1,0:T(8,128)} %get-tuple-element.73.rest_0_, ...), custom_call_target="tpu_custom_call", output_to_operand_aliasing={{0}: (1, {}), {1}: (2, {}), {2}: (3, {})} | custom-call | bytes 9437184 | tf_op jit(solution)/shard_map/finish/pallas_call | solution.py:407
  (24 shorter events, 0.1 us)
Async XLA Ops:
  1.3 1.2 %copy-start = (bf16[16,16,8,256]{3,2,1,0:T(8,128)(2,1)S(1)}, bf16[16,16,8,256]{3,2,1,0:T(8,128)(2,1)}, u32[]{:S(2)}) copy-start(bf16[16,16,8,256]{3,2,1,0:T(8,128)(2,1)} %param.6) | copy-start | bytes 3145732
  2.5 0.9 %copy-start.1 = (bf16[16,8,4,256]{3,2,1,0:T(4,128)(2,1)S(1)}, bf16[16,8,4,256]{3,2,1,0:T(4,128)(2,1)}, u32[]{:S(2)}) copy-start(bf16[16,8,4,256]{3,2,1,0:T(4,128)(2,1)} %cot_ref.3) | copy-start | bytes 786436
  3.5 8.9 %copy-start.2 = (bf16[16,8,4,256]{3,2,1,0:T(4,128)(2,1)S(1)}, bf16[16,8,4,256]{3,2,1,0:T(4,128)(2,1)}, u32[]{:S(2)}) copy-start(bf16[16,8,4,256]{3,2,1,0:T(4,128)(2,1)} %cot_ref.3) | copy-start | bytes 786436
  3.5 8.9 %copy-start.4 = (bf16[2,2,256,256]{3,2,1,0:T(8,128)(2,1)S(1)}, bf16[2,2,256,256]{3,2,1,0:T(8,128)(2,1)}, u32[]{:S(2)}) copy-start(bf16[2,2,256,256]{3,2,1,0:T(8,128)(2,1)} %param.10) | copy-start | bytes 1572868
  3.5 8.9 %copy-start.5 = (bf16[3,256,256]{2,1,0:T(8,128)(2,1)S(1)}, bf16[3,256,256]{2,1,0:T(8,128)(2,1)}, u32[]{:S(2)}) copy-start(bf16[3,256,256]{2,1,0:T(8,128)(2,1)} %wt_ref.5) | copy-start | bytes 1179652
  3.8 6.7 %collective-permute-start = (bf16[128,256]{1,0:T(8,128)(2,1)S(1)}, bf16[128,256]{1,0:T(8,128)(2,1)S(1)}, u32[]{:S(2)}, u32[]{:S(2)}) collective-permute-start(bf16[128,256]{1,0:T(8,128)(2,1)S(1)} %get-tuple-element.42), channel_id=1, source_target_pairs={{0,1},{1,0},{2,3},{3,2},{4,5},{5,4},{6,7},{7,6},{8,9},{9,8},{10,11... | collective-permute-start | bytes 196616 | tf_op jit(solution)/shard_map/ppermute | solution.py:485
  6.8 5.5 %collective-permute-start.1 = (bf16[2,8,4,256]{3,2,1,0:T(4,128)(2,1)S(1)}, bf16[2,8,4,256]{3,2,1,0:T(4,128)(2,1)S(1)}, u32[]{:S(2)}, u32[]{:S(2)}) collective-permute-start(bf16[2,8,4,256]{3,2,1,0:T(4,128)(2,1)S(1)} %get-tuple-element.45), channel_id=1, source_target_pairs={{0,30},{2,0},{4,2},{6,4},{8,6},{10,8},{12,10},{14,12},{16,14},{18,... | collective-permute-start | bytes 98312 | tf_op jit(solution)/shard_map/ppermute | solution.py:480
  12.3 7.3 %collective-permute-start.3 = (bf16[288,256]{1,0:T(8,128)(2,1)S(1)}, bf16[288,256]{1,0:T(8,128)(2,1)S(1)}, u32[]{:S(2)}, u32[]{:S(2)}) collective-permute-start(bf16[288,256]{1,0:T(8,128)(2,1)S(1)} %get-tuple-element.50), channel_id=1, source_target_pairs={{0,2},{2,4},{4,6},{6,8},{8,10},{10,12},{12,14},{14,16},{16,18},{18... | collective-permute-start | bytes 442376 | tf_op jit(solution)/shard_map/ppermute | solution.py:480
  12.3 7.2 %copy-start.3 = (bf16[3,3,256,256]{3,2,1,0:T(8,128)(2,1)S(1)}, bf16[3,3,256,256]{3,2,1,0:T(8,128)(2,1)}, u32[]{:S(2)}) copy-start(bf16[3,3,256,256]{3,2,1,0:T(8,128)(2,1)} %param.8) | copy-start | bytes 3538948
  19.5 3.6 %collective-permute-start.4 = (bf16[16,9,16,128]{3,2,1,0:T(8,128)(2,1)S(1)}, bf16[16,9,16,128]{3,2,1,0:T(8,128)(2,1)S(1)}, u32[]{:S(2)}, u32[]{:S(2)}) collective-permute-start(bf16[16,9,16,128]{3,2,1,0:T(8,128)(2,1)S(1)} %pass.2._), channel_id=1, source_target_pairs={{0,2},{1,3},{2,0},{3,1},{4,6},{5,7},{6,4},{7,5},{8,10},{9,11},{10,... | collective-permute-start | bytes 1769480 | tf_op jit(solution)/shard_map/ppermute | solution.py:431
  23.3 7.2 %collective-permute-start.5 = (bf16[4,9,16,128]{3,2,1,0:T(8,128)(2,1)S(1)}, bf16[4,9,16,128]{3,2,1,0:T(8,128)(2,1)S(1)}, u32[]{:S(2)}, u32[]{:S(2)}) collective-permute-start(bf16[4,9,16,128]{3,2,1,0:T(8,128)(2,1)S(1)} %get-tuple-element.56.rest_1_), channel_id=1, source_target_pairs={{0,5},{1,4},{2,7},{3,6},{4,1},{5,0},{6,3},{7,2},{8,13},{9,12},{10,... | collective-permute-start | bytes 442376 | tf_op jit(solution)/shard_map/ppermute | solution.py:431
  30.5 1.8 %collective-permute-start.8 = (bf16[16,7,16,128]{3,2,1,0:T(8,128)(2,1)S(1)}, bf16[16,7,16,128]{3,2,1,0:T(8,128)(2,1)S(1)}, u32[]{:S(2)}, u32[]{:S(2)}) collective-permute-start(bf16[16,7,16,128]{3,2,1,0:T(8,128)(2,1)S(1)} %pass.3), channel_id=1, source_target_pairs={{0,2},{1,3},{2,0},{3,1},{4,6},{5,7},{6,4},{7,5},{8,10},{9,11},{10,... | collective-permute-start | bytes 1376264 | tf_op jit(solution)/shard_map/ppermute | solution.py:431
  30.5 6.5 %collective-permute-start.6 = (bf16[4,9,16,128]{3,2,1,0:T(8,128)(2,1)S(1)}, bf16[4,9,16,128]{3,2,1,0:T(8,128)(2,1)S(1)}, u32[]{:S(2)}, u32[]{:S(2)}) collective-permute-start(bf16[4,9,16,128]{3,2,1,0:T(8,128)(2,1)S(1)} %get-tuple-element.57.rest_2_), channel_id=1, source_target_pairs={{0,1},{1,0},{2,3},{3,2},{4,5},{5,4},{6,7},{7,6},{8,9},{9,8},{10,11... | collective-permute-start | bytes 442376 | tf_op jit(solution)/shard_map/ppermute | solution.py:431
  31.1 6.7 %collective-permute-start.7 = (bf16[4,9,16,128]{3,2,1,0:T(8,128)(2,1)S(1)}, bf16[4,9,16,128]{3,2,1,0:T(8,128)(2,1)S(1)}, u32[]{:S(2)}, u32[]{:S(2)}) collective-permute-start(bf16[4,9,16,128]{3,2,1,0:T(8,128)(2,1)S(1)} %get-tuple-element.58.rest_3_), channel_id=1, source_target_pairs={{0,4},{1,5},{2,6},{3,7},{4,0},{5,1},{6,2},{7,3},{8,12},{9,13},{10,... | collective-permute-start | bytes 442376 | tf_op jit(solution)/shard_map/ppermute | solution.py:431
  32.5 8.7 %collective-permute-start.9 = (bf16[4,7,16,128]{3,2,1,0:T(8,128)(2,1)S(1)}, bf16[4,7,16,128]{3,2,1,0:T(8,128)(2,1)S(1)}, u32[]{:S(2)}, u32[]{:S(2)}) collective-permute-start(bf16[4,7,16,128]{3,2,1,0:T(8,128)(2,1)S(1)} %get-tuple-element.63), channel_id=1, source_target_pairs={{0,5},{1,4},{2,7},{3,6},{4,1},{5,0},{6,3},{7,2},{8,13},{9,12},{10,... | collective-permute-start | bytes 344072 | tf_op jit(solution)/shard_map/ppermute | solution.py:431
  34.2 7.5 %collective-permute-start.10 = (bf16[4,7,16,128]{3,2,1,0:T(8,128)(2,1)S(1)}, bf16[4,7,16,128]{3,2,1,0:T(8,128)(2,1)S(1)}, u32[]{:S(2)}, u32[]{:S(2)}) collective-permute-start(bf16[4,7,16,128]{3,2,1,0:T(8,128)(2,1)S(1)} %get-tuple-element.64), channel_id=1, source_target_pairs={{0,1},{1,0},{2,3},{3,2},{4,5},{5,4},{6,7},{7,6},{8,9},{9,8},{10,11... | collective-permute-start | bytes 344072 | tf_op jit(solution)/shard_map/ppermute | solution.py:431
  34.8 7.3 %collective-permute-start.11 = (bf16[4,7,16,128]{3,2,1,0:T(8,128)(2,1)S(1)}, bf16[4,7,16,128]{3,2,1,0:T(8,128)(2,1)S(1)}, u32[]{:S(2)}, u32[]{:S(2)}) collective-permute-start(bf16[4,7,16,128]{3,2,1,0:T(8,128)(2,1)S(1)} %get-tuple-element.65), channel_id=1, source_target_pairs={{0,4},{1,5},{2,6},{3,7},{4,0},{5,1},{6,2},{7,3},{8,12},{9,13},{10,... | collective-permute-start | bytes 344072 | tf_op jit(solution)/shard_map/ppermute | solution.py:431
  42.2 8.4 %collective-permute-start.12 = (bf16[16,16,128]{2,1,0:T(8,128)(2,1)S(1)}, bf16[16,16,128]{2,1,0:T(8,128)(2,1)S(1)}, u32[]{:S(2)}, u32[]{:S(2)}) collective-permute-start(bf16[16,16,128]{2,1,0:T(8,128)(2,1)S(1)} %get-tuple-element.67), channel_id=1, source_target_pairs={{0,24},{1,25},{2,26},{3,27},{4,28},{5,29},{6,30},{7,31},{8,16},{9,... | collective-permute-start | bytes 196616 | tf_op jit(solution)/shard_map/ppermute | solution.py:431
  44.3 6.2 %collective-permute-start.13 = (bf16[16,16,128]{2,1,0:T(8,128)(2,1)S(1)}, bf16[16,16,128]{2,1,0:T(8,128)(2,1)S(1)}, u32[]{:S(2)}, u32[]{:S(2)}) collective-permute-start(bf16[16,16,128]{2,1,0:T(8,128)(2,1)S(1)} %get-tuple-element.68), channel_id=1, source_target_pairs={{0,16},{1,17},{2,18},{3,19},{4,20},{5,21},{6,22},{7,23},{8,24},{9,... | collective-permute-start | bytes 196616 | tf_op jit(solution)/shard_map/ppermute | solution.py:431
  44.3 6.2 %collective-permute-start.14 = (bf16[16,16,128]{2,1,0:T(8,128)(2,1)S(1)}, bf16[16,16,128]{2,1,0:T(8,128)(2,1)S(1)}, u32[]{:S(2)}, u32[]{:S(2)}) collective-permute-start(bf16[16,16,128]{2,1,0:T(8,128)(2,1)S(1)} %get-tuple-element.69), channel_id=1, source_target_pairs={{0,8},{1,9},{2,10},{3,11},{4,12},{5,13},{6,14},{7,15},{8,0},{9,1},... | collective-permute-start | bytes 196616 | tf_op jit(solution)/shard_map/ppermute | solution.py:431
  46.6 3.9 %collective-permute-start.2 = (bf16[64,256]{1,0:T(8,128)(2,1)S(1)}, bf16[64,256]{1,0:T(8,128)(2,1)S(1)}, u32[]{:S(2)}, u32[]{:S(2)}) collective-permute-start(bf16[64,256]{1,0:T(8,128)(2,1)S(1)} %get-tuple-element.48), channel_id=1, source_target_pairs={{0,1},{1,0},{2,3},{3,2},{4,5},{5,4},{6,7},{7,6},{8,9},{9,8},{10,11... | collective-permute-start | bytes 98312 | tf_op jit(solution)/shard_map/ppermute | solution.py:485
  50.6 4.6 %collective-permute-start.17 = (bf16[16,16,128]{2,1,0:T(8,128)(2,1)S(1)}, bf16[16,16,128]{2,1,0:T(8,128)(2,1)S(1)}, u32[]{:S(2)}, u32[]{:S(2)}) collective-permute-start(bf16[16,16,128]{2,1,0:T(8,128)(2,1)S(1)} %line_sum.1.a_ref), channel_id=1, source_target_pairs={{0,8},{1,9},{2,10},{3,11},{4,12},{5,13},{6,14},{7,15},{8,0},{9,1},... | collective-permute-start | bytes 196616 | tf_op jit(solution)/shard_map/ppermute | solution.py:431
  51.0 5.7 %collective-permute-start.16 = (bf16[16,16,128]{2,1,0:T(8,128)(2,1)S(1)}, bf16[16,16,128]{2,1,0:T(8,128)(2,1)S(1)}, u32[]{:S(2)}, u32[]{:S(2)}) collective-permute-start(bf16[16,16,128]{2,1,0:T(8,128)(2,1)S(1)} %line_sum.1.a_ref), channel_id=1, source_target_pairs={{0,16},{1,17},{2,18},{3,19},{4,20},{5,21},{6,22},{7,23},{8,24},{9,... | collective-permute-start | bytes 196616 | tf_op jit(solution)/shard_map/ppermute | solution.py:431
  53.4 6.1 %collective-permute-start.15 = (bf16[16,16,128]{2,1,0:T(8,128)(2,1)S(1)}, bf16[16,16,128]{2,1,0:T(8,128)(2,1)S(1)}, u32[]{:S(2)}, u32[]{:S(2)}) collective-permute-start(bf16[16,16,128]{2,1,0:T(8,128)(2,1)S(1)} %line_sum.1.a_ref), channel_id=1, source_target_pairs={{0,24},{1,25},{2,26},{3,27},{4,28},{5,29},{6,30},{7,31},{8,16},{9,... | collective-permute-start | bytes 196616 | tf_op jit(solution)/shard_map/ppermute | solution.py:431
  59.5 11.0 %collective-permute-start.20 = (bf16[4,16,16,128]{3,2,1,0:T(8,128)(2,1)S(1)}, bf16[4,16,16,128]{3,2,1,0:T(8,128)(2,1)S(1)}, u32[]{:S(2)}, u32[]{:S(2)}) collective-permute-start(bf16[4,16,16,128]{3,2,1,0:T(8,128)(2,1)S(1)} %line_gather.1.rest_0_.a_ref), channel_id=1, source_target_pairs={{0,4},{1,5},{2,6},{3,7},{4,0},{5,1},{6,2},{7,3},{8,12},{9,13},{10,... | collective-permute-start | bytes 786440 | tf_op jit(solution)/shard_map/ppermute | solution.py:431
  60.4 12.0 %collective-permute-start.19 = (bf16[4,16,16,128]{3,2,1,0:T(8,128)(2,1)S(1)}, bf16[4,16,16,128]{3,2,1,0:T(8,128)(2,1)S(1)}, u32[]{:S(2)}, u32[]{:S(2)}) collective-permute-start(bf16[4,16,16,128]{3,2,1,0:T(8,128)(2,1)S(1)} %line_gather.1.rest_0_.a_ref), channel_id=1, source_target_pairs={{0,1},{1,0},{2,3},{3,2},{4,5},{5,4},{6,7},{7,6},{8,9},{9,8},{10,11... | collective-permute-start | bytes 786440 | tf_op jit(solution)/shard_map/ppermute | solution.py:431
  61.7 10.7 %collective-permute-start.18 = (bf16[4,16,16,128]{3,2,1,0:T(8,128)(2,1)S(1)}, bf16[4,16,16,128]{3,2,1,0:T(8,128)(2,1)S(1)}, u32[]{:S(2)}, u32[]{:S(2)}) collective-permute-start(bf16[4,16,16,128]{3,2,1,0:T(8,128)(2,1)S(1)} %line_gather.1.rest_0_.a_ref), channel_id=1, source_target_pairs={{0,5},{1,4},{2,7},{3,6},{4,1},{5,0},{6,3},{7,2},{8,13},{9,12},{10,... | collective-permute-start | bytes 786440 | tf_op jit(solution)/shard_map/ppermute | solution.py:431
  72.5 2.7 %collective-permute-start.21 = (bf16[16,16,16,128]{3,2,1,0:T(8,128)(2,1)S(1)}, bf16[16,16,16,128]{3,2,1,0:T(8,128)(2,1)S(1)}, u32[]{:S(2)}, u32[]{:S(2)}) collective-permute-start(bf16[16,16,16,128]{3,2,1,0:T(8,128)(2,1)S(1)} %plane_gather.1.half_ref), channel_id=1, source_target_pairs={{0,2},{1,3},{2,0},{3,1},{4,6},{5,7},{6,4},{7,5},{8,10},{9,11},{10,... | collective-permute-start | bytes 3145736 | tf_op jit(solution)/shard_map/ppermute | solution.py:431

commit v13 on v12

--- a/solution.py
+++ b/solution.py
@@ -141,7 +141,8 @@
     last_ref[2 * rows * cols :] = mm(pick, jnp.concatenate(halo, 0)).astype(BF)
 
 
-def spatial_kernel(count_ref, acts_in, prev_ref, ws_ref, _, acts_ref, sp_ref):
+def spatial_kernel(count_ref, acts_in, prev_ref, ws_ref, *rest):
+    acts_ref, sp_ref = rest[-2:]
     rows, cols = sp_ref.shape[0], sp_ref.shape[1]
     a, b = iotas(256, 32)
     place = ((a >> 4) == (b & 15)) & ((a & 15) == OWN + (b >> 4)) & (lax.axis_index("tm") > 0)
@@ -531,29 +532,28 @@
     send_a = passed(send_a, [prev])
     got_a = core_round(send_a, tm, grp)
     cot_top, cot_bot = from_bands(edge)
+    _, plane, line, others = plan(tm, grp)
+    parts_a = plane_send(keep_a, got_a, [])
     acts, sp = call(
         spatial_kernel,
         "spatial",
-        [count, (VMEM, acts), (VMEM, prev), (VMEM, ws), (ANY, send_a)],
+        [count, (VMEM, acts), (VMEM, prev), (VMEM, ws)] + [(ANY, a) for a in parts_a[1:]],
         [(VMEM, padded), (VMEM, tile)],
         flops=9 * tap,
         alias={1: 0},
     )
-    _, plane, line, others = plan(tm, grp)
-    parts_a = plane_send(keep_a, got_a, [sp])
+    parts_a = four_round(parts_a, plane, tm, grp)
     half = (16, 7, 16, ch // 2)
     down, keep_b, send_b = call(
         forward_kernel,
         "forward",
         [count, (VMEM, xt), (VMEM, sp), (VMEM, cott), (VMEM, gy), (VMEM, wt), (VMEM, wd),
-         *((ANY, a) for a in parts_a)],
+         *((ANY, a) for a in parts_a[1:])],
         [(VMEM, (slots * wide // 4, ch)), (VMEM, half), (VMEM, half)],
         [pltpu.VMEM(v, BF) for v in (tile, (3 * ch, slots * wide), (4 * ch, slots * wide // 4))],
         flops=10 * tap,
         grant=14,
     )
-    parts_a = four_round(parts_a, plane, tm, grp)
-    send_b = passed(send_b, parts_a[1:2])
     parts_b = plane_send(keep_b, core_round(send_b, tm, grp), [])
     parts_b = four_round(parts_b, plane, tm, grp)
     parts = call(

time: 76.8 us -> 79.5 us (1.035)
  waiting for transfers between devices: 23.4 us -> 24.8 us
  starting transfers between devices: 25.7 us -> 27 us
    ppermute x18, starting transfers between devices: 17.5 us -> 19.7 us  [swap(): return lax.ppermute(value, AXES, [(d, d ^ flip) for d in range(tm * grp)])]
    ppermute x2, starting transfers between devices: 4.49 us -> 3.61 us  [from_bands(): got = lax.ppermute(parts[0], 'grp', [(0, 1), (1, 0)])]
    ppermute x2, waiting for transfers between devices: 2.46 us -> 3.34 us  [from_bands(): got = lax.ppermute(parts[0], 'grp', [(0, 1), (1, 0)])]
    pallas_call x16 -> x15, Pallas kernels: 23.9 us -> 23.8 us  [call(): pl.pallas_call(kernel, out_shape=shapes, in_specs=[s for s, _ in ins], ou...]
  transfers between devices with their start and end apart: 22 -> 22, of which waited for: 14 -> 14; matrix products, arithmetic and copies ran while one was open for 0% -> 0% of each run, Pallas kernels for 28% -> 24%
where the time goes in v13:
time: 79.5 us; the launch traced here: 79.3 us
  starting transfers between devices  27 us (34%)
  waiting for transfers between devices  24.8 us (31%)
  Pallas kernels  23.8 us (30%)
  local copies, waits for them, and re-layouts  2.18 us (3%)
  between operations  1.45 us (2%)
    pallas_call x15, Pallas kernels, call(): pl.pallas_call(kernel, out_shape=shapes, in_specs=[s for s, _ in ins], ou...  23.8 us
    ppermute x18, starting transfers between devices, swap(): return lax.ppermute(value, AXES, [(d, d ^ flip) for d in range(tm * grp)])  19.7 us
    ppermute x18, waiting for transfers between devices, swap(): return lax.ppermute(value, AXES, [(d, d ^ flip) for d in range(tm * grp)])  18.8 us
    ppermute x2, starting transfers between devices, around(): lax.ppermute(value, axis, [(i, (i + by) % count) for i in range(count)])  3.7 us
    ppermute x2, starting transfers between devices, from_bands(): got = lax.ppermute(parts[0], 'grp', [(0, 1), (1, 0)])  3.61 us
    ppermute x2, waiting for transfers between devices, from_bands(): got = lax.ppermute(parts[0], 'grp', [(0, 1), (1, 0)])  3.34 us
    ppermute x2, waiting for transfers between devices, around(): lax.ppermute(value, axis, [(i, (i + by) % count) for i in range(count)])  2.67 us
    unnamed x12, local copies, waits for them, and re-layouts  2.18 us
  transfers between devices with their start and end apart: 22, of which 14 were waited for; matrix products, arithmetic and copies ran while one was open for 0% of the time, Pallas kernels for 24%

profile of v13, /device:TPU:0, one launch (start us, length us, event | category | flops | bytes accessed | tf_op | source)
XLA Modules:
  0.0 79.3 jit_solution(2257463879022727732)
XLA Ops:
  1.3 1.2 %copy-done = bf16[16,16,8,256]{3,2,1,0:T(8,128)(2,1)S(1)} copy-done((bf16[16,16,8,256]{3,2,1,0:T(8,128)(2,1)S(1)}, bf16[16,16,8,256]{3,2,1,0:T(8,128)(2,1)}, u32[]{:S(2)}) %copy-start) | copy-done | bytes 1048600
  2.5 0.9 %copy-done.1 = bf16[16,8,4,256]{3,2,1,0:T(4,128)(2,1)S(1)} copy-done((bf16[16,8,4,256]{3,2,1,0:T(4,128)(2,1)S(1)}, bf16[16,8,4,256]{3,2,1,0:T(4,128)(2,1)}, u32[]{:S(2)}) %copy-start.1) | copy-done | bytes 262168
  3.5 0.3 edges.1
  3.8 3.0 %collective-permute-start = (bf16[128,256]{1,0:T(8,128)(2,1)S(1)}, bf16[128,256]{1,0:T(8,128)(2,1)S(1)}, u32[]{:S(2)}, u32[]{:S(2)}) collective-permute-start(bf16[128,256]{1,0:T(8,128)(2,1)S(1)} %get-tuple-element.42), channel_id=1, source_target_pairs={{0,1},{1,0},{2,3},{3,2},{4,5},{5,4},{6,7},{7,6},{8,9},{9,8},{10,11... | collective-permute-start | bytes 196616 | tf_op jit(solution)/shard_map/ppermute | solution.py:486
  6.8 3.7 %collective-permute-start.1 = (bf16[2,8,4,256]{3,2,1,0:T(4,128)(2,1)S(1)}, bf16[2,8,4,256]{3,2,1,0:T(4,128)(2,1)S(1)}, u32[]{:S(2)}, u32[]{:S(2)}) collective-permute-start(bf16[2,8,4,256]{3,2,1,0:T(4,128)(2,1)S(1)} %get-tuple-element.45), channel_id=1, source_target_pairs={{0,30},{2,0},{4,2},{6,4},{8,6},{10,8},{12,10},{14,12},{16,14},{18,... | collective-permute-start | bytes 98312 | tf_op jit(solution)/shard_map/ppermute | solution.py:481
  10.5 1.8 %acts.1 = (bf16[16,8,16,256]{3,2,1,0:T(8,128)(2,1)S(1)}, bf16[18,10,16,256]{3,2,1,0:T(8,128)(2,1)S(1)}, bf16[768,2560]{1,0:T(8,128)(2,1)S(1)}, bf16[288,256]{1,0:T(8,128)(2,1)S(1)}) custom-call(s32[1]{0:T(128)S(6)} %copy.21.count_ref, bf16[16,128,256]{2,1,0:T(8,128)(2,1)S(1)} %bitcast.7, bf16[128,256]{1,0:T(8,128)(2,1)S(1)} %collective-permute-done.top_ref.bot_ref, ...), custom_call_target="tpu_custom_call" | custom-call | flops 536870912 | bytes 7782404 | tf_op jit(solution)/shard_map/acts/pallas_call | solution.py:408
  12.3 0.0 collective-permute-start.3
  12.3 4.5 %grad_spatial.1 = (bf16[8,4,16,256]{3,2,1,0:T(8,128)(2,1)S(1)}, bf16[16,8,16,256]{3,2,1,0:T(8,128)(2,1)S(1)}, bf16[16,10,16,256]{3,2,1,0:T(8,128)(2,1)S(1)}, bf1...) custom-call(s32[1]{0:T(128)S(6)} %copy.21.count_ref, ...), custom_call_target="tpu_custom_call" | custom-call | flops 3758096384 | bytes 8978436 | tf_op jit(solution)/shard_map/grad_spatial/pallas_call | solution.py:408
  16.9 2.7 %collective-permute-done.3.__1_.prev_ref = bf16[288,256]{1,0:T(8,128)(2,1)S(1)} collective-permute-done((bf16[288,256]{1,0:T(8,128)(2,1)S(1)}, bf16[288,256]{1,0:T(8,128)(2,1)S(1)}, u32[]{:S(2)}, u32[]{:S(2)}) %collective-permute-start.3) | collective-permute-done | bytes 147488 | tf_op jit(solution)/shard_map/ppermute | solution.py:481
  19.6 2.0 %collective-permute-done.4.got_ref = bf16[16,9,16,128]{3,2,1,0:T(8,128)(2,1)S(1)} collective-permute-done((bf16[16,9,16,128]{3,2,1,0:T(8,128)(2,1)S(1)}, bf16[16,9,16,128]{3,2,1,0:T(8,128)(2,1)S(1)}, u32[]{:S(2)}, u32[]{:S(2)}) %collective-permute-start.4) | collective-permute-done | bytes 589856 | tf_op jit(solution)/shard_map/ppermute | solution.py:432
  21.6 0.1 plane_send.2
  21.7 0.2 collective-permute-start.5
  21.9 0.5 collective-permute-start.6
  22.5 2.8 %collective-permute-start.7 = (bf16[4,9,16,128]{3,2,1,0:T(8,128)(2,1)S(1)}, bf16[4,9,16,128]{3,2,1,0:T(8,128)(2,1)S(1)}, u32[]{:S(2)}, u32[]{:S(2)}) collective-permute-start(bf16[4,9,16,128]{3,2,1,0:T(8,128)(2,1)S(1)} %get-tuple-element.55.rest_2_), channel_id=1, source_target_pairs={{0,4},{1,5},{2,6},{3,7},{4,0},{5,1},{6,2},{7,3},{8,12},{9,13},{10,... | collective-permute-start | bytes 442376 | tf_op jit(solution)/shard_map/ppermute | solution.py:432
  25.3 3.6 %spatial.1 = (bf16[18,10,16,256]{3,2,1,0:T(8,128)(2,1)S(1)}, bf16[16,8,16,256]{3,2,1,0:T(8,128)(2,1)S(1)}) custom-call(s32[1]{0:T(128)S(6)} %copy.21.count_ref, bf16[18,10,16,256]{3,2,1,0:T(8,128)(2,1)S(1)} %get-tuple-element.49.acts_in, bf16[288,256]{1,0:T(8,128)(2,1)S(1)} %collective-permute-done.3.__1_.prev_ref, ...), custom_call_target="tpu_custom_call", output_to_operand_aliasing={{0}: (1, {})} | custom-call | flops 2415919104 | bytes 5324804 | tf_op jit(solution)/shard_map/spatial/pallas_call | solution.py:408
  28.8 0.6 collective-permute-done.5.rest_0_.refs_1_
  29.4 1.5 %collective-permute-done.6.rest_1_.refs_2_ = bf16[4,9,16,128]{3,2,1,0:T(8,128)(2,1)S(1)} collective-permute-done((bf16[4,9,16,128]{3,2,1,0:T(8,128)(2,1)S(1)}, bf16[4,9,16,128]{3,2,1,0:T(8,128)(2,1)S(1)}, u32[]{:S(2)}, u32[]{:S(2)}) %collective-permute-start.6) | collective-permute-done | bytes 147488 | tf_op jit(solution)/shard_map/ppermute | solution.py:432
  30.9 2.8 %forward.1 = (bf16[512,256]{1,0:T(8,128)(2,1)S(1)}, bf16[16,7,16,128]{3,2,1,0:T(8,128)(2,1)S(1)}, bf16[16,7,16,128]{3,2,1,0:T(8,128)(2,1)S(1)}) custom-call(s32[1]{0:T(128)S(6)} %copy.21.count_ref, bf16[16,8,16,256]{3,2,1,0:T(8,128)(2,1)S(1)} %get-tuple-element.43.xt_ref, bf16[16,8,16,256]{3,2,1,0:T(8,128)(2,1)S(1)} %get-tuple-element.56.sp_ref, ...), custom_call_target="tpu_custom_call" | custom-call | flops 2684354560 | bytes 5505028 | tf_op jit(solution)/shard_map/forward/pallas_call | solution.py:408
  33.8 0.1 collective-permute-start.8
  33.8 1.8 %collective-permute-done.8.got_ref = bf16[16,7,16,128]{3,2,1,0:T(8,128)(2,1)S(1)} collective-permute-done((bf16[16,7,16,128]{3,2,1,0:T(8,128)(2,1)S(1)}, bf16[16,7,16,128]{3,2,1,0:T(8,128)(2,1)S(1)}, u32[]{:S(2)}, u32[]{:S(2)}) %collective-permute-start.8) | collective-permute-done | bytes 458784 | tf_op jit(solution)/shard_map/ppermute | solution.py:432
  35.6 0.1 plane_send.3
  35.7 1.2 %collective-permute-start.9 = (bf16[4,7,16,128]{3,2,1,0:T(8,128)(2,1)S(1)}, bf16[4,7,16,128]{3,2,1,0:T(8,128)(2,1)S(1)}, u32[]{:S(2)}, u32[]{:S(2)}) collective-permute-start(bf16[4,7,16,128]{3,2,1,0:T(8,128)(2,1)S(1)} %get-tuple-element.63), channel_id=1, source_target_pairs={{0,5},{1,4},{2,7},{3,6},{4,1},{5,0},{6,3},{7,2},{8,13},{9,12},{10,... | collective-permute-start | bytes 344072 | tf_op jit(solution)/shard_map/ppermute | solution.py:432
  37.0 0.6 collective-permute-start.10
  37.6 1.8 %collective-permute-start.11 = (bf16[4,7,16,128]{3,2,1,0:T(8,128)(2,1)S(1)}, bf16[4,7,16,128]{3,2,1,0:T(8,128)(2,1)S(1)}, u32[]{:S(2)}, u32[]{:S(2)}) collective-permute-start(bf16[4,7,16,128]{3,2,1,0:T(8,128)(2,1)S(1)} %get-tuple-element.65), channel_id=1, source_target_pairs={{0,4},{1,5},{2,6},{3,7},{4,0},{5,1},{6,2},{7,3},{8,12},{9,13},{10,... | collective-permute-start | bytes 344072 | tf_op jit(solution)/shard_map/ppermute | solution.py:432
  39.3 3.4 %collective-permute-done.9.refs_5_ = bf16[4,7,16,128]{3,2,1,0:T(8,128)(2,1)S(1)} collective-permute-done((bf16[4,7,16,128]{3,2,1,0:T(8,128)(2,1)S(1)}, bf16[4,7,16,128]{3,2,1,0:T(8,128)(2,1)S(1)}, u32[]{:S(2)}, u32[]{:S(2)}) %collective-permute-start.9) | collective-permute-done | bytes 114720 | tf_op jit(solution)/shard_map/ppermute | solution.py:432
  42.7 1.6 %collective-permute-done.10.refs_6_ = bf16[4,7,16,128]{3,2,1,0:T(8,128)(2,1)S(1)} collective-permute-done((bf16[4,7,16,128]{3,2,1,0:T(8,128)(2,1)S(1)}, bf16[4,7,16,128]{3,2,1,0:T(8,128)(2,1)S(1)}, u32[]{:S(2)}, u32[]{:S(2)}) %collective-permute-start.10) | collective-permute-done | bytes 114720 | tf_op jit(solution)/shard_map/ppermute | solution.py:432
  44.4 0.1 line_send.1
  44.5 2.3 %collective-permute-start.12 = (bf16[16,16,128]{2,1,0:T(8,128)(2,1)S(1)}, bf16[16,16,128]{2,1,0:T(8,128)(2,1)S(1)}, u32[]{:S(2)}, u32[]{:S(2)}) collective-permute-start(bf16[16,16,128]{2,1,0:T(8,128)(2,1)S(1)} %get-tuple-element.67), channel_id=1, source_target_pairs={{0,24},{1,25},{2,26},{3,27},{4,28},{5,29},{6,30},{7,31},{8,16},{9,... | collective-permute-start | bytes 196616 | tf_op jit(solution)/shard_map/ppermute | solution.py:432
  46.8 2.1 %collective-permute-start.14 = (bf16[16,16,128]{2,1,0:T(8,128)(2,1)S(1)}, bf16[16,16,128]{2,1,0:T(8,128)(2,1)S(1)}, u32[]{:S(2)}, u32[]{:S(2)}) collective-permute-start(bf16[16,16,128]{2,1,0:T(8,128)(2,1)S(1)} %get-tuple-element.69), channel_id=1, source_target_pairs={{0,8},{1,9},{2,10},{3,11},{4,12},{5,13},{6,14},{7,15},{8,0},{9,1},... | collective-permute-start | bytes 196616 | tf_op jit(solution)/shard_map/ppermute | solution.py:432
  49.0 0.6 collective-permute-start.2
  49.5 3.3 %collective-permute-done.2.rest_0_.top_ref.bot_ref = bf16[64,256]{1,0:T(8,128)(2,1)S(1)} collective-permute-done((bf16[64,256]{1,0:T(8,128)(2,1)S(1)}, bf16[64,256]{1,0:T(8,128)(2,1)S(1)}, u32[]{:S(2)}, u32[]{:S(2)}) %collective-permute-start.2) | collective-permute-done | bytes 32800 | tf_op jit(solution)/shard_map/ppermute | solution.py:486
  52.9 0.3 collective-permute-done.13.c_ref
  53.2 0.4 collective-permute-start.17
  53.7 2.4 %collective-permute-start.16 = (bf16[16,16,128]{2,1,0:T(8,128)(2,1)S(1)}, bf16[16,16,128]{2,1,0:T(8,128)(2,1)S(1)}, u32[]{:S(2)}, u32[]{:S(2)}) collective-permute-start(bf16[16,16,128]{2,1,0:T(8,128)(2,1)S(1)} %line_sum.1.a_ref), channel_id=1, source_target_pairs={{0,16},{1,17},{2,18},{3,19},{4,20},{5,21},{6,22},{7,23},{8,24},{9,... | collective-permute-start | bytes 196616 | tf_op jit(solution)/shard_map/ppermute | solution.py:432
  56.0 1.7 %collective-permute-start.15 = (bf16[16,16,128]{2,1,0:T(8,128)(2,1)S(1)}, bf16[16,16,128]{2,1,0:T(8,128)(2,1)S(1)}, u32[]{:S(2)}, u32[]{:S(2)}) collective-permute-start(bf16[16,16,128]{2,1,0:T(8,128)(2,1)S(1)} %line_sum.1.a_ref), channel_id=1, source_target_pairs={{0,24},{1,25},{2,26},{3,27},{4,28},{5,29},{6,30},{7,31},{8,16},{9,... | collective-permute-start | bytes 196616 | tf_op jit(solution)/shard_map/ppermute | solution.py:432
  57.7 0.6 collective-permute-done.17.d_ref
  58.3 3.1 %collective-permute-done.16.c_ref = bf16[16,16,128]{2,1,0:T(8,128)(2,1)S(1)} collective-permute-done((bf16[16,16,128]{2,1,0:T(8,128)(2,1)S(1)}, bf16[16,16,128]{2,1,0:T(8,128)(2,1)S(1)}, u32[]{:S(2)}, u32[]{:S(2)}) %collective-permute-start.16) | collective-permute-done | bytes 65568 | tf_op jit(solution)/shard_map/ppermute | solution.py:432
  61.4 0.8 %collective-permute-done.15.b_ref = bf16[16,16,128]{2,1,0:T(8,128)(2,1)S(1)} collective-permute-done((bf16[16,16,128]{2,1,0:T(8,128)(2,1)S(1)}, bf16[16,16,128]{2,1,0:T(8,128)(2,1)S(1)}, u32[]{:S(2)}, u32[]{:S(2)}) %collective-permute-start.15) | collective-permute-done | bytes 65568 | tf_op jit(solution)/shard_map/ppermute | solution.py:432
  62.2 1.4 %collective-permute-start.20 = (bf16[4,16,16,128]{3,2,1,0:T(8,128)(2,1)S(1)}, bf16[4,16,16,128]{3,2,1,0:T(8,128)(2,1)S(1)}, u32[]{:S(2)}, u32[]{:S(2)}) collective-permute-start(bf16[4,16,16,128]{3,2,1,0:T(8,128)(2,1)S(1)} %line_gather.1.rest_0_.a_ref), channel_id=1, source_target_pairs={{0,4},{1,5},{2,6},{3,7},{4,0},{5,1},{6,2},{7,3},{8,12},{9,13},{10,... | collective-permute-start | bytes 786440 | tf_op jit(solution)/shard_map/ppermute | solution.py:432
  63.6 0.8 %collective-permute-start.19 = (bf16[4,16,16,128]{3,2,1,0:T(8,128)(2,1)S(1)}, bf16[4,16,16,128]{3,2,1,0:T(8,128)(2,1)S(1)}, u32[]{:S(2)}, u32[]{:S(2)}) collective-permute-start(bf16[4,16,16,128]{3,2,1,0:T(8,128)(2,1)S(1)} %line_gather.1.rest_0_.a_ref), channel_id=1, source_target_pairs={{0,1},{1,0},{2,3},{3,2},{4,5},{5,4},{6,7},{7,6},{8,9},{9,8},{10,11... | collective-permute-start | bytes 786440 | tf_op jit(solution)/shard_map/ppermute | solution.py:432
  64.5 1.3 %collective-permute-start.18 = (bf16[4,16,16,128]{3,2,1,0:T(8,128)(2,1)S(1)}, bf16[4,16,16,128]{3,2,1,0:T(8,128)(2,1)S(1)}, u32[]{:S(2)}, u32[]{:S(2)}) collective-permute-start(bf16[4,16,16,128]{3,2,1,0:T(8,128)(2,1)S(1)} %line_gather.1.rest_0_.a_ref), channel_id=1, source_target_pairs={{0,5},{1,4},{2,7},{3,6},{4,1},{5,0},{6,3},{7,2},{8,13},{9,12},{10,... | collective-permute-start | bytes 786440 | tf_op jit(solution)/shard_map/ppermute | solution.py:432
  65.8 7.4 %grad_x.1 = (bf16[16,128,256]{2,1,0:T(8,128)(2,1)}, bf16[16,8,4,256]{3,2,1,0:T(4,128)(2,1)}, f32[8,128]{1,0:T(8,128)S(1)}) custom-call(s32[1]{0:T(128)S(6)} %copy.21.count_ref, bf16[16,8,16,256]{3,2,1,0:T(8,128)(2,1)S(1)} %get-tuple-element.43.xt_ref, bf16[16,8,16,256]{3,2,1,0:T(8,128)(2,1)S(1)} %get-tuple-element.46.gy_ref, ...), custom_call_target="tpu_custom_call" | custom-call | flops 2684354560 | bytes 7147524 | tf_op jit(solution)/shard_map/grad_x/pallas_call | solution.py:408
  73.2 1.8 %collective-permute-done.19.c_ref = bf16[4,16,16,128]{3,2,1,0:T(8,128)(2,1)S(1)} collective-permute-done((bf16[4,16,16,128]{3,2,1,0:T(8,128)(2,1)S(1)}, bf16[4,16,16,128]{3,2,1,0:T(8,128)(2,1)S(1)}, u32[]{:S(2)}, u32[]{:S(2)}) %collective-permute-start.19) | collective-permute-done | bytes 262176 | tf_op jit(solution)/shard_map/ppermute | solution.py:432
  75.1 0.1 plane_gather.1.half_ref
  75.2 0.1 collective-permute-start.21
  75.2 1.5 %finish.2 = (f32[9,256,256]{2,1,0:T(8,128)}, f32[3,256,256]{2,1,0:T(8,128)}, f32[4,256,256]{2,1,0:T(8,128)}) custom-call(bf16[16,16,16,128]{3,2,1,0:T(8,128)(2,1)S(1)} %plane_gather.1.half_ref), custom_call_target="tpu_custom_call" | custom-call | bytes 5242880 | tf_op jit(solution)/shard_map/finish/pallas_call | solution.py:408
  76.7 1.2 %collective-permute-done.21.half_ref = bf16[16,16,16,128]{3,2,1,0:T(8,128)(2,1)S(1)} collective-permute-done((bf16[16,16,16,128]{3,2,1,0:T(8,128)(2,1)S(1)}, bf16[16,16,16,128]{3,2,1,0:T(8,128)(2,1)S(1)}, u32[]{:S(2)}, u32[]{:S(2)}) %collective-permute-start.21) | collective-permute-done | bytes 1048608 | tf_op jit(solution)/shard_map/ppermute | solution.py:432
  77.9 1.5 %finish.3 = (f32[9,256,256]{2,1,0:T(8,128)}, f32[3,256,256]{2,1,0:T(8,128)}, f32[4,256,256]{2,1,0:T(8,128)}) custom-call(bf16[16,16,16,128]{3,2,1,0:T(8,128)(2,1)S(1)} %collective-permute-done.21.half_ref, f32[9,256,256]{2,1,0:T(8,128)} %get-tuple-element.73.rest_0_, ...), custom_call_target="tpu_custom_call", output_to_operand_aliasing={{0}: (1, {}), {1}: (2, {}), {2}: (3, {})} | custom-call | bytes 9437184 | tf_op jit(solution)/shard_map/finish/pallas_call | solution.py:408
  (23 shorter events, 0.1 us)
Async XLA Ops:
  1.3 1.2 %copy-start = (bf16[16,16,8,256]{3,2,1,0:T(8,128)(2,1)S(1)}, bf16[16,16,8,256]{3,2,1,0:T(8,128)(2,1)}, u32[]{:S(2)}) copy-start(bf16[16,16,8,256]{3,2,1,0:T(8,128)(2,1)} %param.6) | copy-start | bytes 3145732
  2.5 0.9 %copy-start.1 = (bf16[16,8,4,256]{3,2,1,0:T(4,128)(2,1)S(1)}, bf16[16,8,4,256]{3,2,1,0:T(4,128)(2,1)}, u32[]{:S(2)}) copy-start(bf16[16,8,4,256]{3,2,1,0:T(4,128)(2,1)} %cot_ref.3) | copy-start | bytes 786436
  3.5 8.9 %copy-start.2 = (bf16[16,8,4,256]{3,2,1,0:T(4,128)(2,1)S(1)}, bf16[16,8,4,256]{3,2,1,0:T(4,128)(2,1)}, u32[]{:S(2)}) copy-start(bf16[16,8,4,256]{3,2,1,0:T(4,128)(2,1)} %cot_ref.3) | copy-start | bytes 786436
  3.5 8.9 %copy-start.4 = (bf16[2,2,256,256]{3,2,1,0:T(8,128)(2,1)S(1)}, bf16[2,2,256,256]{3,2,1,0:T(8,128)(2,1)}, u32[]{:S(2)}) copy-start(bf16[2,2,256,256]{3,2,1,0:T(8,128)(2,1)} %param.10) | copy-start | bytes 1572868
  3.5 8.9 %copy-start.5 = (bf16[3,256,256]{2,1,0:T(8,128)(2,1)S(1)}, bf16[3,256,256]{2,1,0:T(8,128)(2,1)}, u32[]{:S(2)}) copy-start(bf16[3,256,256]{2,1,0:T(8,128)(2,1)} %wt_ref.5) | copy-start | bytes 1179652
  3.8 6.7 %collective-permute-start = (bf16[128,256]{1,0:T(8,128)(2,1)S(1)}, bf16[128,256]{1,0:T(8,128)(2,1)S(1)}, u32[]{:S(2)}, u32[]{:S(2)}) collective-permute-start(bf16[128,256]{1,0:T(8,128)(2,1)S(1)} %get-tuple-element.42), channel_id=1, source_target_pairs={{0,1},{1,0},{2,3},{3,2},{4,5},{5,4},{6,7},{7,6},{8,9},{9,8},{10,11... | collective-permute-start | bytes 196616 | tf_op jit(solution)/shard_map/ppermute | solution.py:486
  6.8 5.5 %collective-permute-start.1 = (bf16[2,8,4,256]{3,2,1,0:T(4,128)(2,1)S(1)}, bf16[2,8,4,256]{3,2,1,0:T(4,128)(2,1)S(1)}, u32[]{:S(2)}, u32[]{:S(2)}) collective-permute-start(bf16[2,8,4,256]{3,2,1,0:T(4,128)(2,1)S(1)} %get-tuple-element.45), channel_id=1, source_target_pairs={{0,30},{2,0},{4,2},{6,4},{8,6},{10,8},{12,10},{14,12},{16,14},{18,... | collective-permute-start | bytes 98312 | tf_op jit(solution)/shard_map/ppermute | solution.py:481
  12.3 7.3 %collective-permute-start.3 = (bf16[288,256]{1,0:T(8,128)(2,1)S(1)}, bf16[288,256]{1,0:T(8,128)(2,1)S(1)}, u32[]{:S(2)}, u32[]{:S(2)}) collective-permute-start(bf16[288,256]{1,0:T(8,128)(2,1)S(1)} %get-tuple-element.50), channel_id=1, source_target_pairs={{0,2},{2,4},{4,6},{6,8},{8,10},{10,12},{12,14},{14,16},{16,18},{18... | collective-permute-start | bytes 442376 | tf_op jit(solution)/shard_map/ppermute | solution.py:481
  16.9 8.4 %copy-start.3 = (bf16[3,3,256,256]{3,2,1,0:T(8,128)(2,1)S(1)}, bf16[3,3,256,256]{3,2,1,0:T(8,128)(2,1)}, u32[]{:S(2)}) copy-start(bf16[3,3,256,256]{3,2,1,0:T(8,128)(2,1)} %param.8) | copy-start | bytes 3538948
  19.5 2.0 %collective-permute-start.4 = (bf16[16,9,16,128]{3,2,1,0:T(8,128)(2,1)S(1)}, bf16[16,9,16,128]{3,2,1,0:T(8,128)(2,1)S(1)}, u32[]{:S(2)}, u32[]{:S(2)}) collective-permute-start(bf16[16,9,16,128]{3,2,1,0:T(8,128)(2,1)S(1)} %pass.1), channel_id=1, source_target_pairs={{0,2},{1,3},{2,0},{3,1},{4,6},{5,7},{6,4},{7,5},{8,10},{9,11},{10,... | collective-permute-start | bytes 1769480 | tf_op jit(solution)/shard_map/ppermute | solution.py:432
  21.7 7.7 %collective-permute-start.5 = (bf16[4,9,16,128]{3,2,1,0:T(8,128)(2,1)S(1)}, bf16[4,9,16,128]{3,2,1,0:T(8,128)(2,1)S(1)}, u32[]{:S(2)}, u32[]{:S(2)}) collective-permute-start(bf16[4,9,16,128]{3,2,1,0:T(8,128)(2,1)S(1)} %get-tuple-element.53.rest_0_), channel_id=1, source_target_pairs={{0,5},{1,4},{2,7},{3,6},{4,1},{5,0},{6,3},{7,2},{8,13},{9,12},{10,... | collective-permute-start | bytes 442376 | tf_op jit(solution)/shard_map/ppermute | solution.py:432
  21.9 9.0 %collective-permute-start.6 = (bf16[4,9,16,128]{3,2,1,0:T(8,128)(2,1)S(1)}, bf16[4,9,16,128]{3,2,1,0:T(8,128)(2,1)S(1)}, u32[]{:S(2)}, u32[]{:S(2)}) collective-permute-start(bf16[4,9,16,128]{3,2,1,0:T(8,128)(2,1)S(1)} %get-tuple-element.54.rest_1_), channel_id=1, source_target_pairs={{0,1},{1,0},{2,3},{3,2},{4,5},{5,4},{6,7},{7,6},{8,9},{9,8},{10,11... | collective-permute-start | bytes 442376 | tf_op jit(solution)/shard_map/ppermute | solution.py:432
  22.5 8.5 %collective-permute-start.7 = (bf16[4,9,16,128]{3,2,1,0:T(8,128)(2,1)S(1)}, bf16[4,9,16,128]{3,2,1,0:T(8,128)(2,1)S(1)}, u32[]{:S(2)}, u32[]{:S(2)}) collective-permute-start(bf16[4,9,16,128]{3,2,1,0:T(8,128)(2,1)S(1)} %get-tuple-element.55.rest_2_), channel_id=1, source_target_pairs={{0,4},{1,5},{2,6},{3,7},{4,0},{5,1},{6,2},{7,3},{8,12},{9,13},{10,... | collective-permute-start | bytes 442376 | tf_op jit(solution)/shard_map/ppermute | solution.py:432
  33.8 1.9 %collective-permute-start.8 = (bf16[16,7,16,128]{3,2,1,0:T(8,128)(2,1)S(1)}, bf16[16,7,16,128]{3,2,1,0:T(8,128)(2,1)S(1)}, u32[]{:S(2)}, u32[]{:S(2)}) collective-permute-start(bf16[16,7,16,128]{3,2,1,0:T(8,128)(2,1)S(1)} %get-tuple-element.61), channel_id=1, source_target_pairs={{0,2},{1,3},{2,0},{3,1},{4,6},{5,7},{6,4},{7,5},{8,10},{9,11},{10,... | collective-permute-start | bytes 1376264 | tf_op jit(solution)/shard_map/ppermute | solution.py:432
  35.7 7.0 %collective-permute-start.9 = (bf16[4,7,16,128]{3,2,1,0:T(8,128)(2,1)S(1)}, bf16[4,7,16,128]{3,2,1,0:T(8,128)(2,1)S(1)}, u32[]{:S(2)}, u32[]{:S(2)}) collective-permute-start(bf16[4,7,16,128]{3,2,1,0:T(8,128)(2,1)S(1)} %get-tuple-element.63), channel_id=1, source_target_pairs={{0,5},{1,4},{2,7},{3,6},{4,1},{5,0},{6,3},{7,2},{8,13},{9,12},{10,... | collective-permute-start | bytes 344072 | tf_op jit(solution)/shard_map/ppermute | solution.py:432
  37.0 7.4 %collective-permute-start.10 = (bf16[4,7,16,128]{3,2,1,0:T(8,128)(2,1)S(1)}, bf16[4,7,16,128]{3,2,1,0:T(8,128)(2,1)S(1)}, u32[]{:S(2)}, u32[]{:S(2)}) collective-permute-start(bf16[4,7,16,128]{3,2,1,0:T(8,128)(2,1)S(1)} %get-tuple-element.64), channel_id=1, source_target_pairs={{0,1},{1,0},{2,3},{3,2},{4,5},{5,4},{6,7},{7,6},{8,9},{9,8},{10,11... | collective-permute-start | bytes 344072 | tf_op jit(solution)/shard_map/ppermute | solution.py:432
  37.6 6.8 %collective-permute-start.11 = (bf16[4,7,16,128]{3,2,1,0:T(8,128)(2,1)S(1)}, bf16[4,7,16,128]{3,2,1,0:T(8,128)(2,1)S(1)}, u32[]{:S(2)}, u32[]{:S(2)}) collective-permute-start(bf16[4,7,16,128]{3,2,1,0:T(8,128)(2,1)S(1)} %get-tuple-element.65), channel_id=1, source_target_pairs={{0,4},{1,5},{2,6},{3,7},{4,0},{5,1},{6,2},{7,3},{8,12},{9,13},{10,... | collective-permute-start | bytes 344072 | tf_op jit(solution)/shard_map/ppermute | solution.py:432
  44.5 8.4 %collective-permute-start.12 = (bf16[16,16,128]{2,1,0:T(8,128)(2,1)S(1)}, bf16[16,16,128]{2,1,0:T(8,128)(2,1)S(1)}, u32[]{:S(2)}, u32[]{:S(2)}) collective-permute-start(bf16[16,16,128]{2,1,0:T(8,128)(2,1)S(1)} %get-tuple-element.67), channel_id=1, source_target_pairs={{0,24},{1,25},{2,26},{3,27},{4,28},{5,29},{6,30},{7,31},{8,16},{9,... | collective-permute-start | bytes 196616 | tf_op jit(solution)/shard_map/ppermute | solution.py:432
  46.8 6.3 %collective-permute-start.13 = (bf16[16,16,128]{2,1,0:T(8,128)(2,1)S(1)}, bf16[16,16,128]{2,1,0:T(8,128)(2,1)S(1)}, u32[]{:S(2)}, u32[]{:S(2)}) collective-permute-start(bf16[16,16,128]{2,1,0:T(8,128)(2,1)S(1)} %get-tuple-element.68), channel_id=1, source_target_pairs={{0,16},{1,17},{2,18},{3,19},{4,20},{5,21},{6,22},{7,23},{8,24},{9,... | collective-permute-start | bytes 196616 | tf_op jit(solution)/shard_map/ppermute | solution.py:432
  46.8 6.3 %collective-permute-start.14 = (bf16[16,16,128]{2,1,0:T(8,128)(2,1)S(1)}, bf16[16,16,128]{2,1,0:T(8,128)(2,1)S(1)}, u32[]{:S(2)}, u32[]{:S(2)}) collective-permute-start(bf16[16,16,128]{2,1,0:T(8,128)(2,1)S(1)} %get-tuple-element.69), channel_id=1, source_target_pairs={{0,8},{1,9},{2,10},{3,11},{4,12},{5,13},{6,14},{7,15},{8,0},{9,1},... | collective-permute-start | bytes 196616 | tf_op jit(solution)/shard_map/ppermute | solution.py:432
  49.0 3.9 %collective-permute-start.2 = (bf16[64,256]{1,0:T(8,128)(2,1)S(1)}, bf16[64,256]{1,0:T(8,128)(2,1)S(1)}, u32[]{:S(2)}, u32[]{:S(2)}) collective-permute-start(bf16[64,256]{1,0:T(8,128)(2,1)S(1)} %get-tuple-element.48), channel_id=1, source_target_pairs={{0,1},{1,0},{2,3},{3,2},{4,5},{5,4},{6,7},{7,6},{8,9},{9,8},{10,11... | collective-permute-start | bytes 98312 | tf_op jit(solution)/shard_map/ppermute | solution.py:486
  53.2 5.0 %collective-permute-start.17 = (bf16[16,16,128]{2,1,0:T(8,128)(2,1)S(1)}, bf16[16,16,128]{2,1,0:T(8,128)(2,1)S(1)}, u32[]{:S(2)}, u32[]{:S(2)}) collective-permute-start(bf16[16,16,128]{2,1,0:T(8,128)(2,1)S(1)} %line_sum.1.a_ref), channel_id=1, source_target_pairs={{0,8},{1,9},{2,10},{3,11},{4,12},{5,13},{6,14},{7,15},{8,0},{9,1},... | collective-permute-start | bytes 196616 | tf_op jit(solution)/shard_map/ppermute | solution.py:432
  53.7 7.7 %collective-permute-start.16 = (bf16[16,16,128]{2,1,0:T(8,128)(2,1)S(1)}, bf16[16,16,128]{2,1,0:T(8,128)(2,1)S(1)}, u32[]{:S(2)}, u32[]{:S(2)}) collective-permute-start(bf16[16,16,128]{2,1,0:T(8,128)(2,1)S(1)} %line_sum.1.a_ref), channel_id=1, source_target_pairs={{0,16},{1,17},{2,18},{3,19},{4,20},{5,21},{6,22},{7,23},{8,24},{9,... | collective-permute-start | bytes 196616 | tf_op jit(solution)/shard_map/ppermute | solution.py:432
  56.0 6.2 %collective-permute-start.15 = (bf16[16,16,128]{2,1,0:T(8,128)(2,1)S(1)}, bf16[16,16,128]{2,1,0:T(8,128)(2,1)S(1)}, u32[]{:S(2)}, u32[]{:S(2)}) collective-permute-start(bf16[16,16,128]{2,1,0:T(8,128)(2,1)S(1)} %line_sum.1.a_ref), channel_id=1, source_target_pairs={{0,24},{1,25},{2,26},{3,27},{4,28},{5,29},{6,30},{7,31},{8,16},{9,... | collective-permute-start | bytes 196616 | tf_op jit(solution)/shard_map/ppermute | solution.py:432
  62.2 11.0 %collective-permute-start.20 = (bf16[4,16,16,128]{3,2,1,0:T(8,128)(2,1)S(1)}, bf16[4,16,16,128]{3,2,1,0:T(8,128)(2,1)S(1)}, u32[]{:S(2)}, u32[]{:S(2)}) collective-permute-start(bf16[4,16,16,128]{3,2,1,0:T(8,128)(2,1)S(1)} %line_gather.1.rest_0_.a_ref), channel_id=1, source_target_pairs={{0,4},{1,5},{2,6},{3,7},{4,0},{5,1},{6,2},{7,3},{8,12},{9,13},{10,... | collective-permute-start | bytes 786440 | tf_op jit(solution)/shard_map/ppermute | solution.py:432
  63.6 11.4 %collective-permute-start.19 = (bf16[4,16,16,128]{3,2,1,0:T(8,128)(2,1)S(1)}, bf16[4,16,16,128]{3,2,1,0:T(8,128)(2,1)S(1)}, u32[]{:S(2)}, u32[]{:S(2)}) collective-permute-start(bf16[4,16,16,128]{3,2,1,0:T(8,128)(2,1)S(1)} %line_gather.1.rest_0_.a_ref), channel_id=1, source_target_pairs={{0,1},{1,0},{2,3},{3,2},{4,5},{5,4},{6,7},{7,6},{8,9},{9,8},{10,11... | collective-permute-start | bytes 786440 | tf_op jit(solution)/shard_map/ppermute | solution.py:432
  64.5 10.6 %collective-permute-start.18 = (bf16[4,16,16,128]{3,2,1,0:T(8,128)(2,1)S(1)}, bf16[4,16,16,128]{3,2,1,0:T(8,128)(2,1)S(1)}, u32[]{:S(2)}, u32[]{:S(2)}) collective-permute-start(bf16[4,16,16,128]{3,2,1,0:T(8,128)(2,1)S(1)} %line_gather.1.rest_0_.a_ref), channel_id=1, source_target_pairs={{0,5},{1,4},{2,7},{3,6},{4,1},{5,0},{6,3},{7,2},{8,13},{9,12},{10,... | collective-permute-start | bytes 786440 | tf_op jit(solution)/shard_map/ppermute | solution.py:432
  75.2 2.7 %collective-permute-start.21 = (bf16[16,16,16,128]{3,2,1,0:T(8,128)(2,1)S(1)}, bf16[16,16,16,128]{3,2,1,0:T(8,128)(2,1)S(1)}, u32[]{:S(2)}, u32[]{:S(2)}) collective-permute-start(bf16[16,16,16,128]{3,2,1,0:T(8,128)(2,1)S(1)} %plane_gather.1.half_ref), channel_id=1, source_target_pairs={{0,2},{1,3},{2,0},{3,1},{4,6},{5,7},{6,4},{7,5},{8,10},{9,11},{10,... | collective-permute-start | bytes 3145736 | tf_op jit(solution)/shard_map/ppermute | solution.py:432

commit v14 on v12

--- a/solution.py
+++ b/solution.py
@@ -103,9 +103,8 @@
         outs[k][...] = silu_norm(v).astype(BF)
 
 
-def acts_kernel(bands, count_ref, x_ref, top_ref, bot_ref, xt_ref, acts_ref, at_ref, last_ref):
+def acts_kernel(count_ref, x_ref, _, xt_ref, acts_ref, at_ref, last_ref):
     count = count_ref[0]
-    band = lax.axis_index("grp")
     rows, cols = xt_ref.shape[0], xt_ref.shape[1]
     edge = jnp.zeros((rows + 2, SLOTS, CH), BF)
     acts_ref[:, 0] = edge
@@ -128,6 +127,13 @@
         return 0
 
     lax.fori_loop(0, rows // 2, rows_of, 0, unroll=4)
+
+
+def halo_kernel(bands, count_ref, top_ref, bot_ref, *rest):
+    acts_ref, at_ref, last_ref = rest[-3:]
+    count = count_ref[0]
+    band = lax.axis_index("grp")
+    rows, cols = acts_ref.shape[0] - 2, acts_ref.shape[1] - 2
     halo = []
     for ref, flag, i, row in ((top_ref, band > 0, 0, 0), (bot_ref, band < bands - 1, 2, rows + 1)):
         a = jnp.where(flag, ref[...].astype(F32), 0.0).astype(BF)
@@ -510,12 +516,22 @@
     )
     top, bot = from_bands(edge)
     nxt_got = around(nxt, "tm", -1)
+    last_shape = (2 * wide + 32, ch)
+    at_shape = (3 * ch, (rows + 4) * 128)
     xt, acts, at, last_two = call(
-        functools.partial(acts_kernel, grp),
+        acts_kernel,
         "acts",
-        [count, (VMEM, x), (VMEM, top), (VMEM, bot)],
-        [(VMEM, tile), (VMEM, padded), (VMEM, (3 * ch, (rows + 4) * 128)), (VMEM, (2 * wide + 32, ch))],
+        [count, (VMEM, x), (ANY, edge[0])],
+        [(VMEM, tile), (VMEM, padded), (VMEM, at_shape), (VMEM, last_shape)],
         flops=2 * tap,
+    )
+    acts, at, last_two = call(
+        functools.partial(halo_kernel, grp),
+        "halo",
+        [count, (VMEM, top), (VMEM, bot), (VMEM, acts), (VMEM, at), (VMEM, last_two)],
+        [(VMEM, padded), (VMEM, at_shape), (VMEM, last_shape)],
+        flops=tap // 8,
+        alias={3: 0, 4: 1, 5: 2},
     )
     prev = around(last_two, "tm", 1)
     half = (16, 9, 16, ch // 2)
@@ -553,7 +569,7 @@
         grant=14,
     )
     parts_a = four_round(parts_a, plane, tm, grp)
-    send_b = passed(send_b, parts_a[1:2])
+    send_b = passed(send_b, parts_a[3:4])
     parts_b = plane_send(keep_b, core_round(send_b, tm, grp), [])
     parts_b = four_round(parts_b, plane, tm, grp)
     parts = call(

time: 76.8 us -> 78.4 us (1.021)
  local copies, waits for them, and re-layouts: 2.18 us -> 3.2 us
    ppermute x18, waiting for transfers between devices: 18.3 us -> 19.4 us  [swap(): return lax.ppermute(value, AXES, [(d, d ^ flip) for d in range(tm * grp)])]
    unnamed x12, local copies, waits for them, and re-layouts: 2.18 us -> 3.2 us
    ppermute x2, waiting for transfers between devices: 2.67 us -> 1.7 us  [around(): lax.ppermute(value, axis, [(i, (i + by) % count) for i in range(count)])]
    pallas_call x16 -> x17, Pallas kernels: 23.9 us -> 23.9 us  [call(): pl.pallas_call(kernel, out_shape=shapes, in_specs=[s for s, _ in ins], ou...]
  transfers between devices with their start and end apart: 22 -> 22, of which waited for: 14 -> 12; matrix products, arithmetic and copies ran while one was open for 0% -> 0% of each run, Pallas kernels for 28% -> 28%
where the time goes in v14:
time: 78.4 us; the launch traced here: 78.2 us
  starting transfers between devices  26 us (33%)
  Pallas kernels  23.9 us (30%)
  waiting for transfers between devices  23.6 us (30%)
  local copies, waits for them, and re-layouts  3.2 us (4%)
  between operations  1.48 us (2%)
    pallas_call x17, Pallas kernels, call(): pl.pallas_call(kernel, out_shape=shapes, in_specs=[s for s, _ in ins], ou...  23.9 us
    ppermute x18, waiting for transfers between devices, swap(): return lax.ppermute(value, AXES, [(d, d ^ flip) for d in range(tm * grp)])  19.4 us
    ppermute x18, starting transfers between devices, swap(): return lax.ppermute(value, AXES, [(d, d ^ flip) for d in range(tm * grp)])  17.9 us
    ppermute x2, starting transfers between devices, from_bands(): got = lax.ppermute(parts[0], 'grp', [(0, 1), (1, 0)])  4.43 us
    ppermute x2, starting transfers between devices, around(): lax.ppermute(value, axis, [(i, (i + by) % count) for i in range(count)])  3.7 us
    unnamed x12, local copies, waits for them, and re-layouts  3.2 us
    ppermute x2, waiting for transfers between devices, from_bands(): got = lax.ppermute(parts[0], 'grp', [(0, 1), (1, 0)])  2.52 us
    ppermute x2, waiting for transfers between devices, around(): lax.ppermute(value, axis, [(i, (i + by) % count) for i in range(count)])  1.7 us
  transfers between devices with their start and end apart: 22, of which 12 were waited for; matrix products, arithmetic and copies ran while one was open for 0% of the time, Pallas kernels for 28%

profile of v14, /device:TPU:0, one launch (start us, length us, event | category | flops | bytes accessed | tf_op | source)
XLA Modules:
  0.0 78.2 jit_solution(13530821390893764464)
XLA Ops:
  1.3 1.2 %copy-done = bf16[16,16,8,256]{3,2,1,0:T(8,128)(2,1)S(1)} copy-done((bf16[16,16,8,256]{3,2,1,0:T(8,128)(2,1)S(1)}, bf16[16,16,8,256]{3,2,1,0:T(8,128)(2,1)}, u32[]{:S(2)}) %copy-start) | copy-done | bytes 1048600
  2.5 0.9 %copy-done.1 = bf16[16,8,4,256]{3,2,1,0:T(4,128)(2,1)S(1)} copy-done((bf16[16,8,4,256]{3,2,1,0:T(4,128)(2,1)S(1)}, bf16[16,8,4,256]{3,2,1,0:T(4,128)(2,1)}, u32[]{:S(2)}) %copy-start.1) | copy-done | bytes 262168
  3.5 0.3 edges.1
  3.8 3.0 %collective-permute-start = (bf16[128,256]{1,0:T(8,128)(2,1)S(1)}, bf16[128,256]{1,0:T(8,128)(2,1)S(1)}, u32[]{:S(2)}, u32[]{:S(2)}) collective-permute-start(bf16[128,256]{1,0:T(8,128)(2,1)S(1)} %get-tuple-element.45._), channel_id=1, source_target_pairs={{0,1},{1,0},{2,3},{3,2},{4,5},{5,4},{6,7},{7,6},{8,9},{9,8},{10,11... | collective-permute-start | bytes 196616 | tf_op jit(solution)/shard_map/ppermute | solution.py:491
  6.8 3.7 %collective-permute-start.1 = (bf16[2,8,4,256]{3,2,1,0:T(4,128)(2,1)S(1)}, bf16[2,8,4,256]{3,2,1,0:T(4,128)(2,1)S(1)}, u32[]{:S(2)}, u32[]{:S(2)}) collective-permute-start(bf16[2,8,4,256]{3,2,1,0:T(4,128)(2,1)S(1)} %get-tuple-element.51), channel_id=1, source_target_pairs={{0,30},{2,0},{4,2},{6,4},{8,6},{10,8},{12,10},{14,12},{16,14},{18,... | collective-permute-start | bytes 98312 | tf_op jit(solution)/shard_map/ppermute | solution.py:486
  10.5 1.6 %acts.1 = (bf16[16,8,16,256]{3,2,1,0:T(8,128)(2,1)S(1)}, bf16[18,10,16,256]{3,2,1,0:T(8,128)(2,1)S(1)}, bf16[768,2560]{1,0:T(8,128)(2,1)S(1)}, bf16[288,256]{1,0:T(8,128)(2,1)S(1)}) custom-call(s32[1]{0:T(128)S(6)} %copy.29.count_ref, bf16[16,128,256]{2,1,0:T(8,128)(2,1)S(1)} %bitcast.7, bf16[128,256]{1,0:T(8,128)(2,1)S(1)} %get-tuple-element.45._), custom_call_target="tpu_custom_call" | custom-call | flops 536870912 | bytes 7651332 | tf_op jit(solution)/shard_map/acts/pallas_call | solution.py:413
  12.2 0.2 halo.1
  12.4 0.7 copy-done.2
  13.1 0.2 copy-done.4
  13.3 0.1 copy-done.5
  13.4 4.5 %grad_spatial.1 = (bf16[8,4,16,256]{3,2,1,0:T(8,128)(2,1)S(1)}, bf16[16,8,16,256]{3,2,1,0:T(8,128)(2,1)S(1)}, bf16[16,10,16,256]{3,2,1,0:T(8,128)(2,1)S(1)}, bf1...) custom-call(s32[1]{0:T(128)S(6)} %copy.29.count_ref, ...), custom_call_target="tpu_custom_call" | custom-call | flops 3758096384 | bytes 8978436 | tf_op jit(solution)/shard_map/grad_spatial/pallas_call | solution.py:413
  17.9 1.7 %collective-permute-done.3.__1_.prev_ref = bf16[288,256]{1,0:T(8,128)(2,1)S(1)} collective-permute-done((bf16[288,256]{1,0:T(8,128)(2,1)S(1)}, bf16[288,256]{1,0:T(8,128)(2,1)S(1)}, u32[]{:S(2)}, u32[]{:S(2)}) %collective-permute-start.3) | collective-permute-done | bytes 147488 | tf_op jit(solution)/shard_map/ppermute | solution.py:486
  19.6 3.6 %spatial.1 = (bf16[18,10,16,256]{3,2,1,0:T(8,128)(2,1)S(1)}, bf16[16,8,16,256]{3,2,1,0:T(8,128)(2,1)S(1)}) custom-call(s32[1]{0:T(128)S(6)} %copy.29.count_ref, bf16[18,10,16,256]{3,2,1,0:T(8,128)(2,1)S(1)} %get-tuple-element.55.acts_in, bf16[288,256]{1,0:T(8,128)(2,1)S(1)} %collective-permute-done.3.__1_.prev_ref, ...), custom_call_target="tpu_custom_call", output_to_operand_aliasing={{0}: (1, {})} | custom-call | flops 2415919104 | bytes 5324804 | tf_op jit(solution)/shard_map/spatial/pallas_call | solution.py:413
  23.2 0.2 plane_send.2
  23.4 0.1 collective-permute-start.7
  23.4 2.8 %forward.1 = (bf16[512,256]{1,0:T(8,128)(2,1)S(1)}, bf16[16,7,16,128]{3,2,1,0:T(8,128)(2,1)S(1)}, bf16[16,7,16,128]{3,2,1,0:T(8,128)(2,1)S(1)}) custom-call(s32[1]{0:T(128)S(6)} %copy.29.count_ref, bf16[16,8,16,256]{3,2,1,0:T(8,128)(2,1)S(1)} %get-tuple-element.46.xt_ref, bf16[16,8,16,256]{3,2,1,0:T(8,128)(2,1)S(1)} %get-tuple-element.58.rest_0_.sp_ref, ...), custom_call_target="tpu_custom_call" | custom-call | flops 2684354560 | bytes 5505028 | tf_op jit(solution)/shard_map/forward/pallas_call | solution.py:413
  26.3 3.4 %collective-permute-done.7.__1_.refs_3_ = bf16[4,9,16,128]{3,2,1,0:T(8,128)(2,1)S(1)} collective-permute-done((bf16[4,9,16,128]{3,2,1,0:T(8,128)(2,1)S(1)}, bf16[4,9,16,128]{3,2,1,0:T(8,128)(2,1)S(1)}, u32[]{:S(2)}, u32[]{:S(2)}) %collective-permute-start.7) | collective-permute-done | bytes 147488 | tf_op jit(solution)/shard_map/ppermute | solution.py:437
  29.7 0.2 collective-permute-start.5
  29.9 1.5 %collective-permute-start.6 = (bf16[4,9,16,128]{3,2,1,0:T(8,128)(2,1)S(1)}, bf16[4,9,16,128]{3,2,1,0:T(8,128)(2,1)S(1)}, u32[]{:S(2)}, u32[]{:S(2)}) collective-permute-start(bf16[4,9,16,128]{3,2,1,0:T(8,128)(2,1)S(1)} %get-tuple-element.63.rest_2_), channel_id=1, source_target_pairs={{0,1},{1,0},{2,3},{3,2},{4,5},{5,4},{6,7},{7,6},{8,9},{9,8},{10,11... | collective-permute-start | bytes 442376 | tf_op jit(solution)/shard_map/ppermute | solution.py:437
  31.4 0.1 collective-permute-done.8.got_ref
  31.5 0.1 plane_send.3
  31.6 1.7 %collective-permute-start.9 = (bf16[4,7,16,128]{3,2,1,0:T(8,128)(2,1)S(1)}, bf16[4,7,16,128]{3,2,1,0:T(8,128)(2,1)S(1)}, u32[]{:S(2)}, u32[]{:S(2)}) collective-permute-start(bf16[4,7,16,128]{3,2,1,0:T(8,128)(2,1)S(1)} %get-tuple-element.69), channel_id=1, source_target_pairs={{0,5},{1,4},{2,7},{3,6},{4,1},{5,0},{6,3},{7,2},{8,13},{9,12},{10,... | collective-permute-start | bytes 344072 | tf_op jit(solution)/shard_map/ppermute | solution.py:437
  33.3 1.5 %collective-permute-start.10 = (bf16[4,7,16,128]{3,2,1,0:T(8,128)(2,1)S(1)}, bf16[4,7,16,128]{3,2,1,0:T(8,128)(2,1)S(1)}, u32[]{:S(2)}, u32[]{:S(2)}) collective-permute-start(bf16[4,7,16,128]{3,2,1,0:T(8,128)(2,1)S(1)} %get-tuple-element.70), channel_id=1, source_target_pairs={{0,1},{1,0},{2,3},{3,2},{4,5},{5,4},{6,7},{7,6},{8,9},{9,8},{10,11... | collective-permute-start | bytes 344072 | tf_op jit(solution)/shard_map/ppermute | solution.py:437
  34.8 0.3 collective-permute-start.11
  35.2 2.2 %collective-permute-done.5.refs_1_ = bf16[4,9,16,128]{3,2,1,0:T(8,128)(2,1)S(1)} collective-permute-done((bf16[4,9,16,128]{3,2,1,0:T(8,128)(2,1)S(1)}, bf16[4,9,16,128]{3,2,1,0:T(8,128)(2,1)S(1)}, u32[]{:S(2)}, u32[]{:S(2)}) %collective-permute-start.5) | collective-permute-done | bytes 147488 | tf_op jit(solution)/shard_map/ppermute | solution.py:437
  37.3 4.9 %collective-permute-done.6.refs_2_ = bf16[4,9,16,128]{3,2,1,0:T(8,128)(2,1)S(1)} collective-permute-done((bf16[4,9,16,128]{3,2,1,0:T(8,128)(2,1)S(1)}, bf16[4,9,16,128]{3,2,1,0:T(8,128)(2,1)S(1)}, u32[]{:S(2)}, u32[]{:S(2)}) %collective-permute-start.6) | collective-permute-done | bytes 147488 | tf_op jit(solution)/shard_map/ppermute | solution.py:437
  42.2 1.8 %collective-permute-done.10.refs_6_ = bf16[4,7,16,128]{3,2,1,0:T(8,128)(2,1)S(1)} collective-permute-done((bf16[4,7,16,128]{3,2,1,0:T(8,128)(2,1)S(1)}, bf16[4,7,16,128]{3,2,1,0:T(8,128)(2,1)S(1)}, u32[]{:S(2)}, u32[]{:S(2)}) %collective-permute-start.10) | collective-permute-done | bytes 114720 | tf_op jit(solution)/shard_map/ppermute | solution.py:437
  44.0 0.1 line_send.1
  44.2 1.5 %collective-permute-start.12 = (bf16[16,16,128]{2,1,0:T(8,128)(2,1)S(1)}, bf16[16,16,128]{2,1,0:T(8,128)(2,1)S(1)}, u32[]{:S(2)}, u32[]{:S(2)}) collective-permute-start(bf16[16,16,128]{2,1,0:T(8,128)(2,1)S(1)} %get-tuple-element.73), channel_id=1, source_target_pairs={{0,24},{1,25},{2,26},{3,27},{4,28},{5,29},{6,30},{7,31},{8,16},{9,... | collective-permute-start | bytes 196616 | tf_op jit(solution)/shard_map/ppermute | solution.py:437
  45.7 2.9 %collective-permute-start.14 = (bf16[16,16,128]{2,1,0:T(8,128)(2,1)S(1)}, bf16[16,16,128]{2,1,0:T(8,128)(2,1)S(1)}, u32[]{:S(2)}, u32[]{:S(2)}) collective-permute-start(bf16[16,16,128]{2,1,0:T(8,128)(2,1)S(1)} %get-tuple-element.75), channel_id=1, source_target_pairs={{0,8},{1,9},{2,10},{3,11},{4,12},{5,13},{6,14},{7,15},{8,0},{9,1},... | collective-permute-start | bytes 196616 | tf_op jit(solution)/shard_map/ppermute | solution.py:437
  48.6 1.4 %collective-permute-start.2 = (bf16[64,256]{1,0:T(8,128)(2,1)S(1)}, bf16[64,256]{1,0:T(8,128)(2,1)S(1)}, u32[]{:S(2)}, u32[]{:S(2)}) collective-permute-start(bf16[64,256]{1,0:T(8,128)(2,1)S(1)} %get-tuple-element.54), channel_id=1, source_target_pairs={{0,1},{1,0},{2,3},{3,2},{4,5},{5,4},{6,7},{7,6},{8,9},{9,8},{10,11... | collective-permute-start | bytes 98312 | tf_op jit(solution)/shard_map/ppermute | solution.py:491
  50.0 2.5 %collective-permute-done.2.rest_0_.top_ref.bot_ref = bf16[64,256]{1,0:T(8,128)(2,1)S(1)} collective-permute-done((bf16[64,256]{1,0:T(8,128)(2,1)S(1)}, bf16[64,256]{1,0:T(8,128)(2,1)S(1)}, u32[]{:S(2)}, u32[]{:S(2)}) %collective-permute-start.2) | collective-permute-done | bytes 32800 | tf_op jit(solution)/shard_map/ppermute | solution.py:491
  52.6 0.4 collective-permute-start.17
  53.0 2.0 %collective-permute-start.16 = (bf16[16,16,128]{2,1,0:T(8,128)(2,1)S(1)}, bf16[16,16,128]{2,1,0:T(8,128)(2,1)S(1)}, u32[]{:S(2)}, u32[]{:S(2)}) collective-permute-start(bf16[16,16,128]{2,1,0:T(8,128)(2,1)S(1)} %line_sum.1.a_ref), channel_id=1, source_target_pairs={{0,16},{1,17},{2,18},{3,19},{4,20},{5,21},{6,22},{7,23},{8,24},{9,... | collective-permute-start | bytes 196616 | tf_op jit(solution)/shard_map/ppermute | solution.py:437
  55.0 2.0 %collective-permute-start.15 = (bf16[16,16,128]{2,1,0:T(8,128)(2,1)S(1)}, bf16[16,16,128]{2,1,0:T(8,128)(2,1)S(1)}, u32[]{:S(2)}, u32[]{:S(2)}) collective-permute-start(bf16[16,16,128]{2,1,0:T(8,128)(2,1)S(1)} %line_sum.1.a_ref), channel_id=1, source_target_pairs={{0,24},{1,25},{2,26},{3,27},{4,28},{5,29},{6,30},{7,31},{8,16},{9,... | collective-permute-start | bytes 196616 | tf_op jit(solution)/shard_map/ppermute | solution.py:437
  57.0 0.3 collective-permute-done.17.d_ref
  57.4 2.8 %collective-permute-done.16.c_ref = bf16[16,16,128]{2,1,0:T(8,128)(2,1)S(1)} collective-permute-done((bf16[16,16,128]{2,1,0:T(8,128)(2,1)S(1)}, bf16[16,16,128]{2,1,0:T(8,128)(2,1)S(1)}, u32[]{:S(2)}, u32[]{:S(2)}) %collective-permute-start.16) | collective-permute-done | bytes 65568 | tf_op jit(solution)/shard_map/ppermute | solution.py:437
  60.2 0.9 %collective-permute-done.15.b_ref = bf16[16,16,128]{2,1,0:T(8,128)(2,1)S(1)} collective-permute-done((bf16[16,16,128]{2,1,0:T(8,128)(2,1)S(1)}, bf16[16,16,128]{2,1,0:T(8,128)(2,1)S(1)}, u32[]{:S(2)}, u32[]{:S(2)}) %collective-permute-start.15) | collective-permute-done | bytes 65568 | tf_op jit(solution)/shard_map/ppermute | solution.py:437
  61.2 0.9 %collective-permute-start.20 = (bf16[4,16,16,128]{3,2,1,0:T(8,128)(2,1)S(1)}, bf16[4,16,16,128]{3,2,1,0:T(8,128)(2,1)S(1)}, u32[]{:S(2)}, u32[]{:S(2)}) collective-permute-start(bf16[4,16,16,128]{3,2,1,0:T(8,128)(2,1)S(1)} %line_gather.1.rest_0_.a_ref), channel_id=1, source_target_pairs={{0,4},{1,5},{2,6},{3,7},{4,0},{5,1},{6,2},{7,3},{8,12},{9,13},{10,... | collective-permute-start | bytes 786440 | tf_op jit(solution)/shard_map/ppermute | solution.py:437
  62.0 1.5 %collective-permute-start.19 = (bf16[4,16,16,128]{3,2,1,0:T(8,128)(2,1)S(1)}, bf16[4,16,16,128]{3,2,1,0:T(8,128)(2,1)S(1)}, u32[]{:S(2)}, u32[]{:S(2)}) collective-permute-start(bf16[4,16,16,128]{3,2,1,0:T(8,128)(2,1)S(1)} %line_gather.1.rest_0_.a_ref), channel_id=1, source_target_pairs={{0,1},{1,0},{2,3},{3,2},{4,5},{5,4},{6,7},{7,6},{8,9},{9,8},{10,11... | collective-permute-start | bytes 786440 | tf_op jit(solution)/shard_map/ppermute | solution.py:437
  63.5 1.2 %collective-permute-start.18 = (bf16[4,16,16,128]{3,2,1,0:T(8,128)(2,1)S(1)}, bf16[4,16,16,128]{3,2,1,0:T(8,128)(2,1)S(1)}, u32[]{:S(2)}, u32[]{:S(2)}) collective-permute-start(bf16[4,16,16,128]{3,2,1,0:T(8,128)(2,1)S(1)} %line_gather.1.rest_0_.a_ref), channel_id=1, source_target_pairs={{0,5},{1,4},{2,7},{3,6},{4,1},{5,0},{6,3},{7,2},{8,13},{9,12},{10,... | collective-permute-start | bytes 786440 | tf_op jit(solution)/shard_map/ppermute | solution.py:437
  64.7 7.4 %grad_x.1 = (bf16[16,128,256]{2,1,0:T(8,128)(2,1)}, bf16[16,8,4,256]{3,2,1,0:T(4,128)(2,1)}, f32[8,128]{1,0:T(8,128)S(1)}) custom-call(s32[1]{0:T(128)S(6)} %copy.29.count_ref, bf16[16,8,16,256]{3,2,1,0:T(8,128)(2,1)S(1)} %get-tuple-element.46.xt_ref, bf16[16,8,16,256]{3,2,1,0:T(8,128)(2,1)S(1)} %get-tuple-element.52.gy_ref, ...), custom_call_target="tpu_custom_call" | custom-call | flops 2684354560 | bytes 7147524 | tf_op jit(solution)/shard_map/grad_x/pallas_call | solution.py:413
  72.2 1.7 %collective-permute-done.19.c_ref = bf16[4,16,16,128]{3,2,1,0:T(8,128)(2,1)S(1)} collective-permute-done((bf16[4,16,16,128]{3,2,1,0:T(8,128)(2,1)S(1)}, bf16[4,16,16,128]{3,2,1,0:T(8,128)(2,1)S(1)}, u32[]{:S(2)}, u32[]{:S(2)}) %collective-permute-start.19) | collective-permute-done | bytes 262176 | tf_op jit(solution)/shard_map/ppermute | solution.py:437
  73.9 0.1 plane_gather.1.half_ref
  74.0 0.1 collective-permute-start.21
  74.1 1.5 %finish.2 = (f32[9,256,256]{2,1,0:T(8,128)}, f32[3,256,256]{2,1,0:T(8,128)}, f32[4,256,256]{2,1,0:T(8,128)}) custom-call(bf16[16,16,16,128]{3,2,1,0:T(8,128)(2,1)S(1)} %plane_gather.1.half_ref), custom_call_target="tpu_custom_call" | custom-call | bytes 5242880 | tf_op jit(solution)/shard_map/finish/pallas_call | solution.py:413
  75.5 1.2 %collective-permute-done.21.half_ref = bf16[16,16,16,128]{3,2,1,0:T(8,128)(2,1)S(1)} collective-permute-done((bf16[16,16,16,128]{3,2,1,0:T(8,128)(2,1)S(1)}, bf16[16,16,16,128]{3,2,1,0:T(8,128)(2,1)S(1)}, u32[]{:S(2)}, u32[]{:S(2)}) %collective-permute-start.21) | collective-permute-done | bytes 1048608 | tf_op jit(solution)/shard_map/ppermute | solution.py:437
  76.7 1.5 %finish.3 = (f32[9,256,256]{2,1,0:T(8,128)}, f32[3,256,256]{2,1,0:T(8,128)}, f32[4,256,256]{2,1,0:T(8,128)}) custom-call(bf16[16,16,16,128]{3,2,1,0:T(8,128)(2,1)S(1)} %collective-permute-done.21.half_ref, f32[9,256,256]{2,1,0:T(8,128)} %get-tuple-element.79.rest_0_, ...), custom_call_target="tpu_custom_call", output_to_operand_aliasing={{0}: (1, {}), {1}: (2, {}), {2}: (3, {})} | custom-call | bytes 9437184 | tf_op jit(solution)/shard_map/finish/pallas_call | solution.py:413
  (25 shorter events, 0.1 us)
Async XLA Ops:
  1.3 1.2 %copy-start = (bf16[16,16,8,256]{3,2,1,0:T(8,128)(2,1)S(1)}, bf16[16,16,8,256]{3,2,1,0:T(8,128)(2,1)}, u32[]{:S(2)}) copy-start(bf16[16,16,8,256]{3,2,1,0:T(8,128)(2,1)} %param.6) | copy-start | bytes 3145732
  2.5 0.9 %copy-start.1 = (bf16[16,8,4,256]{3,2,1,0:T(4,128)(2,1)S(1)}, bf16[16,8,4,256]{3,2,1,0:T(4,128)(2,1)}, u32[]{:S(2)}) copy-start(bf16[16,8,4,256]{3,2,1,0:T(4,128)(2,1)} %cot_ref.3) | copy-start | bytes 786436
  3.8 8.4 %collective-permute-start = (bf16[128,256]{1,0:T(8,128)(2,1)S(1)}, bf16[128,256]{1,0:T(8,128)(2,1)S(1)}, u32[]{:S(2)}, u32[]{:S(2)}) collective-permute-start(bf16[128,256]{1,0:T(8,128)(2,1)S(1)} %get-tuple-element.45._), channel_id=1, source_target_pairs={{0,1},{1,0},{2,3},{3,2},{4,5},{5,4},{6,7},{7,6},{8,9},{9,8},{10,11... | collective-permute-start | bytes 196616 | tf_op jit(solution)/shard_map/ppermute | solution.py:491
  6.8 5.6 %collective-permute-start.1 = (bf16[2,8,4,256]{3,2,1,0:T(4,128)(2,1)S(1)}, bf16[2,8,4,256]{3,2,1,0:T(4,128)(2,1)S(1)}, u32[]{:S(2)}, u32[]{:S(2)}) collective-permute-start(bf16[2,8,4,256]{3,2,1,0:T(4,128)(2,1)S(1)} %get-tuple-element.51), channel_id=1, source_target_pairs={{0,30},{2,0},{4,2},{6,4},{8,6},{10,8},{12,10},{14,12},{16,14},{18,... | collective-permute-start | bytes 98312 | tf_op jit(solution)/shard_map/ppermute | solution.py:486
  12.1 1.0 %copy-start.2 = (bf16[16,8,4,256]{3,2,1,0:T(4,128)(2,1)S(1)}, bf16[16,8,4,256]{3,2,1,0:T(4,128)(2,1)}, u32[]{:S(2)}) copy-start(bf16[16,8,4,256]{3,2,1,0:T(4,128)(2,1)} %cot_ref.3) | copy-start | bytes 786436
  12.2 1.1 %copy-start.4 = (bf16[2,2,256,256]{3,2,1,0:T(8,128)(2,1)S(1)}, bf16[2,2,256,256]{3,2,1,0:T(8,128)(2,1)}, u32[]{:S(2)}) copy-start(bf16[2,2,256,256]{3,2,1,0:T(8,128)(2,1)} %param.10) | copy-start | bytes 1572868
  12.2 1.2 %copy-start.5 = (bf16[3,256,256]{2,1,0:T(8,128)(2,1)S(1)}, bf16[3,256,256]{2,1,0:T(8,128)(2,1)}, u32[]{:S(2)}) copy-start(bf16[3,256,256]{2,1,0:T(8,128)(2,1)} %wt_ref.5) | copy-start | bytes 1179652
  12.3 7.3 %collective-permute-start.3 = (bf16[288,256]{1,0:T(8,128)(2,1)S(1)}, bf16[288,256]{1,0:T(8,128)(2,1)S(1)}, u32[]{:S(2)}, u32[]{:S(2)}) collective-permute-start(bf16[288,256]{1,0:T(8,128)(2,1)S(1)} %get-tuple-element.56), channel_id=1, source_target_pairs={{0,2},{2,4},{4,6},{6,8},{8,10},{10,12},{12,14},{14,16},{16,18},{18... | collective-permute-start | bytes 442376 | tf_op jit(solution)/shard_map/ppermute | solution.py:486
  13.4 6.2 %copy-start.3 = (bf16[3,3,256,256]{3,2,1,0:T(8,128)(2,1)S(1)}, bf16[3,3,256,256]{3,2,1,0:T(8,128)(2,1)}, u32[]{:S(2)}) copy-start(bf16[3,3,256,256]{3,2,1,0:T(8,128)(2,1)} %param.8) | copy-start | bytes 3538948
  19.6 3.6 %collective-permute-start.4 = (bf16[16,9,16,128]{3,2,1,0:T(8,128)(2,1)S(1)}, bf16[16,9,16,128]{3,2,1,0:T(8,128)(2,1)S(1)}, u32[]{:S(2)}, u32[]{:S(2)}) collective-permute-start(bf16[16,9,16,128]{3,2,1,0:T(8,128)(2,1)S(1)} %pass.2._), channel_id=1, source_target_pairs={{0,2},{1,3},{2,0},{3,1},{4,6},{5,7},{6,4},{7,5},{8,10},{9,11},{10,... | collective-permute-start | bytes 1769480 | tf_op jit(solution)/shard_map/ppermute | solution.py:437
  23.4 6.3 %collective-permute-start.7 = (bf16[4,9,16,128]{3,2,1,0:T(8,128)(2,1)S(1)}, bf16[4,9,16,128]{3,2,1,0:T(8,128)(2,1)S(1)}, u32[]{:S(2)}, u32[]{:S(2)}) collective-permute-start(bf16[4,9,16,128]{3,2,1,0:T(8,128)(2,1)S(1)} %get-tuple-element.64.rest_3_), channel_id=1, source_target_pairs={{0,4},{1,5},{2,6},{3,7},{4,0},{5,1},{6,2},{7,3},{8,12},{9,13},{10,... | collective-permute-start | bytes 442376 | tf_op jit(solution)/shard_map/ppermute | solution.py:437
  29.7 1.8 %collective-permute-start.8 = (bf16[16,7,16,128]{3,2,1,0:T(8,128)(2,1)S(1)}, bf16[16,7,16,128]{3,2,1,0:T(8,128)(2,1)S(1)}, u32[]{:S(2)}, u32[]{:S(2)}) collective-permute-start(bf16[16,7,16,128]{3,2,1,0:T(8,128)(2,1)S(1)} %pass.3), channel_id=1, source_target_pairs={{0,2},{1,3},{2,0},{3,1},{4,6},{5,7},{6,4},{7,5},{8,10},{9,11},{10,... | collective-permute-start | bytes 1376264 | tf_op jit(solution)/shard_map/ppermute | solution.py:437
  29.7 7.6 %collective-permute-start.5 = (bf16[4,9,16,128]{3,2,1,0:T(8,128)(2,1)S(1)}, bf16[4,9,16,128]{3,2,1,0:T(8,128)(2,1)S(1)}, u32[]{:S(2)}, u32[]{:S(2)}) collective-permute-start(bf16[4,9,16,128]{3,2,1,0:T(8,128)(2,1)S(1)} %get-tuple-element.62.rest_1_), channel_id=1, source_target_pairs={{0,5},{1,4},{2,7},{3,6},{4,1},{5,0},{6,3},{7,2},{8,13},{9,12},{10,... | collective-permute-start | bytes 442376 | tf_op jit(solution)/shard_map/ppermute | solution.py:437
  29.9 12.3 %collective-permute-start.6 = (bf16[4,9,16,128]{3,2,1,0:T(8,128)(2,1)S(1)}, bf16[4,9,16,128]{3,2,1,0:T(8,128)(2,1)S(1)}, u32[]{:S(2)}, u32[]{:S(2)}) collective-permute-start(bf16[4,9,16,128]{3,2,1,0:T(8,128)(2,1)S(1)} %get-tuple-element.63.rest_2_), channel_id=1, source_target_pairs={{0,1},{1,0},{2,3},{3,2},{4,5},{5,4},{6,7},{7,6},{8,9},{9,8},{10,11... | collective-permute-start | bytes 442376 | tf_op jit(solution)/shard_map/ppermute | solution.py:437
  31.6 10.6 %collective-permute-start.9 = (bf16[4,7,16,128]{3,2,1,0:T(8,128)(2,1)S(1)}, bf16[4,7,16,128]{3,2,1,0:T(8,128)(2,1)S(1)}, u32[]{:S(2)}, u32[]{:S(2)}) collective-permute-start(bf16[4,7,16,128]{3,2,1,0:T(8,128)(2,1)S(1)} %get-tuple-element.69), channel_id=1, source_target_pairs={{0,5},{1,4},{2,7},{3,6},{4,1},{5,0},{6,3},{7,2},{8,13},{9,12},{10,... | collective-permute-start | bytes 344072 | tf_op jit(solution)/shard_map/ppermute | solution.py:437
  33.3 10.7 %collective-permute-start.10 = (bf16[4,7,16,128]{3,2,1,0:T(8,128)(2,1)S(1)}, bf16[4,7,16,128]{3,2,1,0:T(8,128)(2,1)S(1)}, u32[]{:S(2)}, u32[]{:S(2)}) collective-permute-start(bf16[4,7,16,128]{3,2,1,0:T(8,128)(2,1)S(1)} %get-tuple-element.70), channel_id=1, source_target_pairs={{0,1},{1,0},{2,3},{3,2},{4,5},{5,4},{6,7},{7,6},{8,9},{9,8},{10,11... | collective-permute-start | bytes 344072 | tf_op jit(solution)/shard_map/ppermute | solution.py:437
  34.8 9.2 %collective-permute-start.11 = (bf16[4,7,16,128]{3,2,1,0:T(8,128)(2,1)S(1)}, bf16[4,7,16,128]{3,2,1,0:T(8,128)(2,1)S(1)}, u32[]{:S(2)}, u32[]{:S(2)}) collective-permute-start(bf16[4,7,16,128]{3,2,1,0:T(8,128)(2,1)S(1)} %get-tuple-element.71), channel_id=1, source_target_pairs={{0,4},{1,5},{2,6},{3,7},{4,0},{5,1},{6,2},{7,3},{8,12},{9,13},{10,... | collective-permute-start | bytes 344072 | tf_op jit(solution)/shard_map/ppermute | solution.py:437
  44.2 8.4 %collective-permute-start.12 = (bf16[16,16,128]{2,1,0:T(8,128)(2,1)S(1)}, bf16[16,16,128]{2,1,0:T(8,128)(2,1)S(1)}, u32[]{:S(2)}, u32[]{:S(2)}) collective-permute-start(bf16[16,16,128]{2,1,0:T(8,128)(2,1)S(1)} %get-tuple-element.73), channel_id=1, source_target_pairs={{0,24},{1,25},{2,26},{3,27},{4,28},{5,29},{6,30},{7,31},{8,16},{9,... | collective-permute-start | bytes 196616 | tf_op jit(solution)/shard_map/ppermute | solution.py:437
  45.7 6.8 %collective-permute-start.13 = (bf16[16,16,128]{2,1,0:T(8,128)(2,1)S(1)}, bf16[16,16,128]{2,1,0:T(8,128)(2,1)S(1)}, u32[]{:S(2)}, u32[]{:S(2)}) collective-permute-start(bf16[16,16,128]{2,1,0:T(8,128)(2,1)S(1)} %get-tuple-element.74), channel_id=1, source_target_pairs={{0,16},{1,17},{2,18},{3,19},{4,20},{5,21},{6,22},{7,23},{8,24},{9,... | collective-permute-start | bytes 196616 | tf_op jit(solution)/shard_map/ppermute | solution.py:437
  45.7 6.8 %collective-permute-start.14 = (bf16[16,16,128]{2,1,0:T(8,128)(2,1)S(1)}, bf16[16,16,128]{2,1,0:T(8,128)(2,1)S(1)}, u32[]{:S(2)}, u32[]{:S(2)}) collective-permute-start(bf16[16,16,128]{2,1,0:T(8,128)(2,1)S(1)} %get-tuple-element.75), channel_id=1, source_target_pairs={{0,8},{1,9},{2,10},{3,11},{4,12},{5,13},{6,14},{7,15},{8,0},{9,1},... | collective-permute-start | bytes 196616 | tf_op jit(solution)/shard_map/ppermute | solution.py:437
  48.6 3.9 %collective-permute-start.2 = (bf16[64,256]{1,0:T(8,128)(2,1)S(1)}, bf16[64,256]{1,0:T(8,128)(2,1)S(1)}, u32[]{:S(2)}, u32[]{:S(2)}) collective-permute-start(bf16[64,256]{1,0:T(8,128)(2,1)S(1)} %get-tuple-element.54), channel_id=1, source_target_pairs={{0,1},{1,0},{2,3},{3,2},{4,5},{5,4},{6,7},{7,6},{8,9},{9,8},{10,11... | collective-permute-start | bytes 98312 | tf_op jit(solution)/shard_map/ppermute | solution.py:491
  52.6 4.8 %collective-permute-start.17 = (bf16[16,16,128]{2,1,0:T(8,128)(2,1)S(1)}, bf16[16,16,128]{2,1,0:T(8,128)(2,1)S(1)}, u32[]{:S(2)}, u32[]{:S(2)}) collective-permute-start(bf16[16,16,128]{2,1,0:T(8,128)(2,1)S(1)} %line_sum.1.a_ref), channel_id=1, source_target_pairs={{0,8},{1,9},{2,10},{3,11},{4,12},{5,13},{6,14},{7,15},{8,0},{9,1},... | collective-permute-start | bytes 196616 | tf_op jit(solution)/shard_map/ppermute | solution.py:437
  53.0 7.2 %collective-permute-start.16 = (bf16[16,16,128]{2,1,0:T(8,128)(2,1)S(1)}, bf16[16,16,128]{2,1,0:T(8,128)(2,1)S(1)}, u32[]{:S(2)}, u32[]{:S(2)}) collective-permute-start(bf16[16,16,128]{2,1,0:T(8,128)(2,1)S(1)} %line_sum.1.a_ref), channel_id=1, source_target_pairs={{0,16},{1,17},{2,18},{3,19},{4,20},{5,21},{6,22},{7,23},{8,24},{9,... | collective-permute-start | bytes 196616 | tf_op jit(solution)/shard_map/ppermute | solution.py:437
  55.0 6.1 %collective-permute-start.15 = (bf16[16,16,128]{2,1,0:T(8,128)(2,1)S(1)}, bf16[16,16,128]{2,1,0:T(8,128)(2,1)S(1)}, u32[]{:S(2)}, u32[]{:S(2)}) collective-permute-start(bf16[16,16,128]{2,1,0:T(8,128)(2,1)S(1)} %line_sum.1.a_ref), channel_id=1, source_target_pairs={{0,24},{1,25},{2,26},{3,27},{4,28},{5,29},{6,30},{7,31},{8,16},{9,... | collective-permute-start | bytes 196616 | tf_op jit(solution)/shard_map/ppermute | solution.py:437
  61.2 11.0 %collective-permute-start.20 = (bf16[4,16,16,128]{3,2,1,0:T(8,128)(2,1)S(1)}, bf16[4,16,16,128]{3,2,1,0:T(8,128)(2,1)S(1)}, u32[]{:S(2)}, u32[]{:S(2)}) collective-permute-start(bf16[4,16,16,128]{3,2,1,0:T(8,128)(2,1)S(1)} %line_gather.1.rest_0_.a_ref), channel_id=1, source_target_pairs={{0,4},{1,5},{2,6},{3,7},{4,0},{5,1},{6,2},{7,3},{8,12},{9,13},{10,... | collective-permute-start | bytes 786440 | tf_op jit(solution)/shard_map/ppermute | solution.py:437
  62.0 11.9 %collective-permute-start.19 = (bf16[4,16,16,128]{3,2,1,0:T(8,128)(2,1)S(1)}, bf16[4,16,16,128]{3,2,1,0:T(8,128)(2,1)S(1)}, u32[]{:S(2)}, u32[]{:S(2)}) collective-permute-start(bf16[4,16,16,128]{3,2,1,0:T(8,128)(2,1)S(1)} %line_gather.1.rest_0_.a_ref), channel_id=1, source_target_pairs={{0,1},{1,0},{2,3},{3,2},{4,5},{5,4},{6,7},{7,6},{8,9},{9,8},{10,11... | collective-permute-start | bytes 786440 | tf_op jit(solution)/shard_map/ppermute | solution.py:437
  63.5 10.4 %collective-permute-start.18 = (bf16[4,16,16,128]{3,2,1,0:T(8,128)(2,1)S(1)}, bf16[4,16,16,128]{3,2,1,0:T(8,128)(2,1)S(1)}, u32[]{:S(2)}, u32[]{:S(2)}) collective-permute-start(bf16[4,16,16,128]{3,2,1,0:T(8,128)(2,1)S(1)} %line_gather.1.rest_0_.a_ref), channel_id=1, source_target_pairs={{0,5},{1,4},{2,7},{3,6},{4,1},{5,0},{6,3},{7,2},{8,13},{9,12},{10,... | collective-permute-start | bytes 786440 | tf_op jit(solution)/shard_map/ppermute | solution.py:437
  74.0 2.7 %collective-permute-start.21 = (bf16[16,16,16,128]{3,2,1,0:T(8,128)(2,1)S(1)}, bf16[16,16,16,128]{3,2,1,0:T(8,128)(2,1)S(1)}, u32[]{:S(2)}, u32[]{:S(2)}) collective-permute-start(bf16[16,16,16,128]{3,2,1,0:T(8,128)(2,1)S(1)} %plane_gather.1.half_ref), channel_id=1, source_target_pairs={{0,2},{1,3},{2,0},{3,1},{4,6},{5,7},{6,4},{7,5},{8,10},{9,11},{10,... | collective-permute-start | bytes 3145736 | tf_op jit(solution)/shard_map/ppermute | solution.py:437

commit v15 on v14

--- a/solution.py
+++ b/solution.py
@@ -406,10 +406,11 @@
 TOKEN = (VMEM, (8, 128), F32)
 
 
-def call(kernel, name, ins, outs, scratch=(), flops=0, alias=None, grant=10):
+def call(kernel, name, ins, outs, scratch=(), flops=0, alias=None, grant=10, moved=None):
     shapes = [jax.ShapeDtypeStruct(o[1], o[2] if len(o) > 2 else BF) for o in outs]
-    moved = sum(a.size * a.dtype.itemsize for s, a in ins if s is not ANY)
-    moved += sum(s.size * s.dtype.itemsize for s in shapes)
+    if moved is None:
+        moved = sum(a.size * a.dtype.itemsize for s, a in ins if s is not ANY)
+        moved += sum(s.size * s.dtype.itemsize for s in shapes)
     return pl.pallas_call(
         kernel,
         out_shape=shapes,
@@ -528,10 +529,11 @@
     acts, at, last_two = call(
         functools.partial(halo_kernel, grp),
         "halo",
-        [count, (VMEM, top), (VMEM, bot), (VMEM, acts), (VMEM, at), (VMEM, last_two)],
+        [count, (VMEM, top), (VMEM, bot), (VMEM, acts), (VMEM, at), (VMEM, last_two),
+         (VMEM, cotangent), (VMEM, wt), (VMEM, wd)],
         [(VMEM, padded), (VMEM, at_shape), (VMEM, last_shape)],
-        flops=tap // 8,
         alias={3: 0, 4: 1, 5: 2},
+        moved=1024,
     )
     prev = around(last_two, "tm", 1)
     half = (16, 9, 16, ch // 2)
@@ -569,7 +571,7 @@
         grant=14,
     )
     parts_a = four_round(parts_a, plane, tm, grp)
-    send_b = passed(send_b, parts_a[3:4])
+    send_b = passed(send_b, parts_a[1:2])
     parts_b = plane_send(keep_b, core_round(send_b, tm, grp), [])
     parts_b = four_round(parts_b, plane, tm, grp)
     parts = call(
@@ -579,7 +581,7 @@
         [(VMEM, (16, 16, ch // 2))] * 4,
     )
     parts = four_round(list(parts), line, tm, grp)
-    ins = [(VMEM, a) for a in parts] + [(ANY, a) for a in [cot_top, cot_bot][:sides]]
+    ins = [(VMEM, a) for a in parts]
     (mine,) = call(line_sum_kernel, "line_sum", ins, [(VMEM, parts[0].shape)])
     for bit in others:
         got = swap(mine, tm, grp, bit)

time: 78.4 us -> 76.2 us (0.972)
  local copies, waits for them, and re-layouts: 3.2 us -> 2.18 us
    ppermute x2, waiting for transfers between devices: 2.52 us -> 0.01 us  [from_bands(): got = lax.ppermute(parts[0], 'grp', [(0, 1), (1, 0)])]
    unnamed x12, local copies, waits for them, and re-layouts: 3.2 us -> 2.18 us
    ppermute x18, waiting for transfers between devices: 19.4 us -> 20.4 us  [swap(): return lax.ppermute(value, AXES, [(d, d ^ flip) for d in range(tm * grp)])]
    ppermute x2, waiting for transfers between devices: 1.7 us -> 2.7 us  [around(): lax.ppermute(value, axis, [(i, (i + by) % count) for i in range(count)])]
    ppermute x18, starting transfers between devices: 17.9 us -> 17 us  [swap(): return lax.ppermute(value, AXES, [(d, d ^ flip) for d in range(tm * grp)])]
  transfers between devices with their start and end apart: 22 -> 22, of which waited for: 12 -> 14; matrix products, arithmetic and copies ran while one was open for 0% -> 0% of each run, Pallas kernels for 28% -> 29%
where the time goes in v15:
time: 76.2 us; the launch traced here: 76 us
  starting transfers between devices  25.4 us (33%)
  Pallas kernels  23.9 us (31%)
  waiting for transfers between devices  23.1 us (30%)
  local copies, waits for them, and re-layouts  2.18 us (3%)
  between operations  1.48 us (2%)
    pallas_call x17, Pallas kernels, call(): pl.pallas_call(kernel, out_shape=shapes, in_specs=[s for s, _ in ins], ou...  23.9 us
    ppermute x18, waiting for transfers between devices, swap(): return lax.ppermute(value, AXES, [(d, d ^ flip) for d in range(tm * grp)])  20.4 us
    ppermute x18, starting transfers between devices, swap(): return lax.ppermute(value, AXES, [(d, d ^ flip) for d in range(tm * grp)])  17 us
    ppermute x2, starting transfers between devices, from_bands(): got = lax.ppermute(parts[0], 'grp', [(0, 1), (1, 0)])  4.67 us
    ppermute x2, starting transfers between devices, around(): lax.ppermute(value, axis, [(i, (i + by) % count) for i in range(count)])  3.69 us
    ppermute x2, waiting for transfers between devices, around(): lax.ppermute(value, axis, [(i, (i + by) % count) for i in range(count)])  2.7 us
    unnamed x12, local copies, waits for them, and re-layouts  2.18 us
  transfers between devices with their start and end apart: 22, of which 14 were waited for; matrix products, arithmetic and copies ran while one was open for 0% of the time, Pallas kernels for 29%

profile of v15, /device:TPU:0, one launch (start us, length us, event | category | flops | bytes accessed | tf_op | source)
XLA Modules:
  0.0 76.0 jit_solution(3172538761737100099)
XLA Ops:
  1.3 0.9 %copy-done = bf16[16,8,4,256]{3,2,1,0:T(4,128)(2,1)S(1)} copy-done((bf16[16,8,4,256]{3,2,1,0:T(4,128)(2,1)S(1)}, bf16[16,8,4,256]{3,2,1,0:T(4,128)(2,1)}, u32[]{:S(2)}) %copy-start) | copy-done | bytes 262168
  2.2 1.2 %copy-done.2 = bf16[16,16,8,256]{3,2,1,0:T(8,128)(2,1)S(1)} copy-done((bf16[16,16,8,256]{3,2,1,0:T(8,128)(2,1)S(1)}, bf16[16,16,8,256]{3,2,1,0:T(8,128)(2,1)}, u32[]{:S(2)}) %copy-start.2) | copy-done | bytes 1048600
  3.5 0.3 edges.1
  3.8 3.0 %collective-permute-start = (bf16[128,256]{1,0:T(8,128)(2,1)S(1)}, bf16[128,256]{1,0:T(8,128)(2,1)S(1)}, u32[]{:S(2)}, u32[]{:S(2)}) collective-permute-start(bf16[128,256]{1,0:T(8,128)(2,1)S(1)} %get-tuple-element.45._), channel_id=1, source_target_pairs={{0,1},{1,0},{2,3},{3,2},{4,5},{5,4},{6,7},{7,6},{8,9},{9,8},{10,11... | collective-permute-start | bytes 196616 | tf_op jit(solution)/shard_map/ppermute | solution.py:492
  6.8 3.7 %collective-permute-start.1 = (bf16[2,8,4,256]{3,2,1,0:T(4,128)(2,1)S(1)}, bf16[2,8,4,256]{3,2,1,0:T(4,128)(2,1)S(1)}, u32[]{:S(2)}, u32[]{:S(2)}) collective-permute-start(bf16[2,8,4,256]{3,2,1,0:T(4,128)(2,1)S(1)} %get-tuple-element.51), channel_id=1, source_target_pairs={{0,30},{2,0},{4,2},{6,4},{8,6},{10,8},{12,10},{14,12},{16,14},{18,... | collective-permute-start | bytes 98312 | tf_op jit(solution)/shard_map/ppermute | solution.py:487
  10.5 1.6 %acts.1 = (bf16[16,8,16,256]{3,2,1,0:T(8,128)(2,1)S(1)}, bf16[18,10,16,256]{3,2,1,0:T(8,128)(2,1)S(1)}, bf16[768,2560]{1,0:T(8,128)(2,1)S(1)}, bf16[288,256]{1,0:T(8,128)(2,1)S(1)}) custom-call(s32[1]{0:T(128)S(6)} %copy.29.count_ref, bf16[16,128,256]{2,1,0:T(8,128)(2,1)S(1)} %bitcast.7, bf16[128,256]{1,0:T(8,128)(2,1)S(1)} %get-tuple-element.45._), custom_call_target="tpu_custom_call" | custom-call | flops 536870912 | bytes 7651332 | tf_op jit(solution)/shard_map/acts/pallas_call | solution.py:414
  12.2 0.2 halo.1
  12.3 0.0 collective-permute-start.3
  12.4 4.5 %grad_spatial.1 = (bf16[8,4,16,256]{3,2,1,0:T(8,128)(2,1)S(1)}, bf16[16,8,16,256]{3,2,1,0:T(8,128)(2,1)S(1)}, bf16[16,10,16,256]{3,2,1,0:T(8,128)(2,1)S(1)}, bf1...) custom-call(s32[1]{0:T(128)S(6)} %copy.29.count_ref, ...), custom_call_target="tpu_custom_call" | custom-call | flops 3758096384 | bytes 8978436 | tf_op jit(solution)/shard_map/grad_spatial/pallas_call | solution.py:414
  16.9 2.7 %collective-permute-done.3.__1_.prev_ref = bf16[288,256]{1,0:T(8,128)(2,1)S(1)} collective-permute-done((bf16[288,256]{1,0:T(8,128)(2,1)S(1)}, bf16[288,256]{1,0:T(8,128)(2,1)S(1)}, u32[]{:S(2)}, u32[]{:S(2)}) %collective-permute-start.3) | collective-permute-done | bytes 147488 | tf_op jit(solution)/shard_map/ppermute | solution.py:487
  19.6 3.6 %spatial.1 = (bf16[18,10,16,256]{3,2,1,0:T(8,128)(2,1)S(1)}, bf16[16,8,16,256]{3,2,1,0:T(8,128)(2,1)S(1)}) custom-call(s32[1]{0:T(128)S(6)} %copy.29.count_ref, bf16[18,10,16,256]{3,2,1,0:T(8,128)(2,1)S(1)} %get-tuple-element.55.acts_in, bf16[288,256]{1,0:T(8,128)(2,1)S(1)} %collective-permute-done.3.__1_.prev_ref, ...), custom_call_target="tpu_custom_call", output_to_operand_aliasing={{0}: (1, {})} | custom-call | flops 2415919104 | bytes 5324804 | tf_op jit(solution)/shard_map/spatial/pallas_call | solution.py:414
  23.2 0.2 plane_send.2
  23.4 0.1 collective-permute-start.5
  23.4 2.8 %forward.1 = (bf16[512,256]{1,0:T(8,128)(2,1)S(1)}, bf16[16,7,16,128]{3,2,1,0:T(8,128)(2,1)S(1)}, bf16[16,7,16,128]{3,2,1,0:T(8,128)(2,1)S(1)}) custom-call(s32[1]{0:T(128)S(6)} %copy.29.count_ref, bf16[16,8,16,256]{3,2,1,0:T(8,128)(2,1)S(1)} %get-tuple-element.46.xt_ref, bf16[16,8,16,256]{3,2,1,0:T(8,128)(2,1)S(1)} %get-tuple-element.58.rest_0_.sp_ref, ...), custom_call_target="tpu_custom_call" | custom-call | flops 2684354560 | bytes 5505028 | tf_op jit(solution)/shard_map/forward/pallas_call | solution.py:414
  26.3 4.3 %collective-permute-done.5.__1_.refs_1_ = bf16[4,9,16,128]{3,2,1,0:T(8,128)(2,1)S(1)} collective-permute-done((bf16[4,9,16,128]{3,2,1,0:T(8,128)(2,1)S(1)}, bf16[4,9,16,128]{3,2,1,0:T(8,128)(2,1)S(1)}, u32[]{:S(2)}, u32[]{:S(2)}) %collective-permute-start.5) | collective-permute-done | bytes 147488 | tf_op jit(solution)/shard_map/ppermute | solution.py:438
  30.6 0.5 collective-permute-start.6
  31.1 0.3 collective-permute-start.7
  31.4 1.0 %collective-permute-done.8.got_ref = bf16[16,7,16,128]{3,2,1,0:T(8,128)(2,1)S(1)} collective-permute-done((bf16[16,7,16,128]{3,2,1,0:T(8,128)(2,1)S(1)}, bf16[16,7,16,128]{3,2,1,0:T(8,128)(2,1)S(1)}, u32[]{:S(2)}, u32[]{:S(2)}) %collective-permute-start.8) | collective-permute-done | bytes 458784 | tf_op jit(solution)/shard_map/ppermute | solution.py:438
  32.4 0.1 plane_send.3
  32.5 1.7 %collective-permute-start.9 = (bf16[4,7,16,128]{3,2,1,0:T(8,128)(2,1)S(1)}, bf16[4,7,16,128]{3,2,1,0:T(8,128)(2,1)S(1)}, u32[]{:S(2)}, u32[]{:S(2)}) collective-permute-start(bf16[4,7,16,128]{3,2,1,0:T(8,128)(2,1)S(1)} %get-tuple-element.69), channel_id=1, source_target_pairs={{0,5},{1,4},{2,7},{3,6},{4,1},{5,0},{6,3},{7,2},{8,13},{9,12},{10,... | collective-permute-start | bytes 344072 | tf_op jit(solution)/shard_map/ppermute | solution.py:438
  34.3 0.5 collective-permute-start.10
  34.8 1.3 %collective-permute-start.11 = (bf16[4,7,16,128]{3,2,1,0:T(8,128)(2,1)S(1)}, bf16[4,7,16,128]{3,2,1,0:T(8,128)(2,1)S(1)}, u32[]{:S(2)}, u32[]{:S(2)}) collective-permute-start(bf16[4,7,16,128]{3,2,1,0:T(8,128)(2,1)S(1)} %get-tuple-element.71), channel_id=1, source_target_pairs={{0,4},{1,5},{2,6},{3,7},{4,0},{5,1},{6,2},{7,3},{8,12},{9,13},{10,... | collective-permute-start | bytes 344072 | tf_op jit(solution)/shard_map/ppermute | solution.py:438
  36.1 1.0 %collective-permute-done.6.refs_2_ = bf16[4,9,16,128]{3,2,1,0:T(8,128)(2,1)S(1)} collective-permute-done((bf16[4,9,16,128]{3,2,1,0:T(8,128)(2,1)S(1)}, bf16[4,9,16,128]{3,2,1,0:T(8,128)(2,1)S(1)}, u32[]{:S(2)}, u32[]{:S(2)}) %collective-permute-start.6) | collective-permute-done | bytes 147488 | tf_op jit(solution)/shard_map/ppermute | solution.py:438
  37.1 0.7 collective-permute-done.7.refs_3_
  37.8 3.5 %collective-permute-done.9.refs_5_ = bf16[4,7,16,128]{3,2,1,0:T(8,128)(2,1)S(1)} collective-permute-done((bf16[4,7,16,128]{3,2,1,0:T(8,128)(2,1)S(1)}, bf16[4,7,16,128]{3,2,1,0:T(8,128)(2,1)S(1)}, u32[]{:S(2)}, u32[]{:S(2)}) %collective-permute-start.9) | collective-permute-done | bytes 114720 | tf_op jit(solution)/shard_map/ppermute | solution.py:438
  41.2 0.5 collective-permute-done.10.refs_6_
  41.8 0.3 collective-permute-done.11.refs_7_
  42.0 0.1 line_send.1
  42.2 0.7 collective-permute-start.12
  42.8 3.8 %collective-permute-start.14 = (bf16[16,16,128]{2,1,0:T(8,128)(2,1)S(1)}, bf16[16,16,128]{2,1,0:T(8,128)(2,1)S(1)}, u32[]{:S(2)}, u32[]{:S(2)}) collective-permute-start(bf16[16,16,128]{2,1,0:T(8,128)(2,1)S(1)} %get-tuple-element.75), channel_id=1, source_target_pairs={{0,8},{1,9},{2,10},{3,11},{4,12},{5,13},{6,14},{7,15},{8,0},{9,1},... | collective-permute-start | bytes 196616 | tf_op jit(solution)/shard_map/ppermute | solution.py:438
  46.6 2.3 %collective-permute-done.12.b_ref = bf16[16,16,128]{2,1,0:T(8,128)(2,1)S(1)} collective-permute-done((bf16[16,16,128]{2,1,0:T(8,128)(2,1)S(1)}, bf16[16,16,128]{2,1,0:T(8,128)(2,1)S(1)}, u32[]{:S(2)}, u32[]{:S(2)}) %collective-permute-start.12) | collective-permute-done | bytes 65568 | tf_op jit(solution)/shard_map/ppermute | solution.py:438
  49.0 0.8 %collective-permute-done.13.c_ref = bf16[16,16,128]{2,1,0:T(8,128)(2,1)S(1)} collective-permute-done((bf16[16,16,128]{2,1,0:T(8,128)(2,1)S(1)}, bf16[16,16,128]{2,1,0:T(8,128)(2,1)S(1)}, u32[]{:S(2)}, u32[]{:S(2)}) %collective-permute-start.13) | collective-permute-done | bytes 65568 | tf_op jit(solution)/shard_map/ppermute | solution.py:438
  49.8 1.1 %collective-permute-start.17 = (bf16[16,16,128]{2,1,0:T(8,128)(2,1)S(1)}, bf16[16,16,128]{2,1,0:T(8,128)(2,1)S(1)}, u32[]{:S(2)}, u32[]{:S(2)}) collective-permute-start(bf16[16,16,128]{2,1,0:T(8,128)(2,1)S(1)} %line_sum.1.a_ref), channel_id=1, source_target_pairs={{0,8},{1,9},{2,10},{3,11},{4,12},{5,13},{6,14},{7,15},{8,0},{9,1},... | collective-permute-start | bytes 196616 | tf_op jit(solution)/shard_map/ppermute | solution.py:438
  51.0 1.4 %collective-permute-start.16 = (bf16[16,16,128]{2,1,0:T(8,128)(2,1)S(1)}, bf16[16,16,128]{2,1,0:T(8,128)(2,1)S(1)}, u32[]{:S(2)}, u32[]{:S(2)}) collective-permute-start(bf16[16,16,128]{2,1,0:T(8,128)(2,1)S(1)} %line_sum.1.a_ref), channel_id=1, source_target_pairs={{0,16},{1,17},{2,18},{3,19},{4,20},{5,21},{6,22},{7,23},{8,24},{9,... | collective-permute-start | bytes 196616 | tf_op jit(solution)/shard_map/ppermute | solution.py:438
  52.4 1.9 %collective-permute-start.15 = (bf16[16,16,128]{2,1,0:T(8,128)(2,1)S(1)}, bf16[16,16,128]{2,1,0:T(8,128)(2,1)S(1)}, u32[]{:S(2)}, u32[]{:S(2)}) collective-permute-start(bf16[16,16,128]{2,1,0:T(8,128)(2,1)S(1)} %line_sum.1.a_ref), channel_id=1, source_target_pairs={{0,24},{1,25},{2,26},{3,27},{4,28},{5,29},{6,30},{7,31},{8,16},{9,... | collective-permute-start | bytes 196616 | tf_op jit(solution)/shard_map/ppermute | solution.py:438
  54.3 1.6 %collective-permute-start.2 = (bf16[64,256]{1,0:T(8,128)(2,1)S(1)}, bf16[64,256]{1,0:T(8,128)(2,1)S(1)}, u32[]{:S(2)}, u32[]{:S(2)}) collective-permute-start(bf16[64,256]{1,0:T(8,128)(2,1)S(1)} %get-tuple-element.54), channel_id=1, source_target_pairs={{0,1},{1,0},{2,3},{3,2},{4,5},{5,4},{6,7},{7,6},{8,9},{9,8},{10,11... | collective-permute-start | bytes 98312 | tf_op jit(solution)/shard_map/ppermute | solution.py:492
  55.9 1.0 %collective-permute-done.16.c_ref = bf16[16,16,128]{2,1,0:T(8,128)(2,1)S(1)} collective-permute-done((bf16[16,16,128]{2,1,0:T(8,128)(2,1)S(1)}, bf16[16,16,128]{2,1,0:T(8,128)(2,1)S(1)}, u32[]{:S(2)}, u32[]{:S(2)}) %collective-permute-start.16) | collective-permute-done | bytes 65568 | tf_op jit(solution)/shard_map/ppermute | solution.py:438
  56.9 1.5 %collective-permute-done.15.b_ref = bf16[16,16,128]{2,1,0:T(8,128)(2,1)S(1)} collective-permute-done((bf16[16,16,128]{2,1,0:T(8,128)(2,1)S(1)}, bf16[16,16,128]{2,1,0:T(8,128)(2,1)S(1)}, u32[]{:S(2)}, u32[]{:S(2)}) %collective-permute-start.15) | collective-permute-done | bytes 65568 | tf_op jit(solution)/shard_map/ppermute | solution.py:438
  58.5 1.0 %collective-permute-start.20 = (bf16[4,16,16,128]{3,2,1,0:T(8,128)(2,1)S(1)}, bf16[4,16,16,128]{3,2,1,0:T(8,128)(2,1)S(1)}, u32[]{:S(2)}, u32[]{:S(2)}) collective-permute-start(bf16[4,16,16,128]{3,2,1,0:T(8,128)(2,1)S(1)} %line_gather.1.rest_0_.a_ref), channel_id=1, source_target_pairs={{0,4},{1,5},{2,6},{3,7},{4,0},{5,1},{6,2},{7,3},{8,12},{9,13},{10,... | collective-permute-start | bytes 786440 | tf_op jit(solution)/shard_map/ppermute | solution.py:438
  59.5 1.4 %collective-permute-start.19 = (bf16[4,16,16,128]{3,2,1,0:T(8,128)(2,1)S(1)}, bf16[4,16,16,128]{3,2,1,0:T(8,128)(2,1)S(1)}, u32[]{:S(2)}, u32[]{:S(2)}) collective-permute-start(bf16[4,16,16,128]{3,2,1,0:T(8,128)(2,1)S(1)} %line_gather.1.rest_0_.a_ref), channel_id=1, source_target_pairs={{0,1},{1,0},{2,3},{3,2},{4,5},{5,4},{6,7},{7,6},{8,9},{9,8},{10,11... | collective-permute-start | bytes 786440 | tf_op jit(solution)/shard_map/ppermute | solution.py:438
  60.9 1.1 %collective-permute-start.18 = (bf16[4,16,16,128]{3,2,1,0:T(8,128)(2,1)S(1)}, bf16[4,16,16,128]{3,2,1,0:T(8,128)(2,1)S(1)}, u32[]{:S(2)}, u32[]{:S(2)}) collective-permute-start(bf16[4,16,16,128]{3,2,1,0:T(8,128)(2,1)S(1)} %line_gather.1.rest_0_.a_ref), channel_id=1, source_target_pairs={{0,5},{1,4},{2,7},{3,6},{4,1},{5,0},{6,3},{7,2},{8,13},{9,12},{10,... | collective-permute-start | bytes 786440 | tf_op jit(solution)/shard_map/ppermute | solution.py:438
  62.0 7.4 %grad_x.1 = (bf16[16,128,256]{2,1,0:T(8,128)(2,1)}, bf16[16,8,4,256]{3,2,1,0:T(4,128)(2,1)}, f32[8,128]{1,0:T(8,128)S(1)}) custom-call(s32[1]{0:T(128)S(6)} %copy.29.count_ref, bf16[16,8,16,256]{3,2,1,0:T(8,128)(2,1)S(1)} %get-tuple-element.46.xt_ref, bf16[16,8,16,256]{3,2,1,0:T(8,128)(2,1)S(1)} %get-tuple-element.52.gy_ref, ...), custom_call_target="tpu_custom_call" | custom-call | flops 2684354560 | bytes 7147524 | tf_op jit(solution)/shard_map/grad_x/pallas_call | solution.py:414
  69.5 2.2 %collective-permute-done.19.c_ref = bf16[4,16,16,128]{3,2,1,0:T(8,128)(2,1)S(1)} collective-permute-done((bf16[4,16,16,128]{3,2,1,0:T(8,128)(2,1)S(1)}, bf16[4,16,16,128]{3,2,1,0:T(8,128)(2,1)S(1)}, u32[]{:S(2)}, u32[]{:S(2)}) %collective-permute-start.19) | collective-permute-done | bytes 262176 | tf_op jit(solution)/shard_map/ppermute | solution.py:438
  71.7 0.1 plane_gather.1.half_ref
  71.8 0.1 collective-permute-start.21
  71.9 1.5 %finish.2 = (f32[9,256,256]{2,1,0:T(8,128)}, f32[3,256,256]{2,1,0:T(8,128)}, f32[4,256,256]{2,1,0:T(8,128)}) custom-call(bf16[16,16,16,128]{3,2,1,0:T(8,128)(2,1)S(1)} %plane_gather.1.half_ref), custom_call_target="tpu_custom_call" | custom-call | bytes 5242880 | tf_op jit(solution)/shard_map/finish/pallas_call | solution.py:414
  73.4 1.2 %collective-permute-done.21.half_ref = bf16[16,16,16,128]{3,2,1,0:T(8,128)(2,1)S(1)} collective-permute-done((bf16[16,16,16,128]{3,2,1,0:T(8,128)(2,1)S(1)}, bf16[16,16,16,128]{3,2,1,0:T(8,128)(2,1)S(1)}, u32[]{:S(2)}, u32[]{:S(2)}) %collective-permute-start.21) | collective-permute-done | bytes 1048608 | tf_op jit(solution)/shard_map/ppermute | solution.py:438
  74.6 1.5 %finish.3 = (f32[9,256,256]{2,1,0:T(8,128)}, f32[3,256,256]{2,1,0:T(8,128)}, f32[4,256,256]{2,1,0:T(8,128)}) custom-call(bf16[16,16,16,128]{3,2,1,0:T(8,128)(2,1)S(1)} %collective-permute-done.21.half_ref, f32[9,256,256]{2,1,0:T(8,128)} %get-tuple-element.79.rest_0_, ...), custom_call_target="tpu_custom_call", output_to_operand_aliasing={{0}: (1, {}), {1}: (2, {}), {2}: (3, {})} | custom-call | bytes 9437184 | tf_op jit(solution)/shard_map/finish/pallas_call | solution.py:414
  (25 shorter events, 0.1 us)
Async XLA Ops:
  1.3 1.0 %copy-start = (bf16[16,8,4,256]{3,2,1,0:T(4,128)(2,1)S(1)}, bf16[16,8,4,256]{3,2,1,0:T(4,128)(2,1)}, u32[]{:S(2)}) copy-start(bf16[16,8,4,256]{3,2,1,0:T(4,128)(2,1)} %cot_ref.3) | copy-start | bytes 786436
  2.2 1.2 %copy-start.2 = (bf16[16,16,8,256]{3,2,1,0:T(8,128)(2,1)S(1)}, bf16[16,16,8,256]{3,2,1,0:T(8,128)(2,1)}, u32[]{:S(2)}) copy-start(bf16[16,16,8,256]{3,2,1,0:T(8,128)(2,1)} %param.6) | copy-start | bytes 3145732
  3.5 8.7 %copy-start.1 = (bf16[16,8,4,256]{3,2,1,0:T(4,128)(2,1)S(1)}, bf16[16,8,4,256]{3,2,1,0:T(4,128)(2,1)}, u32[]{:S(2)}) copy-start(bf16[16,8,4,256]{3,2,1,0:T(4,128)(2,1)} %cot_ref.3) | copy-start | bytes 786436
  3.5 8.7 %copy-start.3 = (bf16[2,2,256,256]{3,2,1,0:T(8,128)(2,1)S(1)}, bf16[2,2,256,256]{3,2,1,0:T(8,128)(2,1)}, u32[]{:S(2)}) copy-start(bf16[2,2,256,256]{3,2,1,0:T(8,128)(2,1)} %param.10) | copy-start | bytes 1572868
  3.5 8.7 %copy-start.4 = (bf16[3,256,256]{2,1,0:T(8,128)(2,1)S(1)}, bf16[3,256,256]{2,1,0:T(8,128)(2,1)}, u32[]{:S(2)}) copy-start(bf16[3,256,256]{2,1,0:T(8,128)(2,1)} %wt_ref.5) | copy-start | bytes 1179652
  3.8 8.4 %collective-permute-start = (bf16[128,256]{1,0:T(8,128)(2,1)S(1)}, bf16[128,256]{1,0:T(8,128)(2,1)S(1)}, u32[]{:S(2)}, u32[]{:S(2)}) collective-permute-start(bf16[128,256]{1,0:T(8,128)(2,1)S(1)} %get-tuple-element.45._), channel_id=1, source_target_pairs={{0,1},{1,0},{2,3},{3,2},{4,5},{5,4},{6,7},{7,6},{8,9},{9,8},{10,11... | collective-permute-start | bytes 196616 | tf_op jit(solution)/shard_map/ppermute | solution.py:492
  6.8 5.6 %collective-permute-start.1 = (bf16[2,8,4,256]{3,2,1,0:T(4,128)(2,1)S(1)}, bf16[2,8,4,256]{3,2,1,0:T(4,128)(2,1)S(1)}, u32[]{:S(2)}, u32[]{:S(2)}) collective-permute-start(bf16[2,8,4,256]{3,2,1,0:T(4,128)(2,1)S(1)} %get-tuple-element.51), channel_id=1, source_target_pairs={{0,30},{2,0},{4,2},{6,4},{8,6},{10,8},{12,10},{14,12},{16,14},{18,... | collective-permute-start | bytes 98312 | tf_op jit(solution)/shard_map/ppermute | solution.py:487
  12.3 7.3 %collective-permute-start.3 = (bf16[288,256]{1,0:T(8,128)(2,1)S(1)}, bf16[288,256]{1,0:T(8,128)(2,1)S(1)}, u32[]{:S(2)}, u32[]{:S(2)}) collective-permute-start(bf16[288,256]{1,0:T(8,128)(2,1)S(1)} %get-tuple-element.56), channel_id=1, source_target_pairs={{0,2},{2,4},{4,6},{6,8},{8,10},{10,12},{12,14},{14,16},{16,18},{18... | collective-permute-start | bytes 442376 | tf_op jit(solution)/shard_map/ppermute | solution.py:487
  12.4 7.2 %copy-start.5 = (bf16[3,3,256,256]{3,2,1,0:T(8,128)(2,1)S(1)}, bf16[3,3,256,256]{3,2,1,0:T(8,128)(2,1)}, u32[]{:S(2)}) copy-start(bf16[3,3,256,256]{3,2,1,0:T(8,128)(2,1)} %param.8) | copy-start | bytes 3538948
  19.6 3.6 %collective-permute-start.4 = (bf16[16,9,16,128]{3,2,1,0:T(8,128)(2,1)S(1)}, bf16[16,9,16,128]{3,2,1,0:T(8,128)(2,1)S(1)}, u32[]{:S(2)}, u32[]{:S(2)}) collective-permute-start(bf16[16,9,16,128]{3,2,1,0:T(8,128)(2,1)S(1)} %pass.2._), channel_id=1, source_target_pairs={{0,2},{1,3},{2,0},{3,1},{4,6},{5,7},{6,4},{7,5},{8,10},{9,11},{10,... | collective-permute-start | bytes 1769480 | tf_op jit(solution)/shard_map/ppermute | solution.py:438
  23.4 7.2 %collective-permute-start.5 = (bf16[4,9,16,128]{3,2,1,0:T(8,128)(2,1)S(1)}, bf16[4,9,16,128]{3,2,1,0:T(8,128)(2,1)S(1)}, u32[]{:S(2)}, u32[]{:S(2)}) collective-permute-start(bf16[4,9,16,128]{3,2,1,0:T(8,128)(2,1)S(1)} %get-tuple-element.62.rest_1_), channel_id=1, source_target_pairs={{0,5},{1,4},{2,7},{3,6},{4,1},{5,0},{6,3},{7,2},{8,13},{9,12},{10,... | collective-permute-start | bytes 442376 | tf_op jit(solution)/shard_map/ppermute | solution.py:438
  30.6 1.8 %collective-permute-start.8 = (bf16[16,7,16,128]{3,2,1,0:T(8,128)(2,1)S(1)}, bf16[16,7,16,128]{3,2,1,0:T(8,128)(2,1)S(1)}, u32[]{:S(2)}, u32[]{:S(2)}) collective-permute-start(bf16[16,7,16,128]{3,2,1,0:T(8,128)(2,1)S(1)} %pass.3), channel_id=1, source_target_pairs={{0,2},{1,3},{2,0},{3,1},{4,6},{5,7},{6,4},{7,5},{8,10},{9,11},{10,... | collective-permute-start | bytes 1376264 | tf_op jit(solution)/shard_map/ppermute | solution.py:438
  30.6 6.5 %collective-permute-start.6 = (bf16[4,9,16,128]{3,2,1,0:T(8,128)(2,1)S(1)}, bf16[4,9,16,128]{3,2,1,0:T(8,128)(2,1)S(1)}, u32[]{:S(2)}, u32[]{:S(2)}) collective-permute-start(bf16[4,9,16,128]{3,2,1,0:T(8,128)(2,1)S(1)} %get-tuple-element.63.rest_2_), channel_id=1, source_target_pairs={{0,1},{1,0},{2,3},{3,2},{4,5},{5,4},{6,7},{7,6},{8,9},{9,8},{10,11... | collective-permute-start | bytes 442376 | tf_op jit(solution)/shard_map/ppermute | solution.py:438
  31.1 6.7 %collective-permute-start.7 = (bf16[4,9,16,128]{3,2,1,0:T(8,128)(2,1)S(1)}, bf16[4,9,16,128]{3,2,1,0:T(8,128)(2,1)S(1)}, u32[]{:S(2)}, u32[]{:S(2)}) collective-permute-start(bf16[4,9,16,128]{3,2,1,0:T(8,128)(2,1)S(1)} %get-tuple-element.64.rest_3_), channel_id=1, source_target_pairs={{0,4},{1,5},{2,6},{3,7},{4,0},{5,1},{6,2},{7,3},{8,12},{9,13},{10,... | collective-permute-start | bytes 442376 | tf_op jit(solution)/shard_map/ppermute | solution.py:438
  32.5 8.7 %collective-permute-start.9 = (bf16[4,7,16,128]{3,2,1,0:T(8,128)(2,1)S(1)}, bf16[4,7,16,128]{3,2,1,0:T(8,128)(2,1)S(1)}, u32[]{:S(2)}, u32[]{:S(2)}) collective-permute-start(bf16[4,7,16,128]{3,2,1,0:T(8,128)(2,1)S(1)} %get-tuple-element.69), channel_id=1, source_target_pairs={{0,5},{1,4},{2,7},{3,6},{4,1},{5,0},{6,3},{7,2},{8,13},{9,12},{10,... | collective-permute-start | bytes 344072 | tf_op jit(solution)/shard_map/ppermute | solution.py:438
  34.3 7.5 %collective-permute-start.10 = (bf16[4,7,16,128]{3,2,1,0:T(8,128)(2,1)S(1)}, bf16[4,7,16,128]{3,2,1,0:T(8,128)(2,1)S(1)}, u32[]{:S(2)}, u32[]{:S(2)}) collective-permute-start(bf16[4,7,16,128]{3,2,1,0:T(8,128)(2,1)S(1)} %get-tuple-element.70), channel_id=1, source_target_pairs={{0,1},{1,0},{2,3},{3,2},{4,5},{5,4},{6,7},{7,6},{8,9},{9,8},{10,11... | collective-permute-start | bytes 344072 | tf_op jit(solution)/shard_map/ppermute | solution.py:438
  34.8 7.3 %collective-permute-start.11 = (bf16[4,7,16,128]{3,2,1,0:T(8,128)(2,1)S(1)}, bf16[4,7,16,128]{3,2,1,0:T(8,128)(2,1)S(1)}, u32[]{:S(2)}, u32[]{:S(2)}) collective-permute-start(bf16[4,7,16,128]{3,2,1,0:T(8,128)(2,1)S(1)} %get-tuple-element.71), channel_id=1, source_target_pairs={{0,4},{1,5},{2,6},{3,7},{4,0},{5,1},{6,2},{7,3},{8,12},{9,13},{10,... | collective-permute-start | bytes 344072 | tf_op jit(solution)/shard_map/ppermute | solution.py:438
  42.2 6.8 %collective-permute-start.12 = (bf16[16,16,128]{2,1,0:T(8,128)(2,1)S(1)}, bf16[16,16,128]{2,1,0:T(8,128)(2,1)S(1)}, u32[]{:S(2)}, u32[]{:S(2)}) collective-permute-start(bf16[16,16,128]{2,1,0:T(8,128)(2,1)S(1)} %get-tuple-element.73), channel_id=1, source_target_pairs={{0,24},{1,25},{2,26},{3,27},{4,28},{5,29},{6,30},{7,31},{8,16},{9,... | collective-permute-start | bytes 196616 | tf_op jit(solution)/shard_map/ppermute | solution.py:438
  42.8 7.0 %collective-permute-start.13 = (bf16[16,16,128]{2,1,0:T(8,128)(2,1)S(1)}, bf16[16,16,128]{2,1,0:T(8,128)(2,1)S(1)}, u32[]{:S(2)}, u32[]{:S(2)}) collective-permute-start(bf16[16,16,128]{2,1,0:T(8,128)(2,1)S(1)} %get-tuple-element.74), channel_id=1, source_target_pairs={{0,16},{1,17},{2,18},{3,19},{4,20},{5,21},{6,22},{7,23},{8,24},{9,... | collective-permute-start | bytes 196616 | tf_op jit(solution)/shard_map/ppermute | solution.py:438
  42.8 7.0 %collective-permute-start.14 = (bf16[16,16,128]{2,1,0:T(8,128)(2,1)S(1)}, bf16[16,16,128]{2,1,0:T(8,128)(2,1)S(1)}, u32[]{:S(2)}, u32[]{:S(2)}) collective-permute-start(bf16[16,16,128]{2,1,0:T(8,128)(2,1)S(1)} %get-tuple-element.75), channel_id=1, source_target_pairs={{0,8},{1,9},{2,10},{3,11},{4,12},{5,13},{6,14},{7,15},{8,0},{9,1},... | collective-permute-start | bytes 196616 | tf_op jit(solution)/shard_map/ppermute | solution.py:438
  49.8 6.1 %collective-permute-start.17 = (bf16[16,16,128]{2,1,0:T(8,128)(2,1)S(1)}, bf16[16,16,128]{2,1,0:T(8,128)(2,1)S(1)}, u32[]{:S(2)}, u32[]{:S(2)}) collective-permute-start(bf16[16,16,128]{2,1,0:T(8,128)(2,1)S(1)} %line_sum.1.a_ref), channel_id=1, source_target_pairs={{0,8},{1,9},{2,10},{3,11},{4,12},{5,13},{6,14},{7,15},{8,0},{9,1},... | collective-permute-start | bytes 196616 | tf_op jit(solution)/shard_map/ppermute | solution.py:438
  51.0 5.9 %collective-permute-start.16 = (bf16[16,16,128]{2,1,0:T(8,128)(2,1)S(1)}, bf16[16,16,128]{2,1,0:T(8,128)(2,1)S(1)}, u32[]{:S(2)}, u32[]{:S(2)}) collective-permute-start(bf16[16,16,128]{2,1,0:T(8,128)(2,1)S(1)} %line_sum.1.a_ref), channel_id=1, source_target_pairs={{0,16},{1,17},{2,18},{3,19},{4,20},{5,21},{6,22},{7,23},{8,24},{9,... | collective-permute-start | bytes 196616 | tf_op jit(solution)/shard_map/ppermute | solution.py:438
  52.4 6.1 %collective-permute-start.15 = (bf16[16,16,128]{2,1,0:T(8,128)(2,1)S(1)}, bf16[16,16,128]{2,1,0:T(8,128)(2,1)S(1)}, u32[]{:S(2)}, u32[]{:S(2)}) collective-permute-start(bf16[16,16,128]{2,1,0:T(8,128)(2,1)S(1)} %line_sum.1.a_ref), channel_id=1, source_target_pairs={{0,24},{1,25},{2,26},{3,27},{4,28},{5,29},{6,30},{7,31},{8,16},{9,... | collective-permute-start | bytes 196616 | tf_op jit(solution)/shard_map/ppermute | solution.py:438
  54.3 7.7 %collective-permute-start.2 = (bf16[64,256]{1,0:T(8,128)(2,1)S(1)}, bf16[64,256]{1,0:T(8,128)(2,1)S(1)}, u32[]{:S(2)}, u32[]{:S(2)}) collective-permute-start(bf16[64,256]{1,0:T(8,128)(2,1)S(1)} %get-tuple-element.54), channel_id=1, source_target_pairs={{0,1},{1,0},{2,3},{3,2},{4,5},{5,4},{6,7},{7,6},{8,9},{9,8},{10,11... | collective-permute-start | bytes 98312 | tf_op jit(solution)/shard_map/ppermute | solution.py:492
  58.5 11.0 %collective-permute-start.20 = (bf16[4,16,16,128]{3,2,1,0:T(8,128)(2,1)S(1)}, bf16[4,16,16,128]{3,2,1,0:T(8,128)(2,1)S(1)}, u32[]{:S(2)}, u32[]{:S(2)}) collective-permute-start(bf16[4,16,16,128]{3,2,1,0:T(8,128)(2,1)S(1)} %line_gather.1.rest_0_.a_ref), channel_id=1, source_target_pairs={{0,4},{1,5},{2,6},{3,7},{4,0},{5,1},{6,2},{7,3},{8,12},{9,13},{10,... | collective-permute-start | bytes 786440 | tf_op jit(solution)/shard_map/ppermute | solution.py:438
  59.5 12.2 %collective-permute-start.19 = (bf16[4,16,16,128]{3,2,1,0:T(8,128)(2,1)S(1)}, bf16[4,16,16,128]{3,2,1,0:T(8,128)(2,1)S(1)}, u32[]{:S(2)}, u32[]{:S(2)}) collective-permute-start(bf16[4,16,16,128]{3,2,1,0:T(8,128)(2,1)S(1)} %line_gather.1.rest_0_.a_ref), channel_id=1, source_target_pairs={{0,1},{1,0},{2,3},{3,2},{4,5},{5,4},{6,7},{7,6},{8,9},{9,8},{10,11... | collective-permute-start | bytes 786440 | tf_op jit(solution)/shard_map/ppermute | solution.py:438
  60.9 10.8 %collective-permute-start.18 = (bf16[4,16,16,128]{3,2,1,0:T(8,128)(2,1)S(1)}, bf16[4,16,16,128]{3,2,1,0:T(8,128)(2,1)S(1)}, u32[]{:S(2)}, u32[]{:S(2)}) collective-permute-start(bf16[4,16,16,128]{3,2,1,0:T(8,128)(2,1)S(1)} %line_gather.1.rest_0_.a_ref), channel_id=1, source_target_pairs={{0,5},{1,4},{2,7},{3,6},{4,1},{5,0},{6,3},{7,2},{8,13},{9,12},{10,... | collective-permute-start | bytes 786440 | tf_op jit(solution)/shard_map/ppermute | solution.py:438
  71.8 2.7 %collective-permute-start.21 = (bf16[16,16,16,128]{3,2,1,0:T(8,128)(2,1)S(1)}, bf16[16,16,16,128]{3,2,1,0:T(8,128)(2,1)S(1)}, u32[]{:S(2)}, u32[]{:S(2)}) collective-permute-start(bf16[16,16,16,128]{3,2,1,0:T(8,128)(2,1)S(1)} %plane_gather.1.half_ref), channel_id=1, source_target_pairs={{0,2},{1,3},{2,0},{3,1},{4,6},{5,7},{6,4},{7,5},{8,10},{9,11},{10,... | collective-permute-start | bytes 3145736 | tf_op jit(solution)/shard_map/ppermute | solution.py:438

commit v16 on v15

--- a/solution.py
+++ b/solution.py
@@ -85,9 +85,7 @@
     send_ref[:, k] = jnp.where(core == 0, high, low).reshape(16, 16, CH // 2)
 
 
-def edges_kernel(bands, count_ref, x_ref, cot_ref, *rest):
-    outs, nxt_ref = rest[:-1], rest[-1]
-    nxt_ref[...] = cot_ref[0:2]
+def edges_kernel(bands, count_ref, x_ref, *outs):
     count = count_ref[0]
     band = lax.axis_index("grp")
     wide = x_ref.shape[1]
@@ -127,6 +125,10 @@
         return 0
 
     lax.fori_loop(0, rows // 2, rows_of, 0, unroll=4)
+
+
+def next_kernel(cot_ref, _, nxt_ref):
+    nxt_ref[...] = cot_ref[0:2]
 
 
 def halo_kernel(bands, count_ref, top_ref, bot_ref, *rest):
@@ -508,15 +510,14 @@
     dma = pltpu.SemaphoreType.DMA
 
     sides = 1 if grp == 2 else 2
-    *edge, nxt = call(
+    edge = call(
         functools.partial(edges_kernel, grp),
         "edges",
-        [count, (VMEM, x), (VMEM, cotangent)],
-        [(VMEM, (cols * slots, ch))] * sides + [(VMEM, (2,) + cotangent.shape[1:])],
+        [count, (VMEM, x)],
+        [(VMEM, (cols * slots, ch))] * sides,
         flops=tap // 8,
     )
     top, bot = from_bands(edge)
-    nxt_got = around(nxt, "tm", -1)
     last_shape = (2 * wide + 32, ch)
     at_shape = (3 * ch, (rows + 4) * 128)
     xt, acts, at, last_two = call(
@@ -526,10 +527,18 @@
         [(VMEM, tile), (VMEM, padded), (VMEM, at_shape), (VMEM, last_shape)],
         flops=2 * tap,
     )
+    (nxt,) = call(
+        next_kernel,
+        "next",
+        [(VMEM, cotangent), (ANY, last_two)],
+        [(VMEM, (2,) + cotangent.shape[1:])],
+        moved=1024,
+    )
+    nxt_got = around(nxt, "tm", -1)
     acts, at, last_two = call(
         functools.partial(halo_kernel, grp),
         "halo",
-        [count, (VMEM, top), (VMEM, bot), (VMEM, acts), (VMEM, at), (VMEM, last_two),
+        [count, (VMEM, top), (VMEM, bot), (VMEM, acts), (VMEM, at), (VMEM, last_two), (ANY, nxt),
          (VMEM, cotangent), (VMEM, wt), (VMEM, wd)],
         [(VMEM, padded), (VMEM, at_shape), (VMEM, last_shape)],
         alias={3: 0, 4: 1, 5: 2},

time: 76.2 us -> 75.9 us (level)
  local copies, waits for them, and re-layouts: 2.18 us -> 1.24 us
  waiting for transfers between devices: 23.1 us -> 23.9 us
    unnamed x12 -> x10, local copies, waits for them, and re-layouts: 2.18 us -> 1.24 us
    ppermute x18, waiting for transfers between devices: 20.4 us -> 21.2 us  [swap(): return lax.ppermute(value, AXES, [(d, d ^ flip) for d in range(tm * grp)])]
    pallas_call x17 -> x18, Pallas kernels: 23.9 us -> 23.9 us  [call(): pl.pallas_call(kernel, out_shape=shapes, in_specs=[s for s, _ in ins], ou...]
  transfers between devices with their start and end apart: 22 -> 22, of which waited for: 14 -> 16; matrix products, arithmetic and copies ran while one was open for 0% -> 0% of each run, Pallas kernels for 29% -> 29%
where the time goes in v16:
time: 75.9 us; the launch traced here: 75.8 us
  starting transfers between devices  25.3 us (33%)
  Pallas kernels  23.9 us (31%)
  waiting for transfers between devices  23.9 us (31%)
  between operations  1.46 us (2%)
  local copies, waits for them, and re-layouts  1.24 us (2%)
    pallas_call x18, Pallas kernels, call(): pl.pallas_call(kernel, out_shape=shapes, in_specs=[s for s, _ in ins], ou...  23.9 us
    ppermute x18, waiting for transfers between devices, swap(): return lax.ppermute(value, AXES, [(d, d ^ flip) for d in range(tm * grp)])  21.2 us
    ppermute x18, starting transfers between devices, swap(): return lax.ppermute(value, AXES, [(d, d ^ flip) for d in range(tm * grp)])  17 us
    ppermute x2, starting transfers between devices, from_bands(): got = lax.ppermute(parts[0], 'grp', [(0, 1), (1, 0)])  4.55 us
    ppermute x2, starting transfers between devices, around(): lax.ppermute(value, axis, [(i, (i + by) % count) for i in range(count)])  3.74 us
    ppermute x2, waiting for transfers between devices, around(): lax.ppermute(value, axis, [(i, (i + by) % count) for i in range(count)])  2.72 us
  transfers between devices with their start and end apart: 22, of which 16 were waited for; matrix products, arithmetic and copies ran while one was open for 0% of the time, Pallas kernels for 29%

profile of v16, /device:TPU:0, one launch (start us, length us, event | category | flops | bytes accessed | tf_op | source)
XLA Modules:
  0.0 75.8 jit_solution(2375510863328333441)
XLA Ops:
  1.3 1.2 %copy-done.1 = bf16[16,16,8,256]{3,2,1,0:T(8,128)(2,1)S(1)} copy-done((bf16[16,16,8,256]{3,2,1,0:T(8,128)(2,1)S(1)}, bf16[16,16,8,256]{3,2,1,0:T(8,128)(2,1)}, u32[]{:S(2)}) %copy-start.1) | copy-done | bytes 1048600
  2.5 0.3 edges.1._
  2.8 3.0 %collective-permute-start = (bf16[128,256]{1,0:T(8,128)(2,1)S(1)}, bf16[128,256]{1,0:T(8,128)(2,1)S(1)}, u32[]{:S(2)}, u32[]{:S(2)}) collective-permute-start(bf16[128,256]{1,0:T(8,128)(2,1)S(1)} %edges.1._), channel_id=1, source_target_pairs={{0,1},{1,0},{2,3},{3,2},{4,5},{5,4},{6,7},{7,6},{8,9},{9,8},{10,11... | collective-permute-start | bytes 196616 | tf_op jit(solution)/shard_map/ppermute | solution.py:494
  5.9 1.6 %acts.1 = (bf16[16,8,16,256]{3,2,1,0:T(8,128)(2,1)S(1)}, bf16[18,10,16,256]{3,2,1,0:T(8,128)(2,1)S(1)}, bf16[768,2560]{1,0:T(8,128)(2,1)S(1)}, bf16[288,256]{1,0:T(8,128)(2,1)S(1)}) custom-call(s32[1]{0:T(128)S(6)} %copy.29.count_ref, bf16[16,128,256]{2,1,0:T(8,128)(2,1)S(1)} %bitcast.7, bf16[128,256]{1,0:T(8,128)(2,1)S(1)} %edges.1._), custom_call_target="tpu_custom_call" | custom-call | flops 536870912 | bytes 7651332 | tf_op jit(solution)/shard_map/acts/pallas_call | solution.py:416
  7.5 3.7 %collective-permute-start.1 = (bf16[2,8,4,256]{3,2,1,0:T(4,128)(2,1)S(1)}, bf16[2,8,4,256]{3,2,1,0:T(4,128)(2,1)S(1)}, u32[]{:S(2)}, u32[]{:S(2)}) collective-permute-start(bf16[2,8,4,256]{3,2,1,0:T(4,128)(2,1)S(1)} %next.1.rest_3_), channel_id=1, source_target_pairs={{0,30},{2,0},{4,2},{6,4},{8,6},{10,8},{12,10},{14,12},{16,14},{18,... | collective-permute-start | bytes 98312 | tf_op jit(solution)/shard_map/ppermute | solution.py:489
  11.3 0.2 halo.1
  11.5 1.4 %collective-permute-done.1.nxt_ref = bf16[2,8,4,256]{3,2,1,0:T(4,128)(2,1)S(1)} collective-permute-done((bf16[2,8,4,256]{3,2,1,0:T(4,128)(2,1)S(1)}, bf16[2,8,4,256]{3,2,1,0:T(4,128)(2,1)S(1)}, u32[]{:S(2)}, u32[]{:S(2)}) %collective-permute-start.1) | collective-permute-done | bytes 32800 | tf_op jit(solution)/shard_map/ppermute | solution.py:489
  12.9 4.5 %grad_spatial.1 = (bf16[8,4,16,256]{3,2,1,0:T(8,128)(2,1)S(1)}, bf16[16,8,16,256]{3,2,1,0:T(8,128)(2,1)S(1)}, bf16[16,10,16,256]{3,2,1,0:T(8,128)(2,1)S(1)}, bf1...) custom-call(s32[1]{0:T(128)S(6)} %copy.29.count_ref, ...), custom_call_target="tpu_custom_call" | custom-call | flops 3758096384 | bytes 8978436 | tf_op jit(solution)/shard_map/grad_spatial/pallas_call | solution.py:416
  17.4 1.3 %collective-permute-done.3.__1_.prev_ref = bf16[288,256]{1,0:T(8,128)(2,1)S(1)} collective-permute-done((bf16[288,256]{1,0:T(8,128)(2,1)S(1)}, bf16[288,256]{1,0:T(8,128)(2,1)S(1)}, u32[]{:S(2)}, u32[]{:S(2)}) %collective-permute-start.3) | collective-permute-done | bytes 147488 | tf_op jit(solution)/shard_map/ppermute | solution.py:489
  18.7 3.6 %spatial.1 = (bf16[18,10,16,256]{3,2,1,0:T(8,128)(2,1)S(1)}, bf16[16,8,16,256]{3,2,1,0:T(8,128)(2,1)S(1)}) custom-call(s32[1]{0:T(128)S(6)} %copy.29.count_ref, bf16[18,10,16,256]{3,2,1,0:T(8,128)(2,1)S(1)} %get-tuple-element.51.acts_in, bf16[288,256]{1,0:T(8,128)(2,1)S(1)} %collective-permute-done.3.__1_.prev_ref, ...), custom_call_target="tpu_custom_call", output_to_operand_aliasing={{0}: (1, {})} | custom-call | flops 2415919104 | bytes 5324804 | tf_op jit(solution)/shard_map/spatial/pallas_call | solution.py:416
  22.3 0.2 plane_send.2
  22.5 0.1 collective-permute-start.5
  22.5 2.8 %forward.1 = (bf16[512,256]{1,0:T(8,128)(2,1)S(1)}, bf16[16,7,16,128]{3,2,1,0:T(8,128)(2,1)S(1)}, bf16[16,7,16,128]{3,2,1,0:T(8,128)(2,1)S(1)}) custom-call(s32[1]{0:T(128)S(6)} %copy.29.count_ref, bf16[16,8,16,256]{3,2,1,0:T(8,128)(2,1)S(1)} %get-tuple-element.43.xt_ref, bf16[16,8,16,256]{3,2,1,0:T(8,128)(2,1)S(1)} %get-tuple-element.54.rest_0_.sp_ref, ...), custom_call_target="tpu_custom_call" | custom-call | flops 2684354560 | bytes 5505028 | tf_op jit(solution)/shard_map/forward/pallas_call | solution.py:416
  25.4 4.3 %collective-permute-done.5.__1_.refs_1_ = bf16[4,9,16,128]{3,2,1,0:T(8,128)(2,1)S(1)} collective-permute-done((bf16[4,9,16,128]{3,2,1,0:T(8,128)(2,1)S(1)}, bf16[4,9,16,128]{3,2,1,0:T(8,128)(2,1)S(1)}, u32[]{:S(2)}, u32[]{:S(2)}) %collective-permute-start.5) | collective-permute-done | bytes 147488 | tf_op jit(solution)/shard_map/ppermute | solution.py:440
  29.7 0.5 collective-permute-start.6
  30.2 0.3 collective-permute-start.7
  30.5 1.0 %collective-permute-done.8.got_ref = bf16[16,7,16,128]{3,2,1,0:T(8,128)(2,1)S(1)} collective-permute-done((bf16[16,7,16,128]{3,2,1,0:T(8,128)(2,1)S(1)}, bf16[16,7,16,128]{3,2,1,0:T(8,128)(2,1)S(1)}, u32[]{:S(2)}, u32[]{:S(2)}) %collective-permute-start.8) | collective-permute-done | bytes 458784 | tf_op jit(solution)/shard_map/ppermute | solution.py:440
  31.5 0.1 plane_send.3
  31.6 1.7 %collective-permute-start.9 = (bf16[4,7,16,128]{3,2,1,0:T(8,128)(2,1)S(1)}, bf16[4,7,16,128]{3,2,1,0:T(8,128)(2,1)S(1)}, u32[]{:S(2)}, u32[]{:S(2)}) collective-permute-start(bf16[4,7,16,128]{3,2,1,0:T(8,128)(2,1)S(1)} %get-tuple-element.65), channel_id=1, source_target_pairs={{0,5},{1,4},{2,7},{3,6},{4,1},{5,0},{6,3},{7,2},{8,13},{9,12},{10,... | collective-permute-start | bytes 344072 | tf_op jit(solution)/shard_map/ppermute | solution.py:440
  33.4 0.5 collective-permute-start.10
  33.9 1.3 %collective-permute-start.11 = (bf16[4,7,16,128]{3,2,1,0:T(8,128)(2,1)S(1)}, bf16[4,7,16,128]{3,2,1,0:T(8,128)(2,1)S(1)}, u32[]{:S(2)}, u32[]{:S(2)}) collective-permute-start(bf16[4,7,16,128]{3,2,1,0:T(8,128)(2,1)S(1)} %get-tuple-element.67), channel_id=1, source_target_pairs={{0,4},{1,5},{2,6},{3,7},{4,0},{5,1},{6,2},{7,3},{8,12},{9,13},{10,... | collective-permute-start | bytes 344072 | tf_op jit(solution)/shard_map/ppermute | solution.py:440
  35.2 1.0 %collective-permute-done.6.refs_2_ = bf16[4,9,16,128]{3,2,1,0:T(8,128)(2,1)S(1)} collective-permute-done((bf16[4,9,16,128]{3,2,1,0:T(8,128)(2,1)S(1)}, bf16[4,9,16,128]{3,2,1,0:T(8,128)(2,1)S(1)}, u32[]{:S(2)}, u32[]{:S(2)}) %collective-permute-start.6) | collective-permute-done | bytes 147488 | tf_op jit(solution)/shard_map/ppermute | solution.py:440
  36.2 0.7 collective-permute-done.7.refs_3_
  36.9 3.5 %collective-permute-done.9.refs_5_ = bf16[4,7,16,128]{3,2,1,0:T(8,128)(2,1)S(1)} collective-permute-done((bf16[4,7,16,128]{3,2,1,0:T(8,128)(2,1)S(1)}, bf16[4,7,16,128]{3,2,1,0:T(8,128)(2,1)S(1)}, u32[]{:S(2)}, u32[]{:S(2)}) %collective-permute-start.9) | collective-permute-done | bytes 114720 | tf_op jit(solution)/shard_map/ppermute | solution.py:440
  40.3 0.5 collective-permute-done.10.refs_6_
  40.9 0.3 collective-permute-done.11.refs_7_
  41.1 0.1 line_send.1
  41.3 2.2 %collective-permute-start.12 = (bf16[16,16,128]{2,1,0:T(8,128)(2,1)S(1)}, bf16[16,16,128]{2,1,0:T(8,128)(2,1)S(1)}, u32[]{:S(2)}, u32[]{:S(2)}) collective-permute-start(bf16[16,16,128]{2,1,0:T(8,128)(2,1)S(1)} %get-tuple-element.69), channel_id=1, source_target_pairs={{0,24},{1,25},{2,26},{3,27},{4,28},{5,29},{6,30},{7,31},{8,16},{9,... | collective-permute-start | bytes 196616 | tf_op jit(solution)/shard_map/ppermute | solution.py:440
  43.5 2.3 %collective-permute-start.14 = (bf16[16,16,128]{2,1,0:T(8,128)(2,1)S(1)}, bf16[16,16,128]{2,1,0:T(8,128)(2,1)S(1)}, u32[]{:S(2)}, u32[]{:S(2)}) collective-permute-start(bf16[16,16,128]{2,1,0:T(8,128)(2,1)S(1)} %get-tuple-element.71), channel_id=1, source_target_pairs={{0,8},{1,9},{2,10},{3,11},{4,12},{5,13},{6,14},{7,15},{8,0},{9,1},... | collective-permute-start | bytes 196616 | tf_op jit(solution)/shard_map/ppermute | solution.py:440
  45.7 1.7 %collective-permute-done.12.b_ref = bf16[16,16,128]{2,1,0:T(8,128)(2,1)S(1)} collective-permute-done((bf16[16,16,128]{2,1,0:T(8,128)(2,1)S(1)}, bf16[16,16,128]{2,1,0:T(8,128)(2,1)S(1)}, u32[]{:S(2)}, u32[]{:S(2)}) %collective-permute-start.12) | collective-permute-done | bytes 65568 | tf_op jit(solution)/shard_map/ppermute | solution.py:440
  47.5 1.9 %collective-permute-done.13.c_ref = bf16[16,16,128]{2,1,0:T(8,128)(2,1)S(1)} collective-permute-done((bf16[16,16,128]{2,1,0:T(8,128)(2,1)S(1)}, bf16[16,16,128]{2,1,0:T(8,128)(2,1)S(1)}, u32[]{:S(2)}, u32[]{:S(2)}) %collective-permute-start.13) | collective-permute-done | bytes 65568 | tf_op jit(solution)/shard_map/ppermute | solution.py:440
  49.4 0.7 collective-permute-start.17
  50.1 2.2 %collective-permute-start.16 = (bf16[16,16,128]{2,1,0:T(8,128)(2,1)S(1)}, bf16[16,16,128]{2,1,0:T(8,128)(2,1)S(1)}, u32[]{:S(2)}, u32[]{:S(2)}) collective-permute-start(bf16[16,16,128]{2,1,0:T(8,128)(2,1)S(1)} %line_sum.1.a_ref), channel_id=1, source_target_pairs={{0,16},{1,17},{2,18},{3,19},{4,20},{5,21},{6,22},{7,23},{8,24},{9,... | collective-permute-start | bytes 196616 | tf_op jit(solution)/shard_map/ppermute | solution.py:440
  52.3 1.6 %collective-permute-start.15 = (bf16[16,16,128]{2,1,0:T(8,128)(2,1)S(1)}, bf16[16,16,128]{2,1,0:T(8,128)(2,1)S(1)}, u32[]{:S(2)}, u32[]{:S(2)}) collective-permute-start(bf16[16,16,128]{2,1,0:T(8,128)(2,1)S(1)} %line_sum.1.a_ref), channel_id=1, source_target_pairs={{0,24},{1,25},{2,26},{3,27},{4,28},{5,29},{6,30},{7,31},{8,16},{9,... | collective-permute-start | bytes 196616 | tf_op jit(solution)/shard_map/ppermute | solution.py:440
  53.9 1.5 %collective-permute-start.2 = (bf16[64,256]{1,0:T(8,128)(2,1)S(1)}, bf16[64,256]{1,0:T(8,128)(2,1)S(1)}, u32[]{:S(2)}, u32[]{:S(2)}) collective-permute-start(bf16[64,256]{1,0:T(8,128)(2,1)S(1)} %get-tuple-element.50), channel_id=1, source_target_pairs={{0,1},{1,0},{2,3},{3,2},{4,5},{5,4},{6,7},{7,6},{8,9},{9,8},{10,11... | collective-permute-start | bytes 98312 | tf_op jit(solution)/shard_map/ppermute | solution.py:494
  55.4 2.0 %collective-permute-done.16.c_ref = bf16[16,16,128]{2,1,0:T(8,128)(2,1)S(1)} collective-permute-done((bf16[16,16,128]{2,1,0:T(8,128)(2,1)S(1)}, bf16[16,16,128]{2,1,0:T(8,128)(2,1)S(1)}, u32[]{:S(2)}, u32[]{:S(2)}) %collective-permute-start.16) | collective-permute-done | bytes 65568 | tf_op jit(solution)/shard_map/ppermute | solution.py:440
  57.3 1.1 %collective-permute-done.15.b_ref = bf16[16,16,128]{2,1,0:T(8,128)(2,1)S(1)} collective-permute-done((bf16[16,16,128]{2,1,0:T(8,128)(2,1)S(1)}, bf16[16,16,128]{2,1,0:T(8,128)(2,1)S(1)}, u32[]{:S(2)}, u32[]{:S(2)}) %collective-permute-start.15) | collective-permute-done | bytes 65568 | tf_op jit(solution)/shard_map/ppermute | solution.py:440
  58.5 0.8 %collective-permute-start.20 = (bf16[4,16,16,128]{3,2,1,0:T(8,128)(2,1)S(1)}, bf16[4,16,16,128]{3,2,1,0:T(8,128)(2,1)S(1)}, u32[]{:S(2)}, u32[]{:S(2)}) collective-permute-start(bf16[4,16,16,128]{3,2,1,0:T(8,128)(2,1)S(1)} %line_gather.1.rest_0_.a_ref), channel_id=1, source_target_pairs={{0,4},{1,5},{2,6},{3,7},{4,0},{5,1},{6,2},{7,3},{8,12},{9,13},{10,... | collective-permute-start | bytes 786440 | tf_op jit(solution)/shard_map/ppermute | solution.py:440
  59.3 1.6 %collective-permute-start.19 = (bf16[4,16,16,128]{3,2,1,0:T(8,128)(2,1)S(1)}, bf16[4,16,16,128]{3,2,1,0:T(8,128)(2,1)S(1)}, u32[]{:S(2)}, u32[]{:S(2)}) collective-permute-start(bf16[4,16,16,128]{3,2,1,0:T(8,128)(2,1)S(1)} %line_gather.1.rest_0_.a_ref), channel_id=1, source_target_pairs={{0,1},{1,0},{2,3},{3,2},{4,5},{5,4},{6,7},{7,6},{8,9},{9,8},{10,11... | collective-permute-start | bytes 786440 | tf_op jit(solution)/shard_map/ppermute | solution.py:440
  61.0 1.1 %collective-permute-start.18 = (bf16[4,16,16,128]{3,2,1,0:T(8,128)(2,1)S(1)}, bf16[4,16,16,128]{3,2,1,0:T(8,128)(2,1)S(1)}, u32[]{:S(2)}, u32[]{:S(2)}) collective-permute-start(bf16[4,16,16,128]{3,2,1,0:T(8,128)(2,1)S(1)} %line_gather.1.rest_0_.a_ref), channel_id=1, source_target_pairs={{0,5},{1,4},{2,7},{3,6},{4,1},{5,0},{6,3},{7,2},{8,13},{9,12},{10,... | collective-permute-start | bytes 786440 | tf_op jit(solution)/shard_map/ppermute | solution.py:440
  62.0 7.4 %grad_x.1 = (bf16[16,128,256]{2,1,0:T(8,128)(2,1)}, bf16[16,8,4,256]{3,2,1,0:T(4,128)(2,1)}, f32[8,128]{1,0:T(8,128)S(1)}) custom-call(s32[1]{0:T(128)S(6)} %copy.29.count_ref, bf16[16,8,16,256]{3,2,1,0:T(8,128)(2,1)S(1)} %get-tuple-element.43.xt_ref, bf16[16,8,16,256]{3,2,1,0:T(8,128)(2,1)S(1)} %get-tuple-element.48.gy_ref, ...), custom_call_target="tpu_custom_call" | custom-call | flops 2684354560 | bytes 7147524 | tf_op jit(solution)/shard_map/grad_x/pallas_call | solution.py:416
  69.5 0.6 collective-permute-done.19.c_ref
  70.1 1.4 %collective-permute-done.18.b_ref = bf16[4,16,16,128]{3,2,1,0:T(8,128)(2,1)S(1)} collective-permute-done((bf16[4,16,16,128]{3,2,1,0:T(8,128)(2,1)S(1)}, bf16[4,16,16,128]{3,2,1,0:T(8,128)(2,1)S(1)}, u32[]{:S(2)}, u32[]{:S(2)}) %collective-permute-start.18) | collective-permute-done | bytes 262176 | tf_op jit(solution)/shard_map/ppermute | solution.py:440
  71.5 0.1 plane_gather.1.half_ref
  71.6 0.1 collective-permute-start.21
  71.7 1.5 %finish.2 = (f32[9,256,256]{2,1,0:T(8,128)}, f32[3,256,256]{2,1,0:T(8,128)}, f32[4,256,256]{2,1,0:T(8,128)}) custom-call(bf16[16,16,16,128]{3,2,1,0:T(8,128)(2,1)S(1)} %plane_gather.1.half_ref), custom_call_target="tpu_custom_call" | custom-call | bytes 5242880 | tf_op jit(solution)/shard_map/finish/pallas_call | solution.py:416
  73.1 1.2 %collective-permute-done.21.half_ref = bf16[16,16,16,128]{3,2,1,0:T(8,128)(2,1)S(1)} collective-permute-done((bf16[16,16,16,128]{3,2,1,0:T(8,128)(2,1)S(1)}, bf16[16,16,16,128]{3,2,1,0:T(8,128)(2,1)S(1)}, u32[]{:S(2)}, u32[]{:S(2)}) %collective-permute-start.21) | collective-permute-done | bytes 1048608 | tf_op jit(solution)/shard_map/ppermute | solution.py:440
  74.3 1.5 %finish.3 = (f32[9,256,256]{2,1,0:T(8,128)}, f32[3,256,256]{2,1,0:T(8,128)}, f32[4,256,256]{2,1,0:T(8,128)}) custom-call(bf16[16,16,16,128]{3,2,1,0:T(8,128)(2,1)S(1)} %collective-permute-done.21.half_ref, f32[9,256,256]{2,1,0:T(8,128)} %get-tuple-element.75.rest_0_, ...), custom_call_target="tpu_custom_call", output_to_operand_aliasing={{0}: (1, {}), {1}: (2, {}), {2}: (3, {})} | custom-call | bytes 9437184 | tf_op jit(solution)/shard_map/finish/pallas_call | solution.py:416
  (24 shorter events, 0.1 us)
Async XLA Ops:
  1.3 1.2 %copy-start.1 = (bf16[16,16,8,256]{3,2,1,0:T(8,128)(2,1)S(1)}, bf16[16,16,8,256]{3,2,1,0:T(8,128)(2,1)}, u32[]{:S(2)}) copy-start(bf16[16,16,8,256]{3,2,1,0:T(8,128)(2,1)} %param.6) | copy-start | bytes 3145732
  2.5 5.0 %copy-start = (bf16[16,8,4,256]{3,2,1,0:T(4,128)(2,1)S(1)}, bf16[16,8,4,256]{3,2,1,0:T(4,128)(2,1)}, u32[]{:S(2)}) copy-start(bf16[16,8,4,256]{3,2,1,0:T(4,128)(2,1)} %cot_ref.3) | copy-start | bytes 786436
  2.8 8.5 %copy-start.2 = (bf16[2,2,256,256]{3,2,1,0:T(8,128)(2,1)S(1)}, bf16[2,2,256,256]{3,2,1,0:T(8,128)(2,1)}, u32[]{:S(2)}) copy-start(bf16[2,2,256,256]{3,2,1,0:T(8,128)(2,1)} %param.10) | copy-start | bytes 1572868
  2.8 8.5 %copy-start.3 = (bf16[3,256,256]{2,1,0:T(8,128)(2,1)S(1)}, bf16[3,256,256]{2,1,0:T(8,128)(2,1)}, u32[]{:S(2)}) copy-start(bf16[3,256,256]{2,1,0:T(8,128)(2,1)} %wt_ref.5) | copy-start | bytes 1179652
  2.8 8.4 %collective-permute-start = (bf16[128,256]{1,0:T(8,128)(2,1)S(1)}, bf16[128,256]{1,0:T(8,128)(2,1)S(1)}, u32[]{:S(2)}, u32[]{:S(2)}) collective-permute-start(bf16[128,256]{1,0:T(8,128)(2,1)S(1)} %edges.1._), channel_id=1, source_target_pairs={{0,1},{1,0},{2,3},{3,2},{4,5},{5,4},{6,7},{7,6},{8,9},{9,8},{10,11... | collective-permute-start | bytes 196616 | tf_op jit(solution)/shard_map/ppermute | solution.py:494
  7.5 5.3 %collective-permute-start.1 = (bf16[2,8,4,256]{3,2,1,0:T(4,128)(2,1)S(1)}, bf16[2,8,4,256]{3,2,1,0:T(4,128)(2,1)S(1)}, u32[]{:S(2)}, u32[]{:S(2)}) collective-permute-start(bf16[2,8,4,256]{3,2,1,0:T(4,128)(2,1)S(1)} %next.1.rest_3_), channel_id=1, source_target_pairs={{0,30},{2,0},{4,2},{6,4},{8,6},{10,8},{12,10},{14,12},{16,14},{18,... | collective-permute-start | bytes 98312 | tf_op jit(solution)/shard_map/ppermute | solution.py:489
  11.4 7.3 %collective-permute-start.3 = (bf16[288,256]{1,0:T(8,128)(2,1)S(1)}, bf16[288,256]{1,0:T(8,128)(2,1)S(1)}, u32[]{:S(2)}, u32[]{:S(2)}) collective-permute-start(bf16[288,256]{1,0:T(8,128)(2,1)S(1)} %get-tuple-element.52), channel_id=1, source_target_pairs={{0,2},{2,4},{4,6},{6,8},{8,10},{10,12},{12,14},{14,16},{16,18},{18... | collective-permute-start | bytes 442376 | tf_op jit(solution)/shard_map/ppermute | solution.py:489
  12.9 5.9 %copy-start.4 = (bf16[3,3,256,256]{3,2,1,0:T(8,128)(2,1)S(1)}, bf16[3,3,256,256]{3,2,1,0:T(8,128)(2,1)}, u32[]{:S(2)}) copy-start(bf16[3,3,256,256]{3,2,1,0:T(8,128)(2,1)} %param.8) | copy-start | bytes 3538948
  18.7 3.6 %collective-permute-start.4 = (bf16[16,9,16,128]{3,2,1,0:T(8,128)(2,1)S(1)}, bf16[16,9,16,128]{3,2,1,0:T(8,128)(2,1)S(1)}, u32[]{:S(2)}, u32[]{:S(2)}) collective-permute-start(bf16[16,9,16,128]{3,2,1,0:T(8,128)(2,1)S(1)} %pass.2._), channel_id=1, source_target_pairs={{0,2},{1,3},{2,0},{3,1},{4,6},{5,7},{6,4},{7,5},{8,10},{9,11},{10,... | collective-permute-start | bytes 1769480 | tf_op jit(solution)/shard_map/ppermute | solution.py:440
  22.5 7.2 %collective-permute-start.5 = (bf16[4,9,16,128]{3,2,1,0:T(8,128)(2,1)S(1)}, bf16[4,9,16,128]{3,2,1,0:T(8,128)(2,1)S(1)}, u32[]{:S(2)}, u32[]{:S(2)}) collective-permute-start(bf16[4,9,16,128]{3,2,1,0:T(8,128)(2,1)S(1)} %get-tuple-element.58.rest_1_), channel_id=1, source_target_pairs={{0,5},{1,4},{2,7},{3,6},{4,1},{5,0},{6,3},{7,2},{8,13},{9,12},{10,... | collective-permute-start | bytes 442376 | tf_op jit(solution)/shard_map/ppermute | solution.py:440
  29.7 1.8 %collective-permute-start.8 = (bf16[16,7,16,128]{3,2,1,0:T(8,128)(2,1)S(1)}, bf16[16,7,16,128]{3,2,1,0:T(8,128)(2,1)S(1)}, u32[]{:S(2)}, u32[]{:S(2)}) collective-permute-start(bf16[16,7,16,128]{3,2,1,0:T(8,128)(2,1)S(1)} %pass.3), channel_id=1, source_target_pairs={{0,2},{1,3},{2,0},{3,1},{4,6},{5,7},{6,4},{7,5},{8,10},{9,11},{10,... | collective-permute-start | bytes 1376264 | tf_op jit(solution)/shard_map/ppermute | solution.py:440
  29.7 6.5 %collective-permute-start.6 = (bf16[4,9,16,128]{3,2,1,0:T(8,128)(2,1)S(1)}, bf16[4,9,16,128]{3,2,1,0:T(8,128)(2,1)S(1)}, u32[]{:S(2)}, u32[]{:S(2)}) collective-permute-start(bf16[4,9,16,128]{3,2,1,0:T(8,128)(2,1)S(1)} %get-tuple-element.59.rest_2_), channel_id=1, source_target_pairs={{0,1},{1,0},{2,3},{3,2},{4,5},{5,4},{6,7},{7,6},{8,9},{9,8},{10,11... | collective-permute-start | bytes 442376 | tf_op jit(solution)/shard_map/ppermute | solution.py:440
  30.2 6.7 %collective-permute-start.7 = (bf16[4,9,16,128]{3,2,1,0:T(8,128)(2,1)S(1)}, bf16[4,9,16,128]{3,2,1,0:T(8,128)(2,1)S(1)}, u32[]{:S(2)}, u32[]{:S(2)}) collective-permute-start(bf16[4,9,16,128]{3,2,1,0:T(8,128)(2,1)S(1)} %get-tuple-element.60.rest_3_), channel_id=1, source_target_pairs={{0,4},{1,5},{2,6},{3,7},{4,0},{5,1},{6,2},{7,3},{8,12},{9,13},{10,... | collective-permute-start | bytes 442376 | tf_op jit(solution)/shard_map/ppermute | solution.py:440
  31.6 8.7 %collective-permute-start.9 = (bf16[4,7,16,128]{3,2,1,0:T(8,128)(2,1)S(1)}, bf16[4,7,16,128]{3,2,1,0:T(8,128)(2,1)S(1)}, u32[]{:S(2)}, u32[]{:S(2)}) collective-permute-start(bf16[4,7,16,128]{3,2,1,0:T(8,128)(2,1)S(1)} %get-tuple-element.65), channel_id=1, source_target_pairs={{0,5},{1,4},{2,7},{3,6},{4,1},{5,0},{6,3},{7,2},{8,13},{9,12},{10,... | collective-permute-start | bytes 344072 | tf_op jit(solution)/shard_map/ppermute | solution.py:440
  33.4 7.5 %collective-permute-start.10 = (bf16[4,7,16,128]{3,2,1,0:T(8,128)(2,1)S(1)}, bf16[4,7,16,128]{3,2,1,0:T(8,128)(2,1)S(1)}, u32[]{:S(2)}, u32[]{:S(2)}) collective-permute-start(bf16[4,7,16,128]{3,2,1,0:T(8,128)(2,1)S(1)} %get-tuple-element.66), channel_id=1, source_target_pairs={{0,1},{1,0},{2,3},{3,2},{4,5},{5,4},{6,7},{7,6},{8,9},{9,8},{10,11... | collective-permute-start | bytes 344072 | tf_op jit(solution)/shard_map/ppermute | solution.py:440
  33.9 7.3 %collective-permute-start.11 = (bf16[4,7,16,128]{3,2,1,0:T(8,128)(2,1)S(1)}, bf16[4,7,16,128]{3,2,1,0:T(8,128)(2,1)S(1)}, u32[]{:S(2)}, u32[]{:S(2)}) collective-permute-start(bf16[4,7,16,128]{3,2,1,0:T(8,128)(2,1)S(1)} %get-tuple-element.67), channel_id=1, source_target_pairs={{0,4},{1,5},{2,6},{3,7},{4,0},{5,1},{6,2},{7,3},{8,12},{9,13},{10,... | collective-permute-start | bytes 344072 | tf_op jit(solution)/shard_map/ppermute | solution.py:440
  41.3 6.2 %collective-permute-start.12 = (bf16[16,16,128]{2,1,0:T(8,128)(2,1)S(1)}, bf16[16,16,128]{2,1,0:T(8,128)(2,1)S(1)}, u32[]{:S(2)}, u32[]{:S(2)}) collective-permute-start(bf16[16,16,128]{2,1,0:T(8,128)(2,1)S(1)} %get-tuple-element.69), channel_id=1, source_target_pairs={{0,24},{1,25},{2,26},{3,27},{4,28},{5,29},{6,30},{7,31},{8,16},{9,... | collective-permute-start | bytes 196616 | tf_op jit(solution)/shard_map/ppermute | solution.py:440
  43.4 5.9 %collective-permute-start.13 = (bf16[16,16,128]{2,1,0:T(8,128)(2,1)S(1)}, bf16[16,16,128]{2,1,0:T(8,128)(2,1)S(1)}, u32[]{:S(2)}, u32[]{:S(2)}) collective-permute-start(bf16[16,16,128]{2,1,0:T(8,128)(2,1)S(1)} %get-tuple-element.70), channel_id=1, source_target_pairs={{0,16},{1,17},{2,18},{3,19},{4,20},{5,21},{6,22},{7,23},{8,24},{9,... | collective-permute-start | bytes 196616 | tf_op jit(solution)/shard_map/ppermute | solution.py:440
  43.5 5.9 %collective-permute-start.14 = (bf16[16,16,128]{2,1,0:T(8,128)(2,1)S(1)}, bf16[16,16,128]{2,1,0:T(8,128)(2,1)S(1)}, u32[]{:S(2)}, u32[]{:S(2)}) collective-permute-start(bf16[16,16,128]{2,1,0:T(8,128)(2,1)S(1)} %get-tuple-element.71), channel_id=1, source_target_pairs={{0,8},{1,9},{2,10},{3,11},{4,12},{5,13},{6,14},{7,15},{8,0},{9,1},... | collective-permute-start | bytes 196616 | tf_op jit(solution)/shard_map/ppermute | solution.py:440
  49.4 6.0 %collective-permute-start.17 = (bf16[16,16,128]{2,1,0:T(8,128)(2,1)S(1)}, bf16[16,16,128]{2,1,0:T(8,128)(2,1)S(1)}, u32[]{:S(2)}, u32[]{:S(2)}) collective-permute-start(bf16[16,16,128]{2,1,0:T(8,128)(2,1)S(1)} %line_sum.1.a_ref), channel_id=1, source_target_pairs={{0,8},{1,9},{2,10},{3,11},{4,12},{5,13},{6,14},{7,15},{8,0},{9,1},... | collective-permute-start | bytes 196616 | tf_op jit(solution)/shard_map/ppermute | solution.py:440
  50.1 7.2 %collective-permute-start.16 = (bf16[16,16,128]{2,1,0:T(8,128)(2,1)S(1)}, bf16[16,16,128]{2,1,0:T(8,128)(2,1)S(1)}, u32[]{:S(2)}, u32[]{:S(2)}) collective-permute-start(bf16[16,16,128]{2,1,0:T(8,128)(2,1)S(1)} %line_sum.1.a_ref), channel_id=1, source_target_pairs={{0,16},{1,17},{2,18},{3,19},{4,20},{5,21},{6,22},{7,23},{8,24},{9,... | collective-permute-start | bytes 196616 | tf_op jit(solution)/shard_map/ppermute | solution.py:440
  52.3 6.2 %collective-permute-start.15 = (bf16[16,16,128]{2,1,0:T(8,128)(2,1)S(1)}, bf16[16,16,128]{2,1,0:T(8,128)(2,1)S(1)}, u32[]{:S(2)}, u32[]{:S(2)}) collective-permute-start(bf16[16,16,128]{2,1,0:T(8,128)(2,1)S(1)} %line_sum.1.a_ref), channel_id=1, source_target_pairs={{0,24},{1,25},{2,26},{3,27},{4,28},{5,29},{6,30},{7,31},{8,16},{9,... | collective-permute-start | bytes 196616 | tf_op jit(solution)/shard_map/ppermute | solution.py:440
  53.9 8.2 %collective-permute-start.2 = (bf16[64,256]{1,0:T(8,128)(2,1)S(1)}, bf16[64,256]{1,0:T(8,128)(2,1)S(1)}, u32[]{:S(2)}, u32[]{:S(2)}) collective-permute-start(bf16[64,256]{1,0:T(8,128)(2,1)S(1)} %get-tuple-element.50), channel_id=1, source_target_pairs={{0,1},{1,0},{2,3},{3,2},{4,5},{5,4},{6,7},{7,6},{8,9},{9,8},{10,11... | collective-permute-start | bytes 98312 | tf_op jit(solution)/shard_map/ppermute | solution.py:494
  58.5 11.0 %collective-permute-start.20 = (bf16[4,16,16,128]{3,2,1,0:T(8,128)(2,1)S(1)}, bf16[4,16,16,128]{3,2,1,0:T(8,128)(2,1)S(1)}, u32[]{:S(2)}, u32[]{:S(2)}) collective-permute-start(bf16[4,16,16,128]{3,2,1,0:T(8,128)(2,1)S(1)} %line_gather.1.rest_0_.a_ref), channel_id=1, source_target_pairs={{0,4},{1,5},{2,6},{3,7},{4,0},{5,1},{6,2},{7,3},{8,12},{9,13},{10,... | collective-permute-start | bytes 786440 | tf_op jit(solution)/shard_map/ppermute | solution.py:440
  59.3 10.8 %collective-permute-start.19 = (bf16[4,16,16,128]{3,2,1,0:T(8,128)(2,1)S(1)}, bf16[4,16,16,128]{3,2,1,0:T(8,128)(2,1)S(1)}, u32[]{:S(2)}, u32[]{:S(2)}) collective-permute-start(bf16[4,16,16,128]{3,2,1,0:T(8,128)(2,1)S(1)} %line_gather.1.rest_0_.a_ref), channel_id=1, source_target_pairs={{0,1},{1,0},{2,3},{3,2},{4,5},{5,4},{6,7},{7,6},{8,9},{9,8},{10,11... | collective-permute-start | bytes 786440 | tf_op jit(solution)/shard_map/ppermute | solution.py:440
  61.0 10.5 %collective-permute-start.18 = (bf16[4,16,16,128]{3,2,1,0:T(8,128)(2,1)S(1)}, bf16[4,16,16,128]{3,2,1,0:T(8,128)(2,1)S(1)}, u32[]{:S(2)}, u32[]{:S(2)}) collective-permute-start(bf16[4,16,16,128]{3,2,1,0:T(8,128)(2,1)S(1)} %line_gather.1.rest_0_.a_ref), channel_id=1, source_target_pairs={{0,5},{1,4},{2,7},{3,6},{4,1},{5,0},{6,3},{7,2},{8,13},{9,12},{10,... | collective-permute-start | bytes 786440 | tf_op jit(solution)/shard_map/ppermute | solution.py:440
  71.6 2.7 %collective-permute-start.21 = (bf16[16,16,16,128]{3,2,1,0:T(8,128)(2,1)S(1)}, bf16[16,16,16,128]{3,2,1,0:T(8,128)(2,1)S(1)}, u32[]{:S(2)}, u32[]{:S(2)}) collective-permute-start(bf16[16,16,16,128]{3,2,1,0:T(8,128)(2,1)S(1)} %plane_gather.1.half_ref), channel_id=1, source_target_pairs={{0,2},{1,3},{2,0},{3,1},{4,6},{5,7},{6,4},{7,5},{8,10},{9,11},{10,... | collective-permute-start | bytes 3145736 | tf_op jit(solution)/shard_map/ppermute | solution.py:440

commit v17 on v16

--- a/solution.py
+++ b/solution.py
@@ -149,8 +149,26 @@
     last_ref[2 * rows * cols :] = mm(pick, jnp.concatenate(halo, 0)).astype(BF)
 
 
-def spatial_kernel(count_ref, acts_in, prev_ref, ws_ref, _, acts_ref, sp_ref):
+def conv_rows(acts_ref, ws_ref, sp_ref, start):
     rows, cols = sp_ref.shape[0], sp_ref.shape[1]
+
+    def rows_of(q, _):
+        total = None
+        for i in range(3):
+            for j in range(3):
+                left = acts_ref[pl.ds(start + 4 * q + i, 4), j : j + cols].reshape(
+                    4 * cols * SLOTS, CH
+                )
+                term = mm(left, ws_ref[i * 3 + j])
+                total = term if total is None else total + term
+        sp_ref[pl.ds(4 * q, 4)] = total.astype(BF).reshape(4, cols, SLOTS, CH)
+        return 0
+
+    lax.fori_loop(0, rows // 4, rows_of, 0)
+
+
+def upper_kernel(acts_in, prev_ref, ws_ref, _, acts_ref, sp_ref):
+    rows, cols = acts_ref.shape[0] - 2, acts_ref.shape[1] - 2
     a, b = iotas(256, 32)
     place = ((a >> 4) == (b & 15)) & ((a & 15) == OWN + (b >> 4)) & (lax.axis_index("tm") > 0)
     place = jnp.where(place, 1.0, 0.0).astype(BF)
@@ -166,17 +184,12 @@
         for k, row in enumerate(range(rows + 2)[both]):
             acts_ref[row, 1 : cols + 1] = acts_ref[row, 1 : cols + 1] + prev[k]
 
-    def rows_of(q, _):
-        total = None
-        for i in range(3):
-            for j in range(3):
-                left = acts_ref[pl.ds(4 * q + i, 4), j : j + cols].reshape(4 * cols * SLOTS, CH)
-                term = mm(left, ws_ref[i * 3 + j])
-                total = term if total is None else total + term
-        sp_ref[pl.ds(4 * q, 4)] = total.astype(BF).reshape(4, cols, SLOTS, CH)
-        return 0
-
-    lax.fori_loop(0, rows // 4, rows_of, 0)
+    conv_rows(acts_ref, ws_ref, sp_ref, 0)
+
+
+def lower_kernel(acts_ref, ws_ref, *rest):
+    sp_ref = rest[-1]
+    conv_rows(acts_ref, ws_ref, sp_ref, sp_ref.shape[0])
 
 
 def grad_spatial_kernel(
@@ -233,28 +246,25 @@
 
 
 def forward_kernel(
-    count_ref, xt_ref, sp_ref, cott_ref, gy_ref, wt_ref, wd_ref, *rest
+    count_ref, xt_ref, upper_ref, lower_ref, cott_ref, gy_ref, wt_ref, wd_ref, *rest
 ):
     down_ref, keep_ref, send_ref, y_ref, st_ref, yt_ref = rest[-6:]
     count = count_ref[0]
     rows, cols = xt_ref.shape[0], xt_ref.shape[1]
-    def rows_of(q, _):
-        s = sp_ref[pl.ds(8 * q, 8)].reshape(8 * cols * SLOTS, CH).astype(F32)
+    for q, sp_ref in enumerate((upper_ref, lower_ref)):
+        s = sp_ref[...].reshape(8 * cols * SLOTS, CH).astype(F32)
         s = s.reshape(8 * cols, SLOTS, CH)
         total = None
         for k in range(3):
             shifted = s if k == 2 else pltpu.roll(s, 2 - k, 1)
             shifted = shifted.astype(BF).reshape(8 * cols * SLOTS, CH)
-            at = pl.ds(pl.multiple_of(q * 1024, 1024), 1024)
+            at = slice(q * 1024, q * 1024 + 1024)
             st_ref[k * CH : k * CH + CH, at] = shifted.T
             term = mm(shifted, wt_ref[k])
             total = term if total is None else total + term
-        x = xt_ref[pl.ds(8 * q, 8)].reshape(8 * cols, SLOTS, CH).astype(F32)
+        x = xt_ref[8 * q : 8 * q + 8].reshape(8 * cols, SLOTS, CH).astype(F32)
         y = jnp.where(slot_mask(x.shape, count), x + total.reshape(x.shape), 0.0).astype(BF)
-        y_ref[pl.ds(8 * q, 8)] = y.reshape(8, cols, SLOTS, CH)
-        return 0
-
-    lax.fori_loop(0, rows // 8, rows_of, 0)
+        y_ref[8 * q : 8 * q + 8] = y.reshape(8, cols, SLOTS, CH)
 
     wide = rows * cols * SLOTS
     value = mm(st_ref[...], gy_ref[...].reshape(wide, CH))
@@ -558,29 +568,37 @@
     send_a = passed(send_a, [prev])
     got_a = core_round(send_a, tm, grp)
     cot_top, cot_bot = from_bands(edge)
-    acts, sp = call(
-        spatial_kernel,
-        "spatial",
-        [count, (VMEM, acts), (VMEM, prev), (VMEM, ws), (ANY, send_a)],
-        [(VMEM, padded), (VMEM, tile)],
-        flops=9 * tap,
-        alias={1: 0},
+    half_tile = (rows // 2, cols, slots, ch)
+    acts, upper = call(
+        upper_kernel,
+        "spatial_upper",
+        [(VMEM, acts), (VMEM, prev), (VMEM, ws), (ANY, send_a)],
+        [(VMEM, padded), (VMEM, half_tile)],
+        flops=5 * tap,
+        alias={0: 0},
     )
     _, plane, line, others = plan(tm, grp)
-    parts_a = plane_send(keep_a, got_a, [sp])
+    parts_a = plane_send(keep_a, got_a, [upper])
+    (lower,) = call(
+        lower_kernel,
+        "spatial_lower",
+        [(VMEM, acts), (VMEM, ws)] + [(ANY, a) for a in parts_a],
+        [(VMEM, half_tile)],
+        flops=4 * tap,
+    )
     half = (16, 7, 16, ch // 2)
     down, keep_b, send_b = call(
         forward_kernel,
         "forward",
-        [count, (VMEM, xt), (VMEM, sp), (VMEM, cott), (VMEM, gy), (VMEM, wt), (VMEM, wd),
+        [count, (VMEM, xt), (VMEM, upper), (VMEM, lower), (VMEM, cott), (VMEM, gy), (VMEM, wt), (VMEM, wd),
          *((ANY, a) for a in parts_a)],
         [(VMEM, (slots * wide // 4, ch)), (VMEM, half), (VMEM, half)],
         [pltpu.VMEM(v, BF) for v in (tile, (3 * ch, slots * wide), (4 * ch, slots * wide // 4))],
-        flops=10 * tap,
+        moved=1024,
         grant=14,
     )
     parts_a = four_round(parts_a, plane, tm, grp)
-    send_b = passed(send_b, parts_a[1:2])
+    send_b = passed(send_b, parts_a[1:3])
     parts_b = plane_send(keep_b, core_round(send_b, tm, grp), [])
     parts_b = four_round(parts_b, plane, tm, grp)
     parts = call(

time: 75.9 us -> 76.3 us (level)
  waiting for transfers between devices: 23.9 us -> 25.6 us
  starting transfers between devices: 25.3 us -> 24.4 us
    ppermute x18, waiting for transfers between devices: 21.2 us -> 22.8 us  [swap(): return lax.ppermute(value, AXES, [(d, d ^ flip) for d in range(tm * grp)])]
    ppermute x2, starting transfers between devices: 4.55 us -> 3.74 us  [from_bands(): got = lax.ppermute(parts[0], 'grp', [(0, 1), (1, 0)])]
    pallas_call x18 -> x19, Pallas kernels: 23.9 us -> 23.5 us  [call(): pl.pallas_call(kernel, out_shape=shapes, in_specs=[s for s, _ in ins], ou...]
  transfers between devices with their start and end apart: 22 -> 22, of which waited for: 16 -> 15; matrix products, arithmetic and copies ran while one was open for 0% -> 0% of each run, Pallas kernels for 29% -> 28%
where the time goes in v17:
time: 76.3 us; the launch traced here: 76.1 us
  waiting for transfers between devices  25.6 us (34%)
  starting transfers between devices  24.4 us (32%)
  Pallas kernels  23.5 us (31%)
  between operations  1.47 us (2%)
  local copies, waits for them, and re-layouts  1.24 us (2%)
    pallas_call x19, Pallas kernels, call(): pl.pallas_call(kernel, out_shape=shapes, in_specs=[s for s, _ in ins], ou...  23.5 us
    ppermute x18, waiting for transfers between devices, swap(): return lax.ppermute(value, AXES, [(d, d ^ flip) for d in range(tm * grp)])  22.8 us
    ppermute x18, starting transfers between devices, swap(): return lax.ppermute(value, AXES, [(d, d ^ flip) for d in range(tm * grp)])  16.9 us
    ppermute x2, starting transfers between devices, around(): lax.ppermute(value, axis, [(i, (i + by) % count) for i in range(count)])  3.74 us
    ppermute x2, starting transfers between devices, from_bands(): got = lax.ppermute(parts[0], 'grp', [(0, 1), (1, 0)])  3.74 us
    ppermute x2, waiting for transfers between devices, around(): lax.ppermute(value, axis, [(i, (i + by) % count) for i in range(count)])  2.72 us
  transfers between devices with their start and end apart: 22, of which 15 were waited for; matrix products, arithmetic and copies ran while one was open for 0% of the time, Pallas kernels for 28%

profile of v17, /device:TPU:0, one launch (start us, length us, event | category | flops | bytes accessed | tf_op | source)
XLA Modules:
  0.0 76.1 jit_solution(6204223842098355370)
XLA Ops:
  1.3 1.2 %copy-done.3 = bf16[16,16,8,256]{3,2,1,0:T(8,128)(2,1)S(1)} copy-done((bf16[16,16,8,256]{3,2,1,0:T(8,128)(2,1)S(1)}, bf16[16,16,8,256]{3,2,1,0:T(8,128)(2,1)}, u32[]{:S(2)}) %copy-start.3) | copy-done | bytes 1048600
  2.5 0.3 edges.1._
  2.8 3.0 %collective-permute-start = (bf16[128,256]{1,0:T(8,128)(2,1)S(1)}, bf16[128,256]{1,0:T(8,128)(2,1)S(1)}, u32[]{:S(2)}, u32[]{:S(2)}) collective-permute-start(bf16[128,256]{1,0:T(8,128)(2,1)S(1)} %edges.1._), channel_id=1, source_target_pairs={{0,1},{1,0},{2,3},{3,2},{4,5},{5,4},{6,7},{7,6},{8,9},{9,8},{10,11... | collective-permute-start | bytes 196616 | tf_op jit(solution)/shard_map/ppermute | solution.py:504
  5.9 1.6 %acts.1 = (bf16[16,8,16,256]{3,2,1,0:T(8,128)(2,1)S(1)}, bf16[18,10,16,256]{3,2,1,0:T(8,128)(2,1)S(1)}, bf16[768,2560]{1,0:T(8,128)(2,1)S(1)}, bf16[288,256]{1,0:T(8,128)(2,1)S(1)}) custom-call(s32[1]{0:T(128)S(6)} %copy.29.count_ref, bf16[16,128,256]{2,1,0:T(8,128)(2,1)S(1)} %bitcast.11, bf16[128,256]{1,0:T(8,128)(2,1)S(1)} %edges.1._), custom_call_target="tpu_custom_call" | custom-call | flops 536870912 | bytes 7651332 | tf_op jit(solution)/shard_map/acts/pallas_call | solution.py:426
  7.5 3.7 %collective-permute-start.1 = (bf16[2,8,4,256]{3,2,1,0:T(4,128)(2,1)S(1)}, bf16[2,8,4,256]{3,2,1,0:T(4,128)(2,1)S(1)}, u32[]{:S(2)}, u32[]{:S(2)}) collective-permute-start(bf16[2,8,4,256]{3,2,1,0:T(4,128)(2,1)S(1)} %next.1.rest_3_), channel_id=1, source_target_pairs={{0,30},{2,0},{4,2},{6,4},{8,6},{10,8},{12,10},{14,12},{16,14},{18,... | collective-permute-start | bytes 98312 | tf_op jit(solution)/shard_map/ppermute | solution.py:499
  11.3 0.2 halo.1
  11.5 1.4 %collective-permute-done.1.nxt_ref = bf16[2,8,4,256]{3,2,1,0:T(4,128)(2,1)S(1)} collective-permute-done((bf16[2,8,4,256]{3,2,1,0:T(4,128)(2,1)S(1)}, bf16[2,8,4,256]{3,2,1,0:T(4,128)(2,1)S(1)}, u32[]{:S(2)}, u32[]{:S(2)}) %collective-permute-start.1) | collective-permute-done | bytes 32800 | tf_op jit(solution)/shard_map/ppermute | solution.py:499
  12.9 4.5 %grad_spatial.1 = (bf16[8,4,16,256]{3,2,1,0:T(8,128)(2,1)S(1)}, bf16[16,8,16,256]{3,2,1,0:T(8,128)(2,1)S(1)}, bf16[16,10,16,256]{3,2,1,0:T(8,128)(2,1)S(1)}, bf1...) custom-call(s32[1]{0:T(128)S(6)} %copy.29.count_ref, ...), custom_call_target="tpu_custom_call" | custom-call | flops 3758096384 | bytes 8978436 | tf_op jit(solution)/shard_map/grad_spatial/pallas_call | solution.py:426
  17.4 1.3 %collective-permute-done.3.__1_.prev_ref = bf16[288,256]{1,0:T(8,128)(2,1)S(1)} collective-permute-done((bf16[288,256]{1,0:T(8,128)(2,1)S(1)}, bf16[288,256]{1,0:T(8,128)(2,1)S(1)}, u32[]{:S(2)}, u32[]{:S(2)}) %collective-permute-start.3) | collective-permute-done | bytes 147488 | tf_op jit(solution)/shard_map/ppermute | solution.py:499
  18.7 2.0 %spatial_upper.1 = (bf16[18,10,16,256]{3,2,1,0:T(8,128)(2,1)S(1)}, bf16[8,8,16,256]{3,2,1,0:T(8,128)(2,1)S(1)}) custom-call(bf16[18,10,16,256]{3,2,1,0:T(8,128)(2,1)S(1)} %get-tuple-element.52.acts_in, bf16[288,256]{1,0:T(8,128)(2,1)S(1)} %collective-permute-done.3.__1_.prev_ref, bf16[9,256,256]{2,1,0:T(8,128)(2,1)S(1)} %bitcast.12, ...), custom_call_target="tpu_custom_call", output_to_operand_aliasing={{0}: (0, {})} | custom-call | flops 1342177280 | bytes 4800512 | tf_op jit(solution)/shard_map/spatial_upper/pallas_call | solution.py:426
  20.8 0.2 plane_send.2
  20.9 0.1 collective-permute-start.5
  21.0 0.6 collective-permute-start.6
  21.6 1.6 %spatial_lower.1.lower_ref = bf16[8,8,16,256]{3,2,1,0:T(8,128)(2,1)S(1)} custom-call(bf16[18,10,16,256]{3,2,1,0:T(8,128)(2,1)S(1)} %get-tuple-element.56.acts_ref, bf16[9,256,256]{2,1,0:T(8,128)(2,1)S(1)} %bitcast.13, bf16[4,9,16,128]{3,2,1,0:T(8,128)(2,1)S(1)} %get-tuple-element.58.rest_0_.refs_0_, bf16[4,9,16,128]{3,2,1,0:T(8,128)(2,1)S(1)} %get-tuple-element.59.rest_1_, ...), custom_call_target="tpu_custom_call" | custom-call | flops 1073741824 | bytes 3178496 | tf_op jit(solution)/shard_map/spatial_lower/pallas_call | solution.py:426
  23.1 2.4 %forward.1 = (bf16[512,256]{1,0:T(8,128)(2,1)S(1)}, bf16[16,7,16,128]{3,2,1,0:T(8,128)(2,1)S(1)}, bf16[16,7,16,128]{3,2,1,0:T(8,128)(2,1)S(1)}) custom-call(s32[1]{0:T(128)S(6)} %copy.29.count_ref, bf16[16,8,16,256]{3,2,1,0:T(8,128)(2,1)S(1)} %get-tuple-element.44.xt_ref, bf16[8,8,16,256]{3,2,1,0:T(8,128)(2,1)S(1)} %get-tuple-element.55.rest_0_.upper_ref, ...), custom_call_target="tpu_custom_call" | custom-call | bytes 1024 | tf_op jit(solution)/shard_map/forward/pallas_call | solution.py:426
  25.5 2.7 %collective-permute-done.5.__1_.refs_1_ = bf16[4,9,16,128]{3,2,1,0:T(8,128)(2,1)S(1)} collective-permute-done((bf16[4,9,16,128]{3,2,1,0:T(8,128)(2,1)S(1)}, bf16[4,9,16,128]{3,2,1,0:T(8,128)(2,1)S(1)}, u32[]{:S(2)}, u32[]{:S(2)}) %collective-permute-start.5) | collective-permute-done | bytes 147488 | tf_op jit(solution)/shard_map/ppermute | solution.py:450
  28.2 2.2 %collective-permute-done.6.__2_.refs_2_ = bf16[4,9,16,128]{3,2,1,0:T(8,128)(2,1)S(1)} collective-permute-done((bf16[4,9,16,128]{3,2,1,0:T(8,128)(2,1)S(1)}, bf16[4,9,16,128]{3,2,1,0:T(8,128)(2,1)S(1)}, u32[]{:S(2)}, u32[]{:S(2)}) %collective-permute-start.6) | collective-permute-done | bytes 147488 | tf_op jit(solution)/shard_map/ppermute | solution.py:450
  30.5 0.2 collective-permute-start.7
  30.7 1.6 %collective-permute-done.8.got_ref = bf16[16,7,16,128]{3,2,1,0:T(8,128)(2,1)S(1)} collective-permute-done((bf16[16,7,16,128]{3,2,1,0:T(8,128)(2,1)S(1)}, bf16[16,7,16,128]{3,2,1,0:T(8,128)(2,1)S(1)}, u32[]{:S(2)}, u32[]{:S(2)}) %collective-permute-start.8) | collective-permute-done | bytes 458784 | tf_op jit(solution)/shard_map/ppermute | solution.py:450
  32.3 0.1 plane_send.3
  32.4 1.2 %collective-permute-start.9 = (bf16[4,7,16,128]{3,2,1,0:T(8,128)(2,1)S(1)}, bf16[4,7,16,128]{3,2,1,0:T(8,128)(2,1)S(1)}, u32[]{:S(2)}, u32[]{:S(2)}) collective-permute-start(bf16[4,7,16,128]{3,2,1,0:T(8,128)(2,1)S(1)} %get-tuple-element.67), channel_id=1, source_target_pairs={{0,5},{1,4},{2,7},{3,6},{4,1},{5,0},{6,3},{7,2},{8,13},{9,12},{10,... | collective-permute-start | bytes 344072 | tf_op jit(solution)/shard_map/ppermute | solution.py:450
  33.6 0.6 collective-permute-start.10
  34.1 1.8 %collective-permute-start.11 = (bf16[4,7,16,128]{3,2,1,0:T(8,128)(2,1)S(1)}, bf16[4,7,16,128]{3,2,1,0:T(8,128)(2,1)S(1)}, u32[]{:S(2)}, u32[]{:S(2)}) collective-permute-start(bf16[4,7,16,128]{3,2,1,0:T(8,128)(2,1)S(1)} %get-tuple-element.69), channel_id=1, source_target_pairs={{0,4},{1,5},{2,6},{3,7},{4,0},{5,1},{6,2},{7,3},{8,12},{9,13},{10,... | collective-permute-start | bytes 344072 | tf_op jit(solution)/shard_map/ppermute | solution.py:450
  36.0 1.2 %collective-permute-done.7.refs_3_ = bf16[4,9,16,128]{3,2,1,0:T(8,128)(2,1)S(1)} collective-permute-done((bf16[4,9,16,128]{3,2,1,0:T(8,128)(2,1)S(1)}, bf16[4,9,16,128]{3,2,1,0:T(8,128)(2,1)S(1)}, u32[]{:S(2)}, u32[]{:S(2)}) %collective-permute-start.7) | collective-permute-done | bytes 147488 | tf_op jit(solution)/shard_map/ppermute | solution.py:450
  37.1 2.4 %collective-permute-done.9.refs_5_ = bf16[4,7,16,128]{3,2,1,0:T(8,128)(2,1)S(1)} collective-permute-done((bf16[4,7,16,128]{3,2,1,0:T(8,128)(2,1)S(1)}, bf16[4,7,16,128]{3,2,1,0:T(8,128)(2,1)S(1)}, u32[]{:S(2)}, u32[]{:S(2)}) %collective-permute-start.9) | collective-permute-done | bytes 114720 | tf_op jit(solution)/shard_map/ppermute | solution.py:450
  39.6 1.4 %collective-permute-done.10.refs_6_ = bf16[4,7,16,128]{3,2,1,0:T(8,128)(2,1)S(1)} collective-permute-done((bf16[4,7,16,128]{3,2,1,0:T(8,128)(2,1)S(1)}, bf16[4,7,16,128]{3,2,1,0:T(8,128)(2,1)S(1)}, u32[]{:S(2)}, u32[]{:S(2)}) %collective-permute-start.10) | collective-permute-done | bytes 114720 | tf_op jit(solution)/shard_map/ppermute | solution.py:450
  40.9 0.8 %collective-permute-done.11.refs_7_ = bf16[4,7,16,128]{3,2,1,0:T(8,128)(2,1)S(1)} collective-permute-done((bf16[4,7,16,128]{3,2,1,0:T(8,128)(2,1)S(1)}, bf16[4,7,16,128]{3,2,1,0:T(8,128)(2,1)S(1)}, u32[]{:S(2)}, u32[]{:S(2)}) %collective-permute-start.11) | collective-permute-done | bytes 114720 | tf_op jit(solution)/shard_map/ppermute | solution.py:450
  41.7 0.1 line_send.1
  41.8 2.1 %collective-permute-start.12 = (bf16[16,16,128]{2,1,0:T(8,128)(2,1)S(1)}, bf16[16,16,128]{2,1,0:T(8,128)(2,1)S(1)}, u32[]{:S(2)}, u32[]{:S(2)}) collective-permute-start(bf16[16,16,128]{2,1,0:T(8,128)(2,1)S(1)} %get-tuple-element.71), channel_id=1, source_target_pairs={{0,24},{1,25},{2,26},{3,27},{4,28},{5,29},{6,30},{7,31},{8,16},{9,... | collective-permute-start | bytes 196616 | tf_op jit(solution)/shard_map/ppermute | solution.py:450
  43.9 2.3 %collective-permute-start.14 = (bf16[16,16,128]{2,1,0:T(8,128)(2,1)S(1)}, bf16[16,16,128]{2,1,0:T(8,128)(2,1)S(1)}, u32[]{:S(2)}, u32[]{:S(2)}) collective-permute-start(bf16[16,16,128]{2,1,0:T(8,128)(2,1)S(1)} %get-tuple-element.73), channel_id=1, source_target_pairs={{0,8},{1,9},{2,10},{3,11},{4,12},{5,13},{6,14},{7,15},{8,0},{9,1},... | collective-permute-start | bytes 196616 | tf_op jit(solution)/shard_map/ppermute | solution.py:450
  46.3 2.0 %collective-permute-done.12.b_ref = bf16[16,16,128]{2,1,0:T(8,128)(2,1)S(1)} collective-permute-done((bf16[16,16,128]{2,1,0:T(8,128)(2,1)S(1)}, bf16[16,16,128]{2,1,0:T(8,128)(2,1)S(1)}, u32[]{:S(2)}, u32[]{:S(2)}) %collective-permute-start.12) | collective-permute-done | bytes 65568 | tf_op jit(solution)/shard_map/ppermute | solution.py:450
  48.3 2.0 %collective-permute-done.13.c_ref = bf16[16,16,128]{2,1,0:T(8,128)(2,1)S(1)} collective-permute-done((bf16[16,16,128]{2,1,0:T(8,128)(2,1)S(1)}, bf16[16,16,128]{2,1,0:T(8,128)(2,1)S(1)}, u32[]{:S(2)}, u32[]{:S(2)}) %collective-permute-start.13) | collective-permute-done | bytes 65568 | tf_op jit(solution)/shard_map/ppermute | solution.py:450
  50.3 0.4 collective-permute-start.17
  50.7 2.4 %collective-permute-start.16 = (bf16[16,16,128]{2,1,0:T(8,128)(2,1)S(1)}, bf16[16,16,128]{2,1,0:T(8,128)(2,1)S(1)}, u32[]{:S(2)}, u32[]{:S(2)}) collective-permute-start(bf16[16,16,128]{2,1,0:T(8,128)(2,1)S(1)} %line_sum.1.a_ref), channel_id=1, source_target_pairs={{0,16},{1,17},{2,18},{3,19},{4,20},{5,21},{6,22},{7,23},{8,24},{9,... | collective-permute-start | bytes 196616 | tf_op jit(solution)/shard_map/ppermute | solution.py:450
  53.1 1.7 %collective-permute-start.15 = (bf16[16,16,128]{2,1,0:T(8,128)(2,1)S(1)}, bf16[16,16,128]{2,1,0:T(8,128)(2,1)S(1)}, u32[]{:S(2)}, u32[]{:S(2)}) collective-permute-start(bf16[16,16,128]{2,1,0:T(8,128)(2,1)S(1)} %line_sum.1.a_ref), channel_id=1, source_target_pairs={{0,24},{1,25},{2,26},{3,27},{4,28},{5,29},{6,30},{7,31},{8,16},{9,... | collective-permute-start | bytes 196616 | tf_op jit(solution)/shard_map/ppermute | solution.py:450
  54.7 0.7 collective-permute-start.2
  55.4 2.9 %collective-permute-done.16.c_ref = bf16[16,16,128]{2,1,0:T(8,128)(2,1)S(1)} collective-permute-done((bf16[16,16,128]{2,1,0:T(8,128)(2,1)S(1)}, bf16[16,16,128]{2,1,0:T(8,128)(2,1)S(1)}, u32[]{:S(2)}, u32[]{:S(2)}) %collective-permute-start.16) | collective-permute-done | bytes 65568 | tf_op jit(solution)/shard_map/ppermute | solution.py:450
  58.4 0.9 %collective-permute-done.15.b_ref = bf16[16,16,128]{2,1,0:T(8,128)(2,1)S(1)} collective-permute-done((bf16[16,16,128]{2,1,0:T(8,128)(2,1)S(1)}, bf16[16,16,128]{2,1,0:T(8,128)(2,1)S(1)}, u32[]{:S(2)}, u32[]{:S(2)}) %collective-permute-start.15) | collective-permute-done | bytes 65568 | tf_op jit(solution)/shard_map/ppermute | solution.py:450
  59.3 0.9 %collective-permute-start.20 = (bf16[4,16,16,128]{3,2,1,0:T(8,128)(2,1)S(1)}, bf16[4,16,16,128]{3,2,1,0:T(8,128)(2,1)S(1)}, u32[]{:S(2)}, u32[]{:S(2)}) collective-permute-start(bf16[4,16,16,128]{3,2,1,0:T(8,128)(2,1)S(1)} %line_gather.1.rest_0_.a_ref), channel_id=1, source_target_pairs={{0,4},{1,5},{2,6},{3,7},{4,0},{5,1},{6,2},{7,3},{8,12},{9,13},{10,... | collective-permute-start | bytes 786440 | tf_op jit(solution)/shard_map/ppermute | solution.py:450
  60.1 1.3 %collective-permute-start.19 = (bf16[4,16,16,128]{3,2,1,0:T(8,128)(2,1)S(1)}, bf16[4,16,16,128]{3,2,1,0:T(8,128)(2,1)S(1)}, u32[]{:S(2)}, u32[]{:S(2)}) collective-permute-start(bf16[4,16,16,128]{3,2,1,0:T(8,128)(2,1)S(1)} %line_gather.1.rest_0_.a_ref), channel_id=1, source_target_pairs={{0,1},{1,0},{2,3},{3,2},{4,5},{5,4},{6,7},{7,6},{8,9},{9,8},{10,11... | collective-permute-start | bytes 786440 | tf_op jit(solution)/shard_map/ppermute | solution.py:450
  61.4 1.4 %collective-permute-start.18 = (bf16[4,16,16,128]{3,2,1,0:T(8,128)(2,1)S(1)}, bf16[4,16,16,128]{3,2,1,0:T(8,128)(2,1)S(1)}, u32[]{:S(2)}, u32[]{:S(2)}) collective-permute-start(bf16[4,16,16,128]{3,2,1,0:T(8,128)(2,1)S(1)} %line_gather.1.rest_0_.a_ref), channel_id=1, source_target_pairs={{0,5},{1,4},{2,7},{3,6},{4,1},{5,0},{6,3},{7,2},{8,13},{9,12},{10,... | collective-permute-start | bytes 786440 | tf_op jit(solution)/shard_map/ppermute | solution.py:450
  62.8 7.4 %grad_x.1 = (bf16[16,128,256]{2,1,0:T(8,128)(2,1)}, bf16[16,8,4,256]{3,2,1,0:T(4,128)(2,1)}, f32[8,128]{1,0:T(8,128)S(1)}) custom-call(s32[1]{0:T(128)S(6)} %copy.29.count_ref, bf16[16,8,16,256]{3,2,1,0:T(8,128)(2,1)S(1)} %get-tuple-element.44.xt_ref, bf16[16,8,16,256]{3,2,1,0:T(8,128)(2,1)S(1)} %get-tuple-element.49.gy_ref, ...), custom_call_target="tpu_custom_call" | custom-call | flops 2684354560 | bytes 7147524 | tf_op jit(solution)/shard_map/grad_x/pallas_call | solution.py:426
  70.3 1.6 %collective-permute-done.19.c_ref = bf16[4,16,16,128]{3,2,1,0:T(8,128)(2,1)S(1)} collective-permute-done((bf16[4,16,16,128]{3,2,1,0:T(8,128)(2,1)S(1)}, bf16[4,16,16,128]{3,2,1,0:T(8,128)(2,1)S(1)}, u32[]{:S(2)}, u32[]{:S(2)}) %collective-permute-start.19) | collective-permute-done | bytes 262176 | tf_op jit(solution)/shard_map/ppermute | solution.py:450
  71.9 0.1 plane_gather.1.half_ref
  72.0 0.1 collective-permute-start.21
  72.0 1.5 %finish.2 = (f32[9,256,256]{2,1,0:T(8,128)}, f32[3,256,256]{2,1,0:T(8,128)}, f32[4,256,256]{2,1,0:T(8,128)}) custom-call(bf16[16,16,16,128]{3,2,1,0:T(8,128)(2,1)S(1)} %plane_gather.1.half_ref), custom_call_target="tpu_custom_call" | custom-call | bytes 5242880 | tf_op jit(solution)/shard_map/finish/pallas_call | solution.py:426
  73.5 1.2 %collective-permute-done.21.half_ref = bf16[16,16,16,128]{3,2,1,0:T(8,128)(2,1)S(1)} collective-permute-done((bf16[16,16,16,128]{3,2,1,0:T(8,128)(2,1)S(1)}, bf16[16,16,16,128]{3,2,1,0:T(8,128)(2,1)S(1)}, u32[]{:S(2)}, u32[]{:S(2)}) %collective-permute-start.21) | collective-permute-done | bytes 1048608 | tf_op jit(solution)/shard_map/ppermute | solution.py:450
  74.7 1.5 %finish.3 = (f32[9,256,256]{2,1,0:T(8,128)}, f32[3,256,256]{2,1,0:T(8,128)}, f32[4,256,256]{2,1,0:T(8,128)}) custom-call(bf16[16,16,16,128]{3,2,1,0:T(8,128)(2,1)S(1)} %collective-permute-done.21.half_ref, f32[9,256,256]{2,1,0:T(8,128)} %get-tuple-element.77.rest_0_, ...), custom_call_target="tpu_custom_call", output_to_operand_aliasing={{0}: (1, {}), {1}: (2, {}), {2}: (3, {})} | custom-call | bytes 9437184 | tf_op jit(solution)/shard_map/finish/pallas_call | solution.py:426
  (25 shorter events, 0.1 us)
Async XLA Ops:
  1.3 1.2 %copy-start.3 = (bf16[16,16,8,256]{3,2,1,0:T(8,128)(2,1)S(1)}, bf16[16,16,8,256]{3,2,1,0:T(8,128)(2,1)}, u32[]{:S(2)}) copy-start(bf16[16,16,8,256]{3,2,1,0:T(8,128)(2,1)} %param.6) | copy-start | bytes 3145732
  2.5 5.0 %copy-start.2 = (bf16[16,8,4,256]{3,2,1,0:T(4,128)(2,1)S(1)}, bf16[16,8,4,256]{3,2,1,0:T(4,128)(2,1)}, u32[]{:S(2)}) copy-start(bf16[16,8,4,256]{3,2,1,0:T(4,128)(2,1)} %cot_ref.3) | copy-start | bytes 786436
  2.8 8.5 %copy-start = (bf16[2,2,256,256]{3,2,1,0:T(8,128)(2,1)S(1)}, bf16[2,2,256,256]{3,2,1,0:T(8,128)(2,1)}, u32[]{:S(2)}) copy-start(bf16[2,2,256,256]{3,2,1,0:T(8,128)(2,1)} %param.10) | copy-start | bytes 1572868
  2.8 8.5 %copy-start.1 = (bf16[3,256,256]{2,1,0:T(8,128)(2,1)S(1)}, bf16[3,256,256]{2,1,0:T(8,128)(2,1)}, u32[]{:S(2)}) copy-start(bf16[3,256,256]{2,1,0:T(8,128)(2,1)} %wt_ref.5) | copy-start | bytes 1179652
  2.8 8.4 %collective-permute-start = (bf16[128,256]{1,0:T(8,128)(2,1)S(1)}, bf16[128,256]{1,0:T(8,128)(2,1)S(1)}, u32[]{:S(2)}, u32[]{:S(2)}) collective-permute-start(bf16[128,256]{1,0:T(8,128)(2,1)S(1)} %edges.1._), channel_id=1, source_target_pairs={{0,1},{1,0},{2,3},{3,2},{4,5},{5,4},{6,7},{7,6},{8,9},{9,8},{10,11... | collective-permute-start | bytes 196616 | tf_op jit(solution)/shard_map/ppermute | solution.py:504
  7.5 5.3 %collective-permute-start.1 = (bf16[2,8,4,256]{3,2,1,0:T(4,128)(2,1)S(1)}, bf16[2,8,4,256]{3,2,1,0:T(4,128)(2,1)S(1)}, u32[]{:S(2)}, u32[]{:S(2)}) collective-permute-start(bf16[2,8,4,256]{3,2,1,0:T(4,128)(2,1)S(1)} %next.1.rest_3_), channel_id=1, source_target_pairs={{0,30},{2,0},{4,2},{6,4},{8,6},{10,8},{12,10},{14,12},{16,14},{18,... | collective-permute-start | bytes 98312 | tf_op jit(solution)/shard_map/ppermute | solution.py:499
  11.4 7.3 %collective-permute-start.3 = (bf16[288,256]{1,0:T(8,128)(2,1)S(1)}, bf16[288,256]{1,0:T(8,128)(2,1)S(1)}, u32[]{:S(2)}, u32[]{:S(2)}) collective-permute-start(bf16[288,256]{1,0:T(8,128)(2,1)S(1)} %get-tuple-element.53), channel_id=1, source_target_pairs={{0,2},{2,4},{4,6},{6,8},{8,10},{10,12},{12,14},{14,16},{16,18},{18... | collective-permute-start | bytes 442376 | tf_op jit(solution)/shard_map/ppermute | solution.py:499
  12.9 5.9 %copy-start.4 = (bf16[3,3,256,256]{3,2,1,0:T(8,128)(2,1)S(1)}, bf16[3,3,256,256]{3,2,1,0:T(8,128)(2,1)}, u32[]{:S(2)}) copy-start(bf16[3,3,256,256]{3,2,1,0:T(8,128)(2,1)} %param.8) | copy-start | bytes 3538948
  18.7 2.0 %collective-permute-start.4 = (bf16[16,9,16,128]{3,2,1,0:T(8,128)(2,1)S(1)}, bf16[16,9,16,128]{3,2,1,0:T(8,128)(2,1)S(1)}, u32[]{:S(2)}, u32[]{:S(2)}) collective-permute-start(bf16[16,9,16,128]{3,2,1,0:T(8,128)(2,1)S(1)} %pass.2._), channel_id=1, source_target_pairs={{0,2},{1,3},{2,0},{3,1},{4,6},{5,7},{6,4},{7,5},{8,10},{9,11},{10,... | collective-permute-start | bytes 1769480 | tf_op jit(solution)/shard_map/ppermute | solution.py:450
  20.9 7.3 %collective-permute-start.5 = (bf16[4,9,16,128]{3,2,1,0:T(8,128)(2,1)S(1)}, bf16[4,9,16,128]{3,2,1,0:T(8,128)(2,1)S(1)}, u32[]{:S(2)}, u32[]{:S(2)}) collective-permute-start(bf16[4,9,16,128]{3,2,1,0:T(8,128)(2,1)S(1)} %get-tuple-element.59.rest_1_), channel_id=1, source_target_pairs={{0,5},{1,4},{2,7},{3,6},{4,1},{5,0},{6,3},{7,2},{8,13},{9,12},{10,... | collective-permute-start | bytes 442376 | tf_op jit(solution)/shard_map/ppermute | solution.py:450
  21.0 9.5 %collective-permute-start.6 = (bf16[4,9,16,128]{3,2,1,0:T(8,128)(2,1)S(1)}, bf16[4,9,16,128]{3,2,1,0:T(8,128)(2,1)S(1)}, u32[]{:S(2)}, u32[]{:S(2)}) collective-permute-start(bf16[4,9,16,128]{3,2,1,0:T(8,128)(2,1)S(1)} %get-tuple-element.60.rest_2_), channel_id=1, source_target_pairs={{0,1},{1,0},{2,3},{3,2},{4,5},{5,4},{6,7},{7,6},{8,9},{9,8},{10,11... | collective-permute-start | bytes 442376 | tf_op jit(solution)/shard_map/ppermute | solution.py:450
  30.5 1.8 %collective-permute-start.8 = (bf16[16,7,16,128]{3,2,1,0:T(8,128)(2,1)S(1)}, bf16[16,7,16,128]{3,2,1,0:T(8,128)(2,1)S(1)}, u32[]{:S(2)}, u32[]{:S(2)}) collective-permute-start(bf16[16,7,16,128]{3,2,1,0:T(8,128)(2,1)S(1)} %pass.3), channel_id=1, source_target_pairs={{0,2},{1,3},{2,0},{3,1},{4,6},{5,7},{6,4},{7,5},{8,10},{9,11},{10,... | collective-permute-start | bytes 1376264 | tf_op jit(solution)/shard_map/ppermute | solution.py:450
  30.5 6.6 %collective-permute-start.7 = (bf16[4,9,16,128]{3,2,1,0:T(8,128)(2,1)S(1)}, bf16[4,9,16,128]{3,2,1,0:T(8,128)(2,1)S(1)}, u32[]{:S(2)}, u32[]{:S(2)}) collective-permute-start(bf16[4,9,16,128]{3,2,1,0:T(8,128)(2,1)S(1)} %get-tuple-element.61.rest_3_), channel_id=1, source_target_pairs={{0,4},{1,5},{2,6},{3,7},{4,0},{5,1},{6,2},{7,3},{8,12},{9,13},{10,... | collective-permute-start | bytes 442376 | tf_op jit(solution)/shard_map/ppermute | solution.py:450
  32.4 7.2 %collective-permute-start.9 = (bf16[4,7,16,128]{3,2,1,0:T(8,128)(2,1)S(1)}, bf16[4,7,16,128]{3,2,1,0:T(8,128)(2,1)S(1)}, u32[]{:S(2)}, u32[]{:S(2)}) collective-permute-start(bf16[4,7,16,128]{3,2,1,0:T(8,128)(2,1)S(1)} %get-tuple-element.67), channel_id=1, source_target_pairs={{0,5},{1,4},{2,7},{3,6},{4,1},{5,0},{6,3},{7,2},{8,13},{9,12},{10,... | collective-permute-start | bytes 344072 | tf_op jit(solution)/shard_map/ppermute | solution.py:450
  33.6 7.4 %collective-permute-start.10 = (bf16[4,7,16,128]{3,2,1,0:T(8,128)(2,1)S(1)}, bf16[4,7,16,128]{3,2,1,0:T(8,128)(2,1)S(1)}, u32[]{:S(2)}, u32[]{:S(2)}) collective-permute-start(bf16[4,7,16,128]{3,2,1,0:T(8,128)(2,1)S(1)} %get-tuple-element.68), channel_id=1, source_target_pairs={{0,1},{1,0},{2,3},{3,2},{4,5},{5,4},{6,7},{7,6},{8,9},{9,8},{10,11... | collective-permute-start | bytes 344072 | tf_op jit(solution)/shard_map/ppermute | solution.py:450
  34.1 7.6 %collective-permute-start.11 = (bf16[4,7,16,128]{3,2,1,0:T(8,128)(2,1)S(1)}, bf16[4,7,16,128]{3,2,1,0:T(8,128)(2,1)S(1)}, u32[]{:S(2)}, u32[]{:S(2)}) collective-permute-start(bf16[4,7,16,128]{3,2,1,0:T(8,128)(2,1)S(1)} %get-tuple-element.69), channel_id=1, source_target_pairs={{0,4},{1,5},{2,6},{3,7},{4,0},{5,1},{6,2},{7,3},{8,12},{9,13},{10,... | collective-permute-start | bytes 344072 | tf_op jit(solution)/shard_map/ppermute | solution.py:450
  41.8 6.4 %collective-permute-start.12 = (bf16[16,16,128]{2,1,0:T(8,128)(2,1)S(1)}, bf16[16,16,128]{2,1,0:T(8,128)(2,1)S(1)}, u32[]{:S(2)}, u32[]{:S(2)}) collective-permute-start(bf16[16,16,128]{2,1,0:T(8,128)(2,1)S(1)} %get-tuple-element.71), channel_id=1, source_target_pairs={{0,24},{1,25},{2,26},{3,27},{4,28},{5,29},{6,30},{7,31},{8,16},{9,... | collective-permute-start | bytes 196616 | tf_op jit(solution)/shard_map/ppermute | solution.py:450
  43.9 6.3 %collective-permute-start.13 = (bf16[16,16,128]{2,1,0:T(8,128)(2,1)S(1)}, bf16[16,16,128]{2,1,0:T(8,128)(2,1)S(1)}, u32[]{:S(2)}, u32[]{:S(2)}) collective-permute-start(bf16[16,16,128]{2,1,0:T(8,128)(2,1)S(1)} %get-tuple-element.72), channel_id=1, source_target_pairs={{0,16},{1,17},{2,18},{3,19},{4,20},{5,21},{6,22},{7,23},{8,24},{9,... | collective-permute-start | bytes 196616 | tf_op jit(solution)/shard_map/ppermute | solution.py:450
  43.9 6.3 %collective-permute-start.14 = (bf16[16,16,128]{2,1,0:T(8,128)(2,1)S(1)}, bf16[16,16,128]{2,1,0:T(8,128)(2,1)S(1)}, u32[]{:S(2)}, u32[]{:S(2)}) collective-permute-start(bf16[16,16,128]{2,1,0:T(8,128)(2,1)S(1)} %get-tuple-element.73), channel_id=1, source_target_pairs={{0,8},{1,9},{2,10},{3,11},{4,12},{5,13},{6,14},{7,15},{8,0},{9,1},... | collective-permute-start | bytes 196616 | tf_op jit(solution)/shard_map/ppermute | solution.py:450
  50.3 5.2 %collective-permute-start.17 = (bf16[16,16,128]{2,1,0:T(8,128)(2,1)S(1)}, bf16[16,16,128]{2,1,0:T(8,128)(2,1)S(1)}, u32[]{:S(2)}, u32[]{:S(2)}) collective-permute-start(bf16[16,16,128]{2,1,0:T(8,128)(2,1)S(1)} %line_sum.1.a_ref), channel_id=1, source_target_pairs={{0,8},{1,9},{2,10},{3,11},{4,12},{5,13},{6,14},{7,15},{8,0},{9,1},... | collective-permute-start | bytes 196616 | tf_op jit(solution)/shard_map/ppermute | solution.py:450
  50.7 7.7 %collective-permute-start.16 = (bf16[16,16,128]{2,1,0:T(8,128)(2,1)S(1)}, bf16[16,16,128]{2,1,0:T(8,128)(2,1)S(1)}, u32[]{:S(2)}, u32[]{:S(2)}) collective-permute-start(bf16[16,16,128]{2,1,0:T(8,128)(2,1)S(1)} %line_sum.1.a_ref), channel_id=1, source_target_pairs={{0,16},{1,17},{2,18},{3,19},{4,20},{5,21},{6,22},{7,23},{8,24},{9,... | collective-permute-start | bytes 196616 | tf_op jit(solution)/shard_map/ppermute | solution.py:450
  53.1 6.2 %collective-permute-start.15 = (bf16[16,16,128]{2,1,0:T(8,128)(2,1)S(1)}, bf16[16,16,128]{2,1,0:T(8,128)(2,1)S(1)}, u32[]{:S(2)}, u32[]{:S(2)}) collective-permute-start(bf16[16,16,128]{2,1,0:T(8,128)(2,1)S(1)} %line_sum.1.a_ref), channel_id=1, source_target_pairs={{0,24},{1,25},{2,26},{3,27},{4,28},{5,29},{6,30},{7,31},{8,16},{9,... | collective-permute-start | bytes 196616 | tf_op jit(solution)/shard_map/ppermute | solution.py:450
  54.7 8.1 %collective-permute-start.2 = (bf16[64,256]{1,0:T(8,128)(2,1)S(1)}, bf16[64,256]{1,0:T(8,128)(2,1)S(1)}, u32[]{:S(2)}, u32[]{:S(2)}) collective-permute-start(bf16[64,256]{1,0:T(8,128)(2,1)S(1)} %get-tuple-element.51), channel_id=1, source_target_pairs={{0,1},{1,0},{2,3},{3,2},{4,5},{5,4},{6,7},{7,6},{8,9},{9,8},{10,11... | collective-permute-start | bytes 98312 | tf_op jit(solution)/shard_map/ppermute | solution.py:504
  59.3 11.0 %collective-permute-start.20 = (bf16[4,16,16,128]{3,2,1,0:T(8,128)(2,1)S(1)}, bf16[4,16,16,128]{3,2,1,0:T(8,128)(2,1)S(1)}, u32[]{:S(2)}, u32[]{:S(2)}) collective-permute-start(bf16[4,16,16,128]{3,2,1,0:T(8,128)(2,1)S(1)} %line_gather.1.rest_0_.a_ref), channel_id=1, source_target_pairs={{0,4},{1,5},{2,6},{3,7},{4,0},{5,1},{6,2},{7,3},{8,12},{9,13},{10,... | collective-permute-start | bytes 786440 | tf_op jit(solution)/shard_map/ppermute | solution.py:450
  60.1 11.7 %collective-permute-start.19 = (bf16[4,16,16,128]{3,2,1,0:T(8,128)(2,1)S(1)}, bf16[4,16,16,128]{3,2,1,0:T(8,128)(2,1)S(1)}, u32[]{:S(2)}, u32[]{:S(2)}) collective-permute-start(bf16[4,16,16,128]{3,2,1,0:T(8,128)(2,1)S(1)} %line_gather.1.rest_0_.a_ref), channel_id=1, source_target_pairs={{0,1},{1,0},{2,3},{3,2},{4,5},{5,4},{6,7},{7,6},{8,9},{9,8},{10,11... | collective-permute-start | bytes 786440 | tf_op jit(solution)/shard_map/ppermute | solution.py:450
  61.4 10.4 %collective-permute-start.18 = (bf16[4,16,16,128]{3,2,1,0:T(8,128)(2,1)S(1)}, bf16[4,16,16,128]{3,2,1,0:T(8,128)(2,1)S(1)}, u32[]{:S(2)}, u32[]{:S(2)}) collective-permute-start(bf16[4,16,16,128]{3,2,1,0:T(8,128)(2,1)S(1)} %line_gather.1.rest_0_.a_ref), channel_id=1, source_target_pairs={{0,5},{1,4},{2,7},{3,6},{4,1},{5,0},{6,3},{7,2},{8,13},{9,12},{10,... | collective-permute-start | bytes 786440 | tf_op jit(solution)/shard_map/ppermute | solution.py:450
  72.0 2.7 %collective-permute-start.21 = (bf16[16,16,16,128]{3,2,1,0:T(8,128)(2,1)S(1)}, bf16[16,16,16,128]{3,2,1,0:T(8,128)(2,1)S(1)}, u32[]{:S(2)}, u32[]{:S(2)}) collective-permute-start(bf16[16,16,16,128]{3,2,1,0:T(8,128)(2,1)S(1)} %plane_gather.1.half_ref), channel_id=1, source_target_pairs={{0,2},{1,3},{2,0},{3,1},{4,6},{5,7},{6,4},{7,5},{8,10},{9,11},{10,... | collective-permute-start | bytes 3145736 | tf_op jit(solution)/shard_map/ppermute | solution.py:450

commit v18 on v17

--- a/solution.py
+++ b/solution.py
@@ -598,7 +598,7 @@
         grant=14,
     )
     parts_a = four_round(parts_a, plane, tm, grp)
-    send_b = passed(send_b, parts_a[1:3])
+    send_b = passed(send_b, parts_a[1:2])
     parts_b = plane_send(keep_b, core_round(send_b, tm, grp), [])
     parts_b = four_round(parts_b, plane, tm, grp)
     parts = call(

time: 76.3 us -> 74.4 us (0.975)
  waiting for transfers between devices: 25.6 us -> 22.7 us
  starting transfers between devices: 24.4 us -> 25.3 us
    ppermute x18, waiting for transfers between devices: 22.8 us -> 20 us  [swap(): return lax.ppermute(value, AXES, [(d, d ^ flip) for d in range(tm * grp)])]
    ppermute x2, starting transfers between devices: 3.74 us -> 4.55 us  [from_bands(): got = lax.ppermute(parts[0], 'grp', [(0, 1), (1, 0)])]
  transfers between devices with their start and end apart: 22 -> 22, of which waited for: 15 -> 16; matrix products, arithmetic and copies ran while one was open for 0% -> 0% of each run, Pallas kernels for 28% -> 29%
where the time goes in v18:
time: 74.4 us; the launch traced here: 74.2 us
  starting transfers between devices  25.3 us (34%)
  Pallas kernels  23.4 us (31%)
  waiting for transfers between devices  22.7 us (31%)
  between operations  1.47 us (2%)
  local copies, waits for them, and re-layouts  1.24 us (2%)
    pallas_call x19, Pallas kernels, call(): pl.pallas_call(kernel, out_shape=shapes, in_specs=[s for s, _ in ins], ou...  23.4 us
    ppermute x18, waiting for transfers between devices, swap(): return lax.ppermute(value, AXES, [(d, d ^ flip) for d in range(tm * grp)])  20 us
    ppermute x18, starting transfers between devices, swap(): return lax.ppermute(value, AXES, [(d, d ^ flip) for d in range(tm * grp)])  17 us
    ppermute x2, starting transfers between devices, from_bands(): got = lax.ppermute(parts[0], 'grp', [(0, 1), (1, 0)])  4.55 us
    ppermute x2, starting transfers between devices, around(): lax.ppermute(value, axis, [(i, (i + by) % count) for i in range(count)])  3.74 us
    ppermute x2, waiting for transfers between devices, around(): lax.ppermute(value, axis, [(i, (i + by) % count) for i in range(count)])  2.72 us
  transfers between devices with their start and end apart: 22, of which 16 were waited for; matrix products, arithmetic and copies ran while one was open for 0% of the time, Pallas kernels for 29%

profile of v18, /device:TPU:0, one launch (start us, length us, event | category | flops | bytes accessed | tf_op | source)
XLA Modules:
  0.0 74.2 jit_solution(17719736824608702243)
XLA Ops:
  1.3 1.2 %copy-done.3 = bf16[16,16,8,256]{3,2,1,0:T(8,128)(2,1)S(1)} copy-done((bf16[16,16,8,256]{3,2,1,0:T(8,128)(2,1)S(1)}, bf16[16,16,8,256]{3,2,1,0:T(8,128)(2,1)}, u32[]{:S(2)}) %copy-start.3) | copy-done | bytes 1048600
  2.5 0.3 edges.1._
  2.8 3.0 %collective-permute-start = (bf16[128,256]{1,0:T(8,128)(2,1)S(1)}, bf16[128,256]{1,0:T(8,128)(2,1)S(1)}, u32[]{:S(2)}, u32[]{:S(2)}) collective-permute-start(bf16[128,256]{1,0:T(8,128)(2,1)S(1)} %edges.1._), channel_id=1, source_target_pairs={{0,1},{1,0},{2,3},{3,2},{4,5},{5,4},{6,7},{7,6},{8,9},{9,8},{10,11... | collective-permute-start | bytes 196616 | tf_op jit(solution)/shard_map/ppermute | solution.py:504
  5.9 1.6 %acts.1 = (bf16[16,8,16,256]{3,2,1,0:T(8,128)(2,1)S(1)}, bf16[18,10,16,256]{3,2,1,0:T(8,128)(2,1)S(1)}, bf16[768,2560]{1,0:T(8,128)(2,1)S(1)}, bf16[288,256]{1,0:T(8,128)(2,1)S(1)}) custom-call(s32[1]{0:T(128)S(6)} %copy.29.count_ref, bf16[16,128,256]{2,1,0:T(8,128)(2,1)S(1)} %bitcast.11, bf16[128,256]{1,0:T(8,128)(2,1)S(1)} %edges.1._), custom_call_target="tpu_custom_call" | custom-call | flops 536870912 | bytes 7651332 | tf_op jit(solution)/shard_map/acts/pallas_call | solution.py:426
  7.5 3.7 %collective-permute-start.1 = (bf16[2,8,4,256]{3,2,1,0:T(4,128)(2,1)S(1)}, bf16[2,8,4,256]{3,2,1,0:T(4,128)(2,1)S(1)}, u32[]{:S(2)}, u32[]{:S(2)}) collective-permute-start(bf16[2,8,4,256]{3,2,1,0:T(4,128)(2,1)S(1)} %next.1.rest_3_), channel_id=1, source_target_pairs={{0,30},{2,0},{4,2},{6,4},{8,6},{10,8},{12,10},{14,12},{16,14},{18,... | collective-permute-start | bytes 98312 | tf_op jit(solution)/shard_map/ppermute | solution.py:499
  11.3 0.2 halo.1
  11.5 1.4 %collective-permute-done.1.nxt_ref = bf16[2,8,4,256]{3,2,1,0:T(4,128)(2,1)S(1)} collective-permute-done((bf16[2,8,4,256]{3,2,1,0:T(4,128)(2,1)S(1)}, bf16[2,8,4,256]{3,2,1,0:T(4,128)(2,1)S(1)}, u32[]{:S(2)}, u32[]{:S(2)}) %collective-permute-start.1) | collective-permute-done | bytes 32800 | tf_op jit(solution)/shard_map/ppermute | solution.py:499
  12.9 4.5 %grad_spatial.1 = (bf16[8,4,16,256]{3,2,1,0:T(8,128)(2,1)S(1)}, bf16[16,8,16,256]{3,2,1,0:T(8,128)(2,1)S(1)}, bf16[16,10,16,256]{3,2,1,0:T(8,128)(2,1)S(1)}, bf1...) custom-call(s32[1]{0:T(128)S(6)} %copy.29.count_ref, ...), custom_call_target="tpu_custom_call" | custom-call | flops 3758096384 | bytes 8978436 | tf_op jit(solution)/shard_map/grad_spatial/pallas_call | solution.py:426
  17.4 1.3 %collective-permute-done.3.__1_.prev_ref = bf16[288,256]{1,0:T(8,128)(2,1)S(1)} collective-permute-done((bf16[288,256]{1,0:T(8,128)(2,1)S(1)}, bf16[288,256]{1,0:T(8,128)(2,1)S(1)}, u32[]{:S(2)}, u32[]{:S(2)}) %collective-permute-start.3) | collective-permute-done | bytes 147488 | tf_op jit(solution)/shard_map/ppermute | solution.py:499
  18.7 2.0 %spatial_upper.1 = (bf16[18,10,16,256]{3,2,1,0:T(8,128)(2,1)S(1)}, bf16[8,8,16,256]{3,2,1,0:T(8,128)(2,1)S(1)}) custom-call(bf16[18,10,16,256]{3,2,1,0:T(8,128)(2,1)S(1)} %get-tuple-element.52.acts_in, bf16[288,256]{1,0:T(8,128)(2,1)S(1)} %collective-permute-done.3.__1_.prev_ref, bf16[9,256,256]{2,1,0:T(8,128)(2,1)S(1)} %bitcast.12, ...), custom_call_target="tpu_custom_call", output_to_operand_aliasing={{0}: (0, {})} | custom-call | flops 1342177280 | bytes 4800512 | tf_op jit(solution)/shard_map/spatial_upper/pallas_call | solution.py:426
  20.8 0.2 plane_send.2
  20.9 0.1 collective-permute-start.5
  21.0 1.6 %spatial_lower.1.lower_ref = bf16[8,8,16,256]{3,2,1,0:T(8,128)(2,1)S(1)} custom-call(bf16[18,10,16,256]{3,2,1,0:T(8,128)(2,1)S(1)} %get-tuple-element.56.acts_ref, bf16[9,256,256]{2,1,0:T(8,128)(2,1)S(1)} %bitcast.13, bf16[4,9,16,128]{3,2,1,0:T(8,128)(2,1)S(1)} %get-tuple-element.58.rest_0_.refs_0_, bf16[4,9,16,128]{3,2,1,0:T(8,128)(2,1)S(1)} %get-tuple-element.59.rest_1_, ...), custom_call_target="tpu_custom_call" | custom-call | flops 1073741824 | bytes 3178496 | tf_op jit(solution)/shard_map/spatial_lower/pallas_call | solution.py:426
  22.6 2.4 %forward.1 = (bf16[512,256]{1,0:T(8,128)(2,1)S(1)}, bf16[16,7,16,128]{3,2,1,0:T(8,128)(2,1)S(1)}, bf16[16,7,16,128]{3,2,1,0:T(8,128)(2,1)S(1)}) custom-call(s32[1]{0:T(128)S(6)} %copy.29.count_ref, bf16[16,8,16,256]{3,2,1,0:T(8,128)(2,1)S(1)} %get-tuple-element.44.xt_ref, bf16[8,8,16,256]{3,2,1,0:T(8,128)(2,1)S(1)} %get-tuple-element.55.rest_0_.upper_ref, ...), custom_call_target="tpu_custom_call" | custom-call | bytes 1024 | tf_op jit(solution)/shard_map/forward/pallas_call | solution.py:426
  24.9 3.2 %collective-permute-done.5.__1_.refs_1_ = bf16[4,9,16,128]{3,2,1,0:T(8,128)(2,1)S(1)} collective-permute-done((bf16[4,9,16,128]{3,2,1,0:T(8,128)(2,1)S(1)}, bf16[4,9,16,128]{3,2,1,0:T(8,128)(2,1)S(1)}, u32[]{:S(2)}, u32[]{:S(2)}) %collective-permute-start.5) | collective-permute-done | bytes 147488 | tf_op jit(solution)/shard_map/ppermute | solution.py:450
  28.1 0.5 collective-permute-start.6
  28.6 0.3 collective-permute-start.7
  29.0 1.0 %collective-permute-done.8.got_ref = bf16[16,7,16,128]{3,2,1,0:T(8,128)(2,1)S(1)} collective-permute-done((bf16[16,7,16,128]{3,2,1,0:T(8,128)(2,1)S(1)}, bf16[16,7,16,128]{3,2,1,0:T(8,128)(2,1)S(1)}, u32[]{:S(2)}, u32[]{:S(2)}) %collective-permute-start.8) | collective-permute-done | bytes 458784 | tf_op jit(solution)/shard_map/ppermute | solution.py:450
  29.9 0.1 plane_send.3
  30.1 1.7 %collective-permute-start.9 = (bf16[4,7,16,128]{3,2,1,0:T(8,128)(2,1)S(1)}, bf16[4,7,16,128]{3,2,1,0:T(8,128)(2,1)S(1)}, u32[]{:S(2)}, u32[]{:S(2)}) collective-permute-start(bf16[4,7,16,128]{3,2,1,0:T(8,128)(2,1)S(1)} %get-tuple-element.67), channel_id=1, source_target_pairs={{0,5},{1,4},{2,7},{3,6},{4,1},{5,0},{6,3},{7,2},{8,13},{9,12},{10,... | collective-permute-start | bytes 344072 | tf_op jit(solution)/shard_map/ppermute | solution.py:450
  31.8 0.5 collective-permute-start.10
  32.3 1.3 %collective-permute-start.11 = (bf16[4,7,16,128]{3,2,1,0:T(8,128)(2,1)S(1)}, bf16[4,7,16,128]{3,2,1,0:T(8,128)(2,1)S(1)}, u32[]{:S(2)}, u32[]{:S(2)}) collective-permute-start(bf16[4,7,16,128]{3,2,1,0:T(8,128)(2,1)S(1)} %get-tuple-element.69), channel_id=1, source_target_pairs={{0,4},{1,5},{2,6},{3,7},{4,0},{5,1},{6,2},{7,3},{8,12},{9,13},{10,... | collective-permute-start | bytes 344072 | tf_op jit(solution)/shard_map/ppermute | solution.py:450
  33.6 1.0 %collective-permute-done.6.refs_2_ = bf16[4,9,16,128]{3,2,1,0:T(8,128)(2,1)S(1)} collective-permute-done((bf16[4,9,16,128]{3,2,1,0:T(8,128)(2,1)S(1)}, bf16[4,9,16,128]{3,2,1,0:T(8,128)(2,1)S(1)}, u32[]{:S(2)}, u32[]{:S(2)}) %collective-permute-start.6) | collective-permute-done | bytes 147488 | tf_op jit(solution)/shard_map/ppermute | solution.py:450
  34.7 0.7 collective-permute-done.7.refs_3_
  35.3 3.5 %collective-permute-done.9.refs_5_ = bf16[4,7,16,128]{3,2,1,0:T(8,128)(2,1)S(1)} collective-permute-done((bf16[4,7,16,128]{3,2,1,0:T(8,128)(2,1)S(1)}, bf16[4,7,16,128]{3,2,1,0:T(8,128)(2,1)S(1)}, u32[]{:S(2)}, u32[]{:S(2)}) %collective-permute-start.9) | collective-permute-done | bytes 114720 | tf_op jit(solution)/shard_map/ppermute | solution.py:450
  38.8 0.5 collective-permute-done.10.refs_6_
  39.3 0.3 collective-permute-done.11.refs_7_
  39.6 0.1 line_send.1
  39.7 2.2 %collective-permute-start.12 = (bf16[16,16,128]{2,1,0:T(8,128)(2,1)S(1)}, bf16[16,16,128]{2,1,0:T(8,128)(2,1)S(1)}, u32[]{:S(2)}, u32[]{:S(2)}) collective-permute-start(bf16[16,16,128]{2,1,0:T(8,128)(2,1)S(1)} %get-tuple-element.71), channel_id=1, source_target_pairs={{0,24},{1,25},{2,26},{3,27},{4,28},{5,29},{6,30},{7,31},{8,16},{9,... | collective-permute-start | bytes 196616 | tf_op jit(solution)/shard_map/ppermute | solution.py:450
  41.9 2.3 %collective-permute-start.14 = (bf16[16,16,128]{2,1,0:T(8,128)(2,1)S(1)}, bf16[16,16,128]{2,1,0:T(8,128)(2,1)S(1)}, u32[]{:S(2)}, u32[]{:S(2)}) collective-permute-start(bf16[16,16,128]{2,1,0:T(8,128)(2,1)S(1)} %get-tuple-element.73), channel_id=1, source_target_pairs={{0,8},{1,9},{2,10},{3,11},{4,12},{5,13},{6,14},{7,15},{8,0},{9,1},... | collective-permute-start | bytes 196616 | tf_op jit(solution)/shard_map/ppermute | solution.py:450
  44.2 1.7 %collective-permute-done.12.b_ref = bf16[16,16,128]{2,1,0:T(8,128)(2,1)S(1)} collective-permute-done((bf16[16,16,128]{2,1,0:T(8,128)(2,1)S(1)}, bf16[16,16,128]{2,1,0:T(8,128)(2,1)S(1)}, u32[]{:S(2)}, u32[]{:S(2)}) %collective-permute-start.12) | collective-permute-done | bytes 65568 | tf_op jit(solution)/shard_map/ppermute | solution.py:450
  45.9 1.9 %collective-permute-done.13.c_ref = bf16[16,16,128]{2,1,0:T(8,128)(2,1)S(1)} collective-permute-done((bf16[16,16,128]{2,1,0:T(8,128)(2,1)S(1)}, bf16[16,16,128]{2,1,0:T(8,128)(2,1)S(1)}, u32[]{:S(2)}, u32[]{:S(2)}) %collective-permute-start.13) | collective-permute-done | bytes 65568 | tf_op jit(solution)/shard_map/ppermute | solution.py:450
  47.8 0.7 collective-permute-start.17
  48.5 2.2 %collective-permute-start.16 = (bf16[16,16,128]{2,1,0:T(8,128)(2,1)S(1)}, bf16[16,16,128]{2,1,0:T(8,128)(2,1)S(1)}, u32[]{:S(2)}, u32[]{:S(2)}) collective-permute-start(bf16[16,16,128]{2,1,0:T(8,128)(2,1)S(1)} %line_sum.1.a_ref), channel_id=1, source_target_pairs={{0,16},{1,17},{2,18},{3,19},{4,20},{5,21},{6,22},{7,23},{8,24},{9,... | collective-permute-start | bytes 196616 | tf_op jit(solution)/shard_map/ppermute | solution.py:450
  50.7 1.6 %collective-permute-start.15 = (bf16[16,16,128]{2,1,0:T(8,128)(2,1)S(1)}, bf16[16,16,128]{2,1,0:T(8,128)(2,1)S(1)}, u32[]{:S(2)}, u32[]{:S(2)}) collective-permute-start(bf16[16,16,128]{2,1,0:T(8,128)(2,1)S(1)} %line_sum.1.a_ref), channel_id=1, source_target_pairs={{0,24},{1,25},{2,26},{3,27},{4,28},{5,29},{6,30},{7,31},{8,16},{9,... | collective-permute-start | bytes 196616 | tf_op jit(solution)/shard_map/ppermute | solution.py:450
  52.3 1.5 %collective-permute-start.2 = (bf16[64,256]{1,0:T(8,128)(2,1)S(1)}, bf16[64,256]{1,0:T(8,128)(2,1)S(1)}, u32[]{:S(2)}, u32[]{:S(2)}) collective-permute-start(bf16[64,256]{1,0:T(8,128)(2,1)S(1)} %get-tuple-element.51), channel_id=1, source_target_pairs={{0,1},{1,0},{2,3},{3,2},{4,5},{5,4},{6,7},{7,6},{8,9},{9,8},{10,11... | collective-permute-start | bytes 98312 | tf_op jit(solution)/shard_map/ppermute | solution.py:504
  53.8 2.0 %collective-permute-done.16.c_ref = bf16[16,16,128]{2,1,0:T(8,128)(2,1)S(1)} collective-permute-done((bf16[16,16,128]{2,1,0:T(8,128)(2,1)S(1)}, bf16[16,16,128]{2,1,0:T(8,128)(2,1)S(1)}, u32[]{:S(2)}, u32[]{:S(2)}) %collective-permute-start.16) | collective-permute-done | bytes 65568 | tf_op jit(solution)/shard_map/ppermute | solution.py:450
  55.8 1.1 %collective-permute-done.15.b_ref = bf16[16,16,128]{2,1,0:T(8,128)(2,1)S(1)} collective-permute-done((bf16[16,16,128]{2,1,0:T(8,128)(2,1)S(1)}, bf16[16,16,128]{2,1,0:T(8,128)(2,1)S(1)}, u32[]{:S(2)}, u32[]{:S(2)}) %collective-permute-start.15) | collective-permute-done | bytes 65568 | tf_op jit(solution)/shard_map/ppermute | solution.py:450
  56.9 0.8 %collective-permute-start.20 = (bf16[4,16,16,128]{3,2,1,0:T(8,128)(2,1)S(1)}, bf16[4,16,16,128]{3,2,1,0:T(8,128)(2,1)S(1)}, u32[]{:S(2)}, u32[]{:S(2)}) collective-permute-start(bf16[4,16,16,128]{3,2,1,0:T(8,128)(2,1)S(1)} %line_gather.1.rest_0_.a_ref), channel_id=1, source_target_pairs={{0,4},{1,5},{2,6},{3,7},{4,0},{5,1},{6,2},{7,3},{8,12},{9,13},{10,... | collective-permute-start | bytes 786440 | tf_op jit(solution)/shard_map/ppermute | solution.py:450
  57.8 1.6 %collective-permute-start.19 = (bf16[4,16,16,128]{3,2,1,0:T(8,128)(2,1)S(1)}, bf16[4,16,16,128]{3,2,1,0:T(8,128)(2,1)S(1)}, u32[]{:S(2)}, u32[]{:S(2)}) collective-permute-start(bf16[4,16,16,128]{3,2,1,0:T(8,128)(2,1)S(1)} %line_gather.1.rest_0_.a_ref), channel_id=1, source_target_pairs={{0,1},{1,0},{2,3},{3,2},{4,5},{5,4},{6,7},{7,6},{8,9},{9,8},{10,11... | collective-permute-start | bytes 786440 | tf_op jit(solution)/shard_map/ppermute | solution.py:450
  59.4 1.1 %collective-permute-start.18 = (bf16[4,16,16,128]{3,2,1,0:T(8,128)(2,1)S(1)}, bf16[4,16,16,128]{3,2,1,0:T(8,128)(2,1)S(1)}, u32[]{:S(2)}, u32[]{:S(2)}) collective-permute-start(bf16[4,16,16,128]{3,2,1,0:T(8,128)(2,1)S(1)} %line_gather.1.rest_0_.a_ref), channel_id=1, source_target_pairs={{0,5},{1,4},{2,7},{3,6},{4,1},{5,0},{6,3},{7,2},{8,13},{9,12},{10,... | collective-permute-start | bytes 786440 | tf_op jit(solution)/shard_map/ppermute | solution.py:450
  60.5 7.4 %grad_x.1 = (bf16[16,128,256]{2,1,0:T(8,128)(2,1)}, bf16[16,8,4,256]{3,2,1,0:T(4,128)(2,1)}, f32[8,128]{1,0:T(8,128)S(1)}) custom-call(s32[1]{0:T(128)S(6)} %copy.29.count_ref, bf16[16,8,16,256]{3,2,1,0:T(8,128)(2,1)S(1)} %get-tuple-element.44.xt_ref, bf16[16,8,16,256]{3,2,1,0:T(8,128)(2,1)S(1)} %get-tuple-element.49.gy_ref, ...), custom_call_target="tpu_custom_call" | custom-call | flops 2684354560 | bytes 7147524 | tf_op jit(solution)/shard_map/grad_x/pallas_call | solution.py:426
  67.9 0.5 collective-permute-done.19.c_ref
  68.4 1.5 %collective-permute-done.18.b_ref = bf16[4,16,16,128]{3,2,1,0:T(8,128)(2,1)S(1)} collective-permute-done((bf16[4,16,16,128]{3,2,1,0:T(8,128)(2,1)S(1)}, bf16[4,16,16,128]{3,2,1,0:T(8,128)(2,1)S(1)}, u32[]{:S(2)}, u32[]{:S(2)}) %collective-permute-start.18) | collective-permute-done | bytes 262176 | tf_op jit(solution)/shard_map/ppermute | solution.py:450
  69.9 0.1 plane_gather.1.half_ref
  70.1 1.5 %finish.2 = (f32[9,256,256]{2,1,0:T(8,128)}, f32[3,256,256]{2,1,0:T(8,128)}, f32[4,256,256]{2,1,0:T(8,128)}) custom-call(bf16[16,16,16,128]{3,2,1,0:T(8,128)(2,1)S(1)} %plane_gather.1.half_ref), custom_call_target="tpu_custom_call" | custom-call | bytes 5242880 | tf_op jit(solution)/shard_map/finish/pallas_call | solution.py:426
  71.6 1.2 %collective-permute-done.21.half_ref = bf16[16,16,16,128]{3,2,1,0:T(8,128)(2,1)S(1)} collective-permute-done((bf16[16,16,16,128]{3,2,1,0:T(8,128)(2,1)S(1)}, bf16[16,16,16,128]{3,2,1,0:T(8,128)(2,1)S(1)}, u32[]{:S(2)}, u32[]{:S(2)}) %collective-permute-start.21) | collective-permute-done | bytes 1048608 | tf_op jit(solution)/shard_map/ppermute | solution.py:450
  72.8 1.5 %finish.3 = (f32[9,256,256]{2,1,0:T(8,128)}, f32[3,256,256]{2,1,0:T(8,128)}, f32[4,256,256]{2,1,0:T(8,128)}) custom-call(bf16[16,16,16,128]{3,2,1,0:T(8,128)(2,1)S(1)} %collective-permute-done.21.half_ref, f32[9,256,256]{2,1,0:T(8,128)} %get-tuple-element.77.rest_0_, ...), custom_call_target="tpu_custom_call", output_to_operand_aliasing={{0}: (1, {}), {1}: (2, {}), {2}: (3, {})} | custom-call | bytes 9437184 | tf_op jit(solution)/shard_map/finish/pallas_call | solution.py:426
  (25 shorter events, 0.2 us)
Async XLA Ops:
  1.3 1.2 %copy-start.3 = (bf16[16,16,8,256]{3,2,1,0:T(8,128)(2,1)S(1)}, bf16[16,16,8,256]{3,2,1,0:T(8,128)(2,1)}, u32[]{:S(2)}) copy-start(bf16[16,16,8,256]{3,2,1,0:T(8,128)(2,1)} %param.6) | copy-start | bytes 3145732
  2.5 5.0 %copy-start.2 = (bf16[16,8,4,256]{3,2,1,0:T(4,128)(2,1)S(1)}, bf16[16,8,4,256]{3,2,1,0:T(4,128)(2,1)}, u32[]{:S(2)}) copy-start(bf16[16,8,4,256]{3,2,1,0:T(4,128)(2,1)} %cot_ref.3) | copy-start | bytes 786436
  2.8 8.5 %copy-start = (bf16[2,2,256,256]{3,2,1,0:T(8,128)(2,1)S(1)}, bf16[2,2,256,256]{3,2,1,0:T(8,128)(2,1)}, u32[]{:S(2)}) copy-start(bf16[2,2,256,256]{3,2,1,0:T(8,128)(2,1)} %param.10) | copy-start | bytes 1572868
  2.8 8.5 %copy-start.1 = (bf16[3,256,256]{2,1,0:T(8,128)(2,1)S(1)}, bf16[3,256,256]{2,1,0:T(8,128)(2,1)}, u32[]{:S(2)}) copy-start(bf16[3,256,256]{2,1,0:T(8,128)(2,1)} %wt_ref.5) | copy-start | bytes 1179652
  2.8 8.4 %collective-permute-start = (bf16[128,256]{1,0:T(8,128)(2,1)S(1)}, bf16[128,256]{1,0:T(8,128)(2,1)S(1)}, u32[]{:S(2)}, u32[]{:S(2)}) collective-permute-start(bf16[128,256]{1,0:T(8,128)(2,1)S(1)} %edges.1._), channel_id=1, source_target_pairs={{0,1},{1,0},{2,3},{3,2},{4,5},{5,4},{6,7},{7,6},{8,9},{9,8},{10,11... | collective-permute-start | bytes 196616 | tf_op jit(solution)/shard_map/ppermute | solution.py:504
  7.5 5.3 %collective-permute-start.1 = (bf16[2,8,4,256]{3,2,1,0:T(4,128)(2,1)S(1)}, bf16[2,8,4,256]{3,2,1,0:T(4,128)(2,1)S(1)}, u32[]{:S(2)}, u32[]{:S(2)}) collective-permute-start(bf16[2,8,4,256]{3,2,1,0:T(4,128)(2,1)S(1)} %next.1.rest_3_), channel_id=1, source_target_pairs={{0,30},{2,0},{4,2},{6,4},{8,6},{10,8},{12,10},{14,12},{16,14},{18,... | collective-permute-start | bytes 98312 | tf_op jit(solution)/shard_map/ppermute | solution.py:499
  11.4 7.3 %collective-permute-start.3 = (bf16[288,256]{1,0:T(8,128)(2,1)S(1)}, bf16[288,256]{1,0:T(8,128)(2,1)S(1)}, u32[]{:S(2)}, u32[]{:S(2)}) collective-permute-start(bf16[288,256]{1,0:T(8,128)(2,1)S(1)} %get-tuple-element.53), channel_id=1, source_target_pairs={{0,2},{2,4},{4,6},{6,8},{8,10},{10,12},{12,14},{14,16},{16,18},{18... | collective-permute-start | bytes 442376 | tf_op jit(solution)/shard_map/ppermute | solution.py:499
  12.9 5.9 %copy-start.4 = (bf16[3,3,256,256]{3,2,1,0:T(8,128)(2,1)S(1)}, bf16[3,3,256,256]{3,2,1,0:T(8,128)(2,1)}, u32[]{:S(2)}) copy-start(bf16[3,3,256,256]{3,2,1,0:T(8,128)(2,1)} %param.8) | copy-start | bytes 3538948
  18.7 2.0 %collective-permute-start.4 = (bf16[16,9,16,128]{3,2,1,0:T(8,128)(2,1)S(1)}, bf16[16,9,16,128]{3,2,1,0:T(8,128)(2,1)S(1)}, u32[]{:S(2)}, u32[]{:S(2)}) collective-permute-start(bf16[16,9,16,128]{3,2,1,0:T(8,128)(2,1)S(1)} %pass.2._), channel_id=1, source_target_pairs={{0,2},{1,3},{2,0},{3,1},{4,6},{5,7},{6,4},{7,5},{8,10},{9,11},{10,... | collective-permute-start | bytes 1769480 | tf_op jit(solution)/shard_map/ppermute | solution.py:450
  20.9 7.2 %collective-permute-start.5 = (bf16[4,9,16,128]{3,2,1,0:T(8,128)(2,1)S(1)}, bf16[4,9,16,128]{3,2,1,0:T(8,128)(2,1)S(1)}, u32[]{:S(2)}, u32[]{:S(2)}) collective-permute-start(bf16[4,9,16,128]{3,2,1,0:T(8,128)(2,1)S(1)} %get-tuple-element.59.rest_1_), channel_id=1, source_target_pairs={{0,5},{1,4},{2,7},{3,6},{4,1},{5,0},{6,3},{7,2},{8,13},{9,12},{10,... | collective-permute-start | bytes 442376 | tf_op jit(solution)/shard_map/ppermute | solution.py:450
  28.1 1.8 %collective-permute-start.8 = (bf16[16,7,16,128]{3,2,1,0:T(8,128)(2,1)S(1)}, bf16[16,7,16,128]{3,2,1,0:T(8,128)(2,1)S(1)}, u32[]{:S(2)}, u32[]{:S(2)}) collective-permute-start(bf16[16,7,16,128]{3,2,1,0:T(8,128)(2,1)S(1)} %pass.3), channel_id=1, source_target_pairs={{0,2},{1,3},{2,0},{3,1},{4,6},{5,7},{6,4},{7,5},{8,10},{9,11},{10,... | collective-permute-start | bytes 1376264 | tf_op jit(solution)/shard_map/ppermute | solution.py:450
  28.1 6.5 %collective-permute-start.6 = (bf16[4,9,16,128]{3,2,1,0:T(8,128)(2,1)S(1)}, bf16[4,9,16,128]{3,2,1,0:T(8,128)(2,1)S(1)}, u32[]{:S(2)}, u32[]{:S(2)}) collective-permute-start(bf16[4,9,16,128]{3,2,1,0:T(8,128)(2,1)S(1)} %get-tuple-element.60.rest_2_), channel_id=1, source_target_pairs={{0,1},{1,0},{2,3},{3,2},{4,5},{5,4},{6,7},{7,6},{8,9},{9,8},{10,11... | collective-permute-start | bytes 442376 | tf_op jit(solution)/shard_map/ppermute | solution.py:450
  28.6 6.7 %collective-permute-start.7 = (bf16[4,9,16,128]{3,2,1,0:T(8,128)(2,1)S(1)}, bf16[4,9,16,128]{3,2,1,0:T(8,128)(2,1)S(1)}, u32[]{:S(2)}, u32[]{:S(2)}) collective-permute-start(bf16[4,9,16,128]{3,2,1,0:T(8,128)(2,1)S(1)} %get-tuple-element.61.rest_3_), channel_id=1, source_target_pairs={{0,4},{1,5},{2,6},{3,7},{4,0},{5,1},{6,2},{7,3},{8,12},{9,13},{10,... | collective-permute-start | bytes 442376 | tf_op jit(solution)/shard_map/ppermute | solution.py:450
  30.1 8.7 %collective-permute-start.9 = (bf16[4,7,16,128]{3,2,1,0:T(8,128)(2,1)S(1)}, bf16[4,7,16,128]{3,2,1,0:T(8,128)(2,1)S(1)}, u32[]{:S(2)}, u32[]{:S(2)}) collective-permute-start(bf16[4,7,16,128]{3,2,1,0:T(8,128)(2,1)S(1)} %get-tuple-element.67), channel_id=1, source_target_pairs={{0,5},{1,4},{2,7},{3,6},{4,1},{5,0},{6,3},{7,2},{8,13},{9,12},{10,... | collective-permute-start | bytes 344072 | tf_op jit(solution)/shard_map/ppermute | solution.py:450
  31.8 7.5 %collective-permute-start.10 = (bf16[4,7,16,128]{3,2,1,0:T(8,128)(2,1)S(1)}, bf16[4,7,16,128]{3,2,1,0:T(8,128)(2,1)S(1)}, u32[]{:S(2)}, u32[]{:S(2)}) collective-permute-start(bf16[4,7,16,128]{3,2,1,0:T(8,128)(2,1)S(1)} %get-tuple-element.68), channel_id=1, source_target_pairs={{0,1},{1,0},{2,3},{3,2},{4,5},{5,4},{6,7},{7,6},{8,9},{9,8},{10,11... | collective-permute-start | bytes 344072 | tf_op jit(solution)/shard_map/ppermute | solution.py:450
  32.3 7.3 %collective-permute-start.11 = (bf16[4,7,16,128]{3,2,1,0:T(8,128)(2,1)S(1)}, bf16[4,7,16,128]{3,2,1,0:T(8,128)(2,1)S(1)}, u32[]{:S(2)}, u32[]{:S(2)}) collective-permute-start(bf16[4,7,16,128]{3,2,1,0:T(8,128)(2,1)S(1)} %get-tuple-element.69), channel_id=1, source_target_pairs={{0,4},{1,5},{2,6},{3,7},{4,0},{5,1},{6,2},{7,3},{8,12},{9,13},{10,... | collective-permute-start | bytes 344072 | tf_op jit(solution)/shard_map/ppermute | solution.py:450
  39.7 6.2 %collective-permute-start.12 = (bf16[16,16,128]{2,1,0:T(8,128)(2,1)S(1)}, bf16[16,16,128]{2,1,0:T(8,128)(2,1)S(1)}, u32[]{:S(2)}, u32[]{:S(2)}) collective-permute-start(bf16[16,16,128]{2,1,0:T(8,128)(2,1)S(1)} %get-tuple-element.71), channel_id=1, source_target_pairs={{0,24},{1,25},{2,26},{3,27},{4,28},{5,29},{6,30},{7,31},{8,16},{9,... | collective-permute-start | bytes 196616 | tf_op jit(solution)/shard_map/ppermute | solution.py:450
  41.9 5.9 %collective-permute-start.13 = (bf16[16,16,128]{2,1,0:T(8,128)(2,1)S(1)}, bf16[16,16,128]{2,1,0:T(8,128)(2,1)S(1)}, u32[]{:S(2)}, u32[]{:S(2)}) collective-permute-start(bf16[16,16,128]{2,1,0:T(8,128)(2,1)S(1)} %get-tuple-element.72), channel_id=1, source_target_pairs={{0,16},{1,17},{2,18},{3,19},{4,20},{5,21},{6,22},{7,23},{8,24},{9,... | collective-permute-start | bytes 196616 | tf_op jit(solution)/shard_map/ppermute | solution.py:450
  41.9 5.9 %collective-permute-start.14 = (bf16[16,16,128]{2,1,0:T(8,128)(2,1)S(1)}, bf16[16,16,128]{2,1,0:T(8,128)(2,1)S(1)}, u32[]{:S(2)}, u32[]{:S(2)}) collective-permute-start(bf16[16,16,128]{2,1,0:T(8,128)(2,1)S(1)} %get-tuple-element.73), channel_id=1, source_target_pairs={{0,8},{1,9},{2,10},{3,11},{4,12},{5,13},{6,14},{7,15},{8,0},{9,1},... | collective-permute-start | bytes 196616 | tf_op jit(solution)/shard_map/ppermute | solution.py:450
  47.8 6.0 %collective-permute-start.17 = (bf16[16,16,128]{2,1,0:T(8,128)(2,1)S(1)}, bf16[16,16,128]{2,1,0:T(8,128)(2,1)S(1)}, u32[]{:S(2)}, u32[]{:S(2)}) collective-permute-start(bf16[16,16,128]{2,1,0:T(8,128)(2,1)S(1)} %line_sum.1.a_ref), channel_id=1, source_target_pairs={{0,8},{1,9},{2,10},{3,11},{4,12},{5,13},{6,14},{7,15},{8,0},{9,1},... | collective-permute-start | bytes 196616 | tf_op jit(solution)/shard_map/ppermute | solution.py:450
  48.5 7.2 %collective-permute-start.16 = (bf16[16,16,128]{2,1,0:T(8,128)(2,1)S(1)}, bf16[16,16,128]{2,1,0:T(8,128)(2,1)S(1)}, u32[]{:S(2)}, u32[]{:S(2)}) collective-permute-start(bf16[16,16,128]{2,1,0:T(8,128)(2,1)S(1)} %line_sum.1.a_ref), channel_id=1, source_target_pairs={{0,16},{1,17},{2,18},{3,19},{4,20},{5,21},{6,22},{7,23},{8,24},{9,... | collective-permute-start | bytes 196616 | tf_op jit(solution)/shard_map/ppermute | solution.py:450
  50.7 6.2 %collective-permute-start.15 = (bf16[16,16,128]{2,1,0:T(8,128)(2,1)S(1)}, bf16[16,16,128]{2,1,0:T(8,128)(2,1)S(1)}, u32[]{:S(2)}, u32[]{:S(2)}) collective-permute-start(bf16[16,16,128]{2,1,0:T(8,128)(2,1)S(1)} %line_sum.1.a_ref), channel_id=1, source_target_pairs={{0,24},{1,25},{2,26},{3,27},{4,28},{5,29},{6,30},{7,31},{8,16},{9,... | collective-permute-start | bytes 196616 | tf_op jit(solution)/shard_map/ppermute | solution.py:450
  52.3 8.2 %collective-permute-start.2 = (bf16[64,256]{1,0:T(8,128)(2,1)S(1)}, bf16[64,256]{1,0:T(8,128)(2,1)S(1)}, u32[]{:S(2)}, u32[]{:S(2)}) collective-permute-start(bf16[64,256]{1,0:T(8,128)(2,1)S(1)} %get-tuple-element.51), channel_id=1, source_target_pairs={{0,1},{1,0},{2,3},{3,2},{4,5},{5,4},{6,7},{7,6},{8,9},{9,8},{10,11... | collective-permute-start | bytes 98312 | tf_op jit(solution)/shard_map/ppermute | solution.py:504
  56.9 11.0 %collective-permute-start.20 = (bf16[4,16,16,128]{3,2,1,0:T(8,128)(2,1)S(1)}, bf16[4,16,16,128]{3,2,1,0:T(8,128)(2,1)S(1)}, u32[]{:S(2)}, u32[]{:S(2)}) collective-permute-start(bf16[4,16,16,128]{3,2,1,0:T(8,128)(2,1)S(1)} %line_gather.1.rest_0_.a_ref), channel_id=1, source_target_pairs={{0,4},{1,5},{2,6},{3,7},{4,0},{5,1},{6,2},{7,3},{8,12},{9,13},{10,... | collective-permute-start | bytes 786440 | tf_op jit(solution)/shard_map/ppermute | solution.py:450
  57.8 10.7 %collective-permute-start.19 = (bf16[4,16,16,128]{3,2,1,0:T(8,128)(2,1)S(1)}, bf16[4,16,16,128]{3,2,1,0:T(8,128)(2,1)S(1)}, u32[]{:S(2)}, u32[]{:S(2)}) collective-permute-start(bf16[4,16,16,128]{3,2,1,0:T(8,128)(2,1)S(1)} %line_gather.1.rest_0_.a_ref), channel_id=1, source_target_pairs={{0,1},{1,0},{2,3},{3,2},{4,5},{5,4},{6,7},{7,6},{8,9},{9,8},{10,11... | collective-permute-start | bytes 786440 | tf_op jit(solution)/shard_map/ppermute | solution.py:450
  59.4 10.5 %collective-permute-start.18 = (bf16[4,16,16,128]{3,2,1,0:T(8,128)(2,1)S(1)}, bf16[4,16,16,128]{3,2,1,0:T(8,128)(2,1)S(1)}, u32[]{:S(2)}, u32[]{:S(2)}) collective-permute-start(bf16[4,16,16,128]{3,2,1,0:T(8,128)(2,1)S(1)} %line_gather.1.rest_0_.a_ref), channel_id=1, source_target_pairs={{0,5},{1,4},{2,7},{3,6},{4,1},{5,0},{6,3},{7,2},{8,13},{9,12},{10,... | collective-permute-start | bytes 786440 | tf_op jit(solution)/shard_map/ppermute | solution.py:450
  70.0 2.7 %collective-permute-start.21 = (bf16[16,16,16,128]{3,2,1,0:T(8,128)(2,1)S(1)}, bf16[16,16,16,128]{3,2,1,0:T(8,128)(2,1)S(1)}, u32[]{:S(2)}, u32[]{:S(2)}) collective-permute-start(bf16[16,16,16,128]{3,2,1,0:T(8,128)(2,1)S(1)} %plane_gather.1.half_ref), channel_id=1, source_target_pairs={{0,2},{1,3},{2,0},{3,1},{4,6},{5,7},{6,4},{7,5},{8,10},{9,11},{10,... | collective-permute-start | bytes 3145736 | tf_op jit(solution)/shard_map/ppermute | solution.py:450

commit v19 on v18

--- a/solution.py
+++ b/solution.py
@@ -57,6 +57,10 @@
 def silu_norm(v):
     scaled = v * lax.rsqrt(jnp.mean(v * v, axis=-1, keepdims=True) + 1e-06)
     return scaled * (0.5 + 0.5 * jnp.tanh(0.5 * scaled))
+
+
+def pick_of(flag, a, b):
+    return jnp.where(flag, a.astype(F32), b.astype(F32)).astype(BF)
 
 
 def slot_mask(shape, count):
@@ -167,18 +171,23 @@
     lax.fori_loop(0, rows // 4, rows_of, 0)
 
 
-def upper_kernel(acts_in, prev_ref, ws_ref, _, acts_ref, sp_ref):
+def upper_kernel(acts_in, inner_ref, outer_ref, ws_ref, _, acts_ref, sp_ref):
     rows, cols = acts_ref.shape[0] - 2, acts_ref.shape[1] - 2
     a, b = iotas(256, 32)
     place = ((a >> 4) == (b & 15)) & ((a & 15) == OWN + (b >> 4)) & (lax.axis_index("tm") > 0)
     place = jnp.where(place, 1.0, 0.0).astype(BF)
     size = rows * cols
+    core, _, _ = place_bits()
+
+    def prev_of(at, n):
+        return pick_of(core == 1, inner_ref[at : at + n], outer_ref[at : at + n])
+
     for q in range(rows // 2 + 1):
         if q == rows // 2:
-            both, prev = slice(0, rows + 2, rows + 1), prev_ref[2 * size :]
+            both, prev = slice(0, rows + 2, rows + 1), prev_of(2 * size, 32)
         else:
             both = slice(2 * q + 1, 2 * q + 3)
-            parts = [prev_ref[f * size + q * 16 : f * size + q * 16 + 16] for f in range(2)]
+            parts = [prev_of(f * size + q * 16, 16) for f in range(2)]
             prev = jnp.concatenate(parts, 0)
         prev = mm(place, prev).astype(BF).reshape(2, cols, SLOTS, CH)
         for k, row in enumerate(range(rows + 2)[both]):
@@ -193,7 +202,7 @@
 
 
 def grad_spatial_kernel(
-    blocks, bands, count_ref, at_ref, cot_ref, nxt_ref, wt_ref, wd_ref,
+    blocks, bands, count_ref, at_ref, cot_ref, inner_ref, outer_ref, wt_ref, wd_ref,
     cott_ref, gy_ref, gs_ref, keep_ref, send_ref, *edge_refs,
 ):
     count = count_ref[0]
@@ -205,10 +214,11 @@
 
     place_next = to_slots(16, SLOTS, own_and_next(count, blocks))
     halves = []
+    core, _, _ = place_bits()
     for q in range(rows * cols // 64):
         four = slice(q * 4, q * 4 + 4)
         piece = jnp.concatenate(
-            [cot_ref[0:OWN, four].reshape(OWN, 16, CH), nxt_ref[:, four].reshape(2, 16, CH)], 0
+            [cot_ref[0:OWN, four].reshape(OWN, 16, CH), pick_of(core == 0, inner_ref[:, four], outer_ref[:, four]).reshape(2, 16, CH)], 0
         ).reshape(SLOTS * 16, CH)
         halves.append(mm(place_next, piece).astype(BF))
     placed = jnp.concatenate(halves, 0)
@@ -494,9 +504,11 @@
     return lax.ppermute(value, axis, pairs)
 
 
-def around(value, axis, by):
-    count = lax.axis_size(axis)
-    return lax.ppermute(value, axis, [(i, (i + by) % count) for i in range(count)])
+def both_neighbours(value):
+    count = lax.axis_size("tm")
+    inner = [(i, i ^ 1) for i in range(count)]
+    outer = [(i, min(max(((i + 1) ^ 1) - 1, 0), count - 1)) for i in range(count)]
+    return lax.ppermute(value, "tm", inner), lax.ppermute(value, "tm", outer)
 
 
 def from_bands(parts):
@@ -544,7 +556,7 @@
         [(VMEM, (2,) + cotangent.shape[1:])],
         moved=1024,
     )
-    nxt_got = around(nxt, "tm", -1)
+    nxt_got = both_neighbours(nxt)
     acts, at, last_two = call(
         functools.partial(halo_kernel, grp),
         "halo",
@@ -554,25 +566,25 @@
         alias={3: 0, 4: 1, 5: 2},
         moved=1024,
     )
-    prev = around(last_two, "tm", 1)
+    prev = both_neighbours(last_two)
     half = (16, 9, 16, ch // 2)
     cott, gy, gs, keep_a, send_a, *edge = call(
         functools.partial(grad_spatial_kernel, tm, grp),
         "grad_spatial",
-        [count, (VMEM, at), (VMEM, cotangent), (VMEM, nxt_got), (VMEM, wt), (VMEM, wd)],
+        [count, (VMEM, at), (VMEM, cotangent), (VMEM, nxt_got[0]), (VMEM, nxt_got[1]), (VMEM, wt), (VMEM, wd)],
         [(VMEM, (rows // 2, cols // 2, slots, ch)), (VMEM, tile),
          (VMEM, (rows, cols + 2, slots, ch)), (VMEM, half), (VMEM, half)]
         + [(VMEM, (cols // 2 * slots, ch))] * sides,
         flops=14 * tap,
     )
-    send_a = passed(send_a, [prev])
+    send_a = passed(send_a, list(prev))
     got_a = core_round(send_a, tm, grp)
     cot_top, cot_bot = from_bands(edge)
     half_tile = (rows // 2, cols, slots, ch)
     acts, upper = call(
         upper_kernel,
         "spatial_upper",
-        [(VMEM, acts), (VMEM, prev), (VMEM, ws), (ANY, send_a)],
+        [(VMEM, acts), (VMEM, prev[0]), (VMEM, prev[1]), (VMEM, ws), (ANY, send_a)],
         [(VMEM, padded), (VMEM, half_tile)],
         flops=5 * tap,
         alias={0: 0},

time: 74.4 us -> 77 us (1.035)
  starting transfers between devices: 25.3 us -> 31.4 us
  waiting for transfers between devices: 22.7 us -> 18 us
  local copies, waits for them, and re-layouts: 1.24 us -> 2.37 us
    ppermute x2 -> x4, starting transfers between devices: 3.74 us -> 7.21 us  [both_neighbours(): return (lax.ppermute(value, 'tm', inner), lax.ppermute(value, 'tm', outer))]
    ppermute x2 -> x4, waiting for transfers between devices: 2.72 us -> 0.01 us  [both_neighbours(): return (lax.ppermute(value, 'tm', inner), lax.ppermute(value, 'tm', outer))]
    ppermute x18, starting transfers between devices: 17 us -> 19.7 us  [swap(): return lax.ppermute(value, AXES, [(d, d ^ flip) for d in range(tm * grp)])]
    ppermute x18, waiting for transfers between devices: 20 us -> 18 us  [swap(): return lax.ppermute(value, AXES, [(d, d ^ flip) for d in range(tm * grp)])]
    unnamed x10, local copies, waits for them, and re-layouts: 1.24 us -> 2.37 us
  transfers between devices with their start and end apart: 22 -> 24, of which waited for: 16 -> 12; matrix products, arithmetic and copies ran while one was open for 0% -> 0% of each run, Pallas kernels for 29% -> 28%
where the time goes in v19:
time: 77 us; the launch traced here: 76.8 us
  starting transfers between devices  31.4 us (41%)
  Pallas kernels  23.5 us (31%)
  waiting for transfers between devices  18 us (23%)
  local copies, waits for them, and re-layouts  2.37 us (3%)
  between operations  1.5 us (2%)
    pallas_call x19, Pallas kernels, call(): pl.pallas_call(kernel, out_shape=shapes, in_specs=[s for s, _ in ins], ou...  23.5 us
    ppermute x18, starting transfers between devices, swap(): return lax.ppermute(value, AXES, [(d, d ^ flip) for d in range(tm * grp)])  19.7 us
    ppermute x18, waiting for transfers between devices, swap(): return lax.ppermute(value, AXES, [(d, d ^ flip) for d in range(tm * grp)])  18 us
    ppermute x4, starting transfers between devices, both_neighbours(): return (lax.ppermute(value, 'tm', inner), lax.ppermute(value, 'tm', outer))  7.21 us
    ppermute x2, starting transfers between devices, from_bands(): got = lax.ppermute(parts[0], 'grp', [(0, 1), (1, 0)])  4.55 us
    unnamed x10, local copies, waits for them, and re-layouts  2.37 us
  transfers between devices with their start and end apart: 24, of which 12 were waited for; matrix products, arithmetic and copies ran while one was open for 0% of the time, Pallas kernels for 28%

profile of v19, /device:TPU:0, one launch (start us, length us, event | category | flops | bytes accessed | tf_op | source)
XLA Modules:
  0.0 76.8 jit_solution(16512278476811380965)
XLA Ops:
  1.3 1.2 %copy-done.3 = bf16[16,16,8,256]{3,2,1,0:T(8,128)(2,1)S(1)} copy-done((bf16[16,16,8,256]{3,2,1,0:T(8,128)(2,1)S(1)}, bf16[16,16,8,256]{3,2,1,0:T(8,128)(2,1)}, u32[]{:S(2)}) %copy-start.3) | copy-done | bytes 1048600
  2.5 0.3 edges.1._
  2.8 3.0 %collective-permute-start = (bf16[128,256]{1,0:T(8,128)(2,1)S(1)}, bf16[128,256]{1,0:T(8,128)(2,1)S(1)}, u32[]{:S(2)}, u32[]{:S(2)}) collective-permute-start(bf16[128,256]{1,0:T(8,128)(2,1)S(1)} %edges.1._), channel_id=1, source_target_pairs={{0,1},{1,0},{2,3},{3,2},{4,5},{5,4},{6,7},{7,6},{8,9},{9,8},{10,11... | collective-permute-start | bytes 196616 | tf_op jit(solution)/shard_map/ppermute | solution.py:516
  5.9 1.6 %acts.1 = (bf16[16,8,16,256]{3,2,1,0:T(8,128)(2,1)S(1)}, bf16[18,10,16,256]{3,2,1,0:T(8,128)(2,1)S(1)}, bf16[768,2560]{1,0:T(8,128)(2,1)S(1)}, bf16[288,256]{1,0:T(8,128)(2,1)S(1)}) custom-call(s32[1]{0:T(128)S(6)} %copy.29.count_ref, bf16[16,128,256]{2,1,0:T(8,128)(2,1)S(1)} %bitcast.11, bf16[128,256]{1,0:T(8,128)(2,1)S(1)} %edges.1._), custom_call_target="tpu_custom_call" | custom-call | flops 536870912 | bytes 7651332 | tf_op jit(solution)/shard_map/acts/pallas_call | solution.py:436
  7.5 0.7 collective-permute-start.2
  8.2 2.9 %collective-permute-start.1 = (bf16[2,8,4,256]{3,2,1,0:T(4,128)(2,1)S(1)}, bf16[2,8,4,256]{3,2,1,0:T(4,128)(2,1)S(1)}, u32[]{:S(2)}, u32[]{:S(2)}) collective-permute-start(bf16[2,8,4,256]{3,2,1,0:T(4,128)(2,1)S(1)} %next.1.rest_3_), channel_id=1, source_target_pairs={{0,2},{2,0},{4,6},{6,4},{8,10},{10,8},{12,14},{14,12},{16,18},{18,... | collective-permute-start | bytes 98312 | tf_op jit(solution)/shard_map/ppermute | solution.py:511
  11.1 0.2 halo.1
  11.3 0.7 collective-permute-start.5
  12.0 3.0 %collective-permute-start.4 = (bf16[288,256]{1,0:T(8,128)(2,1)S(1)}, bf16[288,256]{1,0:T(8,128)(2,1)S(1)}, u32[]{:S(2)}, u32[]{:S(2)}) collective-permute-start(bf16[288,256]{1,0:T(8,128)(2,1)S(1)} %get-tuple-element.53), channel_id=1, source_target_pairs={{0,2},{2,0},{4,6},{6,4},{8,10},{10,8},{12,14},{14,12},{16,18},{18,... | collective-permute-start | bytes 442376 | tf_op jit(solution)/shard_map/ppermute | solution.py:511
  14.9 4.5 %grad_spatial.1 = (bf16[8,4,16,256]{3,2,1,0:T(8,128)(2,1)S(1)}, bf16[16,8,16,256]{3,2,1,0:T(8,128)(2,1)S(1)}, bf16[16,10,16,256]{3,2,1,0:T(8,128)(2,1)S(1)}, bf1...) custom-call(s32[1]{0:T(128)S(6)} %copy.29.count_ref, ...), custom_call_target="tpu_custom_call" | custom-call | flops 3758096384 | bytes 9011204 | tf_op jit(solution)/shard_map/grad_spatial/pallas_call | solution.py:436
  19.5 0.1 collective-permute-start.6
  19.6 1.1 %copy-done.4 = bf16[3,3,256,256]{3,2,1,0:T(8,128)(2,1)S(1)} copy-done((bf16[3,3,256,256]{3,2,1,0:T(8,128)(2,1)S(1)}, bf16[3,3,256,256]{3,2,1,0:T(8,128)(2,1)}, u32[]{:S(2)}) %copy-start.4) | copy-done | bytes 1179672
  20.8 2.0 %spatial_upper.1 = (bf16[18,10,16,256]{3,2,1,0:T(8,128)(2,1)S(1)}, bf16[8,8,16,256]{3,2,1,0:T(8,128)(2,1)S(1)}) custom-call(bf16[18,10,16,256]{3,2,1,0:T(8,128)(2,1)S(1)} %get-tuple-element.52.acts_in, bf16[288,256]{1,0:T(8,128)(2,1)S(1)} %collective-permute-done.4.__1_.inner_ref, ...), custom_call_target="tpu_custom_call", output_to_operand_aliasing={{0}: (0, {})} | custom-call | flops 1342177280 | bytes 4947968 | tf_op jit(solution)/shard_map/spatial_upper/pallas_call | solution.py:436
  22.8 0.2 plane_send.2
  22.9 1.5 %collective-permute-start.7 = (bf16[4,9,16,128]{3,2,1,0:T(8,128)(2,1)S(1)}, bf16[4,9,16,128]{3,2,1,0:T(8,128)(2,1)S(1)}, u32[]{:S(2)}, u32[]{:S(2)}) collective-permute-start(bf16[4,9,16,128]{3,2,1,0:T(8,128)(2,1)S(1)} %get-tuple-element.59.rest_1_), channel_id=1, source_target_pairs={{0,5},{1,4},{2,7},{3,6},{4,1},{5,0},{6,3},{7,2},{8,13},{9,12},{10,... | collective-permute-start | bytes 442376 | tf_op jit(solution)/shard_map/ppermute | solution.py:460
  24.4 1.6 %spatial_lower.1.lower_ref = bf16[8,8,16,256]{3,2,1,0:T(8,128)(2,1)S(1)} custom-call(bf16[18,10,16,256]{3,2,1,0:T(8,128)(2,1)S(1)} %get-tuple-element.56.acts_ref, bf16[9,256,256]{2,1,0:T(8,128)(2,1)S(1)} %bitcast.13, bf16[4,9,16,128]{3,2,1,0:T(8,128)(2,1)S(1)} %get-tuple-element.58.rest_0_.refs_0_, bf16[4,9,16,128]{3,2,1,0:T(8,128)(2,1)S(1)} %get-tuple-element.59.rest_1_, ...), custom_call_target="tpu_custom_call" | custom-call | flops 1073741824 | bytes 3178496 | tf_op jit(solution)/shard_map/spatial_lower/pallas_call | solution.py:436
  26.0 2.4 %forward.1 = (bf16[512,256]{1,0:T(8,128)(2,1)S(1)}, bf16[16,7,16,128]{3,2,1,0:T(8,128)(2,1)S(1)}, bf16[16,7,16,128]{3,2,1,0:T(8,128)(2,1)S(1)}) custom-call(s32[1]{0:T(128)S(6)} %copy.29.count_ref, bf16[16,8,16,256]{3,2,1,0:T(8,128)(2,1)S(1)} %get-tuple-element.44.xt_ref, bf16[8,8,16,256]{3,2,1,0:T(8,128)(2,1)S(1)} %get-tuple-element.55.rest_0_.upper_ref, ...), custom_call_target="tpu_custom_call" | custom-call | bytes 1024 | tf_op jit(solution)/shard_map/forward/pallas_call | solution.py:436
  28.4 1.3 %collective-permute-done.7.__1_.refs_1_ = bf16[4,9,16,128]{3,2,1,0:T(8,128)(2,1)S(1)} collective-permute-done((bf16[4,9,16,128]{3,2,1,0:T(8,128)(2,1)S(1)}, bf16[4,9,16,128]{3,2,1,0:T(8,128)(2,1)S(1)}, u32[]{:S(2)}, u32[]{:S(2)}) %collective-permute-start.7) | collective-permute-done | bytes 147488 | tf_op jit(solution)/shard_map/ppermute | solution.py:460
  29.7 0.5 collective-permute-start.8
  30.2 1.5 %collective-permute-start.9 = (bf16[4,9,16,128]{3,2,1,0:T(8,128)(2,1)S(1)}, bf16[4,9,16,128]{3,2,1,0:T(8,128)(2,1)S(1)}, u32[]{:S(2)}, u32[]{:S(2)}) collective-permute-start(bf16[4,9,16,128]{3,2,1,0:T(8,128)(2,1)S(1)} %get-tuple-element.61.rest_3_), channel_id=1, source_target_pairs={{0,4},{1,5},{2,6},{3,7},{4,0},{5,1},{6,2},{7,3},{8,12},{9,13},{10,... | collective-permute-start | bytes 442376 | tf_op jit(solution)/shard_map/ppermute | solution.py:460
  31.7 0.1 plane_send.3
  31.8 1.6 %collective-permute-start.11 = (bf16[4,7,16,128]{3,2,1,0:T(8,128)(2,1)S(1)}, bf16[4,7,16,128]{3,2,1,0:T(8,128)(2,1)S(1)}, u32[]{:S(2)}, u32[]{:S(2)}) collective-permute-start(bf16[4,7,16,128]{3,2,1,0:T(8,128)(2,1)S(1)} %get-tuple-element.67), channel_id=1, source_target_pairs={{0,5},{1,4},{2,7},{3,6},{4,1},{5,0},{6,3},{7,2},{8,13},{9,12},{10,... | collective-permute-start | bytes 344072 | tf_op jit(solution)/shard_map/ppermute | solution.py:460
  33.4 1.3 %collective-permute-start.12 = (bf16[4,7,16,128]{3,2,1,0:T(8,128)(2,1)S(1)}, bf16[4,7,16,128]{3,2,1,0:T(8,128)(2,1)S(1)}, u32[]{:S(2)}, u32[]{:S(2)}) collective-permute-start(bf16[4,7,16,128]{3,2,1,0:T(8,128)(2,1)S(1)} %get-tuple-element.68), channel_id=1, source_target_pairs={{0,1},{1,0},{2,3},{3,2},{4,5},{5,4},{6,7},{7,6},{8,9},{9,8},{10,11... | collective-permute-start | bytes 344072 | tf_op jit(solution)/shard_map/ppermute | solution.py:460
  34.6 0.7 collective-permute-start.13
  35.4 0.9 %collective-permute-done.8.refs_2_ = bf16[4,9,16,128]{3,2,1,0:T(8,128)(2,1)S(1)} collective-permute-done((bf16[4,9,16,128]{3,2,1,0:T(8,128)(2,1)S(1)}, bf16[4,9,16,128]{3,2,1,0:T(8,128)(2,1)S(1)}, u32[]{:S(2)}, u32[]{:S(2)}) %collective-permute-start.8) | collective-permute-done | bytes 147488 | tf_op jit(solution)/shard_map/ppermute | solution.py:460
  36.2 0.7 collective-permute-done.9.refs_3_
  36.9 3.5 %collective-permute-done.11.refs_5_ = bf16[4,7,16,128]{3,2,1,0:T(8,128)(2,1)S(1)} collective-permute-done((bf16[4,7,16,128]{3,2,1,0:T(8,128)(2,1)S(1)}, bf16[4,7,16,128]{3,2,1,0:T(8,128)(2,1)S(1)}, u32[]{:S(2)}, u32[]{:S(2)}) %collective-permute-start.11) | collective-permute-done | bytes 114720 | tf_op jit(solution)/shard_map/ppermute | solution.py:460
  40.3 0.5 collective-permute-done.12.refs_6_
  40.9 0.3 collective-permute-done.13.refs_7_
  41.1 0.1 line_send.1
  41.3 3.6 %collective-permute-start.14 = (bf16[16,16,128]{2,1,0:T(8,128)(2,1)S(1)}, bf16[16,16,128]{2,1,0:T(8,128)(2,1)S(1)}, u32[]{:S(2)}, u32[]{:S(2)}) collective-permute-start(bf16[16,16,128]{2,1,0:T(8,128)(2,1)S(1)} %get-tuple-element.71), channel_id=1, source_target_pairs={{0,24},{1,25},{2,26},{3,27},{4,28},{5,29},{6,30},{7,31},{8,16},{9,... | collective-permute-start | bytes 196616 | tf_op jit(solution)/shard_map/ppermute | solution.py:460
  44.8 0.9 %collective-permute-start.16 = (bf16[16,16,128]{2,1,0:T(8,128)(2,1)S(1)}, bf16[16,16,128]{2,1,0:T(8,128)(2,1)S(1)}, u32[]{:S(2)}, u32[]{:S(2)}) collective-permute-start(bf16[16,16,128]{2,1,0:T(8,128)(2,1)S(1)} %get-tuple-element.73), channel_id=1, source_target_pairs={{0,8},{1,9},{2,10},{3,11},{4,12},{5,13},{6,14},{7,15},{8,0},{9,1},... | collective-permute-start | bytes 196616 | tf_op jit(solution)/shard_map/ppermute | solution.py:460
  45.7 2.3 %collective-permute-done.14.b_ref = bf16[16,16,128]{2,1,0:T(8,128)(2,1)S(1)} collective-permute-done((bf16[16,16,128]{2,1,0:T(8,128)(2,1)S(1)}, bf16[16,16,128]{2,1,0:T(8,128)(2,1)S(1)}, u32[]{:S(2)}, u32[]{:S(2)}) %collective-permute-start.14) | collective-permute-done | bytes 65568 | tf_op jit(solution)/shard_map/ppermute | solution.py:460
  48.1 2.1 %collective-permute-done.15.c_ref = bf16[16,16,128]{2,1,0:T(8,128)(2,1)S(1)} collective-permute-done((bf16[16,16,128]{2,1,0:T(8,128)(2,1)S(1)}, bf16[16,16,128]{2,1,0:T(8,128)(2,1)S(1)}, u32[]{:S(2)}, u32[]{:S(2)}) %collective-permute-start.15) | collective-permute-done | bytes 65568 | tf_op jit(solution)/shard_map/ppermute | solution.py:460
  50.2 1.0 %collective-permute-start.19 = (bf16[16,16,128]{2,1,0:T(8,128)(2,1)S(1)}, bf16[16,16,128]{2,1,0:T(8,128)(2,1)S(1)}, u32[]{:S(2)}, u32[]{:S(2)}) collective-permute-start(bf16[16,16,128]{2,1,0:T(8,128)(2,1)S(1)} %line_sum.1.a_ref), channel_id=1, source_target_pairs={{0,8},{1,9},{2,10},{3,11},{4,12},{5,13},{6,14},{7,15},{8,0},{9,1},... | collective-permute-start | bytes 196616 | tf_op jit(solution)/shard_map/ppermute | solution.py:460
  51.2 2.2 %collective-permute-start.18 = (bf16[16,16,128]{2,1,0:T(8,128)(2,1)S(1)}, bf16[16,16,128]{2,1,0:T(8,128)(2,1)S(1)}, u32[]{:S(2)}, u32[]{:S(2)}) collective-permute-start(bf16[16,16,128]{2,1,0:T(8,128)(2,1)S(1)} %line_sum.1.a_ref), channel_id=1, source_target_pairs={{0,16},{1,17},{2,18},{3,19},{4,20},{5,21},{6,22},{7,23},{8,24},{9,... | collective-permute-start | bytes 196616 | tf_op jit(solution)/shard_map/ppermute | solution.py:460
  53.4 1.2 %collective-permute-start.17 = (bf16[16,16,128]{2,1,0:T(8,128)(2,1)S(1)}, bf16[16,16,128]{2,1,0:T(8,128)(2,1)S(1)}, u32[]{:S(2)}, u32[]{:S(2)}) collective-permute-start(bf16[16,16,128]{2,1,0:T(8,128)(2,1)S(1)} %line_sum.1.a_ref), channel_id=1, source_target_pairs={{0,24},{1,25},{2,26},{3,27},{4,28},{5,29},{6,30},{7,31},{8,16},{9,... | collective-permute-start | bytes 196616 | tf_op jit(solution)/shard_map/ppermute | solution.py:460
  54.6 1.5 %collective-permute-start.3 = (bf16[64,256]{1,0:T(8,128)(2,1)S(1)}, bf16[64,256]{1,0:T(8,128)(2,1)S(1)}, u32[]{:S(2)}, u32[]{:S(2)}) collective-permute-start(bf16[64,256]{1,0:T(8,128)(2,1)S(1)} %get-tuple-element.51), channel_id=1, source_target_pairs={{0,1},{1,0},{2,3},{3,2},{4,5},{5,4},{6,7},{7,6},{8,9},{9,8},{10,11... | collective-permute-start | bytes 98312 | tf_op jit(solution)/shard_map/ppermute | solution.py:516
  56.2 1.2 %collective-permute-done.18.c_ref = bf16[16,16,128]{2,1,0:T(8,128)(2,1)S(1)} collective-permute-done((bf16[16,16,128]{2,1,0:T(8,128)(2,1)S(1)}, bf16[16,16,128]{2,1,0:T(8,128)(2,1)S(1)}, u32[]{:S(2)}, u32[]{:S(2)}) %collective-permute-start.18) | collective-permute-done | bytes 65568 | tf_op jit(solution)/shard_map/ppermute | solution.py:460
  57.3 2.2 %collective-permute-done.17.b_ref = bf16[16,16,128]{2,1,0:T(8,128)(2,1)S(1)} collective-permute-done((bf16[16,16,128]{2,1,0:T(8,128)(2,1)S(1)}, bf16[16,16,128]{2,1,0:T(8,128)(2,1)S(1)}, u32[]{:S(2)}, u32[]{:S(2)}) %collective-permute-start.17) | collective-permute-done | bytes 65568 | tf_op jit(solution)/shard_map/ppermute | solution.py:460
  59.5 1.5 %collective-permute-start.22 = (bf16[4,16,16,128]{3,2,1,0:T(8,128)(2,1)S(1)}, bf16[4,16,16,128]{3,2,1,0:T(8,128)(2,1)S(1)}, u32[]{:S(2)}, u32[]{:S(2)}) collective-permute-start(bf16[4,16,16,128]{3,2,1,0:T(8,128)(2,1)S(1)} %line_gather.1.rest_0_.a_ref), channel_id=1, source_target_pairs={{0,4},{1,5},{2,6},{3,7},{4,0},{5,1},{6,2},{7,3},{8,12},{9,13},{10,... | collective-permute-start | bytes 786440 | tf_op jit(solution)/shard_map/ppermute | solution.py:460
  61.0 1.5 %collective-permute-start.21 = (bf16[4,16,16,128]{3,2,1,0:T(8,128)(2,1)S(1)}, bf16[4,16,16,128]{3,2,1,0:T(8,128)(2,1)S(1)}, u32[]{:S(2)}, u32[]{:S(2)}) collective-permute-start(bf16[4,16,16,128]{3,2,1,0:T(8,128)(2,1)S(1)} %line_gather.1.rest_0_.a_ref), channel_id=1, source_target_pairs={{0,1},{1,0},{2,3},{3,2},{4,5},{5,4},{6,7},{7,6},{8,9},{9,8},{10,11... | collective-permute-start | bytes 786440 | tf_op jit(solution)/shard_map/ppermute | solution.py:460
  62.5 0.6 collective-permute-start.20
  63.1 7.4 %grad_x.1 = (bf16[16,128,256]{2,1,0:T(8,128)(2,1)}, bf16[16,8,4,256]{3,2,1,0:T(4,128)(2,1)}, f32[8,128]{1,0:T(8,128)S(1)}) custom-call(s32[1]{0:T(128)S(6)} %copy.29.count_ref, bf16[16,8,16,256]{3,2,1,0:T(8,128)(2,1)S(1)} %get-tuple-element.44.xt_ref, bf16[16,8,16,256]{3,2,1,0:T(8,128)(2,1)S(1)} %get-tuple-element.49.gy_ref, ...), custom_call_target="tpu_custom_call" | custom-call | flops 2684354560 | bytes 7147524 | tf_op jit(solution)/shard_map/grad_x/pallas_call | solution.py:436
  70.5 2.0 %collective-permute-done.21.c_ref = bf16[4,16,16,128]{3,2,1,0:T(8,128)(2,1)S(1)} collective-permute-done((bf16[4,16,16,128]{3,2,1,0:T(8,128)(2,1)S(1)}, bf16[4,16,16,128]{3,2,1,0:T(8,128)(2,1)S(1)}, u32[]{:S(2)}, u32[]{:S(2)}) %collective-permute-start.21) | collective-permute-done | bytes 262176 | tf_op jit(solution)/shard_map/ppermute | solution.py:460
  72.7 1.5 %finish.2 = (f32[9,256,256]{2,1,0:T(8,128)}, f32[3,256,256]{2,1,0:T(8,128)}, f32[4,256,256]{2,1,0:T(8,128)}) custom-call(bf16[16,16,16,128]{3,2,1,0:T(8,128)(2,1)S(1)} %plane_gather.1.half_ref), custom_call_target="tpu_custom_call" | custom-call | bytes 5242880 | tf_op jit(solution)/shard_map/finish/pallas_call | solution.py:436
  74.2 1.2 %collective-permute-done.23.half_ref = bf16[16,16,16,128]{3,2,1,0:T(8,128)(2,1)S(1)} collective-permute-done((bf16[16,16,16,128]{3,2,1,0:T(8,128)(2,1)S(1)}, bf16[16,16,16,128]{3,2,1,0:T(8,128)(2,1)S(1)}, u32[]{:S(2)}, u32[]{:S(2)}) %collective-permute-start.23) | collective-permute-done | bytes 1048608 | tf_op jit(solution)/shard_map/ppermute | solution.py:460
  75.3 1.5 %finish.3 = (f32[9,256,256]{2,1,0:T(8,128)}, f32[3,256,256]{2,1,0:T(8,128)}, f32[4,256,256]{2,1,0:T(8,128)}) custom-call(bf16[16,16,16,128]{3,2,1,0:T(8,128)(2,1)S(1)} %collective-permute-done.23.half_ref, f32[9,256,256]{2,1,0:T(8,128)} %get-tuple-element.77.rest_0_, ...), custom_call_target="tpu_custom_call", output_to_operand_aliasing={{0}: (1, {}), {1}: (2, {}), {2}: (3, {})} | custom-call | bytes 9437184 | tf_op jit(solution)/shard_map/finish/pallas_call | solution.py:436
  (29 shorter events, 0.3 us)
Async XLA Ops:
  1.3 1.2 %copy-start.3 = (bf16[16,16,8,256]{3,2,1,0:T(8,128)(2,1)S(1)}, bf16[16,16,8,256]{3,2,1,0:T(8,128)(2,1)}, u32[]{:S(2)}) copy-start(bf16[16,16,8,256]{3,2,1,0:T(8,128)(2,1)} %param.6) | copy-start | bytes 3145732
  2.5 5.0 %copy-start.2 = (bf16[16,8,4,256]{3,2,1,0:T(4,128)(2,1)S(1)}, bf16[16,8,4,256]{3,2,1,0:T(4,128)(2,1)}, u32[]{:S(2)}) copy-start(bf16[16,8,4,256]{3,2,1,0:T(4,128)(2,1)} %cot_ref.3) | copy-start | bytes 786436
  2.8 8.3 %copy-start = (bf16[2,2,256,256]{3,2,1,0:T(8,128)(2,1)S(1)}, bf16[2,2,256,256]{3,2,1,0:T(8,128)(2,1)}, u32[]{:S(2)}) copy-start(bf16[2,2,256,256]{3,2,1,0:T(8,128)(2,1)} %param.10) | copy-start | bytes 1572868
  2.8 8.3 %copy-start.1 = (bf16[3,256,256]{2,1,0:T(8,128)(2,1)S(1)}, bf16[3,256,256]{2,1,0:T(8,128)(2,1)}, u32[]{:S(2)}) copy-start(bf16[3,256,256]{2,1,0:T(8,128)(2,1)} %wt_ref.5) | copy-start | bytes 1179652
  2.8 8.3 %collective-permute-start = (bf16[128,256]{1,0:T(8,128)(2,1)S(1)}, bf16[128,256]{1,0:T(8,128)(2,1)S(1)}, u32[]{:S(2)}, u32[]{:S(2)}) collective-permute-start(bf16[128,256]{1,0:T(8,128)(2,1)S(1)} %edges.1._), channel_id=1, source_target_pairs={{0,1},{1,0},{2,3},{3,2},{4,5},{5,4},{6,7},{7,6},{8,9},{9,8},{10,11... | collective-permute-start | bytes 196616 | tf_op jit(solution)/shard_map/ppermute | solution.py:516
  7.5 7.4 %collective-permute-start.2 = (bf16[2,8,4,256]{3,2,1,0:T(4,128)(2,1)S(1)}, bf16[2,8,4,256]{3,2,1,0:T(4,128)(2,1)S(1)}, u32[]{:S(2)}, u32[]{:S(2)}) collective-permute-start(bf16[2,8,4,256]{3,2,1,0:T(4,128)(2,1)S(1)} %next.1.rest_3_), channel_id=1, source_target_pairs={{0,0},{2,4},{4,2},{6,8},{8,6},{10,12},{12,10},{14,16},{16,14},{18,... | collective-permute-start | bytes 98312 | tf_op jit(solution)/shard_map/ppermute | solution.py:511
  8.2 6.7 %collective-permute-start.1 = (bf16[2,8,4,256]{3,2,1,0:T(4,128)(2,1)S(1)}, bf16[2,8,4,256]{3,2,1,0:T(4,128)(2,1)S(1)}, u32[]{:S(2)}, u32[]{:S(2)}) collective-permute-start(bf16[2,8,4,256]{3,2,1,0:T(4,128)(2,1)S(1)} %next.1.rest_3_), channel_id=1, source_target_pairs={{0,2},{2,0},{4,6},{6,4},{8,10},{10,8},{12,14},{14,12},{16,18},{18,... | collective-permute-start | bytes 98312 | tf_op jit(solution)/shard_map/ppermute | solution.py:511
  11.3 8.2 %collective-permute-start.5 = (bf16[288,256]{1,0:T(8,128)(2,1)S(1)}, bf16[288,256]{1,0:T(8,128)(2,1)S(1)}, u32[]{:S(2)}, u32[]{:S(2)}) collective-permute-start(bf16[288,256]{1,0:T(8,128)(2,1)S(1)} %get-tuple-element.53), channel_id=1, source_target_pairs={{0,0},{2,4},{4,2},{6,8},{8,6},{10,12},{12,10},{14,16},{16,14},{18,... | collective-permute-start | bytes 442376 | tf_op jit(solution)/shard_map/ppermute | solution.py:511
  12.0 7.5 %collective-permute-start.4 = (bf16[288,256]{1,0:T(8,128)(2,1)S(1)}, bf16[288,256]{1,0:T(8,128)(2,1)S(1)}, u32[]{:S(2)}, u32[]{:S(2)}) collective-permute-start(bf16[288,256]{1,0:T(8,128)(2,1)S(1)} %get-tuple-element.53), channel_id=1, source_target_pairs={{0,2},{2,0},{4,6},{6,4},{8,10},{10,8},{12,14},{14,12},{16,18},{18,... | collective-permute-start | bytes 442376 | tf_op jit(solution)/shard_map/ppermute | solution.py:511
  19.5 1.3 %copy-start.4 = (bf16[3,3,256,256]{3,2,1,0:T(8,128)(2,1)S(1)}, bf16[3,3,256,256]{3,2,1,0:T(8,128)(2,1)}, u32[]{:S(2)}) copy-start(bf16[3,3,256,256]{3,2,1,0:T(8,128)(2,1)} %param.8) | copy-start | bytes 3538948
  19.5 3.3 %collective-permute-start.6 = (bf16[16,9,16,128]{3,2,1,0:T(8,128)(2,1)S(1)}, bf16[16,9,16,128]{3,2,1,0:T(8,128)(2,1)S(1)}, u32[]{:S(2)}, u32[]{:S(2)}) collective-permute-start(bf16[16,9,16,128]{3,2,1,0:T(8,128)(2,1)S(1)} %pass.2._), channel_id=1, source_target_pairs={{0,2},{1,3},{2,0},{3,1},{4,6},{5,7},{6,4},{7,5},{8,10},{9,11},{10,... | collective-permute-start | bytes 1769480 | tf_op jit(solution)/shard_map/ppermute | solution.py:460
  22.9 6.7 %collective-permute-start.7 = (bf16[4,9,16,128]{3,2,1,0:T(8,128)(2,1)S(1)}, bf16[4,9,16,128]{3,2,1,0:T(8,128)(2,1)S(1)}, u32[]{:S(2)}, u32[]{:S(2)}) collective-permute-start(bf16[4,9,16,128]{3,2,1,0:T(8,128)(2,1)S(1)} %get-tuple-element.59.rest_1_), channel_id=1, source_target_pairs={{0,5},{1,4},{2,7},{3,6},{4,1},{5,0},{6,3},{7,2},{8,13},{9,12},{10,... | collective-permute-start | bytes 442376 | tf_op jit(solution)/shard_map/ppermute | solution.py:460
  29.7 2.0 %collective-permute-start.10 = (bf16[16,7,16,128]{3,2,1,0:T(8,128)(2,1)S(1)}, bf16[16,7,16,128]{3,2,1,0:T(8,128)(2,1)S(1)}, u32[]{:S(2)}, u32[]{:S(2)}) collective-permute-start(bf16[16,7,16,128]{3,2,1,0:T(8,128)(2,1)S(1)} %pass.3), channel_id=1, source_target_pairs={{0,2},{1,3},{2,0},{3,1},{4,6},{5,7},{6,4},{7,5},{8,10},{9,11},{10,... | collective-permute-start | bytes 1376264 | tf_op jit(solution)/shard_map/ppermute | solution.py:460
  29.7 6.5 %collective-permute-start.8 = (bf16[4,9,16,128]{3,2,1,0:T(8,128)(2,1)S(1)}, bf16[4,9,16,128]{3,2,1,0:T(8,128)(2,1)S(1)}, u32[]{:S(2)}, u32[]{:S(2)}) collective-permute-start(bf16[4,9,16,128]{3,2,1,0:T(8,128)(2,1)S(1)} %get-tuple-element.60.rest_2_), channel_id=1, source_target_pairs={{0,1},{1,0},{2,3},{3,2},{4,5},{5,4},{6,7},{7,6},{8,9},{9,8},{10,11... | collective-permute-start | bytes 442376 | tf_op jit(solution)/shard_map/ppermute | solution.py:460
  30.2 6.7 %collective-permute-start.9 = (bf16[4,9,16,128]{3,2,1,0:T(8,128)(2,1)S(1)}, bf16[4,9,16,128]{3,2,1,0:T(8,128)(2,1)S(1)}, u32[]{:S(2)}, u32[]{:S(2)}) collective-permute-start(bf16[4,9,16,128]{3,2,1,0:T(8,128)(2,1)S(1)} %get-tuple-element.61.rest_3_), channel_id=1, source_target_pairs={{0,4},{1,5},{2,6},{3,7},{4,0},{5,1},{6,2},{7,3},{8,12},{9,13},{10,... | collective-permute-start | bytes 442376 | tf_op jit(solution)/shard_map/ppermute | solution.py:460
  31.8 8.5 %collective-permute-start.11 = (bf16[4,7,16,128]{3,2,1,0:T(8,128)(2,1)S(1)}, bf16[4,7,16,128]{3,2,1,0:T(8,128)(2,1)S(1)}, u32[]{:S(2)}, u32[]{:S(2)}) collective-permute-start(bf16[4,7,16,128]{3,2,1,0:T(8,128)(2,1)S(1)} %get-tuple-element.67), channel_id=1, source_target_pairs={{0,5},{1,4},{2,7},{3,6},{4,1},{5,0},{6,3},{7,2},{8,13},{9,12},{10,... | collective-permute-start | bytes 344072 | tf_op jit(solution)/shard_map/ppermute | solution.py:460
  33.4 7.5 %collective-permute-start.12 = (bf16[4,7,16,128]{3,2,1,0:T(8,128)(2,1)S(1)}, bf16[4,7,16,128]{3,2,1,0:T(8,128)(2,1)S(1)}, u32[]{:S(2)}, u32[]{:S(2)}) collective-permute-start(bf16[4,7,16,128]{3,2,1,0:T(8,128)(2,1)S(1)} %get-tuple-element.68), channel_id=1, source_target_pairs={{0,1},{1,0},{2,3},{3,2},{4,5},{5,4},{6,7},{7,6},{8,9},{9,8},{10,11... | collective-permute-start | bytes 344072 | tf_op jit(solution)/shard_map/ppermute | solution.py:460
  34.6 6.5 %collective-permute-start.13 = (bf16[4,7,16,128]{3,2,1,0:T(8,128)(2,1)S(1)}, bf16[4,7,16,128]{3,2,1,0:T(8,128)(2,1)S(1)}, u32[]{:S(2)}, u32[]{:S(2)}) collective-permute-start(bf16[4,7,16,128]{3,2,1,0:T(8,128)(2,1)S(1)} %get-tuple-element.69), channel_id=1, source_target_pairs={{0,4},{1,5},{2,6},{3,7},{4,0},{5,1},{6,2},{7,3},{8,12},{9,13},{10,... | collective-permute-start | bytes 344072 | tf_op jit(solution)/shard_map/ppermute | solution.py:460
  41.3 6.8 %collective-permute-start.14 = (bf16[16,16,128]{2,1,0:T(8,128)(2,1)S(1)}, bf16[16,16,128]{2,1,0:T(8,128)(2,1)S(1)}, u32[]{:S(2)}, u32[]{:S(2)}) collective-permute-start(bf16[16,16,128]{2,1,0:T(8,128)(2,1)S(1)} %get-tuple-element.71), channel_id=1, source_target_pairs={{0,24},{1,25},{2,26},{3,27},{4,28},{5,29},{6,30},{7,31},{8,16},{9,... | collective-permute-start | bytes 196616 | tf_op jit(solution)/shard_map/ppermute | solution.py:460
  44.8 5.3 %collective-permute-start.15 = (bf16[16,16,128]{2,1,0:T(8,128)(2,1)S(1)}, bf16[16,16,128]{2,1,0:T(8,128)(2,1)S(1)}, u32[]{:S(2)}, u32[]{:S(2)}) collective-permute-start(bf16[16,16,128]{2,1,0:T(8,128)(2,1)S(1)} %get-tuple-element.72), channel_id=1, source_target_pairs={{0,16},{1,17},{2,18},{3,19},{4,20},{5,21},{6,22},{7,23},{8,24},{9,... | collective-permute-start | bytes 196616 | tf_op jit(solution)/shard_map/ppermute | solution.py:460
  44.8 5.3 %collective-permute-start.16 = (bf16[16,16,128]{2,1,0:T(8,128)(2,1)S(1)}, bf16[16,16,128]{2,1,0:T(8,128)(2,1)S(1)}, u32[]{:S(2)}, u32[]{:S(2)}) collective-permute-start(bf16[16,16,128]{2,1,0:T(8,128)(2,1)S(1)} %get-tuple-element.73), channel_id=1, source_target_pairs={{0,8},{1,9},{2,10},{3,11},{4,12},{5,13},{6,14},{7,15},{8,0},{9,1},... | collective-permute-start | bytes 196616 | tf_op jit(solution)/shard_map/ppermute | solution.py:460
  50.2 6.0 %collective-permute-start.19 = (bf16[16,16,128]{2,1,0:T(8,128)(2,1)S(1)}, bf16[16,16,128]{2,1,0:T(8,128)(2,1)S(1)}, u32[]{:S(2)}, u32[]{:S(2)}) collective-permute-start(bf16[16,16,128]{2,1,0:T(8,128)(2,1)S(1)} %line_sum.1.a_ref), channel_id=1, source_target_pairs={{0,8},{1,9},{2,10},{3,11},{4,12},{5,13},{6,14},{7,15},{8,0},{9,1},... | collective-permute-start | bytes 196616 | tf_op jit(solution)/shard_map/ppermute | solution.py:460
  51.2 6.1 %collective-permute-start.18 = (bf16[16,16,128]{2,1,0:T(8,128)(2,1)S(1)}, bf16[16,16,128]{2,1,0:T(8,128)(2,1)S(1)}, u32[]{:S(2)}, u32[]{:S(2)}) collective-permute-start(bf16[16,16,128]{2,1,0:T(8,128)(2,1)S(1)} %line_sum.1.a_ref), channel_id=1, source_target_pairs={{0,16},{1,17},{2,18},{3,19},{4,20},{5,21},{6,22},{7,23},{8,24},{9,... | collective-permute-start | bytes 196616 | tf_op jit(solution)/shard_map/ppermute | solution.py:460
  53.4 6.1 %collective-permute-start.17 = (bf16[16,16,128]{2,1,0:T(8,128)(2,1)S(1)}, bf16[16,16,128]{2,1,0:T(8,128)(2,1)S(1)}, u32[]{:S(2)}, u32[]{:S(2)}) collective-permute-start(bf16[16,16,128]{2,1,0:T(8,128)(2,1)S(1)} %line_sum.1.a_ref), channel_id=1, source_target_pairs={{0,24},{1,25},{2,26},{3,27},{4,28},{5,29},{6,30},{7,31},{8,16},{9,... | collective-permute-start | bytes 196616 | tf_op jit(solution)/shard_map/ppermute | solution.py:460
  54.6 8.4 %collective-permute-start.3 = (bf16[64,256]{1,0:T(8,128)(2,1)S(1)}, bf16[64,256]{1,0:T(8,128)(2,1)S(1)}, u32[]{:S(2)}, u32[]{:S(2)}) collective-permute-start(bf16[64,256]{1,0:T(8,128)(2,1)S(1)} %get-tuple-element.51), channel_id=1, source_target_pairs={{0,1},{1,0},{2,3},{3,2},{4,5},{5,4},{6,7},{7,6},{8,9},{9,8},{10,11... | collective-permute-start | bytes 98312 | tf_op jit(solution)/shard_map/ppermute | solution.py:516
  59.5 11.0 %collective-permute-start.22 = (bf16[4,16,16,128]{3,2,1,0:T(8,128)(2,1)S(1)}, bf16[4,16,16,128]{3,2,1,0:T(8,128)(2,1)S(1)}, u32[]{:S(2)}, u32[]{:S(2)}) collective-permute-start(bf16[4,16,16,128]{3,2,1,0:T(8,128)(2,1)S(1)} %line_gather.1.rest_0_.a_ref), channel_id=1, source_target_pairs={{0,4},{1,5},{2,6},{3,7},{4,0},{5,1},{6,2},{7,3},{8,12},{9,13},{10,... | collective-permute-start | bytes 786440 | tf_op jit(solution)/shard_map/ppermute | solution.py:460
  61.0 11.6 %collective-permute-start.21 = (bf16[4,16,16,128]{3,2,1,0:T(8,128)(2,1)S(1)}, bf16[4,16,16,128]{3,2,1,0:T(8,128)(2,1)S(1)}, u32[]{:S(2)}, u32[]{:S(2)}) collective-permute-start(bf16[4,16,16,128]{3,2,1,0:T(8,128)(2,1)S(1)} %line_gather.1.rest_0_.a_ref), channel_id=1, source_target_pairs={{0,1},{1,0},{2,3},{3,2},{4,5},{5,4},{6,7},{7,6},{8,9},{9,8},{10,11... | collective-permute-start | bytes 786440 | tf_op jit(solution)/shard_map/ppermute | solution.py:460
  62.5 10.0 %collective-permute-start.20 = (bf16[4,16,16,128]{3,2,1,0:T(8,128)(2,1)S(1)}, bf16[4,16,16,128]{3,2,1,0:T(8,128)(2,1)S(1)}, u32[]{:S(2)}, u32[]{:S(2)}) collective-permute-start(bf16[4,16,16,128]{3,2,1,0:T(8,128)(2,1)S(1)} %line_gather.1.rest_0_.a_ref), channel_id=1, source_target_pairs={{0,5},{1,4},{2,7},{3,6},{4,1},{5,0},{6,3},{7,2},{8,13},{9,12},{10,... | collective-permute-start | bytes 786440 | tf_op jit(solution)/shard_map/ppermute | solution.py:460
  72.6 2.7 %collective-permute-start.23 = (bf16[16,16,16,128]{3,2,1,0:T(8,128)(2,1)S(1)}, bf16[16,16,16,128]{3,2,1,0:T(8,128)(2,1)S(1)}, u32[]{:S(2)}, u32[]{:S(2)}) collective-permute-start(bf16[16,16,16,128]{3,2,1,0:T(8,128)(2,1)S(1)} %plane_gather.1.half_ref), channel_id=1, source_target_pairs={{0,2},{1,3},{2,0},{3,1},{4,6},{5,7},{6,4},{7,5},{8,10},{9,11},{10,... | collective-permute-start | bytes 3145736 | tf_op jit(solution)/shard_map/ppermute | solution.py:460

commit v20 on v18

--- a/solution.py
+++ b/solution.py
@@ -544,7 +544,7 @@
         [(VMEM, (2,) + cotangent.shape[1:])],
         moved=1024,
     )
-    nxt_got = around(nxt, "tm", -1)
+    nxt_got = along(nxt, "tm", -1)
     acts, at, last_two = call(
         functools.partial(halo_kernel, grp),
         "halo",

time: 74.4 us -> 74.2 us (level)
  waiting for transfers between devices: 22.7 us -> 20.1 us
  starting transfers between devices: 25.3 us -> 27.8 us
    ppermute x18, starting transfers between devices: 17 us -> 20.8 us  [swap(): return lax.ppermute(value, AXES, [(d, d ^ flip) for d in range(tm * grp)])]
    ppermute x2 -> x1, starting transfers between devices: 3.74 us -> 1.13 us  [around(): lax.ppermute(value, axis, [(i, (i + by) % count) for i in range(count)])]
    ppermute x18, waiting for transfers between devices: 20 us -> 17.7 us  [swap(): return lax.ppermute(value, AXES, [(d, d ^ flip) for d in range(tm * grp)])]
    ppermute x0 -> x1, starting transfers between devices: none -> 1.29 us  [along(): return lax.ppermute(value, axis, pairs)]
    ppermute x2 -> x1, waiting for transfers between devices: 2.72 us -> 1.95 us  [around(): lax.ppermute(value, axis, [(i, (i + by) % count) for i in range(count)])]
  transfers between devices with their start and end apart: 22 -> 22, of which waited for: 16 -> 14; matrix products, arithmetic and copies ran while one was open for 0% -> 0% of each run, Pallas kernels for 29% -> 29%
where the time goes in v20:
time: 74.2 us; the launch traced here: 74 us
  starting transfers between devices  27.8 us (37%)
  Pallas kernels  23.4 us (32%)
  waiting for transfers between devices  20.1 us (27%)
  between operations  1.48 us (2%)
  local copies, waits for them, and re-layouts  1.24 us (2%)
    pallas_call x19, Pallas kernels, call(): pl.pallas_call(kernel, out_shape=shapes, in_specs=[s for s, _ in ins], ou...  23.4 us
    ppermute x18, starting transfers between devices, swap(): return lax.ppermute(value, AXES, [(d, d ^ flip) for d in range(tm * grp)])  20.8 us
    ppermute x18, waiting for transfers between devices, swap(): return lax.ppermute(value, AXES, [(d, d ^ flip) for d in range(tm * grp)])  17.7 us
    ppermute x2, starting transfers between devices, from_bands(): got = lax.ppermute(parts[0], 'grp', [(0, 1), (1, 0)])  4.58 us
    ppermute x1, waiting for transfers between devices, around(): lax.ppermute(value, axis, [(i, (i + by) % count) for i in range(count)])  1.95 us
  transfers between devices with their start and end apart: 22, of which 14 were waited for; matrix products, arithmetic and copies ran while one was open for 0% of the time, Pallas kernels for 29%

profile of v20, /device:TPU:0, one launch (start us, length us, event | category | flops | bytes accessed | tf_op | source)
XLA Modules:
  0.0 74.0 jit_solution(2506130357736234648)
XLA Ops:
  1.3 1.2 %copy-done.3 = bf16[16,16,8,256]{3,2,1,0:T(8,128)(2,1)S(1)} copy-done((bf16[16,16,8,256]{3,2,1,0:T(8,128)(2,1)S(1)}, bf16[16,16,8,256]{3,2,1,0:T(8,128)(2,1)}, u32[]{:S(2)}) %copy-start.3) | copy-done | bytes 1048600
  2.5 0.3 edges.1._
  2.8 3.0 %collective-permute-start = (bf16[128,256]{1,0:T(8,128)(2,1)S(1)}, bf16[128,256]{1,0:T(8,128)(2,1)S(1)}, u32[]{:S(2)}, u32[]{:S(2)}) collective-permute-start(bf16[128,256]{1,0:T(8,128)(2,1)S(1)} %edges.1._), channel_id=1, source_target_pairs={{0,1},{1,0},{2,3},{3,2},{4,5},{5,4},{6,7},{7,6},{8,9},{9,8},{10,11... | collective-permute-start | bytes 196616 | tf_op jit(solution)/shard_map/ppermute | solution.py:504
  5.9 1.6 %acts.1 = (bf16[16,8,16,256]{3,2,1,0:T(8,128)(2,1)S(1)}, bf16[18,10,16,256]{3,2,1,0:T(8,128)(2,1)S(1)}, bf16[768,2560]{1,0:T(8,128)(2,1)S(1)}, bf16[288,256]{1,0:T(8,128)(2,1)S(1)}) custom-call(s32[1]{0:T(128)S(6)} %copy.29.count_ref, bf16[16,128,256]{2,1,0:T(8,128)(2,1)S(1)} %bitcast.11, bf16[128,256]{1,0:T(8,128)(2,1)S(1)} %edges.1._), custom_call_target="tpu_custom_call" | custom-call | flops 536870912 | bytes 7651332 | tf_op jit(solution)/shard_map/acts/pallas_call | solution.py:426
  7.5 1.3 %collective-permute-start.1 = (bf16[2,8,4,256]{3,2,1,0:T(4,128)(2,1)S(1)}, bf16[2,8,4,256]{3,2,1,0:T(4,128)(2,1)S(1)}, u32[]{:S(2)}, u32[]{:S(2)}) collective-permute-start(bf16[2,8,4,256]{3,2,1,0:T(4,128)(2,1)S(1)} %next.1.rest_3_), channel_id=1, source_target_pairs={{2,0},{4,2},{6,4},{8,6},{10,8},{12,10},{14,12},{16,14},{18,16},{20... | collective-permute-start | bytes 98312 | tf_op jit(solution)/shard_map/ppermute | solution.py:494
  8.9 0.2 halo.1
  9.0 1.1 %collective-permute-start.3 = (bf16[288,256]{1,0:T(8,128)(2,1)S(1)}, bf16[288,256]{1,0:T(8,128)(2,1)S(1)}, u32[]{:S(2)}, u32[]{:S(2)}) collective-permute-start(bf16[288,256]{1,0:T(8,128)(2,1)S(1)} %get-tuple-element.53), channel_id=1, source_target_pairs={{0,2},{2,4},{4,6},{6,8},{8,10},{10,12},{12,14},{14,16},{16,18},{18... | collective-permute-start | bytes 442376 | tf_op jit(solution)/shard_map/ppermute | solution.py:499
  10.2 0.5 collective-permute-done.1.nxt_ref
  10.6 4.5 %grad_spatial.1 = (bf16[8,4,16,256]{3,2,1,0:T(8,128)(2,1)S(1)}, bf16[16,8,16,256]{3,2,1,0:T(8,128)(2,1)S(1)}, bf16[16,10,16,256]{3,2,1,0:T(8,128)(2,1)S(1)}, bf1...) custom-call(s32[1]{0:T(128)S(6)} %copy.29.count_ref, ...), custom_call_target="tpu_custom_call" | custom-call | flops 3758096384 | bytes 8978436 | tf_op jit(solution)/shard_map/grad_spatial/pallas_call | solution.py:426
  15.2 2.0 %collective-permute-done.3.__1_.prev_ref = bf16[288,256]{1,0:T(8,128)(2,1)S(1)} collective-permute-done((bf16[288,256]{1,0:T(8,128)(2,1)S(1)}, bf16[288,256]{1,0:T(8,128)(2,1)S(1)}, u32[]{:S(2)}, u32[]{:S(2)}) %collective-permute-start.3) | collective-permute-done | bytes 147488 | tf_op jit(solution)/shard_map/ppermute | solution.py:499
  17.1 0.2 collective-permute-start.4
  17.3 2.0 %spatial_upper.1 = (bf16[18,10,16,256]{3,2,1,0:T(8,128)(2,1)S(1)}, bf16[8,8,16,256]{3,2,1,0:T(8,128)(2,1)S(1)}) custom-call(bf16[18,10,16,256]{3,2,1,0:T(8,128)(2,1)S(1)} %get-tuple-element.52.acts_in, bf16[288,256]{1,0:T(8,128)(2,1)S(1)} %collective-permute-done.3.__1_.prev_ref, bf16[9,256,256]{2,1,0:T(8,128)(2,1)S(1)} %bitcast.12, ...), custom_call_target="tpu_custom_call", output_to_operand_aliasing={{0}: (0, {})} | custom-call | flops 1342177280 | bytes 4800512 | tf_op jit(solution)/shard_map/spatial_upper/pallas_call | solution.py:426
  19.3 0.2 plane_send.2
  19.5 2.2 %collective-permute-start.5 = (bf16[4,9,16,128]{3,2,1,0:T(8,128)(2,1)S(1)}, bf16[4,9,16,128]{3,2,1,0:T(8,128)(2,1)S(1)}, u32[]{:S(2)}, u32[]{:S(2)}) collective-permute-start(bf16[4,9,16,128]{3,2,1,0:T(8,128)(2,1)S(1)} %get-tuple-element.59.rest_1_), channel_id=1, source_target_pairs={{0,5},{1,4},{2,7},{3,6},{4,1},{5,0},{6,3},{7,2},{8,13},{9,12},{10,... | collective-permute-start | bytes 442376 | tf_op jit(solution)/shard_map/ppermute | solution.py:450
  21.6 1.6 %spatial_lower.1.lower_ref = bf16[8,8,16,256]{3,2,1,0:T(8,128)(2,1)S(1)} custom-call(bf16[18,10,16,256]{3,2,1,0:T(8,128)(2,1)S(1)} %get-tuple-element.56.acts_ref, bf16[9,256,256]{2,1,0:T(8,128)(2,1)S(1)} %bitcast.13, bf16[4,9,16,128]{3,2,1,0:T(8,128)(2,1)S(1)} %get-tuple-element.58.rest_0_.refs_0_, bf16[4,9,16,128]{3,2,1,0:T(8,128)(2,1)S(1)} %get-tuple-element.59.rest_1_, ...), custom_call_target="tpu_custom_call" | custom-call | flops 1073741824 | bytes 3178496 | tf_op jit(solution)/shard_map/spatial_lower/pallas_call | solution.py:426
  23.2 2.4 %forward.1 = (bf16[512,256]{1,0:T(8,128)(2,1)S(1)}, bf16[16,7,16,128]{3,2,1,0:T(8,128)(2,1)S(1)}, bf16[16,7,16,128]{3,2,1,0:T(8,128)(2,1)S(1)}) custom-call(s32[1]{0:T(128)S(6)} %copy.29.count_ref, bf16[16,8,16,256]{3,2,1,0:T(8,128)(2,1)S(1)} %get-tuple-element.44.xt_ref, bf16[8,8,16,256]{3,2,1,0:T(8,128)(2,1)S(1)} %get-tuple-element.55.rest_0_.upper_ref, ...), custom_call_target="tpu_custom_call" | custom-call | bytes 1024 | tf_op jit(solution)/shard_map/forward/pallas_call | solution.py:426
  25.6 1.0 %collective-permute-done.5.__1_.refs_1_ = bf16[4,9,16,128]{3,2,1,0:T(8,128)(2,1)S(1)} collective-permute-done((bf16[4,9,16,128]{3,2,1,0:T(8,128)(2,1)S(1)}, bf16[4,9,16,128]{3,2,1,0:T(8,128)(2,1)S(1)}, u32[]{:S(2)}, u32[]{:S(2)}) %collective-permute-start.5) | collective-permute-done | bytes 147488 | tf_op jit(solution)/shard_map/ppermute | solution.py:450
  26.5 0.7 collective-permute-start.6
  27.3 1.6 %collective-permute-start.7 = (bf16[4,9,16,128]{3,2,1,0:T(8,128)(2,1)S(1)}, bf16[4,9,16,128]{3,2,1,0:T(8,128)(2,1)S(1)}, u32[]{:S(2)}, u32[]{:S(2)}) collective-permute-start(bf16[4,9,16,128]{3,2,1,0:T(8,128)(2,1)S(1)} %get-tuple-element.61.rest_3_), channel_id=1, source_target_pairs={{0,4},{1,5},{2,6},{3,7},{4,0},{5,1},{6,2},{7,3},{8,12},{9,13},{10,... | collective-permute-start | bytes 442376 | tf_op jit(solution)/shard_map/ppermute | solution.py:450
  28.9 0.1 plane_send.3
  29.0 1.3 %collective-permute-start.9 = (bf16[4,7,16,128]{3,2,1,0:T(8,128)(2,1)S(1)}, bf16[4,7,16,128]{3,2,1,0:T(8,128)(2,1)S(1)}, u32[]{:S(2)}, u32[]{:S(2)}) collective-permute-start(bf16[4,7,16,128]{3,2,1,0:T(8,128)(2,1)S(1)} %get-tuple-element.67), channel_id=1, source_target_pairs={{0,5},{1,4},{2,7},{3,6},{4,1},{5,0},{6,3},{7,2},{8,13},{9,12},{10,... | collective-permute-start | bytes 344072 | tf_op jit(solution)/shard_map/ppermute | solution.py:450
  30.3 1.5 %collective-permute-start.10 = (bf16[4,7,16,128]{3,2,1,0:T(8,128)(2,1)S(1)}, bf16[4,7,16,128]{3,2,1,0:T(8,128)(2,1)S(1)}, u32[]{:S(2)}, u32[]{:S(2)}) collective-permute-start(bf16[4,7,16,128]{3,2,1,0:T(8,128)(2,1)S(1)} %get-tuple-element.68), channel_id=1, source_target_pairs={{0,1},{1,0},{2,3},{3,2},{4,5},{5,4},{6,7},{7,6},{8,9},{9,8},{10,11... | collective-permute-start | bytes 344072 | tf_op jit(solution)/shard_map/ppermute | solution.py:450
  31.8 0.7 collective-permute-start.11
  32.5 0.3 collective-permute-done.6.refs_2_
  32.8 0.9 %collective-permute-done.7.refs_3_ = bf16[4,9,16,128]{3,2,1,0:T(8,128)(2,1)S(1)} collective-permute-done((bf16[4,9,16,128]{3,2,1,0:T(8,128)(2,1)S(1)}, bf16[4,9,16,128]{3,2,1,0:T(8,128)(2,1)S(1)}, u32[]{:S(2)}, u32[]{:S(2)}) %collective-permute-start.7) | collective-permute-done | bytes 147488 | tf_op jit(solution)/shard_map/ppermute | solution.py:450
  33.7 3.5 %collective-permute-done.9.refs_5_ = bf16[4,7,16,128]{3,2,1,0:T(8,128)(2,1)S(1)} collective-permute-done((bf16[4,7,16,128]{3,2,1,0:T(8,128)(2,1)S(1)}, bf16[4,7,16,128]{3,2,1,0:T(8,128)(2,1)S(1)}, u32[]{:S(2)}, u32[]{:S(2)}) %collective-permute-start.9) | collective-permute-done | bytes 114720 | tf_op jit(solution)/shard_map/ppermute | solution.py:450
  37.2 0.5 collective-permute-done.10.refs_6_
  37.7 0.4 collective-permute-done.11.refs_7_
  38.1 0.1 line_send.1
  38.3 3.2 %collective-permute-start.12 = (bf16[16,16,128]{2,1,0:T(8,128)(2,1)S(1)}, bf16[16,16,128]{2,1,0:T(8,128)(2,1)S(1)}, u32[]{:S(2)}, u32[]{:S(2)}) collective-permute-start(bf16[16,16,128]{2,1,0:T(8,128)(2,1)S(1)} %get-tuple-element.71), channel_id=1, source_target_pairs={{0,24},{1,25},{2,26},{3,27},{4,28},{5,29},{6,30},{7,31},{8,16},{9,... | collective-permute-start | bytes 196616 | tf_op jit(solution)/shard_map/ppermute | solution.py:450
  41.4 1.3 %collective-permute-start.14 = (bf16[16,16,128]{2,1,0:T(8,128)(2,1)S(1)}, bf16[16,16,128]{2,1,0:T(8,128)(2,1)S(1)}, u32[]{:S(2)}, u32[]{:S(2)}) collective-permute-start(bf16[16,16,128]{2,1,0:T(8,128)(2,1)S(1)} %get-tuple-element.73), channel_id=1, source_target_pairs={{0,8},{1,9},{2,10},{3,11},{4,12},{5,13},{6,14},{7,15},{8,0},{9,1},... | collective-permute-start | bytes 196616 | tf_op jit(solution)/shard_map/ppermute | solution.py:450
  42.7 2.5 %collective-permute-done.12.b_ref = bf16[16,16,128]{2,1,0:T(8,128)(2,1)S(1)} collective-permute-done((bf16[16,16,128]{2,1,0:T(8,128)(2,1)S(1)}, bf16[16,16,128]{2,1,0:T(8,128)(2,1)S(1)}, u32[]{:S(2)}, u32[]{:S(2)}) %collective-permute-start.12) | collective-permute-done | bytes 65568 | tf_op jit(solution)/shard_map/ppermute | solution.py:450
  45.2 2.0 %collective-permute-done.13.c_ref = bf16[16,16,128]{2,1,0:T(8,128)(2,1)S(1)} collective-permute-done((bf16[16,16,128]{2,1,0:T(8,128)(2,1)S(1)}, bf16[16,16,128]{2,1,0:T(8,128)(2,1)S(1)}, u32[]{:S(2)}, u32[]{:S(2)}) %collective-permute-start.13) | collective-permute-done | bytes 65568 | tf_op jit(solution)/shard_map/ppermute | solution.py:450
  47.2 0.6 collective-permute-start.17
  47.8 2.7 %collective-permute-start.16 = (bf16[16,16,128]{2,1,0:T(8,128)(2,1)S(1)}, bf16[16,16,128]{2,1,0:T(8,128)(2,1)S(1)}, u32[]{:S(2)}, u32[]{:S(2)}) collective-permute-start(bf16[16,16,128]{2,1,0:T(8,128)(2,1)S(1)} %line_sum.1.a_ref), channel_id=1, source_target_pairs={{0,16},{1,17},{2,18},{3,19},{4,20},{5,21},{6,22},{7,23},{8,24},{9,... | collective-permute-start | bytes 196616 | tf_op jit(solution)/shard_map/ppermute | solution.py:450
  50.5 1.2 %collective-permute-start.15 = (bf16[16,16,128]{2,1,0:T(8,128)(2,1)S(1)}, bf16[16,16,128]{2,1,0:T(8,128)(2,1)S(1)}, u32[]{:S(2)}, u32[]{:S(2)}) collective-permute-start(bf16[16,16,128]{2,1,0:T(8,128)(2,1)S(1)} %line_sum.1.a_ref), channel_id=1, source_target_pairs={{0,24},{1,25},{2,26},{3,27},{4,28},{5,29},{6,30},{7,31},{8,16},{9,... | collective-permute-start | bytes 196616 | tf_op jit(solution)/shard_map/ppermute | solution.py:450
  51.7 1.5 %collective-permute-start.2 = (bf16[64,256]{1,0:T(8,128)(2,1)S(1)}, bf16[64,256]{1,0:T(8,128)(2,1)S(1)}, u32[]{:S(2)}, u32[]{:S(2)}) collective-permute-start(bf16[64,256]{1,0:T(8,128)(2,1)S(1)} %get-tuple-element.51), channel_id=1, source_target_pairs={{0,1},{1,0},{2,3},{3,2},{4,5},{5,4},{6,7},{7,6},{8,9},{9,8},{10,11... | collective-permute-start | bytes 98312 | tf_op jit(solution)/shard_map/ppermute | solution.py:504
  53.2 1.1 %collective-permute-done.16.c_ref = bf16[16,16,128]{2,1,0:T(8,128)(2,1)S(1)} collective-permute-done((bf16[16,16,128]{2,1,0:T(8,128)(2,1)S(1)}, bf16[16,16,128]{2,1,0:T(8,128)(2,1)S(1)}, u32[]{:S(2)}, u32[]{:S(2)}) %collective-permute-start.16) | collective-permute-done | bytes 65568 | tf_op jit(solution)/shard_map/ppermute | solution.py:450
  54.4 2.2 %collective-permute-done.15.b_ref = bf16[16,16,128]{2,1,0:T(8,128)(2,1)S(1)} collective-permute-done((bf16[16,16,128]{2,1,0:T(8,128)(2,1)S(1)}, bf16[16,16,128]{2,1,0:T(8,128)(2,1)S(1)}, u32[]{:S(2)}, u32[]{:S(2)}) %collective-permute-start.15) | collective-permute-done | bytes 65568 | tf_op jit(solution)/shard_map/ppermute | solution.py:450
  56.6 1.4 %collective-permute-start.20 = (bf16[4,16,16,128]{3,2,1,0:T(8,128)(2,1)S(1)}, bf16[4,16,16,128]{3,2,1,0:T(8,128)(2,1)S(1)}, u32[]{:S(2)}, u32[]{:S(2)}) collective-permute-start(bf16[4,16,16,128]{3,2,1,0:T(8,128)(2,1)S(1)} %line_gather.1.rest_0_.a_ref), channel_id=1, source_target_pairs={{0,4},{1,5},{2,6},{3,7},{4,0},{5,1},{6,2},{7,3},{8,12},{9,13},{10,... | collective-permute-start | bytes 786440 | tf_op jit(solution)/shard_map/ppermute | solution.py:450
  58.0 1.5 %collective-permute-start.19 = (bf16[4,16,16,128]{3,2,1,0:T(8,128)(2,1)S(1)}, bf16[4,16,16,128]{3,2,1,0:T(8,128)(2,1)S(1)}, u32[]{:S(2)}, u32[]{:S(2)}) collective-permute-start(bf16[4,16,16,128]{3,2,1,0:T(8,128)(2,1)S(1)} %line_gather.1.rest_0_.a_ref), channel_id=1, source_target_pairs={{0,1},{1,0},{2,3},{3,2},{4,5},{5,4},{6,7},{7,6},{8,9},{9,8},{10,11... | collective-permute-start | bytes 786440 | tf_op jit(solution)/shard_map/ppermute | solution.py:450
  59.5 0.7 collective-permute-start.18
  60.2 7.4 %grad_x.1 = (bf16[16,128,256]{2,1,0:T(8,128)(2,1)}, bf16[16,8,4,256]{3,2,1,0:T(4,128)(2,1)}, f32[8,128]{1,0:T(8,128)S(1)}) custom-call(s32[1]{0:T(128)S(6)} %copy.29.count_ref, bf16[16,8,16,256]{3,2,1,0:T(8,128)(2,1)S(1)} %get-tuple-element.44.xt_ref, bf16[16,8,16,256]{3,2,1,0:T(8,128)(2,1)S(1)} %get-tuple-element.49.gy_ref, ...), custom_call_target="tpu_custom_call" | custom-call | flops 2684354560 | bytes 7147524 | tf_op jit(solution)/shard_map/grad_x/pallas_call | solution.py:426
  67.6 2.1 %collective-permute-done.19.c_ref = bf16[4,16,16,128]{3,2,1,0:T(8,128)(2,1)S(1)} collective-permute-done((bf16[4,16,16,128]{3,2,1,0:T(8,128)(2,1)S(1)}, bf16[4,16,16,128]{3,2,1,0:T(8,128)(2,1)S(1)}, u32[]{:S(2)}, u32[]{:S(2)}) %collective-permute-start.19) | collective-permute-done | bytes 262176 | tf_op jit(solution)/shard_map/ppermute | solution.py:450
  69.8 0.1 plane_gather.1.half_ref
  69.9 1.5 %finish.2 = (f32[9,256,256]{2,1,0:T(8,128)}, f32[3,256,256]{2,1,0:T(8,128)}, f32[4,256,256]{2,1,0:T(8,128)}) custom-call(bf16[16,16,16,128]{3,2,1,0:T(8,128)(2,1)S(1)} %plane_gather.1.half_ref), custom_call_target="tpu_custom_call" | custom-call | bytes 5242880 | tf_op jit(solution)/shard_map/finish/pallas_call | solution.py:426
  71.4 1.2 %collective-permute-done.21.half_ref = bf16[16,16,16,128]{3,2,1,0:T(8,128)(2,1)S(1)} collective-permute-done((bf16[16,16,16,128]{3,2,1,0:T(8,128)(2,1)S(1)}, bf16[16,16,16,128]{3,2,1,0:T(8,128)(2,1)S(1)}, u32[]{:S(2)}, u32[]{:S(2)}) %collective-permute-start.21) | collective-permute-done | bytes 1048608 | tf_op jit(solution)/shard_map/ppermute | solution.py:450
  72.6 1.5 %finish.3 = (f32[9,256,256]{2,1,0:T(8,128)}, f32[3,256,256]{2,1,0:T(8,128)}, f32[4,256,256]{2,1,0:T(8,128)}) custom-call(bf16[16,16,16,128]{3,2,1,0:T(8,128)(2,1)S(1)} %collective-permute-done.21.half_ref, f32[9,256,256]{2,1,0:T(8,128)} %get-tuple-element.77.rest_0_, ...), custom_call_target="tpu_custom_call", output_to_operand_aliasing={{0}: (1, {}), {1}: (2, {}), {2}: (3, {})} | custom-call | bytes 9437184 | tf_op jit(solution)/shard_map/finish/pallas_call | solution.py:426
  (25 shorter events, 0.2 us)
Async XLA Ops:
  1.3 1.2 %copy-start.3 = (bf16[16,16,8,256]{3,2,1,0:T(8,128)(2,1)S(1)}, bf16[16,16,8,256]{3,2,1,0:T(8,128)(2,1)}, u32[]{:S(2)}) copy-start(bf16[16,16,8,256]{3,2,1,0:T(8,128)(2,1)} %param.6) | copy-start | bytes 3145732
  2.5 5.0 %copy-start.2 = (bf16[16,8,4,256]{3,2,1,0:T(4,128)(2,1)S(1)}, bf16[16,8,4,256]{3,2,1,0:T(4,128)(2,1)}, u32[]{:S(2)}) copy-start(bf16[16,8,4,256]{3,2,1,0:T(4,128)(2,1)} %cot_ref.3) | copy-start | bytes 786436
  2.8 6.0 %copy-start = (bf16[2,2,256,256]{3,2,1,0:T(8,128)(2,1)S(1)}, bf16[2,2,256,256]{3,2,1,0:T(8,128)(2,1)}, u32[]{:S(2)}) copy-start(bf16[2,2,256,256]{3,2,1,0:T(8,128)(2,1)} %param.10) | copy-start | bytes 1572868
  2.8 6.0 %copy-start.1 = (bf16[3,256,256]{2,1,0:T(8,128)(2,1)S(1)}, bf16[3,256,256]{2,1,0:T(8,128)(2,1)}, u32[]{:S(2)}) copy-start(bf16[3,256,256]{2,1,0:T(8,128)(2,1)} %wt_ref.5) | copy-start | bytes 1179652
  2.8 6.0 %collective-permute-start = (bf16[128,256]{1,0:T(8,128)(2,1)S(1)}, bf16[128,256]{1,0:T(8,128)(2,1)S(1)}, u32[]{:S(2)}, u32[]{:S(2)}) collective-permute-start(bf16[128,256]{1,0:T(8,128)(2,1)S(1)} %edges.1._), channel_id=1, source_target_pairs={{0,1},{1,0},{2,3},{3,2},{4,5},{5,4},{6,7},{7,6},{8,9},{9,8},{10,11... | collective-permute-start | bytes 196616 | tf_op jit(solution)/shard_map/ppermute | solution.py:504
  7.5 3.1 %collective-permute-start.1 = (bf16[2,8,4,256]{3,2,1,0:T(4,128)(2,1)S(1)}, bf16[2,8,4,256]{3,2,1,0:T(4,128)(2,1)S(1)}, u32[]{:S(2)}, u32[]{:S(2)}) collective-permute-start(bf16[2,8,4,256]{3,2,1,0:T(4,128)(2,1)S(1)} %next.1.rest_3_), channel_id=1, source_target_pairs={{2,0},{4,2},{6,4},{8,6},{10,8},{12,10},{14,12},{16,14},{18,16},{20... | collective-permute-start | bytes 98312 | tf_op jit(solution)/shard_map/ppermute | solution.py:494
  9.0 8.1 %collective-permute-start.3 = (bf16[288,256]{1,0:T(8,128)(2,1)S(1)}, bf16[288,256]{1,0:T(8,128)(2,1)S(1)}, u32[]{:S(2)}, u32[]{:S(2)}) collective-permute-start(bf16[288,256]{1,0:T(8,128)(2,1)S(1)} %get-tuple-element.53), channel_id=1, source_target_pairs={{0,2},{2,4},{4,6},{6,8},{8,10},{10,12},{12,14},{14,16},{16,18},{18... | collective-permute-start | bytes 442376 | tf_op jit(solution)/shard_map/ppermute | solution.py:499
  10.6 6.6 %copy-start.4 = (bf16[3,3,256,256]{3,2,1,0:T(8,128)(2,1)S(1)}, bf16[3,3,256,256]{3,2,1,0:T(8,128)(2,1)}, u32[]{:S(2)}) copy-start(bf16[3,3,256,256]{3,2,1,0:T(8,128)(2,1)} %param.8) | copy-start | bytes 3538948
  17.1 2.2 %collective-permute-start.4 = (bf16[16,9,16,128]{3,2,1,0:T(8,128)(2,1)S(1)}, bf16[16,9,16,128]{3,2,1,0:T(8,128)(2,1)S(1)}, u32[]{:S(2)}, u32[]{:S(2)}) collective-permute-start(bf16[16,9,16,128]{3,2,1,0:T(8,128)(2,1)S(1)} %pass.2._), channel_id=1, source_target_pairs={{0,2},{1,3},{2,0},{3,1},{4,6},{5,7},{6,4},{7,5},{8,10},{9,11},{10,... | collective-permute-start | bytes 1769480 | tf_op jit(solution)/shard_map/ppermute | solution.py:450
  19.5 7.1 %collective-permute-start.5 = (bf16[4,9,16,128]{3,2,1,0:T(8,128)(2,1)S(1)}, bf16[4,9,16,128]{3,2,1,0:T(8,128)(2,1)S(1)}, u32[]{:S(2)}, u32[]{:S(2)}) collective-permute-start(bf16[4,9,16,128]{3,2,1,0:T(8,128)(2,1)S(1)} %get-tuple-element.59.rest_1_), channel_id=1, source_target_pairs={{0,5},{1,4},{2,7},{3,6},{4,1},{5,0},{6,3},{7,2},{8,13},{9,12},{10,... | collective-permute-start | bytes 442376 | tf_op jit(solution)/shard_map/ppermute | solution.py:450
  26.5 2.3 %collective-permute-start.8 = (bf16[16,7,16,128]{3,2,1,0:T(8,128)(2,1)S(1)}, bf16[16,7,16,128]{3,2,1,0:T(8,128)(2,1)S(1)}, u32[]{:S(2)}, u32[]{:S(2)}) collective-permute-start(bf16[16,7,16,128]{3,2,1,0:T(8,128)(2,1)S(1)} %pass.3), channel_id=1, source_target_pairs={{0,2},{1,3},{2,0},{3,1},{4,6},{5,7},{6,4},{7,5},{8,10},{9,11},{10,... | collective-permute-start | bytes 1376264 | tf_op jit(solution)/shard_map/ppermute | solution.py:450
  26.5 6.3 %collective-permute-start.6 = (bf16[4,9,16,128]{3,2,1,0:T(8,128)(2,1)S(1)}, bf16[4,9,16,128]{3,2,1,0:T(8,128)(2,1)S(1)}, u32[]{:S(2)}, u32[]{:S(2)}) collective-permute-start(bf16[4,9,16,128]{3,2,1,0:T(8,128)(2,1)S(1)} %get-tuple-element.60.rest_2_), channel_id=1, source_target_pairs={{0,1},{1,0},{2,3},{3,2},{4,5},{5,4},{6,7},{7,6},{8,9},{9,8},{10,11... | collective-permute-start | bytes 442376 | tf_op jit(solution)/shard_map/ppermute | solution.py:450
  27.3 6.5 %collective-permute-start.7 = (bf16[4,9,16,128]{3,2,1,0:T(8,128)(2,1)S(1)}, bf16[4,9,16,128]{3,2,1,0:T(8,128)(2,1)S(1)}, u32[]{:S(2)}, u32[]{:S(2)}) collective-permute-start(bf16[4,9,16,128]{3,2,1,0:T(8,128)(2,1)S(1)} %get-tuple-element.61.rest_3_), channel_id=1, source_target_pairs={{0,4},{1,5},{2,6},{3,7},{4,0},{5,1},{6,2},{7,3},{8,12},{9,13},{10,... | collective-permute-start | bytes 442376 | tf_op jit(solution)/shard_map/ppermute | solution.py:450
  29.0 8.2 %collective-permute-start.9 = (bf16[4,7,16,128]{3,2,1,0:T(8,128)(2,1)S(1)}, bf16[4,7,16,128]{3,2,1,0:T(8,128)(2,1)S(1)}, u32[]{:S(2)}, u32[]{:S(2)}) collective-permute-start(bf16[4,7,16,128]{3,2,1,0:T(8,128)(2,1)S(1)} %get-tuple-element.67), channel_id=1, source_target_pairs={{0,5},{1,4},{2,7},{3,6},{4,1},{5,0},{6,3},{7,2},{8,13},{9,12},{10,... | collective-permute-start | bytes 344072 | tf_op jit(solution)/shard_map/ppermute | solution.py:450
  30.3 7.4 %collective-permute-start.10 = (bf16[4,7,16,128]{3,2,1,0:T(8,128)(2,1)S(1)}, bf16[4,7,16,128]{3,2,1,0:T(8,128)(2,1)S(1)}, u32[]{:S(2)}, u32[]{:S(2)}) collective-permute-start(bf16[4,7,16,128]{3,2,1,0:T(8,128)(2,1)S(1)} %get-tuple-element.68), channel_id=1, source_target_pairs={{0,1},{1,0},{2,3},{3,2},{4,5},{5,4},{6,7},{7,6},{8,9},{9,8},{10,11... | collective-permute-start | bytes 344072 | tf_op jit(solution)/shard_map/ppermute | solution.py:450
  31.8 6.3 %collective-permute-start.11 = (bf16[4,7,16,128]{3,2,1,0:T(8,128)(2,1)S(1)}, bf16[4,7,16,128]{3,2,1,0:T(8,128)(2,1)S(1)}, u32[]{:S(2)}, u32[]{:S(2)}) collective-permute-start(bf16[4,7,16,128]{3,2,1,0:T(8,128)(2,1)S(1)} %get-tuple-element.69), channel_id=1, source_target_pairs={{0,4},{1,5},{2,6},{3,7},{4,0},{5,1},{6,2},{7,3},{8,12},{9,13},{10,... | collective-permute-start | bytes 344072 | tf_op jit(solution)/shard_map/ppermute | solution.py:450
  38.3 6.9 %collective-permute-start.12 = (bf16[16,16,128]{2,1,0:T(8,128)(2,1)S(1)}, bf16[16,16,128]{2,1,0:T(8,128)(2,1)S(1)}, u32[]{:S(2)}, u32[]{:S(2)}) collective-permute-start(bf16[16,16,128]{2,1,0:T(8,128)(2,1)S(1)} %get-tuple-element.71), channel_id=1, source_target_pairs={{0,24},{1,25},{2,26},{3,27},{4,28},{5,29},{6,30},{7,31},{8,16},{9,... | collective-permute-start | bytes 196616 | tf_op jit(solution)/shard_map/ppermute | solution.py:450
  41.4 5.8 %collective-permute-start.13 = (bf16[16,16,128]{2,1,0:T(8,128)(2,1)S(1)}, bf16[16,16,128]{2,1,0:T(8,128)(2,1)S(1)}, u32[]{:S(2)}, u32[]{:S(2)}) collective-permute-start(bf16[16,16,128]{2,1,0:T(8,128)(2,1)S(1)} %get-tuple-element.72), channel_id=1, source_target_pairs={{0,16},{1,17},{2,18},{3,19},{4,20},{5,21},{6,22},{7,23},{8,24},{9,... | collective-permute-start | bytes 196616 | tf_op jit(solution)/shard_map/ppermute | solution.py:450
  41.4 5.8 %collective-permute-start.14 = (bf16[16,16,128]{2,1,0:T(8,128)(2,1)S(1)}, bf16[16,16,128]{2,1,0:T(8,128)(2,1)S(1)}, u32[]{:S(2)}, u32[]{:S(2)}) collective-permute-start(bf16[16,16,128]{2,1,0:T(8,128)(2,1)S(1)} %get-tuple-element.73), channel_id=1, source_target_pairs={{0,8},{1,9},{2,10},{3,11},{4,12},{5,13},{6,14},{7,15},{8,0},{9,1},... | collective-permute-start | bytes 196616 | tf_op jit(solution)/shard_map/ppermute | solution.py:450
  47.2 6.0 %collective-permute-start.17 = (bf16[16,16,128]{2,1,0:T(8,128)(2,1)S(1)}, bf16[16,16,128]{2,1,0:T(8,128)(2,1)S(1)}, u32[]{:S(2)}, u32[]{:S(2)}) collective-permute-start(bf16[16,16,128]{2,1,0:T(8,128)(2,1)S(1)} %line_sum.1.a_ref), channel_id=1, source_target_pairs={{0,8},{1,9},{2,10},{3,11},{4,12},{5,13},{6,14},{7,15},{8,0},{9,1},... | collective-permute-start | bytes 196616 | tf_op jit(solution)/shard_map/ppermute | solution.py:450
  47.8 6.6 %collective-permute-start.16 = (bf16[16,16,128]{2,1,0:T(8,128)(2,1)S(1)}, bf16[16,16,128]{2,1,0:T(8,128)(2,1)S(1)}, u32[]{:S(2)}, u32[]{:S(2)}) collective-permute-start(bf16[16,16,128]{2,1,0:T(8,128)(2,1)S(1)} %line_sum.1.a_ref), channel_id=1, source_target_pairs={{0,16},{1,17},{2,18},{3,19},{4,20},{5,21},{6,22},{7,23},{8,24},{9,... | collective-permute-start | bytes 196616 | tf_op jit(solution)/shard_map/ppermute | solution.py:450
  50.5 6.1 %collective-permute-start.15 = (bf16[16,16,128]{2,1,0:T(8,128)(2,1)S(1)}, bf16[16,16,128]{2,1,0:T(8,128)(2,1)S(1)}, u32[]{:S(2)}, u32[]{:S(2)}) collective-permute-start(bf16[16,16,128]{2,1,0:T(8,128)(2,1)S(1)} %line_sum.1.a_ref), channel_id=1, source_target_pairs={{0,24},{1,25},{2,26},{3,27},{4,28},{5,29},{6,30},{7,31},{8,16},{9,... | collective-permute-start | bytes 196616 | tf_op jit(solution)/shard_map/ppermute | solution.py:450
  51.7 8.5 %collective-permute-start.2 = (bf16[64,256]{1,0:T(8,128)(2,1)S(1)}, bf16[64,256]{1,0:T(8,128)(2,1)S(1)}, u32[]{:S(2)}, u32[]{:S(2)}) collective-permute-start(bf16[64,256]{1,0:T(8,128)(2,1)S(1)} %get-tuple-element.51), channel_id=1, source_target_pairs={{0,1},{1,0},{2,3},{3,2},{4,5},{5,4},{6,7},{7,6},{8,9},{9,8},{10,11... | collective-permute-start | bytes 98312 | tf_op jit(solution)/shard_map/ppermute | solution.py:504
  56.6 11.0 %collective-permute-start.20 = (bf16[4,16,16,128]{3,2,1,0:T(8,128)(2,1)S(1)}, bf16[4,16,16,128]{3,2,1,0:T(8,128)(2,1)S(1)}, u32[]{:S(2)}, u32[]{:S(2)}) collective-permute-start(bf16[4,16,16,128]{3,2,1,0:T(8,128)(2,1)S(1)} %line_gather.1.rest_0_.a_ref), channel_id=1, source_target_pairs={{0,4},{1,5},{2,6},{3,7},{4,0},{5,1},{6,2},{7,3},{8,12},{9,13},{10,... | collective-permute-start | bytes 786440 | tf_op jit(solution)/shard_map/ppermute | solution.py:450
  58.0 11.8 %collective-permute-start.19 = (bf16[4,16,16,128]{3,2,1,0:T(8,128)(2,1)S(1)}, bf16[4,16,16,128]{3,2,1,0:T(8,128)(2,1)S(1)}, u32[]{:S(2)}, u32[]{:S(2)}) collective-permute-start(bf16[4,16,16,128]{3,2,1,0:T(8,128)(2,1)S(1)} %line_gather.1.rest_0_.a_ref), channel_id=1, source_target_pairs={{0,1},{1,0},{2,3},{3,2},{4,5},{5,4},{6,7},{7,6},{8,9},{9,8},{10,11... | collective-permute-start | bytes 786440 | tf_op jit(solution)/shard_map/ppermute | solution.py:450
  59.5 10.3 %collective-permute-start.18 = (bf16[4,16,16,128]{3,2,1,0:T(8,128)(2,1)S(1)}, bf16[4,16,16,128]{3,2,1,0:T(8,128)(2,1)S(1)}, u32[]{:S(2)}, u32[]{:S(2)}) collective-permute-start(bf16[4,16,16,128]{3,2,1,0:T(8,128)(2,1)S(1)} %line_gather.1.rest_0_.a_ref), channel_id=1, source_target_pairs={{0,5},{1,4},{2,7},{3,6},{4,1},{5,0},{6,3},{7,2},{8,13},{9,12},{10,... | collective-permute-start | bytes 786440 | tf_op jit(solution)/shard_map/ppermute | solution.py:450
  69.9 2.7 %collective-permute-start.21 = (bf16[16,16,16,128]{3,2,1,0:T(8,128)(2,1)S(1)}, bf16[16,16,16,128]{3,2,1,0:T(8,128)(2,1)S(1)}, u32[]{:S(2)}, u32[]{:S(2)}) collective-permute-start(bf16[16,16,16,128]{3,2,1,0:T(8,128)(2,1)S(1)} %plane_gather.1.half_ref), channel_id=1, source_target_pairs={{0,2},{1,3},{2,0},{3,1},{4,6},{5,7},{6,4},{7,5},{8,10},{9,11},{10,... | collective-permute-start | bytes 3145736 | tf_op jit(solution)/shard_map/ppermute | solution.py:450

commit v21 on v20

--- a/solution.py
+++ b/solution.py
@@ -124,7 +124,7 @@
             at_ref[i * CH : i * CH + CH, pl.ds(at, 256)] = flipped
         return 0
 
-    lax.fori_loop(0, rows // 2, rows_of, 0, unroll=4)
+    lax.fori_loop(0, rows // 2, rows_of, 0, unroll=True)
 
 
 def next_kernel(cot_ref, _, nxt_ref):
@@ -164,7 +164,7 @@
         sp_ref[pl.ds(4 * q, 4)] = total.astype(BF).reshape(4, cols, SLOTS, CH)
         return 0
 
-    lax.fori_loop(0, rows // 4, rows_of, 0)
+    lax.fori_loop(0, rows // 4, rows_of, 0, unroll=True)
 
 
 def upper_kernel(acts_in, prev_ref, ws_ref, _, acts_ref, sp_ref):

time: 74.2 us -> 73.6 us (level)
  Pallas kernels: 23.4 us -> 22.5 us
    pallas_call x19, Pallas kernels: 23.4 us -> 22.5 us  [call(): pl.pallas_call(kernel, out_shape=shapes, in_specs=[s for s, _ in ins], ou...]
  transfers between devices with their start and end apart: 22 -> 22, of which waited for: 14 -> 14; matrix products, arithmetic and copies ran while one was open for 0% -> 0% of each run, Pallas kernels for 29% -> 28%
where the time goes in v21:
time: 73.6 us; the launch traced here: 73.4 us
  starting transfers between devices  27.8 us (38%)
  Pallas kernels  22.5 us (31%)
  waiting for transfers between devices  20.5 us (28%)
  between operations  1.47 us (2%)
  local copies, waits for them, and re-layouts  1.24 us (2%)
    pallas_call x19, Pallas kernels, call(): pl.pallas_call(kernel, out_shape=shapes, in_specs=[s for s, _ in ins], ou...  22.5 us
    ppermute x18, starting transfers between devices, swap(): return lax.ppermute(value, AXES, [(d, d ^ flip) for d in range(tm * grp)])  20.7 us
    ppermute x18, waiting for transfers between devices, swap(): return lax.ppermute(value, AXES, [(d, d ^ flip) for d in range(tm * grp)])  18.1 us
    ppermute x2, starting transfers between devices, from_bands(): got = lax.ppermute(parts[0], 'grp', [(0, 1), (1, 0)])  4.66 us
    ppermute x1, waiting for transfers between devices, around(): lax.ppermute(value, axis, [(i, (i + by) % count) for i in range(count)])  1.95 us
  transfers between devices with their start and end apart: 22, of which 14 were waited for; matrix products, arithmetic and copies ran while one was open for 0% of the time, Pallas kernels for 28%

profile of v21, /device:TPU:0, one launch (start us, length us, event | category | flops | bytes accessed | tf_op | source)
XLA Modules:
  0.0 73.4 jit_solution(7762415856256075318)
XLA Ops:
  1.3 1.2 %copy-done.3 = bf16[16,16,8,256]{3,2,1,0:T(8,128)(2,1)S(1)} copy-done((bf16[16,16,8,256]{3,2,1,0:T(8,128)(2,1)S(1)}, bf16[16,16,8,256]{3,2,1,0:T(8,128)(2,1)}, u32[]{:S(2)}) %copy-start.3) | copy-done | bytes 1048600
  2.5 0.3 edges.1._
  2.8 3.0 %collective-permute-start = (bf16[128,256]{1,0:T(8,128)(2,1)S(1)}, bf16[128,256]{1,0:T(8,128)(2,1)S(1)}, u32[]{:S(2)}, u32[]{:S(2)}) collective-permute-start(bf16[128,256]{1,0:T(8,128)(2,1)S(1)} %edges.1._), channel_id=1, source_target_pairs={{0,1},{1,0},{2,3},{3,2},{4,5},{5,4},{6,7},{7,6},{8,9},{9,8},{10,11... | collective-permute-start | bytes 196616 | tf_op jit(solution)/shard_map/ppermute | solution.py:504
  5.9 1.1 %acts.1 = (bf16[16,8,16,256]{3,2,1,0:T(8,128)(2,1)S(1)}, bf16[18,10,16,256]{3,2,1,0:T(8,128)(2,1)S(1)}, bf16[768,2560]{1,0:T(8,128)(2,1)S(1)}, bf16[288,256]{1,0:T(8,128)(2,1)S(1)}) custom-call(s32[1]{0:T(128)S(6)} %copy.29.count_ref, bf16[16,128,256]{2,1,0:T(8,128)(2,1)S(1)} %bitcast.11, bf16[128,256]{1,0:T(8,128)(2,1)S(1)} %edges.1._), custom_call_target="tpu_custom_call" | custom-call | flops 536870912 | bytes 7651332 | tf_op jit(solution)/shard_map/acts/pallas_call | solution.py:426
  7.0 1.3 %collective-permute-start.1 = (bf16[2,8,4,256]{3,2,1,0:T(4,128)(2,1)S(1)}, bf16[2,8,4,256]{3,2,1,0:T(4,128)(2,1)S(1)}, u32[]{:S(2)}, u32[]{:S(2)}) collective-permute-start(bf16[2,8,4,256]{3,2,1,0:T(4,128)(2,1)S(1)} %next.1.rest_3_), channel_id=1, source_target_pairs={{2,0},{4,2},{6,4},{8,6},{10,8},{12,10},{14,12},{16,14},{18,16},{20... | collective-permute-start | bytes 98312 | tf_op jit(solution)/shard_map/ppermute | solution.py:494
  8.4 0.2 halo.1
  8.5 1.1 %collective-permute-start.3 = (bf16[288,256]{1,0:T(8,128)(2,1)S(1)}, bf16[288,256]{1,0:T(8,128)(2,1)S(1)}, u32[]{:S(2)}, u32[]{:S(2)}) collective-permute-start(bf16[288,256]{1,0:T(8,128)(2,1)S(1)} %get-tuple-element.53), channel_id=1, source_target_pairs={{0,2},{2,4},{4,6},{6,8},{8,10},{10,12},{12,14},{14,16},{16,18},{18... | collective-permute-start | bytes 442376 | tf_op jit(solution)/shard_map/ppermute | solution.py:499
  9.7 0.5 collective-permute-done.1.nxt_ref
  10.1 4.5 %grad_spatial.1 = (bf16[8,4,16,256]{3,2,1,0:T(8,128)(2,1)S(1)}, bf16[16,8,16,256]{3,2,1,0:T(8,128)(2,1)S(1)}, bf16[16,10,16,256]{3,2,1,0:T(8,128)(2,1)S(1)}, bf1...) custom-call(s32[1]{0:T(128)S(6)} %copy.29.count_ref, ...), custom_call_target="tpu_custom_call" | custom-call | flops 3758096384 | bytes 8978436 | tf_op jit(solution)/shard_map/grad_spatial/pallas_call | solution.py:426
  14.7 1.9 %collective-permute-done.3.__1_.prev_ref = bf16[288,256]{1,0:T(8,128)(2,1)S(1)} collective-permute-done((bf16[288,256]{1,0:T(8,128)(2,1)S(1)}, bf16[288,256]{1,0:T(8,128)(2,1)S(1)}, u32[]{:S(2)}, u32[]{:S(2)}) %collective-permute-start.3) | collective-permute-done | bytes 147488 | tf_op jit(solution)/shard_map/ppermute | solution.py:499
  16.6 0.1 collective-permute-start.4
  16.8 1.7 %spatial_upper.1 = (bf16[18,10,16,256]{3,2,1,0:T(8,128)(2,1)S(1)}, bf16[8,8,16,256]{3,2,1,0:T(8,128)(2,1)S(1)}) custom-call(bf16[18,10,16,256]{3,2,1,0:T(8,128)(2,1)S(1)} %get-tuple-element.52.acts_in, bf16[288,256]{1,0:T(8,128)(2,1)S(1)} %collective-permute-done.3.__1_.prev_ref, bf16[9,256,256]{2,1,0:T(8,128)(2,1)S(1)} %bitcast.12, ...), custom_call_target="tpu_custom_call", output_to_operand_aliasing={{0}: (0, {})} | custom-call | flops 1342177280 | bytes 4800512 | tf_op jit(solution)/shard_map/spatial_upper/pallas_call | solution.py:426
  18.5 0.1 collective-permute-done.4.got_ref
  18.6 0.1 plane_send.2
  18.8 2.0 %collective-permute-start.5 = (bf16[4,9,16,128]{3,2,1,0:T(8,128)(2,1)S(1)}, bf16[4,9,16,128]{3,2,1,0:T(8,128)(2,1)S(1)}, u32[]{:S(2)}, u32[]{:S(2)}) collective-permute-start(bf16[4,9,16,128]{3,2,1,0:T(8,128)(2,1)S(1)} %get-tuple-element.59.rest_1_), channel_id=1, source_target_pairs={{0,5},{1,4},{2,7},{3,6},{4,1},{5,0},{6,3},{7,2},{8,13},{9,12},{10,... | collective-permute-start | bytes 442376 | tf_op jit(solution)/shard_map/ppermute | solution.py:450
  20.7 1.4 %spatial_lower.1.lower_ref = bf16[8,8,16,256]{3,2,1,0:T(8,128)(2,1)S(1)} custom-call(bf16[18,10,16,256]{3,2,1,0:T(8,128)(2,1)S(1)} %get-tuple-element.56.acts_ref, bf16[9,256,256]{2,1,0:T(8,128)(2,1)S(1)} %bitcast.13, bf16[4,9,16,128]{3,2,1,0:T(8,128)(2,1)S(1)} %get-tuple-element.58.rest_0_.refs_0_, bf16[4,9,16,128]{3,2,1,0:T(8,128)(2,1)S(1)} %get-tuple-element.59.rest_1_, ...), custom_call_target="tpu_custom_call" | custom-call | flops 1073741824 | bytes 3178496 | tf_op jit(solution)/shard_map/spatial_lower/pallas_call | solution.py:426
  22.1 2.4 %forward.1 = (bf16[512,256]{1,0:T(8,128)(2,1)S(1)}, bf16[16,7,16,128]{3,2,1,0:T(8,128)(2,1)S(1)}, bf16[16,7,16,128]{3,2,1,0:T(8,128)(2,1)S(1)}) custom-call(s32[1]{0:T(128)S(6)} %copy.29.count_ref, bf16[16,8,16,256]{3,2,1,0:T(8,128)(2,1)S(1)} %get-tuple-element.44.xt_ref, bf16[8,8,16,256]{3,2,1,0:T(8,128)(2,1)S(1)} %get-tuple-element.55.rest_0_.upper_ref, ...), custom_call_target="tpu_custom_call" | custom-call | bytes 1024 | tf_op jit(solution)/shard_map/forward/pallas_call | solution.py:426
  24.5 1.2 %collective-permute-done.5.__1_.refs_1_ = bf16[4,9,16,128]{3,2,1,0:T(8,128)(2,1)S(1)} collective-permute-done((bf16[4,9,16,128]{3,2,1,0:T(8,128)(2,1)S(1)}, bf16[4,9,16,128]{3,2,1,0:T(8,128)(2,1)S(1)}, u32[]{:S(2)}, u32[]{:S(2)}) %collective-permute-start.5) | collective-permute-done | bytes 147488 | tf_op jit(solution)/shard_map/ppermute | solution.py:450
  25.7 0.9 %collective-permute-start.6 = (bf16[4,9,16,128]{3,2,1,0:T(8,128)(2,1)S(1)}, bf16[4,9,16,128]{3,2,1,0:T(8,128)(2,1)S(1)}, u32[]{:S(2)}, u32[]{:S(2)}) collective-permute-start(bf16[4,9,16,128]{3,2,1,0:T(8,128)(2,1)S(1)} %get-tuple-element.60.rest_2_), channel_id=1, source_target_pairs={{0,1},{1,0},{2,3},{3,2},{4,5},{5,4},{6,7},{7,6},{8,9},{9,8},{10,11... | collective-permute-start | bytes 442376 | tf_op jit(solution)/shard_map/ppermute | solution.py:450
  26.7 1.5 %collective-permute-start.7 = (bf16[4,9,16,128]{3,2,1,0:T(8,128)(2,1)S(1)}, bf16[4,9,16,128]{3,2,1,0:T(8,128)(2,1)S(1)}, u32[]{:S(2)}, u32[]{:S(2)}) collective-permute-start(bf16[4,9,16,128]{3,2,1,0:T(8,128)(2,1)S(1)} %get-tuple-element.61.rest_3_), channel_id=1, source_target_pairs={{0,4},{1,5},{2,6},{3,7},{4,0},{5,1},{6,2},{7,3},{8,12},{9,13},{10,... | collective-permute-start | bytes 442376 | tf_op jit(solution)/shard_map/ppermute | solution.py:450
  28.2 0.1 plane_send.3
  28.3 1.3 %collective-permute-start.9 = (bf16[4,7,16,128]{3,2,1,0:T(8,128)(2,1)S(1)}, bf16[4,7,16,128]{3,2,1,0:T(8,128)(2,1)S(1)}, u32[]{:S(2)}, u32[]{:S(2)}) collective-permute-start(bf16[4,7,16,128]{3,2,1,0:T(8,128)(2,1)S(1)} %get-tuple-element.67), channel_id=1, source_target_pairs={{0,5},{1,4},{2,7},{3,6},{4,1},{5,0},{6,3},{7,2},{8,13},{9,12},{10,... | collective-permute-start | bytes 344072 | tf_op jit(solution)/shard_map/ppermute | solution.py:450
  29.6 1.6 %collective-permute-start.10 = (bf16[4,7,16,128]{3,2,1,0:T(8,128)(2,1)S(1)}, bf16[4,7,16,128]{3,2,1,0:T(8,128)(2,1)S(1)}, u32[]{:S(2)}, u32[]{:S(2)}) collective-permute-start(bf16[4,7,16,128]{3,2,1,0:T(8,128)(2,1)S(1)} %get-tuple-element.68), channel_id=1, source_target_pairs={{0,1},{1,0},{2,3},{3,2},{4,5},{5,4},{6,7},{7,6},{8,9},{9,8},{10,11... | collective-permute-start | bytes 344072 | tf_op jit(solution)/shard_map/ppermute | solution.py:450
  31.3 0.6 collective-permute-start.11
  31.9 0.1 collective-permute-done.6.refs_2_
  32.0 1.3 %collective-permute-done.7.refs_3_ = bf16[4,9,16,128]{3,2,1,0:T(8,128)(2,1)S(1)} collective-permute-done((bf16[4,9,16,128]{3,2,1,0:T(8,128)(2,1)S(1)}, bf16[4,9,16,128]{3,2,1,0:T(8,128)(2,1)S(1)}, u32[]{:S(2)}, u32[]{:S(2)}) %collective-permute-start.7) | collective-permute-done | bytes 147488 | tf_op jit(solution)/shard_map/ppermute | solution.py:450
  33.3 3.1 %collective-permute-done.9.refs_5_ = bf16[4,7,16,128]{3,2,1,0:T(8,128)(2,1)S(1)} collective-permute-done((bf16[4,7,16,128]{3,2,1,0:T(8,128)(2,1)S(1)}, bf16[4,7,16,128]{3,2,1,0:T(8,128)(2,1)S(1)}, u32[]{:S(2)}, u32[]{:S(2)}) %collective-permute-start.9) | collective-permute-done | bytes 114720 | tf_op jit(solution)/shard_map/ppermute | solution.py:450
  36.4 0.6 collective-permute-done.10.refs_6_
  37.0 0.6 collective-permute-done.11.refs_7_
  37.6 0.1 line_send.1
  37.8 3.1 %collective-permute-start.12 = (bf16[16,16,128]{2,1,0:T(8,128)(2,1)S(1)}, bf16[16,16,128]{2,1,0:T(8,128)(2,1)S(1)}, u32[]{:S(2)}, u32[]{:S(2)}) collective-permute-start(bf16[16,16,128]{2,1,0:T(8,128)(2,1)S(1)} %get-tuple-element.71), channel_id=1, source_target_pairs={{0,24},{1,25},{2,26},{3,27},{4,28},{5,29},{6,30},{7,31},{8,16},{9,... | collective-permute-start | bytes 196616 | tf_op jit(solution)/shard_map/ppermute | solution.py:450
  40.9 1.3 %collective-permute-start.14 = (bf16[16,16,128]{2,1,0:T(8,128)(2,1)S(1)}, bf16[16,16,128]{2,1,0:T(8,128)(2,1)S(1)}, u32[]{:S(2)}, u32[]{:S(2)}) collective-permute-start(bf16[16,16,128]{2,1,0:T(8,128)(2,1)S(1)} %get-tuple-element.73), channel_id=1, source_target_pairs={{0,8},{1,9},{2,10},{3,11},{4,12},{5,13},{6,14},{7,15},{8,0},{9,1},... | collective-permute-start | bytes 196616 | tf_op jit(solution)/shard_map/ppermute | solution.py:450
  42.2 2.5 %collective-permute-done.12.b_ref = bf16[16,16,128]{2,1,0:T(8,128)(2,1)S(1)} collective-permute-done((bf16[16,16,128]{2,1,0:T(8,128)(2,1)S(1)}, bf16[16,16,128]{2,1,0:T(8,128)(2,1)S(1)}, u32[]{:S(2)}, u32[]{:S(2)}) %collective-permute-start.12) | collective-permute-done | bytes 65568 | tf_op jit(solution)/shard_map/ppermute | solution.py:450
  44.7 1.9 %collective-permute-done.13.c_ref = bf16[16,16,128]{2,1,0:T(8,128)(2,1)S(1)} collective-permute-done((bf16[16,16,128]{2,1,0:T(8,128)(2,1)S(1)}, bf16[16,16,128]{2,1,0:T(8,128)(2,1)S(1)}, u32[]{:S(2)}, u32[]{:S(2)}) %collective-permute-start.13) | collective-permute-done | bytes 65568 | tf_op jit(solution)/shard_map/ppermute | solution.py:450
  46.7 0.6 collective-permute-start.17
  47.2 2.7 %collective-permute-start.16 = (bf16[16,16,128]{2,1,0:T(8,128)(2,1)S(1)}, bf16[16,16,128]{2,1,0:T(8,128)(2,1)S(1)}, u32[]{:S(2)}, u32[]{:S(2)}) collective-permute-start(bf16[16,16,128]{2,1,0:T(8,128)(2,1)S(1)} %line_sum.1.a_ref), channel_id=1, source_target_pairs={{0,16},{1,17},{2,18},{3,19},{4,20},{5,21},{6,22},{7,23},{8,24},{9,... | collective-permute-start | bytes 196616 | tf_op jit(solution)/shard_map/ppermute | solution.py:450
  50.0 1.2 %collective-permute-start.15 = (bf16[16,16,128]{2,1,0:T(8,128)(2,1)S(1)}, bf16[16,16,128]{2,1,0:T(8,128)(2,1)S(1)}, u32[]{:S(2)}, u32[]{:S(2)}) collective-permute-start(bf16[16,16,128]{2,1,0:T(8,128)(2,1)S(1)} %line_sum.1.a_ref), channel_id=1, source_target_pairs={{0,24},{1,25},{2,26},{3,27},{4,28},{5,29},{6,30},{7,31},{8,16},{9,... | collective-permute-start | bytes 196616 | tf_op jit(solution)/shard_map/ppermute | solution.py:450
  51.1 1.6 %collective-permute-start.2 = (bf16[64,256]{1,0:T(8,128)(2,1)S(1)}, bf16[64,256]{1,0:T(8,128)(2,1)S(1)}, u32[]{:S(2)}, u32[]{:S(2)}) collective-permute-start(bf16[64,256]{1,0:T(8,128)(2,1)S(1)} %get-tuple-element.51), channel_id=1, source_target_pairs={{0,1},{1,0},{2,3},{3,2},{4,5},{5,4},{6,7},{7,6},{8,9},{9,8},{10,11... | collective-permute-start | bytes 98312 | tf_op jit(solution)/shard_map/ppermute | solution.py:504
  52.8 3.2 %collective-permute-done.15.b_ref = bf16[16,16,128]{2,1,0:T(8,128)(2,1)S(1)} collective-permute-done((bf16[16,16,128]{2,1,0:T(8,128)(2,1)S(1)}, bf16[16,16,128]{2,1,0:T(8,128)(2,1)S(1)}, u32[]{:S(2)}, u32[]{:S(2)}) %collective-permute-start.15) | collective-permute-done | bytes 65568 | tf_op jit(solution)/shard_map/ppermute | solution.py:450
  56.0 1.4 %collective-permute-start.20 = (bf16[4,16,16,128]{3,2,1,0:T(8,128)(2,1)S(1)}, bf16[4,16,16,128]{3,2,1,0:T(8,128)(2,1)S(1)}, u32[]{:S(2)}, u32[]{:S(2)}) collective-permute-start(bf16[4,16,16,128]{3,2,1,0:T(8,128)(2,1)S(1)} %line_gather.1.rest_0_.a_ref), channel_id=1, source_target_pairs={{0,4},{1,5},{2,6},{3,7},{4,0},{5,1},{6,2},{7,3},{8,12},{9,13},{10,... | collective-permute-start | bytes 786440 | tf_op jit(solution)/shard_map/ppermute | solution.py:450
  57.4 1.5 %collective-permute-start.19 = (bf16[4,16,16,128]{3,2,1,0:T(8,128)(2,1)S(1)}, bf16[4,16,16,128]{3,2,1,0:T(8,128)(2,1)S(1)}, u32[]{:S(2)}, u32[]{:S(2)}) collective-permute-start(bf16[4,16,16,128]{3,2,1,0:T(8,128)(2,1)S(1)} %line_gather.1.rest_0_.a_ref), channel_id=1, source_target_pairs={{0,1},{1,0},{2,3},{3,2},{4,5},{5,4},{6,7},{7,6},{8,9},{9,8},{10,11... | collective-permute-start | bytes 786440 | tf_op jit(solution)/shard_map/ppermute | solution.py:450
  58.9 0.7 collective-permute-start.18
  59.6 7.4 %grad_x.1 = (bf16[16,128,256]{2,1,0:T(8,128)(2,1)}, bf16[16,8,4,256]{3,2,1,0:T(4,128)(2,1)}, f32[8,128]{1,0:T(8,128)S(1)}) custom-call(s32[1]{0:T(128)S(6)} %copy.29.count_ref, bf16[16,8,16,256]{3,2,1,0:T(8,128)(2,1)S(1)} %get-tuple-element.44.xt_ref, bf16[16,8,16,256]{3,2,1,0:T(8,128)(2,1)S(1)} %get-tuple-element.49.gy_ref, ...), custom_call_target="tpu_custom_call" | custom-call | flops 2684354560 | bytes 7147524 | tf_op jit(solution)/shard_map/grad_x/pallas_call | solution.py:426
  67.1 2.1 %collective-permute-done.19.c_ref = bf16[4,16,16,128]{3,2,1,0:T(8,128)(2,1)S(1)} collective-permute-done((bf16[4,16,16,128]{3,2,1,0:T(8,128)(2,1)S(1)}, bf16[4,16,16,128]{3,2,1,0:T(8,128)(2,1)S(1)}, u32[]{:S(2)}, u32[]{:S(2)}) %collective-permute-start.19) | collective-permute-done | bytes 262176 | tf_op jit(solution)/shard_map/ppermute | solution.py:450
  69.2 0.1 plane_gather.1.half_ref
  69.3 1.5 %finish.2 = (f32[9,256,256]{2,1,0:T(8,128)}, f32[3,256,256]{2,1,0:T(8,128)}, f32[4,256,256]{2,1,0:T(8,128)}) custom-call(bf16[16,16,16,128]{3,2,1,0:T(8,128)(2,1)S(1)} %plane_gather.1.half_ref), custom_call_target="tpu_custom_call" | custom-call | bytes 5242880 | tf_op jit(solution)/shard_map/finish/pallas_call | solution.py:426
  70.8 1.2 %collective-permute-done.21.half_ref = bf16[16,16,16,128]{3,2,1,0:T(8,128)(2,1)S(1)} collective-permute-done((bf16[16,16,16,128]{3,2,1,0:T(8,128)(2,1)S(1)}, bf16[16,16,16,128]{3,2,1,0:T(8,128)(2,1)S(1)}, u32[]{:S(2)}, u32[]{:S(2)}) %collective-permute-start.21) | collective-permute-done | bytes 1048608 | tf_op jit(solution)/shard_map/ppermute | solution.py:450
  72.0 1.5 %finish.3 = (f32[9,256,256]{2,1,0:T(8,128)}, f32[3,256,256]{2,1,0:T(8,128)}, f32[4,256,256]{2,1,0:T(8,128)}) custom-call(bf16[16,16,16,128]{3,2,1,0:T(8,128)(2,1)S(1)} %collective-permute-done.21.half_ref, f32[9,256,256]{2,1,0:T(8,128)} %get-tuple-element.77.rest_0_, ...), custom_call_target="tpu_custom_call", output_to_operand_aliasing={{0}: (1, {}), {1}: (2, {}), {2}: (3, {})} | custom-call | bytes 9437184 | tf_op jit(solution)/shard_map/finish/pallas_call | solution.py:426
  (25 shorter events, 0.2 us)
Async XLA Ops:
  1.3 1.2 %copy-start.3 = (bf16[16,16,8,256]{3,2,1,0:T(8,128)(2,1)S(1)}, bf16[16,16,8,256]{3,2,1,0:T(8,128)(2,1)}, u32[]{:S(2)}) copy-start(bf16[16,16,8,256]{3,2,1,0:T(8,128)(2,1)} %param.6) | copy-start | bytes 3145732
  2.5 4.5 %copy-start.2 = (bf16[16,8,4,256]{3,2,1,0:T(4,128)(2,1)S(1)}, bf16[16,8,4,256]{3,2,1,0:T(4,128)(2,1)}, u32[]{:S(2)}) copy-start(bf16[16,8,4,256]{3,2,1,0:T(4,128)(2,1)} %cot_ref.3) | copy-start | bytes 786436
  2.8 5.5 %copy-start = (bf16[2,2,256,256]{3,2,1,0:T(8,128)(2,1)S(1)}, bf16[2,2,256,256]{3,2,1,0:T(8,128)(2,1)}, u32[]{:S(2)}) copy-start(bf16[2,2,256,256]{3,2,1,0:T(8,128)(2,1)} %param.10) | copy-start | bytes 1572868
  2.8 5.5 %copy-start.1 = (bf16[3,256,256]{2,1,0:T(8,128)(2,1)S(1)}, bf16[3,256,256]{2,1,0:T(8,128)(2,1)}, u32[]{:S(2)}) copy-start(bf16[3,256,256]{2,1,0:T(8,128)(2,1)} %wt_ref.5) | copy-start | bytes 1179652
  2.8 5.5 %collective-permute-start = (bf16[128,256]{1,0:T(8,128)(2,1)S(1)}, bf16[128,256]{1,0:T(8,128)(2,1)S(1)}, u32[]{:S(2)}, u32[]{:S(2)}) collective-permute-start(bf16[128,256]{1,0:T(8,128)(2,1)S(1)} %edges.1._), channel_id=1, source_target_pairs={{0,1},{1,0},{2,3},{3,2},{4,5},{5,4},{6,7},{7,6},{8,9},{9,8},{10,11... | collective-permute-start | bytes 196616 | tf_op jit(solution)/shard_map/ppermute | solution.py:504
  7.0 3.1 %collective-permute-start.1 = (bf16[2,8,4,256]{3,2,1,0:T(4,128)(2,1)S(1)}, bf16[2,8,4,256]{3,2,1,0:T(4,128)(2,1)S(1)}, u32[]{:S(2)}, u32[]{:S(2)}) collective-permute-start(bf16[2,8,4,256]{3,2,1,0:T(4,128)(2,1)S(1)} %next.1.rest_3_), channel_id=1, source_target_pairs={{2,0},{4,2},{6,4},{8,6},{10,8},{12,10},{14,12},{16,14},{18,16},{20... | collective-permute-start | bytes 98312 | tf_op jit(solution)/shard_map/ppermute | solution.py:494
  8.5 8.1 %collective-permute-start.3 = (bf16[288,256]{1,0:T(8,128)(2,1)S(1)}, bf16[288,256]{1,0:T(8,128)(2,1)S(1)}, u32[]{:S(2)}, u32[]{:S(2)}) collective-permute-start(bf16[288,256]{1,0:T(8,128)(2,1)S(1)} %get-tuple-element.53), channel_id=1, source_target_pairs={{0,2},{2,4},{4,6},{6,8},{8,10},{10,12},{12,14},{14,16},{16,18},{18... | collective-permute-start | bytes 442376 | tf_op jit(solution)/shard_map/ppermute | solution.py:499
  10.1 6.6 %copy-start.4 = (bf16[3,3,256,256]{3,2,1,0:T(8,128)(2,1)S(1)}, bf16[3,3,256,256]{3,2,1,0:T(8,128)(2,1)}, u32[]{:S(2)}) copy-start(bf16[3,3,256,256]{3,2,1,0:T(8,128)(2,1)} %param.8) | copy-start | bytes 3538948
  16.6 2.0 %collective-permute-start.4 = (bf16[16,9,16,128]{3,2,1,0:T(8,128)(2,1)S(1)}, bf16[16,9,16,128]{3,2,1,0:T(8,128)(2,1)S(1)}, u32[]{:S(2)}, u32[]{:S(2)}) collective-permute-start(bf16[16,9,16,128]{3,2,1,0:T(8,128)(2,1)S(1)} %pass.2._), channel_id=1, source_target_pairs={{0,2},{1,3},{2,0},{3,1},{4,6},{5,7},{6,4},{7,5},{8,10},{9,11},{10,... | collective-permute-start | bytes 1769480 | tf_op jit(solution)/shard_map/ppermute | solution.py:450
  18.8 7.0 %collective-permute-start.5 = (bf16[4,9,16,128]{3,2,1,0:T(8,128)(2,1)S(1)}, bf16[4,9,16,128]{3,2,1,0:T(8,128)(2,1)S(1)}, u32[]{:S(2)}, u32[]{:S(2)}) collective-permute-start(bf16[4,9,16,128]{3,2,1,0:T(8,128)(2,1)S(1)} %get-tuple-element.59.rest_1_), channel_id=1, source_target_pairs={{0,5},{1,4},{2,7},{3,6},{4,1},{5,0},{6,3},{7,2},{8,13},{9,12},{10,... | collective-permute-start | bytes 442376 | tf_op jit(solution)/shard_map/ppermute | solution.py:450
  25.7 2.5 %collective-permute-start.8 = (bf16[16,7,16,128]{3,2,1,0:T(8,128)(2,1)S(1)}, bf16[16,7,16,128]{3,2,1,0:T(8,128)(2,1)S(1)}, u32[]{:S(2)}, u32[]{:S(2)}) collective-permute-start(bf16[16,7,16,128]{3,2,1,0:T(8,128)(2,1)S(1)} %pass.3), channel_id=1, source_target_pairs={{0,2},{1,3},{2,0},{3,1},{4,6},{5,7},{6,4},{7,5},{8,10},{9,11},{10,... | collective-permute-start | bytes 1376264 | tf_op jit(solution)/shard_map/ppermute | solution.py:450
  25.7 6.3 %collective-permute-start.6 = (bf16[4,9,16,128]{3,2,1,0:T(8,128)(2,1)S(1)}, bf16[4,9,16,128]{3,2,1,0:T(8,128)(2,1)S(1)}, u32[]{:S(2)}, u32[]{:S(2)}) collective-permute-start(bf16[4,9,16,128]{3,2,1,0:T(8,128)(2,1)S(1)} %get-tuple-element.60.rest_2_), channel_id=1, source_target_pairs={{0,1},{1,0},{2,3},{3,2},{4,5},{5,4},{6,7},{7,6},{8,9},{9,8},{10,11... | collective-permute-start | bytes 442376 | tf_op jit(solution)/shard_map/ppermute | solution.py:450
  26.7 6.6 %collective-permute-start.7 = (bf16[4,9,16,128]{3,2,1,0:T(8,128)(2,1)S(1)}, bf16[4,9,16,128]{3,2,1,0:T(8,128)(2,1)S(1)}, u32[]{:S(2)}, u32[]{:S(2)}) collective-permute-start(bf16[4,9,16,128]{3,2,1,0:T(8,128)(2,1)S(1)} %get-tuple-element.61.rest_3_), channel_id=1, source_target_pairs={{0,4},{1,5},{2,6},{3,7},{4,0},{5,1},{6,2},{7,3},{8,12},{9,13},{10,... | collective-permute-start | bytes 442376 | tf_op jit(solution)/shard_map/ppermute | solution.py:450
  28.3 8.1 %collective-permute-start.9 = (bf16[4,7,16,128]{3,2,1,0:T(8,128)(2,1)S(1)}, bf16[4,7,16,128]{3,2,1,0:T(8,128)(2,1)S(1)}, u32[]{:S(2)}, u32[]{:S(2)}) collective-permute-start(bf16[4,7,16,128]{3,2,1,0:T(8,128)(2,1)S(1)} %get-tuple-element.67), channel_id=1, source_target_pairs={{0,5},{1,4},{2,7},{3,6},{4,1},{5,0},{6,3},{7,2},{8,13},{9,12},{10,... | collective-permute-start | bytes 344072 | tf_op jit(solution)/shard_map/ppermute | solution.py:450
  29.6 7.4 %collective-permute-start.10 = (bf16[4,7,16,128]{3,2,1,0:T(8,128)(2,1)S(1)}, bf16[4,7,16,128]{3,2,1,0:T(8,128)(2,1)S(1)}, u32[]{:S(2)}, u32[]{:S(2)}) collective-permute-start(bf16[4,7,16,128]{3,2,1,0:T(8,128)(2,1)S(1)} %get-tuple-element.68), channel_id=1, source_target_pairs={{0,1},{1,0},{2,3},{3,2},{4,5},{5,4},{6,7},{7,6},{8,9},{9,8},{10,11... | collective-permute-start | bytes 344072 | tf_op jit(solution)/shard_map/ppermute | solution.py:450
  31.3 6.4 %collective-permute-start.11 = (bf16[4,7,16,128]{3,2,1,0:T(8,128)(2,1)S(1)}, bf16[4,7,16,128]{3,2,1,0:T(8,128)(2,1)S(1)}, u32[]{:S(2)}, u32[]{:S(2)}) collective-permute-start(bf16[4,7,16,128]{3,2,1,0:T(8,128)(2,1)S(1)} %get-tuple-element.69), channel_id=1, source_target_pairs={{0,4},{1,5},{2,6},{3,7},{4,0},{5,1},{6,2},{7,3},{8,12},{9,13},{10,... | collective-permute-start | bytes 344072 | tf_op jit(solution)/shard_map/ppermute | solution.py:450
  37.8 6.9 %collective-permute-start.12 = (bf16[16,16,128]{2,1,0:T(8,128)(2,1)S(1)}, bf16[16,16,128]{2,1,0:T(8,128)(2,1)S(1)}, u32[]{:S(2)}, u32[]{:S(2)}) collective-permute-start(bf16[16,16,128]{2,1,0:T(8,128)(2,1)S(1)} %get-tuple-element.71), channel_id=1, source_target_pairs={{0,24},{1,25},{2,26},{3,27},{4,28},{5,29},{6,30},{7,31},{8,16},{9,... | collective-permute-start | bytes 196616 | tf_op jit(solution)/shard_map/ppermute | solution.py:450
  40.9 5.8 %collective-permute-start.13 = (bf16[16,16,128]{2,1,0:T(8,128)(2,1)S(1)}, bf16[16,16,128]{2,1,0:T(8,128)(2,1)S(1)}, u32[]{:S(2)}, u32[]{:S(2)}) collective-permute-start(bf16[16,16,128]{2,1,0:T(8,128)(2,1)S(1)} %get-tuple-element.72), channel_id=1, source_target_pairs={{0,16},{1,17},{2,18},{3,19},{4,20},{5,21},{6,22},{7,23},{8,24},{9,... | collective-permute-start | bytes 196616 | tf_op jit(solution)/shard_map/ppermute | solution.py:450
  40.9 5.8 %collective-permute-start.14 = (bf16[16,16,128]{2,1,0:T(8,128)(2,1)S(1)}, bf16[16,16,128]{2,1,0:T(8,128)(2,1)S(1)}, u32[]{:S(2)}, u32[]{:S(2)}) collective-permute-start(bf16[16,16,128]{2,1,0:T(8,128)(2,1)S(1)} %get-tuple-element.73), channel_id=1, source_target_pairs={{0,8},{1,9},{2,10},{3,11},{4,12},{5,13},{6,14},{7,15},{8,0},{9,1},... | collective-permute-start | bytes 196616 | tf_op jit(solution)/shard_map/ppermute | solution.py:450
  46.7 6.1 %collective-permute-start.17 = (bf16[16,16,128]{2,1,0:T(8,128)(2,1)S(1)}, bf16[16,16,128]{2,1,0:T(8,128)(2,1)S(1)}, u32[]{:S(2)}, u32[]{:S(2)}) collective-permute-start(bf16[16,16,128]{2,1,0:T(8,128)(2,1)S(1)} %line_sum.1.a_ref), channel_id=1, source_target_pairs={{0,8},{1,9},{2,10},{3,11},{4,12},{5,13},{6,14},{7,15},{8,0},{9,1},... | collective-permute-start | bytes 196616 | tf_op jit(solution)/shard_map/ppermute | solution.py:450
  47.2 5.5 %collective-permute-start.16 = (bf16[16,16,128]{2,1,0:T(8,128)(2,1)S(1)}, bf16[16,16,128]{2,1,0:T(8,128)(2,1)S(1)}, u32[]{:S(2)}, u32[]{:S(2)}) collective-permute-start(bf16[16,16,128]{2,1,0:T(8,128)(2,1)S(1)} %line_sum.1.a_ref), channel_id=1, source_target_pairs={{0,16},{1,17},{2,18},{3,19},{4,20},{5,21},{6,22},{7,23},{8,24},{9,... | collective-permute-start | bytes 196616 | tf_op jit(solution)/shard_map/ppermute | solution.py:450
  50.0 6.1 %collective-permute-start.15 = (bf16[16,16,128]{2,1,0:T(8,128)(2,1)S(1)}, bf16[16,16,128]{2,1,0:T(8,128)(2,1)S(1)}, u32[]{:S(2)}, u32[]{:S(2)}) collective-permute-start(bf16[16,16,128]{2,1,0:T(8,128)(2,1)S(1)} %line_sum.1.a_ref), channel_id=1, source_target_pairs={{0,24},{1,25},{2,26},{3,27},{4,28},{5,29},{6,30},{7,31},{8,16},{9,... | collective-permute-start | bytes 196616 | tf_op jit(solution)/shard_map/ppermute | solution.py:450
  51.1 8.5 %collective-permute-start.2 = (bf16[64,256]{1,0:T(8,128)(2,1)S(1)}, bf16[64,256]{1,0:T(8,128)(2,1)S(1)}, u32[]{:S(2)}, u32[]{:S(2)}) collective-permute-start(bf16[64,256]{1,0:T(8,128)(2,1)S(1)} %get-tuple-element.51), channel_id=1, source_target_pairs={{0,1},{1,0},{2,3},{3,2},{4,5},{5,4},{6,7},{7,6},{8,9},{9,8},{10,11... | collective-permute-start | bytes 98312 | tf_op jit(solution)/shard_map/ppermute | solution.py:504
  56.0 11.0 %collective-permute-start.20 = (bf16[4,16,16,128]{3,2,1,0:T(8,128)(2,1)S(1)}, bf16[4,16,16,128]{3,2,1,0:T(8,128)(2,1)S(1)}, u32[]{:S(2)}, u32[]{:S(2)}) collective-permute-start(bf16[4,16,16,128]{3,2,1,0:T(8,128)(2,1)S(1)} %line_gather.1.rest_0_.a_ref), channel_id=1, source_target_pairs={{0,4},{1,5},{2,6},{3,7},{4,0},{5,1},{6,2},{7,3},{8,12},{9,13},{10,... | collective-permute-start | bytes 786440 | tf_op jit(solution)/shard_map/ppermute | solution.py:450
  57.4 11.7 %collective-permute-start.19 = (bf16[4,16,16,128]{3,2,1,0:T(8,128)(2,1)S(1)}, bf16[4,16,16,128]{3,2,1,0:T(8,128)(2,1)S(1)}, u32[]{:S(2)}, u32[]{:S(2)}) collective-permute-start(bf16[4,16,16,128]{3,2,1,0:T(8,128)(2,1)S(1)} %line_gather.1.rest_0_.a_ref), channel_id=1, source_target_pairs={{0,1},{1,0},{2,3},{3,2},{4,5},{5,4},{6,7},{7,6},{8,9},{9,8},{10,11... | collective-permute-start | bytes 786440 | tf_op jit(solution)/shard_map/ppermute | solution.py:450
  58.9 10.2 %collective-permute-start.18 = (bf16[4,16,16,128]{3,2,1,0:T(8,128)(2,1)S(1)}, bf16[4,16,16,128]{3,2,1,0:T(8,128)(2,1)S(1)}, u32[]{:S(2)}, u32[]{:S(2)}) collective-permute-start(bf16[4,16,16,128]{3,2,1,0:T(8,128)(2,1)S(1)} %line_gather.1.rest_0_.a_ref), channel_id=1, source_target_pairs={{0,5},{1,4},{2,7},{3,6},{4,1},{5,0},{6,3},{7,2},{8,13},{9,12},{10,... | collective-permute-start | bytes 786440 | tf_op jit(solution)/shard_map/ppermute | solution.py:450
  69.2 2.7 %collective-permute-start.21 = (bf16[16,16,16,128]{3,2,1,0:T(8,128)(2,1)S(1)}, bf16[16,16,16,128]{3,2,1,0:T(8,128)(2,1)S(1)}, u32[]{:S(2)}, u32[]{:S(2)}) collective-permute-start(bf16[16,16,16,128]{3,2,1,0:T(8,128)(2,1)S(1)} %plane_gather.1.half_ref), channel_id=1, source_target_pairs={{0,2},{1,3},{2,0},{3,1},{4,6},{5,7},{6,4},{7,5},{8,10},{9,11},{10,... | collective-permute-start | bytes 3145736 | tf_op jit(solution)/shard_map/ppermute | solution.py:450

commit v22 on v21

--- a/solution.py
+++ b/solution.py
@@ -235,7 +235,7 @@
         gy_ref[pl.ds(8 * q, 8)] = g.astype(BF).reshape(8, cols, SLOTS, CH)
         return 0
 
-    lax.fori_loop(0, rows // 8, grads_of, 0)
+    lax.fori_loop(0, rows // 8, grads_of, 0, unroll=True)
 
     wide = rows * cols * SLOTS
     for j in range(3):

time: 73.6 us -> 73.8 us (level)
  transfers between devices with their start and end apart: 22 -> 22, of which waited for: 14 -> 13; matrix products, arithmetic and copies ran while one was open for 0% -> 0% of each run, Pallas kernels for 28% -> 28%
where the time goes in v22:
time: 73.8 us; the launch traced here: 73.6 us
  starting transfers between devices  28.1 us (38%)
  Pallas kernels  22.6 us (31%)
  waiting for transfers between devices  20.1 us (27%)
  between operations  1.48 us (2%)
  local copies, waits for them, and re-layouts  1.24 us (2%)
    pallas_call x19, Pallas kernels, call(): pl.pallas_call(kernel, out_shape=shapes, in_specs=[s for s, _ in ins], ou...  22.6 us
    ppermute x18, starting transfers between devices, swap(): return lax.ppermute(value, AXES, [(d, d ^ flip) for d in range(tm * grp)])  21 us
    ppermute x18, waiting for transfers between devices, swap(): return lax.ppermute(value, AXES, [(d, d ^ flip) for d in range(tm * grp)])  17.8 us
    ppermute x2, starting transfers between devices, from_bands(): got = lax.ppermute(parts[0], 'grp', [(0, 1), (1, 0)])  4.66 us
    ppermute x1, waiting for transfers between devices, around(): lax.ppermute(value, axis, [(i, (i + by) % count) for i in range(count)])  1.79 us
  transfers between devices with their start and end apart: 22, of which 13 were waited for; matrix products, arithmetic and copies ran while one was open for 0% of the time, Pallas kernels for 28%

profile of v22, /device:TPU:0, one launch (start us, length us, event | category | flops | bytes accessed | tf_op | source)
XLA Modules:
  0.0 73.6 jit_solution(13700746666637465071)
XLA Ops:
  1.3 1.2 %copy-done.3 = bf16[16,16,8,256]{3,2,1,0:T(8,128)(2,1)S(1)} copy-done((bf16[16,16,8,256]{3,2,1,0:T(8,128)(2,1)S(1)}, bf16[16,16,8,256]{3,2,1,0:T(8,128)(2,1)}, u32[]{:S(2)}) %copy-start.3) | copy-done | bytes 1048600
  2.5 0.3 edges.1._
  2.8 3.0 %collective-permute-start = (bf16[128,256]{1,0:T(8,128)(2,1)S(1)}, bf16[128,256]{1,0:T(8,128)(2,1)S(1)}, u32[]{:S(2)}, u32[]{:S(2)}) collective-permute-start(bf16[128,256]{1,0:T(8,128)(2,1)S(1)} %edges.1._), channel_id=1, source_target_pairs={{0,1},{1,0},{2,3},{3,2},{4,5},{5,4},{6,7},{7,6},{8,9},{9,8},{10,11... | collective-permute-start | bytes 196616 | tf_op jit(solution)/shard_map/ppermute | solution.py:504
  5.9 1.1 %acts.1 = (bf16[16,8,16,256]{3,2,1,0:T(8,128)(2,1)S(1)}, bf16[18,10,16,256]{3,2,1,0:T(8,128)(2,1)S(1)}, bf16[768,2560]{1,0:T(8,128)(2,1)S(1)}, bf16[288,256]{1,0:T(8,128)(2,1)S(1)}) custom-call(s32[1]{0:T(128)S(6)} %copy.29.count_ref, bf16[16,128,256]{2,1,0:T(8,128)(2,1)S(1)} %bitcast.11, bf16[128,256]{1,0:T(8,128)(2,1)S(1)} %edges.1._), custom_call_target="tpu_custom_call" | custom-call | flops 536870912 | bytes 7651332 | tf_op jit(solution)/shard_map/acts/pallas_call | solution.py:426
  7.0 1.3 %collective-permute-start.1 = (bf16[2,8,4,256]{3,2,1,0:T(4,128)(2,1)S(1)}, bf16[2,8,4,256]{3,2,1,0:T(4,128)(2,1)S(1)}, u32[]{:S(2)}, u32[]{:S(2)}) collective-permute-start(bf16[2,8,4,256]{3,2,1,0:T(4,128)(2,1)S(1)} %next.1.rest_3_), channel_id=1, source_target_pairs={{2,0},{4,2},{6,4},{8,6},{10,8},{12,10},{14,12},{16,14},{18,16},{20... | collective-permute-start | bytes 98312 | tf_op jit(solution)/shard_map/ppermute | solution.py:494
  8.4 0.2 halo.1
  8.5 1.1 %collective-permute-start.3 = (bf16[288,256]{1,0:T(8,128)(2,1)S(1)}, bf16[288,256]{1,0:T(8,128)(2,1)S(1)}, u32[]{:S(2)}, u32[]{:S(2)}) collective-permute-start(bf16[288,256]{1,0:T(8,128)(2,1)S(1)} %get-tuple-element.53), channel_id=1, source_target_pairs={{0,2},{2,4},{4,6},{6,8},{8,10},{10,12},{12,14},{14,16},{16,18},{18... | collective-permute-start | bytes 442376 | tf_op jit(solution)/shard_map/ppermute | solution.py:499
  9.7 0.5 collective-permute-done.1.nxt_ref
  10.1 4.7 %grad_spatial.1 = (bf16[8,4,16,256]{3,2,1,0:T(8,128)(2,1)S(1)}, bf16[16,8,16,256]{3,2,1,0:T(8,128)(2,1)S(1)}, bf16[16,10,16,256]{3,2,1,0:T(8,128)(2,1)S(1)}, bf1...) custom-call(s32[1]{0:T(128)S(6)} %copy.29.count_ref, ...), custom_call_target="tpu_custom_call" | custom-call | flops 3758096384 | bytes 8978436 | tf_op jit(solution)/shard_map/grad_spatial/pallas_call | solution.py:426
  14.8 1.8 %collective-permute-done.3.__1_.prev_ref = bf16[288,256]{1,0:T(8,128)(2,1)S(1)} collective-permute-done((bf16[288,256]{1,0:T(8,128)(2,1)S(1)}, bf16[288,256]{1,0:T(8,128)(2,1)S(1)}, u32[]{:S(2)}, u32[]{:S(2)}) %collective-permute-start.3) | collective-permute-done | bytes 147488 | tf_op jit(solution)/shard_map/ppermute | solution.py:499
  16.6 0.3 collective-permute-start.4
  16.9 1.7 %spatial_upper.1 = (bf16[18,10,16,256]{3,2,1,0:T(8,128)(2,1)S(1)}, bf16[8,8,16,256]{3,2,1,0:T(8,128)(2,1)S(1)}) custom-call(bf16[18,10,16,256]{3,2,1,0:T(8,128)(2,1)S(1)} %get-tuple-element.52.acts_in, bf16[288,256]{1,0:T(8,128)(2,1)S(1)} %collective-permute-done.3.__1_.prev_ref, bf16[9,256,256]{2,1,0:T(8,128)(2,1)S(1)} %bitcast.12, ...), custom_call_target="tpu_custom_call", output_to_operand_aliasing={{0}: (0, {})} | custom-call | flops 1342177280 | bytes 4800512 | tf_op jit(solution)/shard_map/spatial_upper/pallas_call | solution.py:426
  18.7 0.2 plane_send.2
  18.8 2.1 %collective-permute-start.5 = (bf16[4,9,16,128]{3,2,1,0:T(8,128)(2,1)S(1)}, bf16[4,9,16,128]{3,2,1,0:T(8,128)(2,1)S(1)}, u32[]{:S(2)}, u32[]{:S(2)}) collective-permute-start(bf16[4,9,16,128]{3,2,1,0:T(8,128)(2,1)S(1)} %get-tuple-element.59.rest_1_), channel_id=1, source_target_pairs={{0,5},{1,4},{2,7},{3,6},{4,1},{5,0},{6,3},{7,2},{8,13},{9,12},{10,... | collective-permute-start | bytes 442376 | tf_op jit(solution)/shard_map/ppermute | solution.py:450
  20.9 1.4 %spatial_lower.1.lower_ref = bf16[8,8,16,256]{3,2,1,0:T(8,128)(2,1)S(1)} custom-call(bf16[18,10,16,256]{3,2,1,0:T(8,128)(2,1)S(1)} %get-tuple-element.56.acts_ref, bf16[9,256,256]{2,1,0:T(8,128)(2,1)S(1)} %bitcast.13, bf16[4,9,16,128]{3,2,1,0:T(8,128)(2,1)S(1)} %get-tuple-element.58.rest_0_.refs_0_, bf16[4,9,16,128]{3,2,1,0:T(8,128)(2,1)S(1)} %get-tuple-element.59.rest_1_, ...), custom_call_target="tpu_custom_call" | custom-call | flops 1073741824 | bytes 3178496 | tf_op jit(solution)/shard_map/spatial_lower/pallas_call | solution.py:426
  22.3 2.4 %forward.1 = (bf16[512,256]{1,0:T(8,128)(2,1)S(1)}, bf16[16,7,16,128]{3,2,1,0:T(8,128)(2,1)S(1)}, bf16[16,7,16,128]{3,2,1,0:T(8,128)(2,1)S(1)}) custom-call(s32[1]{0:T(128)S(6)} %copy.29.count_ref, bf16[16,8,16,256]{3,2,1,0:T(8,128)(2,1)S(1)} %get-tuple-element.44.xt_ref, bf16[8,8,16,256]{3,2,1,0:T(8,128)(2,1)S(1)} %get-tuple-element.55.rest_0_.upper_ref, ...), custom_call_target="tpu_custom_call" | custom-call | bytes 1024 | tf_op jit(solution)/shard_map/forward/pallas_call | solution.py:426
  24.7 1.1 %collective-permute-done.5.__1_.refs_1_ = bf16[4,9,16,128]{3,2,1,0:T(8,128)(2,1)S(1)} collective-permute-done((bf16[4,9,16,128]{3,2,1,0:T(8,128)(2,1)S(1)}, bf16[4,9,16,128]{3,2,1,0:T(8,128)(2,1)S(1)}, u32[]{:S(2)}, u32[]{:S(2)}) %collective-permute-start.5) | collective-permute-done | bytes 147488 | tf_op jit(solution)/shard_map/ppermute | solution.py:450
  25.8 1.0 %collective-permute-start.6 = (bf16[4,9,16,128]{3,2,1,0:T(8,128)(2,1)S(1)}, bf16[4,9,16,128]{3,2,1,0:T(8,128)(2,1)S(1)}, u32[]{:S(2)}, u32[]{:S(2)}) collective-permute-start(bf16[4,9,16,128]{3,2,1,0:T(8,128)(2,1)S(1)} %get-tuple-element.60.rest_2_), channel_id=1, source_target_pairs={{0,1},{1,0},{2,3},{3,2},{4,5},{5,4},{6,7},{7,6},{8,9},{9,8},{10,11... | collective-permute-start | bytes 442376 | tf_op jit(solution)/shard_map/ppermute | solution.py:450
  26.8 1.6 %collective-permute-start.7 = (bf16[4,9,16,128]{3,2,1,0:T(8,128)(2,1)S(1)}, bf16[4,9,16,128]{3,2,1,0:T(8,128)(2,1)S(1)}, u32[]{:S(2)}, u32[]{:S(2)}) collective-permute-start(bf16[4,9,16,128]{3,2,1,0:T(8,128)(2,1)S(1)} %get-tuple-element.61.rest_3_), channel_id=1, source_target_pairs={{0,4},{1,5},{2,6},{3,7},{4,0},{5,1},{6,2},{7,3},{8,12},{9,13},{10,... | collective-permute-start | bytes 442376 | tf_op jit(solution)/shard_map/ppermute | solution.py:450
  28.4 0.1 plane_send.3
  28.5 1.3 %collective-permute-start.9 = (bf16[4,7,16,128]{3,2,1,0:T(8,128)(2,1)S(1)}, bf16[4,7,16,128]{3,2,1,0:T(8,128)(2,1)S(1)}, u32[]{:S(2)}, u32[]{:S(2)}) collective-permute-start(bf16[4,7,16,128]{3,2,1,0:T(8,128)(2,1)S(1)} %get-tuple-element.67), channel_id=1, source_target_pairs={{0,5},{1,4},{2,7},{3,6},{4,1},{5,0},{6,3},{7,2},{8,13},{9,12},{10,... | collective-permute-start | bytes 344072 | tf_op jit(solution)/shard_map/ppermute | solution.py:450
  29.8 1.6 %collective-permute-start.10 = (bf16[4,7,16,128]{3,2,1,0:T(8,128)(2,1)S(1)}, bf16[4,7,16,128]{3,2,1,0:T(8,128)(2,1)S(1)}, u32[]{:S(2)}, u32[]{:S(2)}) collective-permute-start(bf16[4,7,16,128]{3,2,1,0:T(8,128)(2,1)S(1)} %get-tuple-element.68), channel_id=1, source_target_pairs={{0,1},{1,0},{2,3},{3,2},{4,5},{5,4},{6,7},{7,6},{8,9},{9,8},{10,11... | collective-permute-start | bytes 344072 | tf_op jit(solution)/shard_map/ppermute | solution.py:450
  31.4 0.6 collective-permute-start.11
  32.0 1.3 %collective-permute-done.7.refs_3_ = bf16[4,9,16,128]{3,2,1,0:T(8,128)(2,1)S(1)} collective-permute-done((bf16[4,9,16,128]{3,2,1,0:T(8,128)(2,1)S(1)}, bf16[4,9,16,128]{3,2,1,0:T(8,128)(2,1)S(1)}, u32[]{:S(2)}, u32[]{:S(2)}) %collective-permute-start.7) | collective-permute-done | bytes 147488 | tf_op jit(solution)/shard_map/ppermute | solution.py:450
  33.3 3.2 %collective-permute-done.9.refs_5_ = bf16[4,7,16,128]{3,2,1,0:T(8,128)(2,1)S(1)} collective-permute-done((bf16[4,7,16,128]{3,2,1,0:T(8,128)(2,1)S(1)}, bf16[4,7,16,128]{3,2,1,0:T(8,128)(2,1)S(1)}, u32[]{:S(2)}, u32[]{:S(2)}) %collective-permute-start.9) | collective-permute-done | bytes 114720 | tf_op jit(solution)/shard_map/ppermute | solution.py:450
  36.5 0.6 collective-permute-done.10.refs_6_
  37.2 0.6 collective-permute-done.11.refs_7_
  37.7 0.1 line_send.1
  37.9 3.2 %collective-permute-start.12 = (bf16[16,16,128]{2,1,0:T(8,128)(2,1)S(1)}, bf16[16,16,128]{2,1,0:T(8,128)(2,1)S(1)}, u32[]{:S(2)}, u32[]{:S(2)}) collective-permute-start(bf16[16,16,128]{2,1,0:T(8,128)(2,1)S(1)} %get-tuple-element.71), channel_id=1, source_target_pairs={{0,24},{1,25},{2,26},{3,27},{4,28},{5,29},{6,30},{7,31},{8,16},{9,... | collective-permute-start | bytes 196616 | tf_op jit(solution)/shard_map/ppermute | solution.py:450
  41.0 1.3 %collective-permute-start.14 = (bf16[16,16,128]{2,1,0:T(8,128)(2,1)S(1)}, bf16[16,16,128]{2,1,0:T(8,128)(2,1)S(1)}, u32[]{:S(2)}, u32[]{:S(2)}) collective-permute-start(bf16[16,16,128]{2,1,0:T(8,128)(2,1)S(1)} %get-tuple-element.73), channel_id=1, source_target_pairs={{0,8},{1,9},{2,10},{3,11},{4,12},{5,13},{6,14},{7,15},{8,0},{9,1},... | collective-permute-start | bytes 196616 | tf_op jit(solution)/shard_map/ppermute | solution.py:450
  42.3 2.5 %collective-permute-done.12.b_ref = bf16[16,16,128]{2,1,0:T(8,128)(2,1)S(1)} collective-permute-done((bf16[16,16,128]{2,1,0:T(8,128)(2,1)S(1)}, bf16[16,16,128]{2,1,0:T(8,128)(2,1)S(1)}, u32[]{:S(2)}, u32[]{:S(2)}) %collective-permute-start.12) | collective-permute-done | bytes 65568 | tf_op jit(solution)/shard_map/ppermute | solution.py:450
  44.8 2.0 %collective-permute-done.13.c_ref = bf16[16,16,128]{2,1,0:T(8,128)(2,1)S(1)} collective-permute-done((bf16[16,16,128]{2,1,0:T(8,128)(2,1)S(1)}, bf16[16,16,128]{2,1,0:T(8,128)(2,1)S(1)}, u32[]{:S(2)}, u32[]{:S(2)}) %collective-permute-start.13) | collective-permute-done | bytes 65568 | tf_op jit(solution)/shard_map/ppermute | solution.py:450
  46.8 0.6 collective-permute-start.17
  47.4 2.7 %collective-permute-start.16 = (bf16[16,16,128]{2,1,0:T(8,128)(2,1)S(1)}, bf16[16,16,128]{2,1,0:T(8,128)(2,1)S(1)}, u32[]{:S(2)}, u32[]{:S(2)}) collective-permute-start(bf16[16,16,128]{2,1,0:T(8,128)(2,1)S(1)} %line_sum.1.a_ref), channel_id=1, source_target_pairs={{0,16},{1,17},{2,18},{3,19},{4,20},{5,21},{6,22},{7,23},{8,24},{9,... | collective-permute-start | bytes 196616 | tf_op jit(solution)/shard_map/ppermute | solution.py:450
  50.1 1.2 %collective-permute-start.15 = (bf16[16,16,128]{2,1,0:T(8,128)(2,1)S(1)}, bf16[16,16,128]{2,1,0:T(8,128)(2,1)S(1)}, u32[]{:S(2)}, u32[]{:S(2)}) collective-permute-start(bf16[16,16,128]{2,1,0:T(8,128)(2,1)S(1)} %line_sum.1.a_ref), channel_id=1, source_target_pairs={{0,24},{1,25},{2,26},{3,27},{4,28},{5,29},{6,30},{7,31},{8,16},{9,... | collective-permute-start | bytes 196616 | tf_op jit(solution)/shard_map/ppermute | solution.py:450
  51.3 1.6 %collective-permute-start.2 = (bf16[64,256]{1,0:T(8,128)(2,1)S(1)}, bf16[64,256]{1,0:T(8,128)(2,1)S(1)}, u32[]{:S(2)}, u32[]{:S(2)}) collective-permute-start(bf16[64,256]{1,0:T(8,128)(2,1)S(1)} %get-tuple-element.51), channel_id=1, source_target_pairs={{0,1},{1,0},{2,3},{3,2},{4,5},{5,4},{6,7},{7,6},{8,9},{9,8},{10,11... | collective-permute-start | bytes 98312 | tf_op jit(solution)/shard_map/ppermute | solution.py:504
  52.9 1.1 %collective-permute-done.16.c_ref = bf16[16,16,128]{2,1,0:T(8,128)(2,1)S(1)} collective-permute-done((bf16[16,16,128]{2,1,0:T(8,128)(2,1)S(1)}, bf16[16,16,128]{2,1,0:T(8,128)(2,1)S(1)}, u32[]{:S(2)}, u32[]{:S(2)}) %collective-permute-start.16) | collective-permute-done | bytes 65568 | tf_op jit(solution)/shard_map/ppermute | solution.py:450
  54.0 2.2 %collective-permute-done.15.b_ref = bf16[16,16,128]{2,1,0:T(8,128)(2,1)S(1)} collective-permute-done((bf16[16,16,128]{2,1,0:T(8,128)(2,1)S(1)}, bf16[16,16,128]{2,1,0:T(8,128)(2,1)S(1)}, u32[]{:S(2)}, u32[]{:S(2)}) %collective-permute-start.15) | collective-permute-done | bytes 65568 | tf_op jit(solution)/shard_map/ppermute | solution.py:450
  56.2 1.4 %collective-permute-start.20 = (bf16[4,16,16,128]{3,2,1,0:T(8,128)(2,1)S(1)}, bf16[4,16,16,128]{3,2,1,0:T(8,128)(2,1)S(1)}, u32[]{:S(2)}, u32[]{:S(2)}) collective-permute-start(bf16[4,16,16,128]{3,2,1,0:T(8,128)(2,1)S(1)} %line_gather.1.rest_0_.a_ref), channel_id=1, source_target_pairs={{0,4},{1,5},{2,6},{3,7},{4,0},{5,1},{6,2},{7,3},{8,12},{9,13},{10,... | collective-permute-start | bytes 786440 | tf_op jit(solution)/shard_map/ppermute | solution.py:450
  57.6 1.5 %collective-permute-start.19 = (bf16[4,16,16,128]{3,2,1,0:T(8,128)(2,1)S(1)}, bf16[4,16,16,128]{3,2,1,0:T(8,128)(2,1)S(1)}, u32[]{:S(2)}, u32[]{:S(2)}) collective-permute-start(bf16[4,16,16,128]{3,2,1,0:T(8,128)(2,1)S(1)} %line_gather.1.rest_0_.a_ref), channel_id=1, source_target_pairs={{0,1},{1,0},{2,3},{3,2},{4,5},{5,4},{6,7},{7,6},{8,9},{9,8},{10,11... | collective-permute-start | bytes 786440 | tf_op jit(solution)/shard_map/ppermute | solution.py:450
  59.1 0.7 collective-permute-start.18
  59.8 7.4 %grad_x.1 = (bf16[16,128,256]{2,1,0:T(8,128)(2,1)}, bf16[16,8,4,256]{3,2,1,0:T(4,128)(2,1)}, f32[8,128]{1,0:T(8,128)S(1)}) custom-call(s32[1]{0:T(128)S(6)} %copy.29.count_ref, bf16[16,8,16,256]{3,2,1,0:T(8,128)(2,1)S(1)} %get-tuple-element.44.xt_ref, bf16[16,8,16,256]{3,2,1,0:T(8,128)(2,1)S(1)} %get-tuple-element.49.gy_ref, ...), custom_call_target="tpu_custom_call" | custom-call | flops 2684354560 | bytes 7147524 | tf_op jit(solution)/shard_map/grad_x/pallas_call | solution.py:426
  67.2 2.1 %collective-permute-done.19.c_ref = bf16[4,16,16,128]{3,2,1,0:T(8,128)(2,1)S(1)} collective-permute-done((bf16[4,16,16,128]{3,2,1,0:T(8,128)(2,1)S(1)}, bf16[4,16,16,128]{3,2,1,0:T(8,128)(2,1)S(1)}, u32[]{:S(2)}, u32[]{:S(2)}) %collective-permute-start.19) | collective-permute-done | bytes 262176 | tf_op jit(solution)/shard_map/ppermute | solution.py:450
  69.3 0.1 plane_gather.1.half_ref
  69.4 0.1 collective-permute-start.21
  69.5 1.5 %finish.2 = (f32[9,256,256]{2,1,0:T(8,128)}, f32[3,256,256]{2,1,0:T(8,128)}, f32[4,256,256]{2,1,0:T(8,128)}) custom-call(bf16[16,16,16,128]{3,2,1,0:T(8,128)(2,1)S(1)} %plane_gather.1.half_ref), custom_call_target="tpu_custom_call" | custom-call | bytes 5242880 | tf_op jit(solution)/shard_map/finish/pallas_call | solution.py:426
  70.9 1.2 %collective-permute-done.21.half_ref = bf16[16,16,16,128]{3,2,1,0:T(8,128)(2,1)S(1)} collective-permute-done((bf16[16,16,16,128]{3,2,1,0:T(8,128)(2,1)S(1)}, bf16[16,16,16,128]{3,2,1,0:T(8,128)(2,1)S(1)}, u32[]{:S(2)}, u32[]{:S(2)}) %collective-permute-start.21) | collective-permute-done | bytes 1048608 | tf_op jit(solution)/shard_map/ppermute | solution.py:450
  72.1 1.5 %finish.3 = (f32[9,256,256]{2,1,0:T(8,128)}, f32[3,256,256]{2,1,0:T(8,128)}, f32[4,256,256]{2,1,0:T(8,128)}) custom-call(bf16[16,16,16,128]{3,2,1,0:T(8,128)(2,1)S(1)} %collective-permute-done.21.half_ref, f32[9,256,256]{2,1,0:T(8,128)} %get-tuple-element.77.rest_0_, ...), custom_call_target="tpu_custom_call", output_to_operand_aliasing={{0}: (1, {}), {1}: (2, {}), {2}: (3, {})} | custom-call | bytes 9437184 | tf_op jit(solution)/shard_map/finish/pallas_call | solution.py:426
  (25 shorter events, 0.1 us)
Async XLA Ops:
  1.3 1.2 %copy-start.3 = (bf16[16,16,8,256]{3,2,1,0:T(8,128)(2,1)S(1)}, bf16[16,16,8,256]{3,2,1,0:T(8,128)(2,1)}, u32[]{:S(2)}) copy-start(bf16[16,16,8,256]{3,2,1,0:T(8,128)(2,1)} %param.6) | copy-start | bytes 3145732
  2.5 4.5 %copy-start.2 = (bf16[16,8,4,256]{3,2,1,0:T(4,128)(2,1)S(1)}, bf16[16,8,4,256]{3,2,1,0:T(4,128)(2,1)}, u32[]{:S(2)}) copy-start(bf16[16,8,4,256]{3,2,1,0:T(4,128)(2,1)} %cot_ref.3) | copy-start | bytes 786436
  2.8 5.5 %copy-start = (bf16[2,2,256,256]{3,2,1,0:T(8,128)(2,1)S(1)}, bf16[2,2,256,256]{3,2,1,0:T(8,128)(2,1)}, u32[]{:S(2)}) copy-start(bf16[2,2,256,256]{3,2,1,0:T(8,128)(2,1)} %param.10) | copy-start | bytes 1572868
  2.8 5.5 %copy-start.1 = (bf16[3,256,256]{2,1,0:T(8,128)(2,1)S(1)}, bf16[3,256,256]{2,1,0:T(8,128)(2,1)}, u32[]{:S(2)}) copy-start(bf16[3,256,256]{2,1,0:T(8,128)(2,1)} %wt_ref.5) | copy-start | bytes 1179652
  2.8 5.5 %collective-permute-start = (bf16[128,256]{1,0:T(8,128)(2,1)S(1)}, bf16[128,256]{1,0:T(8,128)(2,1)S(1)}, u32[]{:S(2)}, u32[]{:S(2)}) collective-permute-start(bf16[128,256]{1,0:T(8,128)(2,1)S(1)} %edges.1._), channel_id=1, source_target_pairs={{0,1},{1,0},{2,3},{3,2},{4,5},{5,4},{6,7},{7,6},{8,9},{9,8},{10,11... | collective-permute-start | bytes 196616 | tf_op jit(solution)/shard_map/ppermute | solution.py:504
  7.0 3.1 %collective-permute-start.1 = (bf16[2,8,4,256]{3,2,1,0:T(4,128)(2,1)S(1)}, bf16[2,8,4,256]{3,2,1,0:T(4,128)(2,1)S(1)}, u32[]{:S(2)}, u32[]{:S(2)}) collective-permute-start(bf16[2,8,4,256]{3,2,1,0:T(4,128)(2,1)S(1)} %next.1.rest_3_), channel_id=1, source_target_pairs={{2,0},{4,2},{6,4},{8,6},{10,8},{12,10},{14,12},{16,14},{18,16},{20... | collective-permute-start | bytes 98312 | tf_op jit(solution)/shard_map/ppermute | solution.py:494
  8.5 8.1 %collective-permute-start.3 = (bf16[288,256]{1,0:T(8,128)(2,1)S(1)}, bf16[288,256]{1,0:T(8,128)(2,1)S(1)}, u32[]{:S(2)}, u32[]{:S(2)}) collective-permute-start(bf16[288,256]{1,0:T(8,128)(2,1)S(1)} %get-tuple-element.53), channel_id=1, source_target_pairs={{0,2},{2,4},{4,6},{6,8},{8,10},{10,12},{12,14},{14,16},{16,18},{18... | collective-permute-start | bytes 442376 | tf_op jit(solution)/shard_map/ppermute | solution.py:499
  10.1 6.8 %copy-start.4 = (bf16[3,3,256,256]{3,2,1,0:T(8,128)(2,1)S(1)}, bf16[3,3,256,256]{3,2,1,0:T(8,128)(2,1)}, u32[]{:S(2)}) copy-start(bf16[3,3,256,256]{3,2,1,0:T(8,128)(2,1)} %param.8) | copy-start | bytes 3538948
  16.6 2.0 %collective-permute-start.4 = (bf16[16,9,16,128]{3,2,1,0:T(8,128)(2,1)S(1)}, bf16[16,9,16,128]{3,2,1,0:T(8,128)(2,1)S(1)}, u32[]{:S(2)}, u32[]{:S(2)}) collective-permute-start(bf16[16,9,16,128]{3,2,1,0:T(8,128)(2,1)S(1)} %pass.2._), channel_id=1, source_target_pairs={{0,2},{1,3},{2,0},{3,1},{4,6},{5,7},{6,4},{7,5},{8,10},{9,11},{10,... | collective-permute-start | bytes 1769480 | tf_op jit(solution)/shard_map/ppermute | solution.py:450
  18.8 7.0 %collective-permute-start.5 = (bf16[4,9,16,128]{3,2,1,0:T(8,128)(2,1)S(1)}, bf16[4,9,16,128]{3,2,1,0:T(8,128)(2,1)S(1)}, u32[]{:S(2)}, u32[]{:S(2)}) collective-permute-start(bf16[4,9,16,128]{3,2,1,0:T(8,128)(2,1)S(1)} %get-tuple-element.59.rest_1_), channel_id=1, source_target_pairs={{0,5},{1,4},{2,7},{3,6},{4,1},{5,0},{6,3},{7,2},{8,13},{9,12},{10,... | collective-permute-start | bytes 442376 | tf_op jit(solution)/shard_map/ppermute | solution.py:450
  25.8 2.6 %collective-permute-start.8 = (bf16[16,7,16,128]{3,2,1,0:T(8,128)(2,1)S(1)}, bf16[16,7,16,128]{3,2,1,0:T(8,128)(2,1)S(1)}, u32[]{:S(2)}, u32[]{:S(2)}) collective-permute-start(bf16[16,7,16,128]{3,2,1,0:T(8,128)(2,1)S(1)} %pass.3), channel_id=1, source_target_pairs={{0,2},{1,3},{2,0},{3,1},{4,6},{5,7},{6,4},{7,5},{8,10},{9,11},{10,... | collective-permute-start | bytes 1376264 | tf_op jit(solution)/shard_map/ppermute | solution.py:450
  25.8 6.3 %collective-permute-start.6 = (bf16[4,9,16,128]{3,2,1,0:T(8,128)(2,1)S(1)}, bf16[4,9,16,128]{3,2,1,0:T(8,128)(2,1)S(1)}, u32[]{:S(2)}, u32[]{:S(2)}) collective-permute-start(bf16[4,9,16,128]{3,2,1,0:T(8,128)(2,1)S(1)} %get-tuple-element.60.rest_2_), channel_id=1, source_target_pairs={{0,1},{1,0},{2,3},{3,2},{4,5},{5,4},{6,7},{7,6},{8,9},{9,8},{10,11... | collective-permute-start | bytes 442376 | tf_op jit(solution)/shard_map/ppermute | solution.py:450
  26.8 6.5 %collective-permute-start.7 = (bf16[4,9,16,128]{3,2,1,0:T(8,128)(2,1)S(1)}, bf16[4,9,16,128]{3,2,1,0:T(8,128)(2,1)S(1)}, u32[]{:S(2)}, u32[]{:S(2)}) collective-permute-start(bf16[4,9,16,128]{3,2,1,0:T(8,128)(2,1)S(1)} %get-tuple-element.61.rest_3_), channel_id=1, source_target_pairs={{0,4},{1,5},{2,6},{3,7},{4,0},{5,1},{6,2},{7,3},{8,12},{9,13},{10,... | collective-permute-start | bytes 442376 | tf_op jit(solution)/shard_map/ppermute | solution.py:450
  28.5 8.1 %collective-permute-start.9 = (bf16[4,7,16,128]{3,2,1,0:T(8,128)(2,1)S(1)}, bf16[4,7,16,128]{3,2,1,0:T(8,128)(2,1)S(1)}, u32[]{:S(2)}, u32[]{:S(2)}) collective-permute-start(bf16[4,7,16,128]{3,2,1,0:T(8,128)(2,1)S(1)} %get-tuple-element.67), channel_id=1, source_target_pairs={{0,5},{1,4},{2,7},{3,6},{4,1},{5,0},{6,3},{7,2},{8,13},{9,12},{10,... | collective-permute-start | bytes 344072 | tf_op jit(solution)/shard_map/ppermute | solution.py:450
  29.8 7.4 %collective-permute-start.10 = (bf16[4,7,16,128]{3,2,1,0:T(8,128)(2,1)S(1)}, bf16[4,7,16,128]{3,2,1,0:T(8,128)(2,1)S(1)}, u32[]{:S(2)}, u32[]{:S(2)}) collective-permute-start(bf16[4,7,16,128]{3,2,1,0:T(8,128)(2,1)S(1)} %get-tuple-element.68), channel_id=1, source_target_pairs={{0,1},{1,0},{2,3},{3,2},{4,5},{5,4},{6,7},{7,6},{8,9},{9,8},{10,11... | collective-permute-start | bytes 344072 | tf_op jit(solution)/shard_map/ppermute | solution.py:450
  31.4 6.3 %collective-permute-start.11 = (bf16[4,7,16,128]{3,2,1,0:T(8,128)(2,1)S(1)}, bf16[4,7,16,128]{3,2,1,0:T(8,128)(2,1)S(1)}, u32[]{:S(2)}, u32[]{:S(2)}) collective-permute-start(bf16[4,7,16,128]{3,2,1,0:T(8,128)(2,1)S(1)} %get-tuple-element.69), channel_id=1, source_target_pairs={{0,4},{1,5},{2,6},{3,7},{4,0},{5,1},{6,2},{7,3},{8,12},{9,13},{10,... | collective-permute-start | bytes 344072 | tf_op jit(solution)/shard_map/ppermute | solution.py:450
  37.9 6.9 %collective-permute-start.12 = (bf16[16,16,128]{2,1,0:T(8,128)(2,1)S(1)}, bf16[16,16,128]{2,1,0:T(8,128)(2,1)S(1)}, u32[]{:S(2)}, u32[]{:S(2)}) collective-permute-start(bf16[16,16,128]{2,1,0:T(8,128)(2,1)S(1)} %get-tuple-element.71), channel_id=1, source_target_pairs={{0,24},{1,25},{2,26},{3,27},{4,28},{5,29},{6,30},{7,31},{8,16},{9,... | collective-permute-start | bytes 196616 | tf_op jit(solution)/shard_map/ppermute | solution.py:450
  41.0 5.8 %collective-permute-start.13 = (bf16[16,16,128]{2,1,0:T(8,128)(2,1)S(1)}, bf16[16,16,128]{2,1,0:T(8,128)(2,1)S(1)}, u32[]{:S(2)}, u32[]{:S(2)}) collective-permute-start(bf16[16,16,128]{2,1,0:T(8,128)(2,1)S(1)} %get-tuple-element.72), channel_id=1, source_target_pairs={{0,16},{1,17},{2,18},{3,19},{4,20},{5,21},{6,22},{7,23},{8,24},{9,... | collective-permute-start | bytes 196616 | tf_op jit(solution)/shard_map/ppermute | solution.py:450
  41.0 5.8 %collective-permute-start.14 = (bf16[16,16,128]{2,1,0:T(8,128)(2,1)S(1)}, bf16[16,16,128]{2,1,0:T(8,128)(2,1)S(1)}, u32[]{:S(2)}, u32[]{:S(2)}) collective-permute-start(bf16[16,16,128]{2,1,0:T(8,128)(2,1)S(1)} %get-tuple-element.73), channel_id=1, source_target_pairs={{0,8},{1,9},{2,10},{3,11},{4,12},{5,13},{6,14},{7,15},{8,0},{9,1},... | collective-permute-start | bytes 196616 | tf_op jit(solution)/shard_map/ppermute | solution.py:450
  46.8 6.1 %collective-permute-start.17 = (bf16[16,16,128]{2,1,0:T(8,128)(2,1)S(1)}, bf16[16,16,128]{2,1,0:T(8,128)(2,1)S(1)}, u32[]{:S(2)}, u32[]{:S(2)}) collective-permute-start(bf16[16,16,128]{2,1,0:T(8,128)(2,1)S(1)} %line_sum.1.a_ref), channel_id=1, source_target_pairs={{0,8},{1,9},{2,10},{3,11},{4,12},{5,13},{6,14},{7,15},{8,0},{9,1},... | collective-permute-start | bytes 196616 | tf_op jit(solution)/shard_map/ppermute | solution.py:450
  47.4 6.6 %collective-permute-start.16 = (bf16[16,16,128]{2,1,0:T(8,128)(2,1)S(1)}, bf16[16,16,128]{2,1,0:T(8,128)(2,1)S(1)}, u32[]{:S(2)}, u32[]{:S(2)}) collective-permute-start(bf16[16,16,128]{2,1,0:T(8,128)(2,1)S(1)} %line_sum.1.a_ref), channel_id=1, source_target_pairs={{0,16},{1,17},{2,18},{3,19},{4,20},{5,21},{6,22},{7,23},{8,24},{9,... | collective-permute-start | bytes 196616 | tf_op jit(solution)/shard_map/ppermute | solution.py:450
  50.1 6.1 %collective-permute-start.15 = (bf16[16,16,128]{2,1,0:T(8,128)(2,1)S(1)}, bf16[16,16,128]{2,1,0:T(8,128)(2,1)S(1)}, u32[]{:S(2)}, u32[]{:S(2)}) collective-permute-start(bf16[16,16,128]{2,1,0:T(8,128)(2,1)S(1)} %line_sum.1.a_ref), channel_id=1, source_target_pairs={{0,24},{1,25},{2,26},{3,27},{4,28},{5,29},{6,30},{7,31},{8,16},{9,... | collective-permute-start | bytes 196616 | tf_op jit(solution)/shard_map/ppermute | solution.py:450
  51.3 8.5 %collective-permute-start.2 = (bf16[64,256]{1,0:T(8,128)(2,1)S(1)}, bf16[64,256]{1,0:T(8,128)(2,1)S(1)}, u32[]{:S(2)}, u32[]{:S(2)}) collective-permute-start(bf16[64,256]{1,0:T(8,128)(2,1)S(1)} %get-tuple-element.51), channel_id=1, source_target_pairs={{0,1},{1,0},{2,3},{3,2},{4,5},{5,4},{6,7},{7,6},{8,9},{9,8},{10,11... | collective-permute-start | bytes 98312 | tf_op jit(solution)/shard_map/ppermute | solution.py:504
  56.2 11.0 %collective-permute-start.20 = (bf16[4,16,16,128]{3,2,1,0:T(8,128)(2,1)S(1)}, bf16[4,16,16,128]{3,2,1,0:T(8,128)(2,1)S(1)}, u32[]{:S(2)}, u32[]{:S(2)}) collective-permute-start(bf16[4,16,16,128]{3,2,1,0:T(8,128)(2,1)S(1)} %line_gather.1.rest_0_.a_ref), channel_id=1, source_target_pairs={{0,4},{1,5},{2,6},{3,7},{4,0},{5,1},{6,2},{7,3},{8,12},{9,13},{10,... | collective-permute-start | bytes 786440 | tf_op jit(solution)/shard_map/ppermute | solution.py:450
  57.6 11.7 %collective-permute-start.19 = (bf16[4,16,16,128]{3,2,1,0:T(8,128)(2,1)S(1)}, bf16[4,16,16,128]{3,2,1,0:T(8,128)(2,1)S(1)}, u32[]{:S(2)}, u32[]{:S(2)}) collective-permute-start(bf16[4,16,16,128]{3,2,1,0:T(8,128)(2,1)S(1)} %line_gather.1.rest_0_.a_ref), channel_id=1, source_target_pairs={{0,1},{1,0},{2,3},{3,2},{4,5},{5,4},{6,7},{7,6},{8,9},{9,8},{10,11... | collective-permute-start | bytes 786440 | tf_op jit(solution)/shard_map/ppermute | solution.py:450
  59.1 10.2 %collective-permute-start.18 = (bf16[4,16,16,128]{3,2,1,0:T(8,128)(2,1)S(1)}, bf16[4,16,16,128]{3,2,1,0:T(8,128)(2,1)S(1)}, u32[]{:S(2)}, u32[]{:S(2)}) collective-permute-start(bf16[4,16,16,128]{3,2,1,0:T(8,128)(2,1)S(1)} %line_gather.1.rest_0_.a_ref), channel_id=1, source_target_pairs={{0,5},{1,4},{2,7},{3,6},{4,1},{5,0},{6,3},{7,2},{8,13},{9,12},{10,... | collective-permute-start | bytes 786440 | tf_op jit(solution)/shard_map/ppermute | solution.py:450
  69.4 2.7 %collective-permute-start.21 = (bf16[16,16,16,128]{3,2,1,0:T(8,128)(2,1)S(1)}, bf16[16,16,16,128]{3,2,1,0:T(8,128)(2,1)S(1)}, u32[]{:S(2)}, u32[]{:S(2)}) collective-permute-start(bf16[16,16,16,128]{3,2,1,0:T(8,128)(2,1)S(1)} %plane_gather.1.half_ref), channel_id=1, source_target_pairs={{0,2},{1,3},{2,0},{3,1},{4,6},{5,7},{6,4},{7,5},{8,10},{9,11},{10,... | collective-permute-start | bytes 3145736 | tf_op jit(solution)/shard_map/ppermute | solution.py:450

commit v23 on v21

--- a/solution.py
+++ b/solution.py
@@ -355,7 +355,7 @@
 
 
 def line_send_kernel(*refs):
-    outs = refs[8:]
+    outs = refs[-4:]
     _, _, z = place_bits()
     for out, r in zip(outs, ORDER):
         at = 0
@@ -604,7 +604,7 @@
     parts = call(
         line_send_kernel,
         "line_send",
-        [(VMEM, a) for a in parts_a + parts_b],
+        [(VMEM, a) for a in parts_a + parts_b] + [(ANY, a) for a in [cot_top, cot_bot][:sides]],
         [(VMEM, (16, 16, ch // 2))] * 4,
     )
     parts = four_round(list(parts), line, tm, grp)

time: 73.6 us -> 73.8 us (level)
    ppermute x18, waiting for transfers between devices: 18.1 us -> 16 us  [swap(): return lax.ppermute(value, AXES, [(d, d ^ flip) for d in range(tm * grp)])]
    ppermute x2, waiting for transfers between devices: 0.01 us -> 1.52 us  [from_bands(): got = lax.ppermute(parts[0], 'grp', [(0, 1), (1, 0)])]
where the time goes in v23:
time: 73.8 us; the launch traced here: 73.6 us
  starting transfers between devices  28.5 us (39%)
  Pallas kernels  22.5 us (30%)
  waiting for transfers between devices  20 us (27%)
  between operations  1.47 us (2%)
  local copies, waits for them, and re-layouts  1.24 us (2%)
    pallas_call x19, Pallas kernels, call(): pl.pallas_call(kernel, out_shape=shapes, in_specs=[s for s, _ in ins], ou...  22.5 us
    ppermute x18, starting transfers between devices, swap(): return lax.ppermute(value, AXES, [(d, d ^ flip) for d in range(tm * grp)])  21.4 us
    ppermute x18, waiting for transfers between devices, swap(): return lax.ppermute(value, AXES, [(d, d ^ flip) for d in range(tm * grp)])  16 us
    ppermute x2, starting transfers between devices, from_bands(): got = lax.ppermute(parts[0], 'grp', [(0, 1), (1, 0)])  4.65 us
    ppermute x1, waiting for transfers between devices, around(): lax.ppermute(value, axis, [(i, (i + by) % count) for i in range(count)])  1.95 us
    ppermute x2, waiting for transfers between devices, from_bands(): got = lax.ppermute(parts[0], 'grp', [(0, 1), (1, 0)])  1.52 us
  transfers between devices with their start and end apart: 22, of which 14 were waited for; matrix products, arithmetic and copies ran while one was open for 0% of the time, Pallas kernels for 28%

profile of v23, /device:TPU:0, one launch (start us, length us, event | category | flops | bytes accessed | tf_op | source)
XLA Modules:
  0.0 73.6 jit_solution(2187035599813236627)
XLA Ops:
  1.3 1.2 %copy-done.3 = bf16[16,16,8,256]{3,2,1,0:T(8,128)(2,1)S(1)} copy-done((bf16[16,16,8,256]{3,2,1,0:T(8,128)(2,1)S(1)}, bf16[16,16,8,256]{3,2,1,0:T(8,128)(2,1)}, u32[]{:S(2)}) %copy-start.3) | copy-done | bytes 1048600
  2.5 0.3 edges.1._
  2.8 3.0 %collective-permute-start = (bf16[128,256]{1,0:T(8,128)(2,1)S(1)}, bf16[128,256]{1,0:T(8,128)(2,1)S(1)}, u32[]{:S(2)}, u32[]{:S(2)}) collective-permute-start(bf16[128,256]{1,0:T(8,128)(2,1)S(1)} %edges.1._), channel_id=1, source_target_pairs={{0,1},{1,0},{2,3},{3,2},{4,5},{5,4},{6,7},{7,6},{8,9},{9,8},{10,11... | collective-permute-start | bytes 196616 | tf_op jit(solution)/shard_map/ppermute | solution.py:504
  5.9 1.1 %acts.1 = (bf16[16,8,16,256]{3,2,1,0:T(8,128)(2,1)S(1)}, bf16[18,10,16,256]{3,2,1,0:T(8,128)(2,1)S(1)}, bf16[768,2560]{1,0:T(8,128)(2,1)S(1)}, bf16[288,256]{1,0:T(8,128)(2,1)S(1)}) custom-call(s32[1]{0:T(128)S(6)} %copy.29.count_ref, bf16[16,128,256]{2,1,0:T(8,128)(2,1)S(1)} %bitcast.11, bf16[128,256]{1,0:T(8,128)(2,1)S(1)} %edges.1._), custom_call_target="tpu_custom_call" | custom-call | flops 536870912 | bytes 7651332 | tf_op jit(solution)/shard_map/acts/pallas_call | solution.py:426
  7.0 1.3 %collective-permute-start.1 = (bf16[2,8,4,256]{3,2,1,0:T(4,128)(2,1)S(1)}, bf16[2,8,4,256]{3,2,1,0:T(4,128)(2,1)S(1)}, u32[]{:S(2)}, u32[]{:S(2)}) collective-permute-start(bf16[2,8,4,256]{3,2,1,0:T(4,128)(2,1)S(1)} %next.1.rest_3_), channel_id=1, source_target_pairs={{2,0},{4,2},{6,4},{8,6},{10,8},{12,10},{14,12},{16,14},{18,16},{20... | collective-permute-start | bytes 98312 | tf_op jit(solution)/shard_map/ppermute | solution.py:494
  8.4 0.2 halo.1
  8.5 1.1 %collective-permute-start.3 = (bf16[288,256]{1,0:T(8,128)(2,1)S(1)}, bf16[288,256]{1,0:T(8,128)(2,1)S(1)}, u32[]{:S(2)}, u32[]{:S(2)}) collective-permute-start(bf16[288,256]{1,0:T(8,128)(2,1)S(1)} %get-tuple-element.53), channel_id=1, source_target_pairs={{0,2},{2,4},{4,6},{6,8},{8,10},{10,12},{12,14},{14,16},{16,18},{18... | collective-permute-start | bytes 442376 | tf_op jit(solution)/shard_map/ppermute | solution.py:499
  9.7 0.5 collective-permute-done.1.nxt_ref
  10.1 4.5 %grad_spatial.1 = (bf16[8,4,16,256]{3,2,1,0:T(8,128)(2,1)S(1)}, bf16[16,8,16,256]{3,2,1,0:T(8,128)(2,1)S(1)}, bf16[16,10,16,256]{3,2,1,0:T(8,128)(2,1)S(1)}, bf1...) custom-call(s32[1]{0:T(128)S(6)} %copy.29.count_ref, ...), custom_call_target="tpu_custom_call" | custom-call | flops 3758096384 | bytes 8978436 | tf_op jit(solution)/shard_map/grad_spatial/pallas_call | solution.py:426
  14.7 1.9 %collective-permute-done.3.__1_.prev_ref = bf16[288,256]{1,0:T(8,128)(2,1)S(1)} collective-permute-done((bf16[288,256]{1,0:T(8,128)(2,1)S(1)}, bf16[288,256]{1,0:T(8,128)(2,1)S(1)}, u32[]{:S(2)}, u32[]{:S(2)}) %collective-permute-start.3) | collective-permute-done | bytes 147488 | tf_op jit(solution)/shard_map/ppermute | solution.py:499
  16.6 0.1 collective-permute-start.4
  16.8 1.7 %spatial_upper.1 = (bf16[18,10,16,256]{3,2,1,0:T(8,128)(2,1)S(1)}, bf16[8,8,16,256]{3,2,1,0:T(8,128)(2,1)S(1)}) custom-call(bf16[18,10,16,256]{3,2,1,0:T(8,128)(2,1)S(1)} %get-tuple-element.52.acts_in, bf16[288,256]{1,0:T(8,128)(2,1)S(1)} %collective-permute-done.3.__1_.prev_ref, bf16[9,256,256]{2,1,0:T(8,128)(2,1)S(1)} %bitcast.12, ...), custom_call_target="tpu_custom_call", output_to_operand_aliasing={{0}: (0, {})} | custom-call | flops 1342177280 | bytes 4800512 | tf_op jit(solution)/shard_map/spatial_upper/pallas_call | solution.py:426
  18.5 0.1 collective-permute-done.4.got_ref
  18.6 0.1 plane_send.2
  18.8 2.0 %collective-permute-start.5 = (bf16[4,9,16,128]{3,2,1,0:T(8,128)(2,1)S(1)}, bf16[4,9,16,128]{3,2,1,0:T(8,128)(2,1)S(1)}, u32[]{:S(2)}, u32[]{:S(2)}) collective-permute-start(bf16[4,9,16,128]{3,2,1,0:T(8,128)(2,1)S(1)} %get-tuple-element.59.rest_1_), channel_id=1, source_target_pairs={{0,5},{1,4},{2,7},{3,6},{4,1},{5,0},{6,3},{7,2},{8,13},{9,12},{10,... | collective-permute-start | bytes 442376 | tf_op jit(solution)/shard_map/ppermute | solution.py:450
  20.7 1.4 %spatial_lower.1.lower_ref = bf16[8,8,16,256]{3,2,1,0:T(8,128)(2,1)S(1)} custom-call(bf16[18,10,16,256]{3,2,1,0:T(8,128)(2,1)S(1)} %get-tuple-element.56.acts_ref, bf16[9,256,256]{2,1,0:T(8,128)(2,1)S(1)} %bitcast.13, bf16[4,9,16,128]{3,2,1,0:T(8,128)(2,1)S(1)} %get-tuple-element.58.rest_0_.refs_0_, bf16[4,9,16,128]{3,2,1,0:T(8,128)(2,1)S(1)} %get-tuple-element.59.rest_1_, ...), custom_call_target="tpu_custom_call" | custom-call | flops 1073741824 | bytes 3178496 | tf_op jit(solution)/shard_map/spatial_lower/pallas_call | solution.py:426
  22.1 2.4 %forward.1 = (bf16[512,256]{1,0:T(8,128)(2,1)S(1)}, bf16[16,7,16,128]{3,2,1,0:T(8,128)(2,1)S(1)}, bf16[16,7,16,128]{3,2,1,0:T(8,128)(2,1)S(1)}) custom-call(s32[1]{0:T(128)S(6)} %copy.29.count_ref, bf16[16,8,16,256]{3,2,1,0:T(8,128)(2,1)S(1)} %get-tuple-element.44.xt_ref, bf16[8,8,16,256]{3,2,1,0:T(8,128)(2,1)S(1)} %get-tuple-element.55.rest_0_.upper_ref, ...), custom_call_target="tpu_custom_call" | custom-call | bytes 1024 | tf_op jit(solution)/shard_map/forward/pallas_call | solution.py:426
  24.5 1.2 %collective-permute-done.5.__1_.refs_1_ = bf16[4,9,16,128]{3,2,1,0:T(8,128)(2,1)S(1)} collective-permute-done((bf16[4,9,16,128]{3,2,1,0:T(8,128)(2,1)S(1)}, bf16[4,9,16,128]{3,2,1,0:T(8,128)(2,1)S(1)}, u32[]{:S(2)}, u32[]{:S(2)}) %collective-permute-start.5) | collective-permute-done | bytes 147488 | tf_op jit(solution)/shard_map/ppermute | solution.py:450
  25.7 0.9 %collective-permute-start.6 = (bf16[4,9,16,128]{3,2,1,0:T(8,128)(2,1)S(1)}, bf16[4,9,16,128]{3,2,1,0:T(8,128)(2,1)S(1)}, u32[]{:S(2)}, u32[]{:S(2)}) collective-permute-start(bf16[4,9,16,128]{3,2,1,0:T(8,128)(2,1)S(1)} %get-tuple-element.60.rest_2_), channel_id=1, source_target_pairs={{0,1},{1,0},{2,3},{3,2},{4,5},{5,4},{6,7},{7,6},{8,9},{9,8},{10,11... | collective-permute-start | bytes 442376 | tf_op jit(solution)/shard_map/ppermute | solution.py:450
  26.7 1.5 %collective-permute-start.7 = (bf16[4,9,16,128]{3,2,1,0:T(8,128)(2,1)S(1)}, bf16[4,9,16,128]{3,2,1,0:T(8,128)(2,1)S(1)}, u32[]{:S(2)}, u32[]{:S(2)}) collective-permute-start(bf16[4,9,16,128]{3,2,1,0:T(8,128)(2,1)S(1)} %get-tuple-element.61.rest_3_), channel_id=1, source_target_pairs={{0,4},{1,5},{2,6},{3,7},{4,0},{5,1},{6,2},{7,3},{8,12},{9,13},{10,... | collective-permute-start | bytes 442376 | tf_op jit(solution)/shard_map/ppermute | solution.py:450
  28.2 1.6 %collective-permute-start.2 = (bf16[64,256]{1,0:T(8,128)(2,1)S(1)}, bf16[64,256]{1,0:T(8,128)(2,1)S(1)}, u32[]{:S(2)}, u32[]{:S(2)}) collective-permute-start(bf16[64,256]{1,0:T(8,128)(2,1)S(1)} %get-tuple-element.51), channel_id=1, source_target_pairs={{0,1},{1,0},{2,3},{3,2},{4,5},{5,4},{6,7},{7,6},{8,9},{9,8},{10,11... | collective-permute-start | bytes 98312 | tf_op jit(solution)/shard_map/ppermute | solution.py:504
  29.8 0.1 plane_send.3
  29.9 0.4 collective-permute-start.9
  30.4 1.1 %collective-permute-start.10 = (bf16[4,7,16,128]{3,2,1,0:T(8,128)(2,1)S(1)}, bf16[4,7,16,128]{3,2,1,0:T(8,128)(2,1)S(1)}, u32[]{:S(2)}, u32[]{:S(2)}) collective-permute-start(bf16[4,7,16,128]{3,2,1,0:T(8,128)(2,1)S(1)} %get-tuple-element.68), channel_id=1, source_target_pairs={{0,1},{1,0},{2,3},{3,2},{4,5},{5,4},{6,7},{7,6},{8,9},{9,8},{10,11... | collective-permute-start | bytes 344072 | tf_op jit(solution)/shard_map/ppermute | solution.py:450
  31.5 1.5 %collective-permute-done.2.refs_8_.top_ref.bot_ref = bf16[64,256]{1,0:T(8,128)(2,1)S(1)} collective-permute-done((bf16[64,256]{1,0:T(8,128)(2,1)S(1)}, bf16[64,256]{1,0:T(8,128)(2,1)S(1)}, u32[]{:S(2)}, u32[]{:S(2)}) %collective-permute-start.2) | collective-permute-done | bytes 32800 | tf_op jit(solution)/shard_map/ppermute | solution.py:504
  33.0 2.8 %collective-permute-start.11 = (bf16[4,7,16,128]{3,2,1,0:T(8,128)(2,1)S(1)}, bf16[4,7,16,128]{3,2,1,0:T(8,128)(2,1)S(1)}, u32[]{:S(2)}, u32[]{:S(2)}) collective-permute-start(bf16[4,7,16,128]{3,2,1,0:T(8,128)(2,1)S(1)} %get-tuple-element.69), channel_id=1, source_target_pairs={{0,4},{1,5},{2,6},{3,7},{4,0},{5,1},{6,2},{7,3},{8,12},{9,13},{10,... | collective-permute-start | bytes 344072 | tf_op jit(solution)/shard_map/ppermute | solution.py:450
  35.8 0.9 %collective-permute-done.9.refs_5_ = bf16[4,7,16,128]{3,2,1,0:T(8,128)(2,1)S(1)} collective-permute-done((bf16[4,7,16,128]{3,2,1,0:T(8,128)(2,1)S(1)}, bf16[4,7,16,128]{3,2,1,0:T(8,128)(2,1)S(1)}, u32[]{:S(2)}, u32[]{:S(2)}) %collective-permute-start.9) | collective-permute-done | bytes 114720 | tf_op jit(solution)/shard_map/ppermute | solution.py:450
  36.6 1.0 %collective-permute-done.10.refs_6_ = bf16[4,7,16,128]{3,2,1,0:T(8,128)(2,1)S(1)} collective-permute-done((bf16[4,7,16,128]{3,2,1,0:T(8,128)(2,1)S(1)}, bf16[4,7,16,128]{3,2,1,0:T(8,128)(2,1)S(1)}, u32[]{:S(2)}, u32[]{:S(2)}) %collective-permute-start.10) | collective-permute-done | bytes 114720 | tf_op jit(solution)/shard_map/ppermute | solution.py:450
  37.6 0.9 %collective-permute-done.11.refs_7_ = bf16[4,7,16,128]{3,2,1,0:T(8,128)(2,1)S(1)} collective-permute-done((bf16[4,7,16,128]{3,2,1,0:T(8,128)(2,1)S(1)}, bf16[4,7,16,128]{3,2,1,0:T(8,128)(2,1)S(1)}, u32[]{:S(2)}, u32[]{:S(2)}) %collective-permute-start.11) | collective-permute-done | bytes 114720 | tf_op jit(solution)/shard_map/ppermute | solution.py:450
  38.5 0.1 line_send.1
  38.7 3.5 %collective-permute-start.12 = (bf16[16,16,128]{2,1,0:T(8,128)(2,1)S(1)}, bf16[16,16,128]{2,1,0:T(8,128)(2,1)S(1)}, u32[]{:S(2)}, u32[]{:S(2)}) collective-permute-start(bf16[16,16,128]{2,1,0:T(8,128)(2,1)S(1)} %get-tuple-element.71), channel_id=1, source_target_pairs={{0,24},{1,25},{2,26},{3,27},{4,28},{5,29},{6,30},{7,31},{8,16},{9,... | collective-permute-start | bytes 196616 | tf_op jit(solution)/shard_map/ppermute | solution.py:450
  42.2 0.9 %collective-permute-start.14 = (bf16[16,16,128]{2,1,0:T(8,128)(2,1)S(1)}, bf16[16,16,128]{2,1,0:T(8,128)(2,1)S(1)}, u32[]{:S(2)}, u32[]{:S(2)}) collective-permute-start(bf16[16,16,128]{2,1,0:T(8,128)(2,1)S(1)} %get-tuple-element.73), channel_id=1, source_target_pairs={{0,8},{1,9},{2,10},{3,11},{4,12},{5,13},{6,14},{7,15},{8,0},{9,1},... | collective-permute-start | bytes 196616 | tf_op jit(solution)/shard_map/ppermute | solution.py:450
  43.1 1.7 %collective-permute-done.12.b_ref = bf16[16,16,128]{2,1,0:T(8,128)(2,1)S(1)} collective-permute-done((bf16[16,16,128]{2,1,0:T(8,128)(2,1)S(1)}, bf16[16,16,128]{2,1,0:T(8,128)(2,1)S(1)}, u32[]{:S(2)}, u32[]{:S(2)}) %collective-permute-start.12) | collective-permute-done | bytes 65568 | tf_op jit(solution)/shard_map/ppermute | solution.py:450
  44.9 2.7 %collective-permute-done.13.c_ref = bf16[16,16,128]{2,1,0:T(8,128)(2,1)S(1)} collective-permute-done((bf16[16,16,128]{2,1,0:T(8,128)(2,1)S(1)}, bf16[16,16,128]{2,1,0:T(8,128)(2,1)S(1)}, u32[]{:S(2)}, u32[]{:S(2)}) %collective-permute-start.13) | collective-permute-done | bytes 65568 | tf_op jit(solution)/shard_map/ppermute | solution.py:450
  47.6 0.4 collective-permute-start.17
  48.0 2.4 %collective-permute-start.16 = (bf16[16,16,128]{2,1,0:T(8,128)(2,1)S(1)}, bf16[16,16,128]{2,1,0:T(8,128)(2,1)S(1)}, u32[]{:S(2)}, u32[]{:S(2)}) collective-permute-start(bf16[16,16,128]{2,1,0:T(8,128)(2,1)S(1)} %line_sum.1.a_ref), channel_id=1, source_target_pairs={{0,16},{1,17},{2,18},{3,19},{4,20},{5,21},{6,22},{7,23},{8,24},{9,... | collective-permute-start | bytes 196616 | tf_op jit(solution)/shard_map/ppermute | solution.py:450
  50.3 1.7 %collective-permute-start.15 = (bf16[16,16,128]{2,1,0:T(8,128)(2,1)S(1)}, bf16[16,16,128]{2,1,0:T(8,128)(2,1)S(1)}, u32[]{:S(2)}, u32[]{:S(2)}) collective-permute-start(bf16[16,16,128]{2,1,0:T(8,128)(2,1)S(1)} %line_sum.1.a_ref), channel_id=1, source_target_pairs={{0,24},{1,25},{2,26},{3,27},{4,28},{5,29},{6,30},{7,31},{8,16},{9,... | collective-permute-start | bytes 196616 | tf_op jit(solution)/shard_map/ppermute | solution.py:450
  52.0 1.3 %collective-permute-done.17.d_ref = bf16[16,16,128]{2,1,0:T(8,128)(2,1)S(1)} collective-permute-done((bf16[16,16,128]{2,1,0:T(8,128)(2,1)S(1)}, bf16[16,16,128]{2,1,0:T(8,128)(2,1)S(1)}, u32[]{:S(2)}, u32[]{:S(2)}) %collective-permute-start.17) | collective-permute-done | bytes 65568 | tf_op jit(solution)/shard_map/ppermute | solution.py:450
  53.3 3.1 %collective-permute-done.15.b_ref = bf16[16,16,128]{2,1,0:T(8,128)(2,1)S(1)} collective-permute-done((bf16[16,16,128]{2,1,0:T(8,128)(2,1)S(1)}, bf16[16,16,128]{2,1,0:T(8,128)(2,1)S(1)}, u32[]{:S(2)}, u32[]{:S(2)}) %collective-permute-start.15) | collective-permute-done | bytes 65568 | tf_op jit(solution)/shard_map/ppermute | solution.py:450
  56.4 1.6 %collective-permute-start.20 = (bf16[4,16,16,128]{3,2,1,0:T(8,128)(2,1)S(1)}, bf16[4,16,16,128]{3,2,1,0:T(8,128)(2,1)S(1)}, u32[]{:S(2)}, u32[]{:S(2)}) collective-permute-start(bf16[4,16,16,128]{3,2,1,0:T(8,128)(2,1)S(1)} %line_gather.1.rest_0_.a_ref), channel_id=1, source_target_pairs={{0,4},{1,5},{2,6},{3,7},{4,0},{5,1},{6,2},{7,3},{8,12},{9,13},{10,... | collective-permute-start | bytes 786440 | tf_op jit(solution)/shard_map/ppermute | solution.py:450
  58.1 0.8 %collective-permute-start.19 = (bf16[4,16,16,128]{3,2,1,0:T(8,128)(2,1)S(1)}, bf16[4,16,16,128]{3,2,1,0:T(8,128)(2,1)S(1)}, u32[]{:S(2)}, u32[]{:S(2)}) collective-permute-start(bf16[4,16,16,128]{3,2,1,0:T(8,128)(2,1)S(1)} %line_gather.1.rest_0_.a_ref), channel_id=1, source_target_pairs={{0,1},{1,0},{2,3},{3,2},{4,5},{5,4},{6,7},{7,6},{8,9},{9,8},{10,11... | collective-permute-start | bytes 786440 | tf_op jit(solution)/shard_map/ppermute | solution.py:450
  58.8 1.2 %collective-permute-start.18 = (bf16[4,16,16,128]{3,2,1,0:T(8,128)(2,1)S(1)}, bf16[4,16,16,128]{3,2,1,0:T(8,128)(2,1)S(1)}, u32[]{:S(2)}, u32[]{:S(2)}) collective-permute-start(bf16[4,16,16,128]{3,2,1,0:T(8,128)(2,1)S(1)} %line_gather.1.rest_0_.a_ref), channel_id=1, source_target_pairs={{0,5},{1,4},{2,7},{3,6},{4,1},{5,0},{6,3},{7,2},{8,13},{9,12},{10,... | collective-permute-start | bytes 786440 | tf_op jit(solution)/shard_map/ppermute | solution.py:450
  60.0 7.4 %grad_x.1 = (bf16[16,128,256]{2,1,0:T(8,128)(2,1)}, bf16[16,8,4,256]{3,2,1,0:T(4,128)(2,1)}, f32[8,128]{1,0:T(8,128)S(1)}) custom-call(s32[1]{0:T(128)S(6)} %copy.29.count_ref, bf16[16,8,16,256]{3,2,1,0:T(8,128)(2,1)S(1)} %get-tuple-element.44.xt_ref, bf16[16,8,16,256]{3,2,1,0:T(8,128)(2,1)S(1)} %get-tuple-element.49.gy_ref, ...), custom_call_target="tpu_custom_call" | custom-call | flops 2684354560 | bytes 7147524 | tf_op jit(solution)/shard_map/grad_x/pallas_call | solution.py:426
  67.4 1.9 %collective-permute-done.19.c_ref = bf16[4,16,16,128]{3,2,1,0:T(8,128)(2,1)S(1)} collective-permute-done((bf16[4,16,16,128]{3,2,1,0:T(8,128)(2,1)S(1)}, bf16[4,16,16,128]{3,2,1,0:T(8,128)(2,1)S(1)}, u32[]{:S(2)}, u32[]{:S(2)}) %collective-permute-start.19) | collective-permute-done | bytes 262176 | tf_op jit(solution)/shard_map/ppermute | solution.py:450
  69.3 0.1 plane_gather.1.half_ref
  69.5 1.5 %finish.2 = (f32[9,256,256]{2,1,0:T(8,128)}, f32[3,256,256]{2,1,0:T(8,128)}, f32[4,256,256]{2,1,0:T(8,128)}) custom-call(bf16[16,16,16,128]{3,2,1,0:T(8,128)(2,1)S(1)} %plane_gather.1.half_ref), custom_call_target="tpu_custom_call" | custom-call | bytes 5242880 | tf_op jit(solution)/shard_map/finish/pallas_call | solution.py:426
  71.0 1.2 %collective-permute-done.21.half_ref = bf16[16,16,16,128]{3,2,1,0:T(8,128)(2,1)S(1)} collective-permute-done((bf16[16,16,16,128]{3,2,1,0:T(8,128)(2,1)S(1)}, bf16[16,16,16,128]{3,2,1,0:T(8,128)(2,1)S(1)}, u32[]{:S(2)}, u32[]{:S(2)}) %collective-permute-start.21) | collective-permute-done | bytes 1048608 | tf_op jit(solution)/shard_map/ppermute | solution.py:450
  72.2 1.5 %finish.3 = (f32[9,256,256]{2,1,0:T(8,128)}, f32[3,256,256]{2,1,0:T(8,128)}, f32[4,256,256]{2,1,0:T(8,128)}) custom-call(bf16[16,16,16,128]{3,2,1,0:T(8,128)(2,1)S(1)} %collective-permute-done.21.half_ref, f32[9,256,256]{2,1,0:T(8,128)} %get-tuple-element.77.rest_0_, ...), custom_call_target="tpu_custom_call", output_to_operand_aliasing={{0}: (1, {}), {1}: (2, {}), {2}: (3, {})} | custom-call | bytes 9437184 | tf_op jit(solution)/shard_map/finish/pallas_call | solution.py:426
  (25 shorter events, 0.2 us)
Async XLA Ops:
  1.3 1.2 %copy-start.3 = (bf16[16,16,8,256]{3,2,1,0:T(8,128)(2,1)S(1)}, bf16[16,16,8,256]{3,2,1,0:T(8,128)(2,1)}, u32[]{:S(2)}) copy-start(bf16[16,16,8,256]{3,2,1,0:T(8,128)(2,1)} %param.6) | copy-start | bytes 3145732
  2.5 4.5 %copy-start.2 = (bf16[16,8,4,256]{3,2,1,0:T(4,128)(2,1)S(1)}, bf16[16,8,4,256]{3,2,1,0:T(4,128)(2,1)}, u32[]{:S(2)}) copy-start(bf16[16,8,4,256]{3,2,1,0:T(4,128)(2,1)} %cot_ref.3) | copy-start | bytes 786436
  2.8 5.5 %copy-start = (bf16[2,2,256,256]{3,2,1,0:T(8,128)(2,1)S(1)}, bf16[2,2,256,256]{3,2,1,0:T(8,128)(2,1)}, u32[]{:S(2)}) copy-start(bf16[2,2,256,256]{3,2,1,0:T(8,128)(2,1)} %param.10) | copy-start | bytes 1572868
  2.8 5.5 %copy-start.1 = (bf16[3,256,256]{2,1,0:T(8,128)(2,1)S(1)}, bf16[3,256,256]{2,1,0:T(8,128)(2,1)}, u32[]{:S(2)}) copy-start(bf16[3,256,256]{2,1,0:T(8,128)(2,1)} %wt_ref.5) | copy-start | bytes 1179652
  2.8 5.5 %collective-permute-start = (bf16[128,256]{1,0:T(8,128)(2,1)S(1)}, bf16[128,256]{1,0:T(8,128)(2,1)S(1)}, u32[]{:S(2)}, u32[]{:S(2)}) collective-permute-start(bf16[128,256]{1,0:T(8,128)(2,1)S(1)} %edges.1._), channel_id=1, source_target_pairs={{0,1},{1,0},{2,3},{3,2},{4,5},{5,4},{6,7},{7,6},{8,9},{9,8},{10,11... | collective-permute-start | bytes 196616 | tf_op jit(solution)/shard_map/ppermute | solution.py:504
  7.0 3.1 %collective-permute-start.1 = (bf16[2,8,4,256]{3,2,1,0:T(4,128)(2,1)S(1)}, bf16[2,8,4,256]{3,2,1,0:T(4,128)(2,1)S(1)}, u32[]{:S(2)}, u32[]{:S(2)}) collective-permute-start(bf16[2,8,4,256]{3,2,1,0:T(4,128)(2,1)S(1)} %next.1.rest_3_), channel_id=1, source_target_pairs={{2,0},{4,2},{6,4},{8,6},{10,8},{12,10},{14,12},{16,14},{18,16},{20... | collective-permute-start | bytes 98312 | tf_op jit(solution)/shard_map/ppermute | solution.py:494
  8.5 8.1 %collective-permute-start.3 = (bf16[288,256]{1,0:T(8,128)(2,1)S(1)}, bf16[288,256]{1,0:T(8,128)(2,1)S(1)}, u32[]{:S(2)}, u32[]{:S(2)}) collective-permute-start(bf16[288,256]{1,0:T(8,128)(2,1)S(1)} %get-tuple-element.53), channel_id=1, source_target_pairs={{0,2},{2,4},{4,6},{6,8},{8,10},{10,12},{12,14},{14,16},{16,18},{18... | collective-permute-start | bytes 442376 | tf_op jit(solution)/shard_map/ppermute | solution.py:499
  10.1 6.6 %copy-start.4 = (bf16[3,3,256,256]{3,2,1,0:T(8,128)(2,1)S(1)}, bf16[3,3,256,256]{3,2,1,0:T(8,128)(2,1)}, u32[]{:S(2)}) copy-start(bf16[3,3,256,256]{3,2,1,0:T(8,128)(2,1)} %param.8) | copy-start | bytes 3538948
  16.6 2.0 %collective-permute-start.4 = (bf16[16,9,16,128]{3,2,1,0:T(8,128)(2,1)S(1)}, bf16[16,9,16,128]{3,2,1,0:T(8,128)(2,1)S(1)}, u32[]{:S(2)}, u32[]{:S(2)}) collective-permute-start(bf16[16,9,16,128]{3,2,1,0:T(8,128)(2,1)S(1)} %pass.2._), channel_id=1, source_target_pairs={{0,2},{1,3},{2,0},{3,1},{4,6},{5,7},{6,4},{7,5},{8,10},{9,11},{10,... | collective-permute-start | bytes 1769480 | tf_op jit(solution)/shard_map/ppermute | solution.py:450
  18.8 7.0 %collective-permute-start.5 = (bf16[4,9,16,128]{3,2,1,0:T(8,128)(2,1)S(1)}, bf16[4,9,16,128]{3,2,1,0:T(8,128)(2,1)S(1)}, u32[]{:S(2)}, u32[]{:S(2)}) collective-permute-start(bf16[4,9,16,128]{3,2,1,0:T(8,128)(2,1)S(1)} %get-tuple-element.59.rest_1_), channel_id=1, source_target_pairs={{0,5},{1,4},{2,7},{3,6},{4,1},{5,0},{6,3},{7,2},{8,13},{9,12},{10,... | collective-permute-start | bytes 442376 | tf_op jit(solution)/shard_map/ppermute | solution.py:450
  25.7 4.1 %collective-permute-start.8 = (bf16[16,7,16,128]{3,2,1,0:T(8,128)(2,1)S(1)}, bf16[16,7,16,128]{3,2,1,0:T(8,128)(2,1)S(1)}, u32[]{:S(2)}, u32[]{:S(2)}) collective-permute-start(bf16[16,7,16,128]{3,2,1,0:T(8,128)(2,1)S(1)} %pass.3), channel_id=1, source_target_pairs={{0,2},{1,3},{2,0},{3,1},{4,6},{5,7},{6,4},{7,5},{8,10},{9,11},{10,... | collective-permute-start | bytes 1376264 | tf_op jit(solution)/shard_map/ppermute | solution.py:450
  25.7 10.0 %collective-permute-start.6 = (bf16[4,9,16,128]{3,2,1,0:T(8,128)(2,1)S(1)}, bf16[4,9,16,128]{3,2,1,0:T(8,128)(2,1)S(1)}, u32[]{:S(2)}, u32[]{:S(2)}) collective-permute-start(bf16[4,9,16,128]{3,2,1,0:T(8,128)(2,1)S(1)} %get-tuple-element.60.rest_2_), channel_id=1, source_target_pairs={{0,1},{1,0},{2,3},{3,2},{4,5},{5,4},{6,7},{7,6},{8,9},{9,8},{10,11... | collective-permute-start | bytes 442376 | tf_op jit(solution)/shard_map/ppermute | solution.py:450
  26.7 9.1 %collective-permute-start.7 = (bf16[4,9,16,128]{3,2,1,0:T(8,128)(2,1)S(1)}, bf16[4,9,16,128]{3,2,1,0:T(8,128)(2,1)S(1)}, u32[]{:S(2)}, u32[]{:S(2)}) collective-permute-start(bf16[4,9,16,128]{3,2,1,0:T(8,128)(2,1)S(1)} %get-tuple-element.61.rest_3_), channel_id=1, source_target_pairs={{0,4},{1,5},{2,6},{3,7},{4,0},{5,1},{6,2},{7,3},{8,12},{9,13},{10,... | collective-permute-start | bytes 442376 | tf_op jit(solution)/shard_map/ppermute | solution.py:450
  28.2 4.8 %collective-permute-start.2 = (bf16[64,256]{1,0:T(8,128)(2,1)S(1)}, bf16[64,256]{1,0:T(8,128)(2,1)S(1)}, u32[]{:S(2)}, u32[]{:S(2)}) collective-permute-start(bf16[64,256]{1,0:T(8,128)(2,1)S(1)} %get-tuple-element.51), channel_id=1, source_target_pairs={{0,1},{1,0},{2,3},{3,2},{4,5},{5,4},{6,7},{7,6},{8,9},{9,8},{10,11... | collective-permute-start | bytes 98312 | tf_op jit(solution)/shard_map/ppermute | solution.py:504
  29.9 6.7 %collective-permute-start.9 = (bf16[4,7,16,128]{3,2,1,0:T(8,128)(2,1)S(1)}, bf16[4,7,16,128]{3,2,1,0:T(8,128)(2,1)S(1)}, u32[]{:S(2)}, u32[]{:S(2)}) collective-permute-start(bf16[4,7,16,128]{3,2,1,0:T(8,128)(2,1)S(1)} %get-tuple-element.67), channel_id=1, source_target_pairs={{0,5},{1,4},{2,7},{3,6},{4,1},{5,0},{6,3},{7,2},{8,13},{9,12},{10,... | collective-permute-start | bytes 344072 | tf_op jit(solution)/shard_map/ppermute | solution.py:450
  30.4 7.3 %collective-permute-start.10 = (bf16[4,7,16,128]{3,2,1,0:T(8,128)(2,1)S(1)}, bf16[4,7,16,128]{3,2,1,0:T(8,128)(2,1)S(1)}, u32[]{:S(2)}, u32[]{:S(2)}) collective-permute-start(bf16[4,7,16,128]{3,2,1,0:T(8,128)(2,1)S(1)} %get-tuple-element.68), channel_id=1, source_target_pairs={{0,1},{1,0},{2,3},{3,2},{4,5},{5,4},{6,7},{7,6},{8,9},{9,8},{10,11... | collective-permute-start | bytes 344072 | tf_op jit(solution)/shard_map/ppermute | solution.py:450
  33.0 5.5 %collective-permute-start.11 = (bf16[4,7,16,128]{3,2,1,0:T(8,128)(2,1)S(1)}, bf16[4,7,16,128]{3,2,1,0:T(8,128)(2,1)S(1)}, u32[]{:S(2)}, u32[]{:S(2)}) collective-permute-start(bf16[4,7,16,128]{3,2,1,0:T(8,128)(2,1)S(1)} %get-tuple-element.69), channel_id=1, source_target_pairs={{0,4},{1,5},{2,6},{3,7},{4,0},{5,1},{6,2},{7,3},{8,12},{9,13},{10,... | collective-permute-start | bytes 344072 | tf_op jit(solution)/shard_map/ppermute | solution.py:450
  38.7 6.2 %collective-permute-start.12 = (bf16[16,16,128]{2,1,0:T(8,128)(2,1)S(1)}, bf16[16,16,128]{2,1,0:T(8,128)(2,1)S(1)}, u32[]{:S(2)}, u32[]{:S(2)}) collective-permute-start(bf16[16,16,128]{2,1,0:T(8,128)(2,1)S(1)} %get-tuple-element.71), channel_id=1, source_target_pairs={{0,24},{1,25},{2,26},{3,27},{4,28},{5,29},{6,30},{7,31},{8,16},{9,... | collective-permute-start | bytes 196616 | tf_op jit(solution)/shard_map/ppermute | solution.py:450
  42.2 5.4 %collective-permute-start.13 = (bf16[16,16,128]{2,1,0:T(8,128)(2,1)S(1)}, bf16[16,16,128]{2,1,0:T(8,128)(2,1)S(1)}, u32[]{:S(2)}, u32[]{:S(2)}) collective-permute-start(bf16[16,16,128]{2,1,0:T(8,128)(2,1)S(1)} %get-tuple-element.72), channel_id=1, source_target_pairs={{0,16},{1,17},{2,18},{3,19},{4,20},{5,21},{6,22},{7,23},{8,24},{9,... | collective-permute-start | bytes 196616 | tf_op jit(solution)/shard_map/ppermute | solution.py:450
  42.2 5.4 %collective-permute-start.14 = (bf16[16,16,128]{2,1,0:T(8,128)(2,1)S(1)}, bf16[16,16,128]{2,1,0:T(8,128)(2,1)S(1)}, u32[]{:S(2)}, u32[]{:S(2)}) collective-permute-start(bf16[16,16,128]{2,1,0:T(8,128)(2,1)S(1)} %get-tuple-element.73), channel_id=1, source_target_pairs={{0,8},{1,9},{2,10},{3,11},{4,12},{5,13},{6,14},{7,15},{8,0},{9,1},... | collective-permute-start | bytes 196616 | tf_op jit(solution)/shard_map/ppermute | solution.py:450
  47.6 5.7 %collective-permute-start.17 = (bf16[16,16,128]{2,1,0:T(8,128)(2,1)S(1)}, bf16[16,16,128]{2,1,0:T(8,128)(2,1)S(1)}, u32[]{:S(2)}, u32[]{:S(2)}) collective-permute-start(bf16[16,16,128]{2,1,0:T(8,128)(2,1)S(1)} %line_sum.1.a_ref), channel_id=1, source_target_pairs={{0,8},{1,9},{2,10},{3,11},{4,12},{5,13},{6,14},{7,15},{8,0},{9,1},... | collective-permute-start | bytes 196616 | tf_op jit(solution)/shard_map/ppermute | solution.py:450
  48.0 5.3 %collective-permute-start.16 = (bf16[16,16,128]{2,1,0:T(8,128)(2,1)S(1)}, bf16[16,16,128]{2,1,0:T(8,128)(2,1)S(1)}, u32[]{:S(2)}, u32[]{:S(2)}) collective-permute-start(bf16[16,16,128]{2,1,0:T(8,128)(2,1)S(1)} %line_sum.1.a_ref), channel_id=1, source_target_pairs={{0,16},{1,17},{2,18},{3,19},{4,20},{5,21},{6,22},{7,23},{8,24},{9,... | collective-permute-start | bytes 196616 | tf_op jit(solution)/shard_map/ppermute | solution.py:450
  50.3 6.1 %collective-permute-start.15 = (bf16[16,16,128]{2,1,0:T(8,128)(2,1)S(1)}, bf16[16,16,128]{2,1,0:T(8,128)(2,1)S(1)}, u32[]{:S(2)}, u32[]{:S(2)}) collective-permute-start(bf16[16,16,128]{2,1,0:T(8,128)(2,1)S(1)} %line_sum.1.a_ref), channel_id=1, source_target_pairs={{0,24},{1,25},{2,26},{3,27},{4,28},{5,29},{6,30},{7,31},{8,16},{9,... | collective-permute-start | bytes 196616 | tf_op jit(solution)/shard_map/ppermute | solution.py:450
  56.4 11.0 %collective-permute-start.20 = (bf16[4,16,16,128]{3,2,1,0:T(8,128)(2,1)S(1)}, bf16[4,16,16,128]{3,2,1,0:T(8,128)(2,1)S(1)}, u32[]{:S(2)}, u32[]{:S(2)}) collective-permute-start(bf16[4,16,16,128]{3,2,1,0:T(8,128)(2,1)S(1)} %line_gather.1.rest_0_.a_ref), channel_id=1, source_target_pairs={{0,4},{1,5},{2,6},{3,7},{4,0},{5,1},{6,2},{7,3},{8,12},{9,13},{10,... | collective-permute-start | bytes 786440 | tf_op jit(solution)/shard_map/ppermute | solution.py:450
  58.1 11.3 %collective-permute-start.19 = (bf16[4,16,16,128]{3,2,1,0:T(8,128)(2,1)S(1)}, bf16[4,16,16,128]{3,2,1,0:T(8,128)(2,1)S(1)}, u32[]{:S(2)}, u32[]{:S(2)}) collective-permute-start(bf16[4,16,16,128]{3,2,1,0:T(8,128)(2,1)S(1)} %line_gather.1.rest_0_.a_ref), channel_id=1, source_target_pairs={{0,1},{1,0},{2,3},{3,2},{4,5},{5,4},{6,7},{7,6},{8,9},{9,8},{10,11... | collective-permute-start | bytes 786440 | tf_op jit(solution)/shard_map/ppermute | solution.py:450
  58.8 10.5 %collective-permute-start.18 = (bf16[4,16,16,128]{3,2,1,0:T(8,128)(2,1)S(1)}, bf16[4,16,16,128]{3,2,1,0:T(8,128)(2,1)S(1)}, u32[]{:S(2)}, u32[]{:S(2)}) collective-permute-start(bf16[4,16,16,128]{3,2,1,0:T(8,128)(2,1)S(1)} %line_gather.1.rest_0_.a_ref), channel_id=1, source_target_pairs={{0,5},{1,4},{2,7},{3,6},{4,1},{5,0},{6,3},{7,2},{8,13},{9,12},{10,... | collective-permute-start | bytes 786440 | tf_op jit(solution)/shard_map/ppermute | solution.py:450
  69.4 2.7 %collective-permute-start.21 = (bf16[16,16,16,128]{3,2,1,0:T(8,128)(2,1)S(1)}, bf16[16,16,16,128]{3,2,1,0:T(8,128)(2,1)S(1)}, u32[]{:S(2)}, u32[]{:S(2)}) collective-permute-start(bf16[16,16,16,128]{3,2,1,0:T(8,128)(2,1)S(1)} %plane_gather.1.half_ref), channel_id=1, source_target_pairs={{0,2},{1,3},{2,0},{3,1},{4,6},{5,7},{6,4},{7,5},{8,10},{9,11},{10,... | collective-permute-start | bytes 3145736 | tf_op jit(solution)/shard_map/ppermute | solution.py:450

commit v24 on v21

--- a/solution.py
+++ b/solution.py
@@ -567,7 +567,6 @@
     )
     send_a = passed(send_a, [prev])
     got_a = core_round(send_a, tm, grp)
-    cot_top, cot_bot = from_bands(edge)
     half_tile = (rows // 2, cols, slots, ch)
     acts, upper = call(
         upper_kernel,
@@ -579,6 +578,7 @@
     )
     _, plane, line, others = plan(tm, grp)
     parts_a = plane_send(keep_a, got_a, [upper])
+    cot_top, cot_bot = from_bands([passed(e, [parts_a[1]]) for e in edge])
     (lower,) = call(
         lower_kernel,
         "spatial_lower",
@@ -598,7 +598,7 @@
         grant=14,
     )
     parts_a = four_round(parts_a, plane, tm, grp)
-    send_b = passed(send_b, parts_a[1:2])
+    send_b = passed(send_b, parts_a[1:2] + [cot_top, cot_bot][:sides])
     parts_b = plane_send(keep_b, core_round(send_b, tm, grp), [])
     parts_b = four_round(parts_b, plane, tm, grp)
     parts = call(

time: 73.6 us -> 74 us (level)
    pallas_call x19 -> x20, Pallas kernels: 22.5 us -> 22.5 us  [call(): pl.pallas_call(kernel, out_shape=shapes, in_specs=[s for s, _ in ins], ou...]
  transfers between devices with their start and end apart: 22 -> 22, of which waited for: 14 -> 15; matrix products, arithmetic and copies ran while one was open for 0% -> 0% of each run, Pallas kernels for 28% -> 28%
where the time goes in v24:
time: 74 us; the launch traced here: 73.8 us
  starting transfers between devices  27.6 us (37%)
  Pallas kernels  22.5 us (30%)
  waiting for transfers between devices  21 us (28%)
  between operations  1.47 us (2%)
  local copies, waits for them, and re-layouts  1.24 us (2%)
    pallas_call x20, Pallas kernels, call(): pl.pallas_call(kernel, out_shape=shapes, in_specs=[s for s, _ in ins], ou...  22.5 us
    ppermute x18, starting transfers between devices, swap(): return lax.ppermute(value, AXES, [(d, d ^ flip) for d in range(tm * grp)])  20.6 us
    ppermute x18, waiting for transfers between devices, swap(): return lax.ppermute(value, AXES, [(d, d ^ flip) for d in range(tm * grp)])  18.2 us
    ppermute x2, starting transfers between devices, from_bands(): got = lax.ppermute(parts[0], 'grp', [(0, 1), (1, 0)])  4.65 us
    ppermute x1, waiting for transfers between devices, around(): lax.ppermute(value, axis, [(i, (i + by) % count) for i in range(count)])  1.95 us
  transfers between devices with their start and end apart: 22, of which 15 were waited for; matrix products, arithmetic and copies ran while one was open for 0% of the time, Pallas kernels for 28%

profile of v24, /device:TPU:0, one launch (start us, length us, event | category | flops | bytes accessed | tf_op | source)
XLA Modules:
  0.0 73.8 jit_solution(17342074125143610849)
XLA Ops:
  1.3 1.2 %copy-done.3 = bf16[16,16,8,256]{3,2,1,0:T(8,128)(2,1)S(1)} copy-done((bf16[16,16,8,256]{3,2,1,0:T(8,128)(2,1)S(1)}, bf16[16,16,8,256]{3,2,1,0:T(8,128)(2,1)}, u32[]{:S(2)}) %copy-start.3) | copy-done | bytes 1048600
  2.5 0.3 edges.1._
  2.8 3.0 %collective-permute-start = (bf16[128,256]{1,0:T(8,128)(2,1)S(1)}, bf16[128,256]{1,0:T(8,128)(2,1)S(1)}, u32[]{:S(2)}, u32[]{:S(2)}) collective-permute-start(bf16[128,256]{1,0:T(8,128)(2,1)S(1)} %edges.1._), channel_id=1, source_target_pairs={{0,1},{1,0},{2,3},{3,2},{4,5},{5,4},{6,7},{7,6},{8,9},{9,8},{10,11... | collective-permute-start | bytes 196616 | tf_op jit(solution)/shard_map/ppermute | solution.py:504
  5.9 1.1 %acts.1 = (bf16[16,8,16,256]{3,2,1,0:T(8,128)(2,1)S(1)}, bf16[18,10,16,256]{3,2,1,0:T(8,128)(2,1)S(1)}, bf16[768,2560]{1,0:T(8,128)(2,1)S(1)}, bf16[288,256]{1,0:T(8,128)(2,1)S(1)}) custom-call(s32[1]{0:T(128)S(6)} %copy.31.count_ref, bf16[16,128,256]{2,1,0:T(8,128)(2,1)S(1)} %bitcast.11, bf16[128,256]{1,0:T(8,128)(2,1)S(1)} %edges.1._), custom_call_target="tpu_custom_call" | custom-call | flops 536870912 | bytes 7651332 | tf_op jit(solution)/shard_map/acts/pallas_call | solution.py:426
  7.0 1.3 %collective-permute-start.1 = (bf16[2,8,4,256]{3,2,1,0:T(4,128)(2,1)S(1)}, bf16[2,8,4,256]{3,2,1,0:T(4,128)(2,1)S(1)}, u32[]{:S(2)}, u32[]{:S(2)}) collective-permute-start(bf16[2,8,4,256]{3,2,1,0:T(4,128)(2,1)S(1)} %next.1.rest_3_), channel_id=1, source_target_pairs={{2,0},{4,2},{6,4},{8,6},{10,8},{12,10},{14,12},{16,14},{18,16},{20... | collective-permute-start | bytes 98312 | tf_op jit(solution)/shard_map/ppermute | solution.py:494
  8.4 0.2 halo.1
  8.5 1.1 %collective-permute-start.2 = (bf16[288,256]{1,0:T(8,128)(2,1)S(1)}, bf16[288,256]{1,0:T(8,128)(2,1)S(1)}, u32[]{:S(2)}, u32[]{:S(2)}) collective-permute-start(bf16[288,256]{1,0:T(8,128)(2,1)S(1)} %get-tuple-element.54), channel_id=1, source_target_pairs={{0,2},{2,4},{4,6},{6,8},{8,10},{10,12},{12,14},{14,16},{16,18},{18... | collective-permute-start | bytes 442376 | tf_op jit(solution)/shard_map/ppermute | solution.py:499
  9.7 0.5 collective-permute-done.1.nxt_ref
  10.1 4.5 %grad_spatial.1 = (bf16[8,4,16,256]{3,2,1,0:T(8,128)(2,1)S(1)}, bf16[16,8,16,256]{3,2,1,0:T(8,128)(2,1)S(1)}, bf16[16,10,16,256]{3,2,1,0:T(8,128)(2,1)S(1)}, bf1...) custom-call(s32[1]{0:T(128)S(6)} %copy.31.count_ref, ...), custom_call_target="tpu_custom_call" | custom-call | flops 3758096384 | bytes 8978436 | tf_op jit(solution)/shard_map/grad_spatial/pallas_call | solution.py:426
  14.7 1.9 %collective-permute-done.2.__1_.prev_ref = bf16[288,256]{1,0:T(8,128)(2,1)S(1)} collective-permute-done((bf16[288,256]{1,0:T(8,128)(2,1)S(1)}, bf16[288,256]{1,0:T(8,128)(2,1)S(1)}, u32[]{:S(2)}, u32[]{:S(2)}) %collective-permute-start.2) | collective-permute-done | bytes 147488 | tf_op jit(solution)/shard_map/ppermute | solution.py:499
  16.6 0.1 collective-permute-start.3
  16.8 1.7 %spatial_upper.1 = (bf16[18,10,16,256]{3,2,1,0:T(8,128)(2,1)S(1)}, bf16[8,8,16,256]{3,2,1,0:T(8,128)(2,1)S(1)}) custom-call(bf16[18,10,16,256]{3,2,1,0:T(8,128)(2,1)S(1)} %get-tuple-element.55.acts_in, bf16[288,256]{1,0:T(8,128)(2,1)S(1)} %collective-permute-done.2.__1_.prev_ref, bf16[9,256,256]{2,1,0:T(8,128)(2,1)S(1)} %bitcast.12, ...), custom_call_target="tpu_custom_call", output_to_operand_aliasing={{0}: (0, {})} | custom-call | flops 1342177280 | bytes 4800512 | tf_op jit(solution)/shard_map/spatial_upper/pallas_call | solution.py:426
  18.5 0.1 collective-permute-done.3.got_ref
  18.6 0.1 plane_send.2
  18.8 2.0 %collective-permute-start.5 = (bf16[4,9,16,128]{3,2,1,0:T(8,128)(2,1)S(1)}, bf16[4,9,16,128]{3,2,1,0:T(8,128)(2,1)S(1)}, u32[]{:S(2)}, u32[]{:S(2)}) collective-permute-start(bf16[4,9,16,128]{3,2,1,0:T(8,128)(2,1)S(1)} %get-tuple-element.57.__1_.rest_1_), channel_id=1, source_target_pairs={{0,5},{1,4},{2,7},{3,6},{4,1},{5,0},{6,3},{7,2},{8,13},{9,12},{10,... | collective-permute-start | bytes 442376 | tf_op jit(solution)/shard_map/ppermute | solution.py:450
  20.7 1.6 %collective-permute-start.4 = (bf16[64,256]{1,0:T(8,128)(2,1)S(1)}, bf16[64,256]{1,0:T(8,128)(2,1)S(1)}, u32[]{:S(2)}, u32[]{:S(2)}) collective-permute-start(bf16[64,256]{1,0:T(8,128)(2,1)S(1)} %pass.4), channel_id=1, source_target_pairs={{0,1},{1,0},{2,3},{3,2},{4,5},{5,4},{6,7},{7,6},{8,9},{9,8},{10,11... | collective-permute-start | bytes 98312 | tf_op jit(solution)/shard_map/ppermute | solution.py:504
  22.4 1.4 %spatial_lower.1.lower_ref = bf16[8,8,16,256]{3,2,1,0:T(8,128)(2,1)S(1)} custom-call(bf16[18,10,16,256]{3,2,1,0:T(8,128)(2,1)S(1)} %get-tuple-element.58.acts_ref, bf16[9,256,256]{2,1,0:T(8,128)(2,1)S(1)} %bitcast.13, bf16[4,9,16,128]{3,2,1,0:T(8,128)(2,1)S(1)} %get-tuple-element.59.rest_0_.refs_0_, ...), custom_call_target="tpu_custom_call" | custom-call | flops 1073741824 | bytes 3178496 | tf_op jit(solution)/shard_map/spatial_lower/pallas_call | solution.py:426
  23.8 2.4 %forward.1 = (bf16[512,256]{1,0:T(8,128)(2,1)S(1)}, bf16[16,7,16,128]{3,2,1,0:T(8,128)(2,1)S(1)}, bf16[16,7,16,128]{3,2,1,0:T(8,128)(2,1)S(1)}) custom-call(s32[1]{0:T(128)S(6)} %copy.31.count_ref, bf16[16,8,16,256]{3,2,1,0:T(8,128)(2,1)S(1)} %get-tuple-element.44.xt_ref, bf16[8,8,16,256]{3,2,1,0:T(8,128)(2,1)S(1)} %get-tuple-element.56.rest_0_.upper_ref, ...), custom_call_target="tpu_custom_call" | custom-call | bytes 1024 | tf_op jit(solution)/shard_map/forward/pallas_call | solution.py:426
  26.1 0.3 collective-permute-done.4.__2_.top_ref.bot_ref
  26.5 1.0 %collective-permute-start.6 = (bf16[4,9,16,128]{3,2,1,0:T(8,128)(2,1)S(1)}, bf16[4,9,16,128]{3,2,1,0:T(8,128)(2,1)S(1)}, u32[]{:S(2)}, u32[]{:S(2)}) collective-permute-start(bf16[4,9,16,128]{3,2,1,0:T(8,128)(2,1)S(1)} %get-tuple-element.60.rest_2_), channel_id=1, source_target_pairs={{0,1},{1,0},{2,3},{3,2},{4,5},{5,4},{6,7},{7,6},{8,9},{9,8},{10,11... | collective-permute-start | bytes 442376 | tf_op jit(solution)/shard_map/ppermute | solution.py:450
  27.5 1.4 %collective-permute-start.7 = (bf16[4,9,16,128]{3,2,1,0:T(8,128)(2,1)S(1)}, bf16[4,9,16,128]{3,2,1,0:T(8,128)(2,1)S(1)}, u32[]{:S(2)}, u32[]{:S(2)}) collective-permute-start(bf16[4,9,16,128]{3,2,1,0:T(8,128)(2,1)S(1)} %get-tuple-element.61.rest_3_), channel_id=1, source_target_pairs={{0,4},{1,5},{2,6},{3,7},{4,0},{5,1},{6,2},{7,3},{8,12},{9,13},{10,... | collective-permute-start | bytes 442376 | tf_op jit(solution)/shard_map/ppermute | solution.py:450
  28.8 0.1 plane_send.3
  28.9 1.3 %collective-permute-start.9 = (bf16[4,7,16,128]{3,2,1,0:T(8,128)(2,1)S(1)}, bf16[4,7,16,128]{3,2,1,0:T(8,128)(2,1)S(1)}, u32[]{:S(2)}, u32[]{:S(2)}) collective-permute-start(bf16[4,7,16,128]{3,2,1,0:T(8,128)(2,1)S(1)} %get-tuple-element.67), channel_id=1, source_target_pairs={{0,5},{1,4},{2,7},{3,6},{4,1},{5,0},{6,3},{7,2},{8,13},{9,12},{10,... | collective-permute-start | bytes 344072 | tf_op jit(solution)/shard_map/ppermute | solution.py:450
  30.2 1.4 %collective-permute-start.10 = (bf16[4,7,16,128]{3,2,1,0:T(8,128)(2,1)S(1)}, bf16[4,7,16,128]{3,2,1,0:T(8,128)(2,1)S(1)}, u32[]{:S(2)}, u32[]{:S(2)}) collective-permute-start(bf16[4,7,16,128]{3,2,1,0:T(8,128)(2,1)S(1)} %get-tuple-element.68), channel_id=1, source_target_pairs={{0,1},{1,0},{2,3},{3,2},{4,5},{5,4},{6,7},{7,6},{8,9},{9,8},{10,11... | collective-permute-start | bytes 344072 | tf_op jit(solution)/shard_map/ppermute | solution.py:450
  31.6 0.9 %collective-permute-start.11 = (bf16[4,7,16,128]{3,2,1,0:T(8,128)(2,1)S(1)}, bf16[4,7,16,128]{3,2,1,0:T(8,128)(2,1)S(1)}, u32[]{:S(2)}, u32[]{:S(2)}) collective-permute-start(bf16[4,7,16,128]{3,2,1,0:T(8,128)(2,1)S(1)} %get-tuple-element.69), channel_id=1, source_target_pairs={{0,4},{1,5},{2,6},{3,7},{4,0},{5,1},{6,2},{7,3},{8,12},{9,13},{10,... | collective-permute-start | bytes 344072 | tf_op jit(solution)/shard_map/ppermute | solution.py:450
  32.5 0.2 collective-permute-done.6.refs_2_
  32.7 1.4 %collective-permute-done.7.refs_3_ = bf16[4,9,16,128]{3,2,1,0:T(8,128)(2,1)S(1)} collective-permute-done((bf16[4,9,16,128]{3,2,1,0:T(8,128)(2,1)S(1)}, bf16[4,9,16,128]{3,2,1,0:T(8,128)(2,1)S(1)}, u32[]{:S(2)}, u32[]{:S(2)}) %collective-permute-start.7) | collective-permute-done | bytes 147488 | tf_op jit(solution)/shard_map/ppermute | solution.py:450
  34.2 3.0 %collective-permute-done.9.refs_5_ = bf16[4,7,16,128]{3,2,1,0:T(8,128)(2,1)S(1)} collective-permute-done((bf16[4,7,16,128]{3,2,1,0:T(8,128)(2,1)S(1)}, bf16[4,7,16,128]{3,2,1,0:T(8,128)(2,1)S(1)}, u32[]{:S(2)}, u32[]{:S(2)}) %collective-permute-start.9) | collective-permute-done | bytes 114720 | tf_op jit(solution)/shard_map/ppermute | solution.py:450
  37.1 0.5 collective-permute-done.10.refs_6_
  37.6 0.7 collective-permute-done.11.refs_7_
  38.3 0.1 line_send.1
  38.4 3.0 %collective-permute-start.12 = (bf16[16,16,128]{2,1,0:T(8,128)(2,1)S(1)}, bf16[16,16,128]{2,1,0:T(8,128)(2,1)S(1)}, u32[]{:S(2)}, u32[]{:S(2)}) collective-permute-start(bf16[16,16,128]{2,1,0:T(8,128)(2,1)S(1)} %get-tuple-element.71), channel_id=1, source_target_pairs={{0,24},{1,25},{2,26},{3,27},{4,28},{5,29},{6,30},{7,31},{8,16},{9,... | collective-permute-start | bytes 196616 | tf_op jit(solution)/shard_map/ppermute | solution.py:450
  41.5 1.4 %collective-permute-start.14 = (bf16[16,16,128]{2,1,0:T(8,128)(2,1)S(1)}, bf16[16,16,128]{2,1,0:T(8,128)(2,1)S(1)}, u32[]{:S(2)}, u32[]{:S(2)}) collective-permute-start(bf16[16,16,128]{2,1,0:T(8,128)(2,1)S(1)} %get-tuple-element.73), channel_id=1, source_target_pairs={{0,8},{1,9},{2,10},{3,11},{4,12},{5,13},{6,14},{7,15},{8,0},{9,1},... | collective-permute-start | bytes 196616 | tf_op jit(solution)/shard_map/ppermute | solution.py:450
  42.9 2.2 %collective-permute-done.12.b_ref = bf16[16,16,128]{2,1,0:T(8,128)(2,1)S(1)} collective-permute-done((bf16[16,16,128]{2,1,0:T(8,128)(2,1)S(1)}, bf16[16,16,128]{2,1,0:T(8,128)(2,1)S(1)}, u32[]{:S(2)}, u32[]{:S(2)}) %collective-permute-start.12) | collective-permute-done | bytes 65568 | tf_op jit(solution)/shard_map/ppermute | solution.py:450
  45.1 2.1 %collective-permute-done.13.c_ref = bf16[16,16,128]{2,1,0:T(8,128)(2,1)S(1)} collective-permute-done((bf16[16,16,128]{2,1,0:T(8,128)(2,1)S(1)}, bf16[16,16,128]{2,1,0:T(8,128)(2,1)S(1)}, u32[]{:S(2)}, u32[]{:S(2)}) %collective-permute-start.13) | collective-permute-done | bytes 65568 | tf_op jit(solution)/shard_map/ppermute | solution.py:450
  47.3 0.5 collective-permute-start.17
  47.8 2.7 %collective-permute-start.16 = (bf16[16,16,128]{2,1,0:T(8,128)(2,1)S(1)}, bf16[16,16,128]{2,1,0:T(8,128)(2,1)S(1)}, u32[]{:S(2)}, u32[]{:S(2)}) collective-permute-start(bf16[16,16,128]{2,1,0:T(8,128)(2,1)S(1)} %line_sum.1.a_ref), channel_id=1, source_target_pairs={{0,16},{1,17},{2,18},{3,19},{4,20},{5,21},{6,22},{7,23},{8,24},{9,... | collective-permute-start | bytes 196616 | tf_op jit(solution)/shard_map/ppermute | solution.py:450
  50.5 1.3 %collective-permute-start.15 = (bf16[16,16,128]{2,1,0:T(8,128)(2,1)S(1)}, bf16[16,16,128]{2,1,0:T(8,128)(2,1)S(1)}, u32[]{:S(2)}, u32[]{:S(2)}) collective-permute-start(bf16[16,16,128]{2,1,0:T(8,128)(2,1)S(1)} %line_sum.1.a_ref), channel_id=1, source_target_pairs={{0,24},{1,25},{2,26},{3,27},{4,28},{5,29},{6,30},{7,31},{8,16},{9,... | collective-permute-start | bytes 196616 | tf_op jit(solution)/shard_map/ppermute | solution.py:450
  51.7 2.6 %collective-permute-done.16.c_ref = bf16[16,16,128]{2,1,0:T(8,128)(2,1)S(1)} collective-permute-done((bf16[16,16,128]{2,1,0:T(8,128)(2,1)S(1)}, bf16[16,16,128]{2,1,0:T(8,128)(2,1)S(1)}, u32[]{:S(2)}, u32[]{:S(2)}) %collective-permute-start.16) | collective-permute-done | bytes 65568 | tf_op jit(solution)/shard_map/ppermute | solution.py:450
  54.3 2.2 %collective-permute-done.15.b_ref = bf16[16,16,128]{2,1,0:T(8,128)(2,1)S(1)} collective-permute-done((bf16[16,16,128]{2,1,0:T(8,128)(2,1)S(1)}, bf16[16,16,128]{2,1,0:T(8,128)(2,1)S(1)}, u32[]{:S(2)}, u32[]{:S(2)}) %collective-permute-start.15) | collective-permute-done | bytes 65568 | tf_op jit(solution)/shard_map/ppermute | solution.py:450
  56.6 1.2 %collective-permute-start.20 = (bf16[4,16,16,128]{3,2,1,0:T(8,128)(2,1)S(1)}, bf16[4,16,16,128]{3,2,1,0:T(8,128)(2,1)S(1)}, u32[]{:S(2)}, u32[]{:S(2)}) collective-permute-start(bf16[4,16,16,128]{3,2,1,0:T(8,128)(2,1)S(1)} %line_gather.1.rest_0_.a_ref), channel_id=1, source_target_pairs={{0,4},{1,5},{2,6},{3,7},{4,0},{5,1},{6,2},{7,3},{8,12},{9,13},{10,... | collective-permute-start | bytes 786440 | tf_op jit(solution)/shard_map/ppermute | solution.py:450
  57.7 1.4 %collective-permute-start.19 = (bf16[4,16,16,128]{3,2,1,0:T(8,128)(2,1)S(1)}, bf16[4,16,16,128]{3,2,1,0:T(8,128)(2,1)S(1)}, u32[]{:S(2)}, u32[]{:S(2)}) collective-permute-start(bf16[4,16,16,128]{3,2,1,0:T(8,128)(2,1)S(1)} %line_gather.1.rest_0_.a_ref), channel_id=1, source_target_pairs={{0,1},{1,0},{2,3},{3,2},{4,5},{5,4},{6,7},{7,6},{8,9},{9,8},{10,11... | collective-permute-start | bytes 786440 | tf_op jit(solution)/shard_map/ppermute | solution.py:450
  59.1 1.0 %collective-permute-start.18 = (bf16[4,16,16,128]{3,2,1,0:T(8,128)(2,1)S(1)}, bf16[4,16,16,128]{3,2,1,0:T(8,128)(2,1)S(1)}, u32[]{:S(2)}, u32[]{:S(2)}) collective-permute-start(bf16[4,16,16,128]{3,2,1,0:T(8,128)(2,1)S(1)} %line_gather.1.rest_0_.a_ref), channel_id=1, source_target_pairs={{0,5},{1,4},{2,7},{3,6},{4,1},{5,0},{6,3},{7,2},{8,13},{9,12},{10,... | collective-permute-start | bytes 786440 | tf_op jit(solution)/shard_map/ppermute | solution.py:450
  60.1 7.4 %grad_x.1 = (bf16[16,128,256]{2,1,0:T(8,128)(2,1)}, bf16[16,8,4,256]{3,2,1,0:T(4,128)(2,1)}, f32[8,128]{1,0:T(8,128)S(1)}) custom-call(s32[1]{0:T(128)S(6)} %copy.31.count_ref, bf16[16,8,16,256]{3,2,1,0:T(8,128)(2,1)S(1)} %get-tuple-element.44.xt_ref, bf16[16,8,16,256]{3,2,1,0:T(8,128)(2,1)S(1)} %get-tuple-element.49.gy_ref, ...), custom_call_target="tpu_custom_call" | custom-call | flops 2684354560 | bytes 7147524 | tf_op jit(solution)/shard_map/grad_x/pallas_call | solution.py:426
  67.6 2.0 %collective-permute-done.19.c_ref = bf16[4,16,16,128]{3,2,1,0:T(8,128)(2,1)S(1)} collective-permute-done((bf16[4,16,16,128]{3,2,1,0:T(8,128)(2,1)S(1)}, bf16[4,16,16,128]{3,2,1,0:T(8,128)(2,1)S(1)}, u32[]{:S(2)}, u32[]{:S(2)}) %collective-permute-start.19) | collective-permute-done | bytes 262176 | tf_op jit(solution)/shard_map/ppermute | solution.py:450
  69.7 1.5 %finish.2 = (f32[9,256,256]{2,1,0:T(8,128)}, f32[3,256,256]{2,1,0:T(8,128)}, f32[4,256,256]{2,1,0:T(8,128)}) custom-call(bf16[16,16,16,128]{3,2,1,0:T(8,128)(2,1)S(1)} %plane_gather.1.half_ref), custom_call_target="tpu_custom_call" | custom-call | bytes 5242880 | tf_op jit(solution)/shard_map/finish/pallas_call | solution.py:426
  71.2 1.2 %collective-permute-done.21.half_ref = bf16[16,16,16,128]{3,2,1,0:T(8,128)(2,1)S(1)} collective-permute-done((bf16[16,16,16,128]{3,2,1,0:T(8,128)(2,1)S(1)}, bf16[16,16,16,128]{3,2,1,0:T(8,128)(2,1)S(1)}, u32[]{:S(2)}, u32[]{:S(2)}) %collective-permute-start.21) | collective-permute-done | bytes 1048608 | tf_op jit(solution)/shard_map/ppermute | solution.py:450
  72.4 1.5 %finish.3 = (f32[9,256,256]{2,1,0:T(8,128)}, f32[3,256,256]{2,1,0:T(8,128)}, f32[4,256,256]{2,1,0:T(8,128)}) custom-call(bf16[16,16,16,128]{3,2,1,0:T(8,128)(2,1)S(1)} %collective-permute-done.21.half_ref, f32[9,256,256]{2,1,0:T(8,128)} %get-tuple-element.77.rest_0_, ...), custom_call_target="tpu_custom_call", output_to_operand_aliasing={{0}: (1, {}), {1}: (2, {}), {2}: (3, {})} | custom-call | bytes 9437184 | tf_op jit(solution)/shard_map/finish/pallas_call | solution.py:426
  (26 shorter events, 0.3 us)
Async XLA Ops:
  1.3 1.2 %copy-start.3 = (bf16[16,16,8,256]{3,2,1,0:T(8,128)(2,1)S(1)}, bf16[16,16,8,256]{3,2,1,0:T(8,128)(2,1)}, u32[]{:S(2)}) copy-start(bf16[16,16,8,256]{3,2,1,0:T(8,128)(2,1)} %param.6) | copy-start | bytes 3145732
  2.5 4.5 %copy-start.2 = (bf16[16,8,4,256]{3,2,1,0:T(4,128)(2,1)S(1)}, bf16[16,8,4,256]{3,2,1,0:T(4,128)(2,1)}, u32[]{:S(2)}) copy-start(bf16[16,8,4,256]{3,2,1,0:T(4,128)(2,1)} %cot_ref.3) | copy-start | bytes 786436
  2.8 5.5 %copy-start = (bf16[2,2,256,256]{3,2,1,0:T(8,128)(2,1)S(1)}, bf16[2,2,256,256]{3,2,1,0:T(8,128)(2,1)}, u32[]{:S(2)}) copy-start(bf16[2,2,256,256]{3,2,1,0:T(8,128)(2,1)} %param.10) | copy-start | bytes 1572868
  2.8 5.5 %copy-start.1 = (bf16[3,256,256]{2,1,0:T(8,128)(2,1)S(1)}, bf16[3,256,256]{2,1,0:T(8,128)(2,1)}, u32[]{:S(2)}) copy-start(bf16[3,256,256]{2,1,0:T(8,128)(2,1)} %wt_ref.5) | copy-start | bytes 1179652
  2.8 5.5 %collective-permute-start = (bf16[128,256]{1,0:T(8,128)(2,1)S(1)}, bf16[128,256]{1,0:T(8,128)(2,1)S(1)}, u32[]{:S(2)}, u32[]{:S(2)}) collective-permute-start(bf16[128,256]{1,0:T(8,128)(2,1)S(1)} %edges.1._), channel_id=1, source_target_pairs={{0,1},{1,0},{2,3},{3,2},{4,5},{5,4},{6,7},{7,6},{8,9},{9,8},{10,11... | collective-permute-start | bytes 196616 | tf_op jit(solution)/shard_map/ppermute | solution.py:504
  7.0 3.1 %collective-permute-start.1 = (bf16[2,8,4,256]{3,2,1,0:T(4,128)(2,1)S(1)}, bf16[2,8,4,256]{3,2,1,0:T(4,128)(2,1)S(1)}, u32[]{:S(2)}, u32[]{:S(2)}) collective-permute-start(bf16[2,8,4,256]{3,2,1,0:T(4,128)(2,1)S(1)} %next.1.rest_3_), channel_id=1, source_target_pairs={{2,0},{4,2},{6,4},{8,6},{10,8},{12,10},{14,12},{16,14},{18,16},{20... | collective-permute-start | bytes 98312 | tf_op jit(solution)/shard_map/ppermute | solution.py:494
  8.5 8.1 %collective-permute-start.2 = (bf16[288,256]{1,0:T(8,128)(2,1)S(1)}, bf16[288,256]{1,0:T(8,128)(2,1)S(1)}, u32[]{:S(2)}, u32[]{:S(2)}) collective-permute-start(bf16[288,256]{1,0:T(8,128)(2,1)S(1)} %get-tuple-element.54), channel_id=1, source_target_pairs={{0,2},{2,4},{4,6},{6,8},{8,10},{10,12},{12,14},{14,16},{16,18},{18... | collective-permute-start | bytes 442376 | tf_op jit(solution)/shard_map/ppermute | solution.py:499
  10.1 6.6 %copy-start.4 = (bf16[3,3,256,256]{3,2,1,0:T(8,128)(2,1)S(1)}, bf16[3,3,256,256]{3,2,1,0:T(8,128)(2,1)}, u32[]{:S(2)}) copy-start(bf16[3,3,256,256]{3,2,1,0:T(8,128)(2,1)} %param.8) | copy-start | bytes 3538948
  16.6 2.0 %collective-permute-start.3 = (bf16[16,9,16,128]{3,2,1,0:T(8,128)(2,1)S(1)}, bf16[16,9,16,128]{3,2,1,0:T(8,128)(2,1)S(1)}, u32[]{:S(2)}, u32[]{:S(2)}) collective-permute-start(bf16[16,9,16,128]{3,2,1,0:T(8,128)(2,1)S(1)} %pass.3._), channel_id=1, source_target_pairs={{0,2},{1,3},{2,0},{3,1},{4,6},{5,7},{6,4},{7,5},{8,10},{9,11},{10,... | collective-permute-start | bytes 1769480 | tf_op jit(solution)/shard_map/ppermute | solution.py:450
  18.8 7.7 %collective-permute-start.5 = (bf16[4,9,16,128]{3,2,1,0:T(8,128)(2,1)S(1)}, bf16[4,9,16,128]{3,2,1,0:T(8,128)(2,1)S(1)}, u32[]{:S(2)}, u32[]{:S(2)}) collective-permute-start(bf16[4,9,16,128]{3,2,1,0:T(8,128)(2,1)S(1)} %get-tuple-element.57.__1_.rest_1_), channel_id=1, source_target_pairs={{0,5},{1,4},{2,7},{3,6},{4,1},{5,0},{6,3},{7,2},{8,13},{9,12},{10,... | collective-permute-start | bytes 442376 | tf_op jit(solution)/shard_map/ppermute | solution.py:450
  20.7 5.7 %collective-permute-start.4 = (bf16[64,256]{1,0:T(8,128)(2,1)S(1)}, bf16[64,256]{1,0:T(8,128)(2,1)S(1)}, u32[]{:S(2)}, u32[]{:S(2)}) collective-permute-start(bf16[64,256]{1,0:T(8,128)(2,1)S(1)} %pass.4), channel_id=1, source_target_pairs={{0,1},{1,0},{2,3},{3,2},{4,5},{5,4},{6,7},{7,6},{8,9},{9,8},{10,11... | collective-permute-start | bytes 98312 | tf_op jit(solution)/shard_map/ppermute | solution.py:504
  26.5 2.4 %collective-permute-start.8 = (bf16[16,7,16,128]{3,2,1,0:T(8,128)(2,1)S(1)}, bf16[16,7,16,128]{3,2,1,0:T(8,128)(2,1)S(1)}, u32[]{:S(2)}, u32[]{:S(2)}) collective-permute-start(bf16[16,7,16,128]{3,2,1,0:T(8,128)(2,1)S(1)} %pass.5), channel_id=1, source_target_pairs={{0,2},{1,3},{2,0},{3,1},{4,6},{5,7},{6,4},{7,5},{8,10},{9,11},{10,... | collective-permute-start | bytes 1376264 | tf_op jit(solution)/shard_map/ppermute | solution.py:450
  26.5 6.3 %collective-permute-start.6 = (bf16[4,9,16,128]{3,2,1,0:T(8,128)(2,1)S(1)}, bf16[4,9,16,128]{3,2,1,0:T(8,128)(2,1)S(1)}, u32[]{:S(2)}, u32[]{:S(2)}) collective-permute-start(bf16[4,9,16,128]{3,2,1,0:T(8,128)(2,1)S(1)} %get-tuple-element.60.rest_2_), channel_id=1, source_target_pairs={{0,1},{1,0},{2,3},{3,2},{4,5},{5,4},{6,7},{7,6},{8,9},{9,8},{10,11... | collective-permute-start | bytes 442376 | tf_op jit(solution)/shard_map/ppermute | solution.py:450
  27.5 6.7 %collective-permute-start.7 = (bf16[4,9,16,128]{3,2,1,0:T(8,128)(2,1)S(1)}, bf16[4,9,16,128]{3,2,1,0:T(8,128)(2,1)S(1)}, u32[]{:S(2)}, u32[]{:S(2)}) collective-permute-start(bf16[4,9,16,128]{3,2,1,0:T(8,128)(2,1)S(1)} %get-tuple-element.61.rest_3_), channel_id=1, source_target_pairs={{0,4},{1,5},{2,6},{3,7},{4,0},{5,1},{6,2},{7,3},{8,12},{9,13},{10,... | collective-permute-start | bytes 442376 | tf_op jit(solution)/shard_map/ppermute | solution.py:450
  28.9 8.2 %collective-permute-start.9 = (bf16[4,7,16,128]{3,2,1,0:T(8,128)(2,1)S(1)}, bf16[4,7,16,128]{3,2,1,0:T(8,128)(2,1)S(1)}, u32[]{:S(2)}, u32[]{:S(2)}) collective-permute-start(bf16[4,7,16,128]{3,2,1,0:T(8,128)(2,1)S(1)} %get-tuple-element.67), channel_id=1, source_target_pairs={{0,5},{1,4},{2,7},{3,6},{4,1},{5,0},{6,3},{7,2},{8,13},{9,12},{10,... | collective-permute-start | bytes 344072 | tf_op jit(solution)/shard_map/ppermute | solution.py:450
  30.2 7.4 %collective-permute-start.10 = (bf16[4,7,16,128]{3,2,1,0:T(8,128)(2,1)S(1)}, bf16[4,7,16,128]{3,2,1,0:T(8,128)(2,1)S(1)}, u32[]{:S(2)}, u32[]{:S(2)}) collective-permute-start(bf16[4,7,16,128]{3,2,1,0:T(8,128)(2,1)S(1)} %get-tuple-element.68), channel_id=1, source_target_pairs={{0,1},{1,0},{2,3},{3,2},{4,5},{5,4},{6,7},{7,6},{8,9},{9,8},{10,11... | collective-permute-start | bytes 344072 | tf_op jit(solution)/shard_map/ppermute | solution.py:450
  31.6 6.7 %collective-permute-start.11 = (bf16[4,7,16,128]{3,2,1,0:T(8,128)(2,1)S(1)}, bf16[4,7,16,128]{3,2,1,0:T(8,128)(2,1)S(1)}, u32[]{:S(2)}, u32[]{:S(2)}) collective-permute-start(bf16[4,7,16,128]{3,2,1,0:T(8,128)(2,1)S(1)} %get-tuple-element.69), channel_id=1, source_target_pairs={{0,4},{1,5},{2,6},{3,7},{4,0},{5,1},{6,2},{7,3},{8,12},{9,13},{10,... | collective-permute-start | bytes 344072 | tf_op jit(solution)/shard_map/ppermute | solution.py:450
  38.4 6.6 %collective-permute-start.12 = (bf16[16,16,128]{2,1,0:T(8,128)(2,1)S(1)}, bf16[16,16,128]{2,1,0:T(8,128)(2,1)S(1)}, u32[]{:S(2)}, u32[]{:S(2)}) collective-permute-start(bf16[16,16,128]{2,1,0:T(8,128)(2,1)S(1)} %get-tuple-element.71), channel_id=1, source_target_pairs={{0,24},{1,25},{2,26},{3,27},{4,28},{5,29},{6,30},{7,31},{8,16},{9,... | collective-permute-start | bytes 196616 | tf_op jit(solution)/shard_map/ppermute | solution.py:450
  41.5 5.8 %collective-permute-start.13 = (bf16[16,16,128]{2,1,0:T(8,128)(2,1)S(1)}, bf16[16,16,128]{2,1,0:T(8,128)(2,1)S(1)}, u32[]{:S(2)}, u32[]{:S(2)}) collective-permute-start(bf16[16,16,128]{2,1,0:T(8,128)(2,1)S(1)} %get-tuple-element.72), channel_id=1, source_target_pairs={{0,16},{1,17},{2,18},{3,19},{4,20},{5,21},{6,22},{7,23},{8,24},{9,... | collective-permute-start | bytes 196616 | tf_op jit(solution)/shard_map/ppermute | solution.py:450
  41.5 5.8 %collective-permute-start.14 = (bf16[16,16,128]{2,1,0:T(8,128)(2,1)S(1)}, bf16[16,16,128]{2,1,0:T(8,128)(2,1)S(1)}, u32[]{:S(2)}, u32[]{:S(2)}) collective-permute-start(bf16[16,16,128]{2,1,0:T(8,128)(2,1)S(1)} %get-tuple-element.73), channel_id=1, source_target_pairs={{0,8},{1,9},{2,10},{3,11},{4,12},{5,13},{6,14},{7,15},{8,0},{9,1},... | collective-permute-start | bytes 196616 | tf_op jit(solution)/shard_map/ppermute | solution.py:450
  47.3 4.5 %collective-permute-start.17 = (bf16[16,16,128]{2,1,0:T(8,128)(2,1)S(1)}, bf16[16,16,128]{2,1,0:T(8,128)(2,1)S(1)}, u32[]{:S(2)}, u32[]{:S(2)}) collective-permute-start(bf16[16,16,128]{2,1,0:T(8,128)(2,1)S(1)} %line_sum.1.a_ref), channel_id=1, source_target_pairs={{0,8},{1,9},{2,10},{3,11},{4,12},{5,13},{6,14},{7,15},{8,0},{9,1},... | collective-permute-start | bytes 196616 | tf_op jit(solution)/shard_map/ppermute | solution.py:450
  47.8 6.6 %collective-permute-start.16 = (bf16[16,16,128]{2,1,0:T(8,128)(2,1)S(1)}, bf16[16,16,128]{2,1,0:T(8,128)(2,1)S(1)}, u32[]{:S(2)}, u32[]{:S(2)}) collective-permute-start(bf16[16,16,128]{2,1,0:T(8,128)(2,1)S(1)} %line_sum.1.a_ref), channel_id=1, source_target_pairs={{0,16},{1,17},{2,18},{3,19},{4,20},{5,21},{6,22},{7,23},{8,24},{9,... | collective-permute-start | bytes 196616 | tf_op jit(solution)/shard_map/ppermute | solution.py:450
  50.5 6.1 %collective-permute-start.15 = (bf16[16,16,128]{2,1,0:T(8,128)(2,1)S(1)}, bf16[16,16,128]{2,1,0:T(8,128)(2,1)S(1)}, u32[]{:S(2)}, u32[]{:S(2)}) collective-permute-start(bf16[16,16,128]{2,1,0:T(8,128)(2,1)S(1)} %line_sum.1.a_ref), channel_id=1, source_target_pairs={{0,24},{1,25},{2,26},{3,27},{4,28},{5,29},{6,30},{7,31},{8,16},{9,... | collective-permute-start | bytes 196616 | tf_op jit(solution)/shard_map/ppermute | solution.py:450
  56.6 11.0 %collective-permute-start.20 = (bf16[4,16,16,128]{3,2,1,0:T(8,128)(2,1)S(1)}, bf16[4,16,16,128]{3,2,1,0:T(8,128)(2,1)S(1)}, u32[]{:S(2)}, u32[]{:S(2)}) collective-permute-start(bf16[4,16,16,128]{3,2,1,0:T(8,128)(2,1)S(1)} %line_gather.1.rest_0_.a_ref), channel_id=1, source_target_pairs={{0,4},{1,5},{2,6},{3,7},{4,0},{5,1},{6,2},{7,3},{8,12},{9,13},{10,... | collective-permute-start | bytes 786440 | tf_op jit(solution)/shard_map/ppermute | solution.py:450
  57.7 11.8 %collective-permute-start.19 = (bf16[4,16,16,128]{3,2,1,0:T(8,128)(2,1)S(1)}, bf16[4,16,16,128]{3,2,1,0:T(8,128)(2,1)S(1)}, u32[]{:S(2)}, u32[]{:S(2)}) collective-permute-start(bf16[4,16,16,128]{3,2,1,0:T(8,128)(2,1)S(1)} %line_gather.1.rest_0_.a_ref), channel_id=1, source_target_pairs={{0,1},{1,0},{2,3},{3,2},{4,5},{5,4},{6,7},{7,6},{8,9},{9,8},{10,11... | collective-permute-start | bytes 786440 | tf_op jit(solution)/shard_map/ppermute | solution.py:450
  59.1 10.4 %collective-permute-start.18 = (bf16[4,16,16,128]{3,2,1,0:T(8,128)(2,1)S(1)}, bf16[4,16,16,128]{3,2,1,0:T(8,128)(2,1)S(1)}, u32[]{:S(2)}, u32[]{:S(2)}) collective-permute-start(bf16[4,16,16,128]{3,2,1,0:T(8,128)(2,1)S(1)} %line_gather.1.rest_0_.a_ref), channel_id=1, source_target_pairs={{0,5},{1,4},{2,7},{3,6},{4,1},{5,0},{6,3},{7,2},{8,13},{9,12},{10,... | collective-permute-start | bytes 786440 | tf_op jit(solution)/shard_map/ppermute | solution.py:450
  69.6 2.7 %collective-permute-start.21 = (bf16[16,16,16,128]{3,2,1,0:T(8,128)(2,1)S(1)}, bf16[16,16,16,128]{3,2,1,0:T(8,128)(2,1)S(1)}, u32[]{:S(2)}, u32[]{:S(2)}) collective-permute-start(bf16[16,16,16,128]{3,2,1,0:T(8,128)(2,1)S(1)} %plane_gather.1.half_ref), channel_id=1, source_target_pairs={{0,2},{1,3},{2,0},{3,1},{4,6},{5,7},{6,4},{7,5},{8,10},{9,11},{10,... | collective-permute-start | bytes 3145736 | tf_op jit(solution)/shard_map/ppermute | solution.py:450

commit v25 on v22

--- a/solution.py
+++ b/solution.py
@@ -65,10 +65,10 @@
 
 def grad_of_temporal(gy, wt_ref, count):
     n = gy.shape[0]
-    flat = gy.reshape(n * SLOTS, CH)
-    total = mm_nt(flat, wt_ref[2]).reshape(n, SLOTS, CH)
+    terms = mm_nt(gy.reshape(n * SLOTS, CH), wt_ref[...].reshape(3 * CH, CH))
+    total = terms[:, 2 * CH :].reshape(n, SLOTS, CH)
     for k in (1, 0):
-        term = mm_nt(flat, wt_ref[k]).reshape(n, SLOTS, CH)
+        term = terms[:, k * CH : k * CH + CH].reshape(n, SLOTS, CH)
         total = total + pltpu.roll(term, SLOTS - (2 - k), 1)
     return jnp.where(slot_mask(total.shape, count), total, 0.0).astype(BF)
 
@@ -228,14 +228,14 @@
         edge_refs[1][...] = first
 
     def grads_of(q, _):
-        g = gy_ref[pl.ds(8 * q, 8)].reshape(8 * cols, SLOTS, CH)
+        g = gy_ref[pl.ds(4 * q, 4)].reshape(4 * cols, SLOTS, CH)
         s = grad_of_temporal(g, wt_ref, count)
-        gs_ref[pl.ds(8 * q, 8), 1 : cols + 1] = s.reshape(8, cols, SLOTS, CH)
+        gs_ref[pl.ds(4 * q, 4), 1 : cols + 1] = s.reshape(4, cols, SLOTS, CH)
         g = jnp.where(slot_mask(g.shape, count), g.astype(F32), 0.0)
-        gy_ref[pl.ds(8 * q, 8)] = g.astype(BF).reshape(8, cols, SLOTS, CH)
+        gy_ref[pl.ds(4 * q, 4)] = g.astype(BF).reshape(4, cols, SLOTS, CH)
         return 0
 
-    lax.fori_loop(0, rows // 8, grads_of, 0, unroll=True)
+    lax.fori_loop(0, rows // 4, grads_of, 0, unroll=True)
 
     wide = rows * cols * SLOTS
     for j in range(3):

time: 73.8 us -> 73 us (0.989)
  waiting for transfers between devices: 20.1 us -> 22.3 us
  starting transfers between devices: 28.1 us -> 26 us
    ppermute x18, starting transfers between devices: 21 us -> 19.4 us  [swap(): return lax.ppermute(value, AXES, [(d, d ^ flip) for d in range(tm * grp)])]
    ppermute x18, waiting for transfers between devices: 17.8 us -> 19.3 us  [swap(): return lax.ppermute(value, AXES, [(d, d ^ flip) for d in range(tm * grp)])]
  transfers between devices with their start and end apart: 22 -> 22, of which waited for: 13 -> 15; matrix products, arithmetic and copies ran while one was open for 0% -> 0% of each run, Pallas kernels for 28% -> 27%
where the time goes in v25:
time: 73 us; the launch traced here: 72.9 us
  starting transfers between devices  26 us (36%)
  waiting for transfers between devices  22.3 us (31%)
  Pallas kernels  21.9 us (30%)
  between operations  1.48 us (2%)
  local copies, waits for them, and re-layouts  1.24 us (2%)
    pallas_call x19, Pallas kernels, call(): pl.pallas_call(kernel, out_shape=shapes, in_specs=[s for s, _ in ins], ou...  21.9 us
    ppermute x18, starting transfers between devices, swap(): return lax.ppermute(value, AXES, [(d, d ^ flip) for d in range(tm * grp)])  19.4 us
    ppermute x18, waiting for transfers between devices, swap(): return lax.ppermute(value, AXES, [(d, d ^ flip) for d in range(tm * grp)])  19.3 us
    ppermute x2, starting transfers between devices, from_bands(): got = lax.ppermute(parts[0], 'grp', [(0, 1), (1, 0)])  4.17 us
    ppermute x1, waiting for transfers between devices, around(): lax.ppermute(value, axis, [(i, (i + by) % count) for i in range(count)])  2.52 us
  transfers between devices with their start and end apart: 22, of which 15 were waited for; matrix products, arithmetic and copies ran while one was open for 0% of the time, Pallas kernels for 27%

profile of v25, /device:TPU:0, one launch (start us, length us, event | category | flops | bytes accessed | tf_op | source)
XLA Modules:
  0.0 72.9 jit_solution(17939198432472709071)
XLA Ops:
  1.3 1.2 %copy-done.3 = bf16[16,16,8,256]{3,2,1,0:T(8,128)(2,1)S(1)} copy-done((bf16[16,16,8,256]{3,2,1,0:T(8,128)(2,1)S(1)}, bf16[16,16,8,256]{3,2,1,0:T(8,128)(2,1)}, u32[]{:S(2)}) %copy-start.3) | copy-done | bytes 1048600
  2.5 0.3 edges.1._
  2.8 3.0 %collective-permute-start = (bf16[128,256]{1,0:T(8,128)(2,1)S(1)}, bf16[128,256]{1,0:T(8,128)(2,1)S(1)}, u32[]{:S(2)}, u32[]{:S(2)}) collective-permute-start(bf16[128,256]{1,0:T(8,128)(2,1)S(1)} %edges.1._), channel_id=1, source_target_pairs={{0,1},{1,0},{2,3},{3,2},{4,5},{5,4},{6,7},{7,6},{8,9},{9,8},{10,11... | collective-permute-start | bytes 196616 | tf_op jit(solution)/shard_map/ppermute | solution.py:504
  5.9 1.1 %acts.1 = (bf16[16,8,16,256]{3,2,1,0:T(8,128)(2,1)S(1)}, bf16[18,10,16,256]{3,2,1,0:T(8,128)(2,1)S(1)}, bf16[768,2560]{1,0:T(8,128)(2,1)S(1)}, bf16[288,256]{1,0:T(8,128)(2,1)S(1)}) custom-call(s32[1]{0:T(128)S(6)} %copy.29.count_ref, bf16[16,128,256]{2,1,0:T(8,128)(2,1)S(1)} %bitcast.11, bf16[128,256]{1,0:T(8,128)(2,1)S(1)} %edges.1._), custom_call_target="tpu_custom_call" | custom-call | flops 536870912 | bytes 7651332 | tf_op jit(solution)/shard_map/acts/pallas_call | solution.py:426
  7.0 1.3 %collective-permute-start.1 = (bf16[2,8,4,256]{3,2,1,0:T(4,128)(2,1)S(1)}, bf16[2,8,4,256]{3,2,1,0:T(4,128)(2,1)S(1)}, u32[]{:S(2)}, u32[]{:S(2)}) collective-permute-start(bf16[2,8,4,256]{3,2,1,0:T(4,128)(2,1)S(1)} %next.1.rest_3_), channel_id=1, source_target_pairs={{2,0},{4,2},{6,4},{8,6},{10,8},{12,10},{14,12},{16,14},{18,16},{20... | collective-permute-start | bytes 98312 | tf_op jit(solution)/shard_map/ppermute | solution.py:494
  8.4 0.2 halo.1
  8.5 1.1 %collective-permute-start.3 = (bf16[288,256]{1,0:T(8,128)(2,1)S(1)}, bf16[288,256]{1,0:T(8,128)(2,1)S(1)}, u32[]{:S(2)}, u32[]{:S(2)}) collective-permute-start(bf16[288,256]{1,0:T(8,128)(2,1)S(1)} %get-tuple-element.53), channel_id=1, source_target_pairs={{0,2},{2,4},{4,6},{6,8},{8,10},{10,12},{12,14},{14,16},{16,18},{18... | collective-permute-start | bytes 442376 | tf_op jit(solution)/shard_map/ppermute | solution.py:499
  9.7 0.5 collective-permute-done.1.nxt_ref
  10.1 3.9 %grad_spatial.1 = (bf16[8,4,16,256]{3,2,1,0:T(8,128)(2,1)S(1)}, bf16[16,8,16,256]{3,2,1,0:T(8,128)(2,1)S(1)}, bf16[16,10,16,256]{3,2,1,0:T(8,128)(2,1)S(1)}, bf1...) custom-call(s32[1]{0:T(128)S(6)} %copy.29.count_ref, ...), custom_call_target="tpu_custom_call" | custom-call | flops 3758096384 | bytes 8978436 | tf_op jit(solution)/shard_map/grad_spatial/pallas_call | solution.py:426
  14.1 2.5 %collective-permute-done.3.__1_.prev_ref = bf16[288,256]{1,0:T(8,128)(2,1)S(1)} collective-permute-done((bf16[288,256]{1,0:T(8,128)(2,1)S(1)}, bf16[288,256]{1,0:T(8,128)(2,1)S(1)}, u32[]{:S(2)}, u32[]{:S(2)}) %collective-permute-start.3) | collective-permute-done | bytes 147488 | tf_op jit(solution)/shard_map/ppermute | solution.py:499
  16.6 1.7 %spatial_upper.1 = (bf16[18,10,16,256]{3,2,1,0:T(8,128)(2,1)S(1)}, bf16[8,8,16,256]{3,2,1,0:T(8,128)(2,1)S(1)}) custom-call(bf16[18,10,16,256]{3,2,1,0:T(8,128)(2,1)S(1)} %get-tuple-element.52.acts_in, bf16[288,256]{1,0:T(8,128)(2,1)S(1)} %collective-permute-done.3.__1_.prev_ref, bf16[9,256,256]{2,1,0:T(8,128)(2,1)S(1)} %bitcast.12, ...), custom_call_target="tpu_custom_call", output_to_operand_aliasing={{0}: (0, {})} | custom-call | flops 1342177280 | bytes 4800512 | tf_op jit(solution)/shard_map/spatial_upper/pallas_call | solution.py:426
  18.4 0.3 collective-permute-done.4.got_ref
  18.6 0.1 plane_send.2
  18.8 1.4 %collective-permute-start.5 = (bf16[4,9,16,128]{3,2,1,0:T(8,128)(2,1)S(1)}, bf16[4,9,16,128]{3,2,1,0:T(8,128)(2,1)S(1)}, u32[]{:S(2)}, u32[]{:S(2)}) collective-permute-start(bf16[4,9,16,128]{3,2,1,0:T(8,128)(2,1)S(1)} %get-tuple-element.59.rest_1_), channel_id=1, source_target_pairs={{0,5},{1,4},{2,7},{3,6},{4,1},{5,0},{6,3},{7,2},{8,13},{9,12},{10,... | collective-permute-start | bytes 442376 | tf_op jit(solution)/shard_map/ppermute | solution.py:450
  20.2 1.4 %spatial_lower.1.lower_ref = bf16[8,8,16,256]{3,2,1,0:T(8,128)(2,1)S(1)} custom-call(bf16[18,10,16,256]{3,2,1,0:T(8,128)(2,1)S(1)} %get-tuple-element.56.acts_ref, bf16[9,256,256]{2,1,0:T(8,128)(2,1)S(1)} %bitcast.13, bf16[4,9,16,128]{3,2,1,0:T(8,128)(2,1)S(1)} %get-tuple-element.58.rest_0_.refs_0_, bf16[4,9,16,128]{3,2,1,0:T(8,128)(2,1)S(1)} %get-tuple-element.59.rest_1_, ...), custom_call_target="tpu_custom_call" | custom-call | flops 1073741824 | bytes 3178496 | tf_op jit(solution)/shard_map/spatial_lower/pallas_call | solution.py:426
  21.5 2.4 %forward.1 = (bf16[512,256]{1,0:T(8,128)(2,1)S(1)}, bf16[16,7,16,128]{3,2,1,0:T(8,128)(2,1)S(1)}, bf16[16,7,16,128]{3,2,1,0:T(8,128)(2,1)S(1)}) custom-call(s32[1]{0:T(128)S(6)} %copy.29.count_ref, bf16[16,8,16,256]{3,2,1,0:T(8,128)(2,1)S(1)} %get-tuple-element.44.xt_ref, bf16[8,8,16,256]{3,2,1,0:T(8,128)(2,1)S(1)} %get-tuple-element.55.rest_0_.upper_ref, ...), custom_call_target="tpu_custom_call" | custom-call | bytes 1024 | tf_op jit(solution)/shard_map/forward/pallas_call | solution.py:426
  23.9 1.8 %collective-permute-done.5.__1_.refs_1_ = bf16[4,9,16,128]{3,2,1,0:T(8,128)(2,1)S(1)} collective-permute-done((bf16[4,9,16,128]{3,2,1,0:T(8,128)(2,1)S(1)}, bf16[4,9,16,128]{3,2,1,0:T(8,128)(2,1)S(1)}, u32[]{:S(2)}, u32[]{:S(2)}) %collective-permute-start.5) | collective-permute-done | bytes 147488 | tf_op jit(solution)/shard_map/ppermute | solution.py:450
  25.7 0.9 %collective-permute-start.6 = (bf16[4,9,16,128]{3,2,1,0:T(8,128)(2,1)S(1)}, bf16[4,9,16,128]{3,2,1,0:T(8,128)(2,1)S(1)}, u32[]{:S(2)}, u32[]{:S(2)}) collective-permute-start(bf16[4,9,16,128]{3,2,1,0:T(8,128)(2,1)S(1)} %get-tuple-element.60.rest_2_), channel_id=1, source_target_pairs={{0,1},{1,0},{2,3},{3,2},{4,5},{5,4},{6,7},{7,6},{8,9},{9,8},{10,11... | collective-permute-start | bytes 442376 | tf_op jit(solution)/shard_map/ppermute | solution.py:450
  26.7 0.9 %collective-permute-start.7 = (bf16[4,9,16,128]{3,2,1,0:T(8,128)(2,1)S(1)}, bf16[4,9,16,128]{3,2,1,0:T(8,128)(2,1)S(1)}, u32[]{:S(2)}, u32[]{:S(2)}) collective-permute-start(bf16[4,9,16,128]{3,2,1,0:T(8,128)(2,1)S(1)} %get-tuple-element.61.rest_3_), channel_id=1, source_target_pairs={{0,4},{1,5},{2,6},{3,7},{4,0},{5,1},{6,2},{7,3},{8,12},{9,13},{10,... | collective-permute-start | bytes 442376 | tf_op jit(solution)/shard_map/ppermute | solution.py:450
  27.6 0.1 plane_send.3
  27.7 1.7 %collective-permute-start.9 = (bf16[4,7,16,128]{3,2,1,0:T(8,128)(2,1)S(1)}, bf16[4,7,16,128]{3,2,1,0:T(8,128)(2,1)S(1)}, u32[]{:S(2)}, u32[]{:S(2)}) collective-permute-start(bf16[4,7,16,128]{3,2,1,0:T(8,128)(2,1)S(1)} %get-tuple-element.67), channel_id=1, source_target_pairs={{0,5},{1,4},{2,7},{3,6},{4,1},{5,0},{6,3},{7,2},{8,13},{9,12},{10,... | collective-permute-start | bytes 344072 | tf_op jit(solution)/shard_map/ppermute | solution.py:450
  29.4 1.3 %collective-permute-start.10 = (bf16[4,7,16,128]{3,2,1,0:T(8,128)(2,1)S(1)}, bf16[4,7,16,128]{3,2,1,0:T(8,128)(2,1)S(1)}, u32[]{:S(2)}, u32[]{:S(2)}) collective-permute-start(bf16[4,7,16,128]{3,2,1,0:T(8,128)(2,1)S(1)} %get-tuple-element.68), channel_id=1, source_target_pairs={{0,1},{1,0},{2,3},{3,2},{4,5},{5,4},{6,7},{7,6},{8,9},{9,8},{10,11... | collective-permute-start | bytes 344072 | tf_op jit(solution)/shard_map/ppermute | solution.py:450
  30.7 0.6 collective-permute-start.11
  31.3 1.0 %collective-permute-done.6.refs_2_ = bf16[4,9,16,128]{3,2,1,0:T(8,128)(2,1)S(1)} collective-permute-done((bf16[4,9,16,128]{3,2,1,0:T(8,128)(2,1)S(1)}, bf16[4,9,16,128]{3,2,1,0:T(8,128)(2,1)S(1)}, u32[]{:S(2)}, u32[]{:S(2)}) %collective-permute-start.6) | collective-permute-done | bytes 147488 | tf_op jit(solution)/shard_map/ppermute | solution.py:450
  32.3 1.1 %collective-permute-done.7.refs_3_ = bf16[4,9,16,128]{3,2,1,0:T(8,128)(2,1)S(1)} collective-permute-done((bf16[4,9,16,128]{3,2,1,0:T(8,128)(2,1)S(1)}, bf16[4,9,16,128]{3,2,1,0:T(8,128)(2,1)S(1)}, u32[]{:S(2)}, u32[]{:S(2)}) %collective-permute-start.7) | collective-permute-done | bytes 147488 | tf_op jit(solution)/shard_map/ppermute | solution.py:450
  33.4 3.0 %collective-permute-done.9.refs_5_ = bf16[4,7,16,128]{3,2,1,0:T(8,128)(2,1)S(1)} collective-permute-done((bf16[4,7,16,128]{3,2,1,0:T(8,128)(2,1)S(1)}, bf16[4,7,16,128]{3,2,1,0:T(8,128)(2,1)S(1)}, u32[]{:S(2)}, u32[]{:S(2)}) %collective-permute-start.9) | collective-permute-done | bytes 114720 | tf_op jit(solution)/shard_map/ppermute | solution.py:450
  36.4 0.5 collective-permute-done.10.refs_6_
  36.9 0.7 collective-permute-done.11.refs_7_
  37.6 0.1 line_send.1
  37.8 2.5 %collective-permute-start.12 = (bf16[16,16,128]{2,1,0:T(8,128)(2,1)S(1)}, bf16[16,16,128]{2,1,0:T(8,128)(2,1)S(1)}, u32[]{:S(2)}, u32[]{:S(2)}) collective-permute-start(bf16[16,16,128]{2,1,0:T(8,128)(2,1)S(1)} %get-tuple-element.71), channel_id=1, source_target_pairs={{0,24},{1,25},{2,26},{3,27},{4,28},{5,29},{6,30},{7,31},{8,16},{9,... | collective-permute-start | bytes 196616 | tf_op jit(solution)/shard_map/ppermute | solution.py:450
  40.3 1.9 %collective-permute-start.14 = (bf16[16,16,128]{2,1,0:T(8,128)(2,1)S(1)}, bf16[16,16,128]{2,1,0:T(8,128)(2,1)S(1)}, u32[]{:S(2)}, u32[]{:S(2)}) collective-permute-start(bf16[16,16,128]{2,1,0:T(8,128)(2,1)S(1)} %get-tuple-element.73), channel_id=1, source_target_pairs={{0,8},{1,9},{2,10},{3,11},{4,12},{5,13},{6,14},{7,15},{8,0},{9,1},... | collective-permute-start | bytes 196616 | tf_op jit(solution)/shard_map/ppermute | solution.py:450
  42.2 1.8 %collective-permute-done.12.b_ref = bf16[16,16,128]{2,1,0:T(8,128)(2,1)S(1)} collective-permute-done((bf16[16,16,128]{2,1,0:T(8,128)(2,1)S(1)}, bf16[16,16,128]{2,1,0:T(8,128)(2,1)S(1)}, u32[]{:S(2)}, u32[]{:S(2)}) %collective-permute-start.12) | collective-permute-done | bytes 65568 | tf_op jit(solution)/shard_map/ppermute | solution.py:450
  44.0 2.6 %collective-permute-done.13.c_ref = bf16[16,16,128]{2,1,0:T(8,128)(2,1)S(1)} collective-permute-done((bf16[16,16,128]{2,1,0:T(8,128)(2,1)S(1)}, bf16[16,16,128]{2,1,0:T(8,128)(2,1)S(1)}, u32[]{:S(2)}, u32[]{:S(2)}) %collective-permute-start.13) | collective-permute-done | bytes 65568 | tf_op jit(solution)/shard_map/ppermute | solution.py:450
  46.6 0.1 collective-permute-start.17
  46.7 3.0 %collective-permute-start.16 = (bf16[16,16,128]{2,1,0:T(8,128)(2,1)S(1)}, bf16[16,16,128]{2,1,0:T(8,128)(2,1)S(1)}, u32[]{:S(2)}, u32[]{:S(2)}) collective-permute-start(bf16[16,16,128]{2,1,0:T(8,128)(2,1)S(1)} %line_sum.1.a_ref), channel_id=1, source_target_pairs={{0,16},{1,17},{2,18},{3,19},{4,20},{5,21},{6,22},{7,23},{8,24},{9,... | collective-permute-start | bytes 196616 | tf_op jit(solution)/shard_map/ppermute | solution.py:450
  49.7 1.4 %collective-permute-start.15 = (bf16[16,16,128]{2,1,0:T(8,128)(2,1)S(1)}, bf16[16,16,128]{2,1,0:T(8,128)(2,1)S(1)}, u32[]{:S(2)}, u32[]{:S(2)}) collective-permute-start(bf16[16,16,128]{2,1,0:T(8,128)(2,1)S(1)} %line_sum.1.a_ref), channel_id=1, source_target_pairs={{0,24},{1,25},{2,26},{3,27},{4,28},{5,29},{6,30},{7,31},{8,16},{9,... | collective-permute-start | bytes 196616 | tf_op jit(solution)/shard_map/ppermute | solution.py:450
  51.1 1.1 %collective-permute-start.2 = (bf16[64,256]{1,0:T(8,128)(2,1)S(1)}, bf16[64,256]{1,0:T(8,128)(2,1)S(1)}, u32[]{:S(2)}, u32[]{:S(2)}) collective-permute-start(bf16[64,256]{1,0:T(8,128)(2,1)S(1)} %get-tuple-element.51), channel_id=1, source_target_pairs={{0,1},{1,0},{2,3},{3,2},{4,5},{5,4},{6,7},{7,6},{8,9},{9,8},{10,11... | collective-permute-start | bytes 98312 | tf_op jit(solution)/shard_map/ppermute | solution.py:504
  52.2 1.9 %collective-permute-done.16.c_ref = bf16[16,16,128]{2,1,0:T(8,128)(2,1)S(1)} collective-permute-done((bf16[16,16,128]{2,1,0:T(8,128)(2,1)S(1)}, bf16[16,16,128]{2,1,0:T(8,128)(2,1)S(1)}, u32[]{:S(2)}, u32[]{:S(2)}) %collective-permute-start.16) | collective-permute-done | bytes 65568 | tf_op jit(solution)/shard_map/ppermute | solution.py:450
  54.1 1.6 %collective-permute-done.15.b_ref = bf16[16,16,128]{2,1,0:T(8,128)(2,1)S(1)} collective-permute-done((bf16[16,16,128]{2,1,0:T(8,128)(2,1)S(1)}, bf16[16,16,128]{2,1,0:T(8,128)(2,1)S(1)}, u32[]{:S(2)}, u32[]{:S(2)}) %collective-permute-start.15) | collective-permute-done | bytes 65568 | tf_op jit(solution)/shard_map/ppermute | solution.py:450
  55.8 1.0 %collective-permute-start.20 = (bf16[4,16,16,128]{3,2,1,0:T(8,128)(2,1)S(1)}, bf16[4,16,16,128]{3,2,1,0:T(8,128)(2,1)S(1)}, u32[]{:S(2)}, u32[]{:S(2)}) collective-permute-start(bf16[4,16,16,128]{3,2,1,0:T(8,128)(2,1)S(1)} %line_gather.1.rest_0_.a_ref), channel_id=1, source_target_pairs={{0,4},{1,5},{2,6},{3,7},{4,0},{5,1},{6,2},{7,3},{8,12},{9,13},{10,... | collective-permute-start | bytes 786440 | tf_op jit(solution)/shard_map/ppermute | solution.py:450
  56.8 1.5 %collective-permute-start.19 = (bf16[4,16,16,128]{3,2,1,0:T(8,128)(2,1)S(1)}, bf16[4,16,16,128]{3,2,1,0:T(8,128)(2,1)S(1)}, u32[]{:S(2)}, u32[]{:S(2)}) collective-permute-start(bf16[4,16,16,128]{3,2,1,0:T(8,128)(2,1)S(1)} %line_gather.1.rest_0_.a_ref), channel_id=1, source_target_pairs={{0,1},{1,0},{2,3},{3,2},{4,5},{5,4},{6,7},{7,6},{8,9},{9,8},{10,11... | collective-permute-start | bytes 786440 | tf_op jit(solution)/shard_map/ppermute | solution.py:450
  58.3 1.0 %collective-permute-start.18 = (bf16[4,16,16,128]{3,2,1,0:T(8,128)(2,1)S(1)}, bf16[4,16,16,128]{3,2,1,0:T(8,128)(2,1)S(1)}, u32[]{:S(2)}, u32[]{:S(2)}) collective-permute-start(bf16[4,16,16,128]{3,2,1,0:T(8,128)(2,1)S(1)} %line_gather.1.rest_0_.a_ref), channel_id=1, source_target_pairs={{0,5},{1,4},{2,7},{3,6},{4,1},{5,0},{6,3},{7,2},{8,13},{9,12},{10,... | collective-permute-start | bytes 786440 | tf_op jit(solution)/shard_map/ppermute | solution.py:450
  59.3 7.5 %grad_x.1 = (bf16[16,128,256]{2,1,0:T(8,128)(2,1)}, bf16[16,8,4,256]{3,2,1,0:T(4,128)(2,1)}, f32[8,128]{1,0:T(8,128)S(1)}) custom-call(s32[1]{0:T(128)S(6)} %copy.29.count_ref, bf16[16,8,16,256]{3,2,1,0:T(8,128)(2,1)S(1)} %get-tuple-element.44.xt_ref, bf16[16,8,16,256]{3,2,1,0:T(8,128)(2,1)S(1)} %get-tuple-element.49.gy_ref, ...), custom_call_target="tpu_custom_call" | custom-call | flops 2684354560 | bytes 7147524 | tf_op jit(solution)/shard_map/grad_x/pallas_call | solution.py:426
  66.8 1.8 %collective-permute-done.19.c_ref = bf16[4,16,16,128]{3,2,1,0:T(8,128)(2,1)S(1)} collective-permute-done((bf16[4,16,16,128]{3,2,1,0:T(8,128)(2,1)S(1)}, bf16[4,16,16,128]{3,2,1,0:T(8,128)(2,1)S(1)}, u32[]{:S(2)}, u32[]{:S(2)}) %collective-permute-start.19) | collective-permute-done | bytes 262176 | tf_op jit(solution)/shard_map/ppermute | solution.py:450
  68.6 0.1 plane_gather.1.half_ref
  68.7 1.5 %finish.2 = (f32[9,256,256]{2,1,0:T(8,128)}, f32[3,256,256]{2,1,0:T(8,128)}, f32[4,256,256]{2,1,0:T(8,128)}) custom-call(bf16[16,16,16,128]{3,2,1,0:T(8,128)(2,1)S(1)} %plane_gather.1.half_ref), custom_call_target="tpu_custom_call" | custom-call | bytes 5242880 | tf_op jit(solution)/shard_map/finish/pallas_call | solution.py:426
  70.2 1.2 %collective-permute-done.21.half_ref = bf16[16,16,16,128]{3,2,1,0:T(8,128)(2,1)S(1)} collective-permute-done((bf16[16,16,16,128]{3,2,1,0:T(8,128)(2,1)S(1)}, bf16[16,16,16,128]{3,2,1,0:T(8,128)(2,1)S(1)}, u32[]{:S(2)}, u32[]{:S(2)}) %collective-permute-start.21) | collective-permute-done | bytes 1048608 | tf_op jit(solution)/shard_map/ppermute | solution.py:450
  71.4 1.5 %finish.3 = (f32[9,256,256]{2,1,0:T(8,128)}, f32[3,256,256]{2,1,0:T(8,128)}, f32[4,256,256]{2,1,0:T(8,128)}) custom-call(bf16[16,16,16,128]{3,2,1,0:T(8,128)(2,1)S(1)} %collective-permute-done.21.half_ref, f32[9,256,256]{2,1,0:T(8,128)} %get-tuple-element.77.rest_0_, ...), custom_call_target="tpu_custom_call", output_to_operand_aliasing={{0}: (1, {}), {1}: (2, {}), {2}: (3, {})} | custom-call | bytes 9437184 | tf_op jit(solution)/shard_map/finish/pallas_call | solution.py:426
  (25 shorter events, 0.2 us)
Async XLA Ops:
  1.3 1.2 %copy-start.3 = (bf16[16,16,8,256]{3,2,1,0:T(8,128)(2,1)S(1)}, bf16[16,16,8,256]{3,2,1,0:T(8,128)(2,1)}, u32[]{:S(2)}) copy-start(bf16[16,16,8,256]{3,2,1,0:T(8,128)(2,1)} %param.6) | copy-start | bytes 3145732
  2.5 4.5 %copy-start.2 = (bf16[16,8,4,256]{3,2,1,0:T(4,128)(2,1)S(1)}, bf16[16,8,4,256]{3,2,1,0:T(4,128)(2,1)}, u32[]{:S(2)}) copy-start(bf16[16,8,4,256]{3,2,1,0:T(4,128)(2,1)} %cot_ref.3) | copy-start | bytes 786436
  2.8 5.5 %copy-start = (bf16[2,2,256,256]{3,2,1,0:T(8,128)(2,1)S(1)}, bf16[2,2,256,256]{3,2,1,0:T(8,128)(2,1)}, u32[]{:S(2)}) copy-start(bf16[2,2,256,256]{3,2,1,0:T(8,128)(2,1)} %param.10) | copy-start | bytes 1572868
  2.8 5.5 %copy-start.1 = (bf16[3,256,256]{2,1,0:T(8,128)(2,1)S(1)}, bf16[3,256,256]{2,1,0:T(8,128)(2,1)}, u32[]{:S(2)}) copy-start(bf16[3,256,256]{2,1,0:T(8,128)(2,1)} %wt_ref.5) | copy-start | bytes 1179652
  2.8 5.5 %collective-permute-start = (bf16[128,256]{1,0:T(8,128)(2,1)S(1)}, bf16[128,256]{1,0:T(8,128)(2,1)S(1)}, u32[]{:S(2)}, u32[]{:S(2)}) collective-permute-start(bf16[128,256]{1,0:T(8,128)(2,1)S(1)} %edges.1._), channel_id=1, source_target_pairs={{0,1},{1,0},{2,3},{3,2},{4,5},{5,4},{6,7},{7,6},{8,9},{9,8},{10,11... | collective-permute-start | bytes 196616 | tf_op jit(solution)/shard_map/ppermute | solution.py:504
  7.0 3.1 %collective-permute-start.1 = (bf16[2,8,4,256]{3,2,1,0:T(4,128)(2,1)S(1)}, bf16[2,8,4,256]{3,2,1,0:T(4,128)(2,1)S(1)}, u32[]{:S(2)}, u32[]{:S(2)}) collective-permute-start(bf16[2,8,4,256]{3,2,1,0:T(4,128)(2,1)S(1)} %next.1.rest_3_), channel_id=1, source_target_pairs={{2,0},{4,2},{6,4},{8,6},{10,8},{12,10},{14,12},{16,14},{18,16},{20... | collective-permute-start | bytes 98312 | tf_op jit(solution)/shard_map/ppermute | solution.py:494
  8.5 8.1 %collective-permute-start.3 = (bf16[288,256]{1,0:T(8,128)(2,1)S(1)}, bf16[288,256]{1,0:T(8,128)(2,1)S(1)}, u32[]{:S(2)}, u32[]{:S(2)}) collective-permute-start(bf16[288,256]{1,0:T(8,128)(2,1)S(1)} %get-tuple-element.53), channel_id=1, source_target_pairs={{0,2},{2,4},{4,6},{6,8},{8,10},{10,12},{12,14},{14,16},{16,18},{18... | collective-permute-start | bytes 442376 | tf_op jit(solution)/shard_map/ppermute | solution.py:499
  10.1 6.5 %copy-start.4 = (bf16[3,3,256,256]{3,2,1,0:T(8,128)(2,1)S(1)}, bf16[3,3,256,256]{3,2,1,0:T(8,128)(2,1)}, u32[]{:S(2)}) copy-start(bf16[3,3,256,256]{3,2,1,0:T(8,128)(2,1)} %param.8) | copy-start | bytes 3538948
  16.6 2.0 %collective-permute-start.4 = (bf16[16,9,16,128]{3,2,1,0:T(8,128)(2,1)S(1)}, bf16[16,9,16,128]{3,2,1,0:T(8,128)(2,1)S(1)}, u32[]{:S(2)}, u32[]{:S(2)}) collective-permute-start(bf16[16,9,16,128]{3,2,1,0:T(8,128)(2,1)S(1)} %pass.2._), channel_id=1, source_target_pairs={{0,2},{1,3},{2,0},{3,1},{4,6},{5,7},{6,4},{7,5},{8,10},{9,11},{10,... | collective-permute-start | bytes 1769480 | tf_op jit(solution)/shard_map/ppermute | solution.py:450
  18.8 7.0 %collective-permute-start.5 = (bf16[4,9,16,128]{3,2,1,0:T(8,128)(2,1)S(1)}, bf16[4,9,16,128]{3,2,1,0:T(8,128)(2,1)S(1)}, u32[]{:S(2)}, u32[]{:S(2)}) collective-permute-start(bf16[4,9,16,128]{3,2,1,0:T(8,128)(2,1)S(1)} %get-tuple-element.59.rest_1_), channel_id=1, source_target_pairs={{0,5},{1,4},{2,7},{3,6},{4,1},{5,0},{6,3},{7,2},{8,13},{9,12},{10,... | collective-permute-start | bytes 442376 | tf_op jit(solution)/shard_map/ppermute | solution.py:450
  25.7 1.9 %collective-permute-start.8 = (bf16[16,7,16,128]{3,2,1,0:T(8,128)(2,1)S(1)}, bf16[16,7,16,128]{3,2,1,0:T(8,128)(2,1)S(1)}, u32[]{:S(2)}, u32[]{:S(2)}) collective-permute-start(bf16[16,7,16,128]{3,2,1,0:T(8,128)(2,1)S(1)} %pass.3), channel_id=1, source_target_pairs={{0,2},{1,3},{2,0},{3,1},{4,6},{5,7},{6,4},{7,5},{8,10},{9,11},{10,... | collective-permute-start | bytes 1376264 | tf_op jit(solution)/shard_map/ppermute | solution.py:450
  25.7 6.5 %collective-permute-start.6 = (bf16[4,9,16,128]{3,2,1,0:T(8,128)(2,1)S(1)}, bf16[4,9,16,128]{3,2,1,0:T(8,128)(2,1)S(1)}, u32[]{:S(2)}, u32[]{:S(2)}) collective-permute-start(bf16[4,9,16,128]{3,2,1,0:T(8,128)(2,1)S(1)} %get-tuple-element.60.rest_2_), channel_id=1, source_target_pairs={{0,1},{1,0},{2,3},{3,2},{4,5},{5,4},{6,7},{7,6},{8,9},{9,8},{10,11... | collective-permute-start | bytes 442376 | tf_op jit(solution)/shard_map/ppermute | solution.py:450
  26.7 6.7 %collective-permute-start.7 = (bf16[4,9,16,128]{3,2,1,0:T(8,128)(2,1)S(1)}, bf16[4,9,16,128]{3,2,1,0:T(8,128)(2,1)S(1)}, u32[]{:S(2)}, u32[]{:S(2)}) collective-permute-start(bf16[4,9,16,128]{3,2,1,0:T(8,128)(2,1)S(1)} %get-tuple-element.61.rest_3_), channel_id=1, source_target_pairs={{0,4},{1,5},{2,6},{3,7},{4,0},{5,1},{6,2},{7,3},{8,12},{9,13},{10,... | collective-permute-start | bytes 442376 | tf_op jit(solution)/shard_map/ppermute | solution.py:450
  27.7 8.6 %collective-permute-start.9 = (bf16[4,7,16,128]{3,2,1,0:T(8,128)(2,1)S(1)}, bf16[4,7,16,128]{3,2,1,0:T(8,128)(2,1)S(1)}, u32[]{:S(2)}, u32[]{:S(2)}) collective-permute-start(bf16[4,7,16,128]{3,2,1,0:T(8,128)(2,1)S(1)} %get-tuple-element.67), channel_id=1, source_target_pairs={{0,5},{1,4},{2,7},{3,6},{4,1},{5,0},{6,3},{7,2},{8,13},{9,12},{10,... | collective-permute-start | bytes 344072 | tf_op jit(solution)/shard_map/ppermute | solution.py:450
  29.4 7.5 %collective-permute-start.10 = (bf16[4,7,16,128]{3,2,1,0:T(8,128)(2,1)S(1)}, bf16[4,7,16,128]{3,2,1,0:T(8,128)(2,1)S(1)}, u32[]{:S(2)}, u32[]{:S(2)}) collective-permute-start(bf16[4,7,16,128]{3,2,1,0:T(8,128)(2,1)S(1)} %get-tuple-element.68), channel_id=1, source_target_pairs={{0,1},{1,0},{2,3},{3,2},{4,5},{5,4},{6,7},{7,6},{8,9},{9,8},{10,11... | collective-permute-start | bytes 344072 | tf_op jit(solution)/shard_map/ppermute | solution.py:450
  30.7 7.0 %collective-permute-start.11 = (bf16[4,7,16,128]{3,2,1,0:T(8,128)(2,1)S(1)}, bf16[4,7,16,128]{3,2,1,0:T(8,128)(2,1)S(1)}, u32[]{:S(2)}, u32[]{:S(2)}) collective-permute-start(bf16[4,7,16,128]{3,2,1,0:T(8,128)(2,1)S(1)} %get-tuple-element.69), channel_id=1, source_target_pairs={{0,4},{1,5},{2,6},{3,7},{4,0},{5,1},{6,2},{7,3},{8,12},{9,13},{10,... | collective-permute-start | bytes 344072 | tf_op jit(solution)/shard_map/ppermute | solution.py:450
  37.8 6.2 %collective-permute-start.12 = (bf16[16,16,128]{2,1,0:T(8,128)(2,1)S(1)}, bf16[16,16,128]{2,1,0:T(8,128)(2,1)S(1)}, u32[]{:S(2)}, u32[]{:S(2)}) collective-permute-start(bf16[16,16,128]{2,1,0:T(8,128)(2,1)S(1)} %get-tuple-element.71), channel_id=1, source_target_pairs={{0,24},{1,25},{2,26},{3,27},{4,28},{5,29},{6,30},{7,31},{8,16},{9,... | collective-permute-start | bytes 196616 | tf_op jit(solution)/shard_map/ppermute | solution.py:450
  40.3 6.3 %collective-permute-start.13 = (bf16[16,16,128]{2,1,0:T(8,128)(2,1)S(1)}, bf16[16,16,128]{2,1,0:T(8,128)(2,1)S(1)}, u32[]{:S(2)}, u32[]{:S(2)}) collective-permute-start(bf16[16,16,128]{2,1,0:T(8,128)(2,1)S(1)} %get-tuple-element.72), channel_id=1, source_target_pairs={{0,16},{1,17},{2,18},{3,19},{4,20},{5,21},{6,22},{7,23},{8,24},{9,... | collective-permute-start | bytes 196616 | tf_op jit(solution)/shard_map/ppermute | solution.py:450
  40.3 6.3 %collective-permute-start.14 = (bf16[16,16,128]{2,1,0:T(8,128)(2,1)S(1)}, bf16[16,16,128]{2,1,0:T(8,128)(2,1)S(1)}, u32[]{:S(2)}, u32[]{:S(2)}) collective-permute-start(bf16[16,16,128]{2,1,0:T(8,128)(2,1)S(1)} %get-tuple-element.73), channel_id=1, source_target_pairs={{0,8},{1,9},{2,10},{3,11},{4,12},{5,13},{6,14},{7,15},{8,0},{9,1},... | collective-permute-start | bytes 196616 | tf_op jit(solution)/shard_map/ppermute | solution.py:450
  46.6 5.6 %collective-permute-start.17 = (bf16[16,16,128]{2,1,0:T(8,128)(2,1)S(1)}, bf16[16,16,128]{2,1,0:T(8,128)(2,1)S(1)}, u32[]{:S(2)}, u32[]{:S(2)}) collective-permute-start(bf16[16,16,128]{2,1,0:T(8,128)(2,1)S(1)} %line_sum.1.a_ref), channel_id=1, source_target_pairs={{0,8},{1,9},{2,10},{3,11},{4,12},{5,13},{6,14},{7,15},{8,0},{9,1},... | collective-permute-start | bytes 196616 | tf_op jit(solution)/shard_map/ppermute | solution.py:450
  46.7 7.5 %collective-permute-start.16 = (bf16[16,16,128]{2,1,0:T(8,128)(2,1)S(1)}, bf16[16,16,128]{2,1,0:T(8,128)(2,1)S(1)}, u32[]{:S(2)}, u32[]{:S(2)}) collective-permute-start(bf16[16,16,128]{2,1,0:T(8,128)(2,1)S(1)} %line_sum.1.a_ref), channel_id=1, source_target_pairs={{0,16},{1,17},{2,18},{3,19},{4,20},{5,21},{6,22},{7,23},{8,24},{9,... | collective-permute-start | bytes 196616 | tf_op jit(solution)/shard_map/ppermute | solution.py:450
  49.7 6.1 %collective-permute-start.15 = (bf16[16,16,128]{2,1,0:T(8,128)(2,1)S(1)}, bf16[16,16,128]{2,1,0:T(8,128)(2,1)S(1)}, u32[]{:S(2)}, u32[]{:S(2)}) collective-permute-start(bf16[16,16,128]{2,1,0:T(8,128)(2,1)S(1)} %line_sum.1.a_ref), channel_id=1, source_target_pairs={{0,24},{1,25},{2,26},{3,27},{4,28},{5,29},{6,30},{7,31},{8,16},{9,... | collective-permute-start | bytes 196616 | tf_op jit(solution)/shard_map/ppermute | solution.py:450
  51.1 8.3 %collective-permute-start.2 = (bf16[64,256]{1,0:T(8,128)(2,1)S(1)}, bf16[64,256]{1,0:T(8,128)(2,1)S(1)}, u32[]{:S(2)}, u32[]{:S(2)}) collective-permute-start(bf16[64,256]{1,0:T(8,128)(2,1)S(1)} %get-tuple-element.51), channel_id=1, source_target_pairs={{0,1},{1,0},{2,3},{3,2},{4,5},{5,4},{6,7},{7,6},{8,9},{9,8},{10,11... | collective-permute-start | bytes 98312 | tf_op jit(solution)/shard_map/ppermute | solution.py:504
  55.8 11.0 %collective-permute-start.20 = (bf16[4,16,16,128]{3,2,1,0:T(8,128)(2,1)S(1)}, bf16[4,16,16,128]{3,2,1,0:T(8,128)(2,1)S(1)}, u32[]{:S(2)}, u32[]{:S(2)}) collective-permute-start(bf16[4,16,16,128]{3,2,1,0:T(8,128)(2,1)S(1)} %line_gather.1.rest_0_.a_ref), channel_id=1, source_target_pairs={{0,4},{1,5},{2,6},{3,7},{4,0},{5,1},{6,2},{7,3},{8,12},{9,13},{10,... | collective-permute-start | bytes 786440 | tf_op jit(solution)/shard_map/ppermute | solution.py:450
  56.8 11.8 %collective-permute-start.19 = (bf16[4,16,16,128]{3,2,1,0:T(8,128)(2,1)S(1)}, bf16[4,16,16,128]{3,2,1,0:T(8,128)(2,1)S(1)}, u32[]{:S(2)}, u32[]{:S(2)}) collective-permute-start(bf16[4,16,16,128]{3,2,1,0:T(8,128)(2,1)S(1)} %line_gather.1.rest_0_.a_ref), channel_id=1, source_target_pairs={{0,1},{1,0},{2,3},{3,2},{4,5},{5,4},{6,7},{7,6},{8,9},{9,8},{10,11... | collective-permute-start | bytes 786440 | tf_op jit(solution)/shard_map/ppermute | solution.py:450
  58.3 10.2 %collective-permute-start.18 = (bf16[4,16,16,128]{3,2,1,0:T(8,128)(2,1)S(1)}, bf16[4,16,16,128]{3,2,1,0:T(8,128)(2,1)S(1)}, u32[]{:S(2)}, u32[]{:S(2)}) collective-permute-start(bf16[4,16,16,128]{3,2,1,0:T(8,128)(2,1)S(1)} %line_gather.1.rest_0_.a_ref), channel_id=1, source_target_pairs={{0,5},{1,4},{2,7},{3,6},{4,1},{5,0},{6,3},{7,2},{8,13},{9,12},{10,... | collective-permute-start | bytes 786440 | tf_op jit(solution)/shard_map/ppermute | solution.py:450
  68.7 2.7 %collective-permute-start.21 = (bf16[16,16,16,128]{3,2,1,0:T(8,128)(2,1)S(1)}, bf16[16,16,16,128]{3,2,1,0:T(8,128)(2,1)S(1)}, u32[]{:S(2)}, u32[]{:S(2)}) collective-permute-start(bf16[16,16,16,128]{3,2,1,0:T(8,128)(2,1)S(1)} %plane_gather.1.half_ref), channel_id=1, source_target_pairs={{0,2},{1,3},{2,0},{3,1},{4,6},{5,7},{6,4},{7,5},{8,10},{9,11},{10,... | collective-permute-start | bytes 3145736 | tf_op jit(solution)/shard_map/ppermute | solution.py:450

commit v26 on v25

--- a/solution.py
+++ b/solution.py
@@ -251,20 +251,20 @@
     down_ref, keep_ref, send_ref, y_ref, st_ref, yt_ref = rest[-6:]
     count = count_ref[0]
     rows, cols = xt_ref.shape[0], xt_ref.shape[1]
-    for q, sp_ref in enumerate((upper_ref, lower_ref)):
-        s = sp_ref[...].reshape(8 * cols * SLOTS, CH).astype(F32)
-        s = s.reshape(8 * cols, SLOTS, CH)
-        total = None
+    for q in range(rows // 4):
+        sp_ref = upper_ref if q < rows // 8 else lower_ref
+        at = 4 * (q % (rows // 8))
+        s = sp_ref[at : at + 4].astype(F32).reshape(4 * cols, SLOTS, CH)
+        taps = []
         for k in range(3):
             shifted = s if k == 2 else pltpu.roll(s, 2 - k, 1)
-            shifted = shifted.astype(BF).reshape(8 * cols * SLOTS, CH)
-            at = slice(q * 1024, q * 1024 + 1024)
-            st_ref[k * CH : k * CH + CH, at] = shifted.T
-            term = mm(shifted, wt_ref[k])
-            total = term if total is None else total + term
-        x = xt_ref[8 * q : 8 * q + 8].reshape(8 * cols, SLOTS, CH).astype(F32)
+            shifted = shifted.astype(BF).reshape(4 * cols * SLOTS, CH)
+            st_ref[k * CH : k * CH + CH, q * 512 : q * 512 + 512] = shifted.T
+            taps.append(shifted)
+        total = mm(jnp.concatenate(taps, axis=1), wt_ref[...].reshape(3 * CH, CH))
+        x = xt_ref[4 * q : 4 * q + 4].reshape(4 * cols, SLOTS, CH).astype(F32)
         y = jnp.where(slot_mask(x.shape, count), x + total.reshape(x.shape), 0.0).astype(BF)
-        y_ref[8 * q : 8 * q + 8] = y.reshape(8, cols, SLOTS, CH)
+        y_ref[4 * q : 4 * q + 4] = y.reshape(4, cols, SLOTS, CH)
 
     wide = rows * cols * SLOTS
     value = mm(st_ref[...], gy_ref[...].reshape(wide, CH))

time: 73 us -> 73 us (level)
  no operation moved by 1% of the time
where the time goes in v26:
time: 73 us; the launch traced here: 72.9 us
  starting transfers between devices  26 us (36%)
  waiting for transfers between devices  22.2 us (30%)
  Pallas kernels  22 us (30%)
  between operations  1.48 us (2%)
  local copies, waits for them, and re-layouts  1.24 us (2%)
    pallas_call x19, Pallas kernels, call(): pl.pallas_call(kernel, out_shape=shapes, in_specs=[s for s, _ in ins], ou...  22 us
    ppermute x18, starting transfers between devices, swap(): return lax.ppermute(value, AXES, [(d, d ^ flip) for d in range(tm * grp)])  19.4 us
    ppermute x18, waiting for transfers between devices, swap(): return lax.ppermute(value, AXES, [(d, d ^ flip) for d in range(tm * grp)])  19.2 us
    ppermute x2, starting transfers between devices, from_bands(): got = lax.ppermute(parts[0], 'grp', [(0, 1), (1, 0)])  4.17 us
    ppermute x1, waiting for transfers between devices, around(): lax.ppermute(value, axis, [(i, (i + by) % count) for i in range(count)])  2.52 us
  transfers between devices with their start and end apart: 22, of which 15 were waited for; matrix products, arithmetic and copies ran while one was open for 0% of the time, Pallas kernels for 27%

profile of v26, /device:TPU:0, one launch (start us, length us, event | category | flops | bytes accessed | tf_op | source)
XLA Modules:
  0.0 72.9 jit_solution(18207605311086800720)
XLA Ops:
  1.3 1.2 %copy-done.3 = bf16[16,16,8,256]{3,2,1,0:T(8,128)(2,1)S(1)} copy-done((bf16[16,16,8,256]{3,2,1,0:T(8,128)(2,1)S(1)}, bf16[16,16,8,256]{3,2,1,0:T(8,128)(2,1)}, u32[]{:S(2)}) %copy-start.3) | copy-done | bytes 1048600
  2.5 0.3 edges.1._
  2.8 3.0 %collective-permute-start = (bf16[128,256]{1,0:T(8,128)(2,1)S(1)}, bf16[128,256]{1,0:T(8,128)(2,1)S(1)}, u32[]{:S(2)}, u32[]{:S(2)}) collective-permute-start(bf16[128,256]{1,0:T(8,128)(2,1)S(1)} %edges.1._), channel_id=1, source_target_pairs={{0,1},{1,0},{2,3},{3,2},{4,5},{5,4},{6,7},{7,6},{8,9},{9,8},{10,11... | collective-permute-start | bytes 196616 | tf_op jit(solution)/shard_map/ppermute | solution.py:504
  5.9 1.1 %acts.1 = (bf16[16,8,16,256]{3,2,1,0:T(8,128)(2,1)S(1)}, bf16[18,10,16,256]{3,2,1,0:T(8,128)(2,1)S(1)}, bf16[768,2560]{1,0:T(8,128)(2,1)S(1)}, bf16[288,256]{1,0:T(8,128)(2,1)S(1)}) custom-call(s32[1]{0:T(128)S(6)} %copy.29.count_ref, bf16[16,128,256]{2,1,0:T(8,128)(2,1)S(1)} %bitcast.11, bf16[128,256]{1,0:T(8,128)(2,1)S(1)} %edges.1._), custom_call_target="tpu_custom_call" | custom-call | flops 536870912 | bytes 7651332 | tf_op jit(solution)/shard_map/acts/pallas_call | solution.py:426
  7.0 1.3 %collective-permute-start.1 = (bf16[2,8,4,256]{3,2,1,0:T(4,128)(2,1)S(1)}, bf16[2,8,4,256]{3,2,1,0:T(4,128)(2,1)S(1)}, u32[]{:S(2)}, u32[]{:S(2)}) collective-permute-start(bf16[2,8,4,256]{3,2,1,0:T(4,128)(2,1)S(1)} %next.1.rest_3_), channel_id=1, source_target_pairs={{2,0},{4,2},{6,4},{8,6},{10,8},{12,10},{14,12},{16,14},{18,16},{20... | collective-permute-start | bytes 98312 | tf_op jit(solution)/shard_map/ppermute | solution.py:494
  8.4 0.2 halo.1
  8.5 1.1 %collective-permute-start.3 = (bf16[288,256]{1,0:T(8,128)(2,1)S(1)}, bf16[288,256]{1,0:T(8,128)(2,1)S(1)}, u32[]{:S(2)}, u32[]{:S(2)}) collective-permute-start(bf16[288,256]{1,0:T(8,128)(2,1)S(1)} %get-tuple-element.53), channel_id=1, source_target_pairs={{0,2},{2,4},{4,6},{6,8},{8,10},{10,12},{12,14},{14,16},{16,18},{18... | collective-permute-start | bytes 442376 | tf_op jit(solution)/shard_map/ppermute | solution.py:499
  9.7 0.5 collective-permute-done.1.nxt_ref
  10.1 3.9 %grad_spatial.1 = (bf16[8,4,16,256]{3,2,1,0:T(8,128)(2,1)S(1)}, bf16[16,8,16,256]{3,2,1,0:T(8,128)(2,1)S(1)}, bf16[16,10,16,256]{3,2,1,0:T(8,128)(2,1)S(1)}, bf1...) custom-call(s32[1]{0:T(128)S(6)} %copy.29.count_ref, ...), custom_call_target="tpu_custom_call" | custom-call | flops 3758096384 | bytes 8978436 | tf_op jit(solution)/shard_map/grad_spatial/pallas_call | solution.py:426
  14.1 2.5 %collective-permute-done.3.__1_.prev_ref = bf16[288,256]{1,0:T(8,128)(2,1)S(1)} collective-permute-done((bf16[288,256]{1,0:T(8,128)(2,1)S(1)}, bf16[288,256]{1,0:T(8,128)(2,1)S(1)}, u32[]{:S(2)}, u32[]{:S(2)}) %collective-permute-start.3) | collective-permute-done | bytes 147488 | tf_op jit(solution)/shard_map/ppermute | solution.py:499
  16.6 1.7 %spatial_upper.1 = (bf16[18,10,16,256]{3,2,1,0:T(8,128)(2,1)S(1)}, bf16[8,8,16,256]{3,2,1,0:T(8,128)(2,1)S(1)}) custom-call(bf16[18,10,16,256]{3,2,1,0:T(8,128)(2,1)S(1)} %get-tuple-element.52.acts_in, bf16[288,256]{1,0:T(8,128)(2,1)S(1)} %collective-permute-done.3.__1_.prev_ref, bf16[9,256,256]{2,1,0:T(8,128)(2,1)S(1)} %bitcast.12, ...), custom_call_target="tpu_custom_call", output_to_operand_aliasing={{0}: (0, {})} | custom-call | flops 1342177280 | bytes 4800512 | tf_op jit(solution)/shard_map/spatial_upper/pallas_call | solution.py:426
  18.4 0.3 collective-permute-done.4.got_ref
  18.6 0.1 plane_send.2
  18.8 1.4 %collective-permute-start.5 = (bf16[4,9,16,128]{3,2,1,0:T(8,128)(2,1)S(1)}, bf16[4,9,16,128]{3,2,1,0:T(8,128)(2,1)S(1)}, u32[]{:S(2)}, u32[]{:S(2)}) collective-permute-start(bf16[4,9,16,128]{3,2,1,0:T(8,128)(2,1)S(1)} %get-tuple-element.59.rest_1_), channel_id=1, source_target_pairs={{0,5},{1,4},{2,7},{3,6},{4,1},{5,0},{6,3},{7,2},{8,13},{9,12},{10,... | collective-permute-start | bytes 442376 | tf_op jit(solution)/shard_map/ppermute | solution.py:450
  20.2 1.4 %spatial_lower.1.lower_ref = bf16[8,8,16,256]{3,2,1,0:T(8,128)(2,1)S(1)} custom-call(bf16[18,10,16,256]{3,2,1,0:T(8,128)(2,1)S(1)} %get-tuple-element.56.acts_ref, bf16[9,256,256]{2,1,0:T(8,128)(2,1)S(1)} %bitcast.13, bf16[4,9,16,128]{3,2,1,0:T(8,128)(2,1)S(1)} %get-tuple-element.58.rest_0_.refs_0_, bf16[4,9,16,128]{3,2,1,0:T(8,128)(2,1)S(1)} %get-tuple-element.59.rest_1_, ...), custom_call_target="tpu_custom_call" | custom-call | flops 1073741824 | bytes 3178496 | tf_op jit(solution)/shard_map/spatial_lower/pallas_call | solution.py:426
  21.5 2.4 %forward.1 = (bf16[512,256]{1,0:T(8,128)(2,1)S(1)}, bf16[16,7,16,128]{3,2,1,0:T(8,128)(2,1)S(1)}, bf16[16,7,16,128]{3,2,1,0:T(8,128)(2,1)S(1)}) custom-call(s32[1]{0:T(128)S(6)} %copy.29.count_ref, bf16[16,8,16,256]{3,2,1,0:T(8,128)(2,1)S(1)} %get-tuple-element.44.xt_ref, bf16[8,8,16,256]{3,2,1,0:T(8,128)(2,1)S(1)} %get-tuple-element.55.rest_0_.upper_ref, ...), custom_call_target="tpu_custom_call" | custom-call | bytes 1024 | tf_op jit(solution)/shard_map/forward/pallas_call | solution.py:426
  24.0 1.8 %collective-permute-done.5.__1_.refs_1_ = bf16[4,9,16,128]{3,2,1,0:T(8,128)(2,1)S(1)} collective-permute-done((bf16[4,9,16,128]{3,2,1,0:T(8,128)(2,1)S(1)}, bf16[4,9,16,128]{3,2,1,0:T(8,128)(2,1)S(1)}, u32[]{:S(2)}, u32[]{:S(2)}) %collective-permute-start.5) | collective-permute-done | bytes 147488 | tf_op jit(solution)/shard_map/ppermute | solution.py:450
  25.7 0.9 %collective-permute-start.6 = (bf16[4,9,16,128]{3,2,1,0:T(8,128)(2,1)S(1)}, bf16[4,9,16,128]{3,2,1,0:T(8,128)(2,1)S(1)}, u32[]{:S(2)}, u32[]{:S(2)}) collective-permute-start(bf16[4,9,16,128]{3,2,1,0:T(8,128)(2,1)S(1)} %get-tuple-element.60.rest_2_), channel_id=1, source_target_pairs={{0,1},{1,0},{2,3},{3,2},{4,5},{5,4},{6,7},{7,6},{8,9},{9,8},{10,11... | collective-permute-start | bytes 442376 | tf_op jit(solution)/shard_map/ppermute | solution.py:450
  26.7 0.9 %collective-permute-start.7 = (bf16[4,9,16,128]{3,2,1,0:T(8,128)(2,1)S(1)}, bf16[4,9,16,128]{3,2,1,0:T(8,128)(2,1)S(1)}, u32[]{:S(2)}, u32[]{:S(2)}) collective-permute-start(bf16[4,9,16,128]{3,2,1,0:T(8,128)(2,1)S(1)} %get-tuple-element.61.rest_3_), channel_id=1, source_target_pairs={{0,4},{1,5},{2,6},{3,7},{4,0},{5,1},{6,2},{7,3},{8,12},{9,13},{10,... | collective-permute-start | bytes 442376 | tf_op jit(solution)/shard_map/ppermute | solution.py:450
  27.6 0.1 plane_send.3
  27.7 1.7 %collective-permute-start.9 = (bf16[4,7,16,128]{3,2,1,0:T(8,128)(2,1)S(1)}, bf16[4,7,16,128]{3,2,1,0:T(8,128)(2,1)S(1)}, u32[]{:S(2)}, u32[]{:S(2)}) collective-permute-start(bf16[4,7,16,128]{3,2,1,0:T(8,128)(2,1)S(1)} %get-tuple-element.67), channel_id=1, source_target_pairs={{0,5},{1,4},{2,7},{3,6},{4,1},{5,0},{6,3},{7,2},{8,13},{9,12},{10,... | collective-permute-start | bytes 344072 | tf_op jit(solution)/shard_map/ppermute | solution.py:450
  29.4 1.3 %collective-permute-start.10 = (bf16[4,7,16,128]{3,2,1,0:T(8,128)(2,1)S(1)}, bf16[4,7,16,128]{3,2,1,0:T(8,128)(2,1)S(1)}, u32[]{:S(2)}, u32[]{:S(2)}) collective-permute-start(bf16[4,7,16,128]{3,2,1,0:T(8,128)(2,1)S(1)} %get-tuple-element.68), channel_id=1, source_target_pairs={{0,1},{1,0},{2,3},{3,2},{4,5},{5,4},{6,7},{7,6},{8,9},{9,8},{10,11... | collective-permute-start | bytes 344072 | tf_op jit(solution)/shard_map/ppermute | solution.py:450
  30.7 0.6 collective-permute-start.11
  31.3 1.0 %collective-permute-done.6.refs_2_ = bf16[4,9,16,128]{3,2,1,0:T(8,128)(2,1)S(1)} collective-permute-done((bf16[4,9,16,128]{3,2,1,0:T(8,128)(2,1)S(1)}, bf16[4,9,16,128]{3,2,1,0:T(8,128)(2,1)S(1)}, u32[]{:S(2)}, u32[]{:S(2)}) %collective-permute-start.6) | collective-permute-done | bytes 147488 | tf_op jit(solution)/shard_map/ppermute | solution.py:450
  32.3 1.1 %collective-permute-done.7.refs_3_ = bf16[4,9,16,128]{3,2,1,0:T(8,128)(2,1)S(1)} collective-permute-done((bf16[4,9,16,128]{3,2,1,0:T(8,128)(2,1)S(1)}, bf16[4,9,16,128]{3,2,1,0:T(8,128)(2,1)S(1)}, u32[]{:S(2)}, u32[]{:S(2)}) %collective-permute-start.7) | collective-permute-done | bytes 147488 | tf_op jit(solution)/shard_map/ppermute | solution.py:450
  33.4 3.0 %collective-permute-done.9.refs_5_ = bf16[4,7,16,128]{3,2,1,0:T(8,128)(2,1)S(1)} collective-permute-done((bf16[4,7,16,128]{3,2,1,0:T(8,128)(2,1)S(1)}, bf16[4,7,16,128]{3,2,1,0:T(8,128)(2,1)S(1)}, u32[]{:S(2)}, u32[]{:S(2)}) %collective-permute-start.9) | collective-permute-done | bytes 114720 | tf_op jit(solution)/shard_map/ppermute | solution.py:450
  36.4 0.5 collective-permute-done.10.refs_6_
  36.9 0.7 collective-permute-done.11.refs_7_
  37.6 0.1 line_send.1
  37.8 2.5 %collective-permute-start.12 = (bf16[16,16,128]{2,1,0:T(8,128)(2,1)S(1)}, bf16[16,16,128]{2,1,0:T(8,128)(2,1)S(1)}, u32[]{:S(2)}, u32[]{:S(2)}) collective-permute-start(bf16[16,16,128]{2,1,0:T(8,128)(2,1)S(1)} %get-tuple-element.71), channel_id=1, source_target_pairs={{0,24},{1,25},{2,26},{3,27},{4,28},{5,29},{6,30},{7,31},{8,16},{9,... | collective-permute-start | bytes 196616 | tf_op jit(solution)/shard_map/ppermute | solution.py:450
  40.3 1.9 %collective-permute-start.14 = (bf16[16,16,128]{2,1,0:T(8,128)(2,1)S(1)}, bf16[16,16,128]{2,1,0:T(8,128)(2,1)S(1)}, u32[]{:S(2)}, u32[]{:S(2)}) collective-permute-start(bf16[16,16,128]{2,1,0:T(8,128)(2,1)S(1)} %get-tuple-element.73), channel_id=1, source_target_pairs={{0,8},{1,9},{2,10},{3,11},{4,12},{5,13},{6,14},{7,15},{8,0},{9,1},... | collective-permute-start | bytes 196616 | tf_op jit(solution)/shard_map/ppermute | solution.py:450
  42.2 1.8 %collective-permute-done.12.b_ref = bf16[16,16,128]{2,1,0:T(8,128)(2,1)S(1)} collective-permute-done((bf16[16,16,128]{2,1,0:T(8,128)(2,1)S(1)}, bf16[16,16,128]{2,1,0:T(8,128)(2,1)S(1)}, u32[]{:S(2)}, u32[]{:S(2)}) %collective-permute-start.12) | collective-permute-done | bytes 65568 | tf_op jit(solution)/shard_map/ppermute | solution.py:450
  44.0 2.6 %collective-permute-done.13.c_ref = bf16[16,16,128]{2,1,0:T(8,128)(2,1)S(1)} collective-permute-done((bf16[16,16,128]{2,1,0:T(8,128)(2,1)S(1)}, bf16[16,16,128]{2,1,0:T(8,128)(2,1)S(1)}, u32[]{:S(2)}, u32[]{:S(2)}) %collective-permute-start.13) | collective-permute-done | bytes 65568 | tf_op jit(solution)/shard_map/ppermute | solution.py:450
  46.6 0.1 collective-permute-start.17
  46.7 3.0 %collective-permute-start.16 = (bf16[16,16,128]{2,1,0:T(8,128)(2,1)S(1)}, bf16[16,16,128]{2,1,0:T(8,128)(2,1)S(1)}, u32[]{:S(2)}, u32[]{:S(2)}) collective-permute-start(bf16[16,16,128]{2,1,0:T(8,128)(2,1)S(1)} %line_sum.1.a_ref), channel_id=1, source_target_pairs={{0,16},{1,17},{2,18},{3,19},{4,20},{5,21},{6,22},{7,23},{8,24},{9,... | collective-permute-start | bytes 196616 | tf_op jit(solution)/shard_map/ppermute | solution.py:450
  49.7 1.4 %collective-permute-start.15 = (bf16[16,16,128]{2,1,0:T(8,128)(2,1)S(1)}, bf16[16,16,128]{2,1,0:T(8,128)(2,1)S(1)}, u32[]{:S(2)}, u32[]{:S(2)}) collective-permute-start(bf16[16,16,128]{2,1,0:T(8,128)(2,1)S(1)} %line_sum.1.a_ref), channel_id=1, source_target_pairs={{0,24},{1,25},{2,26},{3,27},{4,28},{5,29},{6,30},{7,31},{8,16},{9,... | collective-permute-start | bytes 196616 | tf_op jit(solution)/shard_map/ppermute | solution.py:450
  51.1 1.1 %collective-permute-start.2 = (bf16[64,256]{1,0:T(8,128)(2,1)S(1)}, bf16[64,256]{1,0:T(8,128)(2,1)S(1)}, u32[]{:S(2)}, u32[]{:S(2)}) collective-permute-start(bf16[64,256]{1,0:T(8,128)(2,1)S(1)} %get-tuple-element.51), channel_id=1, source_target_pairs={{0,1},{1,0},{2,3},{3,2},{4,5},{5,4},{6,7},{7,6},{8,9},{9,8},{10,11... | collective-permute-start | bytes 98312 | tf_op jit(solution)/shard_map/ppermute | solution.py:504
  52.2 1.9 %collective-permute-done.16.c_ref = bf16[16,16,128]{2,1,0:T(8,128)(2,1)S(1)} collective-permute-done((bf16[16,16,128]{2,1,0:T(8,128)(2,1)S(1)}, bf16[16,16,128]{2,1,0:T(8,128)(2,1)S(1)}, u32[]{:S(2)}, u32[]{:S(2)}) %collective-permute-start.16) | collective-permute-done | bytes 65568 | tf_op jit(solution)/shard_map/ppermute | solution.py:450
  54.1 1.6 %collective-permute-done.15.b_ref = bf16[16,16,128]{2,1,0:T(8,128)(2,1)S(1)} collective-permute-done((bf16[16,16,128]{2,1,0:T(8,128)(2,1)S(1)}, bf16[16,16,128]{2,1,0:T(8,128)(2,1)S(1)}, u32[]{:S(2)}, u32[]{:S(2)}) %collective-permute-start.15) | collective-permute-done | bytes 65568 | tf_op jit(solution)/shard_map/ppermute | solution.py:450
  55.8 1.0 %collective-permute-start.20 = (bf16[4,16,16,128]{3,2,1,0:T(8,128)(2,1)S(1)}, bf16[4,16,16,128]{3,2,1,0:T(8,128)(2,1)S(1)}, u32[]{:S(2)}, u32[]{:S(2)}) collective-permute-start(bf16[4,16,16,128]{3,2,1,0:T(8,128)(2,1)S(1)} %line_gather.1.rest_0_.a_ref), channel_id=1, source_target_pairs={{0,4},{1,5},{2,6},{3,7},{4,0},{5,1},{6,2},{7,3},{8,12},{9,13},{10,... | collective-permute-start | bytes 786440 | tf_op jit(solution)/shard_map/ppermute | solution.py:450
  56.8 1.5 %collective-permute-start.19 = (bf16[4,16,16,128]{3,2,1,0:T(8,128)(2,1)S(1)}, bf16[4,16,16,128]{3,2,1,0:T(8,128)(2,1)S(1)}, u32[]{:S(2)}, u32[]{:S(2)}) collective-permute-start(bf16[4,16,16,128]{3,2,1,0:T(8,128)(2,1)S(1)} %line_gather.1.rest_0_.a_ref), channel_id=1, source_target_pairs={{0,1},{1,0},{2,3},{3,2},{4,5},{5,4},{6,7},{7,6},{8,9},{9,8},{10,11... | collective-permute-start | bytes 786440 | tf_op jit(solution)/shard_map/ppermute | solution.py:450
  58.3 1.0 %collective-permute-start.18 = (bf16[4,16,16,128]{3,2,1,0:T(8,128)(2,1)S(1)}, bf16[4,16,16,128]{3,2,1,0:T(8,128)(2,1)S(1)}, u32[]{:S(2)}, u32[]{:S(2)}) collective-permute-start(bf16[4,16,16,128]{3,2,1,0:T(8,128)(2,1)S(1)} %line_gather.1.rest_0_.a_ref), channel_id=1, source_target_pairs={{0,5},{1,4},{2,7},{3,6},{4,1},{5,0},{6,3},{7,2},{8,13},{9,12},{10,... | collective-permute-start | bytes 786440 | tf_op jit(solution)/shard_map/ppermute | solution.py:450
  59.3 7.5 %grad_x.1 = (bf16[16,128,256]{2,1,0:T(8,128)(2,1)}, bf16[16,8,4,256]{3,2,1,0:T(4,128)(2,1)}, f32[8,128]{1,0:T(8,128)S(1)}) custom-call(s32[1]{0:T(128)S(6)} %copy.29.count_ref, bf16[16,8,16,256]{3,2,1,0:T(8,128)(2,1)S(1)} %get-tuple-element.44.xt_ref, bf16[16,8,16,256]{3,2,1,0:T(8,128)(2,1)S(1)} %get-tuple-element.49.gy_ref, ...), custom_call_target="tpu_custom_call" | custom-call | flops 2684354560 | bytes 7147524 | tf_op jit(solution)/shard_map/grad_x/pallas_call | solution.py:426
  66.8 1.8 %collective-permute-done.19.c_ref = bf16[4,16,16,128]{3,2,1,0:T(8,128)(2,1)S(1)} collective-permute-done((bf16[4,16,16,128]{3,2,1,0:T(8,128)(2,1)S(1)}, bf16[4,16,16,128]{3,2,1,0:T(8,128)(2,1)S(1)}, u32[]{:S(2)}, u32[]{:S(2)}) %collective-permute-start.19) | collective-permute-done | bytes 262176 | tf_op jit(solution)/shard_map/ppermute | solution.py:450
  68.6 0.1 plane_gather.1.half_ref
  68.7 1.5 %finish.2 = (f32[9,256,256]{2,1,0:T(8,128)}, f32[3,256,256]{2,1,0:T(8,128)}, f32[4,256,256]{2,1,0:T(8,128)}) custom-call(bf16[16,16,16,128]{3,2,1,0:T(8,128)(2,1)S(1)} %plane_gather.1.half_ref), custom_call_target="tpu_custom_call" | custom-call | bytes 5242880 | tf_op jit(solution)/shard_map/finish/pallas_call | solution.py:426
  70.2 1.2 %collective-permute-done.21.half_ref = bf16[16,16,16,128]{3,2,1,0:T(8,128)(2,1)S(1)} collective-permute-done((bf16[16,16,16,128]{3,2,1,0:T(8,128)(2,1)S(1)}, bf16[16,16,16,128]{3,2,1,0:T(8,128)(2,1)S(1)}, u32[]{:S(2)}, u32[]{:S(2)}) %collective-permute-start.21) | collective-permute-done | bytes 1048608 | tf_op jit(solution)/shard_map/ppermute | solution.py:450
  71.4 1.5 %finish.3 = (f32[9,256,256]{2,1,0:T(8,128)}, f32[3,256,256]{2,1,0:T(8,128)}, f32[4,256,256]{2,1,0:T(8,128)}) custom-call(bf16[16,16,16,128]{3,2,1,0:T(8,128)(2,1)S(1)} %collective-permute-done.21.half_ref, f32[9,256,256]{2,1,0:T(8,128)} %get-tuple-element.77.rest_0_, ...), custom_call_target="tpu_custom_call", output_to_operand_aliasing={{0}: (1, {}), {1}: (2, {}), {2}: (3, {})} | custom-call | bytes 9437184 | tf_op jit(solution)/shard_map/finish/pallas_call | solution.py:426
  (25 shorter events, 0.2 us)
Async XLA Ops:
  1.3 1.2 %copy-start.3 = (bf16[16,16,8,256]{3,2,1,0:T(8,128)(2,1)S(1)}, bf16[16,16,8,256]{3,2,1,0:T(8,128)(2,1)}, u32[]{:S(2)}) copy-start(bf16[16,16,8,256]{3,2,1,0:T(8,128)(2,1)} %param.6) | copy-start | bytes 3145732
  2.5 4.5 %copy-start.2 = (bf16[16,8,4,256]{3,2,1,0:T(4,128)(2,1)S(1)}, bf16[16,8,4,256]{3,2,1,0:T(4,128)(2,1)}, u32[]{:S(2)}) copy-start(bf16[16,8,4,256]{3,2,1,0:T(4,128)(2,1)} %cot_ref.3) | copy-start | bytes 786436
  2.8 5.5 %copy-start = (bf16[2,2,256,256]{3,2,1,0:T(8,128)(2,1)S(1)}, bf16[2,2,256,256]{3,2,1,0:T(8,128)(2,1)}, u32[]{:S(2)}) copy-start(bf16[2,2,256,256]{3,2,1,0:T(8,128)(2,1)} %param.10) | copy-start | bytes 1572868
  2.8 5.5 %copy-start.1 = (bf16[3,256,256]{2,1,0:T(8,128)(2,1)S(1)}, bf16[3,256,256]{2,1,0:T(8,128)(2,1)}, u32[]{:S(2)}) copy-start(bf16[3,256,256]{2,1,0:T(8,128)(2,1)} %wt_ref.5) | copy-start | bytes 1179652
  2.8 5.5 %collective-permute-start = (bf16[128,256]{1,0:T(8,128)(2,1)S(1)}, bf16[128,256]{1,0:T(8,128)(2,1)S(1)}, u32[]{:S(2)}, u32[]{:S(2)}) collective-permute-start(bf16[128,256]{1,0:T(8,128)(2,1)S(1)} %edges.1._), channel_id=1, source_target_pairs={{0,1},{1,0},{2,3},{3,2},{4,5},{5,4},{6,7},{7,6},{8,9},{9,8},{10,11... | collective-permute-start | bytes 196616 | tf_op jit(solution)/shard_map/ppermute | solution.py:504
  7.0 3.1 %collective-permute-start.1 = (bf16[2,8,4,256]{3,2,1,0:T(4,128)(2,1)S(1)}, bf16[2,8,4,256]{3,2,1,0:T(4,128)(2,1)S(1)}, u32[]{:S(2)}, u32[]{:S(2)}) collective-permute-start(bf16[2,8,4,256]{3,2,1,0:T(4,128)(2,1)S(1)} %next.1.rest_3_), channel_id=1, source_target_pairs={{2,0},{4,2},{6,4},{8,6},{10,8},{12,10},{14,12},{16,14},{18,16},{20... | collective-permute-start | bytes 98312 | tf_op jit(solution)/shard_map/ppermute | solution.py:494
  8.5 8.1 %collective-permute-start.3 = (bf16[288,256]{1,0:T(8,128)(2,1)S(1)}, bf16[288,256]{1,0:T(8,128)(2,1)S(1)}, u32[]{:S(2)}, u32[]{:S(2)}) collective-permute-start(bf16[288,256]{1,0:T(8,128)(2,1)S(1)} %get-tuple-element.53), channel_id=1, source_target_pairs={{0,2},{2,4},{4,6},{6,8},{8,10},{10,12},{12,14},{14,16},{16,18},{18... | collective-permute-start | bytes 442376 | tf_op jit(solution)/shard_map/ppermute | solution.py:499
  10.1 6.5 %copy-start.4 = (bf16[3,3,256,256]{3,2,1,0:T(8,128)(2,1)S(1)}, bf16[3,3,256,256]{3,2,1,0:T(8,128)(2,1)}, u32[]{:S(2)}) copy-start(bf16[3,3,256,256]{3,2,1,0:T(8,128)(2,1)} %param.8) | copy-start | bytes 3538948
  16.6 2.0 %collective-permute-start.4 = (bf16[16,9,16,128]{3,2,1,0:T(8,128)(2,1)S(1)}, bf16[16,9,16,128]{3,2,1,0:T(8,128)(2,1)S(1)}, u32[]{:S(2)}, u32[]{:S(2)}) collective-permute-start(bf16[16,9,16,128]{3,2,1,0:T(8,128)(2,1)S(1)} %pass.2._), channel_id=1, source_target_pairs={{0,2},{1,3},{2,0},{3,1},{4,6},{5,7},{6,4},{7,5},{8,10},{9,11},{10,... | collective-permute-start | bytes 1769480 | tf_op jit(solution)/shard_map/ppermute | solution.py:450
  18.8 7.0 %collective-permute-start.5 = (bf16[4,9,16,128]{3,2,1,0:T(8,128)(2,1)S(1)}, bf16[4,9,16,128]{3,2,1,0:T(8,128)(2,1)S(1)}, u32[]{:S(2)}, u32[]{:S(2)}) collective-permute-start(bf16[4,9,16,128]{3,2,1,0:T(8,128)(2,1)S(1)} %get-tuple-element.59.rest_1_), channel_id=1, source_target_pairs={{0,5},{1,4},{2,7},{3,6},{4,1},{5,0},{6,3},{7,2},{8,13},{9,12},{10,... | collective-permute-start | bytes 442376 | tf_op jit(solution)/shard_map/ppermute | solution.py:450
  25.7 1.9 %collective-permute-start.8 = (bf16[16,7,16,128]{3,2,1,0:T(8,128)(2,1)S(1)}, bf16[16,7,16,128]{3,2,1,0:T(8,128)(2,1)S(1)}, u32[]{:S(2)}, u32[]{:S(2)}) collective-permute-start(bf16[16,7,16,128]{3,2,1,0:T(8,128)(2,1)S(1)} %pass.3), channel_id=1, source_target_pairs={{0,2},{1,3},{2,0},{3,1},{4,6},{5,7},{6,4},{7,5},{8,10},{9,11},{10,... | collective-permute-start | bytes 1376264 | tf_op jit(solution)/shard_map/ppermute | solution.py:450
  25.7 6.5 %collective-permute-start.6 = (bf16[4,9,16,128]{3,2,1,0:T(8,128)(2,1)S(1)}, bf16[4,9,16,128]{3,2,1,0:T(8,128)(2,1)S(1)}, u32[]{:S(2)}, u32[]{:S(2)}) collective-permute-start(bf16[4,9,16,128]{3,2,1,0:T(8,128)(2,1)S(1)} %get-tuple-element.60.rest_2_), channel_id=1, source_target_pairs={{0,1},{1,0},{2,3},{3,2},{4,5},{5,4},{6,7},{7,6},{8,9},{9,8},{10,11... | collective-permute-start | bytes 442376 | tf_op jit(solution)/shard_map/ppermute | solution.py:450
  26.7 6.7 %collective-permute-start.7 = (bf16[4,9,16,128]{3,2,1,0:T(8,128)(2,1)S(1)}, bf16[4,9,16,128]{3,2,1,0:T(8,128)(2,1)S(1)}, u32[]{:S(2)}, u32[]{:S(2)}) collective-permute-start(bf16[4,9,16,128]{3,2,1,0:T(8,128)(2,1)S(1)} %get-tuple-element.61.rest_3_), channel_id=1, source_target_pairs={{0,4},{1,5},{2,6},{3,7},{4,0},{5,1},{6,2},{7,3},{8,12},{9,13},{10,... | collective-permute-start | bytes 442376 | tf_op jit(solution)/shard_map/ppermute | solution.py:450
  27.7 8.6 %collective-permute-start.9 = (bf16[4,7,16,128]{3,2,1,0:T(8,128)(2,1)S(1)}, bf16[4,7,16,128]{3,2,1,0:T(8,128)(2,1)S(1)}, u32[]{:S(2)}, u32[]{:S(2)}) collective-permute-start(bf16[4,7,16,128]{3,2,1,0:T(8,128)(2,1)S(1)} %get-tuple-element.67), channel_id=1, source_target_pairs={{0,5},{1,4},{2,7},{3,6},{4,1},{5,0},{6,3},{7,2},{8,13},{9,12},{10,... | collective-permute-start | bytes 344072 | tf_op jit(solution)/shard_map/ppermute | solution.py:450
  29.4 7.5 %collective-permute-start.10 = (bf16[4,7,16,128]{3,2,1,0:T(8,128)(2,1)S(1)}, bf16[4,7,16,128]{3,2,1,0:T(8,128)(2,1)S(1)}, u32[]{:S(2)}, u32[]{:S(2)}) collective-permute-start(bf16[4,7,16,128]{3,2,1,0:T(8,128)(2,1)S(1)} %get-tuple-element.68), channel_id=1, source_target_pairs={{0,1},{1,0},{2,3},{3,2},{4,5},{5,4},{6,7},{7,6},{8,9},{9,8},{10,11... | collective-permute-start | bytes 344072 | tf_op jit(solution)/shard_map/ppermute | solution.py:450
  30.7 7.0 %collective-permute-start.11 = (bf16[4,7,16,128]{3,2,1,0:T(8,128)(2,1)S(1)}, bf16[4,7,16,128]{3,2,1,0:T(8,128)(2,1)S(1)}, u32[]{:S(2)}, u32[]{:S(2)}) collective-permute-start(bf16[4,7,16,128]{3,2,1,0:T(8,128)(2,1)S(1)} %get-tuple-element.69), channel_id=1, source_target_pairs={{0,4},{1,5},{2,6},{3,7},{4,0},{5,1},{6,2},{7,3},{8,12},{9,13},{10,... | collective-permute-start | bytes 344072 | tf_op jit(solution)/shard_map/ppermute | solution.py:450
  37.8 6.2 %collective-permute-start.12 = (bf16[16,16,128]{2,1,0:T(8,128)(2,1)S(1)}, bf16[16,16,128]{2,1,0:T(8,128)(2,1)S(1)}, u32[]{:S(2)}, u32[]{:S(2)}) collective-permute-start(bf16[16,16,128]{2,1,0:T(8,128)(2,1)S(1)} %get-tuple-element.71), channel_id=1, source_target_pairs={{0,24},{1,25},{2,26},{3,27},{4,28},{5,29},{6,30},{7,31},{8,16},{9,... | collective-permute-start | bytes 196616 | tf_op jit(solution)/shard_map/ppermute | solution.py:450
  40.3 6.3 %collective-permute-start.13 = (bf16[16,16,128]{2,1,0:T(8,128)(2,1)S(1)}, bf16[16,16,128]{2,1,0:T(8,128)(2,1)S(1)}, u32[]{:S(2)}, u32[]{:S(2)}) collective-permute-start(bf16[16,16,128]{2,1,0:T(8,128)(2,1)S(1)} %get-tuple-element.72), channel_id=1, source_target_pairs={{0,16},{1,17},{2,18},{3,19},{4,20},{5,21},{6,22},{7,23},{8,24},{9,... | collective-permute-start | bytes 196616 | tf_op jit(solution)/shard_map/ppermute | solution.py:450
  40.3 6.3 %collective-permute-start.14 = (bf16[16,16,128]{2,1,0:T(8,128)(2,1)S(1)}, bf16[16,16,128]{2,1,0:T(8,128)(2,1)S(1)}, u32[]{:S(2)}, u32[]{:S(2)}) collective-permute-start(bf16[16,16,128]{2,1,0:T(8,128)(2,1)S(1)} %get-tuple-element.73), channel_id=1, source_target_pairs={{0,8},{1,9},{2,10},{3,11},{4,12},{5,13},{6,14},{7,15},{8,0},{9,1},... | collective-permute-start | bytes 196616 | tf_op jit(solution)/shard_map/ppermute | solution.py:450
  46.6 5.6 %collective-permute-start.17 = (bf16[16,16,128]{2,1,0:T(8,128)(2,1)S(1)}, bf16[16,16,128]{2,1,0:T(8,128)(2,1)S(1)}, u32[]{:S(2)}, u32[]{:S(2)}) collective-permute-start(bf16[16,16,128]{2,1,0:T(8,128)(2,1)S(1)} %line_sum.1.a_ref), channel_id=1, source_target_pairs={{0,8},{1,9},{2,10},{3,11},{4,12},{5,13},{6,14},{7,15},{8,0},{9,1},... | collective-permute-start | bytes 196616 | tf_op jit(solution)/shard_map/ppermute | solution.py:450
  46.7 7.5 %collective-permute-start.16 = (bf16[16,16,128]{2,1,0:T(8,128)(2,1)S(1)}, bf16[16,16,128]{2,1,0:T(8,128)(2,1)S(1)}, u32[]{:S(2)}, u32[]{:S(2)}) collective-permute-start(bf16[16,16,128]{2,1,0:T(8,128)(2,1)S(1)} %line_sum.1.a_ref), channel_id=1, source_target_pairs={{0,16},{1,17},{2,18},{3,19},{4,20},{5,21},{6,22},{7,23},{8,24},{9,... | collective-permute-start | bytes 196616 | tf_op jit(solution)/shard_map/ppermute | solution.py:450
  49.7 6.1 %collective-permute-start.15 = (bf16[16,16,128]{2,1,0:T(8,128)(2,1)S(1)}, bf16[16,16,128]{2,1,0:T(8,128)(2,1)S(1)}, u32[]{:S(2)}, u32[]{:S(2)}) collective-permute-start(bf16[16,16,128]{2,1,0:T(8,128)(2,1)S(1)} %line_sum.1.a_ref), channel_id=1, source_target_pairs={{0,24},{1,25},{2,26},{3,27},{4,28},{5,29},{6,30},{7,31},{8,16},{9,... | collective-permute-start | bytes 196616 | tf_op jit(solution)/shard_map/ppermute | solution.py:450
  51.1 8.3 %collective-permute-start.2 = (bf16[64,256]{1,0:T(8,128)(2,1)S(1)}, bf16[64,256]{1,0:T(8,128)(2,1)S(1)}, u32[]{:S(2)}, u32[]{:S(2)}) collective-permute-start(bf16[64,256]{1,0:T(8,128)(2,1)S(1)} %get-tuple-element.51), channel_id=1, source_target_pairs={{0,1},{1,0},{2,3},{3,2},{4,5},{5,4},{6,7},{7,6},{8,9},{9,8},{10,11... | collective-permute-start | bytes 98312 | tf_op jit(solution)/shard_map/ppermute | solution.py:504
  55.8 11.0 %collective-permute-start.20 = (bf16[4,16,16,128]{3,2,1,0:T(8,128)(2,1)S(1)}, bf16[4,16,16,128]{3,2,1,0:T(8,128)(2,1)S(1)}, u32[]{:S(2)}, u32[]{:S(2)}) collective-permute-start(bf16[4,16,16,128]{3,2,1,0:T(8,128)(2,1)S(1)} %line_gather.1.rest_0_.a_ref), channel_id=1, source_target_pairs={{0,4},{1,5},{2,6},{3,7},{4,0},{5,1},{6,2},{7,3},{8,12},{9,13},{10,... | collective-permute-start | bytes 786440 | tf_op jit(solution)/shard_map/ppermute | solution.py:450
  56.8 11.8 %collective-permute-start.19 = (bf16[4,16,16,128]{3,2,1,0:T(8,128)(2,1)S(1)}, bf16[4,16,16,128]{3,2,1,0:T(8,128)(2,1)S(1)}, u32[]{:S(2)}, u32[]{:S(2)}) collective-permute-start(bf16[4,16,16,128]{3,2,1,0:T(8,128)(2,1)S(1)} %line_gather.1.rest_0_.a_ref), channel_id=1, source_target_pairs={{0,1},{1,0},{2,3},{3,2},{4,5},{5,4},{6,7},{7,6},{8,9},{9,8},{10,11... | collective-permute-start | bytes 786440 | tf_op jit(solution)/shard_map/ppermute | solution.py:450
  58.3 10.2 %collective-permute-start.18 = (bf16[4,16,16,128]{3,2,1,0:T(8,128)(2,1)S(1)}, bf16[4,16,16,128]{3,2,1,0:T(8,128)(2,1)S(1)}, u32[]{:S(2)}, u32[]{:S(2)}) collective-permute-start(bf16[4,16,16,128]{3,2,1,0:T(8,128)(2,1)S(1)} %line_gather.1.rest_0_.a_ref), channel_id=1, source_target_pairs={{0,5},{1,4},{2,7},{3,6},{4,1},{5,0},{6,3},{7,2},{8,13},{9,12},{10,... | collective-permute-start | bytes 786440 | tf_op jit(solution)/shard_map/ppermute | solution.py:450
  68.7 2.7 %collective-permute-start.21 = (bf16[16,16,16,128]{3,2,1,0:T(8,128)(2,1)S(1)}, bf16[16,16,16,128]{3,2,1,0:T(8,128)(2,1)S(1)}, u32[]{:S(2)}, u32[]{:S(2)}) collective-permute-start(bf16[16,16,16,128]{3,2,1,0:T(8,128)(2,1)S(1)} %plane_gather.1.half_ref), channel_id=1, source_target_pairs={{0,2},{1,3},{2,0},{3,1},{4,6},{5,7},{6,4},{7,5},{8,10},{9,11},{10,... | collective-permute-start | bytes 3145736 | tf_op jit(solution)/shard_map/ppermute | solution.py:450

commit v27 on v25

--- a/solution.py
+++ b/solution.py
@@ -213,9 +213,11 @@
         halves.append(mm(place_next, piece).astype(BF))
     placed = jnp.concatenate(halves, 0)
     cott_ref[...] = placed.reshape(rows // 2, cols // 2, SLOTS, CH)
+    all_four = mm_nt(placed, wd_ref[...].reshape(4 * CH, CH)).astype(BF)
     for i in range(2):
         for j in range(2):
-            g = mm_nt(placed, wd_ref[i * 2 + j]).astype(BF).reshape(rows // 2, cols // 2, SLOTS, CH)
+            at = (i * 2 + j) * CH
+            g = all_four[:, at : at + CH].reshape(rows // 2, cols // 2, SLOTS, CH)
             for r in range(rows // 2):
                 for c in range(cols // 2):
                     gy_ref[2 * r + i, 2 * c + j] = g[r, c]

time: 73 us -> 73 us (level)
  no operation moved by 1% of the time
where the time goes in v27:
time: 73 us; the launch traced here: 72.9 us
  starting transfers between devices  26 us (36%)
  waiting for transfers between devices  22.3 us (31%)
  Pallas kernels  21.9 us (30%)
  between operations  1.48 us (2%)
  local copies, waits for them, and re-layouts  1.24 us (2%)
    pallas_call x19, Pallas kernels, call(): pl.pallas_call(kernel, out_shape=shapes, in_specs=[s for s, _ in ins], ou...  21.9 us
    ppermute x18, starting transfers between devices, swap(): return lax.ppermute(value, AXES, [(d, d ^ flip) for d in range(tm * grp)])  19.4 us
    ppermute x18, waiting for transfers between devices, swap(): return lax.ppermute(value, AXES, [(d, d ^ flip) for d in range(tm * grp)])  19.3 us
    ppermute x2, starting transfers between devices, from_bands(): got = lax.ppermute(parts[0], 'grp', [(0, 1), (1, 0)])  4.17 us
    ppermute x1, waiting for transfers between devices, around(): lax.ppermute(value, axis, [(i, (i + by) % count) for i in range(count)])  2.52 us
  transfers between devices with their start and end apart: 22, of which 15 were waited for; matrix products, arithmetic and copies ran while one was open for 0% of the time, Pallas kernels for 27%

profile of v27, /device:TPU:0, one launch (start us, length us, event | category | flops | bytes accessed | tf_op | source)
XLA Modules:
  0.0 72.9 jit_solution(17939198432472709071)
XLA Ops:
  1.3 1.2 %copy-done.3 = bf16[16,16,8,256]{3,2,1,0:T(8,128)(2,1)S(1)} copy-done((bf16[16,16,8,256]{3,2,1,0:T(8,128)(2,1)S(1)}, bf16[16,16,8,256]{3,2,1,0:T(8,128)(2,1)}, u32[]{:S(2)}) %copy-start.3) | copy-done | bytes 1048600
  2.5 0.3 edges.1._
  2.8 3.0 %collective-permute-start = (bf16[128,256]{1,0:T(8,128)(2,1)S(1)}, bf16[128,256]{1,0:T(8,128)(2,1)S(1)}, u32[]{:S(2)}, u32[]{:S(2)}) collective-permute-start(bf16[128,256]{1,0:T(8,128)(2,1)S(1)} %edges.1._), channel_id=1, source_target_pairs={{0,1},{1,0},{2,3},{3,2},{4,5},{5,4},{6,7},{7,6},{8,9},{9,8},{10,11... | collective-permute-start | bytes 196616 | tf_op jit(solution)/shard_map/ppermute | solution.py:506
  5.9 1.1 %acts.1 = (bf16[16,8,16,256]{3,2,1,0:T(8,128)(2,1)S(1)}, bf16[18,10,16,256]{3,2,1,0:T(8,128)(2,1)S(1)}, bf16[768,2560]{1,0:T(8,128)(2,1)S(1)}, bf16[288,256]{1,0:T(8,128)(2,1)S(1)}) custom-call(s32[1]{0:T(128)S(6)} %copy.29.count_ref, bf16[16,128,256]{2,1,0:T(8,128)(2,1)S(1)} %bitcast.11, bf16[128,256]{1,0:T(8,128)(2,1)S(1)} %edges.1._), custom_call_target="tpu_custom_call" | custom-call | flops 536870912 | bytes 7651332 | tf_op jit(solution)/shard_map/acts/pallas_call | solution.py:428
  7.0 1.3 %collective-permute-start.1 = (bf16[2,8,4,256]{3,2,1,0:T(4,128)(2,1)S(1)}, bf16[2,8,4,256]{3,2,1,0:T(4,128)(2,1)S(1)}, u32[]{:S(2)}, u32[]{:S(2)}) collective-permute-start(bf16[2,8,4,256]{3,2,1,0:T(4,128)(2,1)S(1)} %next.1.rest_3_), channel_id=1, source_target_pairs={{2,0},{4,2},{6,4},{8,6},{10,8},{12,10},{14,12},{16,14},{18,16},{20... | collective-permute-start | bytes 98312 | tf_op jit(solution)/shard_map/ppermute | solution.py:496
  8.4 0.2 halo.1
  8.5 1.1 %collective-permute-start.3 = (bf16[288,256]{1,0:T(8,128)(2,1)S(1)}, bf16[288,256]{1,0:T(8,128)(2,1)S(1)}, u32[]{:S(2)}, u32[]{:S(2)}) collective-permute-start(bf16[288,256]{1,0:T(8,128)(2,1)S(1)} %get-tuple-element.53), channel_id=1, source_target_pairs={{0,2},{2,4},{4,6},{6,8},{8,10},{10,12},{12,14},{14,16},{16,18},{18... | collective-permute-start | bytes 442376 | tf_op jit(solution)/shard_map/ppermute | solution.py:501
  9.7 0.5 collective-permute-done.1.nxt_ref
  10.1 3.9 %grad_spatial.1 = (bf16[8,4,16,256]{3,2,1,0:T(8,128)(2,1)S(1)}, bf16[16,8,16,256]{3,2,1,0:T(8,128)(2,1)S(1)}, bf16[16,10,16,256]{3,2,1,0:T(8,128)(2,1)S(1)}, bf1...) custom-call(s32[1]{0:T(128)S(6)} %copy.29.count_ref, ...), custom_call_target="tpu_custom_call" | custom-call | flops 3758096384 | bytes 8978436 | tf_op jit(solution)/shard_map/grad_spatial/pallas_call | solution.py:428
  14.1 2.5 %collective-permute-done.3.__1_.prev_ref = bf16[288,256]{1,0:T(8,128)(2,1)S(1)} collective-permute-done((bf16[288,256]{1,0:T(8,128)(2,1)S(1)}, bf16[288,256]{1,0:T(8,128)(2,1)S(1)}, u32[]{:S(2)}, u32[]{:S(2)}) %collective-permute-start.3) | collective-permute-done | bytes 147488 | tf_op jit(solution)/shard_map/ppermute | solution.py:501
  16.6 1.7 %spatial_upper.1 = (bf16[18,10,16,256]{3,2,1,0:T(8,128)(2,1)S(1)}, bf16[8,8,16,256]{3,2,1,0:T(8,128)(2,1)S(1)}) custom-call(bf16[18,10,16,256]{3,2,1,0:T(8,128)(2,1)S(1)} %get-tuple-element.52.acts_in, bf16[288,256]{1,0:T(8,128)(2,1)S(1)} %collective-permute-done.3.__1_.prev_ref, bf16[9,256,256]{2,1,0:T(8,128)(2,1)S(1)} %bitcast.12, ...), custom_call_target="tpu_custom_call", output_to_operand_aliasing={{0}: (0, {})} | custom-call | flops 1342177280 | bytes 4800512 | tf_op jit(solution)/shard_map/spatial_upper/pallas_call | solution.py:428
  18.4 0.3 collective-permute-done.4.got_ref
  18.6 0.1 plane_send.2
  18.8 1.4 %collective-permute-start.5 = (bf16[4,9,16,128]{3,2,1,0:T(8,128)(2,1)S(1)}, bf16[4,9,16,128]{3,2,1,0:T(8,128)(2,1)S(1)}, u32[]{:S(2)}, u32[]{:S(2)}) collective-permute-start(bf16[4,9,16,128]{3,2,1,0:T(8,128)(2,1)S(1)} %get-tuple-element.59.rest_1_), channel_id=1, source_target_pairs={{0,5},{1,4},{2,7},{3,6},{4,1},{5,0},{6,3},{7,2},{8,13},{9,12},{10,... | collective-permute-start | bytes 442376 | tf_op jit(solution)/shard_map/ppermute | solution.py:452
  20.2 1.4 %spatial_lower.1.lower_ref = bf16[8,8,16,256]{3,2,1,0:T(8,128)(2,1)S(1)} custom-call(bf16[18,10,16,256]{3,2,1,0:T(8,128)(2,1)S(1)} %get-tuple-element.56.acts_ref, bf16[9,256,256]{2,1,0:T(8,128)(2,1)S(1)} %bitcast.13, bf16[4,9,16,128]{3,2,1,0:T(8,128)(2,1)S(1)} %get-tuple-element.58.rest_0_.refs_0_, bf16[4,9,16,128]{3,2,1,0:T(8,128)(2,1)S(1)} %get-tuple-element.59.rest_1_, ...), custom_call_target="tpu_custom_call" | custom-call | flops 1073741824 | bytes 3178496 | tf_op jit(solution)/shard_map/spatial_lower/pallas_call | solution.py:428
  21.5 2.4 %forward.1 = (bf16[512,256]{1,0:T(8,128)(2,1)S(1)}, bf16[16,7,16,128]{3,2,1,0:T(8,128)(2,1)S(1)}, bf16[16,7,16,128]{3,2,1,0:T(8,128)(2,1)S(1)}) custom-call(s32[1]{0:T(128)S(6)} %copy.29.count_ref, bf16[16,8,16,256]{3,2,1,0:T(8,128)(2,1)S(1)} %get-tuple-element.44.xt_ref, bf16[8,8,16,256]{3,2,1,0:T(8,128)(2,1)S(1)} %get-tuple-element.55.rest_0_.upper_ref, ...), custom_call_target="tpu_custom_call" | custom-call | bytes 1024 | tf_op jit(solution)/shard_map/forward/pallas_call | solution.py:428
  23.9 1.8 %collective-permute-done.5.__1_.refs_1_ = bf16[4,9,16,128]{3,2,1,0:T(8,128)(2,1)S(1)} collective-permute-done((bf16[4,9,16,128]{3,2,1,0:T(8,128)(2,1)S(1)}, bf16[4,9,16,128]{3,2,1,0:T(8,128)(2,1)S(1)}, u32[]{:S(2)}, u32[]{:S(2)}) %collective-permute-start.5) | collective-permute-done | bytes 147488 | tf_op jit(solution)/shard_map/ppermute | solution.py:452
  25.7 0.9 %collective-permute-start.6 = (bf16[4,9,16,128]{3,2,1,0:T(8,128)(2,1)S(1)}, bf16[4,9,16,128]{3,2,1,0:T(8,128)(2,1)S(1)}, u32[]{:S(2)}, u32[]{:S(2)}) collective-permute-start(bf16[4,9,16,128]{3,2,1,0:T(8,128)(2,1)S(1)} %get-tuple-element.60.rest_2_), channel_id=1, source_target_pairs={{0,1},{1,0},{2,3},{3,2},{4,5},{5,4},{6,7},{7,6},{8,9},{9,8},{10,11... | collective-permute-start | bytes 442376 | tf_op jit(solution)/shard_map/ppermute | solution.py:452
  26.7 0.9 %collective-permute-start.7 = (bf16[4,9,16,128]{3,2,1,0:T(8,128)(2,1)S(1)}, bf16[4,9,16,128]{3,2,1,0:T(8,128)(2,1)S(1)}, u32[]{:S(2)}, u32[]{:S(2)}) collective-permute-start(bf16[4,9,16,128]{3,2,1,0:T(8,128)(2,1)S(1)} %get-tuple-element.61.rest_3_), channel_id=1, source_target_pairs={{0,4},{1,5},{2,6},{3,7},{4,0},{5,1},{6,2},{7,3},{8,12},{9,13},{10,... | collective-permute-start | bytes 442376 | tf_op jit(solution)/shard_map/ppermute | solution.py:452
  27.6 0.1 plane_send.3
  27.7 1.7 %collective-permute-start.9 = (bf16[4,7,16,128]{3,2,1,0:T(8,128)(2,1)S(1)}, bf16[4,7,16,128]{3,2,1,0:T(8,128)(2,1)S(1)}, u32[]{:S(2)}, u32[]{:S(2)}) collective-permute-start(bf16[4,7,16,128]{3,2,1,0:T(8,128)(2,1)S(1)} %get-tuple-element.67), channel_id=1, source_target_pairs={{0,5},{1,4},{2,7},{3,6},{4,1},{5,0},{6,3},{7,2},{8,13},{9,12},{10,... | collective-permute-start | bytes 344072 | tf_op jit(solution)/shard_map/ppermute | solution.py:452
  29.4 1.3 %collective-permute-start.10 = (bf16[4,7,16,128]{3,2,1,0:T(8,128)(2,1)S(1)}, bf16[4,7,16,128]{3,2,1,0:T(8,128)(2,1)S(1)}, u32[]{:S(2)}, u32[]{:S(2)}) collective-permute-start(bf16[4,7,16,128]{3,2,1,0:T(8,128)(2,1)S(1)} %get-tuple-element.68), channel_id=1, source_target_pairs={{0,1},{1,0},{2,3},{3,2},{4,5},{5,4},{6,7},{7,6},{8,9},{9,8},{10,11... | collective-permute-start | bytes 344072 | tf_op jit(solution)/shard_map/ppermute | solution.py:452
  30.7 0.6 collective-permute-start.11
  31.3 1.0 %collective-permute-done.6.refs_2_ = bf16[4,9,16,128]{3,2,1,0:T(8,128)(2,1)S(1)} collective-permute-done((bf16[4,9,16,128]{3,2,1,0:T(8,128)(2,1)S(1)}, bf16[4,9,16,128]{3,2,1,0:T(8,128)(2,1)S(1)}, u32[]{:S(2)}, u32[]{:S(2)}) %collective-permute-start.6) | collective-permute-done | bytes 147488 | tf_op jit(solution)/shard_map/ppermute | solution.py:452
  32.3 1.1 %collective-permute-done.7.refs_3_ = bf16[4,9,16,128]{3,2,1,0:T(8,128)(2,1)S(1)} collective-permute-done((bf16[4,9,16,128]{3,2,1,0:T(8,128)(2,1)S(1)}, bf16[4,9,16,128]{3,2,1,0:T(8,128)(2,1)S(1)}, u32[]{:S(2)}, u32[]{:S(2)}) %collective-permute-start.7) | collective-permute-done | bytes 147488 | tf_op jit(solution)/shard_map/ppermute | solution.py:452
  33.4 3.0 %collective-permute-done.9.refs_5_ = bf16[4,7,16,128]{3,2,1,0:T(8,128)(2,1)S(1)} collective-permute-done((bf16[4,7,16,128]{3,2,1,0:T(8,128)(2,1)S(1)}, bf16[4,7,16,128]{3,2,1,0:T(8,128)(2,1)S(1)}, u32[]{:S(2)}, u32[]{:S(2)}) %collective-permute-start.9) | collective-permute-done | bytes 114720 | tf_op jit(solution)/shard_map/ppermute | solution.py:452
  36.4 0.5 collective-permute-done.10.refs_6_
  36.9 0.7 collective-permute-done.11.refs_7_
  37.6 0.1 line_send.1
  37.8 2.5 %collective-permute-start.12 = (bf16[16,16,128]{2,1,0:T(8,128)(2,1)S(1)}, bf16[16,16,128]{2,1,0:T(8,128)(2,1)S(1)}, u32[]{:S(2)}, u32[]{:S(2)}) collective-permute-start(bf16[16,16,128]{2,1,0:T(8,128)(2,1)S(1)} %get-tuple-element.71), channel_id=1, source_target_pairs={{0,24},{1,25},{2,26},{3,27},{4,28},{5,29},{6,30},{7,31},{8,16},{9,... | collective-permute-start | bytes 196616 | tf_op jit(solution)/shard_map/ppermute | solution.py:452
  40.3 1.9 %collective-permute-start.14 = (bf16[16,16,128]{2,1,0:T(8,128)(2,1)S(1)}, bf16[16,16,128]{2,1,0:T(8,128)(2,1)S(1)}, u32[]{:S(2)}, u32[]{:S(2)}) collective-permute-start(bf16[16,16,128]{2,1,0:T(8,128)(2,1)S(1)} %get-tuple-element.73), channel_id=1, source_target_pairs={{0,8},{1,9},{2,10},{3,11},{4,12},{5,13},{6,14},{7,15},{8,0},{9,1},... | collective-permute-start | bytes 196616 | tf_op jit(solution)/shard_map/ppermute | solution.py:452
  42.2 1.8 %collective-permute-done.12.b_ref = bf16[16,16,128]{2,1,0:T(8,128)(2,1)S(1)} collective-permute-done((bf16[16,16,128]{2,1,0:T(8,128)(2,1)S(1)}, bf16[16,16,128]{2,1,0:T(8,128)(2,1)S(1)}, u32[]{:S(2)}, u32[]{:S(2)}) %collective-permute-start.12) | collective-permute-done | bytes 65568 | tf_op jit(solution)/shard_map/ppermute | solution.py:452
  44.0 2.6 %collective-permute-done.13.c_ref = bf16[16,16,128]{2,1,0:T(8,128)(2,1)S(1)} collective-permute-done((bf16[16,16,128]{2,1,0:T(8,128)(2,1)S(1)}, bf16[16,16,128]{2,1,0:T(8,128)(2,1)S(1)}, u32[]{:S(2)}, u32[]{:S(2)}) %collective-permute-start.13) | collective-permute-done | bytes 65568 | tf_op jit(solution)/shard_map/ppermute | solution.py:452
  46.6 0.1 collective-permute-start.17
  46.7 3.0 %collective-permute-start.16 = (bf16[16,16,128]{2,1,0:T(8,128)(2,1)S(1)}, bf16[16,16,128]{2,1,0:T(8,128)(2,1)S(1)}, u32[]{:S(2)}, u32[]{:S(2)}) collective-permute-start(bf16[16,16,128]{2,1,0:T(8,128)(2,1)S(1)} %line_sum.1.a_ref), channel_id=1, source_target_pairs={{0,16},{1,17},{2,18},{3,19},{4,20},{5,21},{6,22},{7,23},{8,24},{9,... | collective-permute-start | bytes 196616 | tf_op jit(solution)/shard_map/ppermute | solution.py:452
  49.7 1.4 %collective-permute-start.15 = (bf16[16,16,128]{2,1,0:T(8,128)(2,1)S(1)}, bf16[16,16,128]{2,1,0:T(8,128)(2,1)S(1)}, u32[]{:S(2)}, u32[]{:S(2)}) collective-permute-start(bf16[16,16,128]{2,1,0:T(8,128)(2,1)S(1)} %line_sum.1.a_ref), channel_id=1, source_target_pairs={{0,24},{1,25},{2,26},{3,27},{4,28},{5,29},{6,30},{7,31},{8,16},{9,... | collective-permute-start | bytes 196616 | tf_op jit(solution)/shard_map/ppermute | solution.py:452
  51.1 1.1 %collective-permute-start.2 = (bf16[64,256]{1,0:T(8,128)(2,1)S(1)}, bf16[64,256]{1,0:T(8,128)(2,1)S(1)}, u32[]{:S(2)}, u32[]{:S(2)}) collective-permute-start(bf16[64,256]{1,0:T(8,128)(2,1)S(1)} %get-tuple-element.51), channel_id=1, source_target_pairs={{0,1},{1,0},{2,3},{3,2},{4,5},{5,4},{6,7},{7,6},{8,9},{9,8},{10,11... | collective-permute-start | bytes 98312 | tf_op jit(solution)/shard_map/ppermute | solution.py:506
  52.2 1.9 %collective-permute-done.16.c_ref = bf16[16,16,128]{2,1,0:T(8,128)(2,1)S(1)} collective-permute-done((bf16[16,16,128]{2,1,0:T(8,128)(2,1)S(1)}, bf16[16,16,128]{2,1,0:T(8,128)(2,1)S(1)}, u32[]{:S(2)}, u32[]{:S(2)}) %collective-permute-start.16) | collective-permute-done | bytes 65568 | tf_op jit(solution)/shard_map/ppermute | solution.py:452
  54.1 1.6 %collective-permute-done.15.b_ref = bf16[16,16,128]{2,1,0:T(8,128)(2,1)S(1)} collective-permute-done((bf16[16,16,128]{2,1,0:T(8,128)(2,1)S(1)}, bf16[16,16,128]{2,1,0:T(8,128)(2,1)S(1)}, u32[]{:S(2)}, u32[]{:S(2)}) %collective-permute-start.15) | collective-permute-done | bytes 65568 | tf_op jit(solution)/shard_map/ppermute | solution.py:452
  55.8 1.0 %collective-permute-start.20 = (bf16[4,16,16,128]{3,2,1,0:T(8,128)(2,1)S(1)}, bf16[4,16,16,128]{3,2,1,0:T(8,128)(2,1)S(1)}, u32[]{:S(2)}, u32[]{:S(2)}) collective-permute-start(bf16[4,16,16,128]{3,2,1,0:T(8,128)(2,1)S(1)} %line_gather.1.rest_0_.a_ref), channel_id=1, source_target_pairs={{0,4},{1,5},{2,6},{3,7},{4,0},{5,1},{6,2},{7,3},{8,12},{9,13},{10,... | collective-permute-start | bytes 786440 | tf_op jit(solution)/shard_map/ppermute | solution.py:452
  56.8 1.5 %collective-permute-start.19 = (bf16[4,16,16,128]{3,2,1,0:T(8,128)(2,1)S(1)}, bf16[4,16,16,128]{3,2,1,0:T(8,128)(2,1)S(1)}, u32[]{:S(2)}, u32[]{:S(2)}) collective-permute-start(bf16[4,16,16,128]{3,2,1,0:T(8,128)(2,1)S(1)} %line_gather.1.rest_0_.a_ref), channel_id=1, source_target_pairs={{0,1},{1,0},{2,3},{3,2},{4,5},{5,4},{6,7},{7,6},{8,9},{9,8},{10,11... | collective-permute-start | bytes 786440 | tf_op jit(solution)/shard_map/ppermute | solution.py:452
  58.3 1.0 %collective-permute-start.18 = (bf16[4,16,16,128]{3,2,1,0:T(8,128)(2,1)S(1)}, bf16[4,16,16,128]{3,2,1,0:T(8,128)(2,1)S(1)}, u32[]{:S(2)}, u32[]{:S(2)}) collective-permute-start(bf16[4,16,16,128]{3,2,1,0:T(8,128)(2,1)S(1)} %line_gather.1.rest_0_.a_ref), channel_id=1, source_target_pairs={{0,5},{1,4},{2,7},{3,6},{4,1},{5,0},{6,3},{7,2},{8,13},{9,12},{10,... | collective-permute-start | bytes 786440 | tf_op jit(solution)/shard_map/ppermute | solution.py:452
  59.3 7.5 %grad_x.1 = (bf16[16,128,256]{2,1,0:T(8,128)(2,1)}, bf16[16,8,4,256]{3,2,1,0:T(4,128)(2,1)}, f32[8,128]{1,0:T(8,128)S(1)}) custom-call(s32[1]{0:T(128)S(6)} %copy.29.count_ref, bf16[16,8,16,256]{3,2,1,0:T(8,128)(2,1)S(1)} %get-tuple-element.44.xt_ref, bf16[16,8,16,256]{3,2,1,0:T(8,128)(2,1)S(1)} %get-tuple-element.49.gy_ref, ...), custom_call_target="tpu_custom_call" | custom-call | flops 2684354560 | bytes 7147524 | tf_op jit(solution)/shard_map/grad_x/pallas_call | solution.py:428
  66.8 1.8 %collective-permute-done.19.c_ref = bf16[4,16,16,128]{3,2,1,0:T(8,128)(2,1)S(1)} collective-permute-done((bf16[4,16,16,128]{3,2,1,0:T(8,128)(2,1)S(1)}, bf16[4,16,16,128]{3,2,1,0:T(8,128)(2,1)S(1)}, u32[]{:S(2)}, u32[]{:S(2)}) %collective-permute-start.19) | collective-permute-done | bytes 262176 | tf_op jit(solution)/shard_map/ppermute | solution.py:452
  68.6 0.1 plane_gather.1.half_ref
  68.7 1.5 %finish.2 = (f32[9,256,256]{2,1,0:T(8,128)}, f32[3,256,256]{2,1,0:T(8,128)}, f32[4,256,256]{2,1,0:T(8,128)}) custom-call(bf16[16,16,16,128]{3,2,1,0:T(8,128)(2,1)S(1)} %plane_gather.1.half_ref), custom_call_target="tpu_custom_call" | custom-call | bytes 5242880 | tf_op jit(solution)/shard_map/finish/pallas_call | solution.py:428
  70.2 1.2 %collective-permute-done.21.half_ref = bf16[16,16,16,128]{3,2,1,0:T(8,128)(2,1)S(1)} collective-permute-done((bf16[16,16,16,128]{3,2,1,0:T(8,128)(2,1)S(1)}, bf16[16,16,16,128]{3,2,1,0:T(8,128)(2,1)S(1)}, u32[]{:S(2)}, u32[]{:S(2)}) %collective-permute-start.21) | collective-permute-done | bytes 1048608 | tf_op jit(solution)/shard_map/ppermute | solution.py:452
  71.4 1.5 %finish.3 = (f32[9,256,256]{2,1,0:T(8,128)}, f32[3,256,256]{2,1,0:T(8,128)}, f32[4,256,256]{2,1,0:T(8,128)}) custom-call(bf16[16,16,16,128]{3,2,1,0:T(8,128)(2,1)S(1)} %collective-permute-done.21.half_ref, f32[9,256,256]{2,1,0:T(8,128)} %get-tuple-element.77.rest_0_, ...), custom_call_target="tpu_custom_call", output_to_operand_aliasing={{0}: (1, {}), {1}: (2, {}), {2}: (3, {})} | custom-call | bytes 9437184 | tf_op jit(solution)/shard_map/finish/pallas_call | solution.py:428
  (25 shorter events, 0.2 us)
Async XLA Ops:
  1.3 1.2 %copy-start.3 = (bf16[16,16,8,256]{3,2,1,0:T(8,128)(2,1)S(1)}, bf16[16,16,8,256]{3,2,1,0:T(8,128)(2,1)}, u32[]{:S(2)}) copy-start(bf16[16,16,8,256]{3,2,1,0:T(8,128)(2,1)} %param.6) | copy-start | bytes 3145732
  2.5 4.5 %copy-start.2 = (bf16[16,8,4,256]{3,2,1,0:T(4,128)(2,1)S(1)}, bf16[16,8,4,256]{3,2,1,0:T(4,128)(2,1)}, u32[]{:S(2)}) copy-start(bf16[16,8,4,256]{3,2,1,0:T(4,128)(2,1)} %cot_ref.3) | copy-start | bytes 786436
  2.8 5.5 %copy-start = (bf16[2,2,256,256]{3,2,1,0:T(8,128)(2,1)S(1)}, bf16[2,2,256,256]{3,2,1,0:T(8,128)(2,1)}, u32[]{:S(2)}) copy-start(bf16[2,2,256,256]{3,2,1,0:T(8,128)(2,1)} %param.10) | copy-start | bytes 1572868
  2.8 5.5 %copy-start.1 = (bf16[3,256,256]{2,1,0:T(8,128)(2,1)S(1)}, bf16[3,256,256]{2,1,0:T(8,128)(2,1)}, u32[]{:S(2)}) copy-start(bf16[3,256,256]{2,1,0:T(8,128)(2,1)} %wt_ref.5) | copy-start | bytes 1179652
  2.8 5.5 %collective-permute-start = (bf16[128,256]{1,0:T(8,128)(2,1)S(1)}, bf16[128,256]{1,0:T(8,128)(2,1)S(1)}, u32[]{:S(2)}, u32[]{:S(2)}) collective-permute-start(bf16[128,256]{1,0:T(8,128)(2,1)S(1)} %edges.1._), channel_id=1, source_target_pairs={{0,1},{1,0},{2,3},{3,2},{4,5},{5,4},{6,7},{7,6},{8,9},{9,8},{10,11... | collective-permute-start | bytes 196616 | tf_op jit(solution)/shard_map/ppermute | solution.py:506
  7.0 3.1 %collective-permute-start.1 = (bf16[2,8,4,256]{3,2,1,0:T(4,128)(2,1)S(1)}, bf16[2,8,4,256]{3,2,1,0:T(4,128)(2,1)S(1)}, u32[]{:S(2)}, u32[]{:S(2)}) collective-permute-start(bf16[2,8,4,256]{3,2,1,0:T(4,128)(2,1)S(1)} %next.1.rest_3_), channel_id=1, source_target_pairs={{2,0},{4,2},{6,4},{8,6},{10,8},{12,10},{14,12},{16,14},{18,16},{20... | collective-permute-start | bytes 98312 | tf_op jit(solution)/shard_map/ppermute | solution.py:496
  8.5 8.1 %collective-permute-start.3 = (bf16[288,256]{1,0:T(8,128)(2,1)S(1)}, bf16[288,256]{1,0:T(8,128)(2,1)S(1)}, u32[]{:S(2)}, u32[]{:S(2)}) collective-permute-start(bf16[288,256]{1,0:T(8,128)(2,1)S(1)} %get-tuple-element.53), channel_id=1, source_target_pairs={{0,2},{2,4},{4,6},{6,8},{8,10},{10,12},{12,14},{14,16},{16,18},{18... | collective-permute-start | bytes 442376 | tf_op jit(solution)/shard_map/ppermute | solution.py:501
  10.1 6.5 %copy-start.4 = (bf16[3,3,256,256]{3,2,1,0:T(8,128)(2,1)S(1)}, bf16[3,3,256,256]{3,2,1,0:T(8,128)(2,1)}, u32[]{:S(2)}) copy-start(bf16[3,3,256,256]{3,2,1,0:T(8,128)(2,1)} %param.8) | copy-start | bytes 3538948
  16.6 2.0 %collective-permute-start.4 = (bf16[16,9,16,128]{3,2,1,0:T(8,128)(2,1)S(1)}, bf16[16,9,16,128]{3,2,1,0:T(8,128)(2,1)S(1)}, u32[]{:S(2)}, u32[]{:S(2)}) collective-permute-start(bf16[16,9,16,128]{3,2,1,0:T(8,128)(2,1)S(1)} %pass.2._), channel_id=1, source_target_pairs={{0,2},{1,3},{2,0},{3,1},{4,6},{5,7},{6,4},{7,5},{8,10},{9,11},{10,... | collective-permute-start | bytes 1769480 | tf_op jit(solution)/shard_map/ppermute | solution.py:452
  18.8 7.0 %collective-permute-start.5 = (bf16[4,9,16,128]{3,2,1,0:T(8,128)(2,1)S(1)}, bf16[4,9,16,128]{3,2,1,0:T(8,128)(2,1)S(1)}, u32[]{:S(2)}, u32[]{:S(2)}) collective-permute-start(bf16[4,9,16,128]{3,2,1,0:T(8,128)(2,1)S(1)} %get-tuple-element.59.rest_1_), channel_id=1, source_target_pairs={{0,5},{1,4},{2,7},{3,6},{4,1},{5,0},{6,3},{7,2},{8,13},{9,12},{10,... | collective-permute-start | bytes 442376 | tf_op jit(solution)/shard_map/ppermute | solution.py:452
  25.7 1.9 %collective-permute-start.8 = (bf16[16,7,16,128]{3,2,1,0:T(8,128)(2,1)S(1)}, bf16[16,7,16,128]{3,2,1,0:T(8,128)(2,1)S(1)}, u32[]{:S(2)}, u32[]{:S(2)}) collective-permute-start(bf16[16,7,16,128]{3,2,1,0:T(8,128)(2,1)S(1)} %pass.3), channel_id=1, source_target_pairs={{0,2},{1,3},{2,0},{3,1},{4,6},{5,7},{6,4},{7,5},{8,10},{9,11},{10,... | collective-permute-start | bytes 1376264 | tf_op jit(solution)/shard_map/ppermute | solution.py:452
  25.7 6.5 %collective-permute-start.6 = (bf16[4,9,16,128]{3,2,1,0:T(8,128)(2,1)S(1)}, bf16[4,9,16,128]{3,2,1,0:T(8,128)(2,1)S(1)}, u32[]{:S(2)}, u32[]{:S(2)}) collective-permute-start(bf16[4,9,16,128]{3,2,1,0:T(8,128)(2,1)S(1)} %get-tuple-element.60.rest_2_), channel_id=1, source_target_pairs={{0,1},{1,0},{2,3},{3,2},{4,5},{5,4},{6,7},{7,6},{8,9},{9,8},{10,11... | collective-permute-start | bytes 442376 | tf_op jit(solution)/shard_map/ppermute | solution.py:452
  26.7 6.7 %collective-permute-start.7 = (bf16[4,9,16,128]{3,2,1,0:T(8,128)(2,1)S(1)}, bf16[4,9,16,128]{3,2,1,0:T(8,128)(2,1)S(1)}, u32[]{:S(2)}, u32[]{:S(2)}) collective-permute-start(bf16[4,9,16,128]{3,2,1,0:T(8,128)(2,1)S(1)} %get-tuple-element.61.rest_3_), channel_id=1, source_target_pairs={{0,4},{1,5},{2,6},{3,7},{4,0},{5,1},{6,2},{7,3},{8,12},{9,13},{10,... | collective-permute-start | bytes 442376 | tf_op jit(solution)/shard_map/ppermute | solution.py:452
  27.7 8.6 %collective-permute-start.9 = (bf16[4,7,16,128]{3,2,1,0:T(8,128)(2,1)S(1)}, bf16[4,7,16,128]{3,2,1,0:T(8,128)(2,1)S(1)}, u32[]{:S(2)}, u32[]{:S(2)}) collective-permute-start(bf16[4,7,16,128]{3,2,1,0:T(8,128)(2,1)S(1)} %get-tuple-element.67), channel_id=1, source_target_pairs={{0,5},{1,4},{2,7},{3,6},{4,1},{5,0},{6,3},{7,2},{8,13},{9,12},{10,... | collective-permute-start | bytes 344072 | tf_op jit(solution)/shard_map/ppermute | solution.py:452
  29.4 7.5 %collective-permute-start.10 = (bf16[4,7,16,128]{3,2,1,0:T(8,128)(2,1)S(1)}, bf16[4,7,16,128]{3,2,1,0:T(8,128)(2,1)S(1)}, u32[]{:S(2)}, u32[]{:S(2)}) collective-permute-start(bf16[4,7,16,128]{3,2,1,0:T(8,128)(2,1)S(1)} %get-tuple-element.68), channel_id=1, source_target_pairs={{0,1},{1,0},{2,3},{3,2},{4,5},{5,4},{6,7},{7,6},{8,9},{9,8},{10,11... | collective-permute-start | bytes 344072 | tf_op jit(solution)/shard_map/ppermute | solution.py:452
  30.7 7.0 %collective-permute-start.11 = (bf16[4,7,16,128]{3,2,1,0:T(8,128)(2,1)S(1)}, bf16[4,7,16,128]{3,2,1,0:T(8,128)(2,1)S(1)}, u32[]{:S(2)}, u32[]{:S(2)}) collective-permute-start(bf16[4,7,16,128]{3,2,1,0:T(8,128)(2,1)S(1)} %get-tuple-element.69), channel_id=1, source_target_pairs={{0,4},{1,5},{2,6},{3,7},{4,0},{5,1},{6,2},{7,3},{8,12},{9,13},{10,... | collective-permute-start | bytes 344072 | tf_op jit(solution)/shard_map/ppermute | solution.py:452
  37.8 6.2 %collective-permute-start.12 = (bf16[16,16,128]{2,1,0:T(8,128)(2,1)S(1)}, bf16[16,16,128]{2,1,0:T(8,128)(2,1)S(1)}, u32[]{:S(2)}, u32[]{:S(2)}) collective-permute-start(bf16[16,16,128]{2,1,0:T(8,128)(2,1)S(1)} %get-tuple-element.71), channel_id=1, source_target_pairs={{0,24},{1,25},{2,26},{3,27},{4,28},{5,29},{6,30},{7,31},{8,16},{9,... | collective-permute-start | bytes 196616 | tf_op jit(solution)/shard_map/ppermute | solution.py:452
  40.3 6.3 %collective-permute-start.13 = (bf16[16,16,128]{2,1,0:T(8,128)(2,1)S(1)}, bf16[16,16,128]{2,1,0:T(8,128)(2,1)S(1)}, u32[]{:S(2)}, u32[]{:S(2)}) collective-permute-start(bf16[16,16,128]{2,1,0:T(8,128)(2,1)S(1)} %get-tuple-element.72), channel_id=1, source_target_pairs={{0,16},{1,17},{2,18},{3,19},{4,20},{5,21},{6,22},{7,23},{8,24},{9,... | collective-permute-start | bytes 196616 | tf_op jit(solution)/shard_map/ppermute | solution.py:452
  40.3 6.3 %collective-permute-start.14 = (bf16[16,16,128]{2,1,0:T(8,128)(2,1)S(1)}, bf16[16,16,128]{2,1,0:T(8,128)(2,1)S(1)}, u32[]{:S(2)}, u32[]{:S(2)}) collective-permute-start(bf16[16,16,128]{2,1,0:T(8,128)(2,1)S(1)} %get-tuple-element.73), channel_id=1, source_target_pairs={{0,8},{1,9},{2,10},{3,11},{4,12},{5,13},{6,14},{7,15},{8,0},{9,1},... | collective-permute-start | bytes 196616 | tf_op jit(solution)/shard_map/ppermute | solution.py:452
  46.6 5.6 %collective-permute-start.17 = (bf16[16,16,128]{2,1,0:T(8,128)(2,1)S(1)}, bf16[16,16,128]{2,1,0:T(8,128)(2,1)S(1)}, u32[]{:S(2)}, u32[]{:S(2)}) collective-permute-start(bf16[16,16,128]{2,1,0:T(8,128)(2,1)S(1)} %line_sum.1.a_ref), channel_id=1, source_target_pairs={{0,8},{1,9},{2,10},{3,11},{4,12},{5,13},{6,14},{7,15},{8,0},{9,1},... | collective-permute-start | bytes 196616 | tf_op jit(solution)/shard_map/ppermute | solution.py:452
  46.7 7.5 %collective-permute-start.16 = (bf16[16,16,128]{2,1,0:T(8,128)(2,1)S(1)}, bf16[16,16,128]{2,1,0:T(8,128)(2,1)S(1)}, u32[]{:S(2)}, u32[]{:S(2)}) collective-permute-start(bf16[16,16,128]{2,1,0:T(8,128)(2,1)S(1)} %line_sum.1.a_ref), channel_id=1, source_target_pairs={{0,16},{1,17},{2,18},{3,19},{4,20},{5,21},{6,22},{7,23},{8,24},{9,... | collective-permute-start | bytes 196616 | tf_op jit(solution)/shard_map/ppermute | solution.py:452
  49.7 6.1 %collective-permute-start.15 = (bf16[16,16,128]{2,1,0:T(8,128)(2,1)S(1)}, bf16[16,16,128]{2,1,0:T(8,128)(2,1)S(1)}, u32[]{:S(2)}, u32[]{:S(2)}) collective-permute-start(bf16[16,16,128]{2,1,0:T(8,128)(2,1)S(1)} %line_sum.1.a_ref), channel_id=1, source_target_pairs={{0,24},{1,25},{2,26},{3,27},{4,28},{5,29},{6,30},{7,31},{8,16},{9,... | collective-permute-start | bytes 196616 | tf_op jit(solution)/shard_map/ppermute | solution.py:452
  51.1 8.3 %collective-permute-start.2 = (bf16[64,256]{1,0:T(8,128)(2,1)S(1)}, bf16[64,256]{1,0:T(8,128)(2,1)S(1)}, u32[]{:S(2)}, u32[]{:S(2)}) collective-permute-start(bf16[64,256]{1,0:T(8,128)(2,1)S(1)} %get-tuple-element.51), channel_id=1, source_target_pairs={{0,1},{1,0},{2,3},{3,2},{4,5},{5,4},{6,7},{7,6},{8,9},{9,8},{10,11... | collective-permute-start | bytes 98312 | tf_op jit(solution)/shard_map/ppermute | solution.py:506
  55.8 11.0 %collective-permute-start.20 = (bf16[4,16,16,128]{3,2,1,0:T(8,128)(2,1)S(1)}, bf16[4,16,16,128]{3,2,1,0:T(8,128)(2,1)S(1)}, u32[]{:S(2)}, u32[]{:S(2)}) collective-permute-start(bf16[4,16,16,128]{3,2,1,0:T(8,128)(2,1)S(1)} %line_gather.1.rest_0_.a_ref), channel_id=1, source_target_pairs={{0,4},{1,5},{2,6},{3,7},{4,0},{5,1},{6,2},{7,3},{8,12},{9,13},{10,... | collective-permute-start | bytes 786440 | tf_op jit(solution)/shard_map/ppermute | solution.py:452
  56.8 11.8 %collective-permute-start.19 = (bf16[4,16,16,128]{3,2,1,0:T(8,128)(2,1)S(1)}, bf16[4,16,16,128]{3,2,1,0:T(8,128)(2,1)S(1)}, u32[]{:S(2)}, u32[]{:S(2)}) collective-permute-start(bf16[4,16,16,128]{3,2,1,0:T(8,128)(2,1)S(1)} %line_gather.1.rest_0_.a_ref), channel_id=1, source_target_pairs={{0,1},{1,0},{2,3},{3,2},{4,5},{5,4},{6,7},{7,6},{8,9},{9,8},{10,11... | collective-permute-start | bytes 786440 | tf_op jit(solution)/shard_map/ppermute | solution.py:452
  58.3 10.2 %collective-permute-start.18 = (bf16[4,16,16,128]{3,2,1,0:T(8,128)(2,1)S(1)}, bf16[4,16,16,128]{3,2,1,0:T(8,128)(2,1)S(1)}, u32[]{:S(2)}, u32[]{:S(2)}) collective-permute-start(bf16[4,16,16,128]{3,2,1,0:T(8,128)(2,1)S(1)} %line_gather.1.rest_0_.a_ref), channel_id=1, source_target_pairs={{0,5},{1,4},{2,7},{3,6},{4,1},{5,0},{6,3},{7,2},{8,13},{9,12},{10,... | collective-permute-start | bytes 786440 | tf_op jit(solution)/shard_map/ppermute | solution.py:452
  68.7 2.7 %collective-permute-start.21 = (bf16[16,16,16,128]{3,2,1,0:T(8,128)(2,1)S(1)}, bf16[16,16,16,128]{3,2,1,0:T(8,128)(2,1)S(1)}, u32[]{:S(2)}, u32[]{:S(2)}) collective-permute-start(bf16[16,16,16,128]{3,2,1,0:T(8,128)(2,1)S(1)} %plane_gather.1.half_ref), channel_id=1, source_target_pairs={{0,2},{1,3},{2,0},{3,1},{4,6},{5,7},{6,4},{7,5},{8,10},{9,11},{10,... | collective-permute-start | bytes 3145736 | tf_op jit(solution)/shard_map/ppermute | solution.py:452
